TPU v7x, 32 devices: a whole 2x2x4 slice. The times are simulated.
32 devices in a mesh: outer: 16 (over z, y, core), inner: 2 (over x).
Axes of the slice: x: 2, y: 2, z: 4, core: 2. Of those that a mesh axis runs over, the one named last changes fastest.
Arguments:
- queries: bfloat16 [16384, 512], P(('outer', 'inner')), may hold values from -5 to 5
- key_matrix: bfloat16 [16384, 512], P(('outer', 'inner')), may hold values from -5 to 5
- value_matrix: bfloat16 [16384, 512], P(('outer', 'inner')), may hold values from -5 to 5
- cotangent: bfloat16 [16384, 512], P(('outer', 'inner')), may hold values from -6 to 6
Outputs:
- attended: bfloat16 [16384, 512], P(('outer', 'inner'))
- query_grad: bfloat16 [16384, 512], P(('outer', 'inner'))
- key_grad: bfloat16 [16384, 512], P(('outer', 'inner'))
- value_grad: bfloat16 [16384, 512], P(('outer', 'inner'))
All inputs are finite; a program needn't handle non-finite values.
Results may differ from a plain program's by a relative error of at most 0.02.
Values may be sent and summed in bfloat16 or wider, within the bound.
No kernel may reach another device: no remote copies, remote signals or barrier semaphores. Data moves between devices by JAX's collectives and lax.ppermute only.
A program may use at most 128 MiB of HBM per device.

v0:
```python
import functools
import math

import jax
import jax.numpy as jnp
from jax import lax
from jax.experimental import pallas as pl
from jax.experimental.pallas import tpu as pltpu
from jax.sharding import PartitionSpec as P

HEAD = 128
BLOCK = 128
PARENT = 256
LEVELS = 3
CHUNKS = 2
INV_ROOT = HEAD**-0.5
TO_LOG2 = INV_ROOT * math.log2(math.e)
MASKED = -1e30
BF = jnp.bfloat16
F32 = jnp.float32


def dot_nt(a, b):
    return lax.dot_general(a, b, (((1,), (1,)), ((), ())), preferred_element_type=F32)


def dot_nn(a, b):
    return jnp.dot(a, b, preferred_element_type=F32)


def order_matrix(inverse):
    row = lax.broadcasted_iota(jnp.int32, (PARENT, PARENT), 0)
    col = lax.broadcasted_iota(jnp.int32, (PARENT, PARENT), 1)
    place, token = (col, row) if inverse else (row, col)
    slab = place // 64
    source = 4 * (place % 64) + 2 * (slab % 2) + slab // 2
    return jnp.where(source == token, 1.0, 0.0).astype(BF)


def pool1(x):
    return ((x[:BLOCK].astype(F32) + x[BLOCK:].astype(F32)) * 0.5).astype(BF)


def pool2(x):
    half = x[:BLOCK].astype(F32) + x[BLOCK:].astype(F32)
    return ((half[:64] + half[64:]) * 0.25).astype(BF)


def pool12(x):
    return ((x[:64].astype(F32) + x[64:].astype(F32)) * 0.5).astype(BF)


def twice(x, axis=0):
    return jnp.concatenate([x, x], axis=axis)


def pack_kernel(where, a_own, a_far, b_own, b_far, own, far):
    width = a_own.shape[1]
    order = order_matrix(False)
    for i in range(a_own.shape[0] // PARENT):
        rows = slice(i * PARENT, (i + 1) * PARENT)
        own[rows, :width] = dot_nn(order, a_own[rows, :]).astype(BF)
        own[rows, width:] = dot_nn(order, b_own[rows, :]).astype(BF)
        far[rows, :width] = dot_nn(order, a_far[rows, :]).astype(BF)
        far[rows, width:] = dot_nn(order, b_far[rows, :]).astype(BF)


def pack(where, a, b, chunk):
    rows, columns = a.shape
    width = columns // 2 // CHUNKS
    near = pl.BlockSpec((rows, width), lambda i, w: (0, w[0] * CHUNKS + chunk))
    away = pl.BlockSpec((rows, width), lambda i, w: (0, (1 - w[0]) * CHUNKS + chunk))
    out = pl.BlockSpec((rows, 2 * width), lambda i, w: (0, 0))
    return pl.pallas_call(
        pack_kernel,
        grid_spec=pltpu.PrefetchScalarGridSpec(
            num_scalar_prefetch=1,
            grid=(1,),
            in_specs=[near, away, near, away],
            out_specs=[out, out],
        ),
        out_shape=[jax.ShapeDtypeStruct((rows, 2 * width), BF)] * 2,
        cost_estimate=pl.CostEstimate(flops=0, bytes_accessed=8 * rows * width * 2, transcendentals=0),
    )(where, a, a, b, b)


def halo_kernel(where, own, got, to_right, to_left):
    def fill(first, second):
        to_right[0:256, :] = second[256:512, :]
        to_right[256:384, :] = pool1(second[0:256, :])
        to_right[384:448, :] = pool2(first[0:256, :])
        to_right[448:512, :] = pool2(first[256:512, :])
        to_left[0:256, :] = first[0:256, :]
        to_left[256:384, :] = pool1(first[256:512, :])
        to_left[384:448, :] = pool2(second[0:256, :])
        to_left[448:512, :] = pool2(second[256:512, :])

    @pl.when(where[0] == 0)
    def _():
        fill(own, got)

    @pl.when(where[0] == 1)
    def _():
        fill(got, own)


def smem():
    return pl.BlockSpec(memory_space=pltpu.SMEM)


def vmem():
    return pl.BlockSpec(memory_space=pltpu.VMEM)


def halo(where, own, got):
    shape = jax.ShapeDtypeStruct(own.shape, BF)
    return pl.pallas_call(
        halo_kernel,
        in_specs=[smem(), vmem(), vmem()],
        out_specs=[vmem(), vmem()],
        out_shape=[shape, shape],
        cost_estimate=pl.CostEstimate(flops=0, bytes_accessed=4 * own.size * 2, transcendentals=0),
    )(where, own, got)


def swap64(x):
    return pltpu.roll(x, 64, 1)


def low_lanes(shape):
    return lax.broadcasted_iota(jnp.int32, shape, 1) < 64


def spread64(x, half):
    other = swap64(x)
    low = low_lanes(x.shape)
    return jnp.where(low, x, other) if half == 0 else jnp.where(low, other, x)


def far_forward(k, v_t, q, bias, p_ref):
    k0, k1, k2, k3 = k
    v0, v1, v2, v3 = v_t
    left, right = bias
    outer = dot_nt(jnp.concatenate([k0, k3], axis=0), q)
    first, last = outer[:BLOCK], outer[BLOCK:]
    mid_low = dot_nt(k2, q[:BLOCK])
    mid_high = dot_nt(k1, q[BLOCK:])
    if left is not None:
        first = first + left
        mid_high = mid_high + left
    if right is not None:
        last = last + right
        mid_low = mid_low + right
    mid = jnp.concatenate([mid_low, mid_high], axis=1)
    peak = jnp.max(jnp.maximum(jnp.maximum(first, last), mid), axis=0, keepdims=True)
    parts = [jnp.exp2((x - peak) * TO_LOG2) for x in (first, last, mid)]
    for n, x in enumerate(parts):
        p_ref[n * BLOCK : (n + 1) * BLOCK, :] = x
    total = jnp.sum(parts[0] + parts[1] + parts[2], axis=0, keepdims=True)
    pb = [x.astype(BF) for x in parts]
    mixed = dot_nn(
        jnp.concatenate([v0, v3], axis=1), jnp.concatenate(pb[:2], axis=0)
    ) + jnp.concatenate([dot_nn(v2, pb[2][:, :BLOCK]), dot_nn(v1, pb[2][:, BLOCK:])], axis=1)
    return peak, total, mixed


def far_backward(k_t, v, q, p_ref, factor, g, ec):
    k0, k1, k2, k3 = k_t
    v0, v1, v2, v3 = v
    e_out = p_ref[: 2 * BLOCK, :] * factor
    e_mid = p_ref[2 * BLOCK :, :] * factor
    eb_out, eb_mid = e_out.astype(BF), e_mid.astype(BF)
    p_out = dot_nt(jnp.concatenate([v0, v3], axis=0), g)
    p_mid = jnp.concatenate([dot_nt(v2, g[:BLOCK]), dot_nt(v1, g[BLOCK:])], axis=1)
    r_out = (e_out * (p_out - ec)).astype(BF)
    r_mid = (e_mid * (p_mid - ec)).astype(BF)
    dv03 = dot_nn(eb_out, g)
    dv2 = dot_nn(eb_mid[:, :BLOCK], g[:BLOCK])
    dv1 = dot_nn(eb_mid[:, BLOCK:], g[BLOCK:])
    dk03 = dot_nn(r_out, q)
    dk2 = dot_nn(r_mid[:, :BLOCK], q[:BLOCK])
    dk1 = dot_nn(r_mid[:, BLOCK:], q[BLOCK:])
    dq_t = dot_nn(jnp.concatenate([k0, k3], axis=1), r_out) + jnp.concatenate(
        [dot_nn(k2, r_mid[:, :BLOCK]), dot_nn(k1, r_mid[:, BLOCK:])], axis=1
    )
    return (dk03[:BLOCK], dk1, dk2, dk03[BLOCK:]), (dv03[:BLOCK], dv1, dv2, dv03[BLOCK:]), dq_t


def main_kernel(
    where, kv_own, kv_got, qg_own, qg_got, from_left, from_right,
    oq_own, oq_far, grad, to_left, to_right,
    raw, raw_t, one, one_t, two, two_t, qs, gs, p0, p1, p2, acc0, acc1, acc2, oq,
):
    side = where[0]
    width = kv_own.shape[1] // 2
    left_bias = (1 - where[1]).astype(F32) * MASKED
    right_bias = (1 - where[2]).astype(F32) * MASKED
    own_at = pl.multiple_of(side * 512, 512)
    got_at = pl.multiple_of((1 - side) * 512, 512)
    for h in range(width // HEAD):
        kc = slice(h * HEAD, (h + 1) * HEAD)
        vc = slice(width + h * HEAD, width + (h + 1) * HEAD)
        for n, cols in ((0, kc), (1, vc)):
            raw[n, 0:256, :] = from_left[0:256, cols]
            raw[n, pl.ds(256 + own_at, 512), :] = kv_own[:, cols]
            raw[n, pl.ds(256 + got_at, 512), :] = kv_got[:, cols]
            raw[n, 1280:1536, :] = from_right[0:256, cols]
            one[n, 0:128, :] = from_left[256:384, cols]
            for i in range(6):
                block = pool1(raw[n, i * PARENT : (i + 1) * PARENT, :])
                at = (i + 1) * BLOCK
                one[n, at : at + BLOCK, :] = block
            one[n, 896:1024, :] = from_right[256:384, cols]
            two[n, 0:128, :] = from_left[384:512, cols]
            two[n, 128:192, :] = pool12(one[n, 0:128, :])
            two[n, 192:256, :] = pool2(raw[n, 0:256, :])
            two[n, 256:320, :] = pool2(raw[n, 1280:1536, :])
            two[n, 320:384, :] = pool12(one[n, 896:1024, :])
            two[n, 384:512, :] = from_right[384:512, cols]
            for i in range(6):
                rows = slice(i * PARENT, (i + 1) * PARENT)
                raw_t[n, :, rows] = raw[n, rows, :].T
            for i in range(8):
                rows = slice(i * BLOCK, (i + 1) * BLOCK)
                one_t[n, :, rows] = one[n, rows, :].T
            for i in range(4):
                rows = slice(i * BLOCK, (i + 1) * BLOCK)
                two_t[n, :, rows] = two[n, rows, :].T
        qs[pl.ds(own_at, 512), :] = qg_own[:, kc]
        qs[pl.ds(got_at, 512), :] = qg_got[:, kc]
        gs[pl.ds(own_at, 512), :] = qg_own[:, vc]
        gs[pl.ds(got_at, 512), :] = qg_got[:, vc]

        def blocks(ref, n, which):
            return [ref[n, b * BLOCK : (b + 1) * BLOCK, :] for b in which]

        def blocks_t(ref, n, which):
            return [ref[n, :, b * BLOCK : (b + 1) * BLOCK] for b in which]

        q_parents = [qs[i * PARENT : (i + 1) * PARENT, :] for i in range(4)]
        q1 = [
            jnp.concatenate([pool1(q_parents[2 * j]), pool1(q_parents[2 * j + 1])], axis=0)
            for j in range(2)
        ]
        q2 = jnp.concatenate([pool2(x) for x in q_parents], axis=0)
        which1 = [(0, 1, 4, 5), (2, 3, 6, 7)]
        bias1 = [(left_bias, None), (None, right_bias)]
        which2 = (0, 1, 2, 3)
        far1 = [
            far_forward(
                blocks(one, 0, which1[j]), blocks_t(one_t, 1, which1[j]), q1[j], bias1[j], p1.at[j]
            )
            for j in range(2)
        ]
        far2 = far_forward(
            blocks(two, 0, which2), blocks_t(two_t, 1, which2), q2, (left_bias, right_bias), p2
        )
        acc0[...] = jnp.zeros_like(acc0)
        g1_t, ec1, f1 = [], [], []
        g2_t, ec2, low2 = [], [], []
        dq0 = []
        for i in range(4):
            rows = slice(i * PARENT, i * PARENT + 3 * PARENT)
            q = q_parents[i]
            g = gs[i * PARENT : (i + 1) * PARENT, :]
            s = dot_nt(raw[0, rows, :], q)
            pieces = [s[:PARENT], s[PARENT : 2 * PARENT], s[2 * PARENT :]]
            if i == 0:
                pieces[0] = pieces[0] + left_bias
            if i == 3:
                pieces[2] = pieces[2] + right_bias
            m0 = jnp.max(
                jnp.maximum(jnp.maximum(pieces[0], pieces[1]), pieces[2]), axis=0, keepdims=True
            )
            e = [jnp.exp2((x - m0) * TO_LOG2) for x in pieces]
            for n in range(3):
                p0[n * PARENT : (n + 1) * PARENT, :] = e[n]
            z0 = jnp.sum(e[0] + e[1] + e[2], axis=0, keepdims=True)
            u0 = dot_nn(raw_t[1, :, rows], jnp.concatenate([x.astype(BF) for x in e], axis=0))
            j, half = i // 2, i % 2
            lanes = slice(half * BLOCK, (half + 1) * BLOCK)
            m1, z1, u1 = (x[:, lanes] for x in far1[j])
            lanes2 = slice(j * BLOCK, (j + 1) * BLOCK)
            m2, z2, u2 = (spread64(x[:, lanes2], half) for x in far2)
            m1w, m2w = twice(m1, 1), twice(m2, 1)
            m = jnp.maximum(jnp.maximum(m0, m1w), m2w)
            a0 = jnp.exp2((m0 - m) * TO_LOG2)
            a1 = 2.0 * jnp.exp2((m1w - m) * TO_LOG2)
            a2 = 4.0 * jnp.exp2((m2w - m) * TO_LOG2)
            z = a0 * z0 + a1 * twice(z1, 1) + a2 * twice(z2, 1)
            inv = 1.0 / z
            o = ((a0 * inv) * u0 + (a1 * inv) * twice(u1, 1) + (a2 * inv) * twice(u2, 1)).astype(BF)
            oq[i, 0, h * HEAD : (h + 1) * HEAD, :] = o
            lg = m * TO_LOG2 + jnp.log2(z)
            g_t = g.astype(F32).T
            dr = jnp.sum(o.astype(F32) * g_t, axis=0, keepdims=True)
            lg_a, lg_b = lg[:, :BLOCK], lg[:, BLOCK:]
            g_a, g_b = g_t[:, :BLOCK], g_t[:, BLOCK:]
            dr_a, dr_b = dr[:, :BLOCK], dr[:, BLOCK:]
            low = jnp.minimum(lg_a, lg_b)
            w_a, w_b = jnp.exp2(low - lg_a), jnp.exp2(low - lg_b)
            g1_t.append((w_a * g_a + w_b * g_b).astype(BF))
            ec1.append(w_a * dr_a + w_b * dr_b)
            f1.append(2.0 * jnp.exp2(m1 * TO_LOG2 - low))
            lower = jnp.minimum(low, swap64(low))
            w_a, w_b = jnp.exp2(lower - lg_a), jnp.exp2(lower - lg_b)
            part = w_a * g_a + w_b * g_b
            g2_t.append(part + swap64(part))
            part = w_a * dr_a + w_b * dr_b
            ec2.append(part + swap64(part))
            low2.append(lower)
            f0 = jnp.exp2(m0 * TO_LOG2 - lg)
            products = dot_nt(raw[1, rows, :], g)
            weights = p0[...] * f0
            eb = weights.astype(BF)
            r = (weights * (products - dr)).astype(BF)
            acc0[1, rows, :] += dot_nn(eb, g)
            acc0[0, rows, :] += dot_nn(r, q)
            dq0.append(dot_nn(raw_t[0, :, rows], r))
        acc1[...] = jnp.zeros_like(acc1)
        dq1 = []
        for j in range(2):
            pair = slice(2 * j, 2 * j + 2)
            g1 = jnp.concatenate([x.astype(F32).T.astype(BF) for x in g1_t[pair]], axis=0)
            dk, dv, dq = far_backward(
                blocks_t(one_t, 0, which1[j]), blocks(one, 1, which1[j]), q1[j], p1.at[j],
                jnp.concatenate(f1[pair], axis=1), g1, jnp.concatenate(ec1[pair], axis=1),
            )
            for n, b in enumerate(which1[j]):
                acc1[0, b * BLOCK : (b + 1) * BLOCK, :] += dk[n]
                acc1[1, b * BLOCK : (b + 1) * BLOCK, :] += dv[n]
            dq1.append(dq)

        def joined(parts):
            return jnp.concatenate(
                [
                    jnp.where(low_lanes(parts[0].shape), parts[2 * j], parts[2 * j + 1])
                    for j in range(2)
                ],
                axis=1,
            )

        g2 = joined(g2_t).T.astype(BF)
        f2 = 4.0 * jnp.exp2(far2[0] * TO_LOG2 - joined(low2))
        dk, dv, dq2 = far_backward(
            blocks_t(two_t, 0, which2), blocks(two, 1, which2), q2, p2, f2, g2, joined(ec2)
        )
        for n in range(4):
            acc2[0, n * BLOCK : (n + 1) * BLOCK, :] = dk[n]
            acc2[1, n * BLOCK : (n + 1) * BLOCK, :] = dv[n]
        for i in range(4):
            j, half = i // 2, i % 2
            d1 = dq1[j][:, half * BLOCK : (half + 1) * BLOCK]
            d2 = spread64(dq2[:, j * BLOCK : (j + 1) * BLOCK], half)
            coarse = 0.5 * d1 + 0.25 * d2
            oq[i, 1, h * HEAD : (h + 1) * HEAD, :] = ((dq0[i] + twice(coarse, 1)) * INV_ROOT).astype(BF)
        for n, cols, scale in ((0, kc, INV_ROOT), (1, vc, 1.0)):
            for i in range(4):
                rows = slice((i + 1) * PARENT, (i + 2) * PARENT)
                coarse = acc1[n, (i + 2) * BLOCK : (i + 3) * BLOCK, :] * (0.5 * scale)
                grad[i * PARENT : (i + 1) * PARENT, cols] = acc0[n, rows, :] * scale + twice(coarse)
            far = acc2[n, 128:256, :] * (0.25 * scale)
            mid = acc1[n, 0:256, :] * (0.5 * scale)
            near = acc0[n, 0:256, :] * scale
            to_left[0:256, cols] = (near + twice(mid[128:] + twice(far[64:]))).astype(BF)
            to_left[256:384, cols] = (mid[:128] + twice(far[:64])).astype(BF)
            to_left[384:512, cols] = (acc2[n, 0:128, :] * (0.25 * scale)).astype(BF)
            far = acc2[n, 256:384, :] * (0.25 * scale)
            mid = acc1[n, 768:1024, :] * (0.5 * scale)
            near = acc0[n, 1280:1536, :] * scale
            to_right[0:256, cols] = (near + twice(mid[:128] + twice(far[:64]))).astype(BF)
            to_right[256:384, cols] = (mid[128:] + twice(far[64:])).astype(BF)
            to_right[384:512, cols] = (acc2[n, 384:512, :] * (0.25 * scale)).astype(BF)
    oq_own[...] = oq[pl.ds(side * 2, 2)]
    oq_far[...] = oq[pl.ds((1 - side) * 2, 2)]


def main(where, kv_own, kv_got, qg_own, qg_got, from_left, from_right):
    rows, both = kv_own.shape
    width = both // 2
    oq_shape = jax.ShapeDtypeStruct((2, 2, width, PARENT), BF)
    halo_shape = jax.ShapeDtypeStruct((512, both), BF)
    return pl.pallas_call(
        main_kernel,
        in_specs=[smem()] + [vmem()] * 6,
        out_specs=[vmem()] * 5,
        out_shape=[
            oq_shape,
            oq_shape,
            jax.ShapeDtypeStruct((2 * rows, both), F32),
            halo_shape,
            halo_shape,
        ],
        scratch_shapes=[
            pltpu.VMEM((2, 1536, HEAD), BF),
            pltpu.VMEM((2, HEAD, 1536), BF),
            pltpu.VMEM((2, 1024, HEAD), BF),
            pltpu.VMEM((2, HEAD, 1024), BF),
            pltpu.VMEM((2, 512, HEAD), BF),
            pltpu.VMEM((2, HEAD, 512), BF),
            pltpu.VMEM((1024, HEAD), BF),
            pltpu.VMEM((1024, HEAD), BF),
            pltpu.VMEM((768, PARENT), F32),
            pltpu.VMEM((2, 384, PARENT), F32),
            pltpu.VMEM((384, PARENT), F32),
            pltpu.VMEM((2, 1536, HEAD), F32),
            pltpu.VMEM((2, 1024, HEAD), F32),
            pltpu.VMEM((2, 512, HEAD), F32),
            pltpu.VMEM((4, 2, width, PARENT), BF),
        ],
        compiler_params=pltpu.CompilerParams(vmem_limit_bytes=32 * 1024 * 1024),
        cost_estimate=pl.CostEstimate(
            flops=4_000_000_000 // CHUNKS, bytes_accessed=6 * 512 * both * 2, transcendentals=1_000_000
        ),
    )(where, kv_own, kv_got, qg_own, qg_got, from_left, from_right)


def join_kernel(where, grad, from_left, from_right, own, far):
    def part(i, ref):
        x = grad[i * PARENT : (i + 1) * PARENT, :]
        tail = ref[384:512, :].astype(F32)
        return x, tail

    def value(i):
        x = grad[i * PARENT : (i + 1) * PARENT, :]
        if i == 0:
            return x + from_left[0:256, :].astype(F32) + twice(twice(from_right[384:448, :].astype(F32)))
        if i == 1:
            return x + twice(
                from_left[256:384, :].astype(F32) + twice(from_right[448:512, :].astype(F32))
            )
        if i == 2:
            return x + twice(
                from_right[256:384, :].astype(F32) + twice(from_left[384:448, :].astype(F32))
            )
        return x + from_right[0:256, :].astype(F32) + twice(twice(from_left[448:512, :].astype(F32)))

    def fill(first, second):
        first[0:256, :] = value(0).astype(BF)
        first[256:512, :] = value(1).astype(BF)
        second[0:256, :] = value(2).astype(BF)
        second[256:512, :] = value(3).astype(BF)

    @pl.when(where[0] == 0)
    def _():
        fill(own, far)

    @pl.when(where[0] == 1)
    def _():
        fill(far, own)


def join(where, grad, from_left, from_right):
    shape = jax.ShapeDtypeStruct(from_left.shape, BF)
    return pl.pallas_call(
        join_kernel,
        in_specs=[smem(), vmem(), vmem(), vmem()],
        out_specs=[vmem(), vmem()],
        out_shape=[shape, shape],
        cost_estimate=pl.CostEstimate(flops=0, bytes_accessed=grad.size * 8, transcendentals=0),
    )(where, grad, from_left, from_right)


def unpack_rows_kernel(where, *refs):
    ins, (first, second) = refs[:-2], refs[-2:]
    order = order_matrix(True)
    width = ins[0].shape[1] // 2
    for c in range(CHUNKS):
        for ref, side in ((ins[c], where[0]), (ins[CHUNKS + c], 1 - where[0])):
            at = pl.ds(pl.multiple_of((side * CHUNKS + c) * width, width), width)
            for i in range(2):
                rows = slice(i * PARENT, (i + 1) * PARENT)
                first[rows, at] = dot_nn(order, ref[rows, :width]).astype(BF)
                second[rows, at] = dot_nn(order, ref[rows, width:]).astype(BF)


def unpack_columns_kernel(where, *refs):
    ins, (first, second) = refs[:-2], refs[-2:]
    order = order_matrix(True)
    width = ins[0].shape[2]
    for c in range(CHUNKS):
        for ref, side in ((ins[c], where[0]), (ins[CHUNKS + c], 1 - where[0])):
            at = pl.ds(pl.multiple_of((side * CHUNKS + c) * width, width), width)
            for i in range(2):
                rows = slice(i * PARENT, (i + 1) * PARENT)
                first[rows, at] = dot_nt(order, ref[i, 0]).astype(BF)
                second[rows, at] = dot_nt(order, ref[i, 1]).astype(BF)


def unpack(kernel, where, own, got, shape):
    out = jax.ShapeDtypeStruct(shape, BF)
    return pl.pallas_call(
        kernel,
        in_specs=[smem()] + [vmem()] * (2 * CHUNKS),
        out_specs=[vmem(), vmem()],
        out_shape=[out, out],
        cost_estimate=pl.CostEstimate(flops=0, bytes_accessed=shape[0] * shape[1] * 8, transcendentals=0),
    )(where, *own, *got)


def on_device(queries, key_matrix, value_matrix, cotangent):
    axes = ("outer", "inner")
    count = lax.axis_size("outer") * lax.axis_size("inner")
    device = lax.axis_index("outer") * lax.axis_size("inner") + lax.axis_index("inner")
    where = jnp.stack(
        [device % 2, (device >= 2).astype(jnp.int32), (device < count - 2).astype(jnp.int32)]
    ).astype(jnp.int32)
    across = [(i, i ^ 1) for i in range(count)]
    rightward = [(i, i + 2) for i in range(count - 2)]
    leftward = [(i + 2, i) for i in range(count - 2)]

    def swap(x):
        return lax.ppermute(x, axes, across)

    kv = [pack(where, key_matrix, value_matrix, c) for c in range(CHUNKS)]
    qg = [pack(where, queries, cotangent, c) for c in range(CHUNKS)]
    oq_own, oq_got, kv_own, kv_got = [], [], [], []
    for c in range(CHUNKS):
        got_kv = swap(kv[c][1])
        got_qg = swap(qg[c][1])
        to_right, to_left = halo(where, kv[c][0], got_kv)
        from_left = lax.ppermute(to_right, axes, rightward)
        from_right = lax.ppermute(to_left, axes, leftward)
        own, far, grad, to_left, to_right = main(
            where, kv[c][0], got_kv, qg[c][0], got_qg, from_left, from_right
        )
        from_left = lax.ppermute(to_right, axes, rightward)
        from_right = lax.ppermute(to_left, axes, leftward)
        oq_own.append(own)
        oq_got.append(swap(far))
        own, far = join(where, grad, from_left, from_right)
        kv_own.append(own)
        kv_got.append(swap(far))
    attended, query_grad = unpack(unpack_columns_kernel, where, oq_own, oq_got, queries.shape)
    key_grad, value_grad = unpack(unpack_rows_kernel, where, kv_own, kv_got, queries.shape)
    return attended, query_grad, key_grad, value_grad


def solution(mesh):
    spec = P(("outer", "inner"), None)
    return jax.shard_map(
        on_device,
        mesh=mesh,
        in_specs=(spec,) * 4,
        out_specs=(spec,) * 4,
        check_vma=False,
    )
```

profile of v0, /device:TPU:8, one launch (start us, length us, event | category | flops | bytes accessed | tf_op | source)
XLA Modules:
  0.0 91.0 jit_solution(11761353011580735528)
XLA Ops:
  1.3 2.9 %shard_map.79 = (bf16[512,256]{1,0:T(8,128)(2,1)}, bf16[512,256]{1,0:T(8,128)(2,1)}) custom-call(s32[3]{0:T(128)} %pad_add_fusion.where, bf16[512,512]{1,0:T(8,128)(2,1)} %a_far.6, bf16[512,512]{1,0:T(8,128)(2,1)} %a_far.6, bf16[512,512]{1,0:T(8,128)(2,1)} %b_far.6, bf16[512,512]{1,0:T(8,128)(2,1)} %b_far.6), custom_call_target="tpu_custom_call" | custom-call | bytes 1048576 | tf_op jit(solution)/shard_map/pallas_call | solution.py:74
  5.7 2.9 %shard_map.75 = (bf16[512,256]{1,0:T(8,128)(2,1)}, bf16[512,256]{1,0:T(8,128)(2,1)}) custom-call(s32[3]{0:T(128)} %pad_add_fusion.where, bf16[512,512]{1,0:T(8,128)(2,1)} %a_far.6, bf16[512,512]{1,0:T(8,128)(2,1)} %a_far.6, bf16[512,512]{1,0:T(8,128)(2,1)} %b_far.6, bf16[512,512]{1,0:T(8,128)(2,1)} %b_far.6), custom_call_target="tpu_custom_call" | custom-call | bytes 1048576 | tf_op jit(solution)/shard_map/pallas_call | solution.py:74
  9.2 3.0 %shard_map.80 = (bf16[512,256]{1,0:T(8,128)(2,1)}, bf16[512,256]{1,0:T(8,128)(2,1)}) custom-call(s32[3]{0:T(128)} %pad_add_fusion.where, bf16[512,512]{1,0:T(8,128)(2,1)} %a_far.7, bf16[512,512]{1,0:T(8,128)(2,1)} %a_far.7, bf16[512,512]{1,0:T(8,128)(2,1)} %b_far.7, bf16[512,512]{1,0:T(8,128)(2,1)} %b_far.7), custom_call_target="tpu_custom_call" | custom-call | bytes 1048576 | tf_op jit(solution)/shard_map/pallas_call | solution.py:74
  14.3 2.0 %shard_map.81 = (bf16[512,256]{1,0:T(8,128)(2,1)}, bf16[512,256]{1,0:T(8,128)(2,1)}) custom-call(s32[3]{0:T(128)} %pad_add_fusion.where, bf16[512,256]{1,0:T(8,128)(2,1)} %get-tuple-element.41.own.kv_own, bf16[512,256]{1,0:T(8,128)(2,1)} %copy-done.6), custom_call_target="tpu_custom_call" | custom-call | bytes 1048576 | tf_op jit(solution)/shard_map/pallas_call | solution.py:117
  16.3 1.9 %collective-permute-start.6 = (bf16[512,256]{1,0:T(8,128)(2,1)}, bf16[512,256]{1,0:T(8,128)(2,1)S(1)}, u32[]{:S(2)}, u32[]{:S(2)}) collective-permute-start(bf16[512,256]{1,0:T(8,128)(2,1)} %get-tuple-element.45), channel_id=1, source_target_pairs={{0,2},{1,3},{2,4},{3,5},{4,6},{5,7},{6,8},{7,9},{8,10},{9,11},{10,... | collective-permute-start | bytes 786440 | tf_op jit(solution)/shard_map/ppermute | solution.py:522
  18.2 4.5 %collective-permute-start.7 = (bf16[512,256]{1,0:T(8,128)(2,1)}, bf16[512,256]{1,0:T(8,128)(2,1)S(1)}, u32[]{:S(2)}, u32[]{:S(2)}) collective-permute-start(bf16[512,256]{1,0:T(8,128)(2,1)} %get-tuple-element.46), channel_id=1, source_target_pairs={{2,0},{3,1},{4,2},{5,3},{6,4},{7,5},{8,6},{9,7},{10,8},{11,9},{12,... | collective-permute-start | bytes 786440 | tf_op jit(solution)/shard_map/ppermute | solution.py:523
  22.8 3.1 %shard_map.76 = (bf16[512,256]{1,0:T(8,128)(2,1)}, bf16[512,256]{1,0:T(8,128)(2,1)}) custom-call(s32[3]{0:T(128)} %pad_add_fusion.where, bf16[512,512]{1,0:T(8,128)(2,1)} %a_far.7, bf16[512,512]{1,0:T(8,128)(2,1)} %a_far.7, bf16[512,512]{1,0:T(8,128)(2,1)} %b_far.7, bf16[512,512]{1,0:T(8,128)(2,1)} %b_far.7), custom_call_target="tpu_custom_call" | custom-call | bytes 1048576 | tf_op jit(solution)/shard_map/pallas_call | solution.py:74
  28.1 2.0 %shard_map.77 = (bf16[512,256]{1,0:T(8,128)(2,1)}, bf16[512,256]{1,0:T(8,128)(2,1)}) custom-call(s32[3]{0:T(128)} %pad_add_fusion.where, bf16[512,256]{1,0:T(8,128)(2,1)} %get-tuple-element.34.own.kv_own, bf16[512,256]{1,0:T(8,128)(2,1)} %copy-done.3), custom_call_target="tpu_custom_call" | custom-call | bytes 1048576 | tf_op jit(solution)/shard_map/pallas_call | solution.py:117
  30.1 1.9 %collective-permute-start.2 = (bf16[512,256]{1,0:T(8,128)(2,1)}, bf16[512,256]{1,0:T(8,128)(2,1)S(1)}, u32[]{:S(2)}, u32[]{:S(2)}) collective-permute-start(bf16[512,256]{1,0:T(8,128)(2,1)} %get-tuple-element.38), channel_id=1, source_target_pairs={{0,2},{1,3},{2,4},{3,5},{4,6},{5,7},{6,8},{7,9},{8,10},{9,11},{10,... | collective-permute-start | bytes 786440 | tf_op jit(solution)/shard_map/ppermute | solution.py:522
  32.0 4.5 %collective-permute-start.3 = (bf16[512,256]{1,0:T(8,128)(2,1)}, bf16[512,256]{1,0:T(8,128)(2,1)S(1)}, u32[]{:S(2)}, u32[]{:S(2)}) collective-permute-start(bf16[512,256]{1,0:T(8,128)(2,1)} %get-tuple-element.39), channel_id=1, source_target_pairs={{2,0},{3,1},{4,2},{5,3},{6,4},{7,5},{8,6},{9,7},{10,8},{11,9},{12,... | collective-permute-start | bytes 786440 | tf_op jit(solution)/shard_map/ppermute | solution.py:523
  36.7 5.9 %shard_map.82 = (bf16[2,2,128,256]{3,2,1,0:T(8,128)(2,1)S(1)}, bf16[2,2,128,256]{3,2,1,0:T(8,128)(2,1)S(1)}, f32[1024,256]{1,0:T(8,128)S(1)}, bf16[512,256]{1,0:T(8,128)(2,1)S(1)}, bf16[512,256]{1,0:T(8,128)(2,1)S(1)}) custom-call(s32[3]{0:T(128)S(1)} %copy-done.10, bf16[512,256]{1,0:T(8,128)(2,1)S(1)} %copy-done.5, bf16[512,256]{1,0:T(8,128)(2,1)S(1)} %copy-done.7, ...), custom_call_target="tpu_custom_call" | custom-call | flops 2000000000 | bytes 1572864 | tf_op jit(solution)/shard_map/pallas_call | solution.py:383
  43.6 1.9 %collective-permute-start.12 = (bf16[512,256]{1,0:T(8,128)(2,1)S(1)}, bf16[512,256]{1,0:T(8,128)(2,1)S(1)}, u32[]{:S(2)}, u32[]{:S(2)}) collective-permute-start(bf16[512,256]{1,0:T(8,128)(2,1)S(1)} %get-tuple-element.57), channel_id=1, source_target_pairs={{0,2},{1,3},{2,4},{3,5},{4,6},{5,7},{6,8},{7,9},{8,10},{9,11},{10,... | collective-permute-start | bytes 786440 | tf_op jit(solution)/shard_map/ppermute | solution.py:527
  45.5 4.7 %collective-permute-start.13 = (bf16[512,256]{1,0:T(8,128)(2,1)S(1)}, bf16[512,256]{1,0:T(8,128)(2,1)S(1)}, u32[]{:S(2)}, u32[]{:S(2)}) collective-permute-start(bf16[512,256]{1,0:T(8,128)(2,1)S(1)} %get-tuple-element.58), channel_id=1, source_target_pairs={{2,0},{3,1},{4,2},{5,3},{6,4},{7,5},{8,6},{9,7},{10,8},{11,9},{12,... | collective-permute-start | bytes 786440 | tf_op jit(solution)/shard_map/ppermute | solution.py:528
  50.3 5.9 %shard_map.78 = (bf16[2,2,128,256]{3,2,1,0:T(8,128)(2,1)S(1)}, bf16[2,2,128,256]{3,2,1,0:T(8,128)(2,1)S(1)}, f32[1024,256]{1,0:T(8,128)S(1)}, bf16[512,256]{1,0:T(8,128)(2,1)S(1)}, bf16[512,256]{1,0:T(8,128)(2,1)S(1)}) custom-call(s32[3]{0:T(128)S(1)} %copy-done.10, bf16[512,256]{1,0:T(8,128)(2,1)S(1)} %copy-done.2, bf16[512,256]{1,0:T(8,128)(2,1)S(1)} %copy-done.4, ...), custom_call_target="tpu_custom_call" | custom-call | flops 2000000000 | bytes 1572864 | tf_op jit(solution)/shard_map/pallas_call | solution.py:383
  58.0 1.9 %collective-permute-start.10 = (bf16[512,256]{1,0:T(8,128)(2,1)S(1)}, bf16[512,256]{1,0:T(8,128)(2,1)S(1)}, u32[]{:S(2)}, u32[]{:S(2)}) collective-permute-start(bf16[512,256]{1,0:T(8,128)(2,1)S(1)} %get-tuple-element.53), channel_id=1, source_target_pairs={{0,2},{1,3},{2,4},{3,5},{4,6},{5,7},{6,8},{7,9},{8,10},{9,11},{10,... | collective-permute-start | bytes 786440 | tf_op jit(solution)/shard_map/ppermute | solution.py:527
  59.9 4.5 %collective-permute-start.11 = (bf16[512,256]{1,0:T(8,128)(2,1)S(1)}, bf16[512,256]{1,0:T(8,128)(2,1)S(1)}, u32[]{:S(2)}, u32[]{:S(2)}) collective-permute-start(bf16[512,256]{1,0:T(8,128)(2,1)S(1)} %get-tuple-element.54), channel_id=1, source_target_pairs={{2,0},{3,1},{4,2},{5,3},{6,4},{7,5},{8,6},{9,7},{10,8},{11,9},{12,... | collective-permute-start | bytes 786440 | tf_op jit(solution)/shard_map/ppermute | solution.py:528
  65.0 1.5 %collective-permute-start.8 = (bf16[2,2,128,256]{3,2,1,0:T(8,128)(2,1)S(1)}, bf16[2,2,128,256]{3,2,1,0:T(8,128)(2,1)S(1)}, u32[]{:S(2)}, u32[]{:S(2)}) collective-permute-start(bf16[2,2,128,256]{3,2,1,0:T(8,128)(2,1)S(1)} %get-tuple-element.48), channel_id=1, source_target_pairs={{0,1},{1,0},{2,3},{3,2},{4,5},{5,4},{6,7},{7,6},{8,9},{9,8},{10,11... | collective-permute-start | bytes 786440 | tf_op jit(solution)/shard_map/ppermute | solution.py:513
  67.3 2.3 %shard_map.85 = (bf16[512,256]{1,0:T(8,128)(2,1)}, bf16[512,256]{1,0:T(8,128)(2,1)}) custom-call(s32[3]{0:T(128)} %pad_add_fusion.where, f32[1024,256]{1,0:T(8,128)} %copy-done, bf16[512,256]{1,0:T(8,128)(2,1)} %copy-done.13, bf16[512,256]{1,0:T(8,128)(2,1)} %copy-done.15), custom_call_target="tpu_custom_call" | custom-call | bytes 2097152 | tf_op jit(solution)/shard_map/pallas_call | solution.py:455
  70.9 2.3 %shard_map.84 = (bf16[512,256]{1,0:T(8,128)(2,1)}, bf16[512,256]{1,0:T(8,128)(2,1)}) custom-call(s32[3]{0:T(128)} %pad_add_fusion.where, f32[1024,256]{1,0:T(8,128)} %copy-done.1, bf16[512,256]{1,0:T(8,128)(2,1)} %copy-done.18, bf16[512,256]{1,0:T(8,128)(2,1)} %copy-done.19), custom_call_target="tpu_custom_call" | custom-call | bytes 2097152 | tf_op jit(solution)/shard_map/pallas_call | solution.py:455
  74.6 4.7 %collective-permute-done.8.refs_2_ = bf16[2,2,128,256]{3,2,1,0:T(8,128)(2,1)S(1)} collective-permute-done((bf16[2,2,128,256]{3,2,1,0:T(8,128)(2,1)S(1)}, bf16[2,2,128,256]{3,2,1,0:T(8,128)(2,1)S(1)}, u32[]{:S(2)}, u32[]{:S(2)}) %collective-permute-start.8) | collective-permute-done | bytes 262176 | tf_op jit(solution)/shard_map/ppermute | solution.py:513
  80.1 2.9 %shard_map.83 = (bf16[512,512]{1,0:T(8,128)(2,1)}, bf16[512,512]{1,0:T(8,128)(2,1)}) custom-call(s32[3]{0:T(128)} %pad_add_fusion.where, bf16[2,2,128,256]{3,2,1,0:T(8,128)(2,1)} %copy-done.9, bf16[2,2,128,256]{3,2,1,0:T(8,128)(2,1)} %copy-done.8, bf16[2,2,128,256]{3,2,1,0:T(8,128)(2,1)} %copy-done.17, bf16[2,2,128,256]{3,2,1,0:T(8,128)(2,1)} %copy-done.14), custom_call_target="tpu_custom_call" | custom-call | bytes 2097152 | tf_op jit(solution)/shard_map/pallas_call | solution.py:492
  82.9 1.7 %collective-permute-done.15.refs_3_ = bf16[512,256]{1,0:T(8,128)(2,1)S(1)} collective-permute-done((bf16[512,256]{1,0:T(8,128)(2,1)}, bf16[512,256]{1,0:T(8,128)(2,1)S(1)}, u32[]{:S(2)}, u32[]{:S(2)}) %collective-permute-start.15) | collective-permute-done | bytes 262176 | tf_op jit(solution)/shard_map/ppermute | solution.py:513
  84.7 2.8 %collective-permute-done.14.refs_2_ = bf16[512,256]{1,0:T(8,128)(2,1)S(1)} collective-permute-done((bf16[512,256]{1,0:T(8,128)(2,1)}, bf16[512,256]{1,0:T(8,128)(2,1)S(1)}, u32[]{:S(2)}, u32[]{:S(2)}) %collective-permute-start.14) | collective-permute-done | bytes 262176 | tf_op jit(solution)/shard_map/ppermute | solution.py:513
  88.2 2.9 %shard_map.86 = (bf16[512,512]{1,0:T(8,128)(2,1)}, bf16[512,512]{1,0:T(8,128)(2,1)}) custom-call(s32[3]{0:T(128)} %pad_add_fusion.where, bf16[512,256]{1,0:T(8,128)(2,1)} %get-tuple-element.55.refs_0_, bf16[512,256]{1,0:T(8,128)(2,1)} %get-tuple-element.59.refs_1_, bf16[512,256]{1,0:T(8,128)(2,1)} %copy-done.20, bf16[512,256]{1,0:T(8,128)(2,1)} %copy-done.16), custom_call_target="tpu_custom_call" | custom-call | bytes 2097152 | tf_op jit(solution)/shard_map/pallas_call | solution.py:492
  (63 shorter events, 15.4 us)
Async XLA Ops:
  4.2 9.4 %collective-permute-start.4 = (bf16[512,256]{1,0:T(8,128)(2,1)}, bf16[512,256]{1,0:T(8,128)(2,1)S(1)}, u32[]{:S(2)}, u32[]{:S(2)}) collective-permute-start(bf16[512,256]{1,0:T(8,128)(2,1)} %get-tuple-element.42), channel_id=1, source_target_pairs={{0,1},{1,0},{2,3},{3,2},{4,5},{5,4},{6,7},{7,6},{8,9},{9,8},{10,11... | collective-permute-start | bytes 786440 | tf_op jit(solution)/shard_map/ppermute | solution.py:513
  8.6 18.7 %collective-permute-start = (bf16[512,256]{1,0:T(8,128)(2,1)}, bf16[512,256]{1,0:T(8,128)(2,1)S(1)}, u32[]{:S(2)}, u32[]{:S(2)}) collective-permute-start(bf16[512,256]{1,0:T(8,128)(2,1)} %get-tuple-element.35), channel_id=1, source_target_pairs={{0,1},{1,0},{2,3},{3,2},{4,5},{5,4},{6,7},{7,6},{8,9},{9,8},{10,11... | collective-permute-start | bytes 786440 | tf_op jit(solution)/shard_map/ppermute | solution.py:513
  12.1 19.9 %collective-permute-start.5 = (bf16[512,256]{1,0:T(8,128)(2,1)}, bf16[512,256]{1,0:T(8,128)(2,1)S(1)}, u32[]{:S(2)}, u32[]{:S(2)}) collective-permute-start(bf16[512,256]{1,0:T(8,128)(2,1)} %get-tuple-element.44), channel_id=1, source_target_pairs={{0,1},{1,0},{2,3},{3,2},{4,5},{5,4},{6,7},{7,6},{8,9},{9,8},{10,11... | collective-permute-start | bytes 786440 | tf_op jit(solution)/shard_map/ppermute | solution.py:513
  16.3 20.3 %collective-permute-start.6 = (bf16[512,256]{1,0:T(8,128)(2,1)}, bf16[512,256]{1,0:T(8,128)(2,1)S(1)}, u32[]{:S(2)}, u32[]{:S(2)}) collective-permute-start(bf16[512,256]{1,0:T(8,128)(2,1)} %get-tuple-element.45), channel_id=1, source_target_pairs={{0,2},{1,3},{2,4},{3,5},{4,6},{5,7},{6,8},{7,9},{8,10},{9,11},{10,... | collective-permute-start | bytes 786440 | tf_op jit(solution)/shard_map/ppermute | solution.py:522
  18.2 18.4 %collective-permute-start.7 = (bf16[512,256]{1,0:T(8,128)(2,1)}, bf16[512,256]{1,0:T(8,128)(2,1)S(1)}, u32[]{:S(2)}, u32[]{:S(2)}) collective-permute-start(bf16[512,256]{1,0:T(8,128)(2,1)} %get-tuple-element.46), channel_id=1, source_target_pairs={{2,0},{3,1},{4,2},{5,3},{6,4},{7,5},{8,6},{9,7},{10,8},{11,9},{12,... | collective-permute-start | bytes 786440 | tf_op jit(solution)/shard_map/ppermute | solution.py:523
  22.8 13.8 %copy-start.12 = (bf16[512,256]{1,0:T(8,128)(2,1)S(1)}, bf16[512,256]{1,0:T(8,128)(2,1)}, u32[]{:S(2)}) copy-start(bf16[512,256]{1,0:T(8,128)(2,1)} %get-tuple-element.43.qg_own) | copy-start | bytes 786436
  25.9 24.4 %collective-permute-start.1 = (bf16[512,256]{1,0:T(8,128)(2,1)}, bf16[512,256]{1,0:T(8,128)(2,1)S(1)}, u32[]{:S(2)}, u32[]{:S(2)}) collective-permute-start(bf16[512,256]{1,0:T(8,128)(2,1)} %get-tuple-element.37), channel_id=1, source_target_pairs={{0,1},{1,0},{2,3},{3,2},{4,5},{5,4},{6,7},{7,6},{8,9},{9,8},{10,11... | collective-permute-start | bytes 786440 | tf_op jit(solution)/shard_map/ppermute | solution.py:513
  28.1 8.6 %copy-start.5 = (bf16[512,256]{1,0:T(8,128)(2,1)S(1)}, bf16[512,256]{1,0:T(8,128)(2,1)}, u32[]{:S(2)}) copy-start(bf16[512,256]{1,0:T(8,128)(2,1)} %get-tuple-element.41.own.kv_own) | copy-start | bytes 786436
  28.1 8.6 %copy-start.7 = (bf16[512,256]{1,0:T(8,128)(2,1)S(1)}, bf16[512,256]{1,0:T(8,128)(2,1)}, u32[]{:S(2)}) copy-start(bf16[512,256]{1,0:T(8,128)(2,1)} %copy-done.6) | copy-start | bytes 786436
  30.1 20.2 %collective-permute-start.2 = (bf16[512,256]{1,0:T(8,128)(2,1)}, bf16[512,256]{1,0:T(8,128)(2,1)S(1)}, u32[]{:S(2)}, u32[]{:S(2)}) collective-permute-start(bf16[512,256]{1,0:T(8,128)(2,1)} %get-tuple-element.38), channel_id=1, source_target_pairs={{0,2},{1,3},{2,4},{3,5},{4,6},{5,7},{6,8},{7,9},{8,10},{9,11},{10,... | collective-permute-start | bytes 786440 | tf_op jit(solution)/shard_map/ppermute | solution.py:522
  32.0 18.2 %collective-permute-start.3 = (bf16[512,256]{1,0:T(8,128)(2,1)}, bf16[512,256]{1,0:T(8,128)(2,1)S(1)}, u32[]{:S(2)}, u32[]{:S(2)}) collective-permute-start(bf16[512,256]{1,0:T(8,128)(2,1)} %get-tuple-element.39), channel_id=1, source_target_pairs={{2,0},{3,1},{4,2},{5,3},{6,4},{7,5},{8,6},{9,7},{10,8},{11,9},{12,... | collective-permute-start | bytes 786440 | tf_op jit(solution)/shard_map/ppermute | solution.py:523
  36.7 13.7 %copy-start.2 = (bf16[512,256]{1,0:T(8,128)(2,1)S(1)}, bf16[512,256]{1,0:T(8,128)(2,1)}, u32[]{:S(2)}) copy-start(bf16[512,256]{1,0:T(8,128)(2,1)} %get-tuple-element.34.own.kv_own) | copy-start | bytes 786436
  36.7 13.6 %copy-start.4 = (bf16[512,256]{1,0:T(8,128)(2,1)S(1)}, bf16[512,256]{1,0:T(8,128)(2,1)}, u32[]{:S(2)}) copy-start(bf16[512,256]{1,0:T(8,128)(2,1)} %copy-done.3) | copy-start | bytes 786436
  36.7 13.6 %copy-start.11 = (bf16[512,256]{1,0:T(8,128)(2,1)S(1)}, bf16[512,256]{1,0:T(8,128)(2,1)}, u32[]{:S(2)}) copy-start(bf16[512,256]{1,0:T(8,128)(2,1)} %get-tuple-element.36.qg_own) | copy-start | bytes 786436
  43.6 12.7 %copy-start.8 = (bf16[2,2,128,256]{3,2,1,0:T(8,128)(2,1)}, bf16[2,2,128,256]{3,2,1,0:T(8,128)(2,1)S(1)}, u32[]{:S(2)}) copy-start(bf16[2,2,128,256]{3,2,1,0:T(8,128)(2,1)S(1)} %get-tuple-element.47.refs_1_) | copy-start | bytes 786436
  43.6 21.4 %collective-permute-start.12 = (bf16[512,256]{1,0:T(8,128)(2,1)S(1)}, bf16[512,256]{1,0:T(8,128)(2,1)S(1)}, u32[]{:S(2)}, u32[]{:S(2)}) collective-permute-start(bf16[512,256]{1,0:T(8,128)(2,1)S(1)} %get-tuple-element.57), channel_id=1, source_target_pairs={{0,2},{1,3},{2,4},{3,5},{4,6},{5,7},{6,8},{7,9},{8,10},{9,11},{10,... | collective-permute-start | bytes 786440 | tf_op jit(solution)/shard_map/ppermute | solution.py:527
  45.5 21.0 %collective-permute-start.13 = (bf16[512,256]{1,0:T(8,128)(2,1)S(1)}, bf16[512,256]{1,0:T(8,128)(2,1)S(1)}, u32[]{:S(2)}, u32[]{:S(2)}) collective-permute-start(bf16[512,256]{1,0:T(8,128)(2,1)S(1)} %get-tuple-element.58), channel_id=1, source_target_pairs={{2,0},{3,1},{4,2},{5,3},{6,4},{7,5},{8,6},{9,7},{10,8},{11,9},{12,... | collective-permute-start | bytes 786440 | tf_op jit(solution)/shard_map/ppermute | solution.py:528
  58.0 12.1 %collective-permute-start.10 = (bf16[512,256]{1,0:T(8,128)(2,1)S(1)}, bf16[512,256]{1,0:T(8,128)(2,1)S(1)}, u32[]{:S(2)}, u32[]{:S(2)}) collective-permute-start(bf16[512,256]{1,0:T(8,128)(2,1)S(1)} %get-tuple-element.53), channel_id=1, source_target_pairs={{0,2},{1,3},{2,4},{3,5},{4,6},{5,7},{6,8},{7,9},{8,10},{9,11},{10,... | collective-permute-start | bytes 786440 | tf_op jit(solution)/shard_map/ppermute | solution.py:527
  59.9 10.2 %collective-permute-start.11 = (bf16[512,256]{1,0:T(8,128)(2,1)S(1)}, bf16[512,256]{1,0:T(8,128)(2,1)S(1)}, u32[]{:S(2)}, u32[]{:S(2)}) collective-permute-start(bf16[512,256]{1,0:T(8,128)(2,1)S(1)} %get-tuple-element.54), channel_id=1, source_target_pairs={{2,0},{3,1},{4,2},{5,3},{6,4},{7,5},{8,6},{9,7},{10,8},{11,9},{12,... | collective-permute-start | bytes 786440 | tf_op jit(solution)/shard_map/ppermute | solution.py:528
  64.5 10.2 %collective-permute-start.9 = (bf16[2,2,128,256]{3,2,1,0:T(8,128)(2,1)S(1)}, bf16[2,2,128,256]{3,2,1,0:T(8,128)(2,1)S(1)}, u32[]{:S(2)}, u32[]{:S(2)}) collective-permute-start(bf16[2,2,128,256]{3,2,1,0:T(8,128)(2,1)S(1)} %get-tuple-element.49), channel_id=1, source_target_pairs={{0,1},{1,0},{2,3},{3,2},{4,5},{5,4},{6,7},{7,6},{8,9},{9,8},{10,11... | collective-permute-start | bytes 786440 | tf_op jit(solution)/shard_map/ppermute | solution.py:513
  65.0 14.3 %collective-permute-start.8 = (bf16[2,2,128,256]{3,2,1,0:T(8,128)(2,1)S(1)}, bf16[2,2,128,256]{3,2,1,0:T(8,128)(2,1)S(1)}, u32[]{:S(2)}, u32[]{:S(2)}) collective-permute-start(bf16[2,2,128,256]{3,2,1,0:T(8,128)(2,1)S(1)} %get-tuple-element.48), channel_id=1, source_target_pairs={{0,1},{1,0},{2,3},{3,2},{4,5},{5,4},{6,7},{7,6},{8,9},{9,8},{10,11... | collective-permute-start | bytes 786440 | tf_op jit(solution)/shard_map/ppermute | solution.py:513
  69.5 15.1 %collective-permute-start.15 = (bf16[512,256]{1,0:T(8,128)(2,1)}, bf16[512,256]{1,0:T(8,128)(2,1)S(1)}, u32[]{:S(2)}, u32[]{:S(2)}) collective-permute-start(bf16[512,256]{1,0:T(8,128)(2,1)} %get-tuple-element.61), channel_id=1, source_target_pairs={{0,1},{1,0},{2,3},{3,2},{4,5},{5,4},{6,7},{7,6},{8,9},{9,8},{10,11... | collective-permute-start | bytes 786440 | tf_op jit(solution)/shard_map/ppermute | solution.py:513
  73.1 14.3 %collective-permute-start.14 = (bf16[512,256]{1,0:T(8,128)(2,1)}, bf16[512,256]{1,0:T(8,128)(2,1)S(1)}, u32[]{:S(2)}, u32[]{:S(2)}) collective-permute-start(bf16[512,256]{1,0:T(8,128)(2,1)} %get-tuple-element.60), channel_id=1, source_target_pairs={{0,1},{1,0},{2,3},{3,2},{4,5},{5,4},{6,7},{7,6},{8,9},{9,8},{10,11... | collective-permute-start | bytes 786440 | tf_op jit(solution)/shard_map/ppermute | solution.py:513
  74.6 4.7 %copy-start.14 = (bf16[2,2,128,256]{3,2,1,0:T(8,128)(2,1)}, bf16[2,2,128,256]{3,2,1,0:T(8,128)(2,1)S(1)}, u32[]{:S(2)}) copy-start(bf16[2,2,128,256]{3,2,1,0:T(8,128)(2,1)S(1)} %collective-permute-done.9.refs_3_) | copy-start | bytes 786436
  (13 other events, 16.6 us)
where the time goes:
time: 91.6 us; the launch traced here: 91 us
  Pallas kernels  38 us (41%)
  starting transfers between devices  35.1 us (38%)
  waiting for transfers between devices  9.29 us (10%)
  local copies, waits for them, and re-layouts  7.03 us (8%)
  between operations  0.93 us (1%)
    ppermute x4, starting transfers between devices, on_device(): from_right = lax.ppermute(to_left, axes, leftward)  18.3 us
    pallas_call x2, Pallas kernels, main(): pl.pallas_call(main_kernel, in_specs=[smem()] + [vmem()] * 6, out_specs=[...  11.9 us
    pallas_call x4, Pallas kernels, pack(): pl.pallas_call(pack_kernel, grid_spec=pltpu.PrefetchScalarGridSpec(num_sc...  11.8 us
    ppermute x8, waiting for transfers between devices, swap(): return lax.ppermute(x, axes, across)  9.27 us
    ppermute x8, starting transfers between devices, swap(): return lax.ppermute(x, axes, across)  9.13 us
    ppermute x4, starting transfers between devices, on_device(): from_left = lax.ppermute(to_right, axes, rightward)  7.63 us
    unnamed x42, local copies, waits for them, and re-layouts  7.03 us
    pallas_call x2, Pallas kernels, unpack(): pl.pallas_call(kernel, in_specs=[smem()] + [vmem()] * (2 * CHUNKS), out_s...  5.73 us
  transfers between devices with their start and end apart: 16, of which 3 were waited for; matrix products, arithmetic and copies ran while one was open for 0% of the time, Pallas kernels for 35%

commit v1 on v0

--- a/solution.py
+++ b/solution.py
@@ -54,34 +54,64 @@
     return jnp.concatenate([x, x], axis=axis)
 
 
-def pack_kernel(where, a_own, a_far, b_own, b_far, own, far):
-    width = a_own.shape[1]
+def pack_kernel(where, a, b, *refs):
+    outs, held, sems = refs[: 2 * CHUNKS], refs[2 * CHUNKS], refs[2 * CHUNKS + 1]
+    rows, columns = a.shape
+    half = columns // 2
+    width = half // CHUNKS
+    copies = []
+    for n, side in enumerate((1 - where[0], where[0])):
+        at = pl.ds(pl.multiple_of(side * half, half), half)
+        for m, ref in enumerate((a, b)):
+            copies.append(
+                pltpu.make_async_copy(ref.at[:, at], held.at[2 * n + m], sems.at[2 * n + m])
+            )
+            copies[-1].start()
     order = order_matrix(False)
-    for i in range(a_own.shape[0] // PARENT):
-        rows = slice(i * PARENT, (i + 1) * PARENT)
-        own[rows, :width] = dot_nn(order, a_own[rows, :]).astype(BF)
-        own[rows, width:] = dot_nn(order, b_own[rows, :]).astype(BF)
-        far[rows, :width] = dot_nn(order, a_far[rows, :]).astype(BF)
-        far[rows, width:] = dot_nn(order, b_far[rows, :]).astype(BF)
-
-
-def pack(where, a, b, chunk):
+    for n in range(2):
+        own = n == 1
+        for m in range(2):
+            copies[2 * n + m].wait()
+            for i in range(rows // PARENT):
+                at = slice(i * PARENT, (i + 1) * PARENT)
+                x = dot_nn(order, held[2 * n + m, at, :]).astype(BF)
+                for c in range(CHUNKS):
+                    ref = outs[c] if own else outs[CHUNKS + c]
+                    ref[at, m * width : (m + 1) * width] = x[:, c * width : (c + 1) * width]
+
+
+def pack(where, a, b):
     rows, columns = a.shape
-    width = columns // 2 // CHUNKS
-    near = pl.BlockSpec((rows, width), lambda i, w: (0, w[0] * CHUNKS + chunk))
-    away = pl.BlockSpec((rows, width), lambda i, w: (0, (1 - w[0]) * CHUNKS + chunk))
-    out = pl.BlockSpec((rows, 2 * width), lambda i, w: (0, 0))
-    return pl.pallas_call(
+    out = jax.ShapeDtypeStruct((rows, columns // CHUNKS), BF)
+    outs = pl.pallas_call(
         pack_kernel,
-        grid_spec=pltpu.PrefetchScalarGridSpec(
-            num_scalar_prefetch=1,
-            grid=(1,),
-            in_specs=[near, away, near, away],
-            out_specs=[out, out],
-        ),
-        out_shape=[jax.ShapeDtypeStruct((rows, 2 * width), BF)] * 2,
-        cost_estimate=pl.CostEstimate(flops=0, bytes_accessed=8 * rows * width * 2, transcendentals=0),
-    )(where, a, a, b, b)
+        in_specs=[smem(), pl.BlockSpec(memory_space=pl.ANY), pl.BlockSpec(memory_space=pl.ANY)],
+        out_specs=[vmem()] * (2 * CHUNKS),
+        out_shape=[out] * (2 * CHUNKS),
+        scratch_shapes=[
+            pltpu.VMEM((4, rows, columns // 2), BF),
+            pltpu.SemaphoreType.DMA((4,)),
+        ],
+        compiler_params=small(),
+        cost_estimate=light(),
+    )(where, a, b)
+    return outs[:CHUNKS], outs[CHUNKS:]
+
+
+def smem():
+    return pl.BlockSpec(memory_space=pltpu.SMEM)
+
+
+def vmem():
+    return pl.BlockSpec(memory_space=pltpu.VMEM)
+
+
+def small():
+    return pltpu.CompilerParams(vmem_limit_bytes=8 * 1024 * 1024)
+
+
+def light():
+    return pl.CostEstimate(flops=1000, bytes_accessed=1000, transcendentals=0)
 
 
 def halo_kernel(where, own, got, to_right, to_left):
@@ -104,14 +134,6 @@
         fill(got, own)
 
 
-def smem():
-    return pl.BlockSpec(memory_space=pltpu.SMEM)
-
-
-def vmem():
-    return pl.BlockSpec(memory_space=pltpu.VMEM)
-
-
 def halo(where, own, got):
     shape = jax.ShapeDtypeStruct(own.shape, BF)
     return pl.pallas_call(
@@ -119,7 +141,8 @@
         in_specs=[smem(), vmem(), vmem()],
         out_specs=[vmem(), vmem()],
         out_shape=[shape, shape],
-        cost_estimate=pl.CostEstimate(flops=0, bytes_accessed=4 * own.size * 2, transcendentals=0),
+        compiler_params=small(),
+        cost_estimate=light(),
     )(where, own, got)
 
 
@@ -408,10 +431,8 @@
             pltpu.VMEM((2, 512, HEAD), F32),
             pltpu.VMEM((4, 2, width, PARENT), BF),
         ],
-        compiler_params=pltpu.CompilerParams(vmem_limit_bytes=32 * 1024 * 1024),
-        cost_estimate=pl.CostEstimate(
-            flops=4_000_000_000 // CHUNKS, bytes_accessed=6 * 512 * both * 2, transcendentals=1_000_000
-        ),
+        compiler_params=pltpu.CompilerParams(vmem_limit_bytes=24 * 1024 * 1024),
+        cost_estimate=light(),
     )(where, kv_own, kv_got, qg_own, qg_got, from_left, from_right)
 
 
@@ -457,7 +478,8 @@
         in_specs=[smem(), vmem(), vmem(), vmem()],
         out_specs=[vmem(), vmem()],
         out_shape=[shape, shape],
-        cost_estimate=pl.CostEstimate(flops=0, bytes_accessed=grad.size * 8, transcendentals=0),
+        compiler_params=small(),
+        cost_estimate=light(),
     )(where, grad, from_left, from_right)
 
 
@@ -494,7 +516,8 @@
         in_specs=[smem()] + [vmem()] * (2 * CHUNKS),
         out_specs=[vmem(), vmem()],
         out_shape=[out, out],
-        cost_estimate=pl.CostEstimate(flops=0, bytes_accessed=shape[0] * shape[1] * 8, transcendentals=0),
+        compiler_params=small(),
+        cost_estimate=light(),
     )(where, *own, *got)
 
 
@@ -512,23 +535,27 @@
     def swap(x):
         return lax.ppermute(x, axes, across)
 
-    kv = [pack(where, key_matrix, value_matrix, c) for c in range(CHUNKS)]
-    qg = [pack(where, queries, cotangent, c) for c in range(CHUNKS)]
+    kv, kv_far = pack(where, key_matrix, value_matrix)
+    qg, qg_far = pack(where, queries, cotangent)
     oq_own, oq_got, kv_own, kv_got = [], [], [], []
+    back = []
     for c in range(CHUNKS):
-        got_kv = swap(kv[c][1])
-        got_qg = swap(qg[c][1])
-        to_right, to_left = halo(where, kv[c][0], got_kv)
+        got_kv = swap(kv_far[c])
+        got_qg = swap(qg_far[c])
+        to_right, to_left = halo(where, kv[c], got_kv)
         from_left = lax.ppermute(to_right, axes, rightward)
         from_right = lax.ppermute(to_left, axes, leftward)
-        own, far, grad, to_left, to_right = main(
-            where, kv[c][0], got_kv, qg[c][0], got_qg, from_left, from_right
-        )
+        inputs = (kv[c], got_kv, qg[c], got_qg, from_left, from_right)
+        if c > 0:
+            oq_got[c - 1], inputs = lax.optimization_barrier((oq_got[c - 1], inputs))
+        own, far, grad, to_left, to_right = main(where, *inputs)
+        oq_own.append(own)
+        oq_got.append(swap(far))
         from_left = lax.ppermute(to_right, axes, rightward)
         from_right = lax.ppermute(to_left, axes, leftward)
-        oq_own.append(own)
-        oq_got.append(swap(far))
-        own, far = join(where, grad, from_left, from_right)
+        back.append((grad, from_left, from_right))
+    for c in range(CHUNKS):
+        own, far = join(where, *back[c])
         kv_own.append(own)
         kv_got.append(swap(far))
     attended, query_grad = unpack(unpack_columns_kernel, where, oq_own, oq_got, queries.shape)

time: 91.6 us -> 77.2 us (0.84)
  the two profiles are of different devices: /device:TPU:8 before, /device:TPU:12 now
where the time goes in v1:
time: 77.2 us; the launch traced here: 76.7 us
  starting transfers between devices  31.1 us (40%)
  Pallas kernels  22.2 us (29%)
  waiting for transfers between devices  20.3 us (26%)
  local copies, waits for them, and re-layouts  2.09 us (3%)
  between operations  0.84 us (1%)
    ppermute x8, waiting for transfers between devices, swap(): return lax.ppermute(x, axes, across)  19.2 us
    ppermute x4, starting transfers between devices, on_device(): from_right = lax.ppermute(to_left, axes, leftward)  13.5 us
    pallas_call x2, Pallas kernels, main(): pl.pallas_call(main_kernel, in_specs=[smem()] + [vmem()] * 6, out_specs=[...  11.9 us
    ppermute x8, starting transfers between devices, swap(): return lax.ppermute(x, axes, across)  9.52 us
    ppermute x4, starting transfers between devices, on_device(): from_left = lax.ppermute(to_right, axes, rightward)  8.13 us
    pallas_call x2, Pallas kernels, unpack(): pl.pallas_call(kernel, in_specs=[smem()] + [vmem()] * (2 * CHUNKS), out_s...  4.42 us
    pallas_call x2, Pallas kernels, pack(): pl.pallas_call(pack_kernel, in_specs=[smem(), pl.BlockSpec(memory_space=p...  3.28 us
    unnamed x8, local copies, waits for them, and re-layouts  2.09 us
  transfers between devices with their start and end apart: 16, of which 6 were waited for; matrix products, arithmetic and copies ran while one was open for 0% of the time, Pallas kernels for 24%

profile of v1, /device:TPU:12, one launch (start us, length us, event | category | flops | bytes accessed | tf_op | source)
XLA Modules:
  0.0 76.7 jit_solution(9143293597970981838)
XLA Ops:
  2.8 1.6 %shard_map.75 = (bf16[512,256]{1,0:T(8,128)(2,1)S(1)}, bf16[512,256]{1,0:T(8,128)(2,1)S(1)}, bf16[512,256]{1,0:T(8,128)(2,1)S(1)}, bf16[512,256]{1,0:T(8,128)(2,1)S(1)}) custom-call(s32[3]{0:T(128)S(1)} %pad_add_fusion.where, bf16[512,512]{1,0:T(8,128)(2,1)S(1)} %copy-done, bf16[512,512]{1,0:T(8,128)(2,1)S(1)} %copy-done.1), custom_call_target="tpu_custom_call" | custom-call | flops 1000 | bytes 1000 | tf_op jit(solution)/shard_map/pallas_call | solution.py:86
  4.4 1.6 %collective-permute-start = (bf16[512,256]{1,0:T(8,128)(2,1)S(1)}, bf16[512,256]{1,0:T(8,128)(2,1)S(1)}, u32[]{:S(2)}, u32[]{:S(2)}) collective-permute-start(bf16[512,256]{1,0:T(8,128)(2,1)S(1)} %get-tuple-element.42), channel_id=1, source_target_pairs={{0,1},{1,0},{2,3},{3,2},{4,5},{5,4},{6,7},{7,6},{8,9},{9,8},{10,11... | collective-permute-start | bytes 786440 | tf_op jit(solution)/shard_map/ppermute | solution.py:536
  6.5 1.7 %shard_map.76 = (bf16[512,256]{1,0:T(8,128)(2,1)S(1)}, bf16[512,256]{1,0:T(8,128)(2,1)S(1)}, bf16[512,256]{1,0:T(8,128)(2,1)S(1)}, bf16[512,256]{1,0:T(8,128)(2,1)S(1)}) custom-call(s32[3]{0:T(128)S(1)} %pad_add_fusion.where, bf16[512,512]{1,0:T(8,128)(2,1)S(1)} %copy-done.2, bf16[512,512]{1,0:T(8,128)(2,1)S(1)} %copy-done.3), custom_call_target="tpu_custom_call" | custom-call | flops 1000 | bytes 1000 | tf_op jit(solution)/shard_map/pallas_call | solution.py:86
  8.2 1.6 %collective-permute-start.1 = (bf16[512,256]{1,0:T(8,128)(2,1)S(1)}, bf16[512,256]{1,0:T(8,128)(2,1)S(1)}, u32[]{:S(2)}, u32[]{:S(2)}) collective-permute-start(bf16[512,256]{1,0:T(8,128)(2,1)S(1)} %get-tuple-element.44), channel_id=1, source_target_pairs={{0,1},{1,0},{2,3},{3,2},{4,5},{5,4},{6,7},{7,6},{8,9},{9,8},{10,11... | collective-permute-start | bytes 786440 | tf_op jit(solution)/shard_map/ppermute | solution.py:536
  9.8 3.9 %collective-permute-done.got.kv_got = bf16[512,256]{1,0:T(8,128)(2,1)S(1)} collective-permute-done((bf16[512,256]{1,0:T(8,128)(2,1)S(1)}, bf16[512,256]{1,0:T(8,128)(2,1)S(1)}, u32[]{:S(2)}, u32[]{:S(2)}) %collective-permute-start) | collective-permute-done | bytes 262176 | tf_op jit(solution)/shard_map/ppermute | solution.py:536
  14.4 1.9 %collective-permute-start.2 = (bf16[512,256]{1,0:T(8,128)(2,1)S(1)}, bf16[512,256]{1,0:T(8,128)(2,1)S(1)}, u32[]{:S(2)}, u32[]{:S(2)}) collective-permute-start(bf16[512,256]{1,0:T(8,128)(2,1)S(1)} %get-tuple-element.45), channel_id=1, source_target_pairs={{0,2},{1,3},{2,4},{3,5},{4,6},{5,7},{6,8},{7,9},{8,10},{9,11},{10,... | collective-permute-start | bytes 786440 | tf_op jit(solution)/shard_map/ppermute | solution.py:546
  16.3 3.6 %collective-permute-start.3 = (bf16[512,256]{1,0:T(8,128)(2,1)S(1)}, bf16[512,256]{1,0:T(8,128)(2,1)S(1)}, u32[]{:S(2)}, u32[]{:S(2)}) collective-permute-start(bf16[512,256]{1,0:T(8,128)(2,1)S(1)} %get-tuple-element.46), channel_id=1, source_target_pairs={{2,0},{3,1},{4,2},{5,3},{6,4},{7,5},{8,6},{9,7},{10,8},{11,9},{12,... | collective-permute-start | bytes 786440 | tf_op jit(solution)/shard_map/ppermute | solution.py:547
  20.0 1.6 %collective-permute-start.6 = (bf16[512,256]{1,0:T(8,128)(2,1)S(1)}, bf16[512,256]{1,0:T(8,128)(2,1)S(1)}, u32[]{:S(2)}, u32[]{:S(2)}) collective-permute-start(bf16[512,256]{1,0:T(8,128)(2,1)S(1)} %get-tuple-element.52), channel_id=1, source_target_pairs={{0,1},{1,0},{2,3},{3,2},{4,5},{5,4},{6,7},{7,6},{8,9},{9,8},{10,11... | collective-permute-start | bytes 786440 | tf_op jit(solution)/shard_map/ppermute | solution.py:536
  22.2 1.9 %collective-permute-start.7 = (bf16[512,256]{1,0:T(8,128)(2,1)S(1)}, bf16[512,256]{1,0:T(8,128)(2,1)S(1)}, u32[]{:S(2)}, u32[]{:S(2)}) collective-permute-start(bf16[512,256]{1,0:T(8,128)(2,1)S(1)} %get-tuple-element.53), channel_id=1, source_target_pairs={{0,2},{1,3},{2,4},{3,5},{4,6},{5,7},{6,8},{7,9},{8,10},{9,11},{10,... | collective-permute-start | bytes 786440 | tf_op jit(solution)/shard_map/ppermute | solution.py:546
  24.9 2.8 %collective-permute-start.8 = (bf16[512,256]{1,0:T(8,128)(2,1)S(1)}, bf16[512,256]{1,0:T(8,128)(2,1)S(1)}, u32[]{:S(2)}, u32[]{:S(2)}) collective-permute-start(bf16[512,256]{1,0:T(8,128)(2,1)S(1)} %get-tuple-element.54), channel_id=1, source_target_pairs={{2,0},{3,1},{4,2},{5,3},{6,4},{7,5},{8,6},{9,7},{10,8},{11,9},{12,... | collective-permute-start | bytes 786440 | tf_op jit(solution)/shard_map/ppermute | solution.py:547
  27.8 5.9 %shard_map.78 = (bf16[2,2,128,256]{3,2,1,0:T(8,128)(2,1)S(1)}, bf16[2,2,128,256]{3,2,1,0:T(8,128)(2,1)S(1)}, f32[1024,256]{1,0:T(8,128)S(1)}, bf16[512,256]{1,0:T(8,128)(2,1)S(1)}, bf16[512,256]{1,0:T(8,128)(2,1)S(1)}) custom-call(s32[3]{0:T(128)S(1)} %pad_add_fusion.where, bf16[512,256]{1,0:T(8,128)(2,1)S(1)} %get-tuple-element.41.own.kv_own, ...), custom_call_target="tpu_custom_call" | custom-call | flops 1000 | bytes 1000 | tf_op jit(solution)/shard_map/pallas_call | solution.py:406
  34.4 2.4 %collective-permute-start.10 = (bf16[512,256]{1,0:T(8,128)(2,1)S(1)}, bf16[512,256]{1,0:T(8,128)(2,1)S(1)}, u32[]{:S(2)}, u32[]{:S(2)}) collective-permute-start(bf16[512,256]{1,0:T(8,128)(2,1)S(1)} %get-tuple-element.67), channel_id=1, source_target_pairs={{0,2},{1,3},{2,4},{3,5},{4,6},{5,7},{6,8},{7,9},{8,10},{9,11},{10,... | collective-permute-start | bytes 786440 | tf_op jit(solution)/shard_map/ppermute | solution.py:554
  36.8 3.4 %collective-permute-start.11 = (bf16[512,256]{1,0:T(8,128)(2,1)S(1)}, bf16[512,256]{1,0:T(8,128)(2,1)S(1)}, u32[]{:S(2)}, u32[]{:S(2)}) collective-permute-start(bf16[512,256]{1,0:T(8,128)(2,1)S(1)} %get-tuple-element.68), channel_id=1, source_target_pairs={{2,0},{3,1},{4,2},{5,3},{6,4},{7,5},{8,6},{9,7},{10,8},{11,9},{12,... | collective-permute-start | bytes 786440 | tf_op jit(solution)/shard_map/ppermute | solution.py:555
  40.2 2.6 %collective-permute-done.4.refs_2_ = bf16[2,2,128,256]{3,2,1,0:T(8,128)(2,1)S(1)} collective-permute-done((bf16[2,2,128,256]{3,2,1,0:T(8,128)(2,1)S(1)}, bf16[2,2,128,256]{3,2,1,0:T(8,128)(2,1)S(1)}, u32[]{:S(2)}, u32[]{:S(2)}) %collective-permute-start.4) | collective-permute-done | bytes 262176 | tf_op jit(solution)/shard_map/ppermute | solution.py:536
  42.8 5.9 %shard_map.80 = (bf16[2,2,128,256]{3,2,1,0:T(8,128)(2,1)S(1)}, bf16[2,2,128,256]{3,2,1,0:T(8,128)(2,1)S(1)}, f32[1024,256]{1,0:T(8,128)S(1)}, bf16[512,256]{1,0:T(8,128)(2,1)S(1)}, bf16[512,256]{1,0:T(8,128)(2,1)S(1)}) custom-call(s32[3]{0:T(128)S(1)} %pad_add_fusion.where, bf16[512,256]{1,0:T(8,128)(2,1)S(1)} %get-tuple-element.55.own.kv_own, ...), custom_call_target="tpu_custom_call" | custom-call | flops 1000 | bytes 1000 | tf_op jit(solution)/shard_map/pallas_call | solution.py:406
  48.7 1.9 %collective-permute-start.12 = (bf16[512,256]{1,0:T(8,128)(2,1)S(1)}, bf16[512,256]{1,0:T(8,128)(2,1)S(1)}, u32[]{:S(2)}, u32[]{:S(2)}) collective-permute-start(bf16[512,256]{1,0:T(8,128)(2,1)S(1)} %get-tuple-element.71), channel_id=1, source_target_pairs={{0,2},{1,3},{2,4},{3,5},{4,6},{5,7},{6,8},{7,9},{8,10},{9,11},{10,... | collective-permute-start | bytes 786440 | tf_op jit(solution)/shard_map/ppermute | solution.py:554
  50.7 3.6 %collective-permute-start.13 = (bf16[512,256]{1,0:T(8,128)(2,1)S(1)}, bf16[512,256]{1,0:T(8,128)(2,1)S(1)}, u32[]{:S(2)}, u32[]{:S(2)}) collective-permute-start(bf16[512,256]{1,0:T(8,128)(2,1)S(1)} %get-tuple-element.72), channel_id=1, source_target_pairs={{2,0},{3,1},{4,2},{5,3},{6,4},{7,5},{8,6},{9,7},{10,8},{11,9},{12,... | collective-permute-start | bytes 786440 | tf_op jit(solution)/shard_map/ppermute | solution.py:555
  55.6 1.5 %collective-permute-start.9 = (bf16[2,2,128,256]{3,2,1,0:T(8,128)(2,1)S(1)}, bf16[2,2,128,256]{3,2,1,0:T(8,128)(2,1)S(1)}, u32[]{:S(2)}, u32[]{:S(2)}) collective-permute-start(bf16[2,2,128,256]{3,2,1,0:T(8,128)(2,1)S(1)} %get-tuple-element.63), channel_id=1, source_target_pairs={{0,1},{1,0},{2,3},{3,2},{4,5},{5,4},{6,7},{7,6},{8,9},{9,8},{10,11... | collective-permute-start | bytes 786440 | tf_op jit(solution)/shard_map/ppermute | solution.py:536
  57.1 1.1 %collective-permute-done.13.from_right = bf16[512,256]{1,0:T(8,128)(2,1)S(1)} collective-permute-done((bf16[512,256]{1,0:T(8,128)(2,1)S(1)}, bf16[512,256]{1,0:T(8,128)(2,1)S(1)}, u32[]{:S(2)}, u32[]{:S(2)}) %collective-permute-start.13) | collective-permute-done | bytes 262176 | tf_op jit(solution)/shard_map/ppermute | solution.py:555
  58.9 1.6 %collective-permute-start.15 = (bf16[512,256]{1,0:T(8,128)(2,1)S(1)}, bf16[512,256]{1,0:T(8,128)(2,1)S(1)}, u32[]{:S(2)}, u32[]{:S(2)}) collective-permute-start(bf16[512,256]{1,0:T(8,128)(2,1)S(1)} %get-tuple-element.75), channel_id=1, source_target_pairs={{0,1},{1,0},{2,3},{3,2},{4,5},{5,4},{6,7},{7,6},{8,9},{9,8},{10,11... | collective-permute-start | bytes 786440 | tf_op jit(solution)/shard_map/ppermute | solution.py:536
  60.4 9.5 %collective-permute-done.9.refs_3_ = bf16[2,2,128,256]{3,2,1,0:T(8,128)(2,1)S(1)} collective-permute-done((bf16[2,2,128,256]{3,2,1,0:T(8,128)(2,1)S(1)}, bf16[2,2,128,256]{3,2,1,0:T(8,128)(2,1)S(1)}, u32[]{:S(2)}, u32[]{:S(2)}) %collective-permute-start.9) | collective-permute-done | bytes 262176 | tf_op jit(solution)/shard_map/ppermute | solution.py:536
  69.9 2.2 %shard_map.81 = (bf16[512,512]{1,0:T(8,128)(2,1)}, bf16[512,512]{1,0:T(8,128)(2,1)}) custom-call(s32[3]{0:T(128)S(1)} %pad_add_fusion.where, bf16[2,2,128,256]{3,2,1,0:T(8,128)(2,1)S(1)} %get-tuple-element.47.refs_0_, bf16[2,2,128,256]{3,2,1,0:T(8,128)(2,1)S(1)} %get-tuple-element.61.refs_1_, bf16[2,2,128,256]{3,2,1,0:T(8,128)(2,1)S(1)} %collective-permute-done.4.refs_2_, ...), custom_call_target="tpu_custom_call" | custom-call | flops 1000 | bytes 1000 | tf_op jit(solution)/shard_map/pallas_call | solution.py:514
  72.1 2.4 %collective-permute-done.15.refs_3_ = bf16[512,256]{1,0:T(8,128)(2,1)S(1)} collective-permute-done((bf16[512,256]{1,0:T(8,128)(2,1)S(1)}, bf16[512,256]{1,0:T(8,128)(2,1)S(1)}, u32[]{:S(2)}, u32[]{:S(2)}) %collective-permute-start.15) | collective-permute-done | bytes 262176 | tf_op jit(solution)/shard_map/ppermute | solution.py:536
  74.5 2.2 %shard_map.84 = (bf16[512,512]{1,0:T(8,128)(2,1)}, bf16[512,512]{1,0:T(8,128)(2,1)}) custom-call(s32[3]{0:T(128)S(1)} %pad_add_fusion.where, bf16[512,256]{1,0:T(8,128)(2,1)S(1)} %get-tuple-element.69.refs_0_, bf16[512,256]{1,0:T(8,128)(2,1)S(1)} %get-tuple-element.73.refs_1_, bf16[512,256]{1,0:T(8,128)(2,1)S(1)} %collective-permute-done.14.refs_2_, ...), custom_call_target="tpu_custom_call" | custom-call | flops 1000 | bytes 1000 | tf_op jit(solution)/shard_map/pallas_call | solution.py:514
  (27 shorter events, 7.4 us)
Async XLA Ops:
  0.7 1.0 %copy-start = (bf16[512,512]{1,0:T(8,128)(2,1)S(1)}, bf16[512,512]{1,0:T(8,128)(2,1)}, u32[]{:S(2)}) copy-start(bf16[512,512]{1,0:T(8,128)(2,1)} %a.2) | copy-start | bytes 1572868
  1.8 1.0 %copy-start.1 = (bf16[512,512]{1,0:T(8,128)(2,1)S(1)}, bf16[512,512]{1,0:T(8,128)(2,1)}, u32[]{:S(2)}) copy-start(bf16[512,512]{1,0:T(8,128)(2,1)} %b.2) | copy-start | bytes 1572868
  2.8 3.7 %copy-start.2 = (bf16[512,512]{1,0:T(8,128)(2,1)S(1)}, bf16[512,512]{1,0:T(8,128)(2,1)}, u32[]{:S(2)}) copy-start(bf16[512,512]{1,0:T(8,128)(2,1)} %a.3) | copy-start | bytes 1572868
  2.8 3.7 %copy-start.3 = (bf16[512,512]{1,0:T(8,128)(2,1)S(1)}, bf16[512,512]{1,0:T(8,128)(2,1)}, u32[]{:S(2)}) copy-start(bf16[512,512]{1,0:T(8,128)(2,1)} %b.3) | copy-start | bytes 1572868
  4.4 9.3 %collective-permute-start = (bf16[512,256]{1,0:T(8,128)(2,1)S(1)}, bf16[512,256]{1,0:T(8,128)(2,1)S(1)}, u32[]{:S(2)}, u32[]{:S(2)}) collective-permute-start(bf16[512,256]{1,0:T(8,128)(2,1)S(1)} %get-tuple-element.42), channel_id=1, source_target_pairs={{0,1},{1,0},{2,3},{3,2},{4,5},{5,4},{6,7},{7,6},{8,9},{9,8},{10,11... | collective-permute-start | bytes 786440 | tf_op jit(solution)/shard_map/ppermute | solution.py:536
  6.0 15.5 %collective-permute-start.5 = (bf16[512,256]{1,0:T(8,128)(2,1)S(1)}, bf16[512,256]{1,0:T(8,128)(2,1)S(1)}, u32[]{:S(2)}, u32[]{:S(2)}) collective-permute-start(bf16[512,256]{1,0:T(8,128)(2,1)S(1)} %get-tuple-element.50), channel_id=1, source_target_pairs={{0,1},{1,0},{2,3},{3,2},{4,5},{5,4},{6,7},{7,6},{8,9},{9,8},{10,11... | collective-permute-start | bytes 786440 | tf_op jit(solution)/shard_map/ppermute | solution.py:536
  8.2 16.7 %collective-permute-start.1 = (bf16[512,256]{1,0:T(8,128)(2,1)S(1)}, bf16[512,256]{1,0:T(8,128)(2,1)S(1)}, u32[]{:S(2)}, u32[]{:S(2)}) collective-permute-start(bf16[512,256]{1,0:T(8,128)(2,1)S(1)} %get-tuple-element.44), channel_id=1, source_target_pairs={{0,1},{1,0},{2,3},{3,2},{4,5},{5,4},{6,7},{7,6},{8,9},{9,8},{10,11... | collective-permute-start | bytes 786440 | tf_op jit(solution)/shard_map/ppermute | solution.py:536
  14.4 13.4 %collective-permute-start.2 = (bf16[512,256]{1,0:T(8,128)(2,1)S(1)}, bf16[512,256]{1,0:T(8,128)(2,1)S(1)}, u32[]{:S(2)}, u32[]{:S(2)}) collective-permute-start(bf16[512,256]{1,0:T(8,128)(2,1)S(1)} %get-tuple-element.45), channel_id=1, source_target_pairs={{0,2},{1,3},{2,4},{3,5},{4,6},{5,7},{6,8},{7,9},{8,10},{9,11},{10,... | collective-permute-start | bytes 786440 | tf_op jit(solution)/shard_map/ppermute | solution.py:546
  16.3 11.5 %collective-permute-start.3 = (bf16[512,256]{1,0:T(8,128)(2,1)S(1)}, bf16[512,256]{1,0:T(8,128)(2,1)S(1)}, u32[]{:S(2)}, u32[]{:S(2)}) collective-permute-start(bf16[512,256]{1,0:T(8,128)(2,1)S(1)} %get-tuple-element.46), channel_id=1, source_target_pairs={{2,0},{3,1},{4,2},{5,3},{6,4},{7,5},{8,6},{9,7},{10,8},{11,9},{12,... | collective-permute-start | bytes 786440 | tf_op jit(solution)/shard_map/ppermute | solution.py:547
  20.0 16.8 %collective-permute-start.6 = (bf16[512,256]{1,0:T(8,128)(2,1)S(1)}, bf16[512,256]{1,0:T(8,128)(2,1)S(1)}, u32[]{:S(2)}, u32[]{:S(2)}) collective-permute-start(bf16[512,256]{1,0:T(8,128)(2,1)S(1)} %get-tuple-element.52), channel_id=1, source_target_pairs={{0,1},{1,0},{2,3},{3,2},{4,5},{5,4},{6,7},{7,6},{8,9},{9,8},{10,11... | collective-permute-start | bytes 786440 | tf_op jit(solution)/shard_map/ppermute | solution.py:536
  22.2 18.0 %collective-permute-start.7 = (bf16[512,256]{1,0:T(8,128)(2,1)S(1)}, bf16[512,256]{1,0:T(8,128)(2,1)S(1)}, u32[]{:S(2)}, u32[]{:S(2)}) collective-permute-start(bf16[512,256]{1,0:T(8,128)(2,1)S(1)} %get-tuple-element.53), channel_id=1, source_target_pairs={{0,2},{1,3},{2,4},{3,5},{4,6},{5,7},{6,8},{7,9},{8,10},{9,11},{10,... | collective-permute-start | bytes 786440 | tf_op jit(solution)/shard_map/ppermute | solution.py:546
  24.9 15.2 %collective-permute-start.8 = (bf16[512,256]{1,0:T(8,128)(2,1)S(1)}, bf16[512,256]{1,0:T(8,128)(2,1)S(1)}, u32[]{:S(2)}, u32[]{:S(2)}) collective-permute-start(bf16[512,256]{1,0:T(8,128)(2,1)S(1)} %get-tuple-element.54), channel_id=1, source_target_pairs={{2,0},{3,1},{4,2},{5,3},{6,4},{7,5},{8,6},{9,7},{10,8},{11,9},{12,... | collective-permute-start | bytes 786440 | tf_op jit(solution)/shard_map/ppermute | solution.py:547
  33.7 9.1 %collective-permute-start.4 = (bf16[2,2,128,256]{3,2,1,0:T(8,128)(2,1)S(1)}, bf16[2,2,128,256]{3,2,1,0:T(8,128)(2,1)S(1)}, u32[]{:S(2)}, u32[]{:S(2)}) collective-permute-start(bf16[2,2,128,256]{3,2,1,0:T(8,128)(2,1)S(1)} %get-tuple-element.48), channel_id=1, source_target_pairs={{0,1},{1,0},{2,3},{3,2},{4,5},{5,4},{6,7},{7,6},{8,9},{9,8},{10,11... | collective-permute-start | bytes 786440 | tf_op jit(solution)/shard_map/ppermute | solution.py:536
  34.4 19.9 %collective-permute-start.10 = (bf16[512,256]{1,0:T(8,128)(2,1)S(1)}, bf16[512,256]{1,0:T(8,128)(2,1)S(1)}, u32[]{:S(2)}, u32[]{:S(2)}) collective-permute-start(bf16[512,256]{1,0:T(8,128)(2,1)S(1)} %get-tuple-element.67), channel_id=1, source_target_pairs={{0,2},{1,3},{2,4},{3,5},{4,6},{5,7},{6,8},{7,9},{8,10},{9,11},{10,... | collective-permute-start | bytes 786440 | tf_op jit(solution)/shard_map/ppermute | solution.py:554
  36.8 17.6 %collective-permute-start.11 = (bf16[512,256]{1,0:T(8,128)(2,1)S(1)}, bf16[512,256]{1,0:T(8,128)(2,1)S(1)}, u32[]{:S(2)}, u32[]{:S(2)}) collective-permute-start(bf16[512,256]{1,0:T(8,128)(2,1)S(1)} %get-tuple-element.68), channel_id=1, source_target_pairs={{2,0},{3,1},{4,2},{5,3},{6,4},{7,5},{8,6},{9,7},{10,8},{11,9},{12,... | collective-permute-start | bytes 786440 | tf_op jit(solution)/shard_map/ppermute | solution.py:555
  48.7 8.4 %collective-permute-start.12 = (bf16[512,256]{1,0:T(8,128)(2,1)S(1)}, bf16[512,256]{1,0:T(8,128)(2,1)S(1)}, u32[]{:S(2)}, u32[]{:S(2)}) collective-permute-start(bf16[512,256]{1,0:T(8,128)(2,1)S(1)} %get-tuple-element.71), channel_id=1, source_target_pairs={{0,2},{1,3},{2,4},{3,5},{4,6},{5,7},{6,8},{7,9},{8,10},{9,11},{10,... | collective-permute-start | bytes 786440 | tf_op jit(solution)/shard_map/ppermute | solution.py:554
  50.7 7.5 %collective-permute-start.13 = (bf16[512,256]{1,0:T(8,128)(2,1)S(1)}, bf16[512,256]{1,0:T(8,128)(2,1)S(1)}, u32[]{:S(2)}, u32[]{:S(2)}) collective-permute-start(bf16[512,256]{1,0:T(8,128)(2,1)S(1)} %get-tuple-element.72), channel_id=1, source_target_pairs={{2,0},{3,1},{4,2},{5,3},{6,4},{7,5},{8,6},{9,7},{10,8},{11,9},{12,... | collective-permute-start | bytes 786440 | tf_op jit(solution)/shard_map/ppermute | solution.py:555
  55.0 17.1 %collective-permute-start.14 = (bf16[512,256]{1,0:T(8,128)(2,1)S(1)}, bf16[512,256]{1,0:T(8,128)(2,1)S(1)}, u32[]{:S(2)}, u32[]{:S(2)}) collective-permute-start(bf16[512,256]{1,0:T(8,128)(2,1)S(1)} %get-tuple-element.74), channel_id=1, source_target_pairs={{0,1},{1,0},{2,3},{3,2},{4,5},{5,4},{6,7},{7,6},{8,9},{9,8},{10,11... | collective-permute-start | bytes 786440 | tf_op jit(solution)/shard_map/ppermute | solution.py:536
  55.6 14.3 %collective-permute-start.9 = (bf16[2,2,128,256]{3,2,1,0:T(8,128)(2,1)S(1)}, bf16[2,2,128,256]{3,2,1,0:T(8,128)(2,1)S(1)}, u32[]{:S(2)}, u32[]{:S(2)}) collective-permute-start(bf16[2,2,128,256]{3,2,1,0:T(8,128)(2,1)S(1)} %get-tuple-element.63), channel_id=1, source_target_pairs={{0,1},{1,0},{2,3},{3,2},{4,5},{5,4},{6,7},{7,6},{8,9},{9,8},{10,11... | collective-permute-start | bytes 786440 | tf_op jit(solution)/shard_map/ppermute | solution.py:536
  58.9 15.6 %collective-permute-start.15 = (bf16[512,256]{1,0:T(8,128)(2,1)S(1)}, bf16[512,256]{1,0:T(8,128)(2,1)S(1)}, u32[]{:S(2)}, u32[]{:S(2)}) collective-permute-start(bf16[512,256]{1,0:T(8,128)(2,1)S(1)} %get-tuple-element.75), channel_id=1, source_target_pairs={{0,1},{1,0},{2,3},{3,2},{4,5},{5,4},{6,7},{7,6},{8,9},{9,8},{10,11... | collective-permute-start | bytes 786440 | tf_op jit(solution)/shard_map/ppermute | solution.py:536

commit v2 on v1

--- a/solution.py
+++ b/solution.py
@@ -127,11 +127,11 @@
 
     @pl.when(where[0] == 0)
     def _():
-        fill(own, got)
+        fill(own, got.at[1])
 
     @pl.when(where[0] == 1)
     def _():
-        fill(got, own)
+        fill(got.at[0], own)
 
 
 def halo(where, own, got):
@@ -226,7 +226,7 @@
         for n, cols in ((0, kc), (1, vc)):
             raw[n, 0:256, :] = from_left[0:256, cols]
             raw[n, pl.ds(256 + own_at, 512), :] = kv_own[:, cols]
-            raw[n, pl.ds(256 + got_at, 512), :] = kv_got[:, cols]
+            raw[n, pl.ds(256 + got_at, 512), :] = kv_got[1 - side, :, cols]
             raw[n, 1280:1536, :] = from_right[0:256, cols]
             one[n, 0:128, :] = from_left[256:384, cols]
             for i in range(6):
@@ -250,9 +250,9 @@
                 rows = slice(i * BLOCK, (i + 1) * BLOCK)
                 two_t[n, :, rows] = two[n, rows, :].T
         qs[pl.ds(own_at, 512), :] = qg_own[:, kc]
-        qs[pl.ds(got_at, 512), :] = qg_got[:, kc]
+        qs[pl.ds(got_at, 512), :] = qg_got[1 - side, :, kc]
         gs[pl.ds(own_at, 512), :] = qg_own[:, vc]
-        gs[pl.ds(got_at, 512), :] = qg_got[:, vc]
+        gs[pl.ds(got_at, 512), :] = qg_got[1 - side, :, vc]
 
         def blocks(ref, n, which):
             return [ref[n, b * BLOCK : (b + 1) * BLOCK, :] for b in which]
@@ -488,7 +488,8 @@
     order = order_matrix(True)
     width = ins[0].shape[1] // 2
     for c in range(CHUNKS):
-        for ref, side in ((ins[c], where[0]), (ins[CHUNKS + c], 1 - where[0])):
+        got = ins[CHUNKS + c].at[1 - where[0]]
+        for ref, side in ((ins[c], where[0]), (got, 1 - where[0])):
             at = pl.ds(pl.multiple_of((side * CHUNKS + c) * width, width), width)
             for i in range(2):
                 rows = slice(i * PARENT, (i + 1) * PARENT)
@@ -501,7 +502,8 @@
     order = order_matrix(True)
     width = ins[0].shape[2]
     for c in range(CHUNKS):
-        for ref, side in ((ins[c], where[0]), (ins[CHUNKS + c], 1 - where[0])):
+        got = ins[CHUNKS + c].at[1 - where[0]]
+        for ref, side in ((ins[c], where[0]), (got, 1 - where[0])):
             at = pl.ds(pl.multiple_of((side * CHUNKS + c) * width, width), width)
             for i in range(2):
                 rows = slice(i * PARENT, (i + 1) * PARENT)
@@ -528,12 +530,14 @@
     where = jnp.stack(
         [device % 2, (device >= 2).astype(jnp.int32), (device < count - 2).astype(jnp.int32)]
     ).astype(jnp.int32)
-    across = [(i, i ^ 1) for i in range(count)]
     rightward = [(i, i + 2) for i in range(count - 2)]
     leftward = [(i + 2, i) for i in range(count - 2)]
 
+    inner = lax.axis_size("inner")
+    pairs = None if inner == 2 else [[i, i + 1] for i in range(0, inner, 2)]
+
     def swap(x):
-        return lax.ppermute(x, axes, across)
+        return lax.all_gather(x, "inner", axis_index_groups=pairs)
 
     kv, kv_far = pack(where, key_matrix, value_matrix)
     qg, qg_far = pack(where, queries, cotangent)

time: 77.2 us -> 117 us (1.52)
  blocking collectives: 0 us -> 68.9 us
  waiting for transfers between devices: 20.3 us -> 0.02 us
  starting transfers between devices: 31.1 us -> 22.3 us
    all_gather x0 -> x8, blocking collectives: none -> 68.9 us  [swap(): return lax.all_gather(x, 'inner', axis_index_groups=pairs)]
    ppermute x8 -> x0, waiting for transfers between devices: 19.2 us -> none  [swap(): return lax.ppermute(x, axes, across)]
    ppermute x8 -> x0, starting transfers between devices: 9.52 us -> none  [swap(): return lax.ppermute(x, axes, across)]
  transfers between devices with their start and end apart: 16 -> 8, of which waited for: 6 -> 0; matrix products, arithmetic and copies ran while one was open for 0% -> 0% of each run, Pallas kernels for 24% -> 15%
where the time goes in v2:
time: 117 us; the launch traced here: 116 us
  blocking collectives  68.9 us (59%)
  starting transfers between devices  22.3 us (19%)
  Pallas kernels  22.2 us (19%)
  local copies, waits for them, and re-layouts  2.09 us (2%)
    all_gather x8, blocking collectives, swap(): return lax.all_gather(x, 'inner', axis_index_groups=pairs)  68.9 us
    ppermute x4, starting transfers between devices, on_device(): from_right = lax.ppermute(to_left, axes, leftward)  14.6 us
    pallas_call x2, Pallas kernels, main(): pl.pallas_call(main_kernel, in_specs=[smem()] + [vmem()] * 6, out_specs=[...  11.8 us
    ppermute x4, starting transfers between devices, on_device(): from_left = lax.ppermute(to_right, axes, rightward)  7.68 us
    pallas_call x2, Pallas kernels, unpack(): pl.pallas_call(kernel, in_specs=[smem()] + [vmem()] * (2 * CHUNKS), out_s...  4.42 us
    pallas_call x2, Pallas kernels, pack(): pl.pallas_call(pack_kernel, in_specs=[smem(), pl.BlockSpec(memory_space=p...  3.27 us
  transfers between devices with their start and end apart: 8, of which 0 were waited for; matrix products, arithmetic and copies ran while one was open for 0% of the time, Pallas kernels for 15%

profile of v2, /device:TPU:12, one launch (start us, length us, event | category | flops | bytes accessed | tf_op | source)
XLA Modules:
  0.0 116.4 jit_solution(144905948429661436)
XLA Ops:
  0.7 1.0 copy-done
  1.8 1.0 copy-done.1
  2.8 1.6 %shard_map.75 = (bf16[512,256]{1,0:T(8,128)(2,1)S(1)}, bf16[512,256]{1,0:T(8,128)(2,1)S(1)}, bf16[512,256]{1,0:T(8,128)(2,1)S(1)}, bf16[512,256]{1,0:T(8,128)(2,1)S(1)}) custom-call(s32[3]{0:T(128)S(1)} %pad_add_fusion.where, bf16[512,512]{1,0:T(8,128)(2,1)S(1)} %copy-done, bf16[512,512]{1,0:T(8,128)(2,1)S(1)} %copy-done.1), custom_call_target="tpu_custom_call" | custom-call | flops 1000 | bytes 1000 | tf_op jit(solution)/shard_map/pallas_call | solution.py:86
  4.5 8.7 %all-gather.3 = bf16[1024,256]{1,0:T(8,128)(2,1)S(1)} all-gather(bf16[512,256]{1,0:T(8,128)(2,1)S(1)} %get-tuple-element.50), channel_id=5, replica_groups=mesh['outer'=16,'inner'=2] {'inner'}, dimensions={0}, use_global_device_ids=true | all-gather | bytes 786432 | tf_op jit(solution)/shard_map/all_gather | solution.py:540
  13.9 1.9 %collective-permute-start.2 = (bf16[512,256]{1,0:T(8,128)(2,1)S(1)}, bf16[512,256]{1,0:T(8,128)(2,1)S(1)}, u32[]{:S(2)}, u32[]{:S(2)}) collective-permute-start(bf16[512,256]{1,0:T(8,128)(2,1)S(1)} %get-tuple-element.53), channel_id=1, source_target_pairs={{0,2},{1,3},{2,4},{3,5},{4,6},{5,7},{6,8},{7,9},{8,10},{9,11},{10,... | collective-permute-start | bytes 786440 | tf_op jit(solution)/shard_map/ppermute | solution.py:550
  15.8 3.6 %collective-permute-start.3 = (bf16[512,256]{1,0:T(8,128)(2,1)S(1)}, bf16[512,256]{1,0:T(8,128)(2,1)S(1)}, u32[]{:S(2)}, u32[]{:S(2)}) collective-permute-start(bf16[512,256]{1,0:T(8,128)(2,1)S(1)} %get-tuple-element.54), channel_id=1, source_target_pairs={{2,0},{3,1},{4,2},{5,3},{6,4},{7,5},{8,6},{9,7},{10,8},{11,9},{12,... | collective-permute-start | bytes 786440 | tf_op jit(solution)/shard_map/ppermute | solution.py:551
  19.4 8.9 %all-gather = bf16[1024,256]{1,0:T(8,128)(2,1)S(1)} all-gather(bf16[512,256]{1,0:T(8,128)(2,1)S(1)} %get-tuple-element.42), channel_id=2, replica_groups=mesh['outer'=16,'inner'=2] {'inner'}, dimensions={0}, use_global_device_ids=true | all-gather | bytes 786432 | tf_op jit(solution)/shard_map/all_gather | solution.py:540
  29.0 1.9 %collective-permute-start = (bf16[512,256]{1,0:T(8,128)(2,1)S(1)}, bf16[512,256]{1,0:T(8,128)(2,1)S(1)}, u32[]{:S(2)}, u32[]{:S(2)}) collective-permute-start(bf16[512,256]{1,0:T(8,128)(2,1)S(1)} %get-tuple-element.45), channel_id=1, source_target_pairs={{0,2},{1,3},{2,4},{3,5},{4,6},{5,7},{6,8},{7,9},{8,10},{9,11},{10,... | collective-permute-start | bytes 786440 | tf_op jit(solution)/shard_map/ppermute | solution.py:550
  30.9 3.6 %collective-permute-start.1 = (bf16[512,256]{1,0:T(8,128)(2,1)S(1)}, bf16[512,256]{1,0:T(8,128)(2,1)S(1)}, u32[]{:S(2)}, u32[]{:S(2)}) collective-permute-start(bf16[512,256]{1,0:T(8,128)(2,1)S(1)} %get-tuple-element.46), channel_id=1, source_target_pairs={{2,0},{3,1},{4,2},{5,3},{6,4},{7,5},{8,6},{9,7},{10,8},{11,9},{12,... | collective-permute-start | bytes 786440 | tf_op jit(solution)/shard_map/ppermute | solution.py:551
  34.6 1.6 %shard_map.76 = (bf16[512,256]{1,0:T(8,128)(2,1)S(1)}, bf16[512,256]{1,0:T(8,128)(2,1)S(1)}, bf16[512,256]{1,0:T(8,128)(2,1)S(1)}, bf16[512,256]{1,0:T(8,128)(2,1)S(1)}) custom-call(s32[3]{0:T(128)S(1)} %pad_add_fusion.where, bf16[512,512]{1,0:T(8,128)(2,1)S(1)} %copy-done.2, bf16[512,512]{1,0:T(8,128)(2,1)S(1)} %copy-done.3), custom_call_target="tpu_custom_call" | custom-call | flops 1000 | bytes 1000 | tf_op jit(solution)/shard_map/pallas_call | solution.py:86
  36.3 8.8 %all-gather.1 = bf16[1024,256]{1,0:T(8,128)(2,1)S(1)} all-gather(bf16[512,256]{1,0:T(8,128)(2,1)S(1)} %get-tuple-element.44), channel_id=3, replica_groups=mesh['outer'=16,'inner'=2] {'inner'}, dimensions={0}, use_global_device_ids=true | all-gather | bytes 786432 | tf_op jit(solution)/shard_map/all_gather | solution.py:540
  45.1 7.9 %all-gather.4 = bf16[1024,256]{1,0:T(8,128)(2,1)S(1)} all-gather(bf16[512,256]{1,0:T(8,128)(2,1)S(1)} %get-tuple-element.52), channel_id=6, replica_groups=mesh['outer'=16,'inner'=2] {'inner'}, dimensions={0}, use_global_device_ids=true | all-gather | bytes 786432 | tf_op jit(solution)/shard_map/all_gather | solution.py:540
  53.0 5.9 %shard_map.78 = (bf16[2,2,128,256]{3,2,1,0:T(8,128)(2,1)S(1)}, bf16[2,2,128,256]{3,2,1,0:T(8,128)(2,1)S(1)}, f32[1024,256]{1,0:T(8,128)S(1)}, bf16[512,256]{1,0:T(8,128)(2,1)S(1)}, bf16[512,256]{1,0:T(8,128)(2,1)S(1)}) custom-call(s32[3]{0:T(128)S(1)} %pad_add_fusion.where, bf16[512,256]{1,0:T(8,128)(2,1)S(1)} %get-tuple-element.41.own.kv_own, ...), custom_call_target="tpu_custom_call" | custom-call | flops 1000 | bytes 1000 | tf_op jit(solution)/shard_map/pallas_call | solution.py:406
  58.9 1.9 %collective-permute-start.4 = (bf16[512,256]{1,0:T(8,128)(2,1)S(1)}, bf16[512,256]{1,0:T(8,128)(2,1)S(1)}, u32[]{:S(2)}, u32[]{:S(2)}) collective-permute-start(bf16[512,256]{1,0:T(8,128)(2,1)S(1)} %get-tuple-element.67), channel_id=1, source_target_pairs={{0,2},{1,3},{2,4},{3,5},{4,6},{5,7},{6,8},{7,9},{8,10},{9,11},{10,... | collective-permute-start | bytes 786440 | tf_op jit(solution)/shard_map/ppermute | solution.py:558
  60.8 3.6 %collective-permute-start.5 = (bf16[512,256]{1,0:T(8,128)(2,1)S(1)}, bf16[512,256]{1,0:T(8,128)(2,1)S(1)}, u32[]{:S(2)}, u32[]{:S(2)}) collective-permute-start(bf16[512,256]{1,0:T(8,128)(2,1)S(1)} %get-tuple-element.68), channel_id=1, source_target_pairs={{2,0},{3,1},{4,2},{5,3},{6,4},{7,5},{8,6},{9,7},{10,8},{11,9},{12,... | collective-permute-start | bytes 786440 | tf_op jit(solution)/shard_map/ppermute | solution.py:559
  64.5 8.1 %all-gather.2 = bf16[4,2,128,256]{3,2,1,0:T(8,128)(2,1)S(1)} all-gather(bf16[2,2,128,256]{3,2,1,0:T(8,128)(2,1)S(1)} %get-tuple-element.48), channel_id=4, replica_groups=mesh['outer'=16,'inner'=2] {'inner'}, dimensions={0}, use_global_device_ids=true | all-gather | bytes 786432 | tf_op jit(solution)/shard_map/all_gather | solution.py:540
  72.6 5.9 %shard_map.80 = (bf16[2,2,128,256]{3,2,1,0:T(8,128)(2,1)S(1)}, bf16[2,2,128,256]{3,2,1,0:T(8,128)(2,1)S(1)}, f32[1024,256]{1,0:T(8,128)S(1)}, bf16[512,256]{1,0:T(8,128)(2,1)S(1)}, bf16[512,256]{1,0:T(8,128)(2,1)S(1)}) custom-call(s32[3]{0:T(128)S(1)} %pad_add_fusion.where, bf16[512,256]{1,0:T(8,128)(2,1)S(1)} %get-tuple-element.55.own.kv_own, ...), custom_call_target="tpu_custom_call" | custom-call | flops 1000 | bytes 1000 | tf_op jit(solution)/shard_map/pallas_call | solution.py:406
  78.5 1.9 %collective-permute-start.6 = (bf16[512,256]{1,0:T(8,128)(2,1)S(1)}, bf16[512,256]{1,0:T(8,128)(2,1)S(1)}, u32[]{:S(2)}, u32[]{:S(2)}) collective-permute-start(bf16[512,256]{1,0:T(8,128)(2,1)S(1)} %get-tuple-element.71), channel_id=1, source_target_pairs={{0,2},{1,3},{2,4},{3,5},{4,6},{5,7},{6,8},{7,9},{8,10},{9,11},{10,... | collective-permute-start | bytes 786440 | tf_op jit(solution)/shard_map/ppermute | solution.py:558
  80.5 3.6 %collective-permute-start.7 = (bf16[512,256]{1,0:T(8,128)(2,1)S(1)}, bf16[512,256]{1,0:T(8,128)(2,1)S(1)}, u32[]{:S(2)}, u32[]{:S(2)}) collective-permute-start(bf16[512,256]{1,0:T(8,128)(2,1)S(1)} %get-tuple-element.72), channel_id=1, source_target_pairs={{2,0},{3,1},{4,2},{5,3},{6,4},{7,5},{8,6},{9,7},{10,8},{11,9},{12,... | collective-permute-start | bytes 786440 | tf_op jit(solution)/shard_map/ppermute | solution.py:559
  84.1 9.7 %all-gather.5 = bf16[4,2,128,256]{3,2,1,0:T(8,128)(2,1)S(1)} all-gather(bf16[2,2,128,256]{3,2,1,0:T(8,128)(2,1)S(1)} %get-tuple-element.63), channel_id=7, replica_groups=mesh['outer'=16,'inner'=2] {'inner'}, dimensions={0}, use_global_device_ids=true | all-gather | bytes 786432 | tf_op jit(solution)/shard_map/all_gather | solution.py:540
  93.8 2.2 %shard_map.81 = (bf16[512,512]{1,0:T(8,128)(2,1)}, bf16[512,512]{1,0:T(8,128)(2,1)}) custom-call(s32[3]{0:T(128)S(1)} %pad_add_fusion.where, bf16[2,2,128,256]{3,2,1,0:T(8,128)(2,1)S(1)} %get-tuple-element.47.refs_0_, bf16[2,2,128,256]{3,2,1,0:T(8,128)(2,1)S(1)} %get-tuple-element.61.refs_1_, bf16[2,2,2,128,256]{4,3,2,1,0:T(8,128)(2,1)S(1)} %bitcast.17, ...), custom_call_target="tpu_custom_call" | custom-call | flops 1000 | bytes 1000 | tf_op jit(solution)/shard_map/pallas_call | solution.py:516
  96.7 8.8 %all-gather.6 = bf16[1024,256]{1,0:T(8,128)(2,1)S(1)} all-gather(bf16[512,256]{1,0:T(8,128)(2,1)S(1)} %get-tuple-element.74), channel_id=8, replica_groups=mesh['outer'=16,'inner'=2] {'inner'}, dimensions={0}, use_global_device_ids=true | all-gather | bytes 786432 | tf_op jit(solution)/shard_map/all_gather | solution.py:540
  106.2 8.0 %all-gather.7 = bf16[1024,256]{1,0:T(8,128)(2,1)S(1)} all-gather(bf16[512,256]{1,0:T(8,128)(2,1)S(1)} %get-tuple-element.75), channel_id=9, replica_groups=mesh['outer'=16,'inner'=2] {'inner'}, dimensions={0}, use_global_device_ids=true | all-gather | bytes 786432 | tf_op jit(solution)/shard_map/all_gather | solution.py:540
  114.2 2.2 %shard_map.84 = (bf16[512,512]{1,0:T(8,128)(2,1)}, bf16[512,512]{1,0:T(8,128)(2,1)}) custom-call(s32[3]{0:T(128)S(1)} %pad_add_fusion.where, bf16[512,256]{1,0:T(8,128)(2,1)S(1)} %get-tuple-element.69.refs_0_, bf16[512,256]{1,0:T(8,128)(2,1)S(1)} %get-tuple-element.73.refs_1_, bf16[2,512,256]{2,1,0:T(8,128)(2,1)S(1)} %bitcast.18, ...), custom_call_target="tpu_custom_call" | custom-call | flops 1000 | bytes 1000 | tf_op jit(solution)/shard_map/pallas_call | solution.py:516
  (19 shorter events, 2.8 us)
Async XLA Ops:
  0.7 1.0 copy-start
  1.8 1.0 copy-start.1
  13.9 58.7 %collective-permute-start.2 = (bf16[512,256]{1,0:T(8,128)(2,1)S(1)}, bf16[512,256]{1,0:T(8,128)(2,1)S(1)}, u32[]{:S(2)}, u32[]{:S(2)}) collective-permute-start(bf16[512,256]{1,0:T(8,128)(2,1)S(1)} %get-tuple-element.53), channel_id=1, source_target_pairs={{0,2},{1,3},{2,4},{3,5},{4,6},{5,7},{6,8},{7,9},{8,10},{9,11},{10,... | collective-permute-start | bytes 786440 | tf_op jit(solution)/shard_map/ppermute | solution.py:550
  15.8 56.8 %collective-permute-start.3 = (bf16[512,256]{1,0:T(8,128)(2,1)S(1)}, bf16[512,256]{1,0:T(8,128)(2,1)S(1)}, u32[]{:S(2)}, u32[]{:S(2)}) collective-permute-start(bf16[512,256]{1,0:T(8,128)(2,1)S(1)} %get-tuple-element.54), channel_id=1, source_target_pairs={{2,0},{3,1},{4,2},{5,3},{6,4},{7,5},{8,6},{9,7},{10,8},{11,9},{12,... | collective-permute-start | bytes 786440 | tf_op jit(solution)/shard_map/ppermute | solution.py:551
  19.4 15.2 %copy-start.3 = (bf16[512,512]{1,0:T(8,128)(2,1)S(1)}, bf16[512,512]{1,0:T(8,128)(2,1)}, u32[]{:S(2)}) copy-start(bf16[512,512]{1,0:T(8,128)(2,1)} %b.3) | copy-start | bytes 1572868
  28.3 6.3 %copy-start.2 = (bf16[512,512]{1,0:T(8,128)(2,1)S(1)}, bf16[512,512]{1,0:T(8,128)(2,1)}, u32[]{:S(2)}) copy-start(bf16[512,512]{1,0:T(8,128)(2,1)} %a.3) | copy-start | bytes 1572868
  29.0 24.0 %collective-permute-start = (bf16[512,256]{1,0:T(8,128)(2,1)S(1)}, bf16[512,256]{1,0:T(8,128)(2,1)S(1)}, u32[]{:S(2)}, u32[]{:S(2)}) collective-permute-start(bf16[512,256]{1,0:T(8,128)(2,1)S(1)} %get-tuple-element.45), channel_id=1, source_target_pairs={{0,2},{1,3},{2,4},{3,5},{4,6},{5,7},{6,8},{7,9},{8,10},{9,11},{10,... | collective-permute-start | bytes 786440 | tf_op jit(solution)/shard_map/ppermute | solution.py:550
  30.9 22.0 %collective-permute-start.1 = (bf16[512,256]{1,0:T(8,128)(2,1)S(1)}, bf16[512,256]{1,0:T(8,128)(2,1)S(1)}, u32[]{:S(2)}, u32[]{:S(2)}) collective-permute-start(bf16[512,256]{1,0:T(8,128)(2,1)S(1)} %get-tuple-element.46), channel_id=1, source_target_pairs={{2,0},{3,1},{4,2},{5,3},{6,4},{7,5},{8,6},{9,7},{10,8},{11,9},{12,... | collective-permute-start | bytes 786440 | tf_op jit(solution)/shard_map/ppermute | solution.py:551
  58.9 37.1 %collective-permute-start.4 = (bf16[512,256]{1,0:T(8,128)(2,1)S(1)}, bf16[512,256]{1,0:T(8,128)(2,1)S(1)}, u32[]{:S(2)}, u32[]{:S(2)}) collective-permute-start(bf16[512,256]{1,0:T(8,128)(2,1)S(1)} %get-tuple-element.67), channel_id=1, source_target_pairs={{0,2},{1,3},{2,4},{3,5},{4,6},{5,7},{6,8},{7,9},{8,10},{9,11},{10,... | collective-permute-start | bytes 786440 | tf_op jit(solution)/shard_map/ppermute | solution.py:558
  60.8 35.2 %collective-permute-start.5 = (bf16[512,256]{1,0:T(8,128)(2,1)S(1)}, bf16[512,256]{1,0:T(8,128)(2,1)S(1)}, u32[]{:S(2)}, u32[]{:S(2)}) collective-permute-start(bf16[512,256]{1,0:T(8,128)(2,1)S(1)} %get-tuple-element.68), channel_id=1, source_target_pairs={{2,0},{3,1},{4,2},{5,3},{6,4},{7,5},{8,6},{9,7},{10,8},{11,9},{12,... | collective-permute-start | bytes 786440 | tf_op jit(solution)/shard_map/ppermute | solution.py:559
  78.5 27.0 %collective-permute-start.6 = (bf16[512,256]{1,0:T(8,128)(2,1)S(1)}, bf16[512,256]{1,0:T(8,128)(2,1)S(1)}, u32[]{:S(2)}, u32[]{:S(2)}) collective-permute-start(bf16[512,256]{1,0:T(8,128)(2,1)S(1)} %get-tuple-element.71), channel_id=1, source_target_pairs={{0,2},{1,3},{2,4},{3,5},{4,6},{5,7},{6,8},{7,9},{8,10},{9,11},{10,... | collective-permute-start | bytes 786440 | tf_op jit(solution)/shard_map/ppermute | solution.py:558
  80.5 25.1 %collective-permute-start.7 = (bf16[512,256]{1,0:T(8,128)(2,1)S(1)}, bf16[512,256]{1,0:T(8,128)(2,1)S(1)}, u32[]{:S(2)}, u32[]{:S(2)}) collective-permute-start(bf16[512,256]{1,0:T(8,128)(2,1)S(1)} %get-tuple-element.72), channel_id=1, source_target_pairs={{2,0},{3,1},{4,2},{5,3},{6,4},{7,5},{8,6},{9,7},{10,8},{11,9},{12,... | collective-permute-start | bytes 786440 | tf_op jit(solution)/shard_map/ppermute | solution.py:559

commit v3 on v1

--- a/solution.py
+++ b/solution.py
@@ -85,7 +85,7 @@
     out = jax.ShapeDtypeStruct((rows, columns // CHUNKS), BF)
     outs = pl.pallas_call(
         pack_kernel,
-        in_specs=[smem(), pl.BlockSpec(memory_space=pl.ANY), pl.BlockSpec(memory_space=pl.ANY)],
+        in_specs=[smem(), pl.BlockSpec(memory_space=pltpu.HBM), pl.BlockSpec(memory_space=pltpu.HBM)],
         out_specs=[vmem()] * (2 * CHUNKS),
         out_shape=[out] * (2 * CHUNKS),
         scratch_shapes=[
@@ -114,8 +114,8 @@
     return pl.CostEstimate(flops=1000, bytes_accessed=1000, transcendentals=0)
 
 
-def halo_kernel(where, own, got, to_right, to_left):
-    def fill(first, second):
+def halo_kernel(where, own, got, near, wide):
+    def fill(first, second, to_right, to_left):
         to_right[0:256, :] = second[256:512, :]
         to_right[256:384, :] = pool1(second[0:256, :])
         to_right[384:448, :] = pool2(first[0:256, :])
@@ -125,13 +125,13 @@
         to_left[384:448, :] = pool2(second[0:256, :])
         to_left[448:512, :] = pool2(second[256:512, :])
 
-    @pl.when(where[0] == 0)
-    def _():
-        fill(own, got)
-
-    @pl.when(where[0] == 1)
-    def _():
-        fill(got, own)
+    for side in range(2):
+        for odd in range(2):
+
+            @pl.when((where[0] == side) & (where[3] == odd))
+            def _(side=side, odd=odd):
+                halves = (own, got) if side == 0 else (got, own)
+                fill(*halves, *((near, wide) if odd == 0 else (wide, near)))
 
 
 def halo(where, own, got):
@@ -210,11 +210,16 @@
 
 
 def main_kernel(
-    where, kv_own, kv_got, qg_own, qg_got, from_left, from_right,
-    oq_own, oq_far, grad, to_left, to_right,
-    raw, raw_t, one, one_t, two, two_t, qs, gs, p0, p1, p2, acc0, acc1, acc2, oq,
+    where, kv_own, kv_got, qg_own, qg_got, near_got, wide_got,
+    oq_own, oq_far, grad, near_out, wide_out,
+    raw, raw_t, one, one_t, two, two_t, qs, gs, p0, p1, p2, acc0, acc1, acc2, oq, halos,
 ):
     side = where[0]
+    odd = where[3]
+    halos[1 - odd] = near_got[...]
+    halos[odd] = wide_got[...]
+    from_left, from_right = halos.at[0], halos.at[1]
+    to_left, to_right = halos.at[0], halos.at[1]
     width = kv_own.shape[1] // 2
     left_bias = (1 - where[1]).astype(F32) * MASKED
     right_bias = (1 - where[2]).astype(F32) * MASKED
@@ -396,9 +401,11 @@
             to_right[384:512, cols] = (acc2[n, 384:512, :] * (0.25 * scale)).astype(BF)
     oq_own[...] = oq[pl.ds(side * 2, 2)]
     oq_far[...] = oq[pl.ds((1 - side) * 2, 2)]
-
-
-def main(where, kv_own, kv_got, qg_own, qg_got, from_left, from_right):
+    near_out[...] = halos[1 - odd]
+    wide_out[...] = halos[odd]
+
+
+def main(where, kv_own, kv_got, qg_own, qg_got, near_got, wide_got):
     rows, both = kv_own.shape
     width = both // 2
     oq_shape = jax.ShapeDtypeStruct((2, 2, width, PARENT), BF)
@@ -430,49 +437,45 @@
             pltpu.VMEM((2, 1024, HEAD), F32),
             pltpu.VMEM((2, 512, HEAD), F32),
             pltpu.VMEM((4, 2, width, PARENT), BF),
+            pltpu.VMEM((2, 512, both), BF),
         ],
         compiler_params=pltpu.CompilerParams(vmem_limit_bytes=24 * 1024 * 1024),
         cost_estimate=light(),
-    )(where, kv_own, kv_got, qg_own, qg_got, from_left, from_right)
-
-
-def join_kernel(where, grad, from_left, from_right, own, far):
-    def part(i, ref):
-        x = grad[i * PARENT : (i + 1) * PARENT, :]
-        tail = ref[384:512, :].astype(F32)
-        return x, tail
-
-    def value(i):
-        x = grad[i * PARENT : (i + 1) * PARENT, :]
-        if i == 0:
-            return x + from_left[0:256, :].astype(F32) + twice(twice(from_right[384:448, :].astype(F32)))
-        if i == 1:
-            return x + twice(
-                from_left[256:384, :].astype(F32) + twice(from_right[448:512, :].astype(F32))
-            )
-        if i == 2:
-            return x + twice(
-                from_right[256:384, :].astype(F32) + twice(from_left[384:448, :].astype(F32))
-            )
-        return x + from_right[0:256, :].astype(F32) + twice(twice(from_left[448:512, :].astype(F32)))
-
-    def fill(first, second):
-        first[0:256, :] = value(0).astype(BF)
-        first[256:512, :] = value(1).astype(BF)
-        second[0:256, :] = value(2).astype(BF)
-        second[256:512, :] = value(3).astype(BF)
-
-    @pl.when(where[0] == 0)
-    def _():
-        fill(own, far)
-
-    @pl.when(where[0] == 1)
-    def _():
-        fill(far, own)
-
-
-def join(where, grad, from_left, from_right):
-    shape = jax.ShapeDtypeStruct(from_left.shape, BF)
+    )(where, kv_own, kv_got, qg_own, qg_got, near_got, wide_got)
+
+
+def join_kernel(where, grad, near_got, wide_got, own, far):
+    def fill(first, second, from_left, from_right):
+        def parent(i):
+            return grad[i * PARENT : (i + 1) * PARENT, :]
+
+        def part(ref, start, stop):
+            return ref[start:stop, :].astype(F32)
+
+        first[0:256, :] = (
+            parent(0) + part(from_left, 0, 256) + twice(twice(part(from_right, 384, 448)))
+        ).astype(BF)
+        first[256:512, :] = (
+            parent(1) + twice(part(from_left, 256, 384) + twice(part(from_right, 448, 512)))
+        ).astype(BF)
+        second[0:256, :] = (
+            parent(2) + twice(part(from_right, 256, 384) + twice(part(from_left, 384, 448)))
+        ).astype(BF)
+        second[256:512, :] = (
+            parent(3) + part(from_right, 0, 256) + twice(twice(part(from_left, 448, 512)))
+        ).astype(BF)
+
+    for side in range(2):
+        for odd in range(2):
+
+            @pl.when((where[0] == side) & (where[3] == odd))
+            def _(side=side, odd=odd):
+                halves = (own, far) if side == 0 else (far, own)
+                fill(*halves, *((wide_got, near_got) if odd == 0 else (near_got, wide_got)))
+
+
+def join(where, grad, near_got, wide_got):
+    shape = jax.ShapeDtypeStruct(near_got.shape, BF)
     return pl.pallas_call(
         join_kernel,
         in_specs=[smem(), vmem(), vmem(), vmem()],
@@ -480,7 +483,7 @@
         out_shape=[shape, shape],
         compiler_params=small(),
         cost_estimate=light(),
-    )(where, grad, from_left, from_right)
+    )(where, grad, near_got, wide_got)
 
 
 def unpack_rows_kernel(where, *refs):
@@ -525,15 +528,19 @@
     axes = ("outer", "inner")
     count = lax.axis_size("outer") * lax.axis_size("inner")
     device = lax.axis_index("outer") * lax.axis_size("inner") + lax.axis_index("inner")
-    where = jnp.stack(
-        [device % 2, (device >= 2).astype(jnp.int32), (device < count - 2).astype(jnp.int32)]
-    ).astype(jnp.int32)
+    pair = device // 2
+    where = jnp.stack([device % 2, pair > 0, pair < count // 2 - 1, pair % 2]).astype(jnp.int32)
     across = [(i, i ^ 1) for i in range(count)]
-    rightward = [(i, i + 2) for i in range(count - 2)]
-    leftward = [(i + 2, i) for i in range(count - 2)]
+    near_edges = [(i, i ^ 2) for i in range(count) if i ^ 2 < count]
+    wide_edges = [(i, i + 2 if i // 2 % 2 else i - 2) for i in range(count)]
+    wide_edges = [(i, j) for i, j in wide_edges if 0 <= j < count]
 
     def swap(x):
         return lax.ppermute(x, axes, across)
+
+    def beside(near, wide):
+        wide = lax.ppermute(wide, axes, wide_edges)
+        return lax.ppermute(near, axes, near_edges), wide
 
     kv, kv_far = pack(where, key_matrix, value_matrix)
     qg, qg_far = pack(where, queries, cotangent)
@@ -542,18 +549,13 @@
     for c in range(CHUNKS):
         got_kv = swap(kv_far[c])
         got_qg = swap(qg_far[c])
-        to_right, to_left = halo(where, kv[c], got_kv)
-        from_left = lax.ppermute(to_right, axes, rightward)
-        from_right = lax.ppermute(to_left, axes, leftward)
-        inputs = (kv[c], got_kv, qg[c], got_qg, from_left, from_right)
+        inputs = (kv[c], got_kv, qg[c], got_qg, *beside(*halo(where, kv[c], got_kv)))
         if c > 0:
             oq_got[c - 1], inputs = lax.optimization_barrier((oq_got[c - 1], inputs))
-        own, far, grad, to_left, to_right = main(where, *inputs)
+        own, far, grad, near, wide = main(where, *inputs)
         oq_own.append(own)
         oq_got.append(swap(far))
-        from_left = lax.ppermute(to_right, axes, rightward)
-        from_right = lax.ppermute(to_left, axes, leftward)
-        back.append((grad, from_left, from_right))
+        back.append((grad, *beside(near, wide)))
     for c in range(CHUNKS):
         own, far = join(where, *back[c])
         kv_own.append(own)

time: 77.2 us -> 74.6 us (0.966); the launches traced: 76.7 us -> 73.3 us
  starting transfers between devices: 31.1 us -> 21.4 us
  waiting for transfers between devices: 20.3 us -> 26.6 us
    ppermute x8, starting transfers between devices: 21.6 us -> 10.9 us  [the longest x4 8.65 us: beside(): wide = lax.ppermute(wide, axes, wide_edges)]
    ppermute x8, waiting for transfers between devices: 1.1 us -> 5.65 us  [the longest x4 5.64 us: beside(): wide = lax.ppermute(wide, axes, wide_edges)]
    ppermute x8, waiting for transfers between devices: 19.2 us -> 20.9 us  [swap(): return lax.ppermute(x, axes, across)]
    ppermute x8, starting transfers between devices: 9.52 us -> 10.4 us  [swap(): return lax.ppermute(x, axes, across)]
  transfers between devices with their start and end apart: 16 -> 16, of which waited for: 6 -> 7; matrix products, arithmetic and copies ran while one was open for 0% -> 0% of each run, Pallas kernels for 24% -> 25%
where the time goes in v3:
time: 74.6 us; the launch traced here: 73.3 us
  waiting for transfers between devices  26.6 us (36%)
  Pallas kernels  22.4 us (30%)
  starting transfers between devices  21.4 us (29%)
  local copies, waits for them, and re-layouts  2.09 us (3%)
  between operations  0.84 us (1%)
    ppermute x8, waiting for transfers between devices, swap(): return lax.ppermute(x, axes, across)  20.9 us
    pallas_call x2, Pallas kernels, main(): pl.pallas_call(main_kernel, in_specs=[smem()] + [vmem()] * 6, out_specs=[...  11.9 us
    ppermute x8, starting transfers between devices, swap(): return lax.ppermute(x, axes, across)  10.4 us
    ppermute x4, starting transfers between devices, beside(): wide = lax.ppermute(wide, axes, wide_edges)  8.65 us
    ppermute x4, waiting for transfers between devices, beside(): wide = lax.ppermute(wide, axes, wide_edges)  5.64 us
    pallas_call x2, Pallas kernels, unpack(): pl.pallas_call(kernel, in_specs=[smem()] + [vmem()] * (2 * CHUNKS), out_s...  4.42 us
    pallas_call x2, Pallas kernels, pack(): pl.pallas_call(pack_kernel, in_specs=[smem(), pl.BlockSpec(memory_space=p...  3.28 us
    ppermute x4, starting transfers between devices, beside(): return (lax.ppermute(near, axes, near_edges), wide)  2.28 us
  transfers between devices with their start and end apart: 16, of which 7 were waited for; matrix products, arithmetic and copies ran while one was open for 0% of the time, Pallas kernels for 25%

profile of v3, /device:TPU:12, one launch (start us, length us, event | category | flops | bytes accessed | tf_op | source)
XLA Modules:
  0.0 73.3 jit_solution(8668348692052012334)
XLA Ops:
  0.7 1.0 %copy-done = bf16[512,512]{1,0:T(8,128)(2,1)S(1)} copy-done((bf16[512,512]{1,0:T(8,128)(2,1)S(1)}, bf16[512,512]{1,0:T(8,128)(2,1)}, u32[]{:S(2)}) %copy-start) | copy-done | bytes 524312
  2.8 1.6 %shard_map.75 = (bf16[512,256]{1,0:T(8,128)(2,1)S(1)}, bf16[512,256]{1,0:T(8,128)(2,1)S(1)}, bf16[512,256]{1,0:T(8,128)(2,1)S(1)}, bf16[512,256]{1,0:T(8,128)(2,1)S(1)}) custom-call(s32[4]{0:T(128)S(1)} %pad_add_fusion.where, bf16[512,512]{1,0:T(8,128)(2,1)S(1)} %copy-done, bf16[512,512]{1,0:T(8,128)(2,1)S(1)} %copy-done.1), custom_call_target="tpu_custom_call" | custom-call | flops 1000 | bytes 1000 | tf_op jit(solution)/shard_map/pallas_call | solution.py:86
  4.5 1.6 %collective-permute-start = (bf16[512,256]{1,0:T(8,128)(2,1)S(1)}, bf16[512,256]{1,0:T(8,128)(2,1)S(1)}, u32[]{:S(2)}, u32[]{:S(2)}) collective-permute-start(bf16[512,256]{1,0:T(8,128)(2,1)S(1)} %get-tuple-element.42), channel_id=1, source_target_pairs={{0,1},{1,0},{2,3},{3,2},{4,5},{5,4},{6,7},{7,6},{8,9},{9,8},{10,11... | collective-permute-start | bytes 786440 | tf_op jit(solution)/shard_map/ppermute | solution.py:539
  6.6 1.6 %shard_map.76 = (bf16[512,256]{1,0:T(8,128)(2,1)S(1)}, bf16[512,256]{1,0:T(8,128)(2,1)S(1)}, bf16[512,256]{1,0:T(8,128)(2,1)S(1)}, bf16[512,256]{1,0:T(8,128)(2,1)S(1)}) custom-call(s32[4]{0:T(128)S(1)} %pad_add_fusion.where, bf16[512,512]{1,0:T(8,128)(2,1)S(1)} %copy-done.2, bf16[512,512]{1,0:T(8,128)(2,1)S(1)} %copy-done.3), custom_call_target="tpu_custom_call" | custom-call | flops 1000 | bytes 1000 | tf_op jit(solution)/shard_map/pallas_call | solution.py:86
  8.2 1.6 %collective-permute-start.1 = (bf16[512,256]{1,0:T(8,128)(2,1)S(1)}, bf16[512,256]{1,0:T(8,128)(2,1)S(1)}, u32[]{:S(2)}, u32[]{:S(2)}) collective-permute-start(bf16[512,256]{1,0:T(8,128)(2,1)S(1)} %get-tuple-element.44), channel_id=1, source_target_pairs={{0,1},{1,0},{2,3},{3,2},{4,5},{5,4},{6,7},{7,6},{8,9},{9,8},{10,11... | collective-permute-start | bytes 786440 | tf_op jit(solution)/shard_map/ppermute | solution.py:539
  9.8 3.9 %collective-permute-done.got.kv_got = bf16[512,256]{1,0:T(8,128)(2,1)S(1)} collective-permute-done((bf16[512,256]{1,0:T(8,128)(2,1)S(1)}, bf16[512,256]{1,0:T(8,128)(2,1)S(1)}, u32[]{:S(2)}, u32[]{:S(2)}) %collective-permute-start) | collective-permute-done | bytes 262176 | tf_op jit(solution)/shard_map/ppermute | solution.py:539
  14.5 2.5 %collective-permute-start.3 = (bf16[512,256]{1,0:T(8,128)(2,1)S(1)}, bf16[512,256]{1,0:T(8,128)(2,1)S(1)}, u32[]{:S(2)}, u32[]{:S(2)}) collective-permute-start(bf16[512,256]{1,0:T(8,128)(2,1)S(1)} %get-tuple-element.46), channel_id=1, source_target_pairs={{2,4},{3,5},{4,2},{5,3},{6,8},{7,9},{8,6},{9,7},{10,12},{11,13},{1... | collective-permute-start | bytes 786440 | tf_op jit(solution)/shard_map/ppermute | solution.py:542
  17.0 1.5 %collective-permute-start.6 = (bf16[512,256]{1,0:T(8,128)(2,1)S(1)}, bf16[512,256]{1,0:T(8,128)(2,1)S(1)}, u32[]{:S(2)}, u32[]{:S(2)}) collective-permute-start(bf16[512,256]{1,0:T(8,128)(2,1)S(1)} %get-tuple-element.52), channel_id=1, source_target_pairs={{0,1},{1,0},{2,3},{3,2},{4,5},{5,4},{6,7},{7,6},{8,9},{9,8},{10,11... | collective-permute-start | bytes 786440 | tf_op jit(solution)/shard_map/ppermute | solution.py:539
  20.1 4.9 %collective-permute-done.1.qg_got = bf16[512,256]{1,0:T(8,128)(2,1)S(1)} collective-permute-done((bf16[512,256]{1,0:T(8,128)(2,1)S(1)}, bf16[512,256]{1,0:T(8,128)(2,1)S(1)}, u32[]{:S(2)}, u32[]{:S(2)}) %collective-permute-start.1) | collective-permute-done | bytes 262176 | tf_op jit(solution)/shard_map/ppermute | solution.py:539
  25.0 1.9 %collective-permute-start.8 = (bf16[512,256]{1,0:T(8,128)(2,1)S(1)}, bf16[512,256]{1,0:T(8,128)(2,1)S(1)}, u32[]{:S(2)}, u32[]{:S(2)}) collective-permute-start(bf16[512,256]{1,0:T(8,128)(2,1)S(1)} %get-tuple-element.54), channel_id=1, source_target_pairs={{2,4},{3,5},{4,2},{5,3},{6,8},{7,9},{8,6},{9,7},{10,12},{11,13},{1... | collective-permute-start | bytes 786440 | tf_op jit(solution)/shard_map/ppermute | solution.py:542
  26.9 6.0 %shard_map.78 = (bf16[2,2,128,256]{3,2,1,0:T(8,128)(2,1)S(1)}, bf16[2,2,128,256]{3,2,1,0:T(8,128)(2,1)S(1)}, f32[1024,256]{1,0:T(8,128)S(1)}, bf16[512,256]{1,0:T(8,128)(2,1)S(1)}, bf16[512,256]{1,0:T(8,128)(2,1)S(1)}) custom-call(s32[4]{0:T(128)S(1)} %pad_add_fusion.where, bf16[512,256]{1,0:T(8,128)(2,1)S(1)} %get-tuple-element.41.own.kv_own, ...), custom_call_target="tpu_custom_call" | custom-call | flops 1000 | bytes 1000 | tf_op jit(solution)/shard_map/pallas_call | solution.py:413
  32.9 1.6 %collective-permute-start.4 = (bf16[2,2,128,256]{3,2,1,0:T(8,128)(2,1)S(1)}, bf16[2,2,128,256]{3,2,1,0:T(8,128)(2,1)S(1)}, u32[]{:S(2)}, u32[]{:S(2)}) collective-permute-start(bf16[2,2,128,256]{3,2,1,0:T(8,128)(2,1)S(1)} %get-tuple-element.48), channel_id=1, source_target_pairs={{0,1},{1,0},{2,3},{3,2},{4,5},{5,4},{6,7},{7,6},{8,9},{9,8},{10,11... | collective-permute-start | bytes 786440 | tf_op jit(solution)/shard_map/ppermute | solution.py:539
  34.4 1.3 %collective-permute-start.10 = (bf16[512,256]{1,0:T(8,128)(2,1)S(1)}, bf16[512,256]{1,0:T(8,128)(2,1)S(1)}, u32[]{:S(2)}, u32[]{:S(2)}) collective-permute-start(bf16[512,256]{1,0:T(8,128)(2,1)S(1)} %get-tuple-element.67), channel_id=1, source_target_pairs={{0,2},{1,3},{2,0},{3,1},{4,6},{5,7},{6,4},{7,5},{8,10},{9,11},{10,... | collective-permute-start | bytes 786440 | tf_op jit(solution)/shard_map/ppermute | solution.py:543
  35.8 2.2 %collective-permute-start.11 = (bf16[512,256]{1,0:T(8,128)(2,1)S(1)}, bf16[512,256]{1,0:T(8,128)(2,1)S(1)}, u32[]{:S(2)}, u32[]{:S(2)}) collective-permute-start(bf16[512,256]{1,0:T(8,128)(2,1)S(1)} %get-tuple-element.68), channel_id=1, source_target_pairs={{2,4},{3,5},{4,2},{5,3},{6,8},{7,9},{8,6},{9,7},{10,12},{11,13},{1... | collective-permute-start | bytes 786440 | tf_op jit(solution)/shard_map/ppermute | solution.py:542
  38.0 3.5 %collective-permute-done.4.refs_2_ = bf16[2,2,128,256]{3,2,1,0:T(8,128)(2,1)S(1)} collective-permute-done((bf16[2,2,128,256]{3,2,1,0:T(8,128)(2,1)S(1)}, bf16[2,2,128,256]{3,2,1,0:T(8,128)(2,1)S(1)}, u32[]{:S(2)}, u32[]{:S(2)}) %collective-permute-start.4) | collective-permute-done | bytes 262176 | tf_op jit(solution)/shard_map/ppermute | solution.py:539
  41.5 6.0 %shard_map.80 = (bf16[2,2,128,256]{3,2,1,0:T(8,128)(2,1)S(1)}, bf16[2,2,128,256]{3,2,1,0:T(8,128)(2,1)S(1)}, f32[1024,256]{1,0:T(8,128)S(1)}, bf16[512,256]{1,0:T(8,128)(2,1)S(1)}, bf16[512,256]{1,0:T(8,128)(2,1)S(1)}) custom-call(s32[4]{0:T(128)S(1)} %pad_add_fusion.where, bf16[512,256]{1,0:T(8,128)(2,1)S(1)} %get-tuple-element.55.own.kv_own, ...), custom_call_target="tpu_custom_call" | custom-call | flops 1000 | bytes 1000 | tf_op jit(solution)/shard_map/pallas_call | solution.py:413
  48.3 2.0 %collective-permute-start.13 = (bf16[512,256]{1,0:T(8,128)(2,1)S(1)}, bf16[512,256]{1,0:T(8,128)(2,1)S(1)}, u32[]{:S(2)}, u32[]{:S(2)}) collective-permute-start(bf16[512,256]{1,0:T(8,128)(2,1)S(1)} %get-tuple-element.72), channel_id=1, source_target_pairs={{2,4},{3,5},{4,2},{5,3},{6,8},{7,9},{8,6},{9,7},{10,12},{11,13},{1... | collective-permute-start | bytes 786440 | tf_op jit(solution)/shard_map/ppermute | solution.py:542
  51.1 1.5 %collective-permute-start.14 = (bf16[512,256]{1,0:T(8,128)(2,1)S(1)}, bf16[512,256]{1,0:T(8,128)(2,1)S(1)}, u32[]{:S(2)}, u32[]{:S(2)}) collective-permute-start(bf16[512,256]{1,0:T(8,128)(2,1)S(1)} %get-tuple-element.74), channel_id=1, source_target_pairs={{0,1},{1,0},{2,3},{3,2},{4,5},{5,4},{6,7},{7,6},{8,9},{9,8},{10,11... | collective-permute-start | bytes 786440 | tf_op jit(solution)/shard_map/ppermute | solution.py:539
  53.1 5.6 %collective-permute-done.13.wide_got = bf16[512,256]{1,0:T(8,128)(2,1)S(1)} collective-permute-done((bf16[512,256]{1,0:T(8,128)(2,1)S(1)}, bf16[512,256]{1,0:T(8,128)(2,1)S(1)}, u32[]{:S(2)}, u32[]{:S(2)}) %collective-permute-start.13) | collective-permute-done | bytes 262176 | tf_op jit(solution)/shard_map/ppermute | solution.py:542
  59.5 1.6 %collective-permute-start.15 = (bf16[512,256]{1,0:T(8,128)(2,1)S(1)}, bf16[512,256]{1,0:T(8,128)(2,1)S(1)}, u32[]{:S(2)}, u32[]{:S(2)}) collective-permute-start(bf16[512,256]{1,0:T(8,128)(2,1)S(1)} %get-tuple-element.75), channel_id=1, source_target_pairs={{0,1},{1,0},{2,3},{3,2},{4,5},{5,4},{6,7},{7,6},{8,9},{9,8},{10,11... | collective-permute-start | bytes 786440 | tf_op jit(solution)/shard_map/ppermute | solution.py:539
  61.0 4.4 %collective-permute-done.9.refs_3_ = bf16[2,2,128,256]{3,2,1,0:T(8,128)(2,1)S(1)} collective-permute-done((bf16[2,2,128,256]{3,2,1,0:T(8,128)(2,1)S(1)}, bf16[2,2,128,256]{3,2,1,0:T(8,128)(2,1)S(1)}, u32[]{:S(2)}, u32[]{:S(2)}) %collective-permute-start.9) | collective-permute-done | bytes 262176 | tf_op jit(solution)/shard_map/ppermute | solution.py:539
  65.5 2.2 %shard_map.81 = (bf16[512,512]{1,0:T(8,128)(2,1)}, bf16[512,512]{1,0:T(8,128)(2,1)}) custom-call(s32[4]{0:T(128)S(1)} %pad_add_fusion.where, bf16[2,2,128,256]{3,2,1,0:T(8,128)(2,1)S(1)} %get-tuple-element.47.refs_0_, bf16[2,2,128,256]{3,2,1,0:T(8,128)(2,1)S(1)} %get-tuple-element.61.refs_1_, bf16[2,2,128,256]{3,2,1,0:T(8,128)(2,1)S(1)} %collective-permute-done.4.refs_2_, ...), custom_call_target="tpu_custom_call" | custom-call | flops 1000 | bytes 1000 | tf_op jit(solution)/shard_map/pallas_call | solution.py:517
  67.7 3.4 %collective-permute-done.15.refs_3_ = bf16[512,256]{1,0:T(8,128)(2,1)S(1)} collective-permute-done((bf16[512,256]{1,0:T(8,128)(2,1)S(1)}, bf16[512,256]{1,0:T(8,128)(2,1)S(1)}, u32[]{:S(2)}, u32[]{:S(2)}) %collective-permute-start.15) | collective-permute-done | bytes 262176 | tf_op jit(solution)/shard_map/ppermute | solution.py:539
  71.1 2.2 %shard_map.84 = (bf16[512,512]{1,0:T(8,128)(2,1)}, bf16[512,512]{1,0:T(8,128)(2,1)}) custom-call(s32[4]{0:T(128)S(1)} %pad_add_fusion.where, bf16[512,256]{1,0:T(8,128)(2,1)S(1)} %get-tuple-element.69.refs_0_, bf16[512,256]{1,0:T(8,128)(2,1)S(1)} %get-tuple-element.73.refs_1_, bf16[512,256]{1,0:T(8,128)(2,1)S(1)} %collective-permute-done.14.refs_2_, ...), custom_call_target="tpu_custom_call" | custom-call | flops 1000 | bytes 1000 | tf_op jit(solution)/shard_map/pallas_call | solution.py:517
  (27 shorter events, 6.7 us)
Async XLA Ops:
  0.7 1.0 %copy-start = (bf16[512,512]{1,0:T(8,128)(2,1)S(1)}, bf16[512,512]{1,0:T(8,128)(2,1)}, u32[]{:S(2)}) copy-start(bf16[512,512]{1,0:T(8,128)(2,1)} %a.2) | copy-start | bytes 1572868
  1.8 1.0 %copy-start.1 = (bf16[512,512]{1,0:T(8,128)(2,1)S(1)}, bf16[512,512]{1,0:T(8,128)(2,1)}, u32[]{:S(2)}) copy-start(bf16[512,512]{1,0:T(8,128)(2,1)} %b.2) | copy-start | bytes 1572868
  2.8 3.7 %copy-start.2 = (bf16[512,512]{1,0:T(8,128)(2,1)S(1)}, bf16[512,512]{1,0:T(8,128)(2,1)}, u32[]{:S(2)}) copy-start(bf16[512,512]{1,0:T(8,128)(2,1)} %a.3) | copy-start | bytes 1572868
  2.8 3.7 %copy-start.3 = (bf16[512,512]{1,0:T(8,128)(2,1)S(1)}, bf16[512,512]{1,0:T(8,128)(2,1)}, u32[]{:S(2)}) copy-start(bf16[512,512]{1,0:T(8,128)(2,1)} %b.3) | copy-start | bytes 1572868
  4.5 9.3 %collective-permute-start = (bf16[512,256]{1,0:T(8,128)(2,1)S(1)}, bf16[512,256]{1,0:T(8,128)(2,1)S(1)}, u32[]{:S(2)}, u32[]{:S(2)}) collective-permute-start(bf16[512,256]{1,0:T(8,128)(2,1)S(1)} %get-tuple-element.42), channel_id=1, source_target_pairs={{0,1},{1,0},{2,3},{3,2},{4,5},{5,4},{6,7},{7,6},{8,9},{9,8},{10,11... | collective-permute-start | bytes 786440 | tf_op jit(solution)/shard_map/ppermute | solution.py:539
  6.0 13.3 %collective-permute-start.5 = (bf16[512,256]{1,0:T(8,128)(2,1)S(1)}, bf16[512,256]{1,0:T(8,128)(2,1)S(1)}, u32[]{:S(2)}, u32[]{:S(2)}) collective-permute-start(bf16[512,256]{1,0:T(8,128)(2,1)S(1)} %get-tuple-element.50), channel_id=1, source_target_pairs={{0,1},{1,0},{2,3},{3,2},{4,5},{5,4},{6,7},{7,6},{8,9},{9,8},{10,11... | collective-permute-start | bytes 786440 | tf_op jit(solution)/shard_map/ppermute | solution.py:539
  8.2 16.7 %collective-permute-start.1 = (bf16[512,256]{1,0:T(8,128)(2,1)S(1)}, bf16[512,256]{1,0:T(8,128)(2,1)S(1)}, u32[]{:S(2)}, u32[]{:S(2)}) collective-permute-start(bf16[512,256]{1,0:T(8,128)(2,1)S(1)} %get-tuple-element.44), channel_id=1, source_target_pairs={{0,1},{1,0},{2,3},{3,2},{4,5},{5,4},{6,7},{7,6},{8,9},{9,8},{10,11... | collective-permute-start | bytes 786440 | tf_op jit(solution)/shard_map/ppermute | solution.py:539
  14.4 12.5 %collective-permute-start.2 = (bf16[512,256]{1,0:T(8,128)(2,1)S(1)}, bf16[512,256]{1,0:T(8,128)(2,1)S(1)}, u32[]{:S(2)}, u32[]{:S(2)}) collective-permute-start(bf16[512,256]{1,0:T(8,128)(2,1)S(1)} %get-tuple-element.45), channel_id=1, source_target_pairs={{0,2},{1,3},{2,0},{3,1},{4,6},{5,7},{6,4},{7,5},{8,10},{9,11},{10,... | collective-permute-start | bytes 786440 | tf_op jit(solution)/shard_map/ppermute | solution.py:543
  14.5 12.4 %collective-permute-start.3 = (bf16[512,256]{1,0:T(8,128)(2,1)S(1)}, bf16[512,256]{1,0:T(8,128)(2,1)S(1)}, u32[]{:S(2)}, u32[]{:S(2)}) collective-permute-start(bf16[512,256]{1,0:T(8,128)(2,1)S(1)} %get-tuple-element.46), channel_id=1, source_target_pairs={{2,4},{3,5},{4,2},{5,3},{6,8},{7,9},{8,6},{9,7},{10,12},{11,13},{1... | collective-permute-start | bytes 786440 | tf_op jit(solution)/shard_map/ppermute | solution.py:542
  17.0 18.8 %collective-permute-start.6 = (bf16[512,256]{1,0:T(8,128)(2,1)S(1)}, bf16[512,256]{1,0:T(8,128)(2,1)S(1)}, u32[]{:S(2)}, u32[]{:S(2)}) collective-permute-start(bf16[512,256]{1,0:T(8,128)(2,1)S(1)} %get-tuple-element.52), channel_id=1, source_target_pairs={{0,1},{1,0},{2,3},{3,2},{4,5},{5,4},{6,7},{7,6},{8,9},{9,8},{10,11... | collective-permute-start | bytes 786440 | tf_op jit(solution)/shard_map/ppermute | solution.py:539
  20.0 18.0 %collective-permute-start.7 = (bf16[512,256]{1,0:T(8,128)(2,1)S(1)}, bf16[512,256]{1,0:T(8,128)(2,1)S(1)}, u32[]{:S(2)}, u32[]{:S(2)}) collective-permute-start(bf16[512,256]{1,0:T(8,128)(2,1)S(1)} %get-tuple-element.53), channel_id=1, source_target_pairs={{0,2},{1,3},{2,0},{3,1},{4,6},{5,7},{6,4},{7,5},{8,10},{9,11},{10,... | collective-permute-start | bytes 786440 | tf_op jit(solution)/shard_map/ppermute | solution.py:543
  25.0 13.0 %collective-permute-start.8 = (bf16[512,256]{1,0:T(8,128)(2,1)S(1)}, bf16[512,256]{1,0:T(8,128)(2,1)S(1)}, u32[]{:S(2)}, u32[]{:S(2)}) collective-permute-start(bf16[512,256]{1,0:T(8,128)(2,1)S(1)} %get-tuple-element.54), channel_id=1, source_target_pairs={{2,4},{3,5},{4,2},{5,3},{6,8},{7,9},{8,6},{9,7},{10,12},{11,13},{1... | collective-permute-start | bytes 786440 | tf_op jit(solution)/shard_map/ppermute | solution.py:542
  32.9 8.6 %collective-permute-start.4 = (bf16[2,2,128,256]{3,2,1,0:T(8,128)(2,1)S(1)}, bf16[2,2,128,256]{3,2,1,0:T(8,128)(2,1)S(1)}, u32[]{:S(2)}, u32[]{:S(2)}) collective-permute-start(bf16[2,2,128,256]{3,2,1,0:T(8,128)(2,1)S(1)} %get-tuple-element.48), channel_id=1, source_target_pairs={{0,1},{1,0},{2,3},{3,2},{4,5},{5,4},{6,7},{7,6},{8,9},{9,8},{10,11... | collective-permute-start | bytes 786440 | tf_op jit(solution)/shard_map/ppermute | solution.py:539
  34.4 15.9 %collective-permute-start.10 = (bf16[512,256]{1,0:T(8,128)(2,1)S(1)}, bf16[512,256]{1,0:T(8,128)(2,1)S(1)}, u32[]{:S(2)}, u32[]{:S(2)}) collective-permute-start(bf16[512,256]{1,0:T(8,128)(2,1)S(1)} %get-tuple-element.67), channel_id=1, source_target_pairs={{0,2},{1,3},{2,0},{3,1},{4,6},{5,7},{6,4},{7,5},{8,10},{9,11},{10,... | collective-permute-start | bytes 786440 | tf_op jit(solution)/shard_map/ppermute | solution.py:543
  35.8 14.6 %collective-permute-start.11 = (bf16[512,256]{1,0:T(8,128)(2,1)S(1)}, bf16[512,256]{1,0:T(8,128)(2,1)S(1)}, u32[]{:S(2)}, u32[]{:S(2)}) collective-permute-start(bf16[512,256]{1,0:T(8,128)(2,1)S(1)} %get-tuple-element.68), channel_id=1, source_target_pairs={{2,4},{3,5},{4,2},{5,3},{6,8},{7,9},{8,6},{9,7},{10,12},{11,13},{1... | collective-permute-start | bytes 786440 | tf_op jit(solution)/shard_map/ppermute | solution.py:542
  47.5 5.7 %collective-permute-start.12 = (bf16[512,256]{1,0:T(8,128)(2,1)S(1)}, bf16[512,256]{1,0:T(8,128)(2,1)S(1)}, u32[]{:S(2)}, u32[]{:S(2)}) collective-permute-start(bf16[512,256]{1,0:T(8,128)(2,1)S(1)} %get-tuple-element.71), channel_id=1, source_target_pairs={{0,2},{1,3},{2,0},{3,1},{4,6},{5,7},{6,4},{7,5},{8,10},{9,11},{10,... | collective-permute-start | bytes 786440 | tf_op jit(solution)/shard_map/ppermute | solution.py:543
  48.3 10.5 %collective-permute-start.13 = (bf16[512,256]{1,0:T(8,128)(2,1)S(1)}, bf16[512,256]{1,0:T(8,128)(2,1)S(1)}, u32[]{:S(2)}, u32[]{:S(2)}) collective-permute-start(bf16[512,256]{1,0:T(8,128)(2,1)S(1)} %get-tuple-element.72), channel_id=1, source_target_pairs={{2,4},{3,5},{4,2},{5,3},{6,8},{7,9},{8,6},{9,7},{10,12},{11,13},{1... | collective-permute-start | bytes 786440 | tf_op jit(solution)/shard_map/ppermute | solution.py:542
  51.1 16.6 %collective-permute-start.14 = (bf16[512,256]{1,0:T(8,128)(2,1)S(1)}, bf16[512,256]{1,0:T(8,128)(2,1)S(1)}, u32[]{:S(2)}, u32[]{:S(2)}) collective-permute-start(bf16[512,256]{1,0:T(8,128)(2,1)S(1)} %get-tuple-element.74), channel_id=1, source_target_pairs={{0,1},{1,0},{2,3},{3,2},{4,5},{5,4},{6,7},{7,6},{8,9},{9,8},{10,11... | collective-permute-start | bytes 786440 | tf_op jit(solution)/shard_map/ppermute | solution.py:539
  52.6 12.9 %collective-permute-start.9 = (bf16[2,2,128,256]{3,2,1,0:T(8,128)(2,1)S(1)}, bf16[2,2,128,256]{3,2,1,0:T(8,128)(2,1)S(1)}, u32[]{:S(2)}, u32[]{:S(2)}) collective-permute-start(bf16[2,2,128,256]{3,2,1,0:T(8,128)(2,1)S(1)} %get-tuple-element.63), channel_id=1, source_target_pairs={{0,1},{1,0},{2,3},{3,2},{4,5},{5,4},{6,7},{7,6},{8,9},{9,8},{10,11... | collective-permute-start | bytes 786440 | tf_op jit(solution)/shard_map/ppermute | solution.py:539
  59.5 11.6 %collective-permute-start.15 = (bf16[512,256]{1,0:T(8,128)(2,1)S(1)}, bf16[512,256]{1,0:T(8,128)(2,1)S(1)}, u32[]{:S(2)}, u32[]{:S(2)}) collective-permute-start(bf16[512,256]{1,0:T(8,128)(2,1)S(1)} %get-tuple-element.75), channel_id=1, source_target_pairs={{0,1},{1,0},{2,3},{3,2},{4,5},{5,4},{6,7},{7,6},{8,9},{9,8},{10,11... | collective-permute-start | bytes 786440 | tf_op jit(solution)/shard_map/ppermute | solution.py:539

commit v4 on v3

--- a/solution.py
+++ b/solution.py
@@ -549,12 +549,12 @@
     for c in range(CHUNKS):
         got_kv = swap(kv_far[c])
         got_qg = swap(qg_far[c])
-        inputs = (kv[c], got_kv, qg[c], got_qg, *beside(*halo(where, kv[c], got_kv)))
-        if c > 0:
-            oq_got[c - 1], inputs = lax.optimization_barrier((oq_got[c - 1], inputs))
-        own, far, grad, near, wide = main(where, *inputs)
+        halos = beside(*halo(where, kv[c], got_kv))
+        own, far, grad, near, wide = main(where, kv[c], got_kv, qg[c], got_qg, *halos)
         oq_own.append(own)
         oq_got.append(swap(far))
+        if c + 1 < CHUNKS:
+            oq_got[c], near, wide = lax.optimization_barrier((oq_got[c], near, wide))
         back.append((grad, *beside(near, wide)))
     for c in range(CHUNKS):
         own, far = join(where, *back[c])

time: 74.6 us -> 71.2 us (0.954)
  waiting for transfers between devices: 26.6 us -> 23.8 us
    ppermute x8, waiting for transfers between devices: 20.9 us -> 15.6 us  [swap(): return lax.ppermute(x, axes, across)]
    ppermute x4, waiting for transfers between devices: 5.64 us -> 8.11 us  [beside(): wide = lax.ppermute(wide, axes, wide_edges)]
  transfers between devices with their start and end apart: 16 -> 16, of which waited for: 7 -> 8; matrix products, arithmetic and copies ran while one was open for 0% -> 0% of each run, Pallas kernels for 25% -> 26%
where the time goes in v4:
time: 71.2 us; the launch traced here: 70.4 us
  waiting for transfers between devices  23.8 us (33%)
  Pallas kernels  22.4 us (31%)
  starting transfers between devices  21.3 us (30%)
  local copies, waits for them, and re-layouts  2.09 us (3%)
  between operations  0.82 us (1%)
    ppermute x8, waiting for transfers between devices, swap(): return lax.ppermute(x, axes, across)  15.6 us
    pallas_call x2, Pallas kernels, main(): pl.pallas_call(main_kernel, in_specs=[smem()] + [vmem()] * 6, out_specs=[...  11.9 us
    ppermute x8, starting transfers between devices, swap(): return lax.ppermute(x, axes, across)  10.3 us
    ppermute x4, starting transfers between devices, beside(): wide = lax.ppermute(wide, axes, wide_edges)  8.66 us
    ppermute x4, waiting for transfers between devices, beside(): wide = lax.ppermute(wide, axes, wide_edges)  8.11 us
    pallas_call x2, Pallas kernels, unpack(): pl.pallas_call(kernel, in_specs=[smem()] + [vmem()] * (2 * CHUNKS), out_s...  4.43 us
    pallas_call x2, Pallas kernels, pack(): pl.pallas_call(pack_kernel, in_specs=[smem(), pl.BlockSpec(memory_space=p...  3.27 us
    ppermute x4, starting transfers between devices, beside(): return (lax.ppermute(near, axes, near_edges), wide)  2.3 us
  transfers between devices with their start and end apart: 16, of which 8 were waited for; matrix products, arithmetic and copies ran while one was open for 0% of the time, Pallas kernels for 26%

profile of v4, /device:TPU:12, one launch (start us, length us, event | category | flops | bytes accessed | tf_op | source)
XLA Modules:
  0.0 70.4 jit_solution(12376732492973946720)
XLA Ops:
  2.8 1.6 %shard_map.75 = (bf16[512,256]{1,0:T(8,128)(2,1)S(1)}, bf16[512,256]{1,0:T(8,128)(2,1)S(1)}, bf16[512,256]{1,0:T(8,128)(2,1)S(1)}, bf16[512,256]{1,0:T(8,128)(2,1)S(1)}) custom-call(s32[4]{0:T(128)S(1)} %pad_add_fusion.where, bf16[512,512]{1,0:T(8,128)(2,1)S(1)} %copy-done, bf16[512,512]{1,0:T(8,128)(2,1)S(1)} %copy-done.1), custom_call_target="tpu_custom_call" | custom-call | flops 1000 | bytes 1000 | tf_op jit(solution)/shard_map/pallas_call | solution.py:86
  4.5 1.6 %collective-permute-start = (bf16[512,256]{1,0:T(8,128)(2,1)S(1)}, bf16[512,256]{1,0:T(8,128)(2,1)S(1)}, u32[]{:S(2)}, u32[]{:S(2)}) collective-permute-start(bf16[512,256]{1,0:T(8,128)(2,1)S(1)} %get-tuple-element.38), channel_id=1, source_target_pairs={{0,1},{1,0},{2,3},{3,2},{4,5},{5,4},{6,7},{7,6},{8,9},{9,8},{10,11... | collective-permute-start | bytes 786440 | tf_op jit(solution)/shard_map/ppermute | solution.py:539
  6.6 1.6 %shard_map.76 = (bf16[512,256]{1,0:T(8,128)(2,1)S(1)}, bf16[512,256]{1,0:T(8,128)(2,1)S(1)}, bf16[512,256]{1,0:T(8,128)(2,1)S(1)}, bf16[512,256]{1,0:T(8,128)(2,1)S(1)}) custom-call(s32[4]{0:T(128)S(1)} %pad_add_fusion.where, bf16[512,512]{1,0:T(8,128)(2,1)S(1)} %copy-done.2, bf16[512,512]{1,0:T(8,128)(2,1)S(1)} %copy-done.3), custom_call_target="tpu_custom_call" | custom-call | flops 1000 | bytes 1000 | tf_op jit(solution)/shard_map/pallas_call | solution.py:86
  8.2 1.6 %collective-permute-start.1 = (bf16[512,256]{1,0:T(8,128)(2,1)S(1)}, bf16[512,256]{1,0:T(8,128)(2,1)S(1)}, u32[]{:S(2)}, u32[]{:S(2)}) collective-permute-start(bf16[512,256]{1,0:T(8,128)(2,1)S(1)} %get-tuple-element.40), channel_id=1, source_target_pairs={{0,1},{1,0},{2,3},{3,2},{4,5},{5,4},{6,7},{7,6},{8,9},{9,8},{10,11... | collective-permute-start | bytes 786440 | tf_op jit(solution)/shard_map/ppermute | solution.py:539
  9.8 3.9 %collective-permute-done.got.kv_got = bf16[512,256]{1,0:T(8,128)(2,1)S(1)} collective-permute-done((bf16[512,256]{1,0:T(8,128)(2,1)S(1)}, bf16[512,256]{1,0:T(8,128)(2,1)S(1)}, u32[]{:S(2)}, u32[]{:S(2)}) %collective-permute-start) | collective-permute-done | bytes 262176 | tf_op jit(solution)/shard_map/ppermute | solution.py:539
  14.5 2.5 %collective-permute-start.3 = (bf16[512,256]{1,0:T(8,128)(2,1)S(1)}, bf16[512,256]{1,0:T(8,128)(2,1)S(1)}, u32[]{:S(2)}, u32[]{:S(2)}) collective-permute-start(bf16[512,256]{1,0:T(8,128)(2,1)S(1)} %get-tuple-element.42), channel_id=1, source_target_pairs={{2,4},{3,5},{4,2},{5,3},{6,8},{7,9},{8,6},{9,7},{10,12},{11,13},{1... | collective-permute-start | bytes 786440 | tf_op jit(solution)/shard_map/ppermute | solution.py:542
  17.0 1.5 %collective-permute-start.5 = (bf16[512,256]{1,0:T(8,128)(2,1)S(1)}, bf16[512,256]{1,0:T(8,128)(2,1)S(1)}, u32[]{:S(2)}, u32[]{:S(2)}) collective-permute-start(bf16[512,256]{1,0:T(8,128)(2,1)S(1)} %get-tuple-element.47), channel_id=1, source_target_pairs={{0,1},{1,0},{2,3},{3,2},{4,5},{5,4},{6,7},{7,6},{8,9},{9,8},{10,11... | collective-permute-start | bytes 786440 | tf_op jit(solution)/shard_map/ppermute | solution.py:539
  20.1 4.9 %collective-permute-done.1.qg_got = bf16[512,256]{1,0:T(8,128)(2,1)S(1)} collective-permute-done((bf16[512,256]{1,0:T(8,128)(2,1)S(1)}, bf16[512,256]{1,0:T(8,128)(2,1)S(1)}, u32[]{:S(2)}, u32[]{:S(2)}) %collective-permute-start.1) | collective-permute-done | bytes 262176 | tf_op jit(solution)/shard_map/ppermute | solution.py:539
  25.0 2.1 %collective-permute-start.7 = (bf16[512,256]{1,0:T(8,128)(2,1)S(1)}, bf16[512,256]{1,0:T(8,128)(2,1)S(1)}, u32[]{:S(2)}, u32[]{:S(2)}) collective-permute-start(bf16[512,256]{1,0:T(8,128)(2,1)S(1)} %get-tuple-element.49), channel_id=1, source_target_pairs={{2,4},{3,5},{4,2},{5,3},{6,8},{7,9},{8,6},{9,7},{10,12},{11,13},{1... | collective-permute-start | bytes 786440 | tf_op jit(solution)/shard_map/ppermute | solution.py:542
  27.1 6.0 %shard_map.78 = (bf16[2,2,128,256]{3,2,1,0:T(8,128)(2,1)S(1)}, bf16[2,2,128,256]{3,2,1,0:T(8,128)(2,1)S(1)}, f32[1024,256]{1,0:T(8,128)S(1)}, bf16[512,256]{1,0:T(8,128)(2,1)S(1)}, bf16[512,256]{1,0:T(8,128)(2,1)S(1)}) custom-call(s32[4]{0:T(128)S(1)} %pad_add_fusion.where, bf16[512,256]{1,0:T(8,128)(2,1)S(1)} %get-tuple-element.37.own.kv_own, ...), custom_call_target="tpu_custom_call" | custom-call | flops 1000 | bytes 1000 | tf_op jit(solution)/shard_map/pallas_call | solution.py:413
  33.1 1.6 %collective-permute-start.8 = (bf16[2,2,128,256]{3,2,1,0:T(8,128)(2,1)S(1)}, bf16[2,2,128,256]{3,2,1,0:T(8,128)(2,1)S(1)}, u32[]{:S(2)}, u32[]{:S(2)}) collective-permute-start(bf16[2,2,128,256]{3,2,1,0:T(8,128)(2,1)S(1)} %get-tuple-element.51), channel_id=1, source_target_pairs={{0,1},{1,0},{2,3},{3,2},{4,5},{5,4},{6,7},{7,6},{8,9},{9,8},{10,11... | collective-permute-start | bytes 786440 | tf_op jit(solution)/shard_map/ppermute | solution.py:539
  35.5 6.0 %shard_map.80 = (bf16[2,2,128,256]{3,2,1,0:T(8,128)(2,1)S(1)}, bf16[2,2,128,256]{3,2,1,0:T(8,128)(2,1)S(1)}, f32[1024,256]{1,0:T(8,128)S(1)}, bf16[512,256]{1,0:T(8,128)(2,1)S(1)}, bf16[512,256]{1,0:T(8,128)(2,1)S(1)}) custom-call(s32[4]{0:T(128)S(1)} %pad_add_fusion.where, bf16[512,256]{1,0:T(8,128)(2,1)S(1)} %get-tuple-element.44.own.kv_own, ...), custom_call_target="tpu_custom_call" | custom-call | flops 1000 | bytes 1000 | tf_op jit(solution)/shard_map/pallas_call | solution.py:413
  42.0 2.0 %collective-permute-start.13 = (bf16[512,256]{1,0:T(8,128)(2,1)S(1)}, bf16[512,256]{1,0:T(8,128)(2,1)S(1)}, u32[]{:S(2)}, u32[]{:S(2)}) collective-permute-start(bf16[512,256]{1,0:T(8,128)(2,1)S(1)} %get-tuple-element.64), channel_id=1, source_target_pairs={{2,4},{3,5},{4,2},{5,3},{6,8},{7,9},{8,6},{9,7},{10,12},{11,13},{1... | collective-permute-start | bytes 786440 | tf_op jit(solution)/shard_map/ppermute | solution.py:542
  44.1 1.6 %collective-permute-start.10 = (bf16[512,256]{1,0:T(8,128)(2,1)S(1)}, bf16[512,256]{1,0:T(8,128)(2,1)S(1)}, u32[]{:S(2)}, u32[]{:S(2)}) collective-permute-start(bf16[512,256]{1,0:T(8,128)(2,1)S(1)} %get-tuple-element.59), channel_id=1, source_target_pairs={{0,2},{1,3},{2,0},{3,1},{4,6},{5,7},{6,4},{7,5},{8,10},{9,11},{10,... | collective-permute-start | bytes 786440 | tf_op jit(solution)/shard_map/ppermute | solution.py:543
  45.6 2.0 %collective-permute-start.11 = (bf16[512,256]{1,0:T(8,128)(2,1)S(1)}, bf16[512,256]{1,0:T(8,128)(2,1)S(1)}, u32[]{:S(2)}, u32[]{:S(2)}) collective-permute-start(bf16[512,256]{1,0:T(8,128)(2,1)S(1)} %get-tuple-element.60), channel_id=1, source_target_pairs={{2,4},{3,5},{4,2},{5,3},{6,8},{7,9},{8,6},{9,7},{10,12},{11,13},{1... | collective-permute-start | bytes 786440 | tf_op jit(solution)/shard_map/ppermute | solution.py:542
  47.7 1.4 %collective-permute-start.9 = (bf16[2,2,128,256]{3,2,1,0:T(8,128)(2,1)S(1)}, bf16[2,2,128,256]{3,2,1,0:T(8,128)(2,1)S(1)}, u32[]{:S(2)}, u32[]{:S(2)}) collective-permute-start(bf16[2,2,128,256]{3,2,1,0:T(8,128)(2,1)S(1)} %get-tuple-element.55), channel_id=1, source_target_pairs={{0,1},{1,0},{2,3},{3,2},{4,5},{5,4},{6,7},{7,6},{8,9},{9,8},{10,11... | collective-permute-start | bytes 786440 | tf_op jit(solution)/shard_map/ppermute | solution.py:539
  49.1 6.2 %collective-permute-done.13.wide_got = bf16[512,256]{1,0:T(8,128)(2,1)S(1)} collective-permute-done((bf16[512,256]{1,0:T(8,128)(2,1)S(1)}, bf16[512,256]{1,0:T(8,128)(2,1)S(1)}, u32[]{:S(2)}, u32[]{:S(2)}) %collective-permute-start.13) | collective-permute-done | bytes 262176 | tf_op jit(solution)/shard_map/ppermute | solution.py:542
  56.0 1.1 %collective-permute-start.15 = (bf16[512,256]{1,0:T(8,128)(2,1)S(1)}, bf16[512,256]{1,0:T(8,128)(2,1)S(1)}, u32[]{:S(2)}, u32[]{:S(2)}) collective-permute-start(bf16[512,256]{1,0:T(8,128)(2,1)S(1)} %get-tuple-element.67), channel_id=1, source_target_pairs={{0,1},{1,0},{2,3},{3,2},{4,5},{5,4},{6,7},{7,6},{8,9},{9,8},{10,11... | collective-permute-start | bytes 786440 | tf_op jit(solution)/shard_map/ppermute | solution.py:539
  57.1 1.1 %collective-permute-done.11.wide_got = bf16[512,256]{1,0:T(8,128)(2,1)S(1)} collective-permute-done((bf16[512,256]{1,0:T(8,128)(2,1)S(1)}, bf16[512,256]{1,0:T(8,128)(2,1)S(1)}, u32[]{:S(2)}, u32[]{:S(2)}) %collective-permute-start.11) | collective-permute-done | bytes 262176 | tf_op jit(solution)/shard_map/ppermute | solution.py:542
  58.8 1.1 %collective-permute-start.14 = (bf16[512,256]{1,0:T(8,128)(2,1)S(1)}, bf16[512,256]{1,0:T(8,128)(2,1)S(1)}, u32[]{:S(2)}, u32[]{:S(2)}) collective-permute-start(bf16[512,256]{1,0:T(8,128)(2,1)S(1)} %get-tuple-element.66), channel_id=1, source_target_pairs={{0,1},{1,0},{2,3},{3,2},{4,5},{5,4},{6,7},{7,6},{8,9},{9,8},{10,11... | collective-permute-start | bytes 786440 | tf_op jit(solution)/shard_map/ppermute | solution.py:539
  59.9 2.2 %shard_map.81 = (bf16[512,512]{1,0:T(8,128)(2,1)}, bf16[512,512]{1,0:T(8,128)(2,1)}) custom-call(s32[4]{0:T(128)S(1)} %pad_add_fusion.where, bf16[2,2,128,256]{3,2,1,0:T(8,128)(2,1)S(1)} %get-tuple-element.43.refs_0_, bf16[2,2,128,256]{3,2,1,0:T(8,128)(2,1)S(1)} %get-tuple-element.50.refs_1_, bf16[2,2,128,256]{3,2,1,0:T(8,128)(2,1)S(1)} %collective-permute-done.8.refs_2_, ...), custom_call_target="tpu_custom_call" | custom-call | flops 1000 | bytes 1000 | tf_op jit(solution)/shard_map/pallas_call | solution.py:517
  62.1 3.2 %collective-permute-done.15.refs_3_ = bf16[512,256]{1,0:T(8,128)(2,1)S(1)} collective-permute-done((bf16[512,256]{1,0:T(8,128)(2,1)S(1)}, bf16[512,256]{1,0:T(8,128)(2,1)S(1)}, u32[]{:S(2)}, u32[]{:S(2)}) %collective-permute-start.15) | collective-permute-done | bytes 262176 | tf_op jit(solution)/shard_map/ppermute | solution.py:539
  65.3 2.8 %collective-permute-done.14.refs_2_ = bf16[512,256]{1,0:T(8,128)(2,1)S(1)} collective-permute-done((bf16[512,256]{1,0:T(8,128)(2,1)S(1)}, bf16[512,256]{1,0:T(8,128)(2,1)S(1)}, u32[]{:S(2)}, u32[]{:S(2)}) %collective-permute-start.14) | collective-permute-done | bytes 262176 | tf_op jit(solution)/shard_map/ppermute | solution.py:539
  68.2 2.2 %shard_map.84 = (bf16[512,512]{1,0:T(8,128)(2,1)}, bf16[512,512]{1,0:T(8,128)(2,1)}) custom-call(s32[4]{0:T(128)S(1)} %pad_add_fusion.where, bf16[512,256]{1,0:T(8,128)(2,1)S(1)} %get-tuple-element.61.refs_0_, bf16[512,256]{1,0:T(8,128)(2,1)S(1)} %get-tuple-element.65.refs_1_, bf16[512,256]{1,0:T(8,128)(2,1)S(1)} %collective-permute-done.14.refs_2_, ...), custom_call_target="tpu_custom_call" | custom-call | flops 1000 | bytes 1000 | tf_op jit(solution)/shard_map/pallas_call | solution.py:517
  (27 shorter events, 7.8 us)
Async XLA Ops:
  0.7 1.0 %copy-start = (bf16[512,512]{1,0:T(8,128)(2,1)S(1)}, bf16[512,512]{1,0:T(8,128)(2,1)}, u32[]{:S(2)}) copy-start(bf16[512,512]{1,0:T(8,128)(2,1)} %a.2) | copy-start | bytes 1572868
  1.8 1.0 %copy-start.1 = (bf16[512,512]{1,0:T(8,128)(2,1)S(1)}, bf16[512,512]{1,0:T(8,128)(2,1)}, u32[]{:S(2)}) copy-start(bf16[512,512]{1,0:T(8,128)(2,1)} %b.2) | copy-start | bytes 1572868
  2.8 3.7 %copy-start.2 = (bf16[512,512]{1,0:T(8,128)(2,1)S(1)}, bf16[512,512]{1,0:T(8,128)(2,1)}, u32[]{:S(2)}) copy-start(bf16[512,512]{1,0:T(8,128)(2,1)} %a.3) | copy-start | bytes 1572868
  2.8 3.7 %copy-start.3 = (bf16[512,512]{1,0:T(8,128)(2,1)S(1)}, bf16[512,512]{1,0:T(8,128)(2,1)}, u32[]{:S(2)}) copy-start(bf16[512,512]{1,0:T(8,128)(2,1)} %b.3) | copy-start | bytes 1572868
  4.5 9.3 %collective-permute-start = (bf16[512,256]{1,0:T(8,128)(2,1)S(1)}, bf16[512,256]{1,0:T(8,128)(2,1)S(1)}, u32[]{:S(2)}, u32[]{:S(2)}) collective-permute-start(bf16[512,256]{1,0:T(8,128)(2,1)S(1)} %get-tuple-element.38), channel_id=1, source_target_pairs={{0,1},{1,0},{2,3},{3,2},{4,5},{5,4},{6,7},{7,6},{8,9},{9,8},{10,11... | collective-permute-start | bytes 786440 | tf_op jit(solution)/shard_map/ppermute | solution.py:539
  6.0 13.3 %collective-permute-start.4 = (bf16[512,256]{1,0:T(8,128)(2,1)S(1)}, bf16[512,256]{1,0:T(8,128)(2,1)S(1)}, u32[]{:S(2)}, u32[]{:S(2)}) collective-permute-start(bf16[512,256]{1,0:T(8,128)(2,1)S(1)} %get-tuple-element.45), channel_id=1, source_target_pairs={{0,1},{1,0},{2,3},{3,2},{4,5},{5,4},{6,7},{7,6},{8,9},{9,8},{10,11... | collective-permute-start | bytes 786440 | tf_op jit(solution)/shard_map/ppermute | solution.py:539
  8.2 16.8 %collective-permute-start.1 = (bf16[512,256]{1,0:T(8,128)(2,1)S(1)}, bf16[512,256]{1,0:T(8,128)(2,1)S(1)}, u32[]{:S(2)}, u32[]{:S(2)}) collective-permute-start(bf16[512,256]{1,0:T(8,128)(2,1)S(1)} %get-tuple-element.40), channel_id=1, source_target_pairs={{0,1},{1,0},{2,3},{3,2},{4,5},{5,4},{6,7},{7,6},{8,9},{9,8},{10,11... | collective-permute-start | bytes 786440 | tf_op jit(solution)/shard_map/ppermute | solution.py:539
  14.4 12.6 %collective-permute-start.2 = (bf16[512,256]{1,0:T(8,128)(2,1)S(1)}, bf16[512,256]{1,0:T(8,128)(2,1)S(1)}, u32[]{:S(2)}, u32[]{:S(2)}) collective-permute-start(bf16[512,256]{1,0:T(8,128)(2,1)S(1)} %get-tuple-element.41), channel_id=1, source_target_pairs={{0,2},{1,3},{2,0},{3,1},{4,6},{5,7},{6,4},{7,5},{8,10},{9,11},{10,... | collective-permute-start | bytes 786440 | tf_op jit(solution)/shard_map/ppermute | solution.py:543
  14.5 12.6 %collective-permute-start.3 = (bf16[512,256]{1,0:T(8,128)(2,1)S(1)}, bf16[512,256]{1,0:T(8,128)(2,1)S(1)}, u32[]{:S(2)}, u32[]{:S(2)}) collective-permute-start(bf16[512,256]{1,0:T(8,128)(2,1)S(1)} %get-tuple-element.42), channel_id=1, source_target_pairs={{2,4},{3,5},{4,2},{5,3},{6,8},{7,9},{8,6},{9,7},{10,12},{11,13},{1... | collective-permute-start | bytes 786440 | tf_op jit(solution)/shard_map/ppermute | solution.py:542
  17.0 17.6 %collective-permute-start.5 = (bf16[512,256]{1,0:T(8,128)(2,1)S(1)}, bf16[512,256]{1,0:T(8,128)(2,1)S(1)}, u32[]{:S(2)}, u32[]{:S(2)}) collective-permute-start(bf16[512,256]{1,0:T(8,128)(2,1)S(1)} %get-tuple-element.47), channel_id=1, source_target_pairs={{0,1},{1,0},{2,3},{3,2},{4,5},{5,4},{6,7},{7,6},{8,9},{9,8},{10,11... | collective-permute-start | bytes 786440 | tf_op jit(solution)/shard_map/ppermute | solution.py:539
  20.0 14.6 %collective-permute-start.6 = (bf16[512,256]{1,0:T(8,128)(2,1)S(1)}, bf16[512,256]{1,0:T(8,128)(2,1)S(1)}, u32[]{:S(2)}, u32[]{:S(2)}) collective-permute-start(bf16[512,256]{1,0:T(8,128)(2,1)S(1)} %get-tuple-element.48), channel_id=1, source_target_pairs={{0,2},{1,3},{2,0},{3,1},{4,6},{5,7},{6,4},{7,5},{8,10},{9,11},{10,... | collective-permute-start | bytes 786440 | tf_op jit(solution)/shard_map/ppermute | solution.py:543
  25.0 10.5 %collective-permute-start.7 = (bf16[512,256]{1,0:T(8,128)(2,1)S(1)}, bf16[512,256]{1,0:T(8,128)(2,1)S(1)}, u32[]{:S(2)}, u32[]{:S(2)}) collective-permute-start(bf16[512,256]{1,0:T(8,128)(2,1)S(1)} %get-tuple-element.49), channel_id=1, source_target_pairs={{2,4},{3,5},{4,2},{5,3},{6,8},{7,9},{8,6},{9,7},{10,12},{11,13},{1... | collective-permute-start | bytes 786440 | tf_op jit(solution)/shard_map/ppermute | solution.py:542
  33.1 11.0 %collective-permute-start.8 = (bf16[2,2,128,256]{3,2,1,0:T(8,128)(2,1)S(1)}, bf16[2,2,128,256]{3,2,1,0:T(8,128)(2,1)S(1)}, u32[]{:S(2)}, u32[]{:S(2)}) collective-permute-start(bf16[2,2,128,256]{3,2,1,0:T(8,128)(2,1)S(1)} %get-tuple-element.51), channel_id=1, source_target_pairs={{0,1},{1,0},{2,3},{3,2},{4,5},{5,4},{6,7},{7,6},{8,9},{9,8},{10,11... | collective-permute-start | bytes 786440 | tf_op jit(solution)/shard_map/ppermute | solution.py:539
  41.4 7.7 %collective-permute-start.12 = (bf16[512,256]{1,0:T(8,128)(2,1)S(1)}, bf16[512,256]{1,0:T(8,128)(2,1)S(1)}, u32[]{:S(2)}, u32[]{:S(2)}) collective-permute-start(bf16[512,256]{1,0:T(8,128)(2,1)S(1)} %get-tuple-element.63), channel_id=1, source_target_pairs={{0,2},{1,3},{2,0},{3,1},{4,6},{5,7},{6,4},{7,5},{8,10},{9,11},{10,... | collective-permute-start | bytes 786440 | tf_op jit(solution)/shard_map/ppermute | solution.py:543
  42.0 13.3 %collective-permute-start.13 = (bf16[512,256]{1,0:T(8,128)(2,1)S(1)}, bf16[512,256]{1,0:T(8,128)(2,1)S(1)}, u32[]{:S(2)}, u32[]{:S(2)}) collective-permute-start(bf16[512,256]{1,0:T(8,128)(2,1)S(1)} %get-tuple-element.64), channel_id=1, source_target_pairs={{2,4},{3,5},{4,2},{5,3},{6,8},{7,9},{8,6},{9,7},{10,12},{11,13},{1... | collective-permute-start | bytes 786440 | tf_op jit(solution)/shard_map/ppermute | solution.py:542
  44.1 13.0 %collective-permute-start.10 = (bf16[512,256]{1,0:T(8,128)(2,1)S(1)}, bf16[512,256]{1,0:T(8,128)(2,1)S(1)}, u32[]{:S(2)}, u32[]{:S(2)}) collective-permute-start(bf16[512,256]{1,0:T(8,128)(2,1)S(1)} %get-tuple-element.59), channel_id=1, source_target_pairs={{0,2},{1,3},{2,0},{3,1},{4,6},{5,7},{6,4},{7,5},{8,10},{9,11},{10,... | collective-permute-start | bytes 786440 | tf_op jit(solution)/shard_map/ppermute | solution.py:543
  45.6 12.5 %collective-permute-start.11 = (bf16[512,256]{1,0:T(8,128)(2,1)S(1)}, bf16[512,256]{1,0:T(8,128)(2,1)S(1)}, u32[]{:S(2)}, u32[]{:S(2)}) collective-permute-start(bf16[512,256]{1,0:T(8,128)(2,1)S(1)} %get-tuple-element.60), channel_id=1, source_target_pairs={{2,4},{3,5},{4,2},{5,3},{6,8},{7,9},{8,6},{9,7},{10,12},{11,13},{1... | collective-permute-start | bytes 786440 | tf_op jit(solution)/shard_map/ppermute | solution.py:542
  47.7 12.2 %collective-permute-start.9 = (bf16[2,2,128,256]{3,2,1,0:T(8,128)(2,1)S(1)}, bf16[2,2,128,256]{3,2,1,0:T(8,128)(2,1)S(1)}, u32[]{:S(2)}, u32[]{:S(2)}) collective-permute-start(bf16[2,2,128,256]{3,2,1,0:T(8,128)(2,1)S(1)} %get-tuple-element.55), channel_id=1, source_target_pairs={{0,1},{1,0},{2,3},{3,2},{4,5},{5,4},{6,7},{7,6},{8,9},{9,8},{10,11... | collective-permute-start | bytes 786440 | tf_op jit(solution)/shard_map/ppermute | solution.py:539
  56.0 9.3 %collective-permute-start.15 = (bf16[512,256]{1,0:T(8,128)(2,1)S(1)}, bf16[512,256]{1,0:T(8,128)(2,1)S(1)}, u32[]{:S(2)}, u32[]{:S(2)}) collective-permute-start(bf16[512,256]{1,0:T(8,128)(2,1)S(1)} %get-tuple-element.67), channel_id=1, source_target_pairs={{0,1},{1,0},{2,3},{3,2},{4,5},{5,4},{6,7},{7,6},{8,9},{9,8},{10,11... | collective-permute-start | bytes 786440 | tf_op jit(solution)/shard_map/ppermute | solution.py:539
  58.8 9.3 %collective-permute-start.14 = (bf16[512,256]{1,0:T(8,128)(2,1)S(1)}, bf16[512,256]{1,0:T(8,128)(2,1)S(1)}, u32[]{:S(2)}, u32[]{:S(2)}) collective-permute-start(bf16[512,256]{1,0:T(8,128)(2,1)S(1)} %get-tuple-element.66), channel_id=1, source_target_pairs={{0,1},{1,0},{2,3},{3,2},{4,5},{5,4},{6,7},{7,6},{8,9},{9,8},{10,11... | collective-permute-start | bytes 786440 | tf_op jit(solution)/shard_map/ppermute | solution.py:539

commit v5 on v4

--- a/solution.py
+++ b/solution.py
@@ -13,6 +13,7 @@
 PARENT = 256
 LEVELS = 3
 CHUNKS = 2
+LATE_CHUNK = 0
 INV_ROOT = HEAD**-0.5
 TO_LOG2 = INV_ROOT * math.log2(math.e)
 MASKED = -1e30
@@ -54,48 +55,46 @@
     return jnp.concatenate([x, x], axis=axis)
 
 
-def pack_kernel(where, a, b, *refs):
-    outs, held, sems = refs[: 2 * CHUNKS], refs[2 * CHUNKS], refs[2 * CHUNKS + 1]
-    rows, columns = a.shape
+def pack_kernel(own, where, *refs):
+    count = 4 if own else 2
+    arrays, outs, (held, sems) = refs[:count], refs[count:-2], refs[-2:]
+    rows, columns = arrays[0].shape
     half = columns // 2
     width = half // CHUNKS
-    copies = []
-    for n, side in enumerate((1 - where[0], where[0])):
-        at = pl.ds(pl.multiple_of(side * half, half), half)
-        for m, ref in enumerate((a, b)):
-            copies.append(
-                pltpu.make_async_copy(ref.at[:, at], held.at[2 * n + m], sems.at[2 * n + m])
-            )
-            copies[-1].start()
+    side = where[0] if own else 1 - where[0]
+    at = pl.ds(pl.multiple_of(side * half, half), half)
+    copies = [
+        pltpu.make_async_copy(ref.at[:, at], held.at[m], sems.at[m]) for m, ref in enumerate(arrays)
+    ]
+    for copy in copies:
+        copy.start()
     order = order_matrix(False)
-    for n in range(2):
-        own = n == 1
-        for m in range(2):
-            copies[2 * n + m].wait()
-            for i in range(rows // PARENT):
-                at = slice(i * PARENT, (i + 1) * PARENT)
-                x = dot_nn(order, held[2 * n + m, at, :]).astype(BF)
-                for c in range(CHUNKS):
-                    ref = outs[c] if own else outs[CHUNKS + c]
-                    ref[at, m * width : (m + 1) * width] = x[:, c * width : (c + 1) * width]
-
-
-def pack(where, a, b):
-    rows, columns = a.shape
-    out = jax.ShapeDtypeStruct((rows, columns // CHUNKS), BF)
-    outs = pl.pallas_call(
-        pack_kernel,
-        in_specs=[smem(), pl.BlockSpec(memory_space=pltpu.HBM), pl.BlockSpec(memory_space=pltpu.HBM)],
-        out_specs=[vmem()] * (2 * CHUNKS),
-        out_shape=[out] * (2 * CHUNKS),
+    for m in range(count):
+        copies[m].wait()
+        first = m % 2 * width
+        for i in range(rows // PARENT):
+            at = slice(i * PARENT, (i + 1) * PARENT)
+            x = dot_nn(order, held[m, at, :]).astype(BF)
+            for c in range(CHUNKS):
+                out = outs[m // 2 * CHUNKS + c]
+                out[at, first : first + width] = x[:, c * width : (c + 1) * width]
+
+
+def pack(own, where, *arrays):
+    rows, columns = arrays[0].shape
+    count = len(arrays)
+    return pl.pallas_call(
+        functools.partial(pack_kernel, own),
+        in_specs=[smem()] + [pl.BlockSpec(memory_space=pltpu.HBM)] * count,
+        out_specs=[vmem()] * (count // 2 * CHUNKS),
+        out_shape=[jax.ShapeDtypeStruct((rows, columns // CHUNKS), BF)] * (count // 2 * CHUNKS),
         scratch_shapes=[
-            pltpu.VMEM((4, rows, columns // 2), BF),
-            pltpu.SemaphoreType.DMA((4,)),
+            pltpu.VMEM((count, rows, columns // 2), BF),
+            pltpu.SemaphoreType.DMA((count,)),
         ],
         compiler_params=small(),
         cost_estimate=light(),
-    )(where, a, b)
-    return outs[:CHUNKS], outs[CHUNKS:]
+    )(where, *arrays)
 
 
 def smem():
@@ -235,22 +234,23 @@
             raw[n, 1280:1536, :] = from_right[0:256, cols]
             one[n, 0:128, :] = from_left[256:384, cols]
             for i in range(6):
-                block = pool1(raw[n, i * PARENT : (i + 1) * PARENT, :])
-                at = (i + 1) * BLOCK
-                one[n, at : at + BLOCK, :] = block
+                rows = slice(i * PARENT, (i + 1) * PARENT)
+                at = slice((i + 1) * BLOCK, (i + 2) * BLOCK)
+                one[n, at, :] = pool1(raw[n, rows, :])
+                flipped = raw[n, rows, :].T
+                raw_t[n, :, rows] = flipped
+                one_t[n, :, at] = (
+                    (flipped[:, :BLOCK].astype(F32) + flipped[:, BLOCK:].astype(F32)) * 0.5
+                ).astype(BF)
             one[n, 896:1024, :] = from_right[256:384, cols]
+            for at in (slice(0, 128), slice(896, 1024)):
+                one_t[n, :, at] = one[n, at, :].T
             two[n, 0:128, :] = from_left[384:512, cols]
             two[n, 128:192, :] = pool12(one[n, 0:128, :])
             two[n, 192:256, :] = pool2(raw[n, 0:256, :])
             two[n, 256:320, :] = pool2(raw[n, 1280:1536, :])
             two[n, 320:384, :] = pool12(one[n, 896:1024, :])
             two[n, 384:512, :] = from_right[384:512, cols]
-            for i in range(6):
-                rows = slice(i * PARENT, (i + 1) * PARENT)
-                raw_t[n, :, rows] = raw[n, rows, :].T
-            for i in range(8):
-                rows = slice(i * BLOCK, (i + 1) * BLOCK)
-                one_t[n, :, rows] = one[n, rows, :].T
             for i in range(4):
                 rows = slice(i * BLOCK, (i + 1) * BLOCK)
                 two_t[n, :, rows] = two[n, rows, :].T
@@ -283,15 +283,10 @@
         far2 = far_forward(
             blocks(two, 0, which2), blocks_t(two_t, 1, which2), q2, (left_bias, right_bias), p2
         )
-        acc0[...] = jnp.zeros_like(acc0)
-        g1_t, ec1, f1 = [], [], []
-        g2_t, ec2, low2 = [], [], []
-        dq0 = []
+        near0 = []
         for i in range(4):
             rows = slice(i * PARENT, i * PARENT + 3 * PARENT)
-            q = q_parents[i]
-            g = gs[i * PARENT : (i + 1) * PARENT, :]
-            s = dot_nt(raw[0, rows, :], q)
+            s = dot_nt(raw[0, rows, :], q_parents[i])
             pieces = [s[:PARENT], s[PARENT : 2 * PARENT], s[2 * PARENT :]]
             if i == 0:
                 pieces[0] = pieces[0] + left_bias
@@ -302,9 +297,19 @@
             )
             e = [jnp.exp2((x - m0) * TO_LOG2) for x in pieces]
             for n in range(3):
-                p0[n * PARENT : (n + 1) * PARENT, :] = e[n]
+                p0[i, n * PARENT : (n + 1) * PARENT, :] = e[n]
             z0 = jnp.sum(e[0] + e[1] + e[2], axis=0, keepdims=True)
             u0 = dot_nn(raw_t[1, :, rows], jnp.concatenate([x.astype(BF) for x in e], axis=0))
+            near0.append((m0, z0, u0))
+        acc0[...] = jnp.zeros_like(acc0)
+        g1_t, ec1, f1 = [], [], []
+        g2_t, ec2, low2 = [], [], []
+        dq0 = []
+        for i in range(4):
+            rows = slice(i * PARENT, i * PARENT + 3 * PARENT)
+            q = q_parents[i]
+            g = gs[i * PARENT : (i + 1) * PARENT, :]
+            m0, z0, u0 = near0[i]
             j, half = i // 2, i % 2
             lanes = slice(half * BLOCK, (half + 1) * BLOCK)
             m1, z1, u1 = (x[:, lanes] for x in far1[j])
@@ -339,7 +344,7 @@
             low2.append(lower)
             f0 = jnp.exp2(m0 * TO_LOG2 - lg)
             products = dot_nt(raw[1, rows, :], g)
-            weights = p0[...] * f0
+            weights = p0[i] * f0
             eb = weights.astype(BF)
             r = (weights * (products - dr)).astype(BF)
             acc0[1, rows, :] += dot_nn(eb, g)
@@ -430,7 +435,7 @@
             pltpu.VMEM((2, HEAD, 512), BF),
             pltpu.VMEM((1024, HEAD), BF),
             pltpu.VMEM((1024, HEAD), BF),
-            pltpu.VMEM((768, PARENT), F32),
+            pltpu.VMEM((4, 768, PARENT), F32),
             pltpu.VMEM((2, 384, PARENT), F32),
             pltpu.VMEM((384, PARENT), F32),
             pltpu.VMEM((2, 1536, HEAD), F32),
@@ -490,13 +495,62 @@
     ins, (first, second) = refs[:-2], refs[-2:]
     order = order_matrix(True)
     width = ins[0].shape[1] // 2
-    for c in range(CHUNKS):
-        for ref, side in ((ins[c], where[0]), (ins[CHUNKS + c], 1 - where[0])):
-            at = pl.ds(pl.multiple_of((side * CHUNKS + c) * width, width), width)
-            for i in range(2):
-                rows = slice(i * PARENT, (i + 1) * PARENT)
-                first[rows, at] = dot_nn(order, ref[rows, :width]).astype(BF)
-                second[rows, at] = dot_nn(order, ref[rows, width:]).astype(BF)
+    side = where[0]
+    blocks = [(side * CHUNKS + c, ins[c]) for c in range(CHUNKS)]
+    blocks += [((1 - side) * CHUNKS + 1 - LATE_CHUNK, ins[CHUNKS])]
+    for block, ref in blocks:
+        at = pl.ds(pl.multiple_of(block * width, width), width)
+        for i in range(2):
+            rows = slice(i * PARENT, (i + 1) * PARENT)
+            first[rows, at] = dot_nn(order, ref[rows, :width]).astype(BF)
+            second[rows, at] = dot_nn(order, ref[rows, width:]).astype(BF)
+
+
+def unpack_rows(where, own, got, shape):
+    out = jax.ShapeDtypeStruct(shape, BF)
+    return pl.pallas_call(
+        unpack_rows_kernel,
+        in_specs=[smem()] + [vmem()] * (CHUNKS + 1),
+        out_specs=[vmem(), vmem()],
+        out_shape=[out, out],
+        compiler_params=small(),
+        cost_estimate=light(),
+    )(where, *own, got)
+
+
+def unpack_last_kernel(where, got, first_in, second_in, first, second, held, sems):
+    del first_in, second_in
+    order = order_matrix(True)
+    width = got.shape[1] // 2
+    block = (1 - where[0]) * CHUNKS + LATE_CHUNK
+    at = pl.ds(pl.multiple_of(block * width, width), width)
+    copies = []
+    for m, ref in enumerate((first, second)):
+        for i in range(2):
+            rows = slice(i * PARENT, (i + 1) * PARENT)
+            held[m, rows, :] = dot_nn(order, got[rows, m * width : (m + 1) * width]).astype(BF)
+        copies.append(pltpu.make_async_copy(held.at[m], ref.at[:, at], sems.at[m]))
+        copies[-1].start()
+    for copy in copies:
+        copy.wait()
+
+
+def unpack_last(where, got, first, second):
+    out = jax.ShapeDtypeStruct(first.shape, BF)
+    hbm = pl.BlockSpec(memory_space=pltpu.HBM)
+    return pl.pallas_call(
+        unpack_last_kernel,
+        in_specs=[smem(), vmem(), hbm, hbm],
+        out_specs=[hbm, hbm],
+        out_shape=[out, out],
+        input_output_aliases={2: 0, 3: 1},
+        scratch_shapes=[
+            pltpu.VMEM((2, got.shape[0], got.shape[1] // 2), BF),
+            pltpu.SemaphoreType.DMA((2,)),
+        ],
+        compiler_params=small(),
+        cost_estimate=light(),
+    )(where, got, first, second)
 
 
 def unpack_columns_kernel(where, *refs):
@@ -512,10 +566,10 @@
                 second[rows, at] = dot_nt(order, ref[i, 1]).astype(BF)
 
 
-def unpack(kernel, where, own, got, shape):
+def unpack_columns(where, own, got, shape):
     out = jax.ShapeDtypeStruct(shape, BF)
     return pl.pallas_call(
-        kernel,
+        unpack_columns_kernel,
         in_specs=[smem()] + [vmem()] * (2 * CHUNKS),
         out_specs=[vmem(), vmem()],
         out_shape=[out, out],
@@ -539,11 +593,13 @@
         return lax.ppermute(x, axes, across)
 
     def beside(near, wide):
-        wide = lax.ppermute(wide, axes, wide_edges)
-        return lax.ppermute(near, axes, near_edges), wide
-
-    kv, kv_far = pack(where, key_matrix, value_matrix)
-    qg, qg_far = pack(where, queries, cotangent)
+        near = lax.ppermute(near, axes, near_edges)
+        return near, lax.ppermute(wide, axes, wide_edges)
+
+    kv_far = pack(False, where, key_matrix, value_matrix)
+    qg_far = pack(False, where, queries, cotangent)
+    packed = pack(True, where, key_matrix, value_matrix, queries, cotangent)
+    kv, qg = packed[:CHUNKS], packed[CHUNKS:]
     oq_own, oq_got, kv_own, kv_got = [], [], [], []
     back = []
     for c in range(CHUNKS):
@@ -560,8 +616,9 @@
         own, far = join(where, *back[c])
         kv_own.append(own)
         kv_got.append(swap(far))
-    attended, query_grad = unpack(unpack_columns_kernel, where, oq_own, oq_got, queries.shape)
-    key_grad, value_grad = unpack(unpack_rows_kernel, where, kv_own, kv_got, queries.shape)
+    attended, query_grad = unpack_columns(where, oq_own, oq_got, queries.shape)
+    key_grad, value_grad = unpack_rows(where, kv_own, kv_got[1 - LATE_CHUNK], queries.shape)
+    key_grad, value_grad = unpack_last(where, kv_got[LATE_CHUNK], key_grad, value_grad)
     return attended, query_grad, key_grad, value_grad
 
 

time: 71.2 us -> 71 us (level)
  Pallas kernels: 22.4 us -> 25.2 us
  waiting for transfers between devices: 23.8 us -> 21.4 us
  starting transfers between devices: 21.3 us -> 20.4 us
    ppermute x8, waiting for transfers between devices: 15.6 us -> 12.9 us  [swap(): return lax.ppermute(x, axes, across)]
    pallas_call x4 -> x6, Pallas kernels: 7.7 us -> 9.68 us  [the longest x3 3.9 us: pack(): pl.pallas_call(functools.partial(pack_kernel, own), in_specs=[smem()] + [...]
    ppermute x8, starting transfers between devices: 10.3 us -> 8.99 us  [swap(): return lax.ppermute(x, axes, across)]
    pallas_call x2, Pallas kernels: 11.9 us -> 12.8 us  [main(): pl.pallas_call(main_kernel, in_specs=[smem()] + [vmem()] * 6, out_specs=[...]
    unnamed x8 -> x12, local copies, waits for them, and re-layouts: 2.09 us -> 2.1 us
  transfers between devices with their start and end apart: 16 -> 16, of which waited for: 8 -> 8; matrix products, arithmetic and copies ran while one was open for 0% -> 0% of each run, Pallas kernels for 26% -> 32%
where the time goes in v5:
time: 71 us; the launch traced here: 70.2 us
  Pallas kernels  25.2 us (35%)
  waiting for transfers between devices  21.4 us (30%)
  starting transfers between devices  20.4 us (29%)
  local copies, waits for them, and re-layouts  2.1 us (3%)
  between operations  0.99 us (1%)
    ppermute x8, waiting for transfers between devices, swap(): return lax.ppermute(x, axes, across)  12.9 us
    pallas_call x2, Pallas kernels, main(): pl.pallas_call(main_kernel, in_specs=[smem()] + [vmem()] * 6, out_specs=[...  12.8 us
    ppermute x8, starting transfers between devices, swap(): return lax.ppermute(x, axes, across)  8.99 us
    ppermute x4, starting transfers between devices, beside(): return (near, lax.ppermute(wide, axes, wide_edges))  8.66 us
    ppermute x4, waiting for transfers between devices, beside(): return (near, lax.ppermute(wide, axes, wide_edges))  8.55 us
    pallas_call x3, Pallas kernels, pack(): pl.pallas_call(functools.partial(pack_kernel, own), in_specs=[smem()] + [...  3.9 us
    ppermute x4, starting transfers between devices, beside(): near = lax.ppermute(near, axes, near_edges)  2.73 us
    pallas_call x1, Pallas kernels, unpack_columns(): pl.pallas_call(unpack_columns_kernel, in_specs=[smem()] + [vmem()] * (2 *...  2.22 us
  transfers between devices with their start and end apart: 16, of which 8 were waited for; matrix products, arithmetic and copies ran while one was open for 0% of the time, Pallas kernels for 32%

profile of v5, /device:TPU:12, one launch (start us, length us, event | category | flops | bytes accessed | tf_op | source)
XLA Modules:
  0.0 70.2 jit_solution(18074684339752568374)
XLA Ops:
  0.7 1.0 %copy-done = bf16[512,512]{1,0:T(8,128)(2,1)S(1)} copy-done((bf16[512,512]{1,0:T(8,128)(2,1)S(1)}, bf16[512,512]{1,0:T(8,128)(2,1)}, u32[]{:S(2)}) %copy-start) | copy-done | bytes 524312
  1.8 1.0 %copy-done.2 = bf16[512,512]{1,0:T(8,128)(2,1)S(1)} copy-done((bf16[512,512]{1,0:T(8,128)(2,1)S(1)}, bf16[512,512]{1,0:T(8,128)(2,1)}, u32[]{:S(2)}) %copy-start.2) | copy-done | bytes 524312
  2.8 1.1 %shard_map.76 = (bf16[512,256]{1,0:T(8,128)(2,1)S(1)}, bf16[512,256]{1,0:T(8,128)(2,1)S(1)}) custom-call(s32[4]{0:T(128)S(1)} %pad_add_fusion.where, bf16[512,512]{1,0:T(8,128)(2,1)S(1)} %copy-done, bf16[512,512]{1,0:T(8,128)(2,1)S(1)} %copy-done.2), custom_call_target="tpu_custom_call" | custom-call | flops 1000 | bytes 1000 | tf_op jit(solution)/shard_map/pallas_call | solution.py:86
  4.0 1.6 %collective-permute-start = (bf16[512,256]{1,0:T(8,128)(2,1)S(1)}, bf16[512,256]{1,0:T(8,128)(2,1)S(1)}, u32[]{:S(2)}, u32[]{:S(2)}) collective-permute-start(bf16[512,256]{1,0:T(8,128)(2,1)S(1)} %get-tuple-element.40), channel_id=1, source_target_pairs={{0,1},{1,0},{2,3},{3,2},{4,5},{5,4},{6,7},{7,6},{8,9},{9,8},{10,11... | collective-permute-start | bytes 786440 | tf_op jit(solution)/shard_map/ppermute | solution.py:593
  6.1 1.1 %shard_map.77 = (bf16[512,256]{1,0:T(8,128)(2,1)S(1)}, bf16[512,256]{1,0:T(8,128)(2,1)S(1)}) custom-call(s32[4]{0:T(128)S(1)} %pad_add_fusion.where, bf16[512,512]{1,0:T(8,128)(2,1)S(1)} %copy-done.4, bf16[512,512]{1,0:T(8,128)(2,1)S(1)} %copy-done.5), custom_call_target="tpu_custom_call" | custom-call | flops 1000 | bytes 1000 | tf_op jit(solution)/shard_map/pallas_call | solution.py:86
  7.2 1.5 %collective-permute-start.1 = (bf16[512,256]{1,0:T(8,128)(2,1)S(1)}, bf16[512,256]{1,0:T(8,128)(2,1)S(1)}, u32[]{:S(2)}, u32[]{:S(2)}) collective-permute-start(bf16[512,256]{1,0:T(8,128)(2,1)S(1)} %get-tuple-element.42), channel_id=1, source_target_pairs={{0,1},{1,0},{2,3},{3,2},{4,5},{5,4},{6,7},{7,6},{8,9},{9,8},{10,11... | collective-permute-start | bytes 786440 | tf_op jit(solution)/shard_map/ppermute | solution.py:593
  8.8 1.6 %shard_map.75 = (bf16[512,256]{1,0:T(8,128)(2,1)S(1)}, bf16[512,256]{1,0:T(8,128)(2,1)S(1)}, bf16[512,256]{1,0:T(8,128)(2,1)S(1)}, bf16[512,256]{1,0:T(8,128)(2,1)S(1)}) custom-call(s32[4]{0:T(128)S(1)} %pad_add_fusion.where, bf16[512,512]{1,0:T(8,128)(2,1)S(1)} %copy-done.1, bf16[512,512]{1,0:T(8,128)(2,1)S(1)} %copy-done.3, ...), custom_call_target="tpu_custom_call" | custom-call | flops 1000 | bytes 1000 | tf_op jit(solution)/shard_map/pallas_call | solution.py:86
  10.4 2.8 %collective-permute-done.got.kv_got = bf16[512,256]{1,0:T(8,128)(2,1)S(1)} collective-permute-done((bf16[512,256]{1,0:T(8,128)(2,1)S(1)}, bf16[512,256]{1,0:T(8,128)(2,1)S(1)}, u32[]{:S(2)}, u32[]{:S(2)}) %collective-permute-start) | collective-permute-done | bytes 262176 | tf_op jit(solution)/shard_map/ppermute | solution.py:593
  14.0 2.5 %collective-permute-start.3 = (bf16[512,256]{1,0:T(8,128)(2,1)S(1)}, bf16[512,256]{1,0:T(8,128)(2,1)S(1)}, u32[]{:S(2)}, u32[]{:S(2)}) collective-permute-start(bf16[512,256]{1,0:T(8,128)(2,1)S(1)} %get-tuple-element.44), channel_id=1, source_target_pairs={{2,4},{3,5},{4,2},{5,3},{6,8},{7,9},{8,6},{9,7},{10,12},{11,13},{1... | collective-permute-start | bytes 786440 | tf_op jit(solution)/shard_map/ppermute | solution.py:597
  16.5 1.6 %collective-permute-start.5 = (bf16[512,256]{1,0:T(8,128)(2,1)S(1)}, bf16[512,256]{1,0:T(8,128)(2,1)S(1)}, u32[]{:S(2)}, u32[]{:S(2)}) collective-permute-start(bf16[512,256]{1,0:T(8,128)(2,1)S(1)} %get-tuple-element.49), channel_id=1, source_target_pairs={{0,1},{1,0},{2,3},{3,2},{4,5},{5,4},{6,7},{7,6},{8,9},{9,8},{10,11... | collective-permute-start | bytes 786440 | tf_op jit(solution)/shard_map/ppermute | solution.py:593
  19.6 4.9 %collective-permute-done.1.qg_got = bf16[512,256]{1,0:T(8,128)(2,1)S(1)} collective-permute-done((bf16[512,256]{1,0:T(8,128)(2,1)S(1)}, bf16[512,256]{1,0:T(8,128)(2,1)S(1)}, u32[]{:S(2)}, u32[]{:S(2)}) %collective-permute-start.1) | collective-permute-done | bytes 262176 | tf_op jit(solution)/shard_map/ppermute | solution.py:593
  24.5 2.1 %collective-permute-start.7 = (bf16[512,256]{1,0:T(8,128)(2,1)S(1)}, bf16[512,256]{1,0:T(8,128)(2,1)S(1)}, u32[]{:S(2)}, u32[]{:S(2)}) collective-permute-start(bf16[512,256]{1,0:T(8,128)(2,1)S(1)} %get-tuple-element.51), channel_id=1, source_target_pairs={{2,4},{3,5},{4,2},{5,3},{6,8},{7,9},{8,6},{9,7},{10,12},{11,13},{1... | collective-permute-start | bytes 786440 | tf_op jit(solution)/shard_map/ppermute | solution.py:597
  26.6 6.4 %shard_map.79 = (bf16[2,2,128,256]{3,2,1,0:T(8,128)(2,1)S(1)}, bf16[2,2,128,256]{3,2,1,0:T(8,128)(2,1)S(1)}, f32[1024,256]{1,0:T(8,128)S(1)}, bf16[512,256]{1,0:T(8,128)(2,1)S(1)}, bf16[512,256]{1,0:T(8,128)(2,1)S(1)}) custom-call(s32[4]{0:T(128)S(1)} %pad_add_fusion.where, bf16[512,256]{1,0:T(8,128)(2,1)S(1)} %get-tuple-element.39.own.kv_own, ...), custom_call_target="tpu_custom_call" | custom-call | flops 1000 | bytes 1000 | tf_op jit(solution)/shard_map/pallas_call | solution.py:418
  33.0 1.6 %collective-permute-start.8 = (bf16[2,2,128,256]{3,2,1,0:T(8,128)(2,1)S(1)}, bf16[2,2,128,256]{3,2,1,0:T(8,128)(2,1)S(1)}, u32[]{:S(2)}, u32[]{:S(2)}) collective-permute-start(bf16[2,2,128,256]{3,2,1,0:T(8,128)(2,1)S(1)} %get-tuple-element.53), channel_id=1, source_target_pairs={{0,1},{1,0},{2,3},{3,2},{4,5},{5,4},{6,7},{7,6},{8,9},{9,8},{10,11... | collective-permute-start | bytes 786440 | tf_op jit(solution)/shard_map/ppermute | solution.py:593
  35.0 6.4 %shard_map.81 = (bf16[2,2,128,256]{3,2,1,0:T(8,128)(2,1)S(1)}, bf16[2,2,128,256]{3,2,1,0:T(8,128)(2,1)S(1)}, f32[1024,256]{1,0:T(8,128)S(1)}, bf16[512,256]{1,0:T(8,128)(2,1)S(1)}, bf16[512,256]{1,0:T(8,128)(2,1)S(1)}) custom-call(s32[4]{0:T(128)S(1)} %pad_add_fusion.where, bf16[512,256]{1,0:T(8,128)(2,1)S(1)} %get-tuple-element.46.own.kv_own, ...), custom_call_target="tpu_custom_call" | custom-call | flops 1000 | bytes 1000 | tf_op jit(solution)/shard_map/pallas_call | solution.py:418
  42.4 2.0 %collective-permute-start.14 = (bf16[512,256]{1,0:T(8,128)(2,1)S(1)}, bf16[512,256]{1,0:T(8,128)(2,1)S(1)}, u32[]{:S(2)}, u32[]{:S(2)}) collective-permute-start(bf16[512,256]{1,0:T(8,128)(2,1)S(1)} %get-tuple-element.67), channel_id=1, source_target_pairs={{2,4},{3,5},{4,2},{5,3},{6,8},{7,9},{8,6},{9,7},{10,12},{11,13},{1... | collective-permute-start | bytes 786440 | tf_op jit(solution)/shard_map/ppermute | solution.py:597
  44.4 1.6 %collective-permute-start.10 = (bf16[512,256]{1,0:T(8,128)(2,1)S(1)}, bf16[512,256]{1,0:T(8,128)(2,1)S(1)}, u32[]{:S(2)}, u32[]{:S(2)}) collective-permute-start(bf16[512,256]{1,0:T(8,128)(2,1)S(1)} %get-tuple-element.61), channel_id=1, source_target_pairs={{0,2},{1,3},{2,0},{3,1},{4,6},{5,7},{6,4},{7,5},{8,10},{9,11},{10,... | collective-permute-start | bytes 786440 | tf_op jit(solution)/shard_map/ppermute | solution.py:596
  46.0 2.0 %collective-permute-start.11 = (bf16[512,256]{1,0:T(8,128)(2,1)S(1)}, bf16[512,256]{1,0:T(8,128)(2,1)S(1)}, u32[]{:S(2)}, u32[]{:S(2)}) collective-permute-start(bf16[512,256]{1,0:T(8,128)(2,1)S(1)} %get-tuple-element.62), channel_id=1, source_target_pairs={{2,4},{3,5},{4,2},{5,3},{6,8},{7,9},{8,6},{9,7},{10,12},{11,13},{1... | collective-permute-start | bytes 786440 | tf_op jit(solution)/shard_map/ppermute | solution.py:597
  49.0 6.7 %collective-permute-done.14.wide_got = bf16[512,256]{1,0:T(8,128)(2,1)S(1)} collective-permute-done((bf16[512,256]{1,0:T(8,128)(2,1)S(1)}, bf16[512,256]{1,0:T(8,128)(2,1)S(1)}, u32[]{:S(2)}, u32[]{:S(2)}) %collective-permute-start.14) | collective-permute-done | bytes 262176 | tf_op jit(solution)/shard_map/ppermute | solution.py:597
  57.0 1.5 %collective-permute-done.11.wide_got = bf16[512,256]{1,0:T(8,128)(2,1)S(1)} collective-permute-done((bf16[512,256]{1,0:T(8,128)(2,1)S(1)}, bf16[512,256]{1,0:T(8,128)(2,1)S(1)}, u32[]{:S(2)}, u32[]{:S(2)}) %collective-permute-start.11) | collective-permute-done | bytes 262176 | tf_op jit(solution)/shard_map/ppermute | solution.py:597
  59.8 2.2 %shard_map.82 = (bf16[512,512]{1,0:T(8,128)(2,1)}, bf16[512,512]{1,0:T(8,128)(2,1)}) custom-call(s32[4]{0:T(128)S(1)} %pad_add_fusion.where, bf16[2,2,128,256]{3,2,1,0:T(8,128)(2,1)S(1)} %get-tuple-element.45.refs_0_, bf16[2,2,128,256]{3,2,1,0:T(8,128)(2,1)S(1)} %get-tuple-element.52.refs_1_, bf16[2,2,128,256]{3,2,1,0:T(8,128)(2,1)S(1)} %collective-permute-done.8.refs_2_, ...), custom_call_target="tpu_custom_call" | custom-call | flops 1000 | bytes 1000 | tf_op jit(solution)/shard_map/pallas_call | solution.py:571
  62.0 3.6 %collective-permute-done.15.refs_2_ = bf16[512,256]{1,0:T(8,128)(2,1)S(1)} collective-permute-done((bf16[512,256]{1,0:T(8,128)(2,1)S(1)}, bf16[512,256]{1,0:T(8,128)(2,1)S(1)}, u32[]{:S(2)}, u32[]{:S(2)}) %collective-permute-start.15) | collective-permute-done | bytes 262176 | tf_op jit(solution)/shard_map/ppermute | solution.py:593
  65.7 2.1 %shard_map.85 = (bf16[512,512]{1,0:T(8,128)(2,1)}, bf16[512,512]{1,0:T(8,128)(2,1)}) custom-call(s32[4]{0:T(128)S(1)} %pad_add_fusion.where, bf16[512,256]{1,0:T(8,128)(2,1)S(1)} %get-tuple-element.64.refs_0_, bf16[512,256]{1,0:T(8,128)(2,1)S(1)} %get-tuple-element.68.refs_1_, bf16[512,256]{1,0:T(8,128)(2,1)S(1)} %collective-permute-done.15.refs_2_), custom_call_target="tpu_custom_call" | custom-call | flops 1000 | bytes 1000 | tf_op jit(solution)/shard_map/pallas_call | solution.py:511
  68.5 1.5 %shard_map.86 = (bf16[512,512]{1,0:T(8,128)(2,1)}, bf16[512,512]{1,0:T(8,128)(2,1)}) custom-call(s32[4]{0:T(128)S(1)} %pad_add_fusion.where, bf16[512,256]{1,0:T(8,128)(2,1)S(1)} %collective-permute-done.12.got, bf16[512,512]{1,0:T(8,128)(2,1)} %get-tuple-element.70.first_in, ...), custom_call_target="tpu_custom_call", output_to_operand_aliasing={{0}: (2, {}), {1}: (3, {})} | custom-call | flops 1000 | bytes 1000 | tf_op jit(solution)/shard_map/pallas_call | solution.py:541
  (33 shorter events, 8.7 us)
Async XLA Ops:
  0.7 1.0 %copy-start = (bf16[512,512]{1,0:T(8,128)(2,1)S(1)}, bf16[512,512]{1,0:T(8,128)(2,1)}, u32[]{:S(2)}) copy-start(bf16[512,512]{1,0:T(8,128)(2,1)} %refs_0_.4) | copy-start | bytes 1572868
  1.8 1.0 %copy-start.2 = (bf16[512,512]{1,0:T(8,128)(2,1)S(1)}, bf16[512,512]{1,0:T(8,128)(2,1)}, u32[]{:S(2)}) copy-start(bf16[512,512]{1,0:T(8,128)(2,1)} %refs_1_.4) | copy-start | bytes 1572868
  2.8 3.2 %copy-start.4 = (bf16[512,512]{1,0:T(8,128)(2,1)S(1)}, bf16[512,512]{1,0:T(8,128)(2,1)}, u32[]{:S(2)}) copy-start(bf16[512,512]{1,0:T(8,128)(2,1)} %refs_0_.5) | copy-start | bytes 1572868
  2.8 3.2 %copy-start.5 = (bf16[512,512]{1,0:T(8,128)(2,1)S(1)}, bf16[512,512]{1,0:T(8,128)(2,1)}, u32[]{:S(2)}) copy-start(bf16[512,512]{1,0:T(8,128)(2,1)} %refs_1_.5) | copy-start | bytes 1572868
  4.0 9.3 %collective-permute-start = (bf16[512,256]{1,0:T(8,128)(2,1)S(1)}, bf16[512,256]{1,0:T(8,128)(2,1)S(1)}, u32[]{:S(2)}, u32[]{:S(2)}) collective-permute-start(bf16[512,256]{1,0:T(8,128)(2,1)S(1)} %get-tuple-element.40), channel_id=1, source_target_pairs={{0,1},{1,0},{2,3},{3,2},{4,5},{5,4},{6,7},{7,6},{8,9},{9,8},{10,11... | collective-permute-start | bytes 786440 | tf_op jit(solution)/shard_map/ppermute | solution.py:593
  5.5 3.2 %copy-start.1 = (bf16[512,512]{1,0:T(8,128)(2,1)S(1)}, bf16[512,512]{1,0:T(8,128)(2,1)}, u32[]{:S(2)}) copy-start(bf16[512,512]{1,0:T(8,128)(2,1)} %refs_0_.4) | copy-start | bytes 1572868
  5.5 3.2 %copy-start.3 = (bf16[512,512]{1,0:T(8,128)(2,1)S(1)}, bf16[512,512]{1,0:T(8,128)(2,1)}, u32[]{:S(2)}) copy-start(bf16[512,512]{1,0:T(8,128)(2,1)} %refs_1_.4) | copy-start | bytes 1572868
  5.5 13.3 %collective-permute-start.4 = (bf16[512,256]{1,0:T(8,128)(2,1)S(1)}, bf16[512,256]{1,0:T(8,128)(2,1)S(1)}, u32[]{:S(2)}, u32[]{:S(2)}) collective-permute-start(bf16[512,256]{1,0:T(8,128)(2,1)S(1)} %get-tuple-element.47), channel_id=1, source_target_pairs={{0,1},{1,0},{2,3},{3,2},{4,5},{5,4},{6,7},{7,6},{8,9},{9,8},{10,11... | collective-permute-start | bytes 786440 | tf_op jit(solution)/shard_map/ppermute | solution.py:593
  7.2 17.3 %collective-permute-start.1 = (bf16[512,256]{1,0:T(8,128)(2,1)S(1)}, bf16[512,256]{1,0:T(8,128)(2,1)S(1)}, u32[]{:S(2)}, u32[]{:S(2)}) collective-permute-start(bf16[512,256]{1,0:T(8,128)(2,1)S(1)} %get-tuple-element.42), channel_id=1, source_target_pairs={{0,1},{1,0},{2,3},{3,2},{4,5},{5,4},{6,7},{7,6},{8,9},{9,8},{10,11... | collective-permute-start | bytes 786440 | tf_op jit(solution)/shard_map/ppermute | solution.py:593
  13.9 12.7 %collective-permute-start.2 = (bf16[512,256]{1,0:T(8,128)(2,1)S(1)}, bf16[512,256]{1,0:T(8,128)(2,1)S(1)}, u32[]{:S(2)}, u32[]{:S(2)}) collective-permute-start(bf16[512,256]{1,0:T(8,128)(2,1)S(1)} %get-tuple-element.43), channel_id=1, source_target_pairs={{0,2},{1,3},{2,0},{3,1},{4,6},{5,7},{6,4},{7,5},{8,10},{9,11},{10,... | collective-permute-start | bytes 786440 | tf_op jit(solution)/shard_map/ppermute | solution.py:596
  14.0 12.6 %collective-permute-start.3 = (bf16[512,256]{1,0:T(8,128)(2,1)S(1)}, bf16[512,256]{1,0:T(8,128)(2,1)S(1)}, u32[]{:S(2)}, u32[]{:S(2)}) collective-permute-start(bf16[512,256]{1,0:T(8,128)(2,1)S(1)} %get-tuple-element.44), channel_id=1, source_target_pairs={{2,4},{3,5},{4,2},{5,3},{6,8},{7,9},{8,6},{9,7},{10,12},{11,13},{1... | collective-permute-start | bytes 786440 | tf_op jit(solution)/shard_map/ppermute | solution.py:597
  16.5 18.1 %collective-permute-start.5 = (bf16[512,256]{1,0:T(8,128)(2,1)S(1)}, bf16[512,256]{1,0:T(8,128)(2,1)S(1)}, u32[]{:S(2)}, u32[]{:S(2)}) collective-permute-start(bf16[512,256]{1,0:T(8,128)(2,1)S(1)} %get-tuple-element.49), channel_id=1, source_target_pairs={{0,1},{1,0},{2,3},{3,2},{4,5},{5,4},{6,7},{7,6},{8,9},{9,8},{10,11... | collective-permute-start | bytes 786440 | tf_op jit(solution)/shard_map/ppermute | solution.py:593
  19.5 15.0 %collective-permute-start.6 = (bf16[512,256]{1,0:T(8,128)(2,1)S(1)}, bf16[512,256]{1,0:T(8,128)(2,1)S(1)}, u32[]{:S(2)}, u32[]{:S(2)}) collective-permute-start(bf16[512,256]{1,0:T(8,128)(2,1)S(1)} %get-tuple-element.50), channel_id=1, source_target_pairs={{0,2},{1,3},{2,0},{3,1},{4,6},{5,7},{6,4},{7,5},{8,10},{9,11},{10,... | collective-permute-start | bytes 786440 | tf_op jit(solution)/shard_map/ppermute | solution.py:596
  24.5 10.5 %collective-permute-start.7 = (bf16[512,256]{1,0:T(8,128)(2,1)S(1)}, bf16[512,256]{1,0:T(8,128)(2,1)S(1)}, u32[]{:S(2)}, u32[]{:S(2)}) collective-permute-start(bf16[512,256]{1,0:T(8,128)(2,1)S(1)} %get-tuple-element.51), channel_id=1, source_target_pairs={{2,4},{3,5},{4,2},{5,3},{6,8},{7,9},{8,6},{9,7},{10,12},{11,13},{1... | collective-permute-start | bytes 786440 | tf_op jit(solution)/shard_map/ppermute | solution.py:597
  33.0 11.4 %collective-permute-start.8 = (bf16[2,2,128,256]{3,2,1,0:T(8,128)(2,1)S(1)}, bf16[2,2,128,256]{3,2,1,0:T(8,128)(2,1)S(1)}, u32[]{:S(2)}, u32[]{:S(2)}) collective-permute-start(bf16[2,2,128,256]{3,2,1,0:T(8,128)(2,1)S(1)} %get-tuple-element.53), channel_id=1, source_target_pairs={{0,1},{1,0},{2,3},{3,2},{4,5},{5,4},{6,7},{7,6},{8,9},{9,8},{10,11... | collective-permute-start | bytes 786440 | tf_op jit(solution)/shard_map/ppermute | solution.py:593
  41.4 7.6 %collective-permute-start.13 = (bf16[512,256]{1,0:T(8,128)(2,1)S(1)}, bf16[512,256]{1,0:T(8,128)(2,1)S(1)}, u32[]{:S(2)}, u32[]{:S(2)}) collective-permute-start(bf16[512,256]{1,0:T(8,128)(2,1)S(1)} %get-tuple-element.66), channel_id=1, source_target_pairs={{0,2},{1,3},{2,0},{3,1},{4,6},{5,7},{6,4},{7,5},{8,10},{9,11},{10,... | collective-permute-start | bytes 786440 | tf_op jit(solution)/shard_map/ppermute | solution.py:596
  42.4 13.3 %collective-permute-start.14 = (bf16[512,256]{1,0:T(8,128)(2,1)S(1)}, bf16[512,256]{1,0:T(8,128)(2,1)S(1)}, u32[]{:S(2)}, u32[]{:S(2)}) collective-permute-start(bf16[512,256]{1,0:T(8,128)(2,1)S(1)} %get-tuple-element.67), channel_id=1, source_target_pairs={{2,4},{3,5},{4,2},{5,3},{6,8},{7,9},{8,6},{9,7},{10,12},{11,13},{1... | collective-permute-start | bytes 786440 | tf_op jit(solution)/shard_map/ppermute | solution.py:597
  44.4 12.6 %collective-permute-start.10 = (bf16[512,256]{1,0:T(8,128)(2,1)S(1)}, bf16[512,256]{1,0:T(8,128)(2,1)S(1)}, u32[]{:S(2)}, u32[]{:S(2)}) collective-permute-start(bf16[512,256]{1,0:T(8,128)(2,1)S(1)} %get-tuple-element.61), channel_id=1, source_target_pairs={{0,2},{1,3},{2,0},{3,1},{4,6},{5,7},{6,4},{7,5},{8,10},{9,11},{10,... | collective-permute-start | bytes 786440 | tf_op jit(solution)/shard_map/ppermute | solution.py:596
  46.0 12.5 %collective-permute-start.11 = (bf16[512,256]{1,0:T(8,128)(2,1)S(1)}, bf16[512,256]{1,0:T(8,128)(2,1)S(1)}, u32[]{:S(2)}, u32[]{:S(2)}) collective-permute-start(bf16[512,256]{1,0:T(8,128)(2,1)S(1)} %get-tuple-element.62), channel_id=1, source_target_pairs={{2,4},{3,5},{4,2},{5,3},{6,8},{7,9},{8,6},{9,7},{10,12},{11,13},{1... | collective-permute-start | bytes 786440 | tf_op jit(solution)/shard_map/ppermute | solution.py:597
  48.1 11.8 %collective-permute-start.9 = (bf16[2,2,128,256]{3,2,1,0:T(8,128)(2,1)S(1)}, bf16[2,2,128,256]{3,2,1,0:T(8,128)(2,1)S(1)}, u32[]{:S(2)}, u32[]{:S(2)}) collective-permute-start(bf16[2,2,128,256]{3,2,1,0:T(8,128)(2,1)S(1)} %get-tuple-element.57), channel_id=1, source_target_pairs={{0,1},{1,0},{2,3},{3,2},{4,5},{5,4},{6,7},{7,6},{8,9},{9,8},{10,11... | collective-permute-start | bytes 786440 | tf_op jit(solution)/shard_map/ppermute | solution.py:593
  56.4 9.3 %collective-permute-start.15 = (bf16[512,256]{1,0:T(8,128)(2,1)S(1)}, bf16[512,256]{1,0:T(8,128)(2,1)S(1)}, u32[]{:S(2)}, u32[]{:S(2)}) collective-permute-start(bf16[512,256]{1,0:T(8,128)(2,1)S(1)} %get-tuple-element.69), channel_id=1, source_target_pairs={{0,1},{1,0},{2,3},{3,2},{4,5},{5,4},{6,7},{7,6},{8,9},{9,8},{10,11... | collective-permute-start | bytes 786440 | tf_op jit(solution)/shard_map/ppermute | solution.py:593
  59.2 9.3 %collective-permute-start.12 = (bf16[512,256]{1,0:T(8,128)(2,1)S(1)}, bf16[512,256]{1,0:T(8,128)(2,1)S(1)}, u32[]{:S(2)}, u32[]{:S(2)}) collective-permute-start(bf16[512,256]{1,0:T(8,128)(2,1)S(1)} %get-tuple-element.63), channel_id=1, source_target_pairs={{0,1},{1,0},{2,3},{3,2},{4,5},{5,4},{6,7},{7,6},{8,9},{9,8},{10,11... | collective-permute-start | bytes 786440 | tf_op jit(solution)/shard_map/ppermute | solution.py:593

commit v6 on v5

--- a/solution.py
+++ b/solution.py
@@ -209,7 +209,7 @@
 
 
 def main_kernel(
-    where, kv_own, kv_got, qg_own, qg_got, near_got, wide_got,
+    where, kv_own, kv_got, near_got, wide_got, qg_own, qg_got,
     oq_own, oq_far, grad, near_out, wide_out,
     raw, raw_t, one, one_t, two, two_t, qs, gs, p0, p1, p2, acc0, acc1, acc2, oq, halos,
 ):
@@ -283,10 +283,15 @@
         far2 = far_forward(
             blocks(two, 0, which2), blocks_t(two_t, 1, which2), q2, (left_bias, right_bias), p2
         )
-        near0 = []
+        acc0[...] = jnp.zeros_like(acc0)
+        g1_t, ec1, f1 = [], [], []
+        g2_t, ec2, low2 = [], [], []
+        dq0 = []
         for i in range(4):
             rows = slice(i * PARENT, i * PARENT + 3 * PARENT)
-            s = dot_nt(raw[0, rows, :], q_parents[i])
+            q = q_parents[i]
+            g = gs[i * PARENT : (i + 1) * PARENT, :]
+            s = dot_nt(raw[0, rows, :], q)
             pieces = [s[:PARENT], s[PARENT : 2 * PARENT], s[2 * PARENT :]]
             if i == 0:
                 pieces[0] = pieces[0] + left_bias
@@ -297,19 +302,9 @@
             )
             e = [jnp.exp2((x - m0) * TO_LOG2) for x in pieces]
             for n in range(3):
-                p0[i, n * PARENT : (n + 1) * PARENT, :] = e[n]
+                p0[n * PARENT : (n + 1) * PARENT, :] = e[n]
             z0 = jnp.sum(e[0] + e[1] + e[2], axis=0, keepdims=True)
             u0 = dot_nn(raw_t[1, :, rows], jnp.concatenate([x.astype(BF) for x in e], axis=0))
-            near0.append((m0, z0, u0))
-        acc0[...] = jnp.zeros_like(acc0)
-        g1_t, ec1, f1 = [], [], []
-        g2_t, ec2, low2 = [], [], []
-        dq0 = []
-        for i in range(4):
-            rows = slice(i * PARENT, i * PARENT + 3 * PARENT)
-            q = q_parents[i]
-            g = gs[i * PARENT : (i + 1) * PARENT, :]
-            m0, z0, u0 = near0[i]
             j, half = i // 2, i % 2
             lanes = slice(half * BLOCK, (half + 1) * BLOCK)
             m1, z1, u1 = (x[:, lanes] for x in far1[j])
@@ -344,7 +339,7 @@
             low2.append(lower)
             f0 = jnp.exp2(m0 * TO_LOG2 - lg)
             products = dot_nt(raw[1, rows, :], g)
-            weights = p0[i] * f0
+            weights = p0[...] * f0
             eb = weights.astype(BF)
             r = (weights * (products - dr)).astype(BF)
             acc0[1, rows, :] += dot_nn(eb, g)
@@ -410,7 +405,7 @@
     wide_out[...] = halos[odd]
 
 
-def main(where, kv_own, kv_got, qg_own, qg_got, near_got, wide_got):
+def main(where, kv_own, kv_got, near_got, wide_got, qg_own, qg_got):
     rows, both = kv_own.shape
     width = both // 2
     oq_shape = jax.ShapeDtypeStruct((2, 2, width, PARENT), BF)
@@ -435,7 +430,7 @@
             pltpu.VMEM((2, HEAD, 512), BF),
             pltpu.VMEM((1024, HEAD), BF),
             pltpu.VMEM((1024, HEAD), BF),
-            pltpu.VMEM((4, 768, PARENT), F32),
+            pltpu.VMEM((768, PARENT), F32),
             pltpu.VMEM((2, 384, PARENT), F32),
             pltpu.VMEM((384, PARENT), F32),
             pltpu.VMEM((2, 1536, HEAD), F32),
@@ -446,7 +441,7 @@
         ],
         compiler_params=pltpu.CompilerParams(vmem_limit_bytes=24 * 1024 * 1024),
         cost_estimate=light(),
-    )(where, kv_own, kv_got, qg_own, qg_got, near_got, wide_got)
+    )(where, kv_own, kv_got, near_got, wide_got, qg_own, qg_got)
 
 
 def join_kernel(where, grad, near_got, wide_got, own, far):
@@ -604,9 +599,9 @@
     back = []
     for c in range(CHUNKS):
         got_kv = swap(kv_far[c])
-        got_qg = swap(qg_far[c])
-        halos = beside(*halo(where, kv[c], got_kv))
-        own, far, grad, near, wide = main(where, kv[c], got_kv, qg[c], got_qg, *halos)
+        near, wide, far = lax.optimization_barrier((*halo(where, kv[c], got_kv), qg_far[c]))
+        near, wide = beside(near, wide)
+        own, far, grad, near, wide = main(where, kv[c], got_kv, near, wide, qg[c], swap(far))
         oq_own.append(own)
         oq_got.append(swap(far))
         if c + 1 < CHUNKS:

time: 71 us -> 70 us (0.986)
  the two profiles are of different devices: /device:TPU:12 before, /device:TPU:9 now
where the time goes in v6:
time: 70 us; the launch traced here: 69.8 us
  Pallas kernels  24.4 us (35%)
  starting transfers between devices  24.3 us (35%)
  waiting for transfers between devices  17.9 us (26%)
  local copies, waits for them, and re-layouts  2.1 us (3%)
  between operations  0.99 us (1%)
    ppermute x4, starting transfers between devices, beside(): return (near, lax.ppermute(wide, axes, wide_edges))  12.7 us
    pallas_call x2, Pallas kernels, main(): pl.pallas_call(main_kernel, in_specs=[smem()] + [vmem()] * 6, out_specs=[...  12 us
    ppermute x4, waiting for transfers between devices, beside(): return (near, lax.ppermute(wide, axes, wide_edges))  10 us
    ppermute x8, waiting for transfers between devices, swap(): return lax.ppermute(x, axes, across)  7.88 us
    ppermute x8, starting transfers between devices, swap(): return lax.ppermute(x, axes, across)  7.51 us
    ppermute x4, starting transfers between devices, beside(): near = lax.ppermute(near, axes, near_edges)  4.12 us
    pallas_call x3, Pallas kernels, pack(): pl.pallas_call(functools.partial(pack_kernel, own), in_specs=[smem()] + [...  3.87 us
    pallas_call x1, Pallas kernels, unpack_columns(): pl.pallas_call(unpack_columns_kernel, in_specs=[smem()] + [vmem()] * (2 *...  2.21 us
  transfers between devices with their start and end apart: 16, of which 6 were waited for; matrix products, arithmetic and copies ran while one was open for 0% of the time, Pallas kernels for 31%

profile of v6, /device:TPU:9, one launch (start us, length us, event | category | flops | bytes accessed | tf_op | source)
XLA Modules:
  0.0 69.8 jit_solution(10813016592100777224)
XLA Ops:
  0.7 1.0 %copy-done = bf16[512,512]{1,0:T(8,128)(2,1)S(1)} copy-done((bf16[512,512]{1,0:T(8,128)(2,1)S(1)}, bf16[512,512]{1,0:T(8,128)(2,1)}, u32[]{:S(2)}) %copy-start) | copy-done | bytes 524312
  1.8 1.0 %copy-done.2 = bf16[512,512]{1,0:T(8,128)(2,1)S(1)} copy-done((bf16[512,512]{1,0:T(8,128)(2,1)S(1)}, bf16[512,512]{1,0:T(8,128)(2,1)}, u32[]{:S(2)}) %copy-start.2) | copy-done | bytes 524312
  2.8 1.1 %shard_map.76 = (bf16[512,256]{1,0:T(8,128)(2,1)S(1)}, bf16[512,256]{1,0:T(8,128)(2,1)S(1)}) custom-call(s32[4]{0:T(128)S(1)} %pad_add_fusion.where, bf16[512,512]{1,0:T(8,128)(2,1)S(1)} %copy-done, bf16[512,512]{1,0:T(8,128)(2,1)S(1)} %copy-done.2), custom_call_target="tpu_custom_call" | custom-call | flops 1000 | bytes 1000 | tf_op jit(solution)/shard_map/pallas_call | solution.py:86
  4.0 1.3 %collective-permute-start = (bf16[512,256]{1,0:T(8,128)(2,1)S(1)}, bf16[512,256]{1,0:T(8,128)(2,1)S(1)}, u32[]{:S(2)}, u32[]{:S(2)}) collective-permute-start(bf16[512,256]{1,0:T(8,128)(2,1)S(1)} %get-tuple-element.46), channel_id=1, source_target_pairs={{0,1},{1,0},{2,3},{3,2},{4,5},{5,4},{6,7},{7,6},{8,9},{9,8},{10,11... | collective-permute-start | bytes 786440 | tf_op jit(solution)/shard_map/ppermute | solution.py:588
  5.5 1.1 %shard_map.78 = (bf16[512,256]{1,0:T(8,128)(2,1)S(1)}, bf16[512,256]{1,0:T(8,128)(2,1)S(1)}) custom-call(s32[4]{0:T(128)S(1)} %pad_add_fusion.where, bf16[512,512]{1,0:T(8,128)(2,1)S(1)} %copy-done.4, bf16[512,512]{1,0:T(8,128)(2,1)S(1)} %copy-done.5), custom_call_target="tpu_custom_call" | custom-call | flops 1000 | bytes 1000 | tf_op jit(solution)/shard_map/pallas_call | solution.py:86
  6.7 1.6 %shard_map.75 = (bf16[512,256]{1,0:T(8,128)(2,1)S(1)}, bf16[512,256]{1,0:T(8,128)(2,1)S(1)}, bf16[512,256]{1,0:T(8,128)(2,1)S(1)}, bf16[512,256]{1,0:T(8,128)(2,1)S(1)}) custom-call(s32[4]{0:T(128)S(1)} %pad_add_fusion.where, bf16[512,512]{1,0:T(8,128)(2,1)S(1)} %copy-done.1, bf16[512,512]{1,0:T(8,128)(2,1)S(1)} %copy-done.3, ...), custom_call_target="tpu_custom_call" | custom-call | flops 1000 | bytes 1000 | tf_op jit(solution)/shard_map/pallas_call | solution.py:86
  8.3 2.9 %collective-permute-done.got.kv_got = bf16[512,256]{1,0:T(8,128)(2,1)S(1)} collective-permute-done((bf16[512,256]{1,0:T(8,128)(2,1)S(1)}, bf16[512,256]{1,0:T(8,128)(2,1)S(1)}, u32[]{:S(2)}, u32[]{:S(2)}) %collective-permute-start) | collective-permute-done | bytes 262176 | tf_op jit(solution)/shard_map/ppermute | solution.py:588
  11.9 2.8 %collective-permute-start.1 = (bf16[512,256]{1,0:T(8,128)(2,1)S(1)}, bf16[512,256]{1,0:T(8,128)(2,1)S(1)}, u32[]{:S(2)}, u32[]{:S(2)}) collective-permute-start(bf16[512,256]{1,0:T(8,128)(2,1)S(1)} %get-tuple-element.50), channel_id=1, source_target_pairs={{0,2},{1,3},{2,0},{3,1},{4,6},{5,7},{6,4},{7,5},{8,10},{9,11},{10,... | collective-permute-start | bytes 786440 | tf_op jit(solution)/shard_map/ppermute | solution.py:591
  14.7 3.0 %collective-permute-start.2 = (bf16[512,256]{1,0:T(8,128)(2,1)S(1)}, bf16[512,256]{1,0:T(8,128)(2,1)S(1)}, u32[]{:S(2)}, u32[]{:S(2)}) collective-permute-start(bf16[512,256]{1,0:T(8,128)(2,1)S(1)} %get-tuple-element.51), channel_id=1, source_target_pairs={{2,4},{3,5},{4,2},{5,3},{6,8},{7,9},{8,6},{9,7},{10,12},{11,13},{1... | collective-permute-start | bytes 786440 | tf_op jit(solution)/shard_map/ppermute | solution.py:592
  17.7 1.3 %collective-permute-start.3 = (bf16[512,256]{1,0:T(8,128)(2,1)S(1)}, bf16[512,256]{1,0:T(8,128)(2,1)S(1)}, u32[]{:S(2)}, u32[]{:S(2)}) collective-permute-start(bf16[512,256]{1,0:T(8,128)(2,1)S(1)} %get-tuple-element.53), channel_id=1, source_target_pairs={{0,1},{1,0},{2,3},{3,2},{4,5},{5,4},{6,7},{7,6},{8,9},{9,8},{10,11... | collective-permute-start | bytes 786440 | tf_op jit(solution)/shard_map/ppermute | solution.py:588
  20.4 3.1 %collective-permute-start.6 = (bf16[512,256]{1,0:T(8,128)(2,1)S(1)}, bf16[512,256]{1,0:T(8,128)(2,1)S(1)}, u32[]{:S(2)}, u32[]{:S(2)}) collective-permute-start(bf16[512,256]{1,0:T(8,128)(2,1)S(1)} %get-tuple-element.61), channel_id=1, source_target_pairs={{2,4},{3,5},{4,2},{5,3},{6,8},{7,9},{8,6},{9,7},{10,12},{11,13},{1... | collective-permute-start | bytes 786440 | tf_op jit(solution)/shard_map/ppermute | solution.py:592
  23.8 1.7 %collective-permute-done.2.wide_got = bf16[512,256]{1,0:T(8,128)(2,1)S(1)} collective-permute-done((bf16[512,256]{1,0:T(8,128)(2,1)S(1)}, bf16[512,256]{1,0:T(8,128)(2,1)S(1)}, u32[]{:S(2)}, u32[]{:S(2)}) %collective-permute-start.2) | collective-permute-done | bytes 262176 | tf_op jit(solution)/shard_map/ppermute | solution.py:592
  25.5 6.0 %shard_map.79 = (bf16[2,2,128,256]{3,2,1,0:T(8,128)(2,1)S(1)}, bf16[2,2,128,256]{3,2,1,0:T(8,128)(2,1)S(1)}, f32[1024,256]{1,0:T(8,128)S(1)}, bf16[512,256]{1,0:T(8,128)(2,1)S(1)}, bf16[512,256]{1,0:T(8,128)(2,1)S(1)}) custom-call(s32[4]{0:T(128)S(1)} %pad_add_fusion.where, bf16[512,256]{1,0:T(8,128)(2,1)S(1)} %get-tuple-element.45.own.kv_own, ...), custom_call_target="tpu_custom_call" | custom-call | flops 1000 | bytes 1000 | tf_op jit(solution)/shard_map/pallas_call | solution.py:413
  31.5 4.1 %collective-permute-start.8 = (bf16[2,2,128,256]{3,2,1,0:T(8,128)(2,1)S(1)}, bf16[2,2,128,256]{3,2,1,0:T(8,128)(2,1)S(1)}, u32[]{:S(2)}, u32[]{:S(2)}) collective-permute-start(bf16[2,2,128,256]{3,2,1,0:T(8,128)(2,1)S(1)} %get-tuple-element.65), channel_id=1, source_target_pairs={{0,1},{1,0},{2,3},{3,2},{4,5},{5,4},{6,7},{7,6},{8,9},{9,8},{10,11... | collective-permute-start | bytes 786440 | tf_op jit(solution)/shard_map/ppermute | solution.py:588
  35.6 6.0 %shard_map.81 = (bf16[2,2,128,256]{3,2,1,0:T(8,128)(2,1)S(1)}, bf16[2,2,128,256]{3,2,1,0:T(8,128)(2,1)S(1)}, f32[1024,256]{1,0:T(8,128)S(1)}, bf16[512,256]{1,0:T(8,128)(2,1)S(1)}, bf16[512,256]{1,0:T(8,128)(2,1)S(1)}) custom-call(s32[4]{0:T(128)S(1)} %pad_add_fusion.where, bf16[512,256]{1,0:T(8,128)(2,1)S(1)} %get-tuple-element.55.own.kv_own, ...), custom_call_target="tpu_custom_call" | custom-call | flops 1000 | bytes 1000 | tf_op jit(solution)/shard_map/pallas_call | solution.py:413
  41.6 1.9 %collective-permute-start.14 = (bf16[512,256]{1,0:T(8,128)(2,1)S(1)}, bf16[512,256]{1,0:T(8,128)(2,1)S(1)}, u32[]{:S(2)}, u32[]{:S(2)}) collective-permute-start(bf16[512,256]{1,0:T(8,128)(2,1)S(1)} %get-tuple-element.79), channel_id=1, source_target_pairs={{2,4},{3,5},{4,2},{5,3},{6,8},{7,9},{8,6},{9,7},{10,12},{11,13},{1... | collective-permute-start | bytes 786440 | tf_op jit(solution)/shard_map/ppermute | solution.py:592
  44.1 4.6 %collective-permute-start.11 = (bf16[512,256]{1,0:T(8,128)(2,1)S(1)}, bf16[512,256]{1,0:T(8,128)(2,1)S(1)}, u32[]{:S(2)}, u32[]{:S(2)}) collective-permute-start(bf16[512,256]{1,0:T(8,128)(2,1)S(1)} %get-tuple-element.74), channel_id=1, source_target_pairs={{2,4},{3,5},{4,2},{5,3},{6,8},{7,9},{8,6},{9,7},{10,12},{11,13},{1... | collective-permute-start | bytes 786440 | tf_op jit(solution)/shard_map/ppermute | solution.py:592
  48.9 6.4 %collective-permute-done.14.wide_got = bf16[512,256]{1,0:T(8,128)(2,1)S(1)} collective-permute-done((bf16[512,256]{1,0:T(8,128)(2,1)S(1)}, bf16[512,256]{1,0:T(8,128)(2,1)S(1)}, u32[]{:S(2)}, u32[]{:S(2)}) %collective-permute-start.14) | collective-permute-done | bytes 262176 | tf_op jit(solution)/shard_map/ppermute | solution.py:592
  56.0 2.0 %collective-permute-done.11.wide_got = bf16[512,256]{1,0:T(8,128)(2,1)S(1)} collective-permute-done((bf16[512,256]{1,0:T(8,128)(2,1)S(1)}, bf16[512,256]{1,0:T(8,128)(2,1)S(1)}, u32[]{:S(2)}, u32[]{:S(2)}) %collective-permute-start.11) | collective-permute-done | bytes 262176 | tf_op jit(solution)/shard_map/ppermute | solution.py:592
  58.8 2.2 %shard_map.82 = (bf16[512,512]{1,0:T(8,128)(2,1)}, bf16[512,512]{1,0:T(8,128)(2,1)}) custom-call(s32[4]{0:T(128)S(1)} %pad_add_fusion.where, bf16[2,2,128,256]{3,2,1,0:T(8,128)(2,1)S(1)} %get-tuple-element.54.refs_0_, bf16[2,2,128,256]{3,2,1,0:T(8,128)(2,1)S(1)} %get-tuple-element.64.refs_1_, bf16[2,2,128,256]{3,2,1,0:T(8,128)(2,1)S(1)} %collective-permute-done.8.refs_2_, ...), custom_call_target="tpu_custom_call" | custom-call | flops 1000 | bytes 1000 | tf_op jit(solution)/shard_map/pallas_call | solution.py:566
  61.1 3.3 %collective-permute-done.15.refs_2_ = bf16[512,256]{1,0:T(8,128)(2,1)S(1)} collective-permute-done((bf16[512,256]{1,0:T(8,128)(2,1)S(1)}, bf16[512,256]{1,0:T(8,128)(2,1)S(1)}, u32[]{:S(2)}, u32[]{:S(2)}) %collective-permute-start.15) | collective-permute-done | bytes 262176 | tf_op jit(solution)/shard_map/ppermute | solution.py:588
  64.4 2.1 %shard_map.85 = (bf16[512,512]{1,0:T(8,128)(2,1)}, bf16[512,512]{1,0:T(8,128)(2,1)}) custom-call(s32[4]{0:T(128)S(1)} %pad_add_fusion.where, bf16[512,256]{1,0:T(8,128)(2,1)S(1)} %get-tuple-element.76.refs_0_, bf16[512,256]{1,0:T(8,128)(2,1)S(1)} %get-tuple-element.80.refs_1_, bf16[512,256]{1,0:T(8,128)(2,1)S(1)} %collective-permute-done.15.refs_2_), custom_call_target="tpu_custom_call" | custom-call | flops 1000 | bytes 1000 | tf_op jit(solution)/shard_map/pallas_call | solution.py:506
  66.5 1.7 %collective-permute-done.12.got = bf16[512,256]{1,0:T(8,128)(2,1)S(1)} collective-permute-done((bf16[512,256]{1,0:T(8,128)(2,1)S(1)}, bf16[512,256]{1,0:T(8,128)(2,1)S(1)}, u32[]{:S(2)}, u32[]{:S(2)}) %collective-permute-start.12) | collective-permute-done | bytes 262176 | tf_op jit(solution)/shard_map/ppermute | solution.py:588
  68.1 1.5 %shard_map.86 = (bf16[512,512]{1,0:T(8,128)(2,1)}, bf16[512,512]{1,0:T(8,128)(2,1)}) custom-call(s32[4]{0:T(128)S(1)} %pad_add_fusion.where, bf16[512,256]{1,0:T(8,128)(2,1)S(1)} %collective-permute-done.12.got, bf16[512,512]{1,0:T(8,128)(2,1)} %get-tuple-element.82.first_in, ...), custom_call_target="tpu_custom_call", output_to_operand_aliasing={{0}: (2, {}), {1}: (3, {})} | custom-call | flops 1000 | bytes 1000 | tf_op jit(solution)/shard_map/pallas_call | solution.py:536
  (33 shorter events, 5.0 us)
Async XLA Ops:
  0.7 1.0 %copy-start = (bf16[512,512]{1,0:T(8,128)(2,1)S(1)}, bf16[512,512]{1,0:T(8,128)(2,1)}, u32[]{:S(2)}) copy-start(bf16[512,512]{1,0:T(8,128)(2,1)} %refs_0_.4) | copy-start | bytes 1572868
  1.8 1.0 %copy-start.2 = (bf16[512,512]{1,0:T(8,128)(2,1)S(1)}, bf16[512,512]{1,0:T(8,128)(2,1)}, u32[]{:S(2)}) copy-start(bf16[512,512]{1,0:T(8,128)(2,1)} %refs_1_.4) | copy-start | bytes 1572868
  2.8 2.7 %copy-start.4 = (bf16[512,512]{1,0:T(8,128)(2,1)S(1)}, bf16[512,512]{1,0:T(8,128)(2,1)}, u32[]{:S(2)}) copy-start(bf16[512,512]{1,0:T(8,128)(2,1)} %refs_0_.5) | copy-start | bytes 1572868
  2.8 2.7 %copy-start.5 = (bf16[512,512]{1,0:T(8,128)(2,1)S(1)}, bf16[512,512]{1,0:T(8,128)(2,1)}, u32[]{:S(2)}) copy-start(bf16[512,512]{1,0:T(8,128)(2,1)} %refs_1_.5) | copy-start | bytes 1572868
  4.0 7.2 %collective-permute-start = (bf16[512,256]{1,0:T(8,128)(2,1)S(1)}, bf16[512,256]{1,0:T(8,128)(2,1)S(1)}, u32[]{:S(2)}, u32[]{:S(2)}) collective-permute-start(bf16[512,256]{1,0:T(8,128)(2,1)S(1)} %get-tuple-element.46), channel_id=1, source_target_pairs={{0,1},{1,0},{2,3},{3,2},{4,5},{5,4},{6,7},{7,6},{8,9},{9,8},{10,11... | collective-permute-start | bytes 786440 | tf_op jit(solution)/shard_map/ppermute | solution.py:588
  5.3 1.4 %copy-start.1 = (bf16[512,512]{1,0:T(8,128)(2,1)S(1)}, bf16[512,512]{1,0:T(8,128)(2,1)}, u32[]{:S(2)}) copy-start(bf16[512,512]{1,0:T(8,128)(2,1)} %refs_0_.4) | copy-start | bytes 1572868
  5.3 1.4 %copy-start.3 = (bf16[512,512]{1,0:T(8,128)(2,1)S(1)}, bf16[512,512]{1,0:T(8,128)(2,1)}, u32[]{:S(2)}) copy-start(bf16[512,512]{1,0:T(8,128)(2,1)} %refs_1_.4) | copy-start | bytes 1572868
  5.3 13.7 %collective-permute-start.4 = (bf16[512,256]{1,0:T(8,128)(2,1)S(1)}, bf16[512,256]{1,0:T(8,128)(2,1)S(1)}, u32[]{:S(2)}, u32[]{:S(2)}) collective-permute-start(bf16[512,256]{1,0:T(8,128)(2,1)S(1)} %get-tuple-element.56), channel_id=1, source_target_pairs={{0,1},{1,0},{2,3},{3,2},{4,5},{5,4},{6,7},{7,6},{8,9},{9,8},{10,11... | collective-permute-start | bytes 786440 | tf_op jit(solution)/shard_map/ppermute | solution.py:588
  11.9 11.6 %collective-permute-start.1 = (bf16[512,256]{1,0:T(8,128)(2,1)S(1)}, bf16[512,256]{1,0:T(8,128)(2,1)S(1)}, u32[]{:S(2)}, u32[]{:S(2)}) collective-permute-start(bf16[512,256]{1,0:T(8,128)(2,1)S(1)} %get-tuple-element.50), channel_id=1, source_target_pairs={{0,2},{1,3},{2,0},{3,1},{4,6},{5,7},{6,4},{7,5},{8,10},{9,11},{10,... | collective-permute-start | bytes 786440 | tf_op jit(solution)/shard_map/ppermute | solution.py:591
  14.7 10.8 %collective-permute-start.2 = (bf16[512,256]{1,0:T(8,128)(2,1)S(1)}, bf16[512,256]{1,0:T(8,128)(2,1)S(1)}, u32[]{:S(2)}, u32[]{:S(2)}) collective-permute-start(bf16[512,256]{1,0:T(8,128)(2,1)S(1)} %get-tuple-element.51), channel_id=1, source_target_pairs={{2,4},{3,5},{4,2},{5,3},{6,8},{7,9},{8,6},{9,7},{10,12},{11,13},{1... | collective-permute-start | bytes 786440 | tf_op jit(solution)/shard_map/ppermute | solution.py:592
  17.7 7.7 %collective-permute-start.3 = (bf16[512,256]{1,0:T(8,128)(2,1)S(1)}, bf16[512,256]{1,0:T(8,128)(2,1)S(1)}, u32[]{:S(2)}, u32[]{:S(2)}) collective-permute-start(bf16[512,256]{1,0:T(8,128)(2,1)S(1)} %get-tuple-element.53), channel_id=1, source_target_pairs={{0,1},{1,0},{2,3},{3,2},{4,5},{5,4},{6,7},{7,6},{8,9},{9,8},{10,11... | collective-permute-start | bytes 786440 | tf_op jit(solution)/shard_map/ppermute | solution.py:588
  19.7 15.9 %collective-permute-start.5 = (bf16[512,256]{1,0:T(8,128)(2,1)S(1)}, bf16[512,256]{1,0:T(8,128)(2,1)S(1)}, u32[]{:S(2)}, u32[]{:S(2)}) collective-permute-start(bf16[512,256]{1,0:T(8,128)(2,1)S(1)} %get-tuple-element.60), channel_id=1, source_target_pairs={{0,2},{1,3},{2,0},{3,1},{4,6},{5,7},{6,4},{7,5},{8,10},{9,11},{10,... | collective-permute-start | bytes 786440 | tf_op jit(solution)/shard_map/ppermute | solution.py:591
  20.4 15.1 %collective-permute-start.6 = (bf16[512,256]{1,0:T(8,128)(2,1)S(1)}, bf16[512,256]{1,0:T(8,128)(2,1)S(1)}, u32[]{:S(2)}, u32[]{:S(2)}) collective-permute-start(bf16[512,256]{1,0:T(8,128)(2,1)S(1)} %get-tuple-element.61), channel_id=1, source_target_pairs={{2,4},{3,5},{4,2},{5,3},{6,8},{7,9},{8,6},{9,7},{10,12},{11,13},{1... | collective-permute-start | bytes 786440 | tf_op jit(solution)/shard_map/ppermute | solution.py:592
  23.5 12.1 %collective-permute-start.7 = (bf16[512,256]{1,0:T(8,128)(2,1)S(1)}, bf16[512,256]{1,0:T(8,128)(2,1)S(1)}, u32[]{:S(2)}, u32[]{:S(2)}) collective-permute-start(bf16[512,256]{1,0:T(8,128)(2,1)S(1)} %get-tuple-element.63), channel_id=1, source_target_pairs={{0,1},{1,0},{2,3},{3,2},{4,5},{5,4},{6,7},{7,6},{8,9},{9,8},{10,11... | collective-permute-start | bytes 786440 | tf_op jit(solution)/shard_map/ppermute | solution.py:588
  31.5 12.1 %collective-permute-start.8 = (bf16[2,2,128,256]{3,2,1,0:T(8,128)(2,1)S(1)}, bf16[2,2,128,256]{3,2,1,0:T(8,128)(2,1)S(1)}, u32[]{:S(2)}, u32[]{:S(2)}) collective-permute-start(bf16[2,2,128,256]{3,2,1,0:T(8,128)(2,1)S(1)} %get-tuple-element.65), channel_id=1, source_target_pairs={{0,1},{1,0},{2,3},{3,2},{4,5},{5,4},{6,7},{7,6},{8,9},{9,8},{10,11... | collective-permute-start | bytes 786440 | tf_op jit(solution)/shard_map/ppermute | solution.py:588
  41.5 7.3 %collective-permute-start.13 = (bf16[512,256]{1,0:T(8,128)(2,1)S(1)}, bf16[512,256]{1,0:T(8,128)(2,1)S(1)}, u32[]{:S(2)}, u32[]{:S(2)}) collective-permute-start(bf16[512,256]{1,0:T(8,128)(2,1)S(1)} %get-tuple-element.78), channel_id=1, source_target_pairs={{0,2},{1,3},{2,0},{3,1},{4,6},{5,7},{6,4},{7,5},{8,10},{9,11},{10,... | collective-permute-start | bytes 786440 | tf_op jit(solution)/shard_map/ppermute | solution.py:591
  41.6 13.6 %collective-permute-start.14 = (bf16[512,256]{1,0:T(8,128)(2,1)S(1)}, bf16[512,256]{1,0:T(8,128)(2,1)S(1)}, u32[]{:S(2)}, u32[]{:S(2)}) collective-permute-start(bf16[512,256]{1,0:T(8,128)(2,1)S(1)} %get-tuple-element.79), channel_id=1, source_target_pairs={{2,4},{3,5},{4,2},{5,3},{6,8},{7,9},{8,6},{9,7},{10,12},{11,13},{1... | collective-permute-start | bytes 786440 | tf_op jit(solution)/shard_map/ppermute | solution.py:592
  43.6 12.5 %collective-permute-start.10 = (bf16[512,256]{1,0:T(8,128)(2,1)S(1)}, bf16[512,256]{1,0:T(8,128)(2,1)S(1)}, u32[]{:S(2)}, u32[]{:S(2)}) collective-permute-start(bf16[512,256]{1,0:T(8,128)(2,1)S(1)} %get-tuple-element.73), channel_id=1, source_target_pairs={{0,2},{1,3},{2,0},{3,1},{4,6},{5,7},{6,4},{7,5},{8,10},{9,11},{10,... | collective-permute-start | bytes 786440 | tf_op jit(solution)/shard_map/ppermute | solution.py:591
  44.1 13.9 %collective-permute-start.11 = (bf16[512,256]{1,0:T(8,128)(2,1)S(1)}, bf16[512,256]{1,0:T(8,128)(2,1)S(1)}, u32[]{:S(2)}, u32[]{:S(2)}) collective-permute-start(bf16[512,256]{1,0:T(8,128)(2,1)S(1)} %get-tuple-element.74), channel_id=1, source_target_pairs={{2,4},{3,5},{4,2},{5,3},{6,8},{7,9},{8,6},{9,7},{10,12},{11,13},{1... | collective-permute-start | bytes 786440 | tf_op jit(solution)/shard_map/ppermute | solution.py:592
  48.8 10.1 %collective-permute-start.9 = (bf16[2,2,128,256]{3,2,1,0:T(8,128)(2,1)S(1)}, bf16[2,2,128,256]{3,2,1,0:T(8,128)(2,1)S(1)}, u32[]{:S(2)}, u32[]{:S(2)}) collective-permute-start(bf16[2,2,128,256]{3,2,1,0:T(8,128)(2,1)S(1)} %get-tuple-element.69), channel_id=1, source_target_pairs={{0,1},{1,0},{2,3},{3,2},{4,5},{5,4},{6,7},{7,6},{8,9},{9,8},{10,11... | collective-permute-start | bytes 786440 | tf_op jit(solution)/shard_map/ppermute | solution.py:588
  55.9 8.5 %collective-permute-start.15 = (bf16[512,256]{1,0:T(8,128)(2,1)S(1)}, bf16[512,256]{1,0:T(8,128)(2,1)S(1)}, u32[]{:S(2)}, u32[]{:S(2)}) collective-permute-start(bf16[512,256]{1,0:T(8,128)(2,1)S(1)} %get-tuple-element.81), channel_id=1, source_target_pairs={{0,1},{1,0},{2,3},{3,2},{4,5},{5,4},{6,7},{7,6},{8,9},{9,8},{10,11... | collective-permute-start | bytes 786440 | tf_op jit(solution)/shard_map/ppermute | solution.py:588
  58.7 9.4 %collective-permute-start.12 = (bf16[512,256]{1,0:T(8,128)(2,1)S(1)}, bf16[512,256]{1,0:T(8,128)(2,1)S(1)}, u32[]{:S(2)}, u32[]{:S(2)}) collective-permute-start(bf16[512,256]{1,0:T(8,128)(2,1)S(1)} %get-tuple-element.75), channel_id=1, source_target_pairs={{0,1},{1,0},{2,3},{3,2},{4,5},{5,4},{6,7},{7,6},{8,9},{9,8},{10,11... | collective-permute-start | bytes 786440 | tf_op jit(solution)/shard_map/ppermute | solution.py:588

commit v7 on v6

--- a/solution.py
+++ b/solution.py
@@ -288,11 +288,10 @@
         g2_t, ec2, low2 = [], [], []
         dq0 = []
         for i in range(4):
-            rows = slice(i * PARENT, i * PARENT + 3 * PARENT)
             q = q_parents[i]
             g = gs[i * PARENT : (i + 1) * PARENT, :]
-            s = dot_nt(raw[0, rows, :], q)
-            pieces = [s[:PARENT], s[PARENT : 2 * PARENT], s[2 * PARENT :]]
+            parents = [slice(n * PARENT, (n + 1) * PARENT) for n in range(i, i + 3)]
+            pieces = [dot_nt(raw[0, at, :], q) for at in parents]
             if i == 0:
                 pieces[0] = pieces[0] + left_bias
             if i == 3:
@@ -304,7 +303,7 @@
             for n in range(3):
                 p0[n * PARENT : (n + 1) * PARENT, :] = e[n]
             z0 = jnp.sum(e[0] + e[1] + e[2], axis=0, keepdims=True)
-            u0 = dot_nn(raw_t[1, :, rows], jnp.concatenate([x.astype(BF) for x in e], axis=0))
+            u0 = sum(dot_nn(raw_t[1, :, at], x.astype(BF)) for at, x in zip(parents, e))
             j, half = i // 2, i % 2
             lanes = slice(half * BLOCK, (half + 1) * BLOCK)
             m1, z1, u1 = (x[:, lanes] for x in far1[j])
@@ -338,13 +337,16 @@
             ec2.append(part + swap64(part))
             low2.append(lower)
             f0 = jnp.exp2(m0 * TO_LOG2 - lg)
-            products = dot_nt(raw[1, rows, :], g)
-            weights = p0[...] * f0
-            eb = weights.astype(BF)
-            r = (weights * (products - dr)).astype(BF)
-            acc0[1, rows, :] += dot_nn(eb, g)
-            acc0[0, rows, :] += dot_nn(r, q)
-            dq0.append(dot_nn(raw_t[0, :, rows], r))
+            dq = None
+            for n, at in enumerate(parents):
+                products = dot_nt(raw[1, at, :], g)
+                weights = p0[n * PARENT : (n + 1) * PARENT, :] * f0
+                r = (weights * (products - dr)).astype(BF)
+                acc0[1, at, :] += dot_nn(weights.astype(BF), g)
+                acc0[0, at, :] += dot_nn(r, q)
+                part = dot_nn(raw_t[0, :, at], r)
+                dq = part if dq is None else dq + part
+            dq0.append(dq)
         acc1[...] = jnp.zeros_like(acc1)
         dq1 = []
         for j in range(2):
@@ -595,8 +597,7 @@
     qg_far = pack(False, where, queries, cotangent)
     packed = pack(True, where, key_matrix, value_matrix, queries, cotangent)
     kv, qg = packed[:CHUNKS], packed[CHUNKS:]
-    oq_own, oq_got, kv_own, kv_got = [], [], [], []
-    back = []
+    oq_own, oq_got, back = [], [], []
     for c in range(CHUNKS):
         got_kv = swap(kv_far[c])
         near, wide, far = lax.optimization_barrier((*halo(where, kv[c], got_kv), qg_far[c]))
@@ -606,11 +607,12 @@
         oq_got.append(swap(far))
         if c + 1 < CHUNKS:
             oq_got[c], near, wide = lax.optimization_barrier((oq_got[c], near, wide))
-        back.append((grad, *beside(near, wide)))
-    for c in range(CHUNKS):
-        own, far = join(where, *back[c])
-        kv_own.append(own)
-        kv_got.append(swap(far))
+        back.append([grad, *beside(near, wide)])
+    kv_own, kv_got = [None] * CHUNKS, [None] * CHUNKS
+    oq_got[-1], back[-1] = lax.optimization_barrier((oq_got[-1], back[-1]))
+    for c in reversed(range(CHUNKS)):
+        kv_own[c], far = join(where, *back[c])
+        kv_got[c] = swap(far)
     attended, query_grad = unpack_columns(where, oq_own, oq_got, queries.shape)
     key_grad, value_grad = unpack_rows(where, kv_own, kv_got[1 - LATE_CHUNK], queries.shape)
     key_grad, value_grad = unpack_last(where, kv_got[LATE_CHUNK], key_grad, value_grad)

time: 70 us -> 69.3 us (0.990)
  the two profiles are of different devices: /device:TPU:9 before, /device:TPU:12 now
where the time goes in v7:
time: 69.3 us; the launch traced here: 68.8 us
  Pallas kernels  25.8 us (37%)
  starting transfers between devices  23.6 us (34%)
  waiting for transfers between devices  16.2 us (23%)
  local copies, waits for them, and re-layouts  2.1 us (3%)
  between operations  1.01 us (1%)
    pallas_call x2, Pallas kernels, main(): pl.pallas_call(main_kernel, in_specs=[smem()] + [vmem()] * 6, out_specs=[...  13.4 us
    ppermute x4, starting transfers between devices, beside(): return (near, lax.ppermute(wide, axes, wide_edges))  11.1 us
    ppermute x8, starting transfers between devices, swap(): return lax.ppermute(x, axes, across)  9.96 us
    ppermute x8, waiting for transfers between devices, swap(): return lax.ppermute(x, axes, across)  8.57 us
    ppermute x4, waiting for transfers between devices, beside(): return (near, lax.ppermute(wide, axes, wide_edges))  7.58 us
    pallas_call x3, Pallas kernels, pack(): pl.pallas_call(functools.partial(pack_kernel, own), in_specs=[smem()] + [...  3.9 us
    ppermute x4, starting transfers between devices, beside(): near = lax.ppermute(near, axes, near_edges)  2.46 us
    pallas_call x1, Pallas kernels, unpack_columns(): pl.pallas_call(unpack_columns_kernel, in_specs=[smem()] + [vmem()] * (2 *...  2.21 us
  transfers between devices with their start and end apart: 16, of which 8 were waited for; matrix products, arithmetic and copies ran while one was open for 0% of the time, Pallas kernels for 34%

profile of v7, /device:TPU:12, one launch (start us, length us, event | category | flops | bytes accessed | tf_op | source)
XLA Modules:
  0.0 68.8 jit_solution(5208342452583010995)
XLA Ops:
  0.7 1.0 %copy-done = bf16[512,512]{1,0:T(8,128)(2,1)S(1)} copy-done((bf16[512,512]{1,0:T(8,128)(2,1)S(1)}, bf16[512,512]{1,0:T(8,128)(2,1)}, u32[]{:S(2)}) %copy-start) | copy-done | bytes 524312
  2.8 1.1 %shard_map.76 = (bf16[512,256]{1,0:T(8,128)(2,1)S(1)}, bf16[512,256]{1,0:T(8,128)(2,1)S(1)}) custom-call(s32[4]{0:T(128)S(1)} %pad_add_fusion.where, bf16[512,512]{1,0:T(8,128)(2,1)S(1)} %copy-done, bf16[512,512]{1,0:T(8,128)(2,1)S(1)} %copy-done.2), custom_call_target="tpu_custom_call" | custom-call | flops 1000 | bytes 1000 | tf_op jit(solution)/shard_map/pallas_call | solution.py:86
  4.0 1.6 %collective-permute-start = (bf16[512,256]{1,0:T(8,128)(2,1)S(1)}, bf16[512,256]{1,0:T(8,128)(2,1)S(1)}, u32[]{:S(2)}, u32[]{:S(2)}) collective-permute-start(bf16[512,256]{1,0:T(8,128)(2,1)S(1)} %get-tuple-element.50), channel_id=1, source_target_pairs={{0,1},{1,0},{2,3},{3,2},{4,5},{5,4},{6,7},{7,6},{8,9},{9,8},{10,11... | collective-permute-start | bytes 786440 | tf_op jit(solution)/shard_map/ppermute | solution.py:590
  6.1 1.1 %shard_map.78 = (bf16[512,256]{1,0:T(8,128)(2,1)S(1)}, bf16[512,256]{1,0:T(8,128)(2,1)S(1)}) custom-call(s32[4]{0:T(128)S(1)} %pad_add_fusion.where, bf16[512,512]{1,0:T(8,128)(2,1)S(1)} %copy-done.4, bf16[512,512]{1,0:T(8,128)(2,1)S(1)} %copy-done.5), custom_call_target="tpu_custom_call" | custom-call | flops 1000 | bytes 1000 | tf_op jit(solution)/shard_map/pallas_call | solution.py:86
  7.2 1.6 %shard_map.75 = (bf16[512,256]{1,0:T(8,128)(2,1)S(1)}, bf16[512,256]{1,0:T(8,128)(2,1)S(1)}, bf16[512,256]{1,0:T(8,128)(2,1)S(1)}, bf16[512,256]{1,0:T(8,128)(2,1)S(1)}) custom-call(s32[4]{0:T(128)S(1)} %pad_add_fusion.where, bf16[512,512]{1,0:T(8,128)(2,1)S(1)} %copy-done.1, bf16[512,512]{1,0:T(8,128)(2,1)S(1)} %copy-done.3, ...), custom_call_target="tpu_custom_call" | custom-call | flops 1000 | bytes 1000 | tf_op jit(solution)/shard_map/pallas_call | solution.py:86
  8.9 4.4 %collective-permute-done.got.kv_got = bf16[512,256]{1,0:T(8,128)(2,1)S(1)} collective-permute-done((bf16[512,256]{1,0:T(8,128)(2,1)S(1)}, bf16[512,256]{1,0:T(8,128)(2,1)S(1)}, u32[]{:S(2)}, u32[]{:S(2)}) %collective-permute-start) | collective-permute-done | bytes 262176 | tf_op jit(solution)/shard_map/ppermute | solution.py:590
  14.0 2.5 %collective-permute-start.2 = (bf16[512,256]{1,0:T(8,128)(2,1)S(1)}, bf16[512,256]{1,0:T(8,128)(2,1)S(1)}, u32[]{:S(2)}, u32[]{:S(2)}) collective-permute-start(bf16[512,256]{1,0:T(8,128)(2,1)S(1)} %get-tuple-element.55), channel_id=1, source_target_pairs={{2,4},{3,5},{4,2},{5,3},{6,8},{7,9},{8,6},{9,7},{10,12},{11,13},{1... | collective-permute-start | bytes 786440 | tf_op jit(solution)/shard_map/ppermute | solution.py:594
  16.5 1.6 %collective-permute-start.3 = (bf16[512,256]{1,0:T(8,128)(2,1)S(1)}, bf16[512,256]{1,0:T(8,128)(2,1)S(1)}, u32[]{:S(2)}, u32[]{:S(2)}) collective-permute-start(bf16[512,256]{1,0:T(8,128)(2,1)S(1)} %get-tuple-element.57), channel_id=1, source_target_pairs={{0,1},{1,0},{2,3},{3,2},{4,5},{5,4},{6,7},{7,6},{8,9},{9,8},{10,11... | collective-permute-start | bytes 786440 | tf_op jit(solution)/shard_map/ppermute | solution.py:590
  19.6 2.8 %collective-permute-start.6 = (bf16[512,256]{1,0:T(8,128)(2,1)S(1)}, bf16[512,256]{1,0:T(8,128)(2,1)S(1)}, u32[]{:S(2)}, u32[]{:S(2)}) collective-permute-start(bf16[512,256]{1,0:T(8,128)(2,1)S(1)} %get-tuple-element.65), channel_id=1, source_target_pairs={{2,4},{3,5},{4,2},{5,3},{6,8},{7,9},{8,6},{9,7},{10,12},{11,13},{1... | collective-permute-start | bytes 786440 | tf_op jit(solution)/shard_map/ppermute | solution.py:594
  23.0 1.5 %collective-permute-done.2.wide_got = bf16[512,256]{1,0:T(8,128)(2,1)S(1)} collective-permute-done((bf16[512,256]{1,0:T(8,128)(2,1)S(1)}, bf16[512,256]{1,0:T(8,128)(2,1)S(1)}, u32[]{:S(2)}, u32[]{:S(2)}) %collective-permute-start.2) | collective-permute-done | bytes 262176 | tf_op jit(solution)/shard_map/ppermute | solution.py:594
  24.5 1.2 %collective-permute-done.3.qg_got = bf16[512,256]{1,0:T(8,128)(2,1)S(1)} collective-permute-done((bf16[512,256]{1,0:T(8,128)(2,1)S(1)}, bf16[512,256]{1,0:T(8,128)(2,1)S(1)}, u32[]{:S(2)}, u32[]{:S(2)}) %collective-permute-start.3) | collective-permute-done | bytes 262176 | tf_op jit(solution)/shard_map/ppermute | solution.py:590
  25.7 6.7 %shard_map.79 = (bf16[2,2,128,256]{3,2,1,0:T(8,128)(2,1)S(1)}, bf16[2,2,128,256]{3,2,1,0:T(8,128)(2,1)S(1)}, f32[1024,256]{1,0:T(8,128)S(1)}, bf16[512,256]{1,0:T(8,128)(2,1)S(1)}, bf16[512,256]{1,0:T(8,128)(2,1)S(1)}) custom-call(s32[4]{0:T(128)S(1)} %pad_add_fusion.where, bf16[512,256]{1,0:T(8,128)(2,1)S(1)} %get-tuple-element.49.own.kv_own, ...), custom_call_target="tpu_custom_call" | custom-call | flops 1000 | bytes 1000 | tf_op jit(solution)/shard_map/pallas_call | solution.py:415
  32.4 1.9 %collective-permute-start.8 = (bf16[2,2,128,256]{3,2,1,0:T(8,128)(2,1)S(1)}, bf16[2,2,128,256]{3,2,1,0:T(8,128)(2,1)S(1)}, u32[]{:S(2)}, u32[]{:S(2)}) collective-permute-start(bf16[2,2,128,256]{3,2,1,0:T(8,128)(2,1)S(1)} %get-tuple-element.69), channel_id=1, source_target_pairs={{0,1},{1,0},{2,3},{3,2},{4,5},{5,4},{6,7},{7,6},{8,9},{9,8},{10,11... | collective-permute-start | bytes 786440 | tf_op jit(solution)/shard_map/ppermute | solution.py:590
  34.3 6.7 %shard_map.81 = (bf16[2,2,128,256]{3,2,1,0:T(8,128)(2,1)S(1)}, bf16[2,2,128,256]{3,2,1,0:T(8,128)(2,1)S(1)}, f32[1024,256]{1,0:T(8,128)S(1)}, bf16[512,256]{1,0:T(8,128)(2,1)S(1)}, bf16[512,256]{1,0:T(8,128)(2,1)S(1)}) custom-call(s32[4]{0:T(128)S(1)} %pad_add_fusion.where, bf16[512,256]{1,0:T(8,128)(2,1)S(1)} %get-tuple-element.59.own.kv_own, ...), custom_call_target="tpu_custom_call" | custom-call | flops 1000 | bytes 1000 | tf_op jit(solution)/shard_map/pallas_call | solution.py:415
  41.3 3.7 %collective-permute-start.11 = (bf16[512,256]{1,0:T(8,128)(2,1)S(1)}, bf16[512,256]{1,0:T(8,128)(2,1)S(1)}, u32[]{:S(2)}, u32[]{:S(2)}) collective-permute-start(bf16[512,256]{1,0:T(8,128)(2,1)S(1)} %get-tuple-element.76), channel_id=1, source_target_pairs={{2,4},{3,5},{4,2},{5,3},{6,8},{7,9},{8,6},{9,7},{10,12},{11,13},{1... | collective-permute-start | bytes 786440 | tf_op jit(solution)/shard_map/ppermute | solution.py:594
  45.0 1.6 %collective-permute-start.12 = (bf16[512,256]{1,0:T(8,128)(2,1)S(1)}, bf16[512,256]{1,0:T(8,128)(2,1)S(1)}, u32[]{:S(2)}, u32[]{:S(2)}) collective-permute-start(bf16[512,256]{1,0:T(8,128)(2,1)S(1)} %get-tuple-element.81), channel_id=1, source_target_pairs={{0,2},{1,3},{2,0},{3,1},{4,6},{5,7},{6,4},{7,5},{8,10},{9,11},{10,... | collective-permute-start | bytes 786440 | tf_op jit(solution)/shard_map/ppermute | solution.py:593
  46.6 2.1 %collective-permute-start.13 = (bf16[512,256]{1,0:T(8,128)(2,1)S(1)}, bf16[512,256]{1,0:T(8,128)(2,1)S(1)}, u32[]{:S(2)}, u32[]{:S(2)}) collective-permute-start(bf16[512,256]{1,0:T(8,128)(2,1)S(1)} %get-tuple-element.82), channel_id=1, source_target_pairs={{2,4},{3,5},{4,2},{5,3},{6,8},{7,9},{8,6},{9,7},{10,12},{11,13},{1... | collective-permute-start | bytes 786440 | tf_op jit(solution)/shard_map/ppermute | solution.py:594
  49.0 5.5 %collective-permute-done.11.wide_got = bf16[512,256]{1,0:T(8,128)(2,1)S(1)} collective-permute-done((bf16[512,256]{1,0:T(8,128)(2,1)S(1)}, bf16[512,256]{1,0:T(8,128)(2,1)S(1)}, u32[]{:S(2)}, u32[]{:S(2)}) %collective-permute-start.11) | collective-permute-done | bytes 262176 | tf_op jit(solution)/shard_map/ppermute | solution.py:594
  55.2 1.7 %collective-permute-start.15 = (bf16[512,256]{1,0:T(8,128)(2,1)S(1)}, bf16[512,256]{1,0:T(8,128)(2,1)S(1)}, u32[]{:S(2)}, u32[]{:S(2)}) collective-permute-start(bf16[512,256]{1,0:T(8,128)(2,1)S(1)} %get-tuple-element.89), channel_id=1, source_target_pairs={{0,1},{1,0},{2,3},{3,2},{4,5},{5,4},{6,7},{7,6},{8,9},{9,8},{10,11... | collective-permute-start | bytes 786440 | tf_op jit(solution)/shard_map/ppermute | solution.py:590
  58.2 1.8 %collective-permute-start.14 = (bf16[512,256]{1,0:T(8,128)(2,1)S(1)}, bf16[512,256]{1,0:T(8,128)(2,1)S(1)}, u32[]{:S(2)}, u32[]{:S(2)}) collective-permute-start(bf16[512,256]{1,0:T(8,128)(2,1)S(1)} %get-tuple-element.83), channel_id=1, source_target_pairs={{0,1},{1,0},{2,3},{3,2},{4,5},{5,4},{6,7},{7,6},{8,9},{9,8},{10,11... | collective-permute-start | bytes 786440 | tf_op jit(solution)/shard_map/ppermute | solution.py:590
  60.0 2.2 %shard_map.82 = (bf16[512,512]{1,0:T(8,128)(2,1)}, bf16[512,512]{1,0:T(8,128)(2,1)}) custom-call(s32[4]{0:T(128)S(1)} %pad_add_fusion.where, bf16[2,2,128,256]{3,2,1,0:T(8,128)(2,1)S(1)} %get-tuple-element.58.refs_0_, bf16[2,2,128,256]{3,2,1,0:T(8,128)(2,1)S(1)} %get-tuple-element.68.refs_1_, bf16[2,2,128,256]{3,2,1,0:T(8,128)(2,1)S(1)} %collective-permute-done.8.refs_2_, ...), custom_call_target="tpu_custom_call" | custom-call | flops 1000 | bytes 1000 | tf_op jit(solution)/shard_map/pallas_call | solution.py:568
  62.2 2.0 %collective-permute-done.15.refs_2_ = bf16[512,256]{1,0:T(8,128)(2,1)S(1)} collective-permute-done((bf16[512,256]{1,0:T(8,128)(2,1)S(1)}, bf16[512,256]{1,0:T(8,128)(2,1)S(1)}, u32[]{:S(2)}, u32[]{:S(2)}) %collective-permute-start.15) | collective-permute-done | bytes 262176 | tf_op jit(solution)/shard_map/ppermute | solution.py:590
  64.3 2.1 %shard_map.85 = (bf16[512,512]{1,0:T(8,128)(2,1)}, bf16[512,512]{1,0:T(8,128)(2,1)}) custom-call(s32[4]{0:T(128)S(1)} %pad_add_fusion.where, bf16[512,256]{1,0:T(8,128)(2,1)S(1)} %get-tuple-element.84.refs_0_, bf16[512,256]{1,0:T(8,128)(2,1)S(1)} %get-tuple-element.88.refs_1_, bf16[512,256]{1,0:T(8,128)(2,1)S(1)} %collective-permute-done.15.refs_2_), custom_call_target="tpu_custom_call" | custom-call | flops 1000 | bytes 1000 | tf_op jit(solution)/shard_map/pallas_call | solution.py:508
  67.1 1.5 %shard_map.86 = (bf16[512,512]{1,0:T(8,128)(2,1)}, bf16[512,512]{1,0:T(8,128)(2,1)}) custom-call(s32[4]{0:T(128)S(1)} %pad_add_fusion.where, bf16[512,256]{1,0:T(8,128)(2,1)S(1)} %collective-permute-done.14.got, bf16[512,512]{1,0:T(8,128)(2,1)} %get-tuple-element.90.first_in, ...), custom_call_target="tpu_custom_call", output_to_operand_aliasing={{0}: (2, {}), {1}: (3, {})} | custom-call | flops 1000 | bytes 1000 | tf_op jit(solution)/shard_map/pallas_call | solution.py:538
  (33 shorter events, 7.7 us)
Async XLA Ops:
  0.7 1.0 %copy-start = (bf16[512,512]{1,0:T(8,128)(2,1)S(1)}, bf16[512,512]{1,0:T(8,128)(2,1)}, u32[]{:S(2)}) copy-start(bf16[512,512]{1,0:T(8,128)(2,1)} %refs_0_.4) | copy-start | bytes 1572868
  1.8 1.0 %copy-start.2 = (bf16[512,512]{1,0:T(8,128)(2,1)S(1)}, bf16[512,512]{1,0:T(8,128)(2,1)}, u32[]{:S(2)}) copy-start(bf16[512,512]{1,0:T(8,128)(2,1)} %refs_1_.4) | copy-start | bytes 1572868
  2.8 3.2 %copy-start.4 = (bf16[512,512]{1,0:T(8,128)(2,1)S(1)}, bf16[512,512]{1,0:T(8,128)(2,1)}, u32[]{:S(2)}) copy-start(bf16[512,512]{1,0:T(8,128)(2,1)} %refs_0_.5) | copy-start | bytes 1572868
  2.8 3.2 %copy-start.5 = (bf16[512,512]{1,0:T(8,128)(2,1)S(1)}, bf16[512,512]{1,0:T(8,128)(2,1)}, u32[]{:S(2)}) copy-start(bf16[512,512]{1,0:T(8,128)(2,1)} %refs_1_.5) | copy-start | bytes 1572868
  4.0 9.3 %collective-permute-start = (bf16[512,256]{1,0:T(8,128)(2,1)S(1)}, bf16[512,256]{1,0:T(8,128)(2,1)S(1)}, u32[]{:S(2)}, u32[]{:S(2)}) collective-permute-start(bf16[512,256]{1,0:T(8,128)(2,1)S(1)} %get-tuple-element.50), channel_id=1, source_target_pairs={{0,1},{1,0},{2,3},{3,2},{4,5},{5,4},{6,7},{7,6},{8,9},{9,8},{10,11... | collective-permute-start | bytes 786440 | tf_op jit(solution)/shard_map/ppermute | solution.py:590
  5.5 1.7 %copy-start.1 = (bf16[512,512]{1,0:T(8,128)(2,1)S(1)}, bf16[512,512]{1,0:T(8,128)(2,1)}, u32[]{:S(2)}) copy-start(bf16[512,512]{1,0:T(8,128)(2,1)} %refs_0_.4) | copy-start | bytes 1572868
  5.5 1.7 %copy-start.3 = (bf16[512,512]{1,0:T(8,128)(2,1)S(1)}, bf16[512,512]{1,0:T(8,128)(2,1)}, u32[]{:S(2)}) copy-start(bf16[512,512]{1,0:T(8,128)(2,1)} %refs_1_.4) | copy-start | bytes 1572868
  5.5 12.5 %collective-permute-start.4 = (bf16[512,256]{1,0:T(8,128)(2,1)S(1)}, bf16[512,256]{1,0:T(8,128)(2,1)S(1)}, u32[]{:S(2)}, u32[]{:S(2)}) collective-permute-start(bf16[512,256]{1,0:T(8,128)(2,1)S(1)} %get-tuple-element.60), channel_id=1, source_target_pairs={{0,1},{1,0},{2,3},{3,2},{4,5},{5,4},{6,7},{7,6},{8,9},{9,8},{10,11... | collective-permute-start | bytes 786440 | tf_op jit(solution)/shard_map/ppermute | solution.py:590
  13.9 8.5 %collective-permute-start.1 = (bf16[512,256]{1,0:T(8,128)(2,1)S(1)}, bf16[512,256]{1,0:T(8,128)(2,1)S(1)}, u32[]{:S(2)}, u32[]{:S(2)}) collective-permute-start(bf16[512,256]{1,0:T(8,128)(2,1)S(1)} %get-tuple-element.54), channel_id=1, source_target_pairs={{0,2},{1,3},{2,0},{3,1},{4,6},{5,7},{6,4},{7,5},{8,10},{9,11},{10,... | collective-permute-start | bytes 786440 | tf_op jit(solution)/shard_map/ppermute | solution.py:593
  14.0 10.5 %collective-permute-start.2 = (bf16[512,256]{1,0:T(8,128)(2,1)S(1)}, bf16[512,256]{1,0:T(8,128)(2,1)S(1)}, u32[]{:S(2)}, u32[]{:S(2)}) collective-permute-start(bf16[512,256]{1,0:T(8,128)(2,1)S(1)} %get-tuple-element.55), channel_id=1, source_target_pairs={{2,4},{3,5},{4,2},{5,3},{6,8},{7,9},{8,6},{9,7},{10,12},{11,13},{1... | collective-permute-start | bytes 786440 | tf_op jit(solution)/shard_map/ppermute | solution.py:594
  16.5 9.2 %collective-permute-start.3 = (bf16[512,256]{1,0:T(8,128)(2,1)S(1)}, bf16[512,256]{1,0:T(8,128)(2,1)S(1)}, u32[]{:S(2)}, u32[]{:S(2)}) collective-permute-start(bf16[512,256]{1,0:T(8,128)(2,1)S(1)} %get-tuple-element.57), channel_id=1, source_target_pairs={{0,1},{1,0},{2,3},{3,2},{4,5},{5,4},{6,7},{7,6},{8,9},{9,8},{10,11... | collective-permute-start | bytes 786440 | tf_op jit(solution)/shard_map/ppermute | solution.py:590
  18.8 15.6 %collective-permute-start.5 = (bf16[512,256]{1,0:T(8,128)(2,1)S(1)}, bf16[512,256]{1,0:T(8,128)(2,1)S(1)}, u32[]{:S(2)}, u32[]{:S(2)}) collective-permute-start(bf16[512,256]{1,0:T(8,128)(2,1)S(1)} %get-tuple-element.64), channel_id=1, source_target_pairs={{0,2},{1,3},{2,0},{3,1},{4,6},{5,7},{6,4},{7,5},{8,10},{9,11},{10,... | collective-permute-start | bytes 786440 | tf_op jit(solution)/shard_map/ppermute | solution.py:593
  19.6 14.7 %collective-permute-start.6 = (bf16[512,256]{1,0:T(8,128)(2,1)S(1)}, bf16[512,256]{1,0:T(8,128)(2,1)S(1)}, u32[]{:S(2)}, u32[]{:S(2)}) collective-permute-start(bf16[512,256]{1,0:T(8,128)(2,1)S(1)} %get-tuple-element.65), channel_id=1, source_target_pairs={{2,4},{3,5},{4,2},{5,3},{6,8},{7,9},{8,6},{9,7},{10,12},{11,13},{1... | collective-permute-start | bytes 786440 | tf_op jit(solution)/shard_map/ppermute | solution.py:594
  22.4 11.9 %collective-permute-start.7 = (bf16[512,256]{1,0:T(8,128)(2,1)S(1)}, bf16[512,256]{1,0:T(8,128)(2,1)S(1)}, u32[]{:S(2)}, u32[]{:S(2)}) collective-permute-start(bf16[512,256]{1,0:T(8,128)(2,1)S(1)} %get-tuple-element.67), channel_id=1, source_target_pairs={{0,1},{1,0},{2,3},{3,2},{4,5},{5,4},{6,7},{7,6},{8,9},{9,8},{10,11... | collective-permute-start | bytes 786440 | tf_op jit(solution)/shard_map/ppermute | solution.py:590
  32.4 12.6 %collective-permute-start.8 = (bf16[2,2,128,256]{3,2,1,0:T(8,128)(2,1)S(1)}, bf16[2,2,128,256]{3,2,1,0:T(8,128)(2,1)S(1)}, u32[]{:S(2)}, u32[]{:S(2)}) collective-permute-start(bf16[2,2,128,256]{3,2,1,0:T(8,128)(2,1)S(1)} %get-tuple-element.69), channel_id=1, source_target_pairs={{0,1},{1,0},{2,3},{3,2},{4,5},{5,4},{6,7},{7,6},{8,9},{9,8},{10,11... | collective-permute-start | bytes 786440 | tf_op jit(solution)/shard_map/ppermute | solution.py:590
  41.1 7.9 %collective-permute-start.9 = (bf16[2,2,128,256]{3,2,1,0:T(8,128)(2,1)S(1)}, bf16[2,2,128,256]{3,2,1,0:T(8,128)(2,1)S(1)}, u32[]{:S(2)}, u32[]{:S(2)}) collective-permute-start(bf16[2,2,128,256]{3,2,1,0:T(8,128)(2,1)S(1)} %get-tuple-element.73), channel_id=1, source_target_pairs={{0,1},{1,0},{2,3},{3,2},{4,5},{5,4},{6,7},{7,6},{8,9},{9,8},{10,11... | collective-permute-start | bytes 786440 | tf_op jit(solution)/shard_map/ppermute | solution.py:590
  41.3 7.6 %collective-permute-start.10 = (bf16[512,256]{1,0:T(8,128)(2,1)S(1)}, bf16[512,256]{1,0:T(8,128)(2,1)S(1)}, u32[]{:S(2)}, u32[]{:S(2)}) collective-permute-start(bf16[512,256]{1,0:T(8,128)(2,1)S(1)} %get-tuple-element.75), channel_id=1, source_target_pairs={{0,2},{1,3},{2,0},{3,1},{4,6},{5,7},{6,4},{7,5},{8,10},{9,11},{10,... | collective-permute-start | bytes 786440 | tf_op jit(solution)/shard_map/ppermute | solution.py:593
  41.3 13.2 %collective-permute-start.11 = (bf16[512,256]{1,0:T(8,128)(2,1)S(1)}, bf16[512,256]{1,0:T(8,128)(2,1)S(1)}, u32[]{:S(2)}, u32[]{:S(2)}) collective-permute-start(bf16[512,256]{1,0:T(8,128)(2,1)S(1)} %get-tuple-element.76), channel_id=1, source_target_pairs={{2,4},{3,5},{4,2},{5,3},{6,8},{7,9},{8,6},{9,7},{10,12},{11,13},{1... | collective-permute-start | bytes 786440 | tf_op jit(solution)/shard_map/ppermute | solution.py:594
  45.0 11.9 %collective-permute-start.12 = (bf16[512,256]{1,0:T(8,128)(2,1)S(1)}, bf16[512,256]{1,0:T(8,128)(2,1)S(1)}, u32[]{:S(2)}, u32[]{:S(2)}) collective-permute-start(bf16[512,256]{1,0:T(8,128)(2,1)S(1)} %get-tuple-element.81), channel_id=1, source_target_pairs={{0,2},{1,3},{2,0},{3,1},{4,6},{5,7},{6,4},{7,5},{8,10},{9,11},{10,... | collective-permute-start | bytes 786440 | tf_op jit(solution)/shard_map/ppermute | solution.py:593
  46.6 10.9 %collective-permute-start.13 = (bf16[512,256]{1,0:T(8,128)(2,1)S(1)}, bf16[512,256]{1,0:T(8,128)(2,1)S(1)}, u32[]{:S(2)}, u32[]{:S(2)}) collective-permute-start(bf16[512,256]{1,0:T(8,128)(2,1)S(1)} %get-tuple-element.82), channel_id=1, source_target_pairs={{2,4},{3,5},{4,2},{5,3},{6,8},{7,9},{8,6},{9,7},{10,12},{11,13},{1... | collective-permute-start | bytes 786440 | tf_op jit(solution)/shard_map/ppermute | solution.py:594
  55.2 9.1 %collective-permute-start.15 = (bf16[512,256]{1,0:T(8,128)(2,1)S(1)}, bf16[512,256]{1,0:T(8,128)(2,1)S(1)}, u32[]{:S(2)}, u32[]{:S(2)}) collective-permute-start(bf16[512,256]{1,0:T(8,128)(2,1)S(1)} %get-tuple-element.89), channel_id=1, source_target_pairs={{0,1},{1,0},{2,3},{3,2},{4,5},{5,4},{6,7},{7,6},{8,9},{9,8},{10,11... | collective-permute-start | bytes 786440 | tf_op jit(solution)/shard_map/ppermute | solution.py:590
  58.2 8.9 %collective-permute-start.14 = (bf16[512,256]{1,0:T(8,128)(2,1)S(1)}, bf16[512,256]{1,0:T(8,128)(2,1)S(1)}, u32[]{:S(2)}, u32[]{:S(2)}) collective-permute-start(bf16[512,256]{1,0:T(8,128)(2,1)S(1)} %get-tuple-element.83), channel_id=1, source_target_pairs={{0,1},{1,0},{2,3},{3,2},{4,5},{5,4},{6,7},{7,6},{8,9},{9,8},{10,11... | collective-permute-start | bytes 786440 | tf_op jit(solution)/shard_map/ppermute | solution.py:590

commit v8 on v6

--- a/solution.py
+++ b/solution.py
@@ -234,23 +234,22 @@
             raw[n, 1280:1536, :] = from_right[0:256, cols]
             one[n, 0:128, :] = from_left[256:384, cols]
             for i in range(6):
-                rows = slice(i * PARENT, (i + 1) * PARENT)
-                at = slice((i + 1) * BLOCK, (i + 2) * BLOCK)
-                one[n, at, :] = pool1(raw[n, rows, :])
-                flipped = raw[n, rows, :].T
-                raw_t[n, :, rows] = flipped
-                one_t[n, :, at] = (
-                    (flipped[:, :BLOCK].astype(F32) + flipped[:, BLOCK:].astype(F32)) * 0.5
-                ).astype(BF)
+                block = pool1(raw[n, i * PARENT : (i + 1) * PARENT, :])
+                at = (i + 1) * BLOCK
+                one[n, at : at + BLOCK, :] = block
             one[n, 896:1024, :] = from_right[256:384, cols]
-            for at in (slice(0, 128), slice(896, 1024)):
-                one_t[n, :, at] = one[n, at, :].T
             two[n, 0:128, :] = from_left[384:512, cols]
             two[n, 128:192, :] = pool12(one[n, 0:128, :])
             two[n, 192:256, :] = pool2(raw[n, 0:256, :])
             two[n, 256:320, :] = pool2(raw[n, 1280:1536, :])
             two[n, 320:384, :] = pool12(one[n, 896:1024, :])
             two[n, 384:512, :] = from_right[384:512, cols]
+            for i in range(6):
+                rows = slice(i * PARENT, (i + 1) * PARENT)
+                raw_t[n, :, rows] = raw[n, rows, :].T
+            for i in range(8):
+                rows = slice(i * BLOCK, (i + 1) * BLOCK)
+                one_t[n, :, rows] = one[n, rows, :].T
             for i in range(4):
                 rows = slice(i * BLOCK, (i + 1) * BLOCK)
                 two_t[n, :, rows] = two[n, rows, :].T
@@ -595,22 +594,25 @@
     qg_far = pack(False, where, queries, cotangent)
     packed = pack(True, where, key_matrix, value_matrix, queries, cotangent)
     kv, qg = packed[:CHUNKS], packed[CHUNKS:]
-    oq_own, oq_got, kv_own, kv_got = [], [], [], []
-    back = []
+    oq_own, oq_got, back = [], [], []
     for c in range(CHUNKS):
         got_kv = swap(kv_far[c])
-        near, wide, far = lax.optimization_barrier((*halo(where, kv[c], got_kv), qg_far[c]))
+        near, wide = halo(where, kv[c], got_kv)
+        far = qg_far[c]
+        if c > 0:
+            near, wide, far = lax.optimization_barrier((near, wide, far))
         near, wide = beside(near, wide)
         own, far, grad, near, wide = main(where, kv[c], got_kv, near, wide, qg[c], swap(far))
         oq_own.append(own)
         oq_got.append(swap(far))
         if c + 1 < CHUNKS:
             oq_got[c], near, wide = lax.optimization_barrier((oq_got[c], near, wide))
-        back.append((grad, *beside(near, wide)))
-    for c in range(CHUNKS):
-        own, far = join(where, *back[c])
-        kv_own.append(own)
-        kv_got.append(swap(far))
+        back.append([grad, *beside(near, wide)])
+    kv_own, kv_got = [None] * CHUNKS, [None] * CHUNKS
+    oq_got[-1], back[-1] = lax.optimization_barrier((oq_got[-1], back[-1]))
+    for c in reversed(range(CHUNKS)):
+        kv_own[c], far = join(where, *back[c])
+        kv_got[c] = swap(far)
     attended, query_grad = unpack_columns(where, oq_own, oq_got, queries.shape)
     key_grad, value_grad = unpack_rows(where, kv_own, kv_got[1 - LATE_CHUNK], queries.shape)
     key_grad, value_grad = unpack_last(where, kv_got[LATE_CHUNK], key_grad, value_grad)

time: 70 us -> 66.1 us (0.944)
  the two profiles are of different devices: /device:TPU:9 before, /device:TPU:12 now
where the time goes in v8:
time: 66.1 us; the launch traced here: 64.9 us
  Pallas kernels  24.3 us (37%)
  starting transfers between devices  20.9 us (32%)
  waiting for transfers between devices  16.5 us (25%)
  local copies, waits for them, and re-layouts  2.1 us (3%)
  between operations  0.99 us (1%)
    pallas_call x2, Pallas kernels, main(): pl.pallas_call(main_kernel, in_specs=[smem()] + [vmem()] * 6, out_specs=[...  11.9 us
    ppermute x4, starting transfers between devices, beside(): return (near, lax.ppermute(wide, axes, wide_edges))  10.1 us
    ppermute x8, starting transfers between devices, swap(): return lax.ppermute(x, axes, across)  9.55 us
    ppermute x4, waiting for transfers between devices, beside(): return (near, lax.ppermute(wide, axes, wide_edges))  8.36 us
    ppermute x8, waiting for transfers between devices, swap(): return lax.ppermute(x, axes, across)  8.14 us
    pallas_call x3, Pallas kernels, pack(): pl.pallas_call(functools.partial(pack_kernel, own), in_specs=[smem()] + [...  3.9 us
    pallas_call x1, Pallas kernels, unpack_columns(): pl.pallas_call(unpack_columns_kernel, in_specs=[smem()] + [vmem()] * (2 *...  2.21 us
    unnamed x12, local copies, waits for them, and re-layouts  2.1 us
  transfers between devices with their start and end apart: 16, of which 7 were waited for; matrix products, arithmetic and copies ran while one was open for 0% of the time, Pallas kernels for 33%

profile of v8, /device:TPU:12, one launch (start us, length us, event | category | flops | bytes accessed | tf_op | source)
XLA Modules:
  0.0 64.9 jit_solution(6779625500624422664)
XLA Ops:
  0.7 1.0 %copy-done = bf16[512,512]{1,0:T(8,128)(2,1)S(1)} copy-done((bf16[512,512]{1,0:T(8,128)(2,1)S(1)}, bf16[512,512]{1,0:T(8,128)(2,1)}, u32[]{:S(2)}) %copy-start) | copy-done | bytes 524312
  2.8 1.1 %shard_map.76 = (bf16[512,256]{1,0:T(8,128)(2,1)S(1)}, bf16[512,256]{1,0:T(8,128)(2,1)S(1)}) custom-call(s32[4]{0:T(128)S(1)} %pad_add_fusion.where, bf16[512,512]{1,0:T(8,128)(2,1)S(1)} %copy-done, bf16[512,512]{1,0:T(8,128)(2,1)S(1)} %copy-done.2), custom_call_target="tpu_custom_call" | custom-call | flops 1000 | bytes 1000 | tf_op jit(solution)/shard_map/pallas_call | solution.py:86
  4.0 1.6 %collective-permute-start = (bf16[512,256]{1,0:T(8,128)(2,1)S(1)}, bf16[512,256]{1,0:T(8,128)(2,1)S(1)}, u32[]{:S(2)}, u32[]{:S(2)}) collective-permute-start(bf16[512,256]{1,0:T(8,128)(2,1)S(1)} %get-tuple-element.47), channel_id=1, source_target_pairs={{0,1},{1,0},{2,3},{3,2},{4,5},{5,4},{6,7},{7,6},{8,9},{9,8},{10,11... | collective-permute-start | bytes 786440 | tf_op jit(solution)/shard_map/ppermute | solution.py:587
  6.1 1.1 %shard_map.78 = (bf16[512,256]{1,0:T(8,128)(2,1)S(1)}, bf16[512,256]{1,0:T(8,128)(2,1)S(1)}) custom-call(s32[4]{0:T(128)S(1)} %pad_add_fusion.where, bf16[512,512]{1,0:T(8,128)(2,1)S(1)} %copy-done.4, bf16[512,512]{1,0:T(8,128)(2,1)S(1)} %copy-done.5), custom_call_target="tpu_custom_call" | custom-call | flops 1000 | bytes 1000 | tf_op jit(solution)/shard_map/pallas_call | solution.py:86
  7.2 1.5 %collective-permute-start.3 = (bf16[512,256]{1,0:T(8,128)(2,1)S(1)}, bf16[512,256]{1,0:T(8,128)(2,1)S(1)}, u32[]{:S(2)}, u32[]{:S(2)}) collective-permute-start(bf16[512,256]{1,0:T(8,128)(2,1)S(1)} %get-tuple-element.51), channel_id=1, source_target_pairs={{0,1},{1,0},{2,3},{3,2},{4,5},{5,4},{6,7},{7,6},{8,9},{9,8},{10,11... | collective-permute-start | bytes 786440 | tf_op jit(solution)/shard_map/ppermute | solution.py:587
  8.8 1.6 %shard_map.75 = (bf16[512,256]{1,0:T(8,128)(2,1)S(1)}, bf16[512,256]{1,0:T(8,128)(2,1)S(1)}, bf16[512,256]{1,0:T(8,128)(2,1)S(1)}, bf16[512,256]{1,0:T(8,128)(2,1)S(1)}) custom-call(s32[4]{0:T(128)S(1)} %pad_add_fusion.where, bf16[512,512]{1,0:T(8,128)(2,1)S(1)} %copy-done.1, bf16[512,512]{1,0:T(8,128)(2,1)S(1)} %copy-done.3, ...), custom_call_target="tpu_custom_call" | custom-call | flops 1000 | bytes 1000 | tf_op jit(solution)/shard_map/pallas_call | solution.py:86
  10.4 2.8 %collective-permute-done.got.kv_got = bf16[512,256]{1,0:T(8,128)(2,1)S(1)} collective-permute-done((bf16[512,256]{1,0:T(8,128)(2,1)S(1)}, bf16[512,256]{1,0:T(8,128)(2,1)S(1)}, u32[]{:S(2)}, u32[]{:S(2)}) %collective-permute-start) | collective-permute-done | bytes 262176 | tf_op jit(solution)/shard_map/ppermute | solution.py:587
  14.0 2.5 %collective-permute-start.2 = (bf16[512,256]{1,0:T(8,128)(2,1)S(1)}, bf16[512,256]{1,0:T(8,128)(2,1)S(1)}, u32[]{:S(2)}, u32[]{:S(2)}) collective-permute-start(bf16[512,256]{1,0:T(8,128)(2,1)S(1)} %get-tuple-element.49), channel_id=1, source_target_pairs={{2,4},{3,5},{4,2},{5,3},{6,8},{7,9},{8,6},{9,7},{10,12},{11,13},{1... | collective-permute-start | bytes 786440 | tf_op jit(solution)/shard_map/ppermute | solution.py:591
  16.5 2.3 %collective-permute-done.4.got.kv_got = bf16[512,256]{1,0:T(8,128)(2,1)S(1)} collective-permute-done((bf16[512,256]{1,0:T(8,128)(2,1)S(1)}, bf16[512,256]{1,0:T(8,128)(2,1)S(1)}, u32[]{:S(2)}, u32[]{:S(2)}) %collective-permute-start.4) | collective-permute-done | bytes 262176 | tf_op jit(solution)/shard_map/ppermute | solution.py:587
  19.6 2.7 %collective-permute-start.6 = (bf16[512,256]{1,0:T(8,128)(2,1)S(1)}, bf16[512,256]{1,0:T(8,128)(2,1)S(1)}, u32[]{:S(2)}, u32[]{:S(2)}) collective-permute-start(bf16[512,256]{1,0:T(8,128)(2,1)S(1)} %get-tuple-element.59), channel_id=1, source_target_pairs={{2,4},{3,5},{4,2},{5,3},{6,8},{7,9},{8,6},{9,7},{10,12},{11,13},{1... | collective-permute-start | bytes 786440 | tf_op jit(solution)/shard_map/ppermute | solution.py:591
  23.3 1.5 %collective-permute-start.7 = (bf16[512,256]{1,0:T(8,128)(2,1)S(1)}, bf16[512,256]{1,0:T(8,128)(2,1)S(1)}, u32[]{:S(2)}, u32[]{:S(2)}) collective-permute-start(bf16[512,256]{1,0:T(8,128)(2,1)S(1)} %get-tuple-element.61), channel_id=1, source_target_pairs={{0,1},{1,0},{2,3},{3,2},{4,5},{5,4},{6,7},{7,6},{8,9},{9,8},{10,11... | collective-permute-start | bytes 786440 | tf_op jit(solution)/shard_map/ppermute | solution.py:587
  24.8 6.0 %shard_map.79 = (bf16[2,2,128,256]{3,2,1,0:T(8,128)(2,1)S(1)}, bf16[2,2,128,256]{3,2,1,0:T(8,128)(2,1)S(1)}, f32[1024,256]{1,0:T(8,128)S(1)}, bf16[512,256]{1,0:T(8,128)(2,1)S(1)}, bf16[512,256]{1,0:T(8,128)(2,1)S(1)}) custom-call(s32[4]{0:T(128)S(1)} %pad_add_fusion.where, bf16[512,256]{1,0:T(8,128)(2,1)S(1)} %get-tuple-element.46.own.kv_own, ...), custom_call_target="tpu_custom_call" | custom-call | flops 1000 | bytes 1000 | tf_op jit(solution)/shard_map/pallas_call | solution.py:412
  30.8 1.2 %collective-permute-start.8 = (bf16[2,2,128,256]{3,2,1,0:T(8,128)(2,1)S(1)}, bf16[2,2,128,256]{3,2,1,0:T(8,128)(2,1)S(1)}, u32[]{:S(2)}, u32[]{:S(2)}) collective-permute-start(bf16[2,2,128,256]{3,2,1,0:T(8,128)(2,1)S(1)} %get-tuple-element.63), channel_id=1, source_target_pairs={{0,1},{1,0},{2,3},{3,2},{4,5},{5,4},{6,7},{7,6},{8,9},{9,8},{10,11... | collective-permute-start | bytes 786440 | tf_op jit(solution)/shard_map/ppermute | solution.py:587
  32.1 6.0 %shard_map.81 = (bf16[2,2,128,256]{3,2,1,0:T(8,128)(2,1)S(1)}, bf16[2,2,128,256]{3,2,1,0:T(8,128)(2,1)S(1)}, f32[1024,256]{1,0:T(8,128)S(1)}, bf16[512,256]{1,0:T(8,128)(2,1)S(1)}, bf16[512,256]{1,0:T(8,128)(2,1)S(1)}) custom-call(s32[4]{0:T(128)S(1)} %pad_add_fusion.where, bf16[512,256]{1,0:T(8,128)(2,1)S(1)} %get-tuple-element.53.own.kv_own, ...), custom_call_target="tpu_custom_call" | custom-call | flops 1000 | bytes 1000 | tf_op jit(solution)/shard_map/pallas_call | solution.py:412
  38.0 1.1 %collective-permute-start.9 = (bf16[2,2,128,256]{3,2,1,0:T(8,128)(2,1)S(1)}, bf16[2,2,128,256]{3,2,1,0:T(8,128)(2,1)S(1)}, u32[]{:S(2)}, u32[]{:S(2)}) collective-permute-start(bf16[2,2,128,256]{3,2,1,0:T(8,128)(2,1)S(1)} %get-tuple-element.67), channel_id=1, source_target_pairs={{0,1},{1,0},{2,3},{3,2},{4,5},{5,4},{6,7},{7,6},{8,9},{9,8},{10,11... | collective-permute-start | bytes 786440 | tf_op jit(solution)/shard_map/ppermute | solution.py:587
  39.2 2.5 %collective-permute-start.11 = (bf16[512,256]{1,0:T(8,128)(2,1)S(1)}, bf16[512,256]{1,0:T(8,128)(2,1)S(1)}, u32[]{:S(2)}, u32[]{:S(2)}) collective-permute-start(bf16[512,256]{1,0:T(8,128)(2,1)S(1)} %get-tuple-element.70), channel_id=1, source_target_pairs={{2,4},{3,5},{4,2},{5,3},{6,8},{7,9},{8,6},{9,7},{10,12},{11,13},{1... | collective-permute-start | bytes 786440 | tf_op jit(solution)/shard_map/ppermute | solution.py:591
  41.7 1.1 %collective-permute-start.12 = (bf16[512,256]{1,0:T(8,128)(2,1)S(1)}, bf16[512,256]{1,0:T(8,128)(2,1)S(1)}, u32[]{:S(2)}, u32[]{:S(2)}) collective-permute-start(bf16[512,256]{1,0:T(8,128)(2,1)S(1)} %get-tuple-element.75), channel_id=1, source_target_pairs={{0,2},{1,3},{2,0},{3,1},{4,6},{5,7},{6,4},{7,5},{8,10},{9,11},{10,... | collective-permute-start | bytes 786440 | tf_op jit(solution)/shard_map/ppermute | solution.py:590
  42.8 2.4 %collective-permute-start.13 = (bf16[512,256]{1,0:T(8,128)(2,1)S(1)}, bf16[512,256]{1,0:T(8,128)(2,1)S(1)}, u32[]{:S(2)}, u32[]{:S(2)}) collective-permute-start(bf16[512,256]{1,0:T(8,128)(2,1)S(1)} %get-tuple-element.76), channel_id=1, source_target_pairs={{2,4},{3,5},{4,2},{5,3},{6,8},{7,9},{8,6},{9,7},{10,12},{11,13},{1... | collective-permute-start | bytes 786440 | tf_op jit(solution)/shard_map/ppermute | solution.py:591
  45.2 7.3 %collective-permute-done.11.wide_got = bf16[512,256]{1,0:T(8,128)(2,1)S(1)} collective-permute-done((bf16[512,256]{1,0:T(8,128)(2,1)S(1)}, bf16[512,256]{1,0:T(8,128)(2,1)S(1)}, u32[]{:S(2)}, u32[]{:S(2)}) %collective-permute-start.11) | collective-permute-done | bytes 262176 | tf_op jit(solution)/shard_map/ppermute | solution.py:591
  54.2 1.1 %collective-permute-done.13.wide_got = bf16[512,256]{1,0:T(8,128)(2,1)S(1)} collective-permute-done((bf16[512,256]{1,0:T(8,128)(2,1)S(1)}, bf16[512,256]{1,0:T(8,128)(2,1)S(1)}, u32[]{:S(2)}, u32[]{:S(2)}) %collective-permute-start.13) | collective-permute-done | bytes 262176 | tf_op jit(solution)/shard_map/ppermute | solution.py:591
  57.0 2.2 %shard_map.82 = (bf16[512,512]{1,0:T(8,128)(2,1)}, bf16[512,512]{1,0:T(8,128)(2,1)}) custom-call(s32[4]{0:T(128)S(1)} %pad_add_fusion.where, bf16[2,2,128,256]{3,2,1,0:T(8,128)(2,1)S(1)} %get-tuple-element.52.refs_0_, bf16[2,2,128,256]{3,2,1,0:T(8,128)(2,1)S(1)} %get-tuple-element.62.refs_1_, bf16[2,2,128,256]{3,2,1,0:T(8,128)(2,1)S(1)} %collective-permute-done.8.refs_2_, ...), custom_call_target="tpu_custom_call" | custom-call | flops 1000 | bytes 1000 | tf_op jit(solution)/shard_map/pallas_call | solution.py:565
  59.2 1.2 %collective-permute-done.15.refs_2_ = bf16[512,256]{1,0:T(8,128)(2,1)S(1)} collective-permute-done((bf16[512,256]{1,0:T(8,128)(2,1)S(1)}, bf16[512,256]{1,0:T(8,128)(2,1)S(1)}, u32[]{:S(2)}, u32[]{:S(2)}) %collective-permute-start.15) | collective-permute-done | bytes 262176 | tf_op jit(solution)/shard_map/ppermute | solution.py:587
  60.4 2.1 %shard_map.85 = (bf16[512,512]{1,0:T(8,128)(2,1)}, bf16[512,512]{1,0:T(8,128)(2,1)}) custom-call(s32[4]{0:T(128)S(1)} %pad_add_fusion.where, bf16[512,256]{1,0:T(8,128)(2,1)S(1)} %get-tuple-element.78.refs_0_, bf16[512,256]{1,0:T(8,128)(2,1)S(1)} %get-tuple-element.82.refs_1_, bf16[512,256]{1,0:T(8,128)(2,1)S(1)} %collective-permute-done.15.refs_2_), custom_call_target="tpu_custom_call" | custom-call | flops 1000 | bytes 1000 | tf_op jit(solution)/shard_map/pallas_call | solution.py:505
  63.2 1.5 %shard_map.86 = (bf16[512,512]{1,0:T(8,128)(2,1)}, bf16[512,512]{1,0:T(8,128)(2,1)}) custom-call(s32[4]{0:T(128)S(1)} %pad_add_fusion.where, bf16[512,256]{1,0:T(8,128)(2,1)S(1)} %collective-permute-done.14.got, bf16[512,512]{1,0:T(8,128)(2,1)} %get-tuple-element.84.first_in, ...), custom_call_target="tpu_custom_call", output_to_operand_aliasing={{0}: (2, {}), {1}: (3, {})} | custom-call | flops 1000 | bytes 1000 | tf_op jit(solution)/shard_map/pallas_call | solution.py:535
  (33 shorter events, 8.3 us)
Async XLA Ops:
  0.7 1.0 %copy-start = (bf16[512,512]{1,0:T(8,128)(2,1)S(1)}, bf16[512,512]{1,0:T(8,128)(2,1)}, u32[]{:S(2)}) copy-start(bf16[512,512]{1,0:T(8,128)(2,1)} %refs_0_.4) | copy-start | bytes 1572868
  1.8 1.0 %copy-start.2 = (bf16[512,512]{1,0:T(8,128)(2,1)S(1)}, bf16[512,512]{1,0:T(8,128)(2,1)}, u32[]{:S(2)}) copy-start(bf16[512,512]{1,0:T(8,128)(2,1)} %refs_1_.4) | copy-start | bytes 1572868
  2.8 3.2 %copy-start.4 = (bf16[512,512]{1,0:T(8,128)(2,1)S(1)}, bf16[512,512]{1,0:T(8,128)(2,1)}, u32[]{:S(2)}) copy-start(bf16[512,512]{1,0:T(8,128)(2,1)} %refs_0_.5) | copy-start | bytes 1572868
  2.8 3.2 %copy-start.5 = (bf16[512,512]{1,0:T(8,128)(2,1)S(1)}, bf16[512,512]{1,0:T(8,128)(2,1)}, u32[]{:S(2)}) copy-start(bf16[512,512]{1,0:T(8,128)(2,1)} %refs_1_.5) | copy-start | bytes 1572868
  4.0 9.3 %collective-permute-start = (bf16[512,256]{1,0:T(8,128)(2,1)S(1)}, bf16[512,256]{1,0:T(8,128)(2,1)S(1)}, u32[]{:S(2)}, u32[]{:S(2)}) collective-permute-start(bf16[512,256]{1,0:T(8,128)(2,1)S(1)} %get-tuple-element.47), channel_id=1, source_target_pairs={{0,1},{1,0},{2,3},{3,2},{4,5},{5,4},{6,7},{7,6},{8,9},{9,8},{10,11... | collective-permute-start | bytes 786440 | tf_op jit(solution)/shard_map/ppermute | solution.py:587
  5.5 3.2 %copy-start.1 = (bf16[512,512]{1,0:T(8,128)(2,1)S(1)}, bf16[512,512]{1,0:T(8,128)(2,1)}, u32[]{:S(2)}) copy-start(bf16[512,512]{1,0:T(8,128)(2,1)} %refs_0_.4) | copy-start | bytes 1572868
  5.5 3.2 %copy-start.3 = (bf16[512,512]{1,0:T(8,128)(2,1)S(1)}, bf16[512,512]{1,0:T(8,128)(2,1)}, u32[]{:S(2)}) copy-start(bf16[512,512]{1,0:T(8,128)(2,1)} %refs_1_.4) | copy-start | bytes 1572868
  5.5 13.3 %collective-permute-start.4 = (bf16[512,256]{1,0:T(8,128)(2,1)S(1)}, bf16[512,256]{1,0:T(8,128)(2,1)S(1)}, u32[]{:S(2)}, u32[]{:S(2)}) collective-permute-start(bf16[512,256]{1,0:T(8,128)(2,1)S(1)} %get-tuple-element.54), channel_id=1, source_target_pairs={{0,1},{1,0},{2,3},{3,2},{4,5},{5,4},{6,7},{7,6},{8,9},{9,8},{10,11... | collective-permute-start | bytes 786440 | tf_op jit(solution)/shard_map/ppermute | solution.py:587
  7.2 16.1 %collective-permute-start.3 = (bf16[512,256]{1,0:T(8,128)(2,1)S(1)}, bf16[512,256]{1,0:T(8,128)(2,1)S(1)}, u32[]{:S(2)}, u32[]{:S(2)}) collective-permute-start(bf16[512,256]{1,0:T(8,128)(2,1)S(1)} %get-tuple-element.51), channel_id=1, source_target_pairs={{0,1},{1,0},{2,3},{3,2},{4,5},{5,4},{6,7},{7,6},{8,9},{9,8},{10,11... | collective-permute-start | bytes 786440 | tf_op jit(solution)/shard_map/ppermute | solution.py:587
  13.9 10.9 %collective-permute-start.1 = (bf16[512,256]{1,0:T(8,128)(2,1)S(1)}, bf16[512,256]{1,0:T(8,128)(2,1)S(1)}, u32[]{:S(2)}, u32[]{:S(2)}) collective-permute-start(bf16[512,256]{1,0:T(8,128)(2,1)S(1)} %get-tuple-element.48), channel_id=1, source_target_pairs={{0,2},{1,3},{2,0},{3,1},{4,6},{5,7},{6,4},{7,5},{8,10},{9,11},{10,... | collective-permute-start | bytes 786440 | tf_op jit(solution)/shard_map/ppermute | solution.py:590
  14.0 10.8 %collective-permute-start.2 = (bf16[512,256]{1,0:T(8,128)(2,1)S(1)}, bf16[512,256]{1,0:T(8,128)(2,1)S(1)}, u32[]{:S(2)}, u32[]{:S(2)}) collective-permute-start(bf16[512,256]{1,0:T(8,128)(2,1)S(1)} %get-tuple-element.49), channel_id=1, source_target_pairs={{2,4},{3,5},{4,2},{5,3},{6,8},{7,9},{8,6},{9,7},{10,12},{11,13},{1... | collective-permute-start | bytes 786440 | tf_op jit(solution)/shard_map/ppermute | solution.py:591
  19.5 12.5 %collective-permute-start.5 = (bf16[512,256]{1,0:T(8,128)(2,1)S(1)}, bf16[512,256]{1,0:T(8,128)(2,1)S(1)}, u32[]{:S(2)}, u32[]{:S(2)}) collective-permute-start(bf16[512,256]{1,0:T(8,128)(2,1)S(1)} %get-tuple-element.58), channel_id=1, source_target_pairs={{0,2},{1,3},{2,0},{3,1},{4,6},{5,7},{6,4},{7,5},{8,10},{9,11},{10,... | collective-permute-start | bytes 786440 | tf_op jit(solution)/shard_map/ppermute | solution.py:590
  19.6 12.4 %collective-permute-start.6 = (bf16[512,256]{1,0:T(8,128)(2,1)S(1)}, bf16[512,256]{1,0:T(8,128)(2,1)S(1)}, u32[]{:S(2)}, u32[]{:S(2)}) collective-permute-start(bf16[512,256]{1,0:T(8,128)(2,1)S(1)} %get-tuple-element.59), channel_id=1, source_target_pairs={{2,4},{3,5},{4,2},{5,3},{6,8},{7,9},{8,6},{9,7},{10,12},{11,13},{1... | collective-permute-start | bytes 786440 | tf_op jit(solution)/shard_map/ppermute | solution.py:591
  23.3 8.7 %collective-permute-start.7 = (bf16[512,256]{1,0:T(8,128)(2,1)S(1)}, bf16[512,256]{1,0:T(8,128)(2,1)S(1)}, u32[]{:S(2)}, u32[]{:S(2)}) collective-permute-start(bf16[512,256]{1,0:T(8,128)(2,1)S(1)} %get-tuple-element.61), channel_id=1, source_target_pairs={{0,1},{1,0},{2,3},{3,2},{4,5},{5,4},{6,7},{7,6},{8,9},{9,8},{10,11... | collective-permute-start | bytes 786440 | tf_op jit(solution)/shard_map/ppermute | solution.py:587
  30.8 10.9 %collective-permute-start.8 = (bf16[2,2,128,256]{3,2,1,0:T(8,128)(2,1)S(1)}, bf16[2,2,128,256]{3,2,1,0:T(8,128)(2,1)S(1)}, u32[]{:S(2)}, u32[]{:S(2)}) collective-permute-start(bf16[2,2,128,256]{3,2,1,0:T(8,128)(2,1)S(1)} %get-tuple-element.63), channel_id=1, source_target_pairs={{0,1},{1,0},{2,3},{3,2},{4,5},{5,4},{6,7},{7,6},{8,9},{9,8},{10,11... | collective-permute-start | bytes 786440 | tf_op jit(solution)/shard_map/ppermute | solution.py:587
  38.0 7.2 %collective-permute-start.9 = (bf16[2,2,128,256]{3,2,1,0:T(8,128)(2,1)S(1)}, bf16[2,2,128,256]{3,2,1,0:T(8,128)(2,1)S(1)}, u32[]{:S(2)}, u32[]{:S(2)}) collective-permute-start(bf16[2,2,128,256]{3,2,1,0:T(8,128)(2,1)S(1)} %get-tuple-element.67), channel_id=1, source_target_pairs={{0,1},{1,0},{2,3},{3,2},{4,5},{5,4},{6,7},{7,6},{8,9},{9,8},{10,11... | collective-permute-start | bytes 786440 | tf_op jit(solution)/shard_map/ppermute | solution.py:587
  39.2 6.0 %collective-permute-start.10 = (bf16[512,256]{1,0:T(8,128)(2,1)S(1)}, bf16[512,256]{1,0:T(8,128)(2,1)S(1)}, u32[]{:S(2)}, u32[]{:S(2)}) collective-permute-start(bf16[512,256]{1,0:T(8,128)(2,1)S(1)} %get-tuple-element.69), channel_id=1, source_target_pairs={{0,2},{1,3},{2,0},{3,1},{4,6},{5,7},{6,4},{7,5},{8,10},{9,11},{10,... | collective-permute-start | bytes 786440 | tf_op jit(solution)/shard_map/ppermute | solution.py:590
  39.2 13.3 %collective-permute-start.11 = (bf16[512,256]{1,0:T(8,128)(2,1)S(1)}, bf16[512,256]{1,0:T(8,128)(2,1)S(1)}, u32[]{:S(2)}, u32[]{:S(2)}) collective-permute-start(bf16[512,256]{1,0:T(8,128)(2,1)S(1)} %get-tuple-element.70), channel_id=1, source_target_pairs={{2,4},{3,5},{4,2},{5,3},{6,8},{7,9},{8,6},{9,7},{10,12},{11,13},{1... | collective-permute-start | bytes 786440 | tf_op jit(solution)/shard_map/ppermute | solution.py:591
  41.7 12.5 %collective-permute-start.12 = (bf16[512,256]{1,0:T(8,128)(2,1)S(1)}, bf16[512,256]{1,0:T(8,128)(2,1)S(1)}, u32[]{:S(2)}, u32[]{:S(2)}) collective-permute-start(bf16[512,256]{1,0:T(8,128)(2,1)S(1)} %get-tuple-element.75), channel_id=1, source_target_pairs={{0,2},{1,3},{2,0},{3,1},{4,6},{5,7},{6,4},{7,5},{8,10},{9,11},{10,... | collective-permute-start | bytes 786440 | tf_op jit(solution)/shard_map/ppermute | solution.py:590
  42.8 12.5 %collective-permute-start.13 = (bf16[512,256]{1,0:T(8,128)(2,1)S(1)}, bf16[512,256]{1,0:T(8,128)(2,1)S(1)}, u32[]{:S(2)}, u32[]{:S(2)}) collective-permute-start(bf16[512,256]{1,0:T(8,128)(2,1)S(1)} %get-tuple-element.76), channel_id=1, source_target_pairs={{2,4},{3,5},{4,2},{5,3},{6,8},{7,9},{8,6},{9,7},{10,12},{11,13},{1... | collective-permute-start | bytes 786440 | tf_op jit(solution)/shard_map/ppermute | solution.py:591
  53.2 7.3 %collective-permute-start.15 = (bf16[512,256]{1,0:T(8,128)(2,1)S(1)}, bf16[512,256]{1,0:T(8,128)(2,1)S(1)}, u32[]{:S(2)}, u32[]{:S(2)}) collective-permute-start(bf16[512,256]{1,0:T(8,128)(2,1)S(1)} %get-tuple-element.83), channel_id=1, source_target_pairs={{0,1},{1,0},{2,3},{3,2},{4,5},{5,4},{6,7},{7,6},{8,9},{9,8},{10,11... | collective-permute-start | bytes 786440 | tf_op jit(solution)/shard_map/ppermute | solution.py:587
  56.0 7.3 %collective-permute-start.14 = (bf16[512,256]{1,0:T(8,128)(2,1)S(1)}, bf16[512,256]{1,0:T(8,128)(2,1)S(1)}, u32[]{:S(2)}, u32[]{:S(2)}) collective-permute-start(bf16[512,256]{1,0:T(8,128)(2,1)S(1)} %get-tuple-element.77), channel_id=1, source_target_pairs={{0,1},{1,0},{2,3},{3,2},{4,5},{5,4},{6,7},{7,6},{8,9},{9,8},{10,11... | collective-permute-start | bytes 786440 | tf_op jit(solution)/shard_map/ppermute | solution.py:587

commit v9 on v8

--- a/solution.py
+++ b/solution.py
@@ -13,7 +13,7 @@
 PARENT = 256
 LEVELS = 3
 CHUNKS = 2
-LATE_CHUNK = 0
+LATE_CHUNK = 1
 INV_ROOT = HEAD**-0.5
 TO_LOG2 = INV_ROOT * math.log2(math.e)
 MASKED = -1e30
@@ -605,14 +605,15 @@
         own, far, grad, near, wide = main(where, kv[c], got_kv, near, wide, qg[c], swap(far))
         oq_own.append(own)
         oq_got.append(swap(far))
-        if c + 1 < CHUNKS:
-            oq_got[c], near, wide = lax.optimization_barrier((oq_got[c], near, wide))
+        if c > 0:
+            oq_got[c - 1], near, wide = lax.optimization_barrier((oq_got[c - 1], near, wide))
         back.append([grad, *beside(near, wide)])
-    kv_own, kv_got = [None] * CHUNKS, [None] * CHUNKS
     oq_got[-1], back[-1] = lax.optimization_barrier((oq_got[-1], back[-1]))
-    for c in reversed(range(CHUNKS)):
-        kv_own[c], far = join(where, *back[c])
-        kv_got[c] = swap(far)
+    kv_own, kv_got = [], []
+    for c in range(CHUNKS):
+        own, far = join(where, *back[c])
+        kv_own.append(own)
+        kv_got.append(swap(far))
     attended, query_grad = unpack_columns(where, oq_own, oq_got, queries.shape)
     key_grad, value_grad = unpack_rows(where, kv_own, kv_got[1 - LATE_CHUNK], queries.shape)
     key_grad, value_grad = unpack_last(where, kv_got[LATE_CHUNK], key_grad, value_grad)

time: 66.1 us -> 63.2 us (0.956)
  waiting for transfers between devices: 16.5 us -> 13.8 us
    ppermute x4, waiting for transfers between devices: 8.36 us -> 3.67 us  [beside(): return (near, lax.ppermute(wide, axes, wide_edges))]
    ppermute x8, waiting for transfers between devices: 8.14 us -> 10.2 us  [swap(): return lax.ppermute(x, axes, across)]
    ppermute x8, starting transfers between devices: 9.55 us -> 10.3 us  [swap(): return lax.ppermute(x, axes, across)]
  transfers between devices with their start and end apart: 16 -> 16, of which waited for: 7 -> 6; matrix products, arithmetic and copies ran while one was open for 0% -> 0% of each run, Pallas kernels for 33% -> 35%
where the time goes in v9:
time: 63.2 us; the launch traced here: 62.6 us
  Pallas kernels  24.3 us (38%)
  starting transfers between devices  21.2 us (34%)
  waiting for transfers between devices  13.8 us (22%)
  local copies, waits for them, and re-layouts  2.1 us (3%)
  between operations  1 us (2%)
    pallas_call x2, Pallas kernels, main(): pl.pallas_call(main_kernel, in_specs=[smem()] + [vmem()] * 6, out_specs=[...  11.9 us
    ppermute x8, starting transfers between devices, swap(): return lax.ppermute(x, axes, across)  10.3 us
    ppermute x8, waiting for transfers between devices, swap(): return lax.ppermute(x, axes, across)  10.2 us
    ppermute x4, starting transfers between devices, beside(): return (near, lax.ppermute(wide, axes, wide_edges))  10.1 us
    pallas_call x3, Pallas kernels, pack(): pl.pallas_call(functools.partial(pack_kernel, own), in_specs=[smem()] + [...  3.9 us
    ppermute x4, waiting for transfers between devices, beside(): return (near, lax.ppermute(wide, axes, wide_edges))  3.67 us
    pallas_call x1, Pallas kernels, unpack_columns(): pl.pallas_call(unpack_columns_kernel, in_specs=[smem()] + [vmem()] * (2 *...  2.21 us
    unnamed x12, local copies, waits for them, and re-layouts  2.1 us
  transfers between devices with their start and end apart: 16, of which 6 were waited for; matrix products, arithmetic and copies ran while one was open for 0% of the time, Pallas kernels for 35%

profile of v9, /device:TPU:12, one launch (start us, length us, event | category | flops | bytes accessed | tf_op | source)
XLA Modules:
  0.0 62.6 jit_solution(13393802790006324652)
XLA Ops:
  2.8 1.1 %shard_map.76 = (bf16[512,256]{1,0:T(8,128)(2,1)S(1)}, bf16[512,256]{1,0:T(8,128)(2,1)S(1)}) custom-call(s32[4]{0:T(128)S(1)} %pad_add_fusion.where, bf16[512,512]{1,0:T(8,128)(2,1)S(1)} %copy-done, bf16[512,512]{1,0:T(8,128)(2,1)S(1)} %copy-done.2), custom_call_target="tpu_custom_call" | custom-call | flops 1000 | bytes 1000 | tf_op jit(solution)/shard_map/pallas_call | solution.py:86
  4.0 1.6 %collective-permute-start = (bf16[512,256]{1,0:T(8,128)(2,1)S(1)}, bf16[512,256]{1,0:T(8,128)(2,1)S(1)}, u32[]{:S(2)}, u32[]{:S(2)}) collective-permute-start(bf16[512,256]{1,0:T(8,128)(2,1)S(1)} %get-tuple-element.47), channel_id=1, source_target_pairs={{0,1},{1,0},{2,3},{3,2},{4,5},{5,4},{6,7},{7,6},{8,9},{9,8},{10,11... | collective-permute-start | bytes 786440 | tf_op jit(solution)/shard_map/ppermute | solution.py:587
  7.2 1.5 %collective-permute-start.3 = (bf16[512,256]{1,0:T(8,128)(2,1)S(1)}, bf16[512,256]{1,0:T(8,128)(2,1)S(1)}, u32[]{:S(2)}, u32[]{:S(2)}) collective-permute-start(bf16[512,256]{1,0:T(8,128)(2,1)S(1)} %get-tuple-element.51), channel_id=1, source_target_pairs={{0,1},{1,0},{2,3},{3,2},{4,5},{5,4},{6,7},{7,6},{8,9},{9,8},{10,11... | collective-permute-start | bytes 786440 | tf_op jit(solution)/shard_map/ppermute | solution.py:587
  8.8 1.6 %shard_map.75 = (bf16[512,256]{1,0:T(8,128)(2,1)S(1)}, bf16[512,256]{1,0:T(8,128)(2,1)S(1)}, bf16[512,256]{1,0:T(8,128)(2,1)S(1)}, bf16[512,256]{1,0:T(8,128)(2,1)S(1)}) custom-call(s32[4]{0:T(128)S(1)} %pad_add_fusion.where, bf16[512,512]{1,0:T(8,128)(2,1)S(1)} %copy-done.1, bf16[512,512]{1,0:T(8,128)(2,1)S(1)} %copy-done.3, ...), custom_call_target="tpu_custom_call" | custom-call | flops 1000 | bytes 1000 | tf_op jit(solution)/shard_map/pallas_call | solution.py:86
  10.4 2.8 %collective-permute-done.got.kv_got = bf16[512,256]{1,0:T(8,128)(2,1)S(1)} collective-permute-done((bf16[512,256]{1,0:T(8,128)(2,1)S(1)}, bf16[512,256]{1,0:T(8,128)(2,1)S(1)}, u32[]{:S(2)}, u32[]{:S(2)}) %collective-permute-start) | collective-permute-done | bytes 262176 | tf_op jit(solution)/shard_map/ppermute | solution.py:587
  14.0 2.5 %collective-permute-start.2 = (bf16[512,256]{1,0:T(8,128)(2,1)S(1)}, bf16[512,256]{1,0:T(8,128)(2,1)S(1)}, u32[]{:S(2)}, u32[]{:S(2)}) collective-permute-start(bf16[512,256]{1,0:T(8,128)(2,1)S(1)} %get-tuple-element.49), channel_id=1, source_target_pairs={{2,4},{3,5},{4,2},{5,3},{6,8},{7,9},{8,6},{9,7},{10,12},{11,13},{1... | collective-permute-start | bytes 786440 | tf_op jit(solution)/shard_map/ppermute | solution.py:591
  16.5 2.3 %collective-permute-done.4.got.kv_got = bf16[512,256]{1,0:T(8,128)(2,1)S(1)} collective-permute-done((bf16[512,256]{1,0:T(8,128)(2,1)S(1)}, bf16[512,256]{1,0:T(8,128)(2,1)S(1)}, u32[]{:S(2)}, u32[]{:S(2)}) %collective-permute-start.4) | collective-permute-done | bytes 262176 | tf_op jit(solution)/shard_map/ppermute | solution.py:587
  19.6 2.5 %collective-permute-start.6 = (bf16[512,256]{1,0:T(8,128)(2,1)S(1)}, bf16[512,256]{1,0:T(8,128)(2,1)S(1)}, u32[]{:S(2)}, u32[]{:S(2)}) collective-permute-start(bf16[512,256]{1,0:T(8,128)(2,1)S(1)} %get-tuple-element.59), channel_id=1, source_target_pairs={{2,4},{3,5},{4,2},{5,3},{6,8},{7,9},{8,6},{9,7},{10,12},{11,13},{1... | collective-permute-start | bytes 786440 | tf_op jit(solution)/shard_map/ppermute | solution.py:591
  22.1 1.2 %collective-permute-done.3.qg_got = bf16[512,256]{1,0:T(8,128)(2,1)S(1)} collective-permute-done((bf16[512,256]{1,0:T(8,128)(2,1)S(1)}, bf16[512,256]{1,0:T(8,128)(2,1)S(1)}, u32[]{:S(2)}, u32[]{:S(2)}) %collective-permute-start.3) | collective-permute-done | bytes 262176 | tf_op jit(solution)/shard_map/ppermute | solution.py:587
  23.3 1.5 %collective-permute-start.7 = (bf16[512,256]{1,0:T(8,128)(2,1)S(1)}, bf16[512,256]{1,0:T(8,128)(2,1)S(1)}, u32[]{:S(2)}, u32[]{:S(2)}) collective-permute-start(bf16[512,256]{1,0:T(8,128)(2,1)S(1)} %get-tuple-element.61), channel_id=1, source_target_pairs={{0,1},{1,0},{2,3},{3,2},{4,5},{5,4},{6,7},{7,6},{8,9},{9,8},{10,11... | collective-permute-start | bytes 786440 | tf_op jit(solution)/shard_map/ppermute | solution.py:587
  24.8 6.0 %shard_map.79 = (bf16[2,2,128,256]{3,2,1,0:T(8,128)(2,1)S(1)}, bf16[2,2,128,256]{3,2,1,0:T(8,128)(2,1)S(1)}, f32[1024,256]{1,0:T(8,128)S(1)}, bf16[512,256]{1,0:T(8,128)(2,1)S(1)}, bf16[512,256]{1,0:T(8,128)(2,1)S(1)}) custom-call(s32[4]{0:T(128)S(1)} %pad_add_fusion.where, bf16[512,256]{1,0:T(8,128)(2,1)S(1)} %get-tuple-element.46.own.kv_own, ...), custom_call_target="tpu_custom_call" | custom-call | flops 1000 | bytes 1000 | tf_op jit(solution)/shard_map/pallas_call | solution.py:412
  30.8 1.2 %collective-permute-start.8 = (bf16[2,2,128,256]{3,2,1,0:T(8,128)(2,1)S(1)}, bf16[2,2,128,256]{3,2,1,0:T(8,128)(2,1)S(1)}, u32[]{:S(2)}, u32[]{:S(2)}) collective-permute-start(bf16[2,2,128,256]{3,2,1,0:T(8,128)(2,1)S(1)} %get-tuple-element.63), channel_id=1, source_target_pairs={{0,1},{1,0},{2,3},{3,2},{4,5},{5,4},{6,7},{7,6},{8,9},{9,8},{10,11... | collective-permute-start | bytes 786440 | tf_op jit(solution)/shard_map/ppermute | solution.py:587
  32.0 2.4 %collective-permute-start.14 = (bf16[512,256]{1,0:T(8,128)(2,1)S(1)}, bf16[512,256]{1,0:T(8,128)(2,1)S(1)}, u32[]{:S(2)}, u32[]{:S(2)}) collective-permute-start(bf16[512,256]{1,0:T(8,128)(2,1)S(1)} %get-tuple-element.80), channel_id=1, source_target_pairs={{2,4},{3,5},{4,2},{5,3},{6,8},{7,9},{8,6},{9,7},{10,12},{11,13},{1... | collective-permute-start | bytes 786440 | tf_op jit(solution)/shard_map/ppermute | solution.py:591
  34.5 6.0 %shard_map.81 = (bf16[2,2,128,256]{3,2,1,0:T(8,128)(2,1)S(1)}, bf16[2,2,128,256]{3,2,1,0:T(8,128)(2,1)S(1)}, f32[1024,256]{1,0:T(8,128)S(1)}, bf16[512,256]{1,0:T(8,128)(2,1)S(1)}, bf16[512,256]{1,0:T(8,128)(2,1)S(1)}) custom-call(s32[4]{0:T(128)S(1)} %pad_add_fusion.where, bf16[512,256]{1,0:T(8,128)(2,1)S(1)} %get-tuple-element.53.own.kv_own, ...), custom_call_target="tpu_custom_call" | custom-call | flops 1000 | bytes 1000 | tf_op jit(solution)/shard_map/pallas_call | solution.py:412
  40.5 1.2 %collective-permute-start.9 = (bf16[2,2,128,256]{3,2,1,0:T(8,128)(2,1)S(1)}, bf16[2,2,128,256]{3,2,1,0:T(8,128)(2,1)S(1)}, u32[]{:S(2)}, u32[]{:S(2)}) collective-permute-start(bf16[2,2,128,256]{3,2,1,0:T(8,128)(2,1)S(1)} %get-tuple-element.67), channel_id=1, source_target_pairs={{0,1},{1,0},{2,3},{3,2},{4,5},{5,4},{6,7},{7,6},{8,9},{9,8},{10,11... | collective-permute-start | bytes 786440 | tf_op jit(solution)/shard_map/ppermute | solution.py:587
  42.4 2.7 %collective-permute-start.11 = (bf16[512,256]{1,0:T(8,128)(2,1)S(1)}, bf16[512,256]{1,0:T(8,128)(2,1)S(1)}, u32[]{:S(2)}, u32[]{:S(2)}) collective-permute-start(bf16[512,256]{1,0:T(8,128)(2,1)S(1)} %get-tuple-element.70), channel_id=1, source_target_pairs={{2,4},{3,5},{4,2},{5,3},{6,8},{7,9},{8,6},{9,7},{10,12},{11,13},{1... | collective-permute-start | bytes 786440 | tf_op jit(solution)/shard_map/ppermute | solution.py:591
  45.8 1.2 %collective-permute-start.15 = (bf16[512,256]{1,0:T(8,128)(2,1)S(1)}, bf16[512,256]{1,0:T(8,128)(2,1)S(1)}, u32[]{:S(2)}, u32[]{:S(2)}) collective-permute-start(bf16[512,256]{1,0:T(8,128)(2,1)S(1)} %get-tuple-element.83), channel_id=1, source_target_pairs={{0,1},{1,0},{2,3},{3,2},{4,5},{5,4},{6,7},{7,6},{8,9},{9,8},{10,11... | collective-permute-start | bytes 786440 | tf_op jit(solution)/shard_map/ppermute | solution.py:587
  47.0 2.2 %collective-permute-done.9.refs_3_ = bf16[2,2,128,256]{3,2,1,0:T(8,128)(2,1)S(1)} collective-permute-done((bf16[2,2,128,256]{3,2,1,0:T(8,128)(2,1)S(1)}, bf16[2,2,128,256]{3,2,1,0:T(8,128)(2,1)S(1)}, u32[]{:S(2)}, u32[]{:S(2)}) %collective-permute-start.9) | collective-permute-done | bytes 262176 | tf_op jit(solution)/shard_map/ppermute | solution.py:587
  49.2 3.7 %collective-permute-done.11.wide_got = bf16[512,256]{1,0:T(8,128)(2,1)S(1)} collective-permute-done((bf16[512,256]{1,0:T(8,128)(2,1)S(1)}, bf16[512,256]{1,0:T(8,128)(2,1)S(1)}, u32[]{:S(2)}, u32[]{:S(2)}) %collective-permute-start.11) | collective-permute-done | bytes 262176 | tf_op jit(solution)/shard_map/ppermute | solution.py:591
  53.6 1.4 %collective-permute-start.12 = (bf16[512,256]{1,0:T(8,128)(2,1)S(1)}, bf16[512,256]{1,0:T(8,128)(2,1)S(1)}, u32[]{:S(2)}, u32[]{:S(2)}) collective-permute-start(bf16[512,256]{1,0:T(8,128)(2,1)S(1)} %get-tuple-element.77), channel_id=1, source_target_pairs={{0,1},{1,0},{2,3},{3,2},{4,5},{5,4},{6,7},{7,6},{8,9},{9,8},{10,11... | collective-permute-start | bytes 786440 | tf_op jit(solution)/shard_map/ppermute | solution.py:587
  55.0 2.2 %shard_map.82 = (bf16[512,512]{1,0:T(8,128)(2,1)}, bf16[512,512]{1,0:T(8,128)(2,1)}) custom-call(s32[4]{0:T(128)S(1)} %pad_add_fusion.where, bf16[2,2,128,256]{3,2,1,0:T(8,128)(2,1)S(1)} %get-tuple-element.52.refs_0_, bf16[2,2,128,256]{3,2,1,0:T(8,128)(2,1)S(1)} %get-tuple-element.62.refs_1_, bf16[2,2,128,256]{3,2,1,0:T(8,128)(2,1)S(1)} %collective-permute-done.8.refs_2_, ...), custom_call_target="tpu_custom_call" | custom-call | flops 1000 | bytes 1000 | tf_op jit(solution)/shard_map/pallas_call | solution.py:565
  57.2 2.1 %shard_map.85 = (bf16[512,512]{1,0:T(8,128)(2,1)}, bf16[512,512]{1,0:T(8,128)(2,1)}) custom-call(s32[4]{0:T(128)S(1)} %pad_add_fusion.where, bf16[512,256]{1,0:T(8,128)(2,1)S(1)} %get-tuple-element.81.refs_0_, bf16[512,256]{1,0:T(8,128)(2,1)S(1)} %get-tuple-element.82.refs_1_, bf16[512,256]{1,0:T(8,128)(2,1)S(1)} %collective-permute-done.15.refs_2_), custom_call_target="tpu_custom_call" | custom-call | flops 1000 | bytes 1000 | tf_op jit(solution)/shard_map/pallas_call | solution.py:505
  59.3 1.6 %collective-permute-done.12.got = bf16[512,256]{1,0:T(8,128)(2,1)S(1)} collective-permute-done((bf16[512,256]{1,0:T(8,128)(2,1)S(1)}, bf16[512,256]{1,0:T(8,128)(2,1)S(1)}, u32[]{:S(2)}, u32[]{:S(2)}) %collective-permute-start.12) | collective-permute-done | bytes 262176 | tf_op jit(solution)/shard_map/ppermute | solution.py:587
  60.9 1.5 %shard_map.86 = (bf16[512,512]{1,0:T(8,128)(2,1)}, bf16[512,512]{1,0:T(8,128)(2,1)}) custom-call(s32[4]{0:T(128)S(1)} %pad_add_fusion.where, bf16[512,256]{1,0:T(8,128)(2,1)S(1)} %collective-permute-done.12.got, bf16[512,512]{1,0:T(8,128)(2,1)} %get-tuple-element.84.first_in, ...), custom_call_target="tpu_custom_call", output_to_operand_aliasing={{0}: (2, {}), {1}: (3, {})} | custom-call | flops 1000 | bytes 1000 | tf_op jit(solution)/shard_map/pallas_call | solution.py:535
  (33 shorter events, 7.5 us)
Async XLA Ops:
  0.7 1.0 %copy-start = (bf16[512,512]{1,0:T(8,128)(2,1)S(1)}, bf16[512,512]{1,0:T(8,128)(2,1)}, u32[]{:S(2)}) copy-start(bf16[512,512]{1,0:T(8,128)(2,1)} %refs_0_.4) | copy-start | bytes 1572868
  1.8 1.0 %copy-start.2 = (bf16[512,512]{1,0:T(8,128)(2,1)S(1)}, bf16[512,512]{1,0:T(8,128)(2,1)}, u32[]{:S(2)}) copy-start(bf16[512,512]{1,0:T(8,128)(2,1)} %refs_1_.4) | copy-start | bytes 1572868
  2.8 3.2 %copy-start.4 = (bf16[512,512]{1,0:T(8,128)(2,1)S(1)}, bf16[512,512]{1,0:T(8,128)(2,1)}, u32[]{:S(2)}) copy-start(bf16[512,512]{1,0:T(8,128)(2,1)} %refs_0_.5) | copy-start | bytes 1572868
  2.8 3.2 %copy-start.5 = (bf16[512,512]{1,0:T(8,128)(2,1)S(1)}, bf16[512,512]{1,0:T(8,128)(2,1)}, u32[]{:S(2)}) copy-start(bf16[512,512]{1,0:T(8,128)(2,1)} %refs_1_.5) | copy-start | bytes 1572868
  4.0 9.3 %collective-permute-start = (bf16[512,256]{1,0:T(8,128)(2,1)S(1)}, bf16[512,256]{1,0:T(8,128)(2,1)S(1)}, u32[]{:S(2)}, u32[]{:S(2)}) collective-permute-start(bf16[512,256]{1,0:T(8,128)(2,1)S(1)} %get-tuple-element.47), channel_id=1, source_target_pairs={{0,1},{1,0},{2,3},{3,2},{4,5},{5,4},{6,7},{7,6},{8,9},{9,8},{10,11... | collective-permute-start | bytes 786440 | tf_op jit(solution)/shard_map/ppermute | solution.py:587
  5.5 3.2 %copy-start.1 = (bf16[512,512]{1,0:T(8,128)(2,1)S(1)}, bf16[512,512]{1,0:T(8,128)(2,1)}, u32[]{:S(2)}) copy-start(bf16[512,512]{1,0:T(8,128)(2,1)} %refs_0_.4) | copy-start | bytes 1572868
  5.5 3.2 %copy-start.3 = (bf16[512,512]{1,0:T(8,128)(2,1)S(1)}, bf16[512,512]{1,0:T(8,128)(2,1)}, u32[]{:S(2)}) copy-start(bf16[512,512]{1,0:T(8,128)(2,1)} %refs_1_.4) | copy-start | bytes 1572868
  5.5 13.3 %collective-permute-start.4 = (bf16[512,256]{1,0:T(8,128)(2,1)S(1)}, bf16[512,256]{1,0:T(8,128)(2,1)S(1)}, u32[]{:S(2)}, u32[]{:S(2)}) collective-permute-start(bf16[512,256]{1,0:T(8,128)(2,1)S(1)} %get-tuple-element.54), channel_id=1, source_target_pairs={{0,1},{1,0},{2,3},{3,2},{4,5},{5,4},{6,7},{7,6},{8,9},{9,8},{10,11... | collective-permute-start | bytes 786440 | tf_op jit(solution)/shard_map/ppermute | solution.py:587
  7.2 16.1 %collective-permute-start.3 = (bf16[512,256]{1,0:T(8,128)(2,1)S(1)}, bf16[512,256]{1,0:T(8,128)(2,1)S(1)}, u32[]{:S(2)}, u32[]{:S(2)}) collective-permute-start(bf16[512,256]{1,0:T(8,128)(2,1)S(1)} %get-tuple-element.51), channel_id=1, source_target_pairs={{0,1},{1,0},{2,3},{3,2},{4,5},{5,4},{6,7},{7,6},{8,9},{9,8},{10,11... | collective-permute-start | bytes 786440 | tf_op jit(solution)/shard_map/ppermute | solution.py:587
  13.9 10.9 %collective-permute-start.1 = (bf16[512,256]{1,0:T(8,128)(2,1)S(1)}, bf16[512,256]{1,0:T(8,128)(2,1)S(1)}, u32[]{:S(2)}, u32[]{:S(2)}) collective-permute-start(bf16[512,256]{1,0:T(8,128)(2,1)S(1)} %get-tuple-element.48), channel_id=1, source_target_pairs={{0,2},{1,3},{2,0},{3,1},{4,6},{5,7},{6,4},{7,5},{8,10},{9,11},{10,... | collective-permute-start | bytes 786440 | tf_op jit(solution)/shard_map/ppermute | solution.py:590
  14.0 10.8 %collective-permute-start.2 = (bf16[512,256]{1,0:T(8,128)(2,1)S(1)}, bf16[512,256]{1,0:T(8,128)(2,1)S(1)}, u32[]{:S(2)}, u32[]{:S(2)}) collective-permute-start(bf16[512,256]{1,0:T(8,128)(2,1)S(1)} %get-tuple-element.49), channel_id=1, source_target_pairs={{2,4},{3,5},{4,2},{5,3},{6,8},{7,9},{8,6},{9,7},{10,12},{11,13},{1... | collective-permute-start | bytes 786440 | tf_op jit(solution)/shard_map/ppermute | solution.py:591
  19.5 12.5 %collective-permute-start.5 = (bf16[512,256]{1,0:T(8,128)(2,1)S(1)}, bf16[512,256]{1,0:T(8,128)(2,1)S(1)}, u32[]{:S(2)}, u32[]{:S(2)}) collective-permute-start(bf16[512,256]{1,0:T(8,128)(2,1)S(1)} %get-tuple-element.58), channel_id=1, source_target_pairs={{0,2},{1,3},{2,0},{3,1},{4,6},{5,7},{6,4},{7,5},{8,10},{9,11},{10,... | collective-permute-start | bytes 786440 | tf_op jit(solution)/shard_map/ppermute | solution.py:590
  19.6 14.8 %collective-permute-start.6 = (bf16[512,256]{1,0:T(8,128)(2,1)S(1)}, bf16[512,256]{1,0:T(8,128)(2,1)S(1)}, u32[]{:S(2)}, u32[]{:S(2)}) collective-permute-start(bf16[512,256]{1,0:T(8,128)(2,1)S(1)} %get-tuple-element.59), channel_id=1, source_target_pairs={{2,4},{3,5},{4,2},{5,3},{6,8},{7,9},{8,6},{9,7},{10,12},{11,13},{1... | collective-permute-start | bytes 786440 | tf_op jit(solution)/shard_map/ppermute | solution.py:591
  23.3 11.1 %collective-permute-start.7 = (bf16[512,256]{1,0:T(8,128)(2,1)S(1)}, bf16[512,256]{1,0:T(8,128)(2,1)S(1)}, u32[]{:S(2)}, u32[]{:S(2)}) collective-permute-start(bf16[512,256]{1,0:T(8,128)(2,1)S(1)} %get-tuple-element.61), channel_id=1, source_target_pairs={{0,1},{1,0},{2,3},{3,2},{4,5},{5,4},{6,7},{7,6},{8,9},{9,8},{10,11... | collective-permute-start | bytes 786440 | tf_op jit(solution)/shard_map/ppermute | solution.py:587
  30.8 10.9 %collective-permute-start.8 = (bf16[2,2,128,256]{3,2,1,0:T(8,128)(2,1)S(1)}, bf16[2,2,128,256]{3,2,1,0:T(8,128)(2,1)S(1)}, u32[]{:S(2)}, u32[]{:S(2)}) collective-permute-start(bf16[2,2,128,256]{3,2,1,0:T(8,128)(2,1)S(1)} %get-tuple-element.63), channel_id=1, source_target_pairs={{0,1},{1,0},{2,3},{3,2},{4,5},{5,4},{6,7},{7,6},{8,9},{9,8},{10,11... | collective-permute-start | bytes 786440 | tf_op jit(solution)/shard_map/ppermute | solution.py:587
  32.0 13.1 %collective-permute-start.13 = (bf16[512,256]{1,0:T(8,128)(2,1)S(1)}, bf16[512,256]{1,0:T(8,128)(2,1)S(1)}, u32[]{:S(2)}, u32[]{:S(2)}) collective-permute-start(bf16[512,256]{1,0:T(8,128)(2,1)S(1)} %get-tuple-element.79), channel_id=1, source_target_pairs={{0,2},{1,3},{2,0},{3,1},{4,6},{5,7},{6,4},{7,5},{8,10},{9,11},{10,... | collective-permute-start | bytes 786440 | tf_op jit(solution)/shard_map/ppermute | solution.py:590
  32.0 13.1 %collective-permute-start.14 = (bf16[512,256]{1,0:T(8,128)(2,1)S(1)}, bf16[512,256]{1,0:T(8,128)(2,1)S(1)}, u32[]{:S(2)}, u32[]{:S(2)}) collective-permute-start(bf16[512,256]{1,0:T(8,128)(2,1)S(1)} %get-tuple-element.80), channel_id=1, source_target_pairs={{2,4},{3,5},{4,2},{5,3},{6,8},{7,9},{8,6},{9,7},{10,12},{11,13},{1... | collective-permute-start | bytes 786440 | tf_op jit(solution)/shard_map/ppermute | solution.py:591
  40.5 8.8 %collective-permute-start.9 = (bf16[2,2,128,256]{3,2,1,0:T(8,128)(2,1)S(1)}, bf16[2,2,128,256]{3,2,1,0:T(8,128)(2,1)S(1)}, u32[]{:S(2)}, u32[]{:S(2)}) collective-permute-start(bf16[2,2,128,256]{3,2,1,0:T(8,128)(2,1)S(1)} %get-tuple-element.67), channel_id=1, source_target_pairs={{0,1},{1,0},{2,3},{3,2},{4,5},{5,4},{6,7},{7,6},{8,9},{9,8},{10,11... | collective-permute-start | bytes 786440 | tf_op jit(solution)/shard_map/ppermute | solution.py:587
  41.7 7.6 %collective-permute-start.10 = (bf16[512,256]{1,0:T(8,128)(2,1)S(1)}, bf16[512,256]{1,0:T(8,128)(2,1)S(1)}, u32[]{:S(2)}, u32[]{:S(2)}) collective-permute-start(bf16[512,256]{1,0:T(8,128)(2,1)S(1)} %get-tuple-element.69), channel_id=1, source_target_pairs={{0,2},{1,3},{2,0},{3,1},{4,6},{5,7},{6,4},{7,5},{8,10},{9,11},{10,... | collective-permute-start | bytes 786440 | tf_op jit(solution)/shard_map/ppermute | solution.py:590
  42.4 10.5 %collective-permute-start.11 = (bf16[512,256]{1,0:T(8,128)(2,1)S(1)}, bf16[512,256]{1,0:T(8,128)(2,1)S(1)}, u32[]{:S(2)}, u32[]{:S(2)}) collective-permute-start(bf16[512,256]{1,0:T(8,128)(2,1)S(1)} %get-tuple-element.70), channel_id=1, source_target_pairs={{2,4},{3,5},{4,2},{5,3},{6,8},{7,9},{8,6},{9,7},{10,12},{11,13},{1... | collective-permute-start | bytes 786440 | tf_op jit(solution)/shard_map/ppermute | solution.py:591
  45.8 11.4 %collective-permute-start.15 = (bf16[512,256]{1,0:T(8,128)(2,1)S(1)}, bf16[512,256]{1,0:T(8,128)(2,1)S(1)}, u32[]{:S(2)}, u32[]{:S(2)}) collective-permute-start(bf16[512,256]{1,0:T(8,128)(2,1)S(1)} %get-tuple-element.83), channel_id=1, source_target_pairs={{0,1},{1,0},{2,3},{3,2},{4,5},{5,4},{6,7},{7,6},{8,9},{9,8},{10,11... | collective-permute-start | bytes 786440 | tf_op jit(solution)/shard_map/ppermute | solution.py:587
  53.6 7.4 %collective-permute-start.12 = (bf16[512,256]{1,0:T(8,128)(2,1)S(1)}, bf16[512,256]{1,0:T(8,128)(2,1)S(1)}, u32[]{:S(2)}, u32[]{:S(2)}) collective-permute-start(bf16[512,256]{1,0:T(8,128)(2,1)S(1)} %get-tuple-element.77), channel_id=1, source_target_pairs={{0,1},{1,0},{2,3},{3,2},{4,5},{5,4},{6,7},{7,6},{8,9},{9,8},{10,11... | collective-permute-start | bytes 786440 | tf_op jit(solution)/shard_map/ppermute | solution.py:587

commit v10 on v9

--- a/solution.py
+++ b/solution.py
@@ -80,7 +80,7 @@
                 out[at, first : first + width] = x[:, c * width : (c + 1) * width]
 
 
-def pack(own, where, *arrays):
+def pack(own, where, *arrays, limit=8):
     rows, columns = arrays[0].shape
     count = len(arrays)
     return pl.pallas_call(
@@ -92,7 +92,7 @@
             pltpu.VMEM((count, rows, columns // 2), BF),
             pltpu.SemaphoreType.DMA((count,)),
         ],
-        compiler_params=small(),
+        compiler_params=pltpu.CompilerParams(vmem_limit_bytes=limit * 1024 * 1024),
         cost_estimate=light(),
     )(where, *arrays)
 
@@ -160,52 +160,36 @@
 
 
 def far_forward(k, v_t, q, bias, p_ref):
-    k0, k1, k2, k3 = k
-    v0, v1, v2, v3 = v_t
     left, right = bias
-    outer = dot_nt(jnp.concatenate([k0, k3], axis=0), q)
-    first, last = outer[:BLOCK], outer[BLOCK:]
-    mid_low = dot_nt(k2, q[:BLOCK])
-    mid_high = dot_nt(k1, q[BLOCK:])
+    s = dot_nt(k, q)
+    masked = jnp.full((BLOCK, BLOCK), MASKED, F32)
+    parts = [
+        s[:BLOCK],
+        jnp.concatenate([masked, s[BLOCK : 2 * BLOCK, BLOCK:]], axis=1),
+        jnp.concatenate([s[2 * BLOCK : 3 * BLOCK, :BLOCK], masked], axis=1),
+        s[3 * BLOCK :],
+    ]
     if left is not None:
-        first = first + left
-        mid_high = mid_high + left
+        parts[:2] = [x + left for x in parts[:2]]
     if right is not None:
-        last = last + right
-        mid_low = mid_low + right
-    mid = jnp.concatenate([mid_low, mid_high], axis=1)
-    peak = jnp.max(jnp.maximum(jnp.maximum(first, last), mid), axis=0, keepdims=True)
-    parts = [jnp.exp2((x - peak) * TO_LOG2) for x in (first, last, mid)]
+        parts[2:] = [x + right for x in parts[2:]]
+    peak = jnp.max(
+        jnp.maximum(jnp.maximum(parts[0], parts[1]), jnp.maximum(parts[2], parts[3])),
+        axis=0,
+        keepdims=True,
+    )
+    parts = [jnp.exp2((x - peak) * TO_LOG2) for x in parts]
     for n, x in enumerate(parts):
         p_ref[n * BLOCK : (n + 1) * BLOCK, :] = x
-    total = jnp.sum(parts[0] + parts[1] + parts[2], axis=0, keepdims=True)
-    pb = [x.astype(BF) for x in parts]
-    mixed = dot_nn(
-        jnp.concatenate([v0, v3], axis=1), jnp.concatenate(pb[:2], axis=0)
-    ) + jnp.concatenate([dot_nn(v2, pb[2][:, :BLOCK]), dot_nn(v1, pb[2][:, BLOCK:])], axis=1)
+    total = jnp.sum((parts[0] + parts[1]) + (parts[2] + parts[3]), axis=0, keepdims=True)
+    mixed = dot_nn(v_t, jnp.concatenate([x.astype(BF) for x in parts], axis=0))
     return peak, total, mixed
 
 
 def far_backward(k_t, v, q, p_ref, factor, g, ec):
-    k0, k1, k2, k3 = k_t
-    v0, v1, v2, v3 = v
-    e_out = p_ref[: 2 * BLOCK, :] * factor
-    e_mid = p_ref[2 * BLOCK :, :] * factor
-    eb_out, eb_mid = e_out.astype(BF), e_mid.astype(BF)
-    p_out = dot_nt(jnp.concatenate([v0, v3], axis=0), g)
-    p_mid = jnp.concatenate([dot_nt(v2, g[:BLOCK]), dot_nt(v1, g[BLOCK:])], axis=1)
-    r_out = (e_out * (p_out - ec)).astype(BF)
-    r_mid = (e_mid * (p_mid - ec)).astype(BF)
-    dv03 = dot_nn(eb_out, g)
-    dv2 = dot_nn(eb_mid[:, :BLOCK], g[:BLOCK])
-    dv1 = dot_nn(eb_mid[:, BLOCK:], g[BLOCK:])
-    dk03 = dot_nn(r_out, q)
-    dk2 = dot_nn(r_mid[:, :BLOCK], q[:BLOCK])
-    dk1 = dot_nn(r_mid[:, BLOCK:], q[BLOCK:])
-    dq_t = dot_nn(jnp.concatenate([k0, k3], axis=1), r_out) + jnp.concatenate(
-        [dot_nn(k2, r_mid[:, :BLOCK]), dot_nn(k1, r_mid[:, BLOCK:])], axis=1
-    )
-    return (dk03[:BLOCK], dk1, dk2, dk03[BLOCK:]), (dv03[:BLOCK], dv1, dv2, dv03[BLOCK:]), dq_t
+    e = p_ref[...] * factor
+    r = (e * (dot_nt(v, g) - ec)).astype(BF)
+    return dot_nn(r, q), dot_nn(e.astype(BF), g), dot_nn(k_t, r)
 
 
 def main_kernel(
@@ -258,11 +242,13 @@
         gs[pl.ds(own_at, 512), :] = qg_own[:, vc]
         gs[pl.ds(got_at, 512), :] = qg_got[:, vc]
 
-        def blocks(ref, n, which):
-            return [ref[n, b * BLOCK : (b + 1) * BLOCK, :] for b in which]
-
-        def blocks_t(ref, n, which):
-            return [ref[n, :, b * BLOCK : (b + 1) * BLOCK] for b in which]
+        def sides(ref, n, j):
+            before, after = slice(2 * j * BLOCK, 2 * j * BLOCK + 256), slice(
+                (2 * j + 4) * BLOCK, (2 * j + 4) * BLOCK + 256
+            )
+            if ref is one:
+                return jnp.concatenate([ref[n, before, :], ref[n, after, :]], axis=0)
+            return jnp.concatenate([ref[n, :, before], ref[n, :, after]], axis=1)
 
         q_parents = [qs[i * PARENT : (i + 1) * PARENT, :] for i in range(4)]
         q1 = [
@@ -270,18 +256,12 @@
             for j in range(2)
         ]
         q2 = jnp.concatenate([pool2(x) for x in q_parents], axis=0)
-        which1 = [(0, 1, 4, 5), (2, 3, 6, 7)]
         bias1 = [(left_bias, None), (None, right_bias)]
-        which2 = (0, 1, 2, 3)
         far1 = [
-            far_forward(
-                blocks(one, 0, which1[j]), blocks_t(one_t, 1, which1[j]), q1[j], bias1[j], p1.at[j]
-            )
+            far_forward(sides(one, 0, j), sides(one_t, 1, j), q1[j], bias1[j], p1.at[j])
             for j in range(2)
         ]
-        far2 = far_forward(
-            blocks(two, 0, which2), blocks_t(two_t, 1, which2), q2, (left_bias, right_bias), p2
-        )
+        far2 = far_forward(two[0], two_t[1], q2, (left_bias, right_bias), p2)
         acc0[...] = jnp.zeros_like(acc0)
         g1_t, ec1, f1 = [], [], []
         g2_t, ec2, low2 = [], [], []
@@ -350,12 +330,12 @@
             pair = slice(2 * j, 2 * j + 2)
             g1 = jnp.concatenate([x.astype(F32).T.astype(BF) for x in g1_t[pair]], axis=0)
             dk, dv, dq = far_backward(
-                blocks_t(one_t, 0, which1[j]), blocks(one, 1, which1[j]), q1[j], p1.at[j],
+                sides(one_t, 0, j), sides(one, 1, j), q1[j], p1.at[j],
                 jnp.concatenate(f1[pair], axis=1), g1, jnp.concatenate(ec1[pair], axis=1),
             )
-            for n, b in enumerate(which1[j]):
-                acc1[0, b * BLOCK : (b + 1) * BLOCK, :] += dk[n]
-                acc1[1, b * BLOCK : (b + 1) * BLOCK, :] += dv[n]
+            for n, x in ((0, dk), (1, dv)):
+                acc1[n, 2 * j * BLOCK : 2 * j * BLOCK + 256, :] += x[:256]
+                acc1[n, (2 * j + 4) * BLOCK : (2 * j + 4) * BLOCK + 256, :] += x[256:]
             dq1.append(dq)
 
         def joined(parts):
@@ -369,12 +349,7 @@
 
         g2 = joined(g2_t).T.astype(BF)
         f2 = 4.0 * jnp.exp2(far2[0] * TO_LOG2 - joined(low2))
-        dk, dv, dq2 = far_backward(
-            blocks_t(two_t, 0, which2), blocks(two, 1, which2), q2, p2, f2, g2, joined(ec2)
-        )
-        for n in range(4):
-            acc2[0, n * BLOCK : (n + 1) * BLOCK, :] = dk[n]
-            acc2[1, n * BLOCK : (n + 1) * BLOCK, :] = dv[n]
+        acc2[0], acc2[1], dq2 = far_backward(two_t[0], two[1], q2, p2, f2, g2, joined(ec2))
         for i in range(4):
             j, half = i // 2, i % 2
             d1 = dq1[j][:, half * BLOCK : (half + 1) * BLOCK]
@@ -430,8 +405,8 @@
             pltpu.VMEM((1024, HEAD), BF),
             pltpu.VMEM((1024, HEAD), BF),
             pltpu.VMEM((768, PARENT), F32),
-            pltpu.VMEM((2, 384, PARENT), F32),
-            pltpu.VMEM((384, PARENT), F32),
+            pltpu.VMEM((2, 512, PARENT), F32),
+            pltpu.VMEM((512, PARENT), F32),
             pltpu.VMEM((2, 1536, HEAD), F32),
             pltpu.VMEM((2, 1024, HEAD), F32),
             pltpu.VMEM((2, 512, HEAD), F32),
@@ -590,7 +565,7 @@
         near = lax.ppermute(near, axes, near_edges)
         return near, lax.ppermute(wide, axes, wide_edges)
 
-    kv_far = pack(False, where, key_matrix, value_matrix)
+    kv_far = pack(False, where, key_matrix, value_matrix, limit=60)
     qg_far = pack(False, where, queries, cotangent)
     packed = pack(True, where, key_matrix, value_matrix, queries, cotangent)
     kv, qg = packed[:CHUNKS], packed[CHUNKS:]

time: 63.2 us -> 64.4 us (1.019)
  Pallas kernels: 24.3 us -> 27 us
  local copies, waits for them, and re-layouts: 2.1 us -> 0.02 us
    unnamed x12 -> x10, local copies, waits for them, and re-layouts: 2.1 us -> 0.02 us
    pallas_call x3, Pallas kernels: 3.9 us -> 5.79 us  [pack(): pl.pallas_call(functools.partial(pack_kernel, own), in_specs=[smem()] + [...]
    pallas_call x2, Pallas kernels: 11.9 us -> 12.7 us  [main(): pl.pallas_call(main_kernel, in_specs=[smem()] + [vmem()] * 6, out_specs=[...]
where the time goes in v10:
time: 64.4 us; the launch traced here: 63.8 us
  Pallas kernels  27 us (42%)
  starting transfers between devices  21.3 us (33%)
  waiting for transfers between devices  14 us (22%)
  between operations  1.01 us (2%)
    pallas_call x2, Pallas kernels, main(): pl.pallas_call(main_kernel, in_specs=[smem()] + [vmem()] * 6, out_specs=[...  12.7 us
    ppermute x8, waiting for transfers between devices, swap(): return lax.ppermute(x, axes, across)  10.3 us
    ppermute x8, starting transfers between devices, swap(): return lax.ppermute(x, axes, across)  10.3 us
    ppermute x4, starting transfers between devices, beside(): return (near, lax.ppermute(wide, axes, wide_edges))  10.1 us
    pallas_call x3, Pallas kernels, pack(): pl.pallas_call(functools.partial(pack_kernel, own), in_specs=[smem()] + [...  5.79 us
    ppermute x4, waiting for transfers between devices, beside(): return (near, lax.ppermute(wide, axes, wide_edges))  3.71 us
    pallas_call x1, Pallas kernels, unpack_columns(): pl.pallas_call(unpack_columns_kernel, in_specs=[smem()] + [vmem()] * (2 *...  2.21 us
    pallas_call x1, Pallas kernels, unpack_rows(): pl.pallas_call(unpack_rows_kernel, in_specs=[smem()] + [vmem()] * (CHUNKS...  2.07 us
  transfers between devices with their start and end apart: 16, of which 6 were waited for; matrix products, arithmetic and copies ran while one was open for 0% of the time, Pallas kernels for 35%

profile of v10, /device:TPU:12, one launch (start us, length us, event | category | flops | bytes accessed | tf_op | source)
XLA Modules:
  0.0 63.8 jit_solution(15241191341036027827)
XLA Ops:
  1.3 3.0 %shard_map.76 = (bf16[512,256]{1,0:T(8,128)(2,1)}, bf16[512,256]{1,0:T(8,128)(2,1)}) custom-call(s32[4]{0:T(128)} %pad_add_fusion.where, bf16[512,512]{1,0:T(8,128)(2,1)} %refs_0_.4, bf16[512,512]{1,0:T(8,128)(2,1)} %refs_1_.4), custom_call_target="tpu_custom_call" | custom-call | flops 1000 | bytes 1000 | tf_op jit(solution)/shard_map/pallas_call | solution.py:86
  4.3 1.6 %collective-permute-start = (bf16[512,256]{1,0:T(8,128)(2,1)}, bf16[512,256]{1,0:T(8,128)(2,1)S(1)}, u32[]{:S(2)}, u32[]{:S(2)}) collective-permute-start(bf16[512,256]{1,0:T(8,128)(2,1)} %get-tuple-element.47), channel_id=1, source_target_pairs={{0,1},{1,0},{2,3},{3,2},{4,5},{5,4},{6,7},{7,6},{8,9},{9,8},{10,11... | collective-permute-start | bytes 786440 | tf_op jit(solution)/shard_map/ppermute | solution.py:562
  7.5 1.6 %collective-permute-start.3 = (bf16[512,256]{1,0:T(8,128)(2,1)S(1)}, bf16[512,256]{1,0:T(8,128)(2,1)S(1)}, u32[]{:S(2)}, u32[]{:S(2)}) collective-permute-start(bf16[512,256]{1,0:T(8,128)(2,1)S(1)} %get-tuple-element.51), channel_id=1, source_target_pairs={{0,1},{1,0},{2,3},{3,2},{4,5},{5,4},{6,7},{7,6},{8,9},{9,8},{10,11... | collective-permute-start | bytes 786440 | tf_op jit(solution)/shard_map/ppermute | solution.py:562
  9.1 1.6 %shard_map.75 = (bf16[512,256]{1,0:T(8,128)(2,1)S(1)}, bf16[512,256]{1,0:T(8,128)(2,1)S(1)}, bf16[512,256]{1,0:T(8,128)(2,1)S(1)}, bf16[512,256]{1,0:T(8,128)(2,1)S(1)}) custom-call(s32[4]{0:T(128)S(1)} %copy-done.4, bf16[512,512]{1,0:T(8,128)(2,1)S(1)} %copy-done, bf16[512,512]{1,0:T(8,128)(2,1)S(1)} %copy-done.1, bf16[512,512]{1,0:T(8,128)(2,1)S(1)} %copy-done.2, ...), custom_call_target="tpu_custom_call" | custom-call | flops 1000 | bytes 1000 | tf_op jit(solution)/shard_map/pallas_call | solution.py:86
  10.8 3.0 %collective-permute-done.got.kv_got = bf16[512,256]{1,0:T(8,128)(2,1)S(1)} collective-permute-done((bf16[512,256]{1,0:T(8,128)(2,1)}, bf16[512,256]{1,0:T(8,128)(2,1)S(1)}, u32[]{:S(2)}, u32[]{:S(2)}) %collective-permute-start) | collective-permute-done | bytes 262176 | tf_op jit(solution)/shard_map/ppermute | solution.py:562
  14.5 2.5 %collective-permute-start.2 = (bf16[512,256]{1,0:T(8,128)(2,1)S(1)}, bf16[512,256]{1,0:T(8,128)(2,1)S(1)}, u32[]{:S(2)}, u32[]{:S(2)}) collective-permute-start(bf16[512,256]{1,0:T(8,128)(2,1)S(1)} %get-tuple-element.49), channel_id=1, source_target_pairs={{2,4},{3,5},{4,2},{5,3},{6,8},{7,9},{8,6},{9,7},{10,12},{11,13},{1... | collective-permute-start | bytes 786440 | tf_op jit(solution)/shard_map/ppermute | solution.py:566
  17.0 2.3 %collective-permute-done.4.got.kv_got = bf16[512,256]{1,0:T(8,128)(2,1)S(1)} collective-permute-done((bf16[512,256]{1,0:T(8,128)(2,1)}, bf16[512,256]{1,0:T(8,128)(2,1)S(1)}, u32[]{:S(2)}, u32[]{:S(2)}) %collective-permute-start.4) | collective-permute-done | bytes 262176 | tf_op jit(solution)/shard_map/ppermute | solution.py:562
  20.1 2.5 %collective-permute-start.6 = (bf16[512,256]{1,0:T(8,128)(2,1)S(1)}, bf16[512,256]{1,0:T(8,128)(2,1)S(1)}, u32[]{:S(2)}, u32[]{:S(2)}) collective-permute-start(bf16[512,256]{1,0:T(8,128)(2,1)S(1)} %get-tuple-element.59), channel_id=1, source_target_pairs={{2,4},{3,5},{4,2},{5,3},{6,8},{7,9},{8,6},{9,7},{10,12},{11,13},{1... | collective-permute-start | bytes 786440 | tf_op jit(solution)/shard_map/ppermute | solution.py:566
  22.7 1.2 %collective-permute-done.3.qg_got = bf16[512,256]{1,0:T(8,128)(2,1)S(1)} collective-permute-done((bf16[512,256]{1,0:T(8,128)(2,1)S(1)}, bf16[512,256]{1,0:T(8,128)(2,1)S(1)}, u32[]{:S(2)}, u32[]{:S(2)}) %collective-permute-start.3) | collective-permute-done | bytes 262176 | tf_op jit(solution)/shard_map/ppermute | solution.py:562
  23.8 1.5 %collective-permute-start.7 = (bf16[512,256]{1,0:T(8,128)(2,1)S(1)}, bf16[512,256]{1,0:T(8,128)(2,1)S(1)}, u32[]{:S(2)}, u32[]{:S(2)}) collective-permute-start(bf16[512,256]{1,0:T(8,128)(2,1)S(1)} %get-tuple-element.61), channel_id=1, source_target_pairs={{0,1},{1,0},{2,3},{3,2},{4,5},{5,4},{6,7},{7,6},{8,9},{9,8},{10,11... | collective-permute-start | bytes 786440 | tf_op jit(solution)/shard_map/ppermute | solution.py:562
  25.3 6.3 %shard_map.79 = (bf16[2,2,128,256]{3,2,1,0:T(8,128)(2,1)S(1)}, bf16[2,2,128,256]{3,2,1,0:T(8,128)(2,1)S(1)}, f32[1024,256]{1,0:T(8,128)S(1)}, bf16[512,256]{1,0:T(8,128)(2,1)S(1)}, bf16[512,256]{1,0:T(8,128)(2,1)S(1)}) custom-call(s32[4]{0:T(128)S(1)} %copy-done.4, bf16[512,256]{1,0:T(8,128)(2,1)S(1)} %get-tuple-element.46.own.kv_own, ...), custom_call_target="tpu_custom_call" | custom-call | flops 1000 | bytes 1000 | tf_op jit(solution)/shard_map/pallas_call | solution.py:387
  31.7 1.2 %collective-permute-start.8 = (bf16[2,2,128,256]{3,2,1,0:T(8,128)(2,1)S(1)}, bf16[2,2,128,256]{3,2,1,0:T(8,128)(2,1)S(1)}, u32[]{:S(2)}, u32[]{:S(2)}) collective-permute-start(bf16[2,2,128,256]{3,2,1,0:T(8,128)(2,1)S(1)} %get-tuple-element.63), channel_id=1, source_target_pairs={{0,1},{1,0},{2,3},{3,2},{4,5},{5,4},{6,7},{7,6},{8,9},{9,8},{10,11... | collective-permute-start | bytes 786440 | tf_op jit(solution)/shard_map/ppermute | solution.py:562
  32.9 2.4 %collective-permute-start.14 = (bf16[512,256]{1,0:T(8,128)(2,1)S(1)}, bf16[512,256]{1,0:T(8,128)(2,1)S(1)}, u32[]{:S(2)}, u32[]{:S(2)}) collective-permute-start(bf16[512,256]{1,0:T(8,128)(2,1)S(1)} %get-tuple-element.80), channel_id=1, source_target_pairs={{2,4},{3,5},{4,2},{5,3},{6,8},{7,9},{8,6},{9,7},{10,12},{11,13},{1... | collective-permute-start | bytes 786440 | tf_op jit(solution)/shard_map/ppermute | solution.py:566
  35.3 6.3 %shard_map.81 = (bf16[2,2,128,256]{3,2,1,0:T(8,128)(2,1)S(1)}, bf16[2,2,128,256]{3,2,1,0:T(8,128)(2,1)S(1)}, f32[1024,256]{1,0:T(8,128)S(1)}, bf16[512,256]{1,0:T(8,128)(2,1)S(1)}, bf16[512,256]{1,0:T(8,128)(2,1)S(1)}) custom-call(s32[4]{0:T(128)S(1)} %copy-done.4, bf16[512,256]{1,0:T(8,128)(2,1)S(1)} %get-tuple-element.53.own.kv_own, ...), custom_call_target="tpu_custom_call" | custom-call | flops 1000 | bytes 1000 | tf_op jit(solution)/shard_map/pallas_call | solution.py:387
  41.7 1.2 %collective-permute-start.9 = (bf16[2,2,128,256]{3,2,1,0:T(8,128)(2,1)S(1)}, bf16[2,2,128,256]{3,2,1,0:T(8,128)(2,1)S(1)}, u32[]{:S(2)}, u32[]{:S(2)}) collective-permute-start(bf16[2,2,128,256]{3,2,1,0:T(8,128)(2,1)S(1)} %get-tuple-element.67), channel_id=1, source_target_pairs={{0,1},{1,0},{2,3},{3,2},{4,5},{5,4},{6,7},{7,6},{8,9},{9,8},{10,11... | collective-permute-start | bytes 786440 | tf_op jit(solution)/shard_map/ppermute | solution.py:562
  43.7 2.7 %collective-permute-start.11 = (bf16[512,256]{1,0:T(8,128)(2,1)S(1)}, bf16[512,256]{1,0:T(8,128)(2,1)S(1)}, u32[]{:S(2)}, u32[]{:S(2)}) collective-permute-start(bf16[512,256]{1,0:T(8,128)(2,1)S(1)} %get-tuple-element.70), channel_id=1, source_target_pairs={{2,4},{3,5},{4,2},{5,3},{6,8},{7,9},{8,6},{9,7},{10,12},{11,13},{1... | collective-permute-start | bytes 786440 | tf_op jit(solution)/shard_map/ppermute | solution.py:566
  47.1 1.3 %collective-permute-start.15 = (bf16[512,256]{1,0:T(8,128)(2,1)S(1)}, bf16[512,256]{1,0:T(8,128)(2,1)S(1)}, u32[]{:S(2)}, u32[]{:S(2)}) collective-permute-start(bf16[512,256]{1,0:T(8,128)(2,1)S(1)} %get-tuple-element.83), channel_id=1, source_target_pairs={{0,1},{1,0},{2,3},{3,2},{4,5},{5,4},{6,7},{7,6},{8,9},{9,8},{10,11... | collective-permute-start | bytes 786440 | tf_op jit(solution)/shard_map/ppermute | solution.py:562
  48.3 2.1 %collective-permute-done.9.refs_3_ = bf16[2,2,128,256]{3,2,1,0:T(8,128)(2,1)S(1)} collective-permute-done((bf16[2,2,128,256]{3,2,1,0:T(8,128)(2,1)S(1)}, bf16[2,2,128,256]{3,2,1,0:T(8,128)(2,1)S(1)}, u32[]{:S(2)}, u32[]{:S(2)}) %collective-permute-start.9) | collective-permute-done | bytes 262176 | tf_op jit(solution)/shard_map/ppermute | solution.py:562
  50.4 3.7 %collective-permute-done.11.wide_got = bf16[512,256]{1,0:T(8,128)(2,1)S(1)} collective-permute-done((bf16[512,256]{1,0:T(8,128)(2,1)S(1)}, bf16[512,256]{1,0:T(8,128)(2,1)S(1)}, u32[]{:S(2)}, u32[]{:S(2)}) %collective-permute-start.11) | collective-permute-done | bytes 262176 | tf_op jit(solution)/shard_map/ppermute | solution.py:566
  54.8 1.4 %collective-permute-start.12 = (bf16[512,256]{1,0:T(8,128)(2,1)S(1)}, bf16[512,256]{1,0:T(8,128)(2,1)S(1)}, u32[]{:S(2)}, u32[]{:S(2)}) collective-permute-start(bf16[512,256]{1,0:T(8,128)(2,1)S(1)} %get-tuple-element.77), channel_id=1, source_target_pairs={{0,1},{1,0},{2,3},{3,2},{4,5},{5,4},{6,7},{7,6},{8,9},{9,8},{10,11... | collective-permute-start | bytes 786440 | tf_op jit(solution)/shard_map/ppermute | solution.py:562
  56.3 2.2 %shard_map.82 = (bf16[512,512]{1,0:T(8,128)(2,1)}, bf16[512,512]{1,0:T(8,128)(2,1)}) custom-call(s32[4]{0:T(128)S(1)} %copy-done.4, bf16[2,2,128,256]{3,2,1,0:T(8,128)(2,1)S(1)} %get-tuple-element.52.refs_0_, bf16[2,2,128,256]{3,2,1,0:T(8,128)(2,1)S(1)} %get-tuple-element.62.refs_1_, bf16[2,2,128,256]{3,2,1,0:T(8,128)(2,1)S(1)} %collective-permute-done.8.refs_2_, ...), custom_call_target="tpu_custom_call" | custom-call | flops 1000 | bytes 1000 | tf_op jit(solution)/shard_map/pallas_call | solution.py:540
  58.5 2.1 %shard_map.85 = (bf16[512,512]{1,0:T(8,128)(2,1)}, bf16[512,512]{1,0:T(8,128)(2,1)}) custom-call(s32[4]{0:T(128)S(1)} %copy-done.4, bf16[512,256]{1,0:T(8,128)(2,1)S(1)} %get-tuple-element.81.refs_0_, bf16[512,256]{1,0:T(8,128)(2,1)S(1)} %get-tuple-element.82.refs_1_, bf16[512,256]{1,0:T(8,128)(2,1)S(1)} %collective-permute-done.15.refs_2_), custom_call_target="tpu_custom_call" | custom-call | flops 1000 | bytes 1000 | tf_op jit(solution)/shard_map/pallas_call | solution.py:480
  60.6 1.6 %collective-permute-done.12.got = bf16[512,256]{1,0:T(8,128)(2,1)S(1)} collective-permute-done((bf16[512,256]{1,0:T(8,128)(2,1)S(1)}, bf16[512,256]{1,0:T(8,128)(2,1)S(1)}, u32[]{:S(2)}, u32[]{:S(2)}) %collective-permute-start.12) | collective-permute-done | bytes 262176 | tf_op jit(solution)/shard_map/ppermute | solution.py:562
  62.2 1.5 %shard_map.86 = (bf16[512,512]{1,0:T(8,128)(2,1)}, bf16[512,512]{1,0:T(8,128)(2,1)}) custom-call(s32[4]{0:T(128)S(1)} %copy-done.4, bf16[512,256]{1,0:T(8,128)(2,1)S(1)} %collective-permute-done.12.got, bf16[512,512]{1,0:T(8,128)(2,1)} %get-tuple-element.84.first_in, ...), custom_call_target="tpu_custom_call", output_to_operand_aliasing={{0}: (2, {}), {1}: (3, {})} | custom-call | flops 1000 | bytes 1000 | tf_op jit(solution)/shard_map/pallas_call | solution.py:510
  (31 shorter events, 5.9 us)
Async XLA Ops:
  1.3 5.1 %copy-start.2 = (bf16[512,512]{1,0:T(8,128)(2,1)S(1)}, bf16[512,512]{1,0:T(8,128)(2,1)}, u32[]{:S(2)}) copy-start(bf16[512,512]{1,0:T(8,128)(2,1)} %refs_0_.5) | copy-start | bytes 1572868
  1.3 5.1 %copy-start.3 = (bf16[512,512]{1,0:T(8,128)(2,1)S(1)}, bf16[512,512]{1,0:T(8,128)(2,1)}, u32[]{:S(2)}) copy-start(bf16[512,512]{1,0:T(8,128)(2,1)} %refs_1_.5) | copy-start | bytes 1572868
  4.3 2.1 %copy-start.4 = (s32[4]{0:T(128)S(1)}, s32[4]{0:T(128)}, u32[]{:S(2)}) copy-start(s32[4]{0:T(128)} %pad_add_fusion.where) | copy-start | bytes 52
  4.3 9.5 %collective-permute-start = (bf16[512,256]{1,0:T(8,128)(2,1)}, bf16[512,256]{1,0:T(8,128)(2,1)S(1)}, u32[]{:S(2)}, u32[]{:S(2)}) collective-permute-start(bf16[512,256]{1,0:T(8,128)(2,1)} %get-tuple-element.47), channel_id=1, source_target_pairs={{0,1},{1,0},{2,3},{3,2},{4,5},{5,4},{6,7},{7,6},{8,9},{9,8},{10,11... | collective-permute-start | bytes 786440 | tf_op jit(solution)/shard_map/ppermute | solution.py:562
  5.8 3.2 %copy-start = (bf16[512,512]{1,0:T(8,128)(2,1)S(1)}, bf16[512,512]{1,0:T(8,128)(2,1)}, u32[]{:S(2)}) copy-start(bf16[512,512]{1,0:T(8,128)(2,1)} %refs_0_.4) | copy-start | bytes 1572868
  5.8 3.2 %copy-start.1 = (bf16[512,512]{1,0:T(8,128)(2,1)S(1)}, bf16[512,512]{1,0:T(8,128)(2,1)}, u32[]{:S(2)}) copy-start(bf16[512,512]{1,0:T(8,128)(2,1)} %refs_1_.4) | copy-start | bytes 1572868
  5.8 13.5 %collective-permute-start.4 = (bf16[512,256]{1,0:T(8,128)(2,1)}, bf16[512,256]{1,0:T(8,128)(2,1)S(1)}, u32[]{:S(2)}, u32[]{:S(2)}) collective-permute-start(bf16[512,256]{1,0:T(8,128)(2,1)} %get-tuple-element.54), channel_id=1, source_target_pairs={{0,1},{1,0},{2,3},{3,2},{4,5},{5,4},{6,7},{7,6},{8,9},{9,8},{10,11... | collective-permute-start | bytes 786440 | tf_op jit(solution)/shard_map/ppermute | solution.py:562
  7.5 16.3 %collective-permute-start.3 = (bf16[512,256]{1,0:T(8,128)(2,1)S(1)}, bf16[512,256]{1,0:T(8,128)(2,1)S(1)}, u32[]{:S(2)}, u32[]{:S(2)}) collective-permute-start(bf16[512,256]{1,0:T(8,128)(2,1)S(1)} %get-tuple-element.51), channel_id=1, source_target_pairs={{0,1},{1,0},{2,3},{3,2},{4,5},{5,4},{6,7},{7,6},{8,9},{9,8},{10,11... | collective-permute-start | bytes 786440 | tf_op jit(solution)/shard_map/ppermute | solution.py:562
  14.4 10.9 %collective-permute-start.1 = (bf16[512,256]{1,0:T(8,128)(2,1)S(1)}, bf16[512,256]{1,0:T(8,128)(2,1)S(1)}, u32[]{:S(2)}, u32[]{:S(2)}) collective-permute-start(bf16[512,256]{1,0:T(8,128)(2,1)S(1)} %get-tuple-element.48), channel_id=1, source_target_pairs={{0,2},{1,3},{2,0},{3,1},{4,6},{5,7},{6,4},{7,5},{8,10},{9,11},{10,... | collective-permute-start | bytes 786440 | tf_op jit(solution)/shard_map/ppermute | solution.py:565
  14.5 10.8 %collective-permute-start.2 = (bf16[512,256]{1,0:T(8,128)(2,1)S(1)}, bf16[512,256]{1,0:T(8,128)(2,1)S(1)}, u32[]{:S(2)}, u32[]{:S(2)}) collective-permute-start(bf16[512,256]{1,0:T(8,128)(2,1)S(1)} %get-tuple-element.49), channel_id=1, source_target_pairs={{2,4},{3,5},{4,2},{5,3},{6,8},{7,9},{8,6},{9,7},{10,12},{11,13},{1... | collective-permute-start | bytes 786440 | tf_op jit(solution)/shard_map/ppermute | solution.py:566
  20.1 12.9 %collective-permute-start.5 = (bf16[512,256]{1,0:T(8,128)(2,1)S(1)}, bf16[512,256]{1,0:T(8,128)(2,1)S(1)}, u32[]{:S(2)}, u32[]{:S(2)}) collective-permute-start(bf16[512,256]{1,0:T(8,128)(2,1)S(1)} %get-tuple-element.58), channel_id=1, source_target_pairs={{0,2},{1,3},{2,0},{3,1},{4,6},{5,7},{6,4},{7,5},{8,10},{9,11},{10,... | collective-permute-start | bytes 786440 | tf_op jit(solution)/shard_map/ppermute | solution.py:565
  20.1 15.2 %collective-permute-start.6 = (bf16[512,256]{1,0:T(8,128)(2,1)S(1)}, bf16[512,256]{1,0:T(8,128)(2,1)S(1)}, u32[]{:S(2)}, u32[]{:S(2)}) collective-permute-start(bf16[512,256]{1,0:T(8,128)(2,1)S(1)} %get-tuple-element.59), channel_id=1, source_target_pairs={{2,4},{3,5},{4,2},{5,3},{6,8},{7,9},{8,6},{9,7},{10,12},{11,13},{1... | collective-permute-start | bytes 786440 | tf_op jit(solution)/shard_map/ppermute | solution.py:566
  23.8 11.5 %collective-permute-start.7 = (bf16[512,256]{1,0:T(8,128)(2,1)S(1)}, bf16[512,256]{1,0:T(8,128)(2,1)S(1)}, u32[]{:S(2)}, u32[]{:S(2)}) collective-permute-start(bf16[512,256]{1,0:T(8,128)(2,1)S(1)} %get-tuple-element.61), channel_id=1, source_target_pairs={{0,1},{1,0},{2,3},{3,2},{4,5},{5,4},{6,7},{7,6},{8,9},{9,8},{10,11... | collective-permute-start | bytes 786440 | tf_op jit(solution)/shard_map/ppermute | solution.py:562
  31.7 11.2 %collective-permute-start.8 = (bf16[2,2,128,256]{3,2,1,0:T(8,128)(2,1)S(1)}, bf16[2,2,128,256]{3,2,1,0:T(8,128)(2,1)S(1)}, u32[]{:S(2)}, u32[]{:S(2)}) collective-permute-start(bf16[2,2,128,256]{3,2,1,0:T(8,128)(2,1)S(1)} %get-tuple-element.63), channel_id=1, source_target_pairs={{0,1},{1,0},{2,3},{3,2},{4,5},{5,4},{6,7},{7,6},{8,9},{9,8},{10,11... | collective-permute-start | bytes 786440 | tf_op jit(solution)/shard_map/ppermute | solution.py:562
  32.9 13.4 %collective-permute-start.13 = (bf16[512,256]{1,0:T(8,128)(2,1)S(1)}, bf16[512,256]{1,0:T(8,128)(2,1)S(1)}, u32[]{:S(2)}, u32[]{:S(2)}) collective-permute-start(bf16[512,256]{1,0:T(8,128)(2,1)S(1)} %get-tuple-element.79), channel_id=1, source_target_pairs={{0,2},{1,3},{2,0},{3,1},{4,6},{5,7},{6,4},{7,5},{8,10},{9,11},{10,... | collective-permute-start | bytes 786440 | tf_op jit(solution)/shard_map/ppermute | solution.py:565
  32.9 13.4 %collective-permute-start.14 = (bf16[512,256]{1,0:T(8,128)(2,1)S(1)}, bf16[512,256]{1,0:T(8,128)(2,1)S(1)}, u32[]{:S(2)}, u32[]{:S(2)}) collective-permute-start(bf16[512,256]{1,0:T(8,128)(2,1)S(1)} %get-tuple-element.80), channel_id=1, source_target_pairs={{2,4},{3,5},{4,2},{5,3},{6,8},{7,9},{8,6},{9,7},{10,12},{11,13},{1... | collective-permute-start | bytes 786440 | tf_op jit(solution)/shard_map/ppermute | solution.py:566
  41.7 8.8 %collective-permute-start.9 = (bf16[2,2,128,256]{3,2,1,0:T(8,128)(2,1)S(1)}, bf16[2,2,128,256]{3,2,1,0:T(8,128)(2,1)S(1)}, u32[]{:S(2)}, u32[]{:S(2)}) collective-permute-start(bf16[2,2,128,256]{3,2,1,0:T(8,128)(2,1)S(1)} %get-tuple-element.67), channel_id=1, source_target_pairs={{0,1},{1,0},{2,3},{3,2},{4,5},{5,4},{6,7},{7,6},{8,9},{9,8},{10,11... | collective-permute-start | bytes 786440 | tf_op jit(solution)/shard_map/ppermute | solution.py:562
  42.9 7.5 %collective-permute-start.10 = (bf16[512,256]{1,0:T(8,128)(2,1)S(1)}, bf16[512,256]{1,0:T(8,128)(2,1)S(1)}, u32[]{:S(2)}, u32[]{:S(2)}) collective-permute-start(bf16[512,256]{1,0:T(8,128)(2,1)S(1)} %get-tuple-element.69), channel_id=1, source_target_pairs={{0,2},{1,3},{2,0},{3,1},{4,6},{5,7},{6,4},{7,5},{8,10},{9,11},{10,... | collective-permute-start | bytes 786440 | tf_op jit(solution)/shard_map/ppermute | solution.py:565
  43.7 10.5 %collective-permute-start.11 = (bf16[512,256]{1,0:T(8,128)(2,1)S(1)}, bf16[512,256]{1,0:T(8,128)(2,1)S(1)}, u32[]{:S(2)}, u32[]{:S(2)}) collective-permute-start(bf16[512,256]{1,0:T(8,128)(2,1)S(1)} %get-tuple-element.70), channel_id=1, source_target_pairs={{2,4},{3,5},{4,2},{5,3},{6,8},{7,9},{8,6},{9,7},{10,12},{11,13},{1... | collective-permute-start | bytes 786440 | tf_op jit(solution)/shard_map/ppermute | solution.py:566
  47.1 11.4 %collective-permute-start.15 = (bf16[512,256]{1,0:T(8,128)(2,1)S(1)}, bf16[512,256]{1,0:T(8,128)(2,1)S(1)}, u32[]{:S(2)}, u32[]{:S(2)}) collective-permute-start(bf16[512,256]{1,0:T(8,128)(2,1)S(1)} %get-tuple-element.83), channel_id=1, source_target_pairs={{0,1},{1,0},{2,3},{3,2},{4,5},{5,4},{6,7},{7,6},{8,9},{9,8},{10,11... | collective-permute-start | bytes 786440 | tf_op jit(solution)/shard_map/ppermute | solution.py:562
  54.8 7.3 %collective-permute-start.12 = (bf16[512,256]{1,0:T(8,128)(2,1)S(1)}, bf16[512,256]{1,0:T(8,128)(2,1)S(1)}, u32[]{:S(2)}, u32[]{:S(2)}) collective-permute-start(bf16[512,256]{1,0:T(8,128)(2,1)S(1)} %get-tuple-element.77), channel_id=1, source_target_pairs={{0,1},{1,0},{2,3},{3,2},{4,5},{5,4},{6,7},{7,6},{8,9},{9,8},{10,11... | collective-permute-start | bytes 786440 | tf_op jit(solution)/shard_map/ppermute | solution.py:562

commit v11 on v9

--- a/solution.py
+++ b/solution.py
@@ -159,7 +159,33 @@
     return jnp.where(low, x, other) if half == 0 else jnp.where(low, other, x)
 
 
-def far_forward(k, v_t, q, bias, p_ref):
+def split2(x):
+    high = x.astype(BF)
+    return high, (x - high.astype(F32)).astype(BF)
+
+
+def scaled_queries(q):
+    return jnp.concatenate(split2(q.astype(F32) * TO_LOG2), axis=1)
+
+
+def with_offset(g_t, offset):
+    high, low = split2(-offset)
+    count = offset.shape[1]
+    row = lax.broadcasted_iota(jnp.int32, (16, count), 0)
+    tail = jnp.where(row == 0, high.astype(F32), jnp.where(row == 1, low.astype(F32), 0.0))
+    zeros = jnp.zeros((HEAD - 16, count), BF)
+    return jnp.concatenate([g_t.astype(BF), tail.astype(BF), zeros], axis=0)
+
+
+def to_rows(factor):
+    return jnp.broadcast_to(factor, (HEAD, factor.shape[1])).T
+
+
+def times(x, rows):
+    return (x.astype(F32) * rows).astype(BF)
+
+
+def far_forward(k, v_t, q, bias, p_ref, pb_ref):
     k0, k1, k2, k3 = k
     v0, v1, v2, v3 = v_t
     left, right = bias
@@ -175,30 +201,26 @@
         mid_low = mid_low + right
     mid = jnp.concatenate([mid_low, mid_high], axis=1)
     peak = jnp.max(jnp.maximum(jnp.maximum(first, last), mid), axis=0, keepdims=True)
-    parts = [jnp.exp2((x - peak) * TO_LOG2) for x in (first, last, mid)]
-    for n, x in enumerate(parts):
+    for n, x in enumerate((first, last, mid)):
+        x = jnp.exp2(x - peak)
         p_ref[n * BLOCK : (n + 1) * BLOCK, :] = x
-    total = jnp.sum(parts[0] + parts[1] + parts[2], axis=0, keepdims=True)
-    pb = [x.astype(BF) for x in parts]
-    mixed = dot_nn(
-        jnp.concatenate([v0, v3], axis=1), jnp.concatenate(pb[:2], axis=0)
-    ) + jnp.concatenate([dot_nn(v2, pb[2][:, :BLOCK]), dot_nn(v1, pb[2][:, BLOCK:])], axis=1)
-    return peak, total, mixed
-
-
-def far_backward(k_t, v, q, p_ref, factor, g, ec):
+        pb_ref[n * BLOCK : (n + 1) * BLOCK, :] = x.astype(BF)
+    mixed = dot_nn(jnp.concatenate([v0, v3], axis=1), pb_ref[: 2 * BLOCK, :]) + jnp.concatenate(
+        [dot_nn(v2, pb_ref[2 * BLOCK :, :BLOCK]), dot_nn(v1, pb_ref[2 * BLOCK :, BLOCK:])], axis=1
+    )
+    return peak, mixed[HEAD : HEAD + 1], mixed[:HEAD]
+
+
+def far_backward(k_t, v, q, p_ref, pb_ref, g, g_t):
     k0, k1, k2, k3 = k_t
     v0, v1, v2, v3 = v
-    e_out = p_ref[: 2 * BLOCK, :] * factor
-    e_mid = p_ref[2 * BLOCK :, :] * factor
-    eb_out, eb_mid = e_out.astype(BF), e_mid.astype(BF)
-    p_out = dot_nt(jnp.concatenate([v0, v3], axis=0), g)
-    p_mid = jnp.concatenate([dot_nt(v2, g[:BLOCK]), dot_nt(v1, g[BLOCK:])], axis=1)
-    r_out = (e_out * (p_out - ec)).astype(BF)
-    r_mid = (e_mid * (p_mid - ec)).astype(BF)
-    dv03 = dot_nn(eb_out, g)
-    dv2 = dot_nn(eb_mid[:, :BLOCK], g[:BLOCK])
-    dv1 = dot_nn(eb_mid[:, BLOCK:], g[BLOCK:])
+    p_out = dot_nn(jnp.concatenate([v0, v3], axis=0), g_t)
+    p_mid = jnp.concatenate([dot_nn(v2, g_t[:, :BLOCK]), dot_nn(v1, g_t[:, BLOCK:])], axis=1)
+    r_out = (p_ref[: 2 * BLOCK, :] * p_out).astype(BF)
+    r_mid = (p_ref[2 * BLOCK :, :] * p_mid).astype(BF)
+    dv03 = dot_nn(pb_ref[: 2 * BLOCK, :], g)
+    dv2 = dot_nn(pb_ref[2 * BLOCK :, :BLOCK], g[:BLOCK])
+    dv1 = dot_nn(pb_ref[2 * BLOCK :, BLOCK:], g[BLOCK:])
     dk03 = dot_nn(r_out, q)
     dk2 = dot_nn(r_mid[:, :BLOCK], q[:BLOCK])
     dk1 = dot_nn(r_mid[:, BLOCK:], q[BLOCK:])
@@ -208,10 +230,19 @@
     return (dk03[:BLOCK], dk1, dk2, dk03[BLOCK:]), (dv03[:BLOCK], dv1, dv2, dv03[BLOCK:]), dq_t
 
 
+def blocks(ref, which):
+    return [ref[b * BLOCK : (b + 1) * BLOCK, :] for b in which]
+
+
+def blocks_t(ref, which):
+    return [ref[:, b * BLOCK : (b + 1) * BLOCK] for b in which]
+
+
 def main_kernel(
     where, kv_own, kv_got, near_got, wide_got, qg_own, qg_got,
     oq_own, oq_far, grad, near_out, wide_out,
-    raw, raw_t, one, one_t, two, two_t, qs, gs, p0, p1, p2, acc0, acc1, acc2, oq, halos,
+    k0, k0t, v0, v0t, k1, k1t, v1, v1t, k2, k2t, v2, v2t,
+    qs, gs, p0, p1, p2, p0b, p1b, p2b, acc0, acc1, acc2, oq, halos,
 ):
     side = where[0]
     odd = where[3]
@@ -224,45 +255,47 @@
     right_bias = (1 - where[2]).astype(F32) * MASKED
     own_at = pl.multiple_of(side * 512, 512)
     got_at = pl.multiple_of((1 - side) * 512, 512)
+    for ref in (v0, v1, v2):
+        shape = (ref.shape[0], HEAD)
+        lane = lax.broadcasted_iota(jnp.int32, shape, 1)
+        ref[:, HEAD:] = jnp.where(lane < 2, 1.0, 0.0).astype(BF)
+    for ref in (v0t, v1t, v2t):
+        row = lax.broadcasted_iota(jnp.int32, (16, ref.shape[1]), 0)
+        ref[HEAD:, :] = jnp.where(row == 0, 1.0, 0.0).astype(BF)
     for h in range(width // HEAD):
         kc = slice(h * HEAD, (h + 1) * HEAD)
         vc = slice(width + h * HEAD, width + (h + 1) * HEAD)
-        for n, cols in ((0, kc), (1, vc)):
-            raw[n, 0:256, :] = from_left[0:256, cols]
-            raw[n, pl.ds(256 + own_at, 512), :] = kv_own[:, cols]
-            raw[n, pl.ds(256 + got_at, 512), :] = kv_got[:, cols]
-            raw[n, 1280:1536, :] = from_right[0:256, cols]
-            one[n, 0:128, :] = from_left[256:384, cols]
+        for raw, raw_t, one, one_t, two, two_t, cols in (
+            (k0, k0t, k1, k1t, k2, k2t, kc),
+            (v0, v0t, v1, v1t, v2, v2t, vc),
+        ):
+            half = slice(0, HEAD)
+            raw[0:256, half] = from_left[0:256, cols]
+            raw[pl.ds(256 + own_at, 512), half] = kv_own[:, cols]
+            raw[pl.ds(256 + got_at, 512), half] = kv_got[:, cols]
+            raw[1280:1536, half] = from_right[0:256, cols]
+            one[0:128, half] = from_left[256:384, cols]
             for i in range(6):
-                block = pool1(raw[n, i * PARENT : (i + 1) * PARENT, :])
-                at = (i + 1) * BLOCK
-                one[n, at : at + BLOCK, :] = block
-            one[n, 896:1024, :] = from_right[256:384, cols]
-            two[n, 0:128, :] = from_left[384:512, cols]
-            two[n, 128:192, :] = pool12(one[n, 0:128, :])
-            two[n, 192:256, :] = pool2(raw[n, 0:256, :])
-            two[n, 256:320, :] = pool2(raw[n, 1280:1536, :])
-            two[n, 320:384, :] = pool12(one[n, 896:1024, :])
-            two[n, 384:512, :] = from_right[384:512, cols]
-            for i in range(6):
-                rows = slice(i * PARENT, (i + 1) * PARENT)
-                raw_t[n, :, rows] = raw[n, rows, :].T
-            for i in range(8):
-                rows = slice(i * BLOCK, (i + 1) * BLOCK)
-                one_t[n, :, rows] = one[n, rows, :].T
-            for i in range(4):
-                rows = slice(i * BLOCK, (i + 1) * BLOCK)
-                two_t[n, :, rows] = two[n, rows, :].T
+                one[(i + 1) * BLOCK : (i + 2) * BLOCK, half] = pool1(
+                    raw[i * PARENT : (i + 1) * PARENT, half]
+                )
+            one[896:1024, half] = from_right[256:384, cols]
+            two[0:128, half] = from_left[384:512, cols]
+            two[128:192, half] = pool12(one[0:128, half])
+            two[192:256, half] = pool2(raw[0:256, half])
+            two[256:320, half] = pool2(raw[1280:1536, half])
+            two[320:384, half] = pool12(one[896:1024, half])
+            two[384:512, half] = from_right[384:512, cols]
+            for ref, ref_t, size in ((raw, raw_t, PARENT), (one, one_t, BLOCK), (two, two_t, BLOCK)):
+                for i in range(ref.shape[0] // size):
+                    rows = slice(i * size, (i + 1) * size)
+                    ref_t[:HEAD, rows] = ref[rows, half].T
+        for ref in (k0, k1, k2):
+            ref[:, HEAD:] = ref[:, :HEAD]
         qs[pl.ds(own_at, 512), :] = qg_own[:, kc]
         qs[pl.ds(got_at, 512), :] = qg_got[:, kc]
         gs[pl.ds(own_at, 512), :] = qg_own[:, vc]
         gs[pl.ds(got_at, 512), :] = qg_got[:, vc]
-
-        def blocks(ref, n, which):
-            return [ref[n, b * BLOCK : (b + 1) * BLOCK, :] for b in which]
-
-        def blocks_t(ref, n, which):
-            return [ref[n, :, b * BLOCK : (b + 1) * BLOCK] for b in which]
 
         q_parents = [qs[i * PARENT : (i + 1) * PARENT, :] for i in range(4)]
         q1 = [
@@ -275,12 +308,14 @@
         which2 = (0, 1, 2, 3)
         far1 = [
             far_forward(
-                blocks(one, 0, which1[j]), blocks_t(one_t, 1, which1[j]), q1[j], bias1[j], p1.at[j]
+                blocks(k1, which1[j]), blocks_t(v1t, which1[j]), scaled_queries(q1[j]), bias1[j],
+                p1.at[j], p1b.at[j],
             )
             for j in range(2)
         ]
         far2 = far_forward(
-            blocks(two, 0, which2), blocks_t(two_t, 1, which2), q2, (left_bias, right_bias), p2
+            blocks(k2, which2), blocks_t(v2t, which2), scaled_queries(q2), (left_bias, right_bias),
+            p2, p2b,
         )
         acc0[...] = jnp.zeros_like(acc0)
         g1_t, ec1, f1 = [], [], []
@@ -290,7 +325,7 @@
             rows = slice(i * PARENT, i * PARENT + 3 * PARENT)
             q = q_parents[i]
             g = gs[i * PARENT : (i + 1) * PARENT, :]
-            s = dot_nt(raw[0, rows, :], q)
+            s = dot_nt(k0[rows, :], scaled_queries(q))
             pieces = [s[:PARENT], s[PARENT : 2 * PARENT], s[2 * PARENT :]]
             if i == 0:
                 pieces[0] = pieces[0] + left_bias
@@ -299,11 +334,12 @@
             m0 = jnp.max(
                 jnp.maximum(jnp.maximum(pieces[0], pieces[1]), pieces[2]), axis=0, keepdims=True
             )
-            e = [jnp.exp2((x - m0) * TO_LOG2) for x in pieces]
-            for n in range(3):
-                p0[n * PARENT : (n + 1) * PARENT, :] = e[n]
-            z0 = jnp.sum(e[0] + e[1] + e[2], axis=0, keepdims=True)
-            u0 = dot_nn(raw_t[1, :, rows], jnp.concatenate([x.astype(BF) for x in e], axis=0))
+            for n, x in enumerate(pieces):
+                x = jnp.exp2(x - m0)
+                p0[n * PARENT : (n + 1) * PARENT, :] = x
+                p0b[n * PARENT : (n + 1) * PARENT, :] = x.astype(BF)
+            u0 = dot_nn(v0t[:, rows], p0b[...])
+            z0, u0 = u0[HEAD : HEAD + 1], u0[:HEAD]
             j, half = i // 2, i % 2
             lanes = slice(half * BLOCK, (half + 1) * BLOCK)
             m1, z1, u1 = (x[:, lanes] for x in far1[j])
@@ -311,14 +347,14 @@
             m2, z2, u2 = (spread64(x[:, lanes2], half) for x in far2)
             m1w, m2w = twice(m1, 1), twice(m2, 1)
             m = jnp.maximum(jnp.maximum(m0, m1w), m2w)
-            a0 = jnp.exp2((m0 - m) * TO_LOG2)
-            a1 = 2.0 * jnp.exp2((m1w - m) * TO_LOG2)
-            a2 = 4.0 * jnp.exp2((m2w - m) * TO_LOG2)
+            a0 = jnp.exp2(m0 - m)
+            a1 = 2.0 * jnp.exp2(m1w - m)
+            a2 = 4.0 * jnp.exp2(m2w - m)
             z = a0 * z0 + a1 * twice(z1, 1) + a2 * twice(z2, 1)
             inv = 1.0 / z
             o = ((a0 * inv) * u0 + (a1 * inv) * twice(u1, 1) + (a2 * inv) * twice(u2, 1)).astype(BF)
             oq[i, 0, h * HEAD : (h + 1) * HEAD, :] = o
-            lg = m * TO_LOG2 + jnp.log2(z)
+            lg = m + jnp.log2(z)
             g_t = g.astype(F32).T
             dr = jnp.sum(o.astype(F32) * g_t, axis=0, keepdims=True)
             lg_a, lg_b = lg[:, :BLOCK], lg[:, BLOCK:]
@@ -326,9 +362,9 @@
             dr_a, dr_b = dr[:, :BLOCK], dr[:, BLOCK:]
             low = jnp.minimum(lg_a, lg_b)
             w_a, w_b = jnp.exp2(low - lg_a), jnp.exp2(low - lg_b)
-            g1_t.append((w_a * g_a + w_b * g_b).astype(BF))
+            g1_t.append(w_a * g_a + w_b * g_b)
             ec1.append(w_a * dr_a + w_b * dr_b)
-            f1.append(2.0 * jnp.exp2(m1 * TO_LOG2 - low))
+            f1.append(2.0 * jnp.exp2(m1 - low))
             lower = jnp.minimum(low, swap64(low))
             w_a, w_b = jnp.exp2(lower - lg_a), jnp.exp2(lower - lg_b)
             part = w_a * g_a + w_b * g_b
@@ -336,27 +372,26 @@
             part = w_a * dr_a + w_b * dr_b
             ec2.append(part + swap64(part))
             low2.append(lower)
-            f0 = jnp.exp2(m0 * TO_LOG2 - lg)
-            products = dot_nt(raw[1, rows, :], g)
-            weights = p0[...] * f0
-            eb = weights.astype(BF)
-            r = (weights * (products - dr)).astype(BF)
-            acc0[1, rows, :] += dot_nn(eb, g)
-            acc0[0, rows, :] += dot_nn(r, q)
-            dq0.append(dot_nn(raw_t[0, :, rows], r))
+            f0 = jnp.exp2(m0 - lg)
+            f_rows = to_rows(f0)
+            products = dot_nn(v0[rows, :], with_offset(g_t, dr))
+            r = (p0[...] * products).astype(BF)
+            acc0[1, rows, :] += dot_nn(p0b[...], times(g, f_rows))
+            acc0[0, rows, :] += dot_nn(r, times(q, f_rows))
+            dq0.append(f0 * dot_nn(k0t[:, rows], r))
         acc1[...] = jnp.zeros_like(acc1)
         dq1 = []
         for j in range(2):
             pair = slice(2 * j, 2 * j + 2)
-            g1 = jnp.concatenate([x.astype(F32).T.astype(BF) for x in g1_t[pair]], axis=0)
+            g_t, ec, f = (jnp.concatenate(x[pair], axis=1) for x in (g1_t, ec1, f1))
             dk, dv, dq = far_backward(
-                blocks_t(one_t, 0, which1[j]), blocks(one, 1, which1[j]), q1[j], p1.at[j],
-                jnp.concatenate(f1[pair], axis=1), g1, jnp.concatenate(ec1[pair], axis=1),
+                blocks_t(k1t, which1[j]), blocks(v1, which1[j]), times(q1[j], to_rows(f)),
+                p1.at[j], p1b.at[j], (g_t * f).T.astype(BF), with_offset(g_t, ec),
             )
             for n, b in enumerate(which1[j]):
                 acc1[0, b * BLOCK : (b + 1) * BLOCK, :] += dk[n]
                 acc1[1, b * BLOCK : (b + 1) * BLOCK, :] += dv[n]
-            dq1.append(dq)
+            dq1.append(f * dq)
 
         def joined(parts):
             return jnp.concatenate(
@@ -367,11 +402,13 @@
                 axis=1,
             )
 
-        g2 = joined(g2_t).T.astype(BF)
-        f2 = 4.0 * jnp.exp2(far2[0] * TO_LOG2 - joined(low2))
+        g_t, ec = joined(g2_t), joined(ec2)
+        f = 4.0 * jnp.exp2(far2[0] - joined(low2))
         dk, dv, dq2 = far_backward(
-            blocks_t(two_t, 0, which2), blocks(two, 1, which2), q2, p2, f2, g2, joined(ec2)
+            blocks_t(k2t, which2), blocks(v2, which2), times(q2, to_rows(f)), p2, p2b,
+            (g_t * f).T.astype(BF), with_offset(g_t, ec),
         )
+        dq2 = f * dq2
         for n in range(4):
             acc2[0, n * BLOCK : (n + 1) * BLOCK, :] = dk[n]
             acc2[1, n * BLOCK : (n + 1) * BLOCK, :] = dv[n]
@@ -421,17 +458,18 @@
             halo_shape,
         ],
         scratch_shapes=[
-            pltpu.VMEM((2, 1536, HEAD), BF),
-            pltpu.VMEM((2, HEAD, 1536), BF),
-            pltpu.VMEM((2, 1024, HEAD), BF),
-            pltpu.VMEM((2, HEAD, 1024), BF),
-            pltpu.VMEM((2, 512, HEAD), BF),
-            pltpu.VMEM((2, HEAD, 512), BF),
+            *(
+                pltpu.VMEM(shape, BF)
+                for rows in (1536, 1024, 512)
+                for shape in ((rows, 2 * HEAD), (HEAD, rows), (rows, 2 * HEAD), (HEAD + 16, rows))
+            ),
             pltpu.VMEM((1024, HEAD), BF),
             pltpu.VMEM((1024, HEAD), BF),
-            pltpu.VMEM((768, PARENT), F32),
-            pltpu.VMEM((2, 384, PARENT), F32),
-            pltpu.VMEM((384, PARENT), F32),
+            *(
+                pltpu.VMEM(shape, kind)
+                for kind in (F32, BF)
+                for shape in ((768, PARENT), (2, 384, PARENT), (384, PARENT))
+            ),
             pltpu.VMEM((2, 1536, HEAD), F32),
             pltpu.VMEM((2, 1024, HEAD), F32),
             pltpu.VMEM((2, 512, HEAD), F32),

time: 63.2 us -> 66.1 us (1.046)
  Pallas kernels: 24.3 us -> 27.3 us
    pallas_call x2, Pallas kernels: 11.9 us -> 14.8 us  [main(): pl.pallas_call(main_kernel, in_specs=[smem()] + [vmem()] * 6, out_specs=[...]
  transfers between devices with their start and end apart: 16 -> 16, of which waited for: 6 -> 6; matrix products, arithmetic and copies ran while one was open for 0% -> 0% of each run, Pallas kernels for 35% -> 38%
where the time goes in v11:
time: 66.1 us; the launch traced here: 65.5 us
  Pallas kernels  27.3 us (41%)
  starting transfers between devices  21.2 us (32%)
  waiting for transfers between devices  13.8 us (21%)
  local copies, waits for them, and re-layouts  2.1 us (3%)
  between operations  1 us (2%)
    pallas_call x2, Pallas kernels, main(): pl.pallas_call(main_kernel, in_specs=[smem()] + [vmem()] * 6, out_specs=[...  14.8 us
    ppermute x8, starting transfers between devices, swap(): return lax.ppermute(x, axes, across)  10.3 us
    ppermute x8, waiting for transfers between devices, swap(): return lax.ppermute(x, axes, across)  10.2 us
    ppermute x4, starting transfers between devices, beside(): return (near, lax.ppermute(wide, axes, wide_edges))  10.1 us
    pallas_call x3, Pallas kernels, pack(): pl.pallas_call(functools.partial(pack_kernel, own), in_specs=[smem()] + [...  3.9 us
    ppermute x4, waiting for transfers between devices, beside(): return (near, lax.ppermute(wide, axes, wide_edges))  3.68 us
    pallas_call x1, Pallas kernels, unpack_columns(): pl.pallas_call(unpack_columns_kernel, in_specs=[smem()] + [vmem()] * (2 *...  2.21 us
    unnamed x12, local copies, waits for them, and re-layouts  2.1 us
  transfers between devices with their start and end apart: 16, of which 6 were waited for; matrix products, arithmetic and copies ran while one was open for 0% of the time, Pallas kernels for 38%

profile of v11, /device:TPU:12, one launch (start us, length us, event | category | flops | bytes accessed | tf_op | source)
XLA Modules:
  0.0 65.5 jit_solution(1235131441666738516)
XLA Ops:
  2.8 1.1 %shard_map.76 = (bf16[512,256]{1,0:T(8,128)(2,1)S(1)}, bf16[512,256]{1,0:T(8,128)(2,1)S(1)}) custom-call(s32[4]{0:T(128)S(1)} %pad_add_fusion.where, bf16[512,512]{1,0:T(8,128)(2,1)S(1)} %copy-done, bf16[512,512]{1,0:T(8,128)(2,1)S(1)} %copy-done.2), custom_call_target="tpu_custom_call" | custom-call | flops 1000 | bytes 1000 | tf_op jit(solution)/shard_map/pallas_call | solution.py:86
  4.0 1.6 %collective-permute-start = (bf16[512,256]{1,0:T(8,128)(2,1)S(1)}, bf16[512,256]{1,0:T(8,128)(2,1)S(1)}, u32[]{:S(2)}, u32[]{:S(2)}) collective-permute-start(bf16[512,256]{1,0:T(8,128)(2,1)S(1)} %get-tuple-element.47), channel_id=1, source_target_pairs={{0,1},{1,0},{2,3},{3,2},{4,5},{5,4},{6,7},{7,6},{8,9},{9,8},{10,11... | collective-permute-start | bytes 786440 | tf_op jit(solution)/shard_map/ppermute | solution.py:625
  7.2 1.5 %collective-permute-start.3 = (bf16[512,256]{1,0:T(8,128)(2,1)S(1)}, bf16[512,256]{1,0:T(8,128)(2,1)S(1)}, u32[]{:S(2)}, u32[]{:S(2)}) collective-permute-start(bf16[512,256]{1,0:T(8,128)(2,1)S(1)} %get-tuple-element.51), channel_id=1, source_target_pairs={{0,1},{1,0},{2,3},{3,2},{4,5},{5,4},{6,7},{7,6},{8,9},{9,8},{10,11... | collective-permute-start | bytes 786440 | tf_op jit(solution)/shard_map/ppermute | solution.py:625
  8.8 1.6 %shard_map.75 = (bf16[512,256]{1,0:T(8,128)(2,1)S(1)}, bf16[512,256]{1,0:T(8,128)(2,1)S(1)}, bf16[512,256]{1,0:T(8,128)(2,1)S(1)}, bf16[512,256]{1,0:T(8,128)(2,1)S(1)}) custom-call(s32[4]{0:T(128)S(1)} %pad_add_fusion.where, bf16[512,512]{1,0:T(8,128)(2,1)S(1)} %copy-done.1, bf16[512,512]{1,0:T(8,128)(2,1)S(1)} %copy-done.3, ...), custom_call_target="tpu_custom_call" | custom-call | flops 1000 | bytes 1000 | tf_op jit(solution)/shard_map/pallas_call | solution.py:86
  10.4 2.8 %collective-permute-done.got.kv_got = bf16[512,256]{1,0:T(8,128)(2,1)S(1)} collective-permute-done((bf16[512,256]{1,0:T(8,128)(2,1)S(1)}, bf16[512,256]{1,0:T(8,128)(2,1)S(1)}, u32[]{:S(2)}, u32[]{:S(2)}) %collective-permute-start) | collective-permute-done | bytes 262176 | tf_op jit(solution)/shard_map/ppermute | solution.py:625
  14.0 2.5 %collective-permute-start.2 = (bf16[512,256]{1,0:T(8,128)(2,1)S(1)}, bf16[512,256]{1,0:T(8,128)(2,1)S(1)}, u32[]{:S(2)}, u32[]{:S(2)}) collective-permute-start(bf16[512,256]{1,0:T(8,128)(2,1)S(1)} %get-tuple-element.49), channel_id=1, source_target_pairs={{2,4},{3,5},{4,2},{5,3},{6,8},{7,9},{8,6},{9,7},{10,12},{11,13},{1... | collective-permute-start | bytes 786440 | tf_op jit(solution)/shard_map/ppermute | solution.py:629
  16.5 2.3 %collective-permute-done.4.got.kv_got = bf16[512,256]{1,0:T(8,128)(2,1)S(1)} collective-permute-done((bf16[512,256]{1,0:T(8,128)(2,1)S(1)}, bf16[512,256]{1,0:T(8,128)(2,1)S(1)}, u32[]{:S(2)}, u32[]{:S(2)}) %collective-permute-start.4) | collective-permute-done | bytes 262176 | tf_op jit(solution)/shard_map/ppermute | solution.py:625
  19.6 2.5 %collective-permute-start.6 = (bf16[512,256]{1,0:T(8,128)(2,1)S(1)}, bf16[512,256]{1,0:T(8,128)(2,1)S(1)}, u32[]{:S(2)}, u32[]{:S(2)}) collective-permute-start(bf16[512,256]{1,0:T(8,128)(2,1)S(1)} %get-tuple-element.59), channel_id=1, source_target_pairs={{2,4},{3,5},{4,2},{5,3},{6,8},{7,9},{8,6},{9,7},{10,12},{11,13},{1... | collective-permute-start | bytes 786440 | tf_op jit(solution)/shard_map/ppermute | solution.py:629
  22.1 1.2 %collective-permute-done.3.qg_got = bf16[512,256]{1,0:T(8,128)(2,1)S(1)} collective-permute-done((bf16[512,256]{1,0:T(8,128)(2,1)S(1)}, bf16[512,256]{1,0:T(8,128)(2,1)S(1)}, u32[]{:S(2)}, u32[]{:S(2)}) %collective-permute-start.3) | collective-permute-done | bytes 262176 | tf_op jit(solution)/shard_map/ppermute | solution.py:625
  23.3 1.5 %collective-permute-start.7 = (bf16[512,256]{1,0:T(8,128)(2,1)S(1)}, bf16[512,256]{1,0:T(8,128)(2,1)S(1)}, u32[]{:S(2)}, u32[]{:S(2)}) collective-permute-start(bf16[512,256]{1,0:T(8,128)(2,1)S(1)} %get-tuple-element.61), channel_id=1, source_target_pairs={{0,1},{1,0},{2,3},{3,2},{4,5},{5,4},{6,7},{7,6},{8,9},{9,8},{10,11... | collective-permute-start | bytes 786440 | tf_op jit(solution)/shard_map/ppermute | solution.py:625
  24.8 7.4 %shard_map.79 = (bf16[2,2,128,256]{3,2,1,0:T(8,128)(2,1)S(1)}, bf16[2,2,128,256]{3,2,1,0:T(8,128)(2,1)S(1)}, f32[1024,256]{1,0:T(8,128)S(1)}, bf16[512,256]{1,0:T(8,128)(2,1)S(1)}, bf16[512,256]{1,0:T(8,128)(2,1)S(1)}) custom-call(s32[4]{0:T(128)S(1)} %pad_add_fusion.where, bf16[512,256]{1,0:T(8,128)(2,1)S(1)} %get-tuple-element.46.own.kv_own, ...), custom_call_target="tpu_custom_call" | custom-call | flops 1000 | bytes 1000 | tf_op jit(solution)/shard_map/pallas_call | solution.py:449
  32.3 1.2 %collective-permute-start.8 = (bf16[2,2,128,256]{3,2,1,0:T(8,128)(2,1)S(1)}, bf16[2,2,128,256]{3,2,1,0:T(8,128)(2,1)S(1)}, u32[]{:S(2)}, u32[]{:S(2)}) collective-permute-start(bf16[2,2,128,256]{3,2,1,0:T(8,128)(2,1)S(1)} %get-tuple-element.63), channel_id=1, source_target_pairs={{0,1},{1,0},{2,3},{3,2},{4,5},{5,4},{6,7},{7,6},{8,9},{9,8},{10,11... | collective-permute-start | bytes 786440 | tf_op jit(solution)/shard_map/ppermute | solution.py:625
  33.5 2.4 %collective-permute-start.14 = (bf16[512,256]{1,0:T(8,128)(2,1)S(1)}, bf16[512,256]{1,0:T(8,128)(2,1)S(1)}, u32[]{:S(2)}, u32[]{:S(2)}) collective-permute-start(bf16[512,256]{1,0:T(8,128)(2,1)S(1)} %get-tuple-element.80), channel_id=1, source_target_pairs={{2,4},{3,5},{4,2},{5,3},{6,8},{7,9},{8,6},{9,7},{10,12},{11,13},{1... | collective-permute-start | bytes 786440 | tf_op jit(solution)/shard_map/ppermute | solution.py:629
  35.9 7.4 %shard_map.81 = (bf16[2,2,128,256]{3,2,1,0:T(8,128)(2,1)S(1)}, bf16[2,2,128,256]{3,2,1,0:T(8,128)(2,1)S(1)}, f32[1024,256]{1,0:T(8,128)S(1)}, bf16[512,256]{1,0:T(8,128)(2,1)S(1)}, bf16[512,256]{1,0:T(8,128)(2,1)S(1)}) custom-call(s32[4]{0:T(128)S(1)} %pad_add_fusion.where, bf16[512,256]{1,0:T(8,128)(2,1)S(1)} %get-tuple-element.53.own.kv_own, ...), custom_call_target="tpu_custom_call" | custom-call | flops 1000 | bytes 1000 | tf_op jit(solution)/shard_map/pallas_call | solution.py:449
  43.4 1.2 %collective-permute-start.9 = (bf16[2,2,128,256]{3,2,1,0:T(8,128)(2,1)S(1)}, bf16[2,2,128,256]{3,2,1,0:T(8,128)(2,1)S(1)}, u32[]{:S(2)}, u32[]{:S(2)}) collective-permute-start(bf16[2,2,128,256]{3,2,1,0:T(8,128)(2,1)S(1)} %get-tuple-element.67), channel_id=1, source_target_pairs={{0,1},{1,0},{2,3},{3,2},{4,5},{5,4},{6,7},{7,6},{8,9},{9,8},{10,11... | collective-permute-start | bytes 786440 | tf_op jit(solution)/shard_map/ppermute | solution.py:625
  45.3 2.7 %collective-permute-start.11 = (bf16[512,256]{1,0:T(8,128)(2,1)S(1)}, bf16[512,256]{1,0:T(8,128)(2,1)S(1)}, u32[]{:S(2)}, u32[]{:S(2)}) collective-permute-start(bf16[512,256]{1,0:T(8,128)(2,1)S(1)} %get-tuple-element.70), channel_id=1, source_target_pairs={{2,4},{3,5},{4,2},{5,3},{6,8},{7,9},{8,6},{9,7},{10,12},{11,13},{1... | collective-permute-start | bytes 786440 | tf_op jit(solution)/shard_map/ppermute | solution.py:629
  48.7 1.2 %collective-permute-start.15 = (bf16[512,256]{1,0:T(8,128)(2,1)S(1)}, bf16[512,256]{1,0:T(8,128)(2,1)S(1)}, u32[]{:S(2)}, u32[]{:S(2)}) collective-permute-start(bf16[512,256]{1,0:T(8,128)(2,1)S(1)} %get-tuple-element.83), channel_id=1, source_target_pairs={{0,1},{1,0},{2,3},{3,2},{4,5},{5,4},{6,7},{7,6},{8,9},{9,8},{10,11... | collective-permute-start | bytes 786440 | tf_op jit(solution)/shard_map/ppermute | solution.py:625
  49.9 2.2 %collective-permute-done.9.refs_3_ = bf16[2,2,128,256]{3,2,1,0:T(8,128)(2,1)S(1)} collective-permute-done((bf16[2,2,128,256]{3,2,1,0:T(8,128)(2,1)S(1)}, bf16[2,2,128,256]{3,2,1,0:T(8,128)(2,1)S(1)}, u32[]{:S(2)}, u32[]{:S(2)}) %collective-permute-start.9) | collective-permute-done | bytes 262176 | tf_op jit(solution)/shard_map/ppermute | solution.py:625
  52.1 3.7 %collective-permute-done.11.wide_got = bf16[512,256]{1,0:T(8,128)(2,1)S(1)} collective-permute-done((bf16[512,256]{1,0:T(8,128)(2,1)S(1)}, bf16[512,256]{1,0:T(8,128)(2,1)S(1)}, u32[]{:S(2)}, u32[]{:S(2)}) %collective-permute-start.11) | collective-permute-done | bytes 262176 | tf_op jit(solution)/shard_map/ppermute | solution.py:629
  56.5 1.4 %collective-permute-start.12 = (bf16[512,256]{1,0:T(8,128)(2,1)S(1)}, bf16[512,256]{1,0:T(8,128)(2,1)S(1)}, u32[]{:S(2)}, u32[]{:S(2)}) collective-permute-start(bf16[512,256]{1,0:T(8,128)(2,1)S(1)} %get-tuple-element.77), channel_id=1, source_target_pairs={{0,1},{1,0},{2,3},{3,2},{4,5},{5,4},{6,7},{7,6},{8,9},{9,8},{10,11... | collective-permute-start | bytes 786440 | tf_op jit(solution)/shard_map/ppermute | solution.py:625
  57.9 2.2 %shard_map.82 = (bf16[512,512]{1,0:T(8,128)(2,1)}, bf16[512,512]{1,0:T(8,128)(2,1)}) custom-call(s32[4]{0:T(128)S(1)} %pad_add_fusion.where, bf16[2,2,128,256]{3,2,1,0:T(8,128)(2,1)S(1)} %get-tuple-element.52.refs_0_, bf16[2,2,128,256]{3,2,1,0:T(8,128)(2,1)S(1)} %get-tuple-element.62.refs_1_, bf16[2,2,128,256]{3,2,1,0:T(8,128)(2,1)S(1)} %collective-permute-done.8.refs_2_, ...), custom_call_target="tpu_custom_call" | custom-call | flops 1000 | bytes 1000 | tf_op jit(solution)/shard_map/pallas_call | solution.py:603
  60.2 2.1 %shard_map.85 = (bf16[512,512]{1,0:T(8,128)(2,1)}, bf16[512,512]{1,0:T(8,128)(2,1)}) custom-call(s32[4]{0:T(128)S(1)} %pad_add_fusion.where, bf16[512,256]{1,0:T(8,128)(2,1)S(1)} %get-tuple-element.81.refs_0_, bf16[512,256]{1,0:T(8,128)(2,1)S(1)} %get-tuple-element.82.refs_1_, bf16[512,256]{1,0:T(8,128)(2,1)S(1)} %collective-permute-done.15.refs_2_), custom_call_target="tpu_custom_call" | custom-call | flops 1000 | bytes 1000 | tf_op jit(solution)/shard_map/pallas_call | solution.py:543
  62.2 1.6 %collective-permute-done.12.got = bf16[512,256]{1,0:T(8,128)(2,1)S(1)} collective-permute-done((bf16[512,256]{1,0:T(8,128)(2,1)S(1)}, bf16[512,256]{1,0:T(8,128)(2,1)S(1)}, u32[]{:S(2)}, u32[]{:S(2)}) %collective-permute-start.12) | collective-permute-done | bytes 262176 | tf_op jit(solution)/shard_map/ppermute | solution.py:625
  63.8 1.5 %shard_map.86 = (bf16[512,512]{1,0:T(8,128)(2,1)}, bf16[512,512]{1,0:T(8,128)(2,1)}) custom-call(s32[4]{0:T(128)S(1)} %pad_add_fusion.where, bf16[512,256]{1,0:T(8,128)(2,1)S(1)} %collective-permute-done.12.got, bf16[512,512]{1,0:T(8,128)(2,1)} %get-tuple-element.84.first_in, ...), custom_call_target="tpu_custom_call", output_to_operand_aliasing={{0}: (2, {}), {1}: (3, {})} | custom-call | flops 1000 | bytes 1000 | tf_op jit(solution)/shard_map/pallas_call | solution.py:573
  (33 shorter events, 7.5 us)
Async XLA Ops:
  0.7 1.0 %copy-start = (bf16[512,512]{1,0:T(8,128)(2,1)S(1)}, bf16[512,512]{1,0:T(8,128)(2,1)}, u32[]{:S(2)}) copy-start(bf16[512,512]{1,0:T(8,128)(2,1)} %refs_0_.4) | copy-start | bytes 1572868
  1.8 1.0 %copy-start.2 = (bf16[512,512]{1,0:T(8,128)(2,1)S(1)}, bf16[512,512]{1,0:T(8,128)(2,1)}, u32[]{:S(2)}) copy-start(bf16[512,512]{1,0:T(8,128)(2,1)} %refs_1_.4) | copy-start | bytes 1572868
  2.8 3.2 %copy-start.4 = (bf16[512,512]{1,0:T(8,128)(2,1)S(1)}, bf16[512,512]{1,0:T(8,128)(2,1)}, u32[]{:S(2)}) copy-start(bf16[512,512]{1,0:T(8,128)(2,1)} %refs_0_.5) | copy-start | bytes 1572868
  2.8 3.2 %copy-start.5 = (bf16[512,512]{1,0:T(8,128)(2,1)S(1)}, bf16[512,512]{1,0:T(8,128)(2,1)}, u32[]{:S(2)}) copy-start(bf16[512,512]{1,0:T(8,128)(2,1)} %refs_1_.5) | copy-start | bytes 1572868
  4.0 9.3 %collective-permute-start = (bf16[512,256]{1,0:T(8,128)(2,1)S(1)}, bf16[512,256]{1,0:T(8,128)(2,1)S(1)}, u32[]{:S(2)}, u32[]{:S(2)}) collective-permute-start(bf16[512,256]{1,0:T(8,128)(2,1)S(1)} %get-tuple-element.47), channel_id=1, source_target_pairs={{0,1},{1,0},{2,3},{3,2},{4,5},{5,4},{6,7},{7,6},{8,9},{9,8},{10,11... | collective-permute-start | bytes 786440 | tf_op jit(solution)/shard_map/ppermute | solution.py:625
  5.5 3.2 %copy-start.1 = (bf16[512,512]{1,0:T(8,128)(2,1)S(1)}, bf16[512,512]{1,0:T(8,128)(2,1)}, u32[]{:S(2)}) copy-start(bf16[512,512]{1,0:T(8,128)(2,1)} %refs_0_.4) | copy-start | bytes 1572868
  5.5 3.2 %copy-start.3 = (bf16[512,512]{1,0:T(8,128)(2,1)S(1)}, bf16[512,512]{1,0:T(8,128)(2,1)}, u32[]{:S(2)}) copy-start(bf16[512,512]{1,0:T(8,128)(2,1)} %refs_1_.4) | copy-start | bytes 1572868
  5.5 13.3 %collective-permute-start.4 = (bf16[512,256]{1,0:T(8,128)(2,1)S(1)}, bf16[512,256]{1,0:T(8,128)(2,1)S(1)}, u32[]{:S(2)}, u32[]{:S(2)}) collective-permute-start(bf16[512,256]{1,0:T(8,128)(2,1)S(1)} %get-tuple-element.54), channel_id=1, source_target_pairs={{0,1},{1,0},{2,3},{3,2},{4,5},{5,4},{6,7},{7,6},{8,9},{9,8},{10,11... | collective-permute-start | bytes 786440 | tf_op jit(solution)/shard_map/ppermute | solution.py:625
  7.2 16.1 %collective-permute-start.3 = (bf16[512,256]{1,0:T(8,128)(2,1)S(1)}, bf16[512,256]{1,0:T(8,128)(2,1)S(1)}, u32[]{:S(2)}, u32[]{:S(2)}) collective-permute-start(bf16[512,256]{1,0:T(8,128)(2,1)S(1)} %get-tuple-element.51), channel_id=1, source_target_pairs={{0,1},{1,0},{2,3},{3,2},{4,5},{5,4},{6,7},{7,6},{8,9},{9,8},{10,11... | collective-permute-start | bytes 786440 | tf_op jit(solution)/shard_map/ppermute | solution.py:625
  13.9 10.9 %collective-permute-start.1 = (bf16[512,256]{1,0:T(8,128)(2,1)S(1)}, bf16[512,256]{1,0:T(8,128)(2,1)S(1)}, u32[]{:S(2)}, u32[]{:S(2)}) collective-permute-start(bf16[512,256]{1,0:T(8,128)(2,1)S(1)} %get-tuple-element.48), channel_id=1, source_target_pairs={{0,2},{1,3},{2,0},{3,1},{4,6},{5,7},{6,4},{7,5},{8,10},{9,11},{10,... | collective-permute-start | bytes 786440 | tf_op jit(solution)/shard_map/ppermute | solution.py:628
  14.0 10.8 %collective-permute-start.2 = (bf16[512,256]{1,0:T(8,128)(2,1)S(1)}, bf16[512,256]{1,0:T(8,128)(2,1)S(1)}, u32[]{:S(2)}, u32[]{:S(2)}) collective-permute-start(bf16[512,256]{1,0:T(8,128)(2,1)S(1)} %get-tuple-element.49), channel_id=1, source_target_pairs={{2,4},{3,5},{4,2},{5,3},{6,8},{7,9},{8,6},{9,7},{10,12},{11,13},{1... | collective-permute-start | bytes 786440 | tf_op jit(solution)/shard_map/ppermute | solution.py:629
  19.5 14.0 %collective-permute-start.5 = (bf16[512,256]{1,0:T(8,128)(2,1)S(1)}, bf16[512,256]{1,0:T(8,128)(2,1)S(1)}, u32[]{:S(2)}, u32[]{:S(2)}) collective-permute-start(bf16[512,256]{1,0:T(8,128)(2,1)S(1)} %get-tuple-element.58), channel_id=1, source_target_pairs={{0,2},{1,3},{2,0},{3,1},{4,6},{5,7},{6,4},{7,5},{8,10},{9,11},{10,... | collective-permute-start | bytes 786440 | tf_op jit(solution)/shard_map/ppermute | solution.py:628
  19.6 16.3 %collective-permute-start.6 = (bf16[512,256]{1,0:T(8,128)(2,1)S(1)}, bf16[512,256]{1,0:T(8,128)(2,1)S(1)}, u32[]{:S(2)}, u32[]{:S(2)}) collective-permute-start(bf16[512,256]{1,0:T(8,128)(2,1)S(1)} %get-tuple-element.59), channel_id=1, source_target_pairs={{2,4},{3,5},{4,2},{5,3},{6,8},{7,9},{8,6},{9,7},{10,12},{11,13},{1... | collective-permute-start | bytes 786440 | tf_op jit(solution)/shard_map/ppermute | solution.py:629
  23.3 12.6 %collective-permute-start.7 = (bf16[512,256]{1,0:T(8,128)(2,1)S(1)}, bf16[512,256]{1,0:T(8,128)(2,1)S(1)}, u32[]{:S(2)}, u32[]{:S(2)}) collective-permute-start(bf16[512,256]{1,0:T(8,128)(2,1)S(1)} %get-tuple-element.61), channel_id=1, source_target_pairs={{0,1},{1,0},{2,3},{3,2},{4,5},{5,4},{6,7},{7,6},{8,9},{9,8},{10,11... | collective-permute-start | bytes 786440 | tf_op jit(solution)/shard_map/ppermute | solution.py:625
  32.3 12.3 %collective-permute-start.8 = (bf16[2,2,128,256]{3,2,1,0:T(8,128)(2,1)S(1)}, bf16[2,2,128,256]{3,2,1,0:T(8,128)(2,1)S(1)}, u32[]{:S(2)}, u32[]{:S(2)}) collective-permute-start(bf16[2,2,128,256]{3,2,1,0:T(8,128)(2,1)S(1)} %get-tuple-element.63), channel_id=1, source_target_pairs={{0,1},{1,0},{2,3},{3,2},{4,5},{5,4},{6,7},{7,6},{8,9},{9,8},{10,11... | collective-permute-start | bytes 786440 | tf_op jit(solution)/shard_map/ppermute | solution.py:625
  33.5 14.5 %collective-permute-start.13 = (bf16[512,256]{1,0:T(8,128)(2,1)S(1)}, bf16[512,256]{1,0:T(8,128)(2,1)S(1)}, u32[]{:S(2)}, u32[]{:S(2)}) collective-permute-start(bf16[512,256]{1,0:T(8,128)(2,1)S(1)} %get-tuple-element.79), channel_id=1, source_target_pairs={{0,2},{1,3},{2,0},{3,1},{4,6},{5,7},{6,4},{7,5},{8,10},{9,11},{10,... | collective-permute-start | bytes 786440 | tf_op jit(solution)/shard_map/ppermute | solution.py:628
  33.5 14.5 %collective-permute-start.14 = (bf16[512,256]{1,0:T(8,128)(2,1)S(1)}, bf16[512,256]{1,0:T(8,128)(2,1)S(1)}, u32[]{:S(2)}, u32[]{:S(2)}) collective-permute-start(bf16[512,256]{1,0:T(8,128)(2,1)S(1)} %get-tuple-element.80), channel_id=1, source_target_pairs={{2,4},{3,5},{4,2},{5,3},{6,8},{7,9},{8,6},{9,7},{10,12},{11,13},{1... | collective-permute-start | bytes 786440 | tf_op jit(solution)/shard_map/ppermute | solution.py:629
  43.4 8.8 %collective-permute-start.9 = (bf16[2,2,128,256]{3,2,1,0:T(8,128)(2,1)S(1)}, bf16[2,2,128,256]{3,2,1,0:T(8,128)(2,1)S(1)}, u32[]{:S(2)}, u32[]{:S(2)}) collective-permute-start(bf16[2,2,128,256]{3,2,1,0:T(8,128)(2,1)S(1)} %get-tuple-element.67), channel_id=1, source_target_pairs={{0,1},{1,0},{2,3},{3,2},{4,5},{5,4},{6,7},{7,6},{8,9},{9,8},{10,11... | collective-permute-start | bytes 786440 | tf_op jit(solution)/shard_map/ppermute | solution.py:625
  44.6 7.5 %collective-permute-start.10 = (bf16[512,256]{1,0:T(8,128)(2,1)S(1)}, bf16[512,256]{1,0:T(8,128)(2,1)S(1)}, u32[]{:S(2)}, u32[]{:S(2)}) collective-permute-start(bf16[512,256]{1,0:T(8,128)(2,1)S(1)} %get-tuple-element.69), channel_id=1, source_target_pairs={{0,2},{1,3},{2,0},{3,1},{4,6},{5,7},{6,4},{7,5},{8,10},{9,11},{10,... | collective-permute-start | bytes 786440 | tf_op jit(solution)/shard_map/ppermute | solution.py:628
  45.3 10.5 %collective-permute-start.11 = (bf16[512,256]{1,0:T(8,128)(2,1)S(1)}, bf16[512,256]{1,0:T(8,128)(2,1)S(1)}, u32[]{:S(2)}, u32[]{:S(2)}) collective-permute-start(bf16[512,256]{1,0:T(8,128)(2,1)S(1)} %get-tuple-element.70), channel_id=1, source_target_pairs={{2,4},{3,5},{4,2},{5,3},{6,8},{7,9},{8,6},{9,7},{10,12},{11,13},{1... | collective-permute-start | bytes 786440 | tf_op jit(solution)/shard_map/ppermute | solution.py:629
  48.7 11.4 %collective-permute-start.15 = (bf16[512,256]{1,0:T(8,128)(2,1)S(1)}, bf16[512,256]{1,0:T(8,128)(2,1)S(1)}, u32[]{:S(2)}, u32[]{:S(2)}) collective-permute-start(bf16[512,256]{1,0:T(8,128)(2,1)S(1)} %get-tuple-element.83), channel_id=1, source_target_pairs={{0,1},{1,0},{2,3},{3,2},{4,5},{5,4},{6,7},{7,6},{8,9},{9,8},{10,11... | collective-permute-start | bytes 786440 | tf_op jit(solution)/shard_map/ppermute | solution.py:625
  56.5 7.4 %collective-permute-start.12 = (bf16[512,256]{1,0:T(8,128)(2,1)S(1)}, bf16[512,256]{1,0:T(8,128)(2,1)S(1)}, u32[]{:S(2)}, u32[]{:S(2)}) collective-permute-start(bf16[512,256]{1,0:T(8,128)(2,1)S(1)} %get-tuple-element.77), channel_id=1, source_target_pairs={{0,1},{1,0},{2,3},{3,2},{4,5},{5,4},{6,7},{7,6},{8,9},{9,8},{10,11... | collective-permute-start | bytes 786440 | tf_op jit(solution)/shard_map/ppermute | solution.py:625

commit v12 on v9

--- a/solution.py
+++ b/solution.py
@@ -97,6 +97,31 @@
     )(where, *arrays)
 
 
+def pack_cut_kernel(a, b, *outs):
+    order = order_matrix(False)
+    width = a.shape[1] // CHUNKS
+    for m, ref in enumerate((a, b)):
+        for i in range(a.shape[0] // PARENT):
+            rows = slice(i * PARENT, (i + 1) * PARENT)
+            x = dot_nn(order, ref[rows, :]).astype(BF)
+            for c in range(CHUNKS):
+                outs[c][rows, m * width : (m + 1) * width] = x[:, c * width : (c + 1) * width]
+
+
+def pack_cut(side, a, b):
+    rows, columns = a.shape
+    half = columns // 2
+    cut = [lax.dynamic_slice_in_dim(x, side * half, half, 1) for x in (a, b)]
+    return pl.pallas_call(
+        pack_cut_kernel,
+        in_specs=[vmem(), vmem()],
+        out_specs=[vmem()] * CHUNKS,
+        out_shape=[jax.ShapeDtypeStruct((rows, columns // CHUNKS), BF)] * CHUNKS,
+        compiler_params=small(),
+        cost_estimate=light(),
+    )(*cut)
+
+
 def smem():
     return pl.BlockSpec(memory_space=pltpu.SMEM)
 
@@ -113,7 +138,7 @@
     return pl.CostEstimate(flops=1000, bytes_accessed=1000, transcendentals=0)
 
 
-def halo_kernel(where, own, got, near, wide):
+def halo_kernel(where, own, got, wide, near):
     def fill(first, second, to_right, to_left):
         to_right[0:256, :] = second[256:512, :]
         to_right[256:384, :] = pool1(second[0:256, :])
@@ -209,7 +234,7 @@
 
 
 def main_kernel(
-    where, kv_own, kv_got, near_got, wide_got, qg_own, qg_got,
+    where, kv_own, kv_got, wide_got, near_got, qg_own, qg_got,
     oq_own, oq_far, grad, near_out, wide_out,
     raw, raw_t, one, one_t, two, two_t, qs, gs, p0, p1, p2, acc0, acc1, acc2, oq, halos,
 ):
@@ -404,7 +429,7 @@
     wide_out[...] = halos[odd]
 
 
-def main(where, kv_own, kv_got, near_got, wide_got, qg_own, qg_got):
+def main(where, kv_own, kv_got, wide_got, near_got, qg_own, qg_got):
     rows, both = kv_own.shape
     width = both // 2
     oq_shape = jax.ShapeDtypeStruct((2, 2, width, PARENT), BF)
@@ -440,10 +465,10 @@
         ],
         compiler_params=pltpu.CompilerParams(vmem_limit_bytes=24 * 1024 * 1024),
         cost_estimate=light(),
-    )(where, kv_own, kv_got, near_got, wide_got, qg_own, qg_got)
-
-
-def join_kernel(where, grad, near_got, wide_got, own, far):
+    )(where, kv_own, kv_got, wide_got, near_got, qg_own, qg_got)
+
+
+def join_kernel(where, grad, wide_got, near_got, own, far):
     def fill(first, second, from_left, from_right):
         def parent(i):
             return grad[i * PARENT : (i + 1) * PARENT, :]
@@ -473,7 +498,7 @@
                 fill(*halves, *((wide_got, near_got) if odd == 0 else (near_got, wide_got)))
 
 
-def join(where, grad, near_got, wide_got):
+def join(where, grad, wide_got, near_got):
     shape = jax.ShapeDtypeStruct(near_got.shape, BF)
     return pl.pallas_call(
         join_kernel,
@@ -482,7 +507,7 @@
         out_shape=[shape, shape],
         compiler_params=small(),
         cost_estimate=light(),
-    )(where, grad, near_got, wide_got)
+    )(where, grad, wide_got, near_got)
 
 
 def unpack_rows_kernel(where, *refs):
@@ -587,26 +612,26 @@
         return lax.ppermute(x, axes, across)
 
     def beside(near, wide):
-        near = lax.ppermute(near, axes, near_edges)
-        return near, lax.ppermute(wide, axes, wide_edges)
-
-    kv_far = pack(False, where, key_matrix, value_matrix)
+        wide = lax.ppermute(wide, axes, wide_edges)
+        return wide, lax.ppermute(near, axes, near_edges)
+
+    kv_far = pack_cut(1 - device % 2, key_matrix, value_matrix)
     qg_far = pack(False, where, queries, cotangent)
     packed = pack(True, where, key_matrix, value_matrix, queries, cotangent)
     kv, qg = packed[:CHUNKS], packed[CHUNKS:]
     oq_own, oq_got, back = [], [], []
     for c in range(CHUNKS):
         got_kv = swap(kv_far[c])
-        near, wide = halo(where, kv[c], got_kv)
+        wide, near = halo(where, kv[c], got_kv)
         far = qg_far[c]
         if c > 0:
-            near, wide, far = lax.optimization_barrier((near, wide, far))
-        near, wide = beside(near, wide)
-        own, far, grad, near, wide = main(where, kv[c], got_kv, near, wide, qg[c], swap(far))
+            wide, near, far = lax.optimization_barrier((wide, near, far))
+        wide, near = beside(near, wide)
+        own, far, grad, near, wide = main(where, kv[c], got_kv, wide, near, qg[c], swap(far))
         oq_own.append(own)
         oq_got.append(swap(far))
         if c > 0:
-            oq_got[c - 1], near, wide = lax.optimization_barrier((oq_got[c - 1], near, wide))
+            oq_got[c - 1], wide, near = lax.optimization_barrier((oq_got[c - 1], wide, near))
         back.append([grad, *beside(near, wide)])
     oq_got[-1], back[-1] = lax.optimization_barrier((oq_got[-1], back[-1]))
     kv_own, kv_got = [], []

time: 63.2 us -> 62.6 us (level)
  the two profiles are of different devices: /device:TPU:12 before, /device:TPU:0 now
where the time goes in v12:
time: 62.6 us; the launch traced here: 62.4 us
  starting transfers between devices  26.6 us (42%)
  Pallas kernels  23.5 us (38%)
  waiting for transfers between devices  10 us (16%)
  local copies, waits for them, and re-layouts  1.15 us (2%)
  between operations  0.97 us (2%)
    ppermute x4, starting transfers between devices, beside(): return (wide, lax.ppermute(near, axes, near_edges))  13.6 us
    pallas_call x2, Pallas kernels, main(): pl.pallas_call(main_kernel, in_specs=[smem()] + [vmem()] * 6, out_specs=[...  11.9 us
    ppermute x8, starting transfers between devices, swap(): return lax.ppermute(x, axes, across)  10.2 us
    ppermute x8, waiting for transfers between devices, swap(): return lax.ppermute(x, axes, across)  10 us
    ppermute x4, starting transfers between devices, beside(): wide = lax.ppermute(wide, axes, wide_edges)  2.87 us
    pallas_call x2, Pallas kernels, pack(): pl.pallas_call(functools.partial(pack_kernel, own), in_specs=[smem()] + [...  2.79 us
    pallas_call x1, Pallas kernels, unpack_columns(): pl.pallas_call(unpack_columns_kernel, in_specs=[smem()] + [vmem()] * (2 *...  2.21 us
    pallas_call x1, Pallas kernels, unpack_rows(): pl.pallas_call(unpack_rows_kernel, in_specs=[smem()] + [vmem()] * (CHUNKS...  2.07 us
  transfers between devices with their start and end apart: 16, of which 5 were waited for; matrix products, arithmetic and copies ran while one was open for 0% of the time, Pallas kernels for 35%

profile of v12, /device:TPU:0, one launch (start us, length us, event | category | flops | bytes accessed | tf_op | source)
XLA Modules:
  0.0 62.4 jit_solution(10527716838267672999)
XLA Ops:
  0.7 1.1 %constant_dynamic-slice_fusion = (bf16[512,256]{1,0:T(8,128)(2,1)S(1)}, bf16[512,256]{1,0:T(8,128)(2,1)S(1)}) fusion(bf16[512,512]{1,0:T(8,128)(2,1)} %refs_1_.2, s32[]{:T(128)S(6)} %select_n.24, bf16[512,512]{1,0:T(8,128)(2,1)} %refs_0_.2), kind=kLoop, calls=%fused_computation.1 | loop fusion | bytes 1048580 | tf_op jit(solution)/shard_map/dynamic_slice | solution.py:114
  2.1 3.0 %collective-permute-start = (bf16[512,256]{1,0:T(8,128)(2,1)S(1)}, bf16[512,256]{1,0:T(8,128)(2,1)S(1)}, u32[]{:S(2)}, u32[]{:S(2)}) collective-permute-start(bf16[512,256]{1,0:T(8,128)(2,1)S(1)} %get-tuple-element.47), channel_id=1, source_target_pairs={{0,1},{1,0},{2,3},{3,2},{4,5},{5,4},{6,7},{7,6},{8,9},{9,8},{10,11... | collective-permute-start | bytes 786440 | tf_op jit(solution)/shard_map/ppermute | solution.py:612
  5.3 1.1 %shard_map.78 = (bf16[512,256]{1,0:T(8,128)(2,1)S(1)}, bf16[512,256]{1,0:T(8,128)(2,1)S(1)}) custom-call(s32[4]{0:T(128)S(1)} %pad_add_fusion.where, bf16[512,512]{1,0:T(8,128)(2,1)S(1)} %copy-done, bf16[512,512]{1,0:T(8,128)(2,1)S(1)} %copy-done.1), custom_call_target="tpu_custom_call" | custom-call | flops 1000 | bytes 1000 | tf_op jit(solution)/shard_map/pallas_call | solution.py:86
  6.4 2.0 %collective-permute-start.3 = (bf16[512,256]{1,0:T(8,128)(2,1)S(1)}, bf16[512,256]{1,0:T(8,128)(2,1)S(1)}, u32[]{:S(2)}, u32[]{:S(2)}) collective-permute-start(bf16[512,256]{1,0:T(8,128)(2,1)S(1)} %get-tuple-element.51), channel_id=1, source_target_pairs={{0,1},{1,0},{2,3},{3,2},{4,5},{5,4},{6,7},{7,6},{8,9},{9,8},{10,11... | collective-permute-start | bytes 786440 | tf_op jit(solution)/shard_map/ppermute | solution.py:612
  8.5 1.6 %shard_map.75 = (bf16[512,256]{1,0:T(8,128)(2,1)S(1)}, bf16[512,256]{1,0:T(8,128)(2,1)S(1)}, bf16[512,256]{1,0:T(8,128)(2,1)S(1)}, bf16[512,256]{1,0:T(8,128)(2,1)S(1)}) custom-call(s32[4]{0:T(128)S(1)} %pad_add_fusion.where, bf16[512,512]{1,0:T(8,128)(2,1)S(1)} %copy-done.2, bf16[512,512]{1,0:T(8,128)(2,1)S(1)} %copy-done.3, bf16[512,512]{1,0:T(8,128)(2,1)S(1)} %copy-done, ...), custom_call_target="tpu_custom_call" | custom-call | flops 1000 | bytes 1000 | tf_op jit(solution)/shard_map/pallas_call | solution.py:86
  10.1 2.1 %collective-permute-done.got.kv_got = bf16[512,256]{1,0:T(8,128)(2,1)S(1)} collective-permute-done((bf16[512,256]{1,0:T(8,128)(2,1)S(1)}, bf16[512,256]{1,0:T(8,128)(2,1)S(1)}, u32[]{:S(2)}, u32[]{:S(2)}) %collective-permute-start) | collective-permute-done | bytes 262176 | tf_op jit(solution)/shard_map/ppermute | solution.py:612
  13.6 3.5 %collective-permute-start.2 = (bf16[512,256]{1,0:T(8,128)(2,1)S(1)}, bf16[512,256]{1,0:T(8,128)(2,1)S(1)}, u32[]{:S(2)}, u32[]{:S(2)}) collective-permute-start(bf16[512,256]{1,0:T(8,128)(2,1)S(1)} %get-tuple-element.49), channel_id=1, source_target_pairs={{0,2},{1,3},{2,0},{3,1},{4,6},{5,7},{6,4},{7,5},{8,10},{9,11},{10,... | collective-permute-start | bytes 786440 | tf_op jit(solution)/shard_map/ppermute | solution.py:616
  17.1 0.7 %collective-permute-done.4.got.kv_got = bf16[512,256]{1,0:T(8,128)(2,1)S(1)} collective-permute-done((bf16[512,256]{1,0:T(8,128)(2,1)S(1)}, bf16[512,256]{1,0:T(8,128)(2,1)S(1)}, u32[]{:S(2)}, u32[]{:S(2)}) %collective-permute-start.4) | collective-permute-done | bytes 262176 | tf_op jit(solution)/shard_map/ppermute | solution.py:612
  19.2 3.5 %collective-permute-start.6 = (bf16[512,256]{1,0:T(8,128)(2,1)S(1)}, bf16[512,256]{1,0:T(8,128)(2,1)S(1)}, u32[]{:S(2)}, u32[]{:S(2)}) collective-permute-start(bf16[512,256]{1,0:T(8,128)(2,1)S(1)} %get-tuple-element.59), channel_id=1, source_target_pairs={{0,2},{1,3},{2,0},{3,1},{4,6},{5,7},{6,4},{7,5},{8,10},{9,11},{10,... | collective-permute-start | bytes 786440 | tf_op jit(solution)/shard_map/ppermute | solution.py:616
  22.7 1.7 %collective-permute-start.7 = (bf16[512,256]{1,0:T(8,128)(2,1)S(1)}, bf16[512,256]{1,0:T(8,128)(2,1)S(1)}, u32[]{:S(2)}, u32[]{:S(2)}) collective-permute-start(bf16[512,256]{1,0:T(8,128)(2,1)S(1)} %get-tuple-element.61), channel_id=1, source_target_pairs={{0,1},{1,0},{2,3},{3,2},{4,5},{5,4},{6,7},{7,6},{8,9},{9,8},{10,11... | collective-permute-start | bytes 786440 | tf_op jit(solution)/shard_map/ppermute | solution.py:612
  24.4 6.0 %shard_map.79 = (bf16[2,2,128,256]{3,2,1,0:T(8,128)(2,1)S(1)}, bf16[2,2,128,256]{3,2,1,0:T(8,128)(2,1)S(1)}, f32[1024,256]{1,0:T(8,128)S(1)}, bf16[512,256]{1,0:T(8,128)(2,1)S(1)}, bf16[512,256]{1,0:T(8,128)(2,1)S(1)}) custom-call(s32[4]{0:T(128)S(1)} %pad_add_fusion.where, bf16[512,256]{1,0:T(8,128)(2,1)S(1)} %get-tuple-element.46.own.kv_own, ...), custom_call_target="tpu_custom_call" | custom-call | flops 1000 | bytes 1000 | tf_op jit(solution)/shard_map/pallas_call | solution.py:437
  30.8 0.8 %collective-permute-start.13 = (bf16[512,256]{1,0:T(8,128)(2,1)S(1)}, bf16[512,256]{1,0:T(8,128)(2,1)S(1)}, u32[]{:S(2)}, u32[]{:S(2)}) collective-permute-start(bf16[512,256]{1,0:T(8,128)(2,1)S(1)} %get-tuple-element.79), channel_id=1, source_target_pairs={{2,4},{3,5},{4,2},{5,3},{6,8},{7,9},{8,6},{9,7},{10,12},{11,13},{1... | collective-permute-start | bytes 786440 | tf_op jit(solution)/shard_map/ppermute | solution.py:615
  31.7 3.7 %collective-permute-start.14 = (bf16[512,256]{1,0:T(8,128)(2,1)S(1)}, bf16[512,256]{1,0:T(8,128)(2,1)S(1)}, u32[]{:S(2)}, u32[]{:S(2)}) collective-permute-start(bf16[512,256]{1,0:T(8,128)(2,1)S(1)} %get-tuple-element.80), channel_id=1, source_target_pairs={{0,2},{1,3},{2,0},{3,1},{4,6},{5,7},{6,4},{7,5},{8,10},{9,11},{10,... | collective-permute-start | bytes 786440 | tf_op jit(solution)/shard_map/ppermute | solution.py:616
  35.3 6.0 %shard_map.81 = (bf16[2,2,128,256]{3,2,1,0:T(8,128)(2,1)S(1)}, bf16[2,2,128,256]{3,2,1,0:T(8,128)(2,1)S(1)}, f32[1024,256]{1,0:T(8,128)S(1)}, bf16[512,256]{1,0:T(8,128)(2,1)S(1)}, bf16[512,256]{1,0:T(8,128)(2,1)S(1)}) custom-call(s32[4]{0:T(128)S(1)} %pad_add_fusion.where, bf16[512,256]{1,0:T(8,128)(2,1)S(1)} %get-tuple-element.53.own.kv_own, ...), custom_call_target="tpu_custom_call" | custom-call | flops 1000 | bytes 1000 | tf_op jit(solution)/shard_map/pallas_call | solution.py:437
  41.3 1.0 %collective-permute-start.9 = (bf16[2,2,128,256]{3,2,1,0:T(8,128)(2,1)S(1)}, bf16[2,2,128,256]{3,2,1,0:T(8,128)(2,1)S(1)}, u32[]{:S(2)}, u32[]{:S(2)}) collective-permute-start(bf16[2,2,128,256]{3,2,1,0:T(8,128)(2,1)S(1)} %get-tuple-element.67), channel_id=1, source_target_pairs={{0,1},{1,0},{2,3},{3,2},{4,5},{5,4},{6,7},{7,6},{8,9},{9,8},{10,11... | collective-permute-start | bytes 786440 | tf_op jit(solution)/shard_map/ppermute | solution.py:612
  43.0 2.9 %collective-permute-start.11 = (bf16[512,256]{1,0:T(8,128)(2,1)S(1)}, bf16[512,256]{1,0:T(8,128)(2,1)S(1)}, u32[]{:S(2)}, u32[]{:S(2)}) collective-permute-start(bf16[512,256]{1,0:T(8,128)(2,1)S(1)} %get-tuple-element.70), channel_id=1, source_target_pairs={{0,2},{1,3},{2,0},{3,1},{4,6},{5,7},{6,4},{7,5},{8,10},{9,11},{10,... | collective-permute-start | bytes 786440 | tf_op jit(solution)/shard_map/ppermute | solution.py:616
  47.2 2.7 %collective-permute-done.9.refs_3_ = bf16[2,2,128,256]{3,2,1,0:T(8,128)(2,1)S(1)} collective-permute-done((bf16[2,2,128,256]{3,2,1,0:T(8,128)(2,1)S(1)}, bf16[2,2,128,256]{3,2,1,0:T(8,128)(2,1)S(1)}, u32[]{:S(2)}, u32[]{:S(2)}) %collective-permute-start.9) | collective-permute-done | bytes 262176 | tf_op jit(solution)/shard_map/ppermute | solution.py:612
  49.9 0.7 %shard_map.83 = (bf16[512,256]{1,0:T(8,128)(2,1)S(1)}, bf16[512,256]{1,0:T(8,128)(2,1)S(1)}) custom-call(s32[4]{0:T(128)S(1)} %pad_add_fusion.where, f32[1024,256]{1,0:T(8,128)S(1)} %get-tuple-element.74.grad, bf16[512,256]{1,0:T(8,128)(2,1)S(1)} %collective-permute-done.10.wide_got, bf16[512,256]{1,0:T(8,128)(2,1)S(1)} %collective-permute-done.11.near_got), custom_call_target="tpu_custom_call" | custom-call | flops 1000 | bytes 1000 | tf_op jit(solution)/shard_map/pallas_call | solution.py:503
  50.6 1.4 %collective-permute-start.12 = (bf16[512,256]{1,0:T(8,128)(2,1)S(1)}, bf16[512,256]{1,0:T(8,128)(2,1)S(1)}, u32[]{:S(2)}, u32[]{:S(2)}) collective-permute-start(bf16[512,256]{1,0:T(8,128)(2,1)S(1)} %get-tuple-element.77), channel_id=1, source_target_pairs={{0,1},{1,0},{2,3},{3,2},{4,5},{5,4},{6,7},{7,6},{8,9},{9,8},{10,11... | collective-permute-start | bytes 786440 | tf_op jit(solution)/shard_map/ppermute | solution.py:612
  52.0 2.2 %shard_map.82 = (bf16[512,512]{1,0:T(8,128)(2,1)}, bf16[512,512]{1,0:T(8,128)(2,1)}) custom-call(s32[4]{0:T(128)S(1)} %pad_add_fusion.where, bf16[2,2,128,256]{3,2,1,0:T(8,128)(2,1)S(1)} %get-tuple-element.52.refs_0_, bf16[2,2,128,256]{3,2,1,0:T(8,128)(2,1)S(1)} %get-tuple-element.62.refs_1_, bf16[2,2,128,256]{3,2,1,0:T(8,128)(2,1)S(1)} %collective-permute-done.8.refs_2_, ...), custom_call_target="tpu_custom_call" | custom-call | flops 1000 | bytes 1000 | tf_op jit(solution)/shard_map/pallas_call | solution.py:590
  54.2 1.1 %collective-permute-done.15.refs_2_ = bf16[512,256]{1,0:T(8,128)(2,1)S(1)} collective-permute-done((bf16[512,256]{1,0:T(8,128)(2,1)S(1)}, bf16[512,256]{1,0:T(8,128)(2,1)S(1)}, u32[]{:S(2)}, u32[]{:S(2)}) %collective-permute-start.15) | collective-permute-done | bytes 262176 | tf_op jit(solution)/shard_map/ppermute | solution.py:612
  55.2 2.1 %shard_map.85 = (bf16[512,512]{1,0:T(8,128)(2,1)}, bf16[512,512]{1,0:T(8,128)(2,1)}) custom-call(s32[4]{0:T(128)S(1)} %pad_add_fusion.where, bf16[512,256]{1,0:T(8,128)(2,1)S(1)} %get-tuple-element.81.refs_0_, bf16[512,256]{1,0:T(8,128)(2,1)S(1)} %get-tuple-element.82.refs_1_, bf16[512,256]{1,0:T(8,128)(2,1)S(1)} %collective-permute-done.15.refs_2_), custom_call_target="tpu_custom_call" | custom-call | flops 1000 | bytes 1000 | tf_op jit(solution)/shard_map/pallas_call | solution.py:530
  57.3 3.4 %collective-permute-done.12.got = bf16[512,256]{1,0:T(8,128)(2,1)S(1)} collective-permute-done((bf16[512,256]{1,0:T(8,128)(2,1)S(1)}, bf16[512,256]{1,0:T(8,128)(2,1)S(1)}, u32[]{:S(2)}, u32[]{:S(2)}) %collective-permute-start.12) | collective-permute-done | bytes 262176 | tf_op jit(solution)/shard_map/ppermute | solution.py:612
  60.7 1.5 %shard_map.86 = (bf16[512,512]{1,0:T(8,128)(2,1)}, bf16[512,512]{1,0:T(8,128)(2,1)}) custom-call(s32[4]{0:T(128)S(1)} %pad_add_fusion.where, bf16[512,256]{1,0:T(8,128)(2,1)S(1)} %collective-permute-done.12.got, bf16[512,512]{1,0:T(8,128)(2,1)} %get-tuple-element.84.first_in, ...), custom_call_target="tpu_custom_call", output_to_operand_aliasing={{0}: (2, {}), {1}: (3, {})} | custom-call | flops 1000 | bytes 1000 | tf_op jit(solution)/shard_map/pallas_call | solution.py:560
  (30 shorter events, 5.6 us)
Async XLA Ops:
  0.7 4.6 %copy-start.1 = (bf16[512,512]{1,0:T(8,128)(2,1)S(1)}, bf16[512,512]{1,0:T(8,128)(2,1)}, u32[]{:S(2)}) copy-start(bf16[512,512]{1,0:T(8,128)(2,1)} %refs_1_.3) | copy-start | bytes 1572868
  1.8 3.5 %copy-start = (bf16[512,512]{1,0:T(8,128)(2,1)S(1)}, bf16[512,512]{1,0:T(8,128)(2,1)}, u32[]{:S(2)}) copy-start(bf16[512,512]{1,0:T(8,128)(2,1)} %refs_0_.3) | copy-start | bytes 1572868
  2.1 10.1 %collective-permute-start = (bf16[512,256]{1,0:T(8,128)(2,1)S(1)}, bf16[512,256]{1,0:T(8,128)(2,1)S(1)}, u32[]{:S(2)}, u32[]{:S(2)}) collective-permute-start(bf16[512,256]{1,0:T(8,128)(2,1)S(1)} %get-tuple-element.47), channel_id=1, source_target_pairs={{0,1},{1,0},{2,3},{3,2},{4,5},{5,4},{6,7},{7,6},{8,9},{9,8},{10,11... | collective-permute-start | bytes 786440 | tf_op jit(solution)/shard_map/ppermute | solution.py:612
  5.1 12.8 %collective-permute-start.4 = (bf16[512,256]{1,0:T(8,128)(2,1)S(1)}, bf16[512,256]{1,0:T(8,128)(2,1)S(1)}, u32[]{:S(2)}, u32[]{:S(2)}) collective-permute-start(bf16[512,256]{1,0:T(8,128)(2,1)S(1)} %get-tuple-element.54), channel_id=1, source_target_pairs={{0,1},{1,0},{2,3},{3,2},{4,5},{5,4},{6,7},{7,6},{8,9},{9,8},{10,11... | collective-permute-start | bytes 786440 | tf_op jit(solution)/shard_map/ppermute | solution.py:612
  5.3 3.2 %copy-start.2 = (bf16[512,512]{1,0:T(8,128)(2,1)S(1)}, bf16[512,512]{1,0:T(8,128)(2,1)}, u32[]{:S(2)}) copy-start(bf16[512,512]{1,0:T(8,128)(2,1)} %refs_0_.2) | copy-start | bytes 1572868
  5.3 3.2 %copy-start.3 = (bf16[512,512]{1,0:T(8,128)(2,1)S(1)}, bf16[512,512]{1,0:T(8,128)(2,1)}, u32[]{:S(2)}) copy-start(bf16[512,512]{1,0:T(8,128)(2,1)} %refs_1_.2) | copy-start | bytes 1572868
  6.4 16.3 %collective-permute-start.3 = (bf16[512,256]{1,0:T(8,128)(2,1)S(1)}, bf16[512,256]{1,0:T(8,128)(2,1)S(1)}, u32[]{:S(2)}, u32[]{:S(2)}) collective-permute-start(bf16[512,256]{1,0:T(8,128)(2,1)S(1)} %get-tuple-element.51), channel_id=1, source_target_pairs={{0,1},{1,0},{2,3},{3,2},{4,5},{5,4},{6,7},{7,6},{8,9},{9,8},{10,11... | collective-permute-start | bytes 786440 | tf_op jit(solution)/shard_map/ppermute | solution.py:612
  12.9 11.5 %collective-permute-start.1 = (bf16[512,256]{1,0:T(8,128)(2,1)S(1)}, bf16[512,256]{1,0:T(8,128)(2,1)S(1)}, u32[]{:S(2)}, u32[]{:S(2)}) collective-permute-start(bf16[512,256]{1,0:T(8,128)(2,1)S(1)} %get-tuple-element.48), channel_id=1, source_target_pairs={{2,4},{3,5},{4,2},{5,3},{6,8},{7,9},{8,6},{9,7},{10,12},{11,13},{1... | collective-permute-start | bytes 786440 | tf_op jit(solution)/shard_map/ppermute | solution.py:615
  13.6 10.8 %collective-permute-start.2 = (bf16[512,256]{1,0:T(8,128)(2,1)S(1)}, bf16[512,256]{1,0:T(8,128)(2,1)S(1)}, u32[]{:S(2)}, u32[]{:S(2)}) collective-permute-start(bf16[512,256]{1,0:T(8,128)(2,1)S(1)} %get-tuple-element.49), channel_id=1, source_target_pairs={{0,2},{1,3},{2,0},{3,1},{4,6},{5,7},{6,4},{7,5},{8,10},{9,11},{10,... | collective-permute-start | bytes 786440 | tf_op jit(solution)/shard_map/ppermute | solution.py:616
  18.6 13.1 %collective-permute-start.5 = (bf16[512,256]{1,0:T(8,128)(2,1)S(1)}, bf16[512,256]{1,0:T(8,128)(2,1)S(1)}, u32[]{:S(2)}, u32[]{:S(2)}) collective-permute-start(bf16[512,256]{1,0:T(8,128)(2,1)S(1)} %get-tuple-element.58), channel_id=1, source_target_pairs={{2,4},{3,5},{4,2},{5,3},{6,8},{7,9},{8,6},{9,7},{10,12},{11,13},{1... | collective-permute-start | bytes 786440 | tf_op jit(solution)/shard_map/ppermute | solution.py:615
  19.2 16.1 %collective-permute-start.6 = (bf16[512,256]{1,0:T(8,128)(2,1)S(1)}, bf16[512,256]{1,0:T(8,128)(2,1)S(1)}, u32[]{:S(2)}, u32[]{:S(2)}) collective-permute-start(bf16[512,256]{1,0:T(8,128)(2,1)S(1)} %get-tuple-element.59), channel_id=1, source_target_pairs={{0,2},{1,3},{2,0},{3,1},{4,6},{5,7},{6,4},{7,5},{8,10},{9,11},{10,... | collective-permute-start | bytes 786440 | tf_op jit(solution)/shard_map/ppermute | solution.py:616
  22.7 12.6 %collective-permute-start.7 = (bf16[512,256]{1,0:T(8,128)(2,1)S(1)}, bf16[512,256]{1,0:T(8,128)(2,1)S(1)}, u32[]{:S(2)}, u32[]{:S(2)}) collective-permute-start(bf16[512,256]{1,0:T(8,128)(2,1)S(1)} %get-tuple-element.61), channel_id=1, source_target_pairs={{0,1},{1,0},{2,3},{3,2},{4,5},{5,4},{6,7},{7,6},{8,9},{9,8},{10,11... | collective-permute-start | bytes 786440 | tf_op jit(solution)/shard_map/ppermute | solution.py:612
  30.4 11.9 %collective-permute-start.8 = (bf16[2,2,128,256]{3,2,1,0:T(8,128)(2,1)S(1)}, bf16[2,2,128,256]{3,2,1,0:T(8,128)(2,1)S(1)}, u32[]{:S(2)}, u32[]{:S(2)}) collective-permute-start(bf16[2,2,128,256]{3,2,1,0:T(8,128)(2,1)S(1)} %get-tuple-element.63), channel_id=1, source_target_pairs={{0,1},{1,0},{2,3},{3,2},{4,5},{5,4},{6,7},{7,6},{8,9},{9,8},{10,11... | collective-permute-start | bytes 786440 | tf_op jit(solution)/shard_map/ppermute | solution.py:612
  30.8 15.1 %collective-permute-start.13 = (bf16[512,256]{1,0:T(8,128)(2,1)S(1)}, bf16[512,256]{1,0:T(8,128)(2,1)S(1)}, u32[]{:S(2)}, u32[]{:S(2)}) collective-permute-start(bf16[512,256]{1,0:T(8,128)(2,1)S(1)} %get-tuple-element.79), channel_id=1, source_target_pairs={{2,4},{3,5},{4,2},{5,3},{6,8},{7,9},{8,6},{9,7},{10,12},{11,13},{1... | collective-permute-start | bytes 786440 | tf_op jit(solution)/shard_map/ppermute | solution.py:615
  31.7 14.2 %collective-permute-start.14 = (bf16[512,256]{1,0:T(8,128)(2,1)S(1)}, bf16[512,256]{1,0:T(8,128)(2,1)S(1)}, u32[]{:S(2)}, u32[]{:S(2)}) collective-permute-start(bf16[512,256]{1,0:T(8,128)(2,1)S(1)} %get-tuple-element.80), channel_id=1, source_target_pairs={{0,2},{1,3},{2,0},{3,1},{4,6},{5,7},{6,4},{7,5},{8,10},{9,11},{10,... | collective-permute-start | bytes 786440 | tf_op jit(solution)/shard_map/ppermute | solution.py:616
  41.3 8.6 %collective-permute-start.9 = (bf16[2,2,128,256]{3,2,1,0:T(8,128)(2,1)S(1)}, bf16[2,2,128,256]{3,2,1,0:T(8,128)(2,1)S(1)}, u32[]{:S(2)}, u32[]{:S(2)}) collective-permute-start(bf16[2,2,128,256]{3,2,1,0:T(8,128)(2,1)S(1)} %get-tuple-element.67), channel_id=1, source_target_pairs={{0,1},{1,0},{2,3},{3,2},{4,5},{5,4},{6,7},{7,6},{8,9},{9,8},{10,11... | collective-permute-start | bytes 786440 | tf_op jit(solution)/shard_map/ppermute | solution.py:612
  42.3 7.6 %collective-permute-start.10 = (bf16[512,256]{1,0:T(8,128)(2,1)S(1)}, bf16[512,256]{1,0:T(8,128)(2,1)S(1)}, u32[]{:S(2)}, u32[]{:S(2)}) collective-permute-start(bf16[512,256]{1,0:T(8,128)(2,1)S(1)} %get-tuple-element.69), channel_id=1, source_target_pairs={{2,4},{3,5},{4,2},{5,3},{6,8},{7,9},{8,6},{9,7},{10,12},{11,13},{1... | collective-permute-start | bytes 786440 | tf_op jit(solution)/shard_map/ppermute | solution.py:615
  43.0 6.9 %collective-permute-start.11 = (bf16[512,256]{1,0:T(8,128)(2,1)S(1)}, bf16[512,256]{1,0:T(8,128)(2,1)S(1)}, u32[]{:S(2)}, u32[]{:S(2)}) collective-permute-start(bf16[512,256]{1,0:T(8,128)(2,1)S(1)} %get-tuple-element.70), channel_id=1, source_target_pairs={{0,2},{1,3},{2,0},{3,1},{4,6},{5,7},{6,4},{7,5},{8,10},{9,11},{10,... | collective-permute-start | bytes 786440 | tf_op jit(solution)/shard_map/ppermute | solution.py:616
  46.6 8.6 %collective-permute-start.15 = (bf16[512,256]{1,0:T(8,128)(2,1)S(1)}, bf16[512,256]{1,0:T(8,128)(2,1)S(1)}, u32[]{:S(2)}, u32[]{:S(2)}) collective-permute-start(bf16[512,256]{1,0:T(8,128)(2,1)S(1)} %get-tuple-element.83), channel_id=1, source_target_pairs={{0,1},{1,0},{2,3},{3,2},{4,5},{5,4},{6,7},{7,6},{8,9},{9,8},{10,11... | collective-permute-start | bytes 786440 | tf_op jit(solution)/shard_map/ppermute | solution.py:612
  50.6 10.1 %collective-permute-start.12 = (bf16[512,256]{1,0:T(8,128)(2,1)S(1)}, bf16[512,256]{1,0:T(8,128)(2,1)S(1)}, u32[]{:S(2)}, u32[]{:S(2)}) collective-permute-start(bf16[512,256]{1,0:T(8,128)(2,1)S(1)} %get-tuple-element.77), channel_id=1, source_target_pairs={{0,1},{1,0},{2,3},{3,2},{4,5},{5,4},{6,7},{7,6},{8,9},{9,8},{10,11... | collective-permute-start | bytes 786440 | tf_op jit(solution)/shard_map/ppermute | solution.py:612

commit v13 on v9

--- a/solution.py
+++ b/solution.py
@@ -95,6 +95,29 @@
         compiler_params=small(),
         cost_estimate=light(),
     )(where, *arrays)
+
+
+def pack_cut_kernel(a, b, out):
+    order = order_matrix(False)
+    width = a.shape[1]
+    for m, ref in enumerate((a, b)):
+        for i in range(a.shape[0] // PARENT):
+            rows = slice(i * PARENT, (i + 1) * PARENT)
+            out[rows, m * width : (m + 1) * width] = dot_nn(order, ref[rows, :]).astype(BF)
+
+
+def pack_cut(side, chunk, a, b):
+    rows, columns = a.shape
+    width = columns // 2 // CHUNKS
+    cut = [lax.dynamic_slice_in_dim(x, (side * CHUNKS + chunk) * width, width, 1) for x in (a, b)]
+    return pl.pallas_call(
+        pack_cut_kernel,
+        in_specs=[vmem(), vmem()],
+        out_specs=vmem(),
+        out_shape=jax.ShapeDtypeStruct((rows, 2 * width), BF),
+        compiler_params=small(),
+        cost_estimate=light(),
+    )(*cut)
 
 
 def smem():
@@ -208,7 +231,13 @@
     return (dk03[:BLOCK], dk1, dk2, dk03[BLOCK:]), (dv03[:BLOCK], dv1, dv2, dv03[BLOCK:]), dq_t
 
 
-def main_kernel(
+def main_kernel(qg_first, where, kv_own, kv_got, *refs):
+    if qg_first:
+        refs = (*refs[2:4], *refs[:2], *refs[4:])
+    one_chunk(where, kv_own, kv_got, *refs)
+
+
+def one_chunk(
     where, kv_own, kv_got, near_got, wide_got, qg_own, qg_got,
     oq_own, oq_far, grad, near_out, wide_out,
     raw, raw_t, one, one_t, two, two_t, qs, gs, p0, p1, p2, acc0, acc1, acc2, oq, halos,
@@ -404,13 +433,16 @@
     wide_out[...] = halos[odd]
 
 
-def main(where, kv_own, kv_got, near_got, wide_got, qg_own, qg_got):
+def main(where, kv_own, kv_got, near_got, wide_got, qg_own, qg_got, qg_first):
     rows, both = kv_own.shape
     width = both // 2
     oq_shape = jax.ShapeDtypeStruct((2, 2, width, PARENT), BF)
     halo_shape = jax.ShapeDtypeStruct((512, both), BF)
-    return pl.pallas_call(
-        main_kernel,
+    operands = [kv_own, kv_got, near_got, wide_got, qg_own, qg_got]
+    if qg_first:
+        operands = operands[:2] + operands[4:] + operands[2:4]
+    return pl.pallas_call(
+        functools.partial(main_kernel, qg_first),
         in_specs=[smem()] + [vmem()] * 6,
         out_specs=[vmem()] * 5,
         out_shape=[
@@ -440,7 +472,7 @@
         ],
         compiler_params=pltpu.CompilerParams(vmem_limit_bytes=24 * 1024 * 1024),
         cost_estimate=light(),
-    )(where, kv_own, kv_got, near_got, wide_got, qg_own, qg_got)
+    )(where, *operands)
 
 
 def join_kernel(where, grad, near_got, wide_got, own, far):
@@ -590,7 +622,10 @@
         near = lax.ppermute(near, axes, near_edges)
         return near, lax.ppermute(wide, axes, wide_edges)
 
-    kv_far = pack(False, where, key_matrix, value_matrix)
+    kv_far = [pack_cut(1 - device % 2, 0, key_matrix, value_matrix)]
+    for c in range(1, CHUNKS):
+        later, kv_far[0] = lax.optimization_barrier(((key_matrix, value_matrix), kv_far[0]))
+        kv_far.append(pack_cut(1 - device % 2, c, *later))
     qg_far = pack(False, where, queries, cotangent)
     packed = pack(True, where, key_matrix, value_matrix, queries, cotangent)
     kv, qg = packed[:CHUNKS], packed[CHUNKS:]
@@ -602,7 +637,7 @@
         if c > 0:
             near, wide, far = lax.optimization_barrier((near, wide, far))
         near, wide = beside(near, wide)
-        own, far, grad, near, wide = main(where, kv[c], got_kv, near, wide, qg[c], swap(far))
+        own, far, grad, near, wide = main(where, kv[c], got_kv, near, wide, qg[c], swap(far), c == 0)
         oq_own.append(own)
         oq_got.append(swap(far))
         if c > 0:

time: 63.2 us -> 61.2 us (0.968)
  local copies, waits for them, and re-layouts: 2.1 us -> 1.16 us
    unnamed x12 -> x8, local copies, waits for them, and re-layouts: 2.1 us -> 0.06 us
    pallas_call x3 -> x2, Pallas kernels: 3.9 us -> 2.76 us  [pack(): pl.pallas_call(functools.partial(pack_kernel, own), in_specs=[smem()] + [...]
    dynamic_slice x0 -> x3, local copies, waits for them, and re-layouts: none -> 1.1 us  [pack_cut(): lax.dynamic_slice_in_dim(x, (side * CHUNKS + chunk) * width, width, 1)]
    pallas_call x2 -> x4, Pallas kernels: 11.9 us -> 12.5 us  [the longest x2 11.9 us: main(): pl.pallas_call(functools.partial(main_kernel, qg_first), in_specs=[smem()...]
  transfers between devices with their start and end apart: 16 -> 16, of which waited for: 6 -> 6; matrix products, arithmetic and copies ran while one was open for 0% -> 0% of each run, Pallas kernels for 35% -> 36%
where the time goes in v13:
time: 61.2 us; the launch traced here: 60.6 us
  Pallas kernels  23.8 us (39%)
  starting transfers between devices  21.3 us (35%)
  waiting for transfers between devices  13.3 us (22%)
  local copies, waits for them, and re-layouts  1.16 us (2%)
  between operations  1.02 us (2%)
    pallas_call x2, Pallas kernels, main(): pl.pallas_call(functools.partial(main_kernel, qg_first), in_specs=[smem()...  11.9 us
    ppermute x8, starting transfers between devices, swap(): return lax.ppermute(x, axes, across)  10.3 us
    ppermute x4, starting transfers between devices, beside(): return (near, lax.ppermute(wide, axes, wide_edges))  10.1 us
    ppermute x8, waiting for transfers between devices, swap(): return lax.ppermute(x, axes, across)  9.62 us
    ppermute x4, waiting for transfers between devices, beside(): return (near, lax.ppermute(wide, axes, wide_edges))  3.7 us
    pallas_call x2, Pallas kernels, pack(): pl.pallas_call(functools.partial(pack_kernel, own), in_specs=[smem()] + [...  2.76 us
    pallas_call x1, Pallas kernels, unpack_columns(): pl.pallas_call(unpack_columns_kernel, in_specs=[smem()] + [vmem()] * (2 *...  2.21 us
    pallas_call x1, Pallas kernels, unpack_rows(): pl.pallas_call(unpack_rows_kernel, in_specs=[smem()] + [vmem()] * (CHUNKS...  2.07 us
  transfers between devices with their start and end apart: 16, of which 6 were waited for; matrix products, arithmetic and copies ran while one was open for 0% of the time, Pallas kernels for 36%

profile of v13, /device:TPU:12, one launch (start us, length us, event | category | flops | bytes accessed | tf_op | source)
XLA Modules:
  0.0 60.6 jit_solution(1212763561163935771)
XLA Ops:
  2.0 1.6 %collective-permute-start = (bf16[512,256]{1,0:T(8,128)(2,1)S(1)}, bf16[512,256]{1,0:T(8,128)(2,1)S(1)}, u32[]{:S(2)}, u32[]{:S(2)}) collective-permute-start(bf16[512,256]{1,0:T(8,128)(2,1)S(1)} %shard_map.76), channel_id=1, source_target_pairs={{0,1},{1,0},{2,3},{3,2},{4,5},{5,4},{6,7},{7,6},{8,9},{9,8},{10,11... | collective-permute-start | bytes 786440 | tf_op jit(solution)/shard_map/ppermute | solution.py:619
  4.8 1.1 %shard_map.77 = (bf16[512,256]{1,0:T(8,128)(2,1)S(1)}, bf16[512,256]{1,0:T(8,128)(2,1)S(1)}) custom-call(s32[4]{0:T(128)S(1)} %pad_add_fusion.where, bf16[512,512]{1,0:T(8,128)(2,1)S(1)} %copy-done, bf16[512,512]{1,0:T(8,128)(2,1)S(1)} %copy-done.1), custom_call_target="tpu_custom_call" | custom-call | flops 1000 | bytes 1000 | tf_op jit(solution)/shard_map/pallas_call | solution.py:86
  5.9 1.4 %collective-permute-start.1 = (bf16[512,256]{1,0:T(8,128)(2,1)S(1)}, bf16[512,256]{1,0:T(8,128)(2,1)S(1)}, u32[]{:S(2)}, u32[]{:S(2)}) collective-permute-start(bf16[512,256]{1,0:T(8,128)(2,1)S(1)} %get-tuple-element.50), channel_id=1, source_target_pairs={{0,1},{1,0},{2,3},{3,2},{4,5},{5,4},{6,7},{7,6},{8,9},{9,8},{10,11... | collective-permute-start | bytes 786440 | tf_op jit(solution)/shard_map/ppermute | solution.py:619
  7.3 1.6 %shard_map.75 = (bf16[512,256]{1,0:T(8,128)(2,1)S(1)}, bf16[512,256]{1,0:T(8,128)(2,1)S(1)}, bf16[512,256]{1,0:T(8,128)(2,1)S(1)}, bf16[512,256]{1,0:T(8,128)(2,1)S(1)}) custom-call(s32[4]{0:T(128)S(1)} %pad_add_fusion.where, bf16[512,512]{1,0:T(8,128)(2,1)S(1)} %copy-done.2, bf16[512,512]{1,0:T(8,128)(2,1)S(1)} %copy-done.3, bf16[512,512]{1,0:T(8,128)(2,1)S(1)} %copy-done, ...), custom_call_target="tpu_custom_call" | custom-call | flops 1000 | bytes 1000 | tf_op jit(solution)/shard_map/pallas_call | solution.py:86
  9.0 2.3 %collective-permute-done.got.kv_got = bf16[512,256]{1,0:T(8,128)(2,1)S(1)} collective-permute-done((bf16[512,256]{1,0:T(8,128)(2,1)S(1)}, bf16[512,256]{1,0:T(8,128)(2,1)S(1)}, u32[]{:S(2)}, u32[]{:S(2)}) %collective-permute-start) | collective-permute-done | bytes 262176 | tf_op jit(solution)/shard_map/ppermute | solution.py:619
  12.0 2.5 %collective-permute-start.3 = (bf16[512,256]{1,0:T(8,128)(2,1)S(1)}, bf16[512,256]{1,0:T(8,128)(2,1)S(1)}, u32[]{:S(2)}, u32[]{:S(2)}) collective-permute-start(bf16[512,256]{1,0:T(8,128)(2,1)S(1)} %get-tuple-element.52), channel_id=1, source_target_pairs={{2,4},{3,5},{4,2},{5,3},{6,8},{7,9},{8,6},{9,7},{10,12},{11,13},{1... | collective-permute-start | bytes 786440 | tf_op jit(solution)/shard_map/ppermute | solution.py:623
  14.6 2.3 %collective-permute-done.4.got.kv_got = bf16[512,256]{1,0:T(8,128)(2,1)S(1)} collective-permute-done((bf16[512,256]{1,0:T(8,128)(2,1)S(1)}, bf16[512,256]{1,0:T(8,128)(2,1)S(1)}, u32[]{:S(2)}, u32[]{:S(2)}) %collective-permute-start.4) | collective-permute-done | bytes 262176 | tf_op jit(solution)/shard_map/ppermute | solution.py:619
  17.7 2.5 %collective-permute-start.6 = (bf16[512,256]{1,0:T(8,128)(2,1)S(1)}, bf16[512,256]{1,0:T(8,128)(2,1)S(1)}, u32[]{:S(2)}, u32[]{:S(2)}) collective-permute-start(bf16[512,256]{1,0:T(8,128)(2,1)S(1)} %get-tuple-element.61), channel_id=1, source_target_pairs={{2,4},{3,5},{4,2},{5,3},{6,8},{7,9},{8,6},{9,7},{10,12},{11,13},{1... | collective-permute-start | bytes 786440 | tf_op jit(solution)/shard_map/ppermute | solution.py:623
  20.2 1.2 %collective-permute-done.1.refs_1_ = bf16[512,256]{1,0:T(8,128)(2,1)S(1)} collective-permute-done((bf16[512,256]{1,0:T(8,128)(2,1)S(1)}, bf16[512,256]{1,0:T(8,128)(2,1)S(1)}, u32[]{:S(2)}, u32[]{:S(2)}) %collective-permute-start.1) | collective-permute-done | bytes 262176 | tf_op jit(solution)/shard_map/ppermute | solution.py:619
  21.4 1.5 %collective-permute-start.7 = (bf16[512,256]{1,0:T(8,128)(2,1)S(1)}, bf16[512,256]{1,0:T(8,128)(2,1)S(1)}, u32[]{:S(2)}, u32[]{:S(2)}) collective-permute-start(bf16[512,256]{1,0:T(8,128)(2,1)S(1)} %get-tuple-element.63), channel_id=1, source_target_pairs={{0,1},{1,0},{2,3},{3,2},{4,5},{5,4},{6,7},{7,6},{8,9},{9,8},{10,11... | collective-permute-start | bytes 786440 | tf_op jit(solution)/shard_map/ppermute | solution.py:619
  22.9 6.0 %shard_map.79 = (bf16[2,2,128,256]{3,2,1,0:T(8,128)(2,1)S(1)}, bf16[2,2,128,256]{3,2,1,0:T(8,128)(2,1)S(1)}, f32[1024,256]{1,0:T(8,128)S(1)}, bf16[512,256]{1,0:T(8,128)(2,1)S(1)}, bf16[512,256]{1,0:T(8,128)(2,1)S(1)}) custom-call(s32[4]{0:T(128)S(1)} %pad_add_fusion.where, bf16[512,256]{1,0:T(8,128)(2,1)S(1)} %get-tuple-element.47.own.kv_own, ...), custom_call_target="tpu_custom_call" | custom-call | flops 1000 | bytes 1000 | tf_op jit(solution)/shard_map/pallas_call | solution.py:444
  28.8 1.2 %collective-permute-start.8 = (bf16[2,2,128,256]{3,2,1,0:T(8,128)(2,1)S(1)}, bf16[2,2,128,256]{3,2,1,0:T(8,128)(2,1)S(1)}, u32[]{:S(2)}, u32[]{:S(2)}) collective-permute-start(bf16[2,2,128,256]{3,2,1,0:T(8,128)(2,1)S(1)} %get-tuple-element.65), channel_id=1, source_target_pairs={{0,1},{1,0},{2,3},{3,2},{4,5},{5,4},{6,7},{7,6},{8,9},{9,8},{10,11... | collective-permute-start | bytes 786440 | tf_op jit(solution)/shard_map/ppermute | solution.py:619
  30.1 2.4 %collective-permute-start.14 = (bf16[512,256]{1,0:T(8,128)(2,1)S(1)}, bf16[512,256]{1,0:T(8,128)(2,1)S(1)}, u32[]{:S(2)}, u32[]{:S(2)}) collective-permute-start(bf16[512,256]{1,0:T(8,128)(2,1)S(1)} %get-tuple-element.82), channel_id=1, source_target_pairs={{2,4},{3,5},{4,2},{5,3},{6,8},{7,9},{8,6},{9,7},{10,12},{11,13},{1... | collective-permute-start | bytes 786440 | tf_op jit(solution)/shard_map/ppermute | solution.py:623
  32.5 6.0 %shard_map.82 = (bf16[2,2,128,256]{3,2,1,0:T(8,128)(2,1)S(1)}, bf16[2,2,128,256]{3,2,1,0:T(8,128)(2,1)S(1)}, f32[1024,256]{1,0:T(8,128)S(1)}, bf16[512,256]{1,0:T(8,128)(2,1)S(1)}, bf16[512,256]{1,0:T(8,128)(2,1)S(1)}) custom-call(s32[4]{0:T(128)S(1)} %pad_add_fusion.where, bf16[512,256]{1,0:T(8,128)(2,1)S(1)} %get-tuple-element.54.own.kv_own, ...), custom_call_target="tpu_custom_call" | custom-call | flops 1000 | bytes 1000 | tf_op jit(solution)/shard_map/pallas_call | solution.py:444
  38.5 1.2 %collective-permute-start.9 = (bf16[2,2,128,256]{3,2,1,0:T(8,128)(2,1)S(1)}, bf16[2,2,128,256]{3,2,1,0:T(8,128)(2,1)S(1)}, u32[]{:S(2)}, u32[]{:S(2)}) collective-permute-start(bf16[2,2,128,256]{3,2,1,0:T(8,128)(2,1)S(1)} %get-tuple-element.69), channel_id=1, source_target_pairs={{0,1},{1,0},{2,3},{3,2},{4,5},{5,4},{6,7},{7,6},{8,9},{9,8},{10,11... | collective-permute-start | bytes 786440 | tf_op jit(solution)/shard_map/ppermute | solution.py:619
  40.5 2.7 %collective-permute-start.11 = (bf16[512,256]{1,0:T(8,128)(2,1)S(1)}, bf16[512,256]{1,0:T(8,128)(2,1)S(1)}, u32[]{:S(2)}, u32[]{:S(2)}) collective-permute-start(bf16[512,256]{1,0:T(8,128)(2,1)S(1)} %get-tuple-element.72), channel_id=1, source_target_pairs={{2,4},{3,5},{4,2},{5,3},{6,8},{7,9},{8,6},{9,7},{10,12},{11,13},{1... | collective-permute-start | bytes 786440 | tf_op jit(solution)/shard_map/ppermute | solution.py:623
  43.9 1.2 %collective-permute-start.15 = (bf16[512,256]{1,0:T(8,128)(2,1)S(1)}, bf16[512,256]{1,0:T(8,128)(2,1)S(1)}, u32[]{:S(2)}, u32[]{:S(2)}) collective-permute-start(bf16[512,256]{1,0:T(8,128)(2,1)S(1)} %get-tuple-element.85), channel_id=1, source_target_pairs={{0,1},{1,0},{2,3},{3,2},{4,5},{5,4},{6,7},{7,6},{8,9},{9,8},{10,11... | collective-permute-start | bytes 786440 | tf_op jit(solution)/shard_map/ppermute | solution.py:619
  45.1 2.2 %collective-permute-done.9.refs_3_ = bf16[2,2,128,256]{3,2,1,0:T(8,128)(2,1)S(1)} collective-permute-done((bf16[2,2,128,256]{3,2,1,0:T(8,128)(2,1)S(1)}, bf16[2,2,128,256]{3,2,1,0:T(8,128)(2,1)S(1)}, u32[]{:S(2)}, u32[]{:S(2)}) %collective-permute-start.9) | collective-permute-done | bytes 262176 | tf_op jit(solution)/shard_map/ppermute | solution.py:619
  47.2 3.7 %collective-permute-done.11.wide_got = bf16[512,256]{1,0:T(8,128)(2,1)S(1)} collective-permute-done((bf16[512,256]{1,0:T(8,128)(2,1)S(1)}, bf16[512,256]{1,0:T(8,128)(2,1)S(1)}, u32[]{:S(2)}, u32[]{:S(2)}) %collective-permute-start.11) | collective-permute-done | bytes 262176 | tf_op jit(solution)/shard_map/ppermute | solution.py:623
  51.6 1.4 %collective-permute-start.12 = (bf16[512,256]{1,0:T(8,128)(2,1)S(1)}, bf16[512,256]{1,0:T(8,128)(2,1)S(1)}, u32[]{:S(2)}, u32[]{:S(2)}) collective-permute-start(bf16[512,256]{1,0:T(8,128)(2,1)S(1)} %get-tuple-element.79), channel_id=1, source_target_pairs={{0,1},{1,0},{2,3},{3,2},{4,5},{5,4},{6,7},{7,6},{8,9},{9,8},{10,11... | collective-permute-start | bytes 786440 | tf_op jit(solution)/shard_map/ppermute | solution.py:619
  53.1 2.2 %shard_map.83 = (bf16[512,512]{1,0:T(8,128)(2,1)}, bf16[512,512]{1,0:T(8,128)(2,1)}) custom-call(s32[4]{0:T(128)S(1)} %pad_add_fusion.where, bf16[2,2,128,256]{3,2,1,0:T(8,128)(2,1)S(1)} %get-tuple-element.53.refs_0_, bf16[2,2,128,256]{3,2,1,0:T(8,128)(2,1)S(1)} %get-tuple-element.64.refs_1_, bf16[2,2,128,256]{3,2,1,0:T(8,128)(2,1)S(1)} %collective-permute-done.8.refs_2_, ...), custom_call_target="tpu_custom_call" | custom-call | flops 1000 | bytes 1000 | tf_op jit(solution)/shard_map/pallas_call | solution.py:597
  55.3 2.1 %shard_map.86 = (bf16[512,512]{1,0:T(8,128)(2,1)}, bf16[512,512]{1,0:T(8,128)(2,1)}) custom-call(s32[4]{0:T(128)S(1)} %pad_add_fusion.where, bf16[512,256]{1,0:T(8,128)(2,1)S(1)} %get-tuple-element.83.refs_0_, bf16[512,256]{1,0:T(8,128)(2,1)S(1)} %get-tuple-element.84.refs_1_, bf16[512,256]{1,0:T(8,128)(2,1)S(1)} %collective-permute-done.15.refs_2_), custom_call_target="tpu_custom_call" | custom-call | flops 1000 | bytes 1000 | tf_op jit(solution)/shard_map/pallas_call | solution.py:537
  57.4 1.6 %collective-permute-done.12.got = bf16[512,256]{1,0:T(8,128)(2,1)S(1)} collective-permute-done((bf16[512,256]{1,0:T(8,128)(2,1)S(1)}, bf16[512,256]{1,0:T(8,128)(2,1)S(1)}, u32[]{:S(2)}, u32[]{:S(2)}) %collective-permute-start.12) | collective-permute-done | bytes 262176 | tf_op jit(solution)/shard_map/ppermute | solution.py:619
  59.0 1.5 %shard_map.87 = (bf16[512,512]{1,0:T(8,128)(2,1)}, bf16[512,512]{1,0:T(8,128)(2,1)}) custom-call(s32[4]{0:T(128)S(1)} %pad_add_fusion.where, bf16[512,256]{1,0:T(8,128)(2,1)S(1)} %collective-permute-done.12.got, bf16[512,512]{1,0:T(8,128)(2,1)} %get-tuple-element.86.first_in, ...), custom_call_target="tpu_custom_call", output_to_operand_aliasing={{0}: (2, {}), {1}: (3, {})} | custom-call | flops 1000 | bytes 1000 | tf_op jit(solution)/shard_map/pallas_call | solution.py:567
  (33 shorter events, 6.1 us)
Async XLA Ops:
  0.7 2.9 %copy-start.2 = (bf16[512,512]{1,0:T(8,128)(2,1)S(1)}, bf16[512,512]{1,0:T(8,128)(2,1)}, u32[]{:S(2)}) copy-start(bf16[512,512]{1,0:T(8,128)(2,1)} %refs_0_.2) | copy-start | bytes 1572868
  1.7 1.9 %copy-start.3 = (bf16[512,512]{1,0:T(8,128)(2,1)S(1)}, bf16[512,512]{1,0:T(8,128)(2,1)}, u32[]{:S(2)}) copy-start(bf16[512,512]{1,0:T(8,128)(2,1)} %refs_1_.2) | copy-start | bytes 1572868
  2.0 9.3 %collective-permute-start = (bf16[512,256]{1,0:T(8,128)(2,1)S(1)}, bf16[512,256]{1,0:T(8,128)(2,1)S(1)}, u32[]{:S(2)}, u32[]{:S(2)}) collective-permute-start(bf16[512,256]{1,0:T(8,128)(2,1)S(1)} %shard_map.76), channel_id=1, source_target_pairs={{0,1},{1,0},{2,3},{3,2},{4,5},{5,4},{6,7},{7,6},{8,9},{9,8},{10,11... | collective-permute-start | bytes 786440 | tf_op jit(solution)/shard_map/ppermute | solution.py:619
  3.6 1.2 %copy-start = (bf16[512,512]{1,0:T(8,128)(2,1)S(1)}, bf16[512,512]{1,0:T(8,128)(2,1)}, u32[]{:S(2)}) copy-start(bf16[512,512]{1,0:T(8,128)(2,1)} %refs_0_.3) | copy-start | bytes 1572868
  3.6 1.2 %copy-start.1 = (bf16[512,512]{1,0:T(8,128)(2,1)S(1)}, bf16[512,512]{1,0:T(8,128)(2,1)}, u32[]{:S(2)}) copy-start(bf16[512,512]{1,0:T(8,128)(2,1)} %refs_1_.3) | copy-start | bytes 1572868
  3.9 13.0 %collective-permute-start.4 = (bf16[512,256]{1,0:T(8,128)(2,1)S(1)}, bf16[512,256]{1,0:T(8,128)(2,1)S(1)}, u32[]{:S(2)}, u32[]{:S(2)}) collective-permute-start(bf16[512,256]{1,0:T(8,128)(2,1)S(1)} %shard_map.80), channel_id=1, source_target_pairs={{0,1},{1,0},{2,3},{3,2},{4,5},{5,4},{6,7},{7,6},{8,9},{9,8},{10,11... | collective-permute-start | bytes 786440 | tf_op jit(solution)/shard_map/ppermute | solution.py:619
  5.9 15.4 %collective-permute-start.1 = (bf16[512,256]{1,0:T(8,128)(2,1)S(1)}, bf16[512,256]{1,0:T(8,128)(2,1)S(1)}, u32[]{:S(2)}, u32[]{:S(2)}) collective-permute-start(bf16[512,256]{1,0:T(8,128)(2,1)S(1)} %get-tuple-element.50), channel_id=1, source_target_pairs={{0,1},{1,0},{2,3},{3,2},{4,5},{5,4},{6,7},{7,6},{8,9},{9,8},{10,11... | collective-permute-start | bytes 786440 | tf_op jit(solution)/shard_map/ppermute | solution.py:619
  12.0 10.9 %collective-permute-start.2 = (bf16[512,256]{1,0:T(8,128)(2,1)S(1)}, bf16[512,256]{1,0:T(8,128)(2,1)S(1)}, u32[]{:S(2)}, u32[]{:S(2)}) collective-permute-start(bf16[512,256]{1,0:T(8,128)(2,1)S(1)} %get-tuple-element.51), channel_id=1, source_target_pairs={{0,2},{1,3},{2,0},{3,1},{4,6},{5,7},{6,4},{7,5},{8,10},{9,11},{10,... | collective-permute-start | bytes 786440 | tf_op jit(solution)/shard_map/ppermute | solution.py:622
  12.0 10.8 %collective-permute-start.3 = (bf16[512,256]{1,0:T(8,128)(2,1)S(1)}, bf16[512,256]{1,0:T(8,128)(2,1)S(1)}, u32[]{:S(2)}, u32[]{:S(2)}) collective-permute-start(bf16[512,256]{1,0:T(8,128)(2,1)S(1)} %get-tuple-element.52), channel_id=1, source_target_pairs={{2,4},{3,5},{4,2},{5,3},{6,8},{7,9},{8,6},{9,7},{10,12},{11,13},{1... | collective-permute-start | bytes 786440 | tf_op jit(solution)/shard_map/ppermute | solution.py:623
  17.6 12.5 %collective-permute-start.5 = (bf16[512,256]{1,0:T(8,128)(2,1)S(1)}, bf16[512,256]{1,0:T(8,128)(2,1)S(1)}, u32[]{:S(2)}, u32[]{:S(2)}) collective-permute-start(bf16[512,256]{1,0:T(8,128)(2,1)S(1)} %get-tuple-element.60), channel_id=1, source_target_pairs={{0,2},{1,3},{2,0},{3,1},{4,6},{5,7},{6,4},{7,5},{8,10},{9,11},{10,... | collective-permute-start | bytes 786440 | tf_op jit(solution)/shard_map/ppermute | solution.py:622
  17.7 14.8 %collective-permute-start.6 = (bf16[512,256]{1,0:T(8,128)(2,1)S(1)}, bf16[512,256]{1,0:T(8,128)(2,1)S(1)}, u32[]{:S(2)}, u32[]{:S(2)}) collective-permute-start(bf16[512,256]{1,0:T(8,128)(2,1)S(1)} %get-tuple-element.61), channel_id=1, source_target_pairs={{2,4},{3,5},{4,2},{5,3},{6,8},{7,9},{8,6},{9,7},{10,12},{11,13},{1... | collective-permute-start | bytes 786440 | tf_op jit(solution)/shard_map/ppermute | solution.py:623
  21.4 11.1 %collective-permute-start.7 = (bf16[512,256]{1,0:T(8,128)(2,1)S(1)}, bf16[512,256]{1,0:T(8,128)(2,1)S(1)}, u32[]{:S(2)}, u32[]{:S(2)}) collective-permute-start(bf16[512,256]{1,0:T(8,128)(2,1)S(1)} %get-tuple-element.63), channel_id=1, source_target_pairs={{0,1},{1,0},{2,3},{3,2},{4,5},{5,4},{6,7},{7,6},{8,9},{9,8},{10,11... | collective-permute-start | bytes 786440 | tf_op jit(solution)/shard_map/ppermute | solution.py:619
  28.8 10.9 %collective-permute-start.8 = (bf16[2,2,128,256]{3,2,1,0:T(8,128)(2,1)S(1)}, bf16[2,2,128,256]{3,2,1,0:T(8,128)(2,1)S(1)}, u32[]{:S(2)}, u32[]{:S(2)}) collective-permute-start(bf16[2,2,128,256]{3,2,1,0:T(8,128)(2,1)S(1)} %get-tuple-element.65), channel_id=1, source_target_pairs={{0,1},{1,0},{2,3},{3,2},{4,5},{5,4},{6,7},{7,6},{8,9},{9,8},{10,11... | collective-permute-start | bytes 786440 | tf_op jit(solution)/shard_map/ppermute | solution.py:619
  30.1 13.1 %collective-permute-start.13 = (bf16[512,256]{1,0:T(8,128)(2,1)S(1)}, bf16[512,256]{1,0:T(8,128)(2,1)S(1)}, u32[]{:S(2)}, u32[]{:S(2)}) collective-permute-start(bf16[512,256]{1,0:T(8,128)(2,1)S(1)} %get-tuple-element.81), channel_id=1, source_target_pairs={{0,2},{1,3},{2,0},{3,1},{4,6},{5,7},{6,4},{7,5},{8,10},{9,11},{10,... | collective-permute-start | bytes 786440 | tf_op jit(solution)/shard_map/ppermute | solution.py:622
  30.1 13.1 %collective-permute-start.14 = (bf16[512,256]{1,0:T(8,128)(2,1)S(1)}, bf16[512,256]{1,0:T(8,128)(2,1)S(1)}, u32[]{:S(2)}, u32[]{:S(2)}) collective-permute-start(bf16[512,256]{1,0:T(8,128)(2,1)S(1)} %get-tuple-element.82), channel_id=1, source_target_pairs={{2,4},{3,5},{4,2},{5,3},{6,8},{7,9},{8,6},{9,7},{10,12},{11,13},{1... | collective-permute-start | bytes 786440 | tf_op jit(solution)/shard_map/ppermute | solution.py:623
  38.5 8.8 %collective-permute-start.9 = (bf16[2,2,128,256]{3,2,1,0:T(8,128)(2,1)S(1)}, bf16[2,2,128,256]{3,2,1,0:T(8,128)(2,1)S(1)}, u32[]{:S(2)}, u32[]{:S(2)}) collective-permute-start(bf16[2,2,128,256]{3,2,1,0:T(8,128)(2,1)S(1)} %get-tuple-element.69), channel_id=1, source_target_pairs={{0,1},{1,0},{2,3},{3,2},{4,5},{5,4},{6,7},{7,6},{8,9},{9,8},{10,11... | collective-permute-start | bytes 786440 | tf_op jit(solution)/shard_map/ppermute | solution.py:619
  39.7 7.5 %collective-permute-start.10 = (bf16[512,256]{1,0:T(8,128)(2,1)S(1)}, bf16[512,256]{1,0:T(8,128)(2,1)S(1)}, u32[]{:S(2)}, u32[]{:S(2)}) collective-permute-start(bf16[512,256]{1,0:T(8,128)(2,1)S(1)} %get-tuple-element.71), channel_id=1, source_target_pairs={{0,2},{1,3},{2,0},{3,1},{4,6},{5,7},{6,4},{7,5},{8,10},{9,11},{10,... | collective-permute-start | bytes 786440 | tf_op jit(solution)/shard_map/ppermute | solution.py:622
  40.5 10.5 %collective-permute-start.11 = (bf16[512,256]{1,0:T(8,128)(2,1)S(1)}, bf16[512,256]{1,0:T(8,128)(2,1)S(1)}, u32[]{:S(2)}, u32[]{:S(2)}) collective-permute-start(bf16[512,256]{1,0:T(8,128)(2,1)S(1)} %get-tuple-element.72), channel_id=1, source_target_pairs={{2,4},{3,5},{4,2},{5,3},{6,8},{7,9},{8,6},{9,7},{10,12},{11,13},{1... | collective-permute-start | bytes 786440 | tf_op jit(solution)/shard_map/ppermute | solution.py:623
  43.9 11.4 %collective-permute-start.15 = (bf16[512,256]{1,0:T(8,128)(2,1)S(1)}, bf16[512,256]{1,0:T(8,128)(2,1)S(1)}, u32[]{:S(2)}, u32[]{:S(2)}) collective-permute-start(bf16[512,256]{1,0:T(8,128)(2,1)S(1)} %get-tuple-element.85), channel_id=1, source_target_pairs={{0,1},{1,0},{2,3},{3,2},{4,5},{5,4},{6,7},{7,6},{8,9},{9,8},{10,11... | collective-permute-start | bytes 786440 | tf_op jit(solution)/shard_map/ppermute | solution.py:619
  51.6 7.3 %collective-permute-start.12 = (bf16[512,256]{1,0:T(8,128)(2,1)S(1)}, bf16[512,256]{1,0:T(8,128)(2,1)S(1)}, u32[]{:S(2)}, u32[]{:S(2)}) collective-permute-start(bf16[512,256]{1,0:T(8,128)(2,1)S(1)} %get-tuple-element.79), channel_id=1, source_target_pairs={{0,1},{1,0},{2,3},{3,2},{4,5},{5,4},{6,7},{7,6},{8,9},{9,8},{10,11... | collective-permute-start | bytes 786440 | tf_op jit(solution)/shard_map/ppermute | solution.py:619

commit v14 on v13

--- a/solution.py
+++ b/solution.py
@@ -240,7 +240,7 @@
 def one_chunk(
     where, kv_own, kv_got, near_got, wide_got, qg_own, qg_got,
     oq_own, oq_far, grad, near_out, wide_out,
-    raw, raw_t, one, one_t, two, two_t, qs, gs, p0, p1, p2, acc0, acc1, acc2, oq, halos,
+    raw, raw_t, one, one_t, two, two_t, qs, gs, p0, p1, p2, acc0_t, acc0, acc1, acc2, oq, halos,
 ):
     side = where[0]
     odd = where[3]
@@ -311,7 +311,7 @@
         far2 = far_forward(
             blocks(two, 0, which2), blocks_t(two_t, 1, which2), q2, (left_bias, right_bias), p2
         )
-        acc0[...] = jnp.zeros_like(acc0)
+        acc0_t[...] = jnp.zeros_like(acc0_t)
         g1_t, ec1, f1 = [], [], []
         g2_t, ec2, low2 = [], [], []
         dq0 = []
@@ -370,9 +370,11 @@
             weights = p0[...] * f0
             eb = weights.astype(BF)
             r = (weights * (products - dr)).astype(BF)
-            acc0[1, rows, :] += dot_nn(eb, g)
-            acc0[0, rows, :] += dot_nn(r, q)
+            acc0_t[1, :, rows] += dot_nt(g_t.astype(BF), eb)
+            acc0_t[0, :, rows] += dot_nt(q.T, r)
             dq0.append(dot_nn(raw_t[0, :, rows], r))
+        for n in range(2):
+            acc0[n] = acc0_t[n].T
         acc1[...] = jnp.zeros_like(acc1)
         dq1 = []
         for j in range(2):
@@ -464,6 +466,7 @@
             pltpu.VMEM((768, PARENT), F32),
             pltpu.VMEM((2, 384, PARENT), F32),
             pltpu.VMEM((384, PARENT), F32),
+            pltpu.VMEM((2, HEAD, 1536), F32),
             pltpu.VMEM((2, 1536, HEAD), F32),
             pltpu.VMEM((2, 1024, HEAD), F32),
             pltpu.VMEM((2, 512, HEAD), F32),

time: 61.2 us -> 62.6 us (1.023)
  Pallas kernels: 23.8 us -> 25.2 us
    pallas_call x2, Pallas kernels: 11.9 us -> 13.3 us  [main(): pl.pallas_call(functools.partial(main_kernel, qg_first), in_specs=[smem()...]
  transfers between devices with their start and end apart: 16 -> 16, of which waited for: 6 -> 6; matrix products, arithmetic and copies ran while one was open for 0% -> 0% of each run, Pallas kernels for 36% -> 38%
where the time goes in v14:
time: 62.6 us; the launch traced here: 62 us
  Pallas kernels  25.2 us (40%)
  starting transfers between devices  21.3 us (34%)
  waiting for transfers between devices  13.3 us (21%)
  local copies, waits for them, and re-layouts  1.16 us (2%)
  between operations  1.02 us (2%)
    pallas_call x2, Pallas kernels, main(): pl.pallas_call(functools.partial(main_kernel, qg_first), in_specs=[smem()...  13.3 us
    ppermute x8, starting transfers between devices, swap(): return lax.ppermute(x, axes, across)  10.3 us
    ppermute x4, starting transfers between devices, beside(): return (near, lax.ppermute(wide, axes, wide_edges))  10.1 us
    ppermute x8, waiting for transfers between devices, swap(): return lax.ppermute(x, axes, across)  9.65 us
    ppermute x4, waiting for transfers between devices, beside(): return (near, lax.ppermute(wide, axes, wide_edges))  3.68 us
    pallas_call x2, Pallas kernels, pack(): pl.pallas_call(functools.partial(pack_kernel, own), in_specs=[smem()] + [...  2.76 us
    pallas_call x1, Pallas kernels, unpack_columns(): pl.pallas_call(unpack_columns_kernel, in_specs=[smem()] + [vmem()] * (2 *...  2.21 us
    pallas_call x1, Pallas kernels, unpack_rows(): pl.pallas_call(unpack_rows_kernel, in_specs=[smem()] + [vmem()] * (CHUNKS...  2.07 us
  transfers between devices with their start and end apart: 16, of which 6 were waited for; matrix products, arithmetic and copies ran while one was open for 0% of the time, Pallas kernels for 38%

profile of v14, /device:TPU:12, one launch (start us, length us, event | category | flops | bytes accessed | tf_op | source)
XLA Modules:
  0.0 62.0 jit_solution(11107573160866674816)
XLA Ops:
  2.0 1.6 %collective-permute-start = (bf16[512,256]{1,0:T(8,128)(2,1)S(1)}, bf16[512,256]{1,0:T(8,128)(2,1)S(1)}, u32[]{:S(2)}, u32[]{:S(2)}) collective-permute-start(bf16[512,256]{1,0:T(8,128)(2,1)S(1)} %shard_map.76), channel_id=1, source_target_pairs={{0,1},{1,0},{2,3},{3,2},{4,5},{5,4},{6,7},{7,6},{8,9},{9,8},{10,11... | collective-permute-start | bytes 786440 | tf_op jit(solution)/shard_map/ppermute | solution.py:622
  4.8 1.1 %shard_map.77 = (bf16[512,256]{1,0:T(8,128)(2,1)S(1)}, bf16[512,256]{1,0:T(8,128)(2,1)S(1)}) custom-call(s32[4]{0:T(128)S(1)} %pad_add_fusion.where, bf16[512,512]{1,0:T(8,128)(2,1)S(1)} %copy-done, bf16[512,512]{1,0:T(8,128)(2,1)S(1)} %copy-done.1), custom_call_target="tpu_custom_call" | custom-call | flops 1000 | bytes 1000 | tf_op jit(solution)/shard_map/pallas_call | solution.py:86
  5.9 1.4 %collective-permute-start.1 = (bf16[512,256]{1,0:T(8,128)(2,1)S(1)}, bf16[512,256]{1,0:T(8,128)(2,1)S(1)}, u32[]{:S(2)}, u32[]{:S(2)}) collective-permute-start(bf16[512,256]{1,0:T(8,128)(2,1)S(1)} %get-tuple-element.50), channel_id=1, source_target_pairs={{0,1},{1,0},{2,3},{3,2},{4,5},{5,4},{6,7},{7,6},{8,9},{9,8},{10,11... | collective-permute-start | bytes 786440 | tf_op jit(solution)/shard_map/ppermute | solution.py:622
  7.3 1.6 %shard_map.75 = (bf16[512,256]{1,0:T(8,128)(2,1)S(1)}, bf16[512,256]{1,0:T(8,128)(2,1)S(1)}, bf16[512,256]{1,0:T(8,128)(2,1)S(1)}, bf16[512,256]{1,0:T(8,128)(2,1)S(1)}) custom-call(s32[4]{0:T(128)S(1)} %pad_add_fusion.where, bf16[512,512]{1,0:T(8,128)(2,1)S(1)} %copy-done.2, bf16[512,512]{1,0:T(8,128)(2,1)S(1)} %copy-done.3, bf16[512,512]{1,0:T(8,128)(2,1)S(1)} %copy-done, ...), custom_call_target="tpu_custom_call" | custom-call | flops 1000 | bytes 1000 | tf_op jit(solution)/shard_map/pallas_call | solution.py:86
  9.0 2.3 %collective-permute-done.got.kv_got = bf16[512,256]{1,0:T(8,128)(2,1)S(1)} collective-permute-done((bf16[512,256]{1,0:T(8,128)(2,1)S(1)}, bf16[512,256]{1,0:T(8,128)(2,1)S(1)}, u32[]{:S(2)}, u32[]{:S(2)}) %collective-permute-start) | collective-permute-done | bytes 262176 | tf_op jit(solution)/shard_map/ppermute | solution.py:622
  12.0 2.5 %collective-permute-start.3 = (bf16[512,256]{1,0:T(8,128)(2,1)S(1)}, bf16[512,256]{1,0:T(8,128)(2,1)S(1)}, u32[]{:S(2)}, u32[]{:S(2)}) collective-permute-start(bf16[512,256]{1,0:T(8,128)(2,1)S(1)} %get-tuple-element.52), channel_id=1, source_target_pairs={{2,4},{3,5},{4,2},{5,3},{6,8},{7,9},{8,6},{9,7},{10,12},{11,13},{1... | collective-permute-start | bytes 786440 | tf_op jit(solution)/shard_map/ppermute | solution.py:626
  14.6 2.3 %collective-permute-done.4.got.kv_got = bf16[512,256]{1,0:T(8,128)(2,1)S(1)} collective-permute-done((bf16[512,256]{1,0:T(8,128)(2,1)S(1)}, bf16[512,256]{1,0:T(8,128)(2,1)S(1)}, u32[]{:S(2)}, u32[]{:S(2)}) %collective-permute-start.4) | collective-permute-done | bytes 262176 | tf_op jit(solution)/shard_map/ppermute | solution.py:622
  17.7 2.5 %collective-permute-start.6 = (bf16[512,256]{1,0:T(8,128)(2,1)S(1)}, bf16[512,256]{1,0:T(8,128)(2,1)S(1)}, u32[]{:S(2)}, u32[]{:S(2)}) collective-permute-start(bf16[512,256]{1,0:T(8,128)(2,1)S(1)} %get-tuple-element.61), channel_id=1, source_target_pairs={{2,4},{3,5},{4,2},{5,3},{6,8},{7,9},{8,6},{9,7},{10,12},{11,13},{1... | collective-permute-start | bytes 786440 | tf_op jit(solution)/shard_map/ppermute | solution.py:626
  20.2 1.2 %collective-permute-done.1.refs_1_ = bf16[512,256]{1,0:T(8,128)(2,1)S(1)} collective-permute-done((bf16[512,256]{1,0:T(8,128)(2,1)S(1)}, bf16[512,256]{1,0:T(8,128)(2,1)S(1)}, u32[]{:S(2)}, u32[]{:S(2)}) %collective-permute-start.1) | collective-permute-done | bytes 262176 | tf_op jit(solution)/shard_map/ppermute | solution.py:622
  21.4 1.5 %collective-permute-start.7 = (bf16[512,256]{1,0:T(8,128)(2,1)S(1)}, bf16[512,256]{1,0:T(8,128)(2,1)S(1)}, u32[]{:S(2)}, u32[]{:S(2)}) collective-permute-start(bf16[512,256]{1,0:T(8,128)(2,1)S(1)} %get-tuple-element.63), channel_id=1, source_target_pairs={{0,1},{1,0},{2,3},{3,2},{4,5},{5,4},{6,7},{7,6},{8,9},{9,8},{10,11... | collective-permute-start | bytes 786440 | tf_op jit(solution)/shard_map/ppermute | solution.py:622
  22.9 6.7 %shard_map.79 = (bf16[2,2,128,256]{3,2,1,0:T(8,128)(2,1)S(1)}, bf16[2,2,128,256]{3,2,1,0:T(8,128)(2,1)S(1)}, f32[1024,256]{1,0:T(8,128)S(1)}, bf16[512,256]{1,0:T(8,128)(2,1)S(1)}, bf16[512,256]{1,0:T(8,128)(2,1)S(1)}) custom-call(s32[4]{0:T(128)S(1)} %pad_add_fusion.where, bf16[512,256]{1,0:T(8,128)(2,1)S(1)} %get-tuple-element.47.own.kv_own, ...), custom_call_target="tpu_custom_call" | custom-call | flops 1000 | bytes 1000 | tf_op jit(solution)/shard_map/pallas_call | solution.py:446
  29.5 1.2 %collective-permute-start.8 = (bf16[2,2,128,256]{3,2,1,0:T(8,128)(2,1)S(1)}, bf16[2,2,128,256]{3,2,1,0:T(8,128)(2,1)S(1)}, u32[]{:S(2)}, u32[]{:S(2)}) collective-permute-start(bf16[2,2,128,256]{3,2,1,0:T(8,128)(2,1)S(1)} %get-tuple-element.65), channel_id=1, source_target_pairs={{0,1},{1,0},{2,3},{3,2},{4,5},{5,4},{6,7},{7,6},{8,9},{9,8},{10,11... | collective-permute-start | bytes 786440 | tf_op jit(solution)/shard_map/ppermute | solution.py:622
  30.8 2.4 %collective-permute-start.14 = (bf16[512,256]{1,0:T(8,128)(2,1)S(1)}, bf16[512,256]{1,0:T(8,128)(2,1)S(1)}, u32[]{:S(2)}, u32[]{:S(2)}) collective-permute-start(bf16[512,256]{1,0:T(8,128)(2,1)S(1)} %get-tuple-element.82), channel_id=1, source_target_pairs={{2,4},{3,5},{4,2},{5,3},{6,8},{7,9},{8,6},{9,7},{10,12},{11,13},{1... | collective-permute-start | bytes 786440 | tf_op jit(solution)/shard_map/ppermute | solution.py:626
  33.2 6.7 %shard_map.82 = (bf16[2,2,128,256]{3,2,1,0:T(8,128)(2,1)S(1)}, bf16[2,2,128,256]{3,2,1,0:T(8,128)(2,1)S(1)}, f32[1024,256]{1,0:T(8,128)S(1)}, bf16[512,256]{1,0:T(8,128)(2,1)S(1)}, bf16[512,256]{1,0:T(8,128)(2,1)S(1)}) custom-call(s32[4]{0:T(128)S(1)} %pad_add_fusion.where, bf16[512,256]{1,0:T(8,128)(2,1)S(1)} %get-tuple-element.54.own.kv_own, ...), custom_call_target="tpu_custom_call" | custom-call | flops 1000 | bytes 1000 | tf_op jit(solution)/shard_map/pallas_call | solution.py:446
  39.9 1.2 %collective-permute-start.9 = (bf16[2,2,128,256]{3,2,1,0:T(8,128)(2,1)S(1)}, bf16[2,2,128,256]{3,2,1,0:T(8,128)(2,1)S(1)}, u32[]{:S(2)}, u32[]{:S(2)}) collective-permute-start(bf16[2,2,128,256]{3,2,1,0:T(8,128)(2,1)S(1)} %get-tuple-element.69), channel_id=1, source_target_pairs={{0,1},{1,0},{2,3},{3,2},{4,5},{5,4},{6,7},{7,6},{8,9},{9,8},{10,11... | collective-permute-start | bytes 786440 | tf_op jit(solution)/shard_map/ppermute | solution.py:622
  41.8 2.7 %collective-permute-start.11 = (bf16[512,256]{1,0:T(8,128)(2,1)S(1)}, bf16[512,256]{1,0:T(8,128)(2,1)S(1)}, u32[]{:S(2)}, u32[]{:S(2)}) collective-permute-start(bf16[512,256]{1,0:T(8,128)(2,1)S(1)} %get-tuple-element.72), channel_id=1, source_target_pairs={{2,4},{3,5},{4,2},{5,3},{6,8},{7,9},{8,6},{9,7},{10,12},{11,13},{1... | collective-permute-start | bytes 786440 | tf_op jit(solution)/shard_map/ppermute | solution.py:626
  45.2 1.2 %collective-permute-start.15 = (bf16[512,256]{1,0:T(8,128)(2,1)S(1)}, bf16[512,256]{1,0:T(8,128)(2,1)S(1)}, u32[]{:S(2)}, u32[]{:S(2)}) collective-permute-start(bf16[512,256]{1,0:T(8,128)(2,1)S(1)} %get-tuple-element.85), channel_id=1, source_target_pairs={{0,1},{1,0},{2,3},{3,2},{4,5},{5,4},{6,7},{7,6},{8,9},{9,8},{10,11... | collective-permute-start | bytes 786440 | tf_op jit(solution)/shard_map/ppermute | solution.py:622
  46.5 2.2 %collective-permute-done.9.refs_3_ = bf16[2,2,128,256]{3,2,1,0:T(8,128)(2,1)S(1)} collective-permute-done((bf16[2,2,128,256]{3,2,1,0:T(8,128)(2,1)S(1)}, bf16[2,2,128,256]{3,2,1,0:T(8,128)(2,1)S(1)}, u32[]{:S(2)}, u32[]{:S(2)}) %collective-permute-start.9) | collective-permute-done | bytes 262176 | tf_op jit(solution)/shard_map/ppermute | solution.py:622
  48.6 3.7 %collective-permute-done.11.wide_got = bf16[512,256]{1,0:T(8,128)(2,1)S(1)} collective-permute-done((bf16[512,256]{1,0:T(8,128)(2,1)S(1)}, bf16[512,256]{1,0:T(8,128)(2,1)S(1)}, u32[]{:S(2)}, u32[]{:S(2)}) %collective-permute-start.11) | collective-permute-done | bytes 262176 | tf_op jit(solution)/shard_map/ppermute | solution.py:626
  53.0 1.4 %collective-permute-start.12 = (bf16[512,256]{1,0:T(8,128)(2,1)S(1)}, bf16[512,256]{1,0:T(8,128)(2,1)S(1)}, u32[]{:S(2)}, u32[]{:S(2)}) collective-permute-start(bf16[512,256]{1,0:T(8,128)(2,1)S(1)} %get-tuple-element.79), channel_id=1, source_target_pairs={{0,1},{1,0},{2,3},{3,2},{4,5},{5,4},{6,7},{7,6},{8,9},{9,8},{10,11... | collective-permute-start | bytes 786440 | tf_op jit(solution)/shard_map/ppermute | solution.py:622
  54.4 2.2 %shard_map.83 = (bf16[512,512]{1,0:T(8,128)(2,1)}, bf16[512,512]{1,0:T(8,128)(2,1)}) custom-call(s32[4]{0:T(128)S(1)} %pad_add_fusion.where, bf16[2,2,128,256]{3,2,1,0:T(8,128)(2,1)S(1)} %get-tuple-element.53.refs_0_, bf16[2,2,128,256]{3,2,1,0:T(8,128)(2,1)S(1)} %get-tuple-element.64.refs_1_, bf16[2,2,128,256]{3,2,1,0:T(8,128)(2,1)S(1)} %collective-permute-done.8.refs_2_, ...), custom_call_target="tpu_custom_call" | custom-call | flops 1000 | bytes 1000 | tf_op jit(solution)/shard_map/pallas_call | solution.py:600
  56.7 2.1 %shard_map.86 = (bf16[512,512]{1,0:T(8,128)(2,1)}, bf16[512,512]{1,0:T(8,128)(2,1)}) custom-call(s32[4]{0:T(128)S(1)} %pad_add_fusion.where, bf16[512,256]{1,0:T(8,128)(2,1)S(1)} %get-tuple-element.83.refs_0_, bf16[512,256]{1,0:T(8,128)(2,1)S(1)} %get-tuple-element.84.refs_1_, bf16[512,256]{1,0:T(8,128)(2,1)S(1)} %collective-permute-done.15.refs_2_), custom_call_target="tpu_custom_call" | custom-call | flops 1000 | bytes 1000 | tf_op jit(solution)/shard_map/pallas_call | solution.py:540
  58.7 1.6 %collective-permute-done.12.got = bf16[512,256]{1,0:T(8,128)(2,1)S(1)} collective-permute-done((bf16[512,256]{1,0:T(8,128)(2,1)S(1)}, bf16[512,256]{1,0:T(8,128)(2,1)S(1)}, u32[]{:S(2)}, u32[]{:S(2)}) %collective-permute-start.12) | collective-permute-done | bytes 262176 | tf_op jit(solution)/shard_map/ppermute | solution.py:622
  60.4 1.5 %shard_map.87 = (bf16[512,512]{1,0:T(8,128)(2,1)}, bf16[512,512]{1,0:T(8,128)(2,1)}) custom-call(s32[4]{0:T(128)S(1)} %pad_add_fusion.where, bf16[512,256]{1,0:T(8,128)(2,1)S(1)} %collective-permute-done.12.got, bf16[512,512]{1,0:T(8,128)(2,1)} %get-tuple-element.86.first_in, ...), custom_call_target="tpu_custom_call", output_to_operand_aliasing={{0}: (2, {}), {1}: (3, {})} | custom-call | flops 1000 | bytes 1000 | tf_op jit(solution)/shard_map/pallas_call | solution.py:570
  (33 shorter events, 6.1 us)
Async XLA Ops:
  0.7 2.9 %copy-start.2 = (bf16[512,512]{1,0:T(8,128)(2,1)S(1)}, bf16[512,512]{1,0:T(8,128)(2,1)}, u32[]{:S(2)}) copy-start(bf16[512,512]{1,0:T(8,128)(2,1)} %refs_0_.2) | copy-start | bytes 1572868
  1.7 1.9 %copy-start.3 = (bf16[512,512]{1,0:T(8,128)(2,1)S(1)}, bf16[512,512]{1,0:T(8,128)(2,1)}, u32[]{:S(2)}) copy-start(bf16[512,512]{1,0:T(8,128)(2,1)} %refs_1_.2) | copy-start | bytes 1572868
  2.0 9.3 %collective-permute-start = (bf16[512,256]{1,0:T(8,128)(2,1)S(1)}, bf16[512,256]{1,0:T(8,128)(2,1)S(1)}, u32[]{:S(2)}, u32[]{:S(2)}) collective-permute-start(bf16[512,256]{1,0:T(8,128)(2,1)S(1)} %shard_map.76), channel_id=1, source_target_pairs={{0,1},{1,0},{2,3},{3,2},{4,5},{5,4},{6,7},{7,6},{8,9},{9,8},{10,11... | collective-permute-start | bytes 786440 | tf_op jit(solution)/shard_map/ppermute | solution.py:622
  3.6 1.2 %copy-start = (bf16[512,512]{1,0:T(8,128)(2,1)S(1)}, bf16[512,512]{1,0:T(8,128)(2,1)}, u32[]{:S(2)}) copy-start(bf16[512,512]{1,0:T(8,128)(2,1)} %refs_0_.3) | copy-start | bytes 1572868
  3.6 1.2 %copy-start.1 = (bf16[512,512]{1,0:T(8,128)(2,1)S(1)}, bf16[512,512]{1,0:T(8,128)(2,1)}, u32[]{:S(2)}) copy-start(bf16[512,512]{1,0:T(8,128)(2,1)} %refs_1_.3) | copy-start | bytes 1572868
  3.9 13.0 %collective-permute-start.4 = (bf16[512,256]{1,0:T(8,128)(2,1)S(1)}, bf16[512,256]{1,0:T(8,128)(2,1)S(1)}, u32[]{:S(2)}, u32[]{:S(2)}) collective-permute-start(bf16[512,256]{1,0:T(8,128)(2,1)S(1)} %shard_map.80), channel_id=1, source_target_pairs={{0,1},{1,0},{2,3},{3,2},{4,5},{5,4},{6,7},{7,6},{8,9},{9,8},{10,11... | collective-permute-start | bytes 786440 | tf_op jit(solution)/shard_map/ppermute | solution.py:622
  5.9 15.4 %collective-permute-start.1 = (bf16[512,256]{1,0:T(8,128)(2,1)S(1)}, bf16[512,256]{1,0:T(8,128)(2,1)S(1)}, u32[]{:S(2)}, u32[]{:S(2)}) collective-permute-start(bf16[512,256]{1,0:T(8,128)(2,1)S(1)} %get-tuple-element.50), channel_id=1, source_target_pairs={{0,1},{1,0},{2,3},{3,2},{4,5},{5,4},{6,7},{7,6},{8,9},{9,8},{10,11... | collective-permute-start | bytes 786440 | tf_op jit(solution)/shard_map/ppermute | solution.py:622
  12.0 10.9 %collective-permute-start.2 = (bf16[512,256]{1,0:T(8,128)(2,1)S(1)}, bf16[512,256]{1,0:T(8,128)(2,1)S(1)}, u32[]{:S(2)}, u32[]{:S(2)}) collective-permute-start(bf16[512,256]{1,0:T(8,128)(2,1)S(1)} %get-tuple-element.51), channel_id=1, source_target_pairs={{0,2},{1,3},{2,0},{3,1},{4,6},{5,7},{6,4},{7,5},{8,10},{9,11},{10,... | collective-permute-start | bytes 786440 | tf_op jit(solution)/shard_map/ppermute | solution.py:625
  12.0 10.8 %collective-permute-start.3 = (bf16[512,256]{1,0:T(8,128)(2,1)S(1)}, bf16[512,256]{1,0:T(8,128)(2,1)S(1)}, u32[]{:S(2)}, u32[]{:S(2)}) collective-permute-start(bf16[512,256]{1,0:T(8,128)(2,1)S(1)} %get-tuple-element.52), channel_id=1, source_target_pairs={{2,4},{3,5},{4,2},{5,3},{6,8},{7,9},{8,6},{9,7},{10,12},{11,13},{1... | collective-permute-start | bytes 786440 | tf_op jit(solution)/shard_map/ppermute | solution.py:626
  17.6 13.2 %collective-permute-start.5 = (bf16[512,256]{1,0:T(8,128)(2,1)S(1)}, bf16[512,256]{1,0:T(8,128)(2,1)S(1)}, u32[]{:S(2)}, u32[]{:S(2)}) collective-permute-start(bf16[512,256]{1,0:T(8,128)(2,1)S(1)} %get-tuple-element.60), channel_id=1, source_target_pairs={{0,2},{1,3},{2,0},{3,1},{4,6},{5,7},{6,4},{7,5},{8,10},{9,11},{10,... | collective-permute-start | bytes 786440 | tf_op jit(solution)/shard_map/ppermute | solution.py:625
  17.7 15.5 %collective-permute-start.6 = (bf16[512,256]{1,0:T(8,128)(2,1)S(1)}, bf16[512,256]{1,0:T(8,128)(2,1)S(1)}, u32[]{:S(2)}, u32[]{:S(2)}) collective-permute-start(bf16[512,256]{1,0:T(8,128)(2,1)S(1)} %get-tuple-element.61), channel_id=1, source_target_pairs={{2,4},{3,5},{4,2},{5,3},{6,8},{7,9},{8,6},{9,7},{10,12},{11,13},{1... | collective-permute-start | bytes 786440 | tf_op jit(solution)/shard_map/ppermute | solution.py:626
  21.4 11.8 %collective-permute-start.7 = (bf16[512,256]{1,0:T(8,128)(2,1)S(1)}, bf16[512,256]{1,0:T(8,128)(2,1)S(1)}, u32[]{:S(2)}, u32[]{:S(2)}) collective-permute-start(bf16[512,256]{1,0:T(8,128)(2,1)S(1)} %get-tuple-element.63), channel_id=1, source_target_pairs={{0,1},{1,0},{2,3},{3,2},{4,5},{5,4},{6,7},{7,6},{8,9},{9,8},{10,11... | collective-permute-start | bytes 786440 | tf_op jit(solution)/shard_map/ppermute | solution.py:622
  29.5 11.6 %collective-permute-start.8 = (bf16[2,2,128,256]{3,2,1,0:T(8,128)(2,1)S(1)}, bf16[2,2,128,256]{3,2,1,0:T(8,128)(2,1)S(1)}, u32[]{:S(2)}, u32[]{:S(2)}) collective-permute-start(bf16[2,2,128,256]{3,2,1,0:T(8,128)(2,1)S(1)} %get-tuple-element.65), channel_id=1, source_target_pairs={{0,1},{1,0},{2,3},{3,2},{4,5},{5,4},{6,7},{7,6},{8,9},{9,8},{10,11... | collective-permute-start | bytes 786440 | tf_op jit(solution)/shard_map/ppermute | solution.py:622
  30.8 13.8 %collective-permute-start.13 = (bf16[512,256]{1,0:T(8,128)(2,1)S(1)}, bf16[512,256]{1,0:T(8,128)(2,1)S(1)}, u32[]{:S(2)}, u32[]{:S(2)}) collective-permute-start(bf16[512,256]{1,0:T(8,128)(2,1)S(1)} %get-tuple-element.81), channel_id=1, source_target_pairs={{0,2},{1,3},{2,0},{3,1},{4,6},{5,7},{6,4},{7,5},{8,10},{9,11},{10,... | collective-permute-start | bytes 786440 | tf_op jit(solution)/shard_map/ppermute | solution.py:625
  30.8 13.8 %collective-permute-start.14 = (bf16[512,256]{1,0:T(8,128)(2,1)S(1)}, bf16[512,256]{1,0:T(8,128)(2,1)S(1)}, u32[]{:S(2)}, u32[]{:S(2)}) collective-permute-start(bf16[512,256]{1,0:T(8,128)(2,1)S(1)} %get-tuple-element.82), channel_id=1, source_target_pairs={{2,4},{3,5},{4,2},{5,3},{6,8},{7,9},{8,6},{9,7},{10,12},{11,13},{1... | collective-permute-start | bytes 786440 | tf_op jit(solution)/shard_map/ppermute | solution.py:626
  39.9 8.8 %collective-permute-start.9 = (bf16[2,2,128,256]{3,2,1,0:T(8,128)(2,1)S(1)}, bf16[2,2,128,256]{3,2,1,0:T(8,128)(2,1)S(1)}, u32[]{:S(2)}, u32[]{:S(2)}) collective-permute-start(bf16[2,2,128,256]{3,2,1,0:T(8,128)(2,1)S(1)} %get-tuple-element.69), channel_id=1, source_target_pairs={{0,1},{1,0},{2,3},{3,2},{4,5},{5,4},{6,7},{7,6},{8,9},{9,8},{10,11... | collective-permute-start | bytes 786440 | tf_op jit(solution)/shard_map/ppermute | solution.py:622
  41.1 7.6 %collective-permute-start.10 = (bf16[512,256]{1,0:T(8,128)(2,1)S(1)}, bf16[512,256]{1,0:T(8,128)(2,1)S(1)}, u32[]{:S(2)}, u32[]{:S(2)}) collective-permute-start(bf16[512,256]{1,0:T(8,128)(2,1)S(1)} %get-tuple-element.71), channel_id=1, source_target_pairs={{0,2},{1,3},{2,0},{3,1},{4,6},{5,7},{6,4},{7,5},{8,10},{9,11},{10,... | collective-permute-start | bytes 786440 | tf_op jit(solution)/shard_map/ppermute | solution.py:625
  41.8 10.5 %collective-permute-start.11 = (bf16[512,256]{1,0:T(8,128)(2,1)S(1)}, bf16[512,256]{1,0:T(8,128)(2,1)S(1)}, u32[]{:S(2)}, u32[]{:S(2)}) collective-permute-start(bf16[512,256]{1,0:T(8,128)(2,1)S(1)} %get-tuple-element.72), channel_id=1, source_target_pairs={{2,4},{3,5},{4,2},{5,3},{6,8},{7,9},{8,6},{9,7},{10,12},{11,13},{1... | collective-permute-start | bytes 786440 | tf_op jit(solution)/shard_map/ppermute | solution.py:626
  45.2 11.4 %collective-permute-start.15 = (bf16[512,256]{1,0:T(8,128)(2,1)S(1)}, bf16[512,256]{1,0:T(8,128)(2,1)S(1)}, u32[]{:S(2)}, u32[]{:S(2)}) collective-permute-start(bf16[512,256]{1,0:T(8,128)(2,1)S(1)} %get-tuple-element.85), channel_id=1, source_target_pairs={{0,1},{1,0},{2,3},{3,2},{4,5},{5,4},{6,7},{7,6},{8,9},{9,8},{10,11... | collective-permute-start | bytes 786440 | tf_op jit(solution)/shard_map/ppermute | solution.py:622
  53.0 7.3 %collective-permute-start.12 = (bf16[512,256]{1,0:T(8,128)(2,1)S(1)}, bf16[512,256]{1,0:T(8,128)(2,1)S(1)}, u32[]{:S(2)}, u32[]{:S(2)}) collective-permute-start(bf16[512,256]{1,0:T(8,128)(2,1)S(1)} %get-tuple-element.79), channel_id=1, source_target_pairs={{0,1},{1,0},{2,3},{3,2},{4,5},{5,4},{6,7},{7,6},{8,9},{9,8},{10,11... | collective-permute-start | bytes 786440 | tf_op jit(solution)/shard_map/ppermute | solution.py:622

commit v15 on v13

--- a/solution.py
+++ b/solution.py
@@ -618,9 +618,11 @@
     def swap(x):
         return lax.ppermute(x, axes, across)
 
-    def beside(near, wide):
-        near = lax.ppermute(near, axes, near_edges)
-        return near, lax.ppermute(wide, axes, wide_edges)
+    def to_near(x):
+        return lax.ppermute(x, axes, near_edges)
+
+    def to_wide(x):
+        return lax.ppermute(x, axes, wide_edges)
 
     kv_far = [pack_cut(1 - device % 2, 0, key_matrix, value_matrix)]
     for c in range(1, CHUNKS):
@@ -636,13 +638,17 @@
         far = qg_far[c]
         if c > 0:
             near, wide, far = lax.optimization_barrier((near, wide, far))
-        near, wide = beside(near, wide)
+        near, wide = to_near(near), to_wide(wide)
         own, far, grad, near, wide = main(where, kv[c], got_kv, near, wide, qg[c], swap(far), c == 0)
         oq_own.append(own)
         oq_got.append(swap(far))
         if c > 0:
-            oq_got[c - 1], near, wide = lax.optimization_barrier((oq_got[c - 1], near, wide))
-        back.append([grad, *beside(near, wide)])
+            oq_got[c - 1], back[c - 1][1], near, wide = lax.optimization_barrier(
+                (oq_got[c - 1], back[c - 1][1], near, wide)
+            )
+        back.append([grad, near, to_wide(wide)])
+    for parts in back:
+        parts[1] = to_near(parts[1])
     oq_got[-1], back[-1] = lax.optimization_barrier((oq_got[-1], back[-1]))
     kv_own, kv_got = [], []
     for c in range(CHUNKS):

time: 61.2 us -> 62.7 us (1.025)
  the two profiles are of different devices: /device:TPU:12 before, /device:TPU:0 now
where the time goes in v15:
time: 62.7 us; the launch traced here: 62.5 us
  Pallas kernels  23.8 us (38%)
  waiting for transfers between devices  19.8 us (32%)
  starting transfers between devices  16.7 us (27%)
  local copies, waits for them, and re-layouts  1.16 us (2%)
  between operations  1.03 us (2%)
    ppermute x8, waiting for transfers between devices, swap(): return lax.ppermute(x, axes, across)  19.7 us
    pallas_call x2, Pallas kernels, main(): pl.pallas_call(functools.partial(main_kernel, qg_first), in_specs=[smem()...  11.9 us
    ppermute x8, starting transfers between devices, swap(): return lax.ppermute(x, axes, across)  10.6 us
    ppermute x4, starting transfers between devices, to_near(): return lax.ppermute(x, axes, near_edges)  3.26 us
    ppermute x4, starting transfers between devices, to_wide(): return lax.ppermute(x, axes, wide_edges)  2.87 us
    pallas_call x2, Pallas kernels, pack(): pl.pallas_call(functools.partial(pack_kernel, own), in_specs=[smem()] + [...  2.76 us
    pallas_call x1, Pallas kernels, unpack_columns(): pl.pallas_call(unpack_columns_kernel, in_specs=[smem()] + [vmem()] * (2 *...  2.21 us
    pallas_call x1, Pallas kernels, unpack_rows(): pl.pallas_call(unpack_rows_kernel, in_specs=[smem()] + [vmem()] * (CHUNKS...  2.07 us
  transfers between devices with their start and end apart: 16, of which 7 were waited for; matrix products, arithmetic and copies ran while one was open for 0% of the time, Pallas kernels for 35%

profile of v15, /device:TPU:0, one launch (start us, length us, event | category | flops | bytes accessed | tf_op | source)
XLA Modules:
  0.0 62.5 jit_solution(17072492194086144841)
XLA Ops:
  0.7 1.1 %constant_dynamic-slice_fusion.2 = (bf16[512,128]{1,0:T(8,128)(2,1)S(1)}, bf16[512,128]{1,0:T(8,128)(2,1)S(1)}) fusion(bf16[512,512]{1,0:T(8,128)(2,1)} %refs_1_.2, s32[]{:T(128)S(6)} %select_n.30, bf16[512,512]{1,0:T(8,128)(2,1)} %refs_0_.2), kind=kLoop, calls=%fused_computation.2 | loop fusion | bytes 524292 | tf_op jit(solution)/shard_map/dynamic_slice | solution.py:112
  2.0 3.0 %collective-permute-start = (bf16[512,256]{1,0:T(8,128)(2,1)S(1)}, bf16[512,256]{1,0:T(8,128)(2,1)S(1)}, u32[]{:S(2)}, u32[]{:S(2)}) collective-permute-start(bf16[512,256]{1,0:T(8,128)(2,1)S(1)} %shard_map.76), channel_id=1, source_target_pairs={{0,1},{1,0},{2,3},{3,2},{4,5},{5,4},{6,7},{7,6},{8,9},{9,8},{10,11... | collective-permute-start | bytes 786440 | tf_op jit(solution)/shard_map/ppermute | solution.py:619
  5.4 0.7 %collective-permute-start.4 = (bf16[512,256]{1,0:T(8,128)(2,1)S(1)}, bf16[512,256]{1,0:T(8,128)(2,1)S(1)}, u32[]{:S(2)}, u32[]{:S(2)}) collective-permute-start(bf16[512,256]{1,0:T(8,128)(2,1)S(1)} %shard_map.80), channel_id=1, source_target_pairs={{0,1},{1,0},{2,3},{3,2},{4,5},{5,4},{6,7},{7,6},{8,9},{9,8},{10,11... | collective-permute-start | bytes 786440 | tf_op jit(solution)/shard_map/ppermute | solution.py:619
  6.2 1.1 %shard_map.77 = (bf16[512,256]{1,0:T(8,128)(2,1)S(1)}, bf16[512,256]{1,0:T(8,128)(2,1)S(1)}) custom-call(s32[4]{0:T(128)S(1)} %pad_add_fusion.where, bf16[512,512]{1,0:T(8,128)(2,1)S(1)} %copy-done, bf16[512,512]{1,0:T(8,128)(2,1)S(1)} %copy-done.1), custom_call_target="tpu_custom_call" | custom-call | flops 1000 | bytes 1000 | tf_op jit(solution)/shard_map/pallas_call | solution.py:86
  7.4 1.4 %collective-permute-start.1 = (bf16[512,256]{1,0:T(8,128)(2,1)S(1)}, bf16[512,256]{1,0:T(8,128)(2,1)S(1)}, u32[]{:S(2)}, u32[]{:S(2)}) collective-permute-start(bf16[512,256]{1,0:T(8,128)(2,1)S(1)} %get-tuple-element.51), channel_id=1, source_target_pairs={{0,1},{1,0},{2,3},{3,2},{4,5},{5,4},{6,7},{7,6},{8,9},{9,8},{10,11... | collective-permute-start | bytes 786440 | tf_op jit(solution)/shard_map/ppermute | solution.py:619
  8.8 1.6 %shard_map.75 = (bf16[512,256]{1,0:T(8,128)(2,1)S(1)}, bf16[512,256]{1,0:T(8,128)(2,1)S(1)}, bf16[512,256]{1,0:T(8,128)(2,1)S(1)}, bf16[512,256]{1,0:T(8,128)(2,1)S(1)}) custom-call(s32[4]{0:T(128)S(1)} %pad_add_fusion.where, bf16[512,512]{1,0:T(8,128)(2,1)S(1)} %copy-done.2, bf16[512,512]{1,0:T(8,128)(2,1)S(1)} %copy-done.3, bf16[512,512]{1,0:T(8,128)(2,1)S(1)} %copy-done, ...), custom_call_target="tpu_custom_call" | custom-call | flops 1000 | bytes 1000 | tf_op jit(solution)/shard_map/pallas_call | solution.py:86
  10.4 1.8 %collective-permute-done.got.kv_got = bf16[512,256]{1,0:T(8,128)(2,1)S(1)} collective-permute-done((bf16[512,256]{1,0:T(8,128)(2,1)S(1)}, bf16[512,256]{1,0:T(8,128)(2,1)S(1)}, u32[]{:S(2)}, u32[]{:S(2)}) %collective-permute-start) | collective-permute-done | bytes 262176 | tf_op jit(solution)/shard_map/ppermute | solution.py:619
  13.6 4.2 %collective-permute-done.4.got.kv_got = bf16[512,256]{1,0:T(8,128)(2,1)S(1)} collective-permute-done((bf16[512,256]{1,0:T(8,128)(2,1)S(1)}, bf16[512,256]{1,0:T(8,128)(2,1)S(1)}, u32[]{:S(2)}, u32[]{:S(2)}) %collective-permute-start.4) | collective-permute-done | bytes 262176 | tf_op jit(solution)/shard_map/ppermute | solution.py:619
  19.2 3.3 %collective-permute-done.1.refs_1_ = bf16[512,256]{1,0:T(8,128)(2,1)S(1)} collective-permute-done((bf16[512,256]{1,0:T(8,128)(2,1)S(1)}, bf16[512,256]{1,0:T(8,128)(2,1)S(1)}, u32[]{:S(2)}, u32[]{:S(2)}) %collective-permute-start.1) | collective-permute-done | bytes 262176 | tf_op jit(solution)/shard_map/ppermute | solution.py:619
  22.6 1.7 %collective-permute-start.7 = (bf16[512,256]{1,0:T(8,128)(2,1)S(1)}, bf16[512,256]{1,0:T(8,128)(2,1)S(1)}, u32[]{:S(2)}, u32[]{:S(2)}) collective-permute-start(bf16[512,256]{1,0:T(8,128)(2,1)S(1)} %get-tuple-element.64), channel_id=1, source_target_pairs={{0,1},{1,0},{2,3},{3,2},{4,5},{5,4},{6,7},{7,6},{8,9},{9,8},{10,11... | collective-permute-start | bytes 786440 | tf_op jit(solution)/shard_map/ppermute | solution.py:619
  24.3 6.0 %shard_map.79 = (bf16[2,2,128,256]{3,2,1,0:T(8,128)(2,1)S(1)}, bf16[2,2,128,256]{3,2,1,0:T(8,128)(2,1)S(1)}, f32[1024,256]{1,0:T(8,128)S(1)}, bf16[512,256]{1,0:T(8,128)(2,1)S(1)}, bf16[512,256]{1,0:T(8,128)(2,1)S(1)}) custom-call(s32[4]{0:T(128)S(1)} %pad_add_fusion.where, bf16[512,256]{1,0:T(8,128)(2,1)S(1)} %get-tuple-element.48.own.kv_own, ...), custom_call_target="tpu_custom_call" | custom-call | flops 1000 | bytes 1000 | tf_op jit(solution)/shard_map/pallas_call | solution.py:444
  30.6 0.8 %collective-permute-start.14 = (bf16[512,256]{1,0:T(8,128)(2,1)S(1)}, bf16[512,256]{1,0:T(8,128)(2,1)S(1)}, u32[]{:S(2)}, u32[]{:S(2)}) collective-permute-start(bf16[512,256]{1,0:T(8,128)(2,1)S(1)} %get-tuple-element.84), channel_id=1, source_target_pairs={{2,4},{3,5},{4,2},{5,3},{6,8},{7,9},{8,6},{9,7},{10,12},{11,13},{1... | collective-permute-start | bytes 786440 | tf_op jit(solution)/shard_map/ppermute | solution.py:625
  31.5 6.0 %shard_map.82 = (bf16[2,2,128,256]{3,2,1,0:T(8,128)(2,1)S(1)}, bf16[2,2,128,256]{3,2,1,0:T(8,128)(2,1)S(1)}, f32[1024,256]{1,0:T(8,128)S(1)}, bf16[512,256]{1,0:T(8,128)(2,1)S(1)}, bf16[512,256]{1,0:T(8,128)(2,1)S(1)}) custom-call(s32[4]{0:T(128)S(1)} %pad_add_fusion.where, bf16[512,256]{1,0:T(8,128)(2,1)S(1)} %get-tuple-element.55.own.kv_own, ...), custom_call_target="tpu_custom_call" | custom-call | flops 1000 | bytes 1000 | tf_op jit(solution)/shard_map/pallas_call | solution.py:444
  37.5 0.7 %collective-permute-done.8.refs_2_ = bf16[2,2,128,256]{3,2,1,0:T(8,128)(2,1)S(1)} collective-permute-done((bf16[2,2,128,256]{3,2,1,0:T(8,128)(2,1)S(1)}, bf16[2,2,128,256]{3,2,1,0:T(8,128)(2,1)S(1)}, u32[]{:S(2)}, u32[]{:S(2)}) %collective-permute-start.8) | collective-permute-done | bytes 262176 | tf_op jit(solution)/shard_map/ppermute | solution.py:619
  38.2 3.1 %collective-permute-start.13 = (bf16[512,256]{1,0:T(8,128)(2,1)S(1)}, bf16[512,256]{1,0:T(8,128)(2,1)S(1)}, u32[]{:S(2)}, u32[]{:S(2)}) collective-permute-start(bf16[512,256]{1,0:T(8,128)(2,1)S(1)} %get-tuple-element.83), channel_id=1, source_target_pairs={{0,2},{1,3},{2,0},{3,1},{4,6},{5,7},{6,4},{7,5},{8,10},{9,11},{10,... | collective-permute-start | bytes 786440 | tf_op jit(solution)/shard_map/ppermute | solution.py:622
  41.3 0.9 %collective-permute-start.9 = (bf16[2,2,128,256]{3,2,1,0:T(8,128)(2,1)S(1)}, bf16[2,2,128,256]{3,2,1,0:T(8,128)(2,1)S(1)}, u32[]{:S(2)}, u32[]{:S(2)}) collective-permute-start(bf16[2,2,128,256]{3,2,1,0:T(8,128)(2,1)S(1)} %get-tuple-element.71), channel_id=1, source_target_pairs={{0,1},{1,0},{2,3},{3,2},{4,5},{5,4},{6,7},{7,6},{8,9},{9,8},{10,11... | collective-permute-start | bytes 786440 | tf_op jit(solution)/shard_map/ppermute | solution.py:619
  43.6 1.2 %collective-permute-start.15 = (bf16[512,256]{1,0:T(8,128)(2,1)S(1)}, bf16[512,256]{1,0:T(8,128)(2,1)S(1)}, u32[]{:S(2)}, u32[]{:S(2)}) collective-permute-start(bf16[512,256]{1,0:T(8,128)(2,1)S(1)} %get-tuple-element.87), channel_id=1, source_target_pairs={{0,1},{1,0},{2,3},{3,2},{4,5},{5,4},{6,7},{7,6},{8,9},{9,8},{10,11... | collective-permute-start | bytes 786440 | tf_op jit(solution)/shard_map/ppermute | solution.py:619
  44.8 5.3 %collective-permute-done.9.refs_3_ = bf16[2,2,128,256]{3,2,1,0:T(8,128)(2,1)S(1)} collective-permute-done((bf16[2,2,128,256]{3,2,1,0:T(8,128)(2,1)S(1)}, bf16[2,2,128,256]{3,2,1,0:T(8,128)(2,1)S(1)}, u32[]{:S(2)}, u32[]{:S(2)}) %collective-permute-start.9) | collective-permute-done | bytes 262176 | tf_op jit(solution)/shard_map/ppermute | solution.py:619
  50.8 1.3 %collective-permute-start.12 = (bf16[512,256]{1,0:T(8,128)(2,1)S(1)}, bf16[512,256]{1,0:T(8,128)(2,1)S(1)}, u32[]{:S(2)}, u32[]{:S(2)}) collective-permute-start(bf16[512,256]{1,0:T(8,128)(2,1)S(1)} %get-tuple-element.81), channel_id=1, source_target_pairs={{0,1},{1,0},{2,3},{3,2},{4,5},{5,4},{6,7},{7,6},{8,9},{9,8},{10,11... | collective-permute-start | bytes 786440 | tf_op jit(solution)/shard_map/ppermute | solution.py:619
  52.0 2.2 %shard_map.83 = (bf16[512,512]{1,0:T(8,128)(2,1)}, bf16[512,512]{1,0:T(8,128)(2,1)}) custom-call(s32[4]{0:T(128)S(1)} %pad_add_fusion.where, bf16[2,2,128,256]{3,2,1,0:T(8,128)(2,1)S(1)} %get-tuple-element.54.refs_0_, bf16[2,2,128,256]{3,2,1,0:T(8,128)(2,1)S(1)} %get-tuple-element.65.refs_1_, bf16[2,2,128,256]{3,2,1,0:T(8,128)(2,1)S(1)} %collective-permute-done.8.refs_2_, ...), custom_call_target="tpu_custom_call" | custom-call | flops 1000 | bytes 1000 | tf_op jit(solution)/shard_map/pallas_call | solution.py:597
  54.2 1.0 %collective-permute-done.15.refs_2_ = bf16[512,256]{1,0:T(8,128)(2,1)S(1)} collective-permute-done((bf16[512,256]{1,0:T(8,128)(2,1)S(1)}, bf16[512,256]{1,0:T(8,128)(2,1)S(1)}, u32[]{:S(2)}, u32[]{:S(2)}) %collective-permute-start.15) | collective-permute-done | bytes 262176 | tf_op jit(solution)/shard_map/ppermute | solution.py:619
  55.2 2.1 %shard_map.86 = (bf16[512,512]{1,0:T(8,128)(2,1)}, bf16[512,512]{1,0:T(8,128)(2,1)}) custom-call(s32[4]{0:T(128)S(1)} %pad_add_fusion.where, bf16[512,256]{1,0:T(8,128)(2,1)S(1)} %get-tuple-element.85.refs_0_, bf16[512,256]{1,0:T(8,128)(2,1)S(1)} %get-tuple-element.86.refs_1_, bf16[512,256]{1,0:T(8,128)(2,1)S(1)} %collective-permute-done.15.refs_2_), custom_call_target="tpu_custom_call" | custom-call | flops 1000 | bytes 1000 | tf_op jit(solution)/shard_map/pallas_call | solution.py:537
  57.3 3.5 %collective-permute-done.12.got = bf16[512,256]{1,0:T(8,128)(2,1)S(1)} collective-permute-done((bf16[512,256]{1,0:T(8,128)(2,1)S(1)}, bf16[512,256]{1,0:T(8,128)(2,1)S(1)}, u32[]{:S(2)}, u32[]{:S(2)}) %collective-permute-start.12) | collective-permute-done | bytes 262176 | tf_op jit(solution)/shard_map/ppermute | solution.py:619
  60.8 1.5 %shard_map.87 = (bf16[512,512]{1,0:T(8,128)(2,1)}, bf16[512,512]{1,0:T(8,128)(2,1)}) custom-call(s32[4]{0:T(128)S(1)} %pad_add_fusion.where, bf16[512,256]{1,0:T(8,128)(2,1)S(1)} %collective-permute-done.12.got, bf16[512,512]{1,0:T(8,128)(2,1)} %get-tuple-element.88.first_in, ...), custom_call_target="tpu_custom_call", output_to_operand_aliasing={{0}: (2, {}), {1}: (3, {})} | custom-call | flops 1000 | bytes 1000 | tf_op jit(solution)/shard_map/pallas_call | solution.py:567
  (33 shorter events, 6.0 us)
Async XLA Ops:
  0.7 4.4 %copy-start.2 = (bf16[512,512]{1,0:T(8,128)(2,1)S(1)}, bf16[512,512]{1,0:T(8,128)(2,1)}, u32[]{:S(2)}) copy-start(bf16[512,512]{1,0:T(8,128)(2,1)} %refs_0_.2) | copy-start | bytes 1572868
  1.7 3.3 %copy-start.3 = (bf16[512,512]{1,0:T(8,128)(2,1)S(1)}, bf16[512,512]{1,0:T(8,128)(2,1)}, u32[]{:S(2)}) copy-start(bf16[512,512]{1,0:T(8,128)(2,1)} %refs_1_.2) | copy-start | bytes 1572868
  2.0 10.1 %collective-permute-start = (bf16[512,256]{1,0:T(8,128)(2,1)S(1)}, bf16[512,256]{1,0:T(8,128)(2,1)S(1)}, u32[]{:S(2)}, u32[]{:S(2)}) collective-permute-start(bf16[512,256]{1,0:T(8,128)(2,1)S(1)} %shard_map.76), channel_id=1, source_target_pairs={{0,1},{1,0},{2,3},{3,2},{4,5},{5,4},{6,7},{7,6},{8,9},{9,8},{10,11... | collective-permute-start | bytes 786440 | tf_op jit(solution)/shard_map/ppermute | solution.py:619
  5.0 1.2 %copy-start = (bf16[512,512]{1,0:T(8,128)(2,1)S(1)}, bf16[512,512]{1,0:T(8,128)(2,1)}, u32[]{:S(2)}) copy-start(bf16[512,512]{1,0:T(8,128)(2,1)} %refs_0_.3) | copy-start | bytes 1572868
  5.0 1.2 %copy-start.1 = (bf16[512,512]{1,0:T(8,128)(2,1)S(1)}, bf16[512,512]{1,0:T(8,128)(2,1)}, u32[]{:S(2)}) copy-start(bf16[512,512]{1,0:T(8,128)(2,1)} %refs_1_.3) | copy-start | bytes 1572868
  5.4 12.4 %collective-permute-start.4 = (bf16[512,256]{1,0:T(8,128)(2,1)S(1)}, bf16[512,256]{1,0:T(8,128)(2,1)S(1)}, u32[]{:S(2)}, u32[]{:S(2)}) collective-permute-start(bf16[512,256]{1,0:T(8,128)(2,1)S(1)} %shard_map.80), channel_id=1, source_target_pairs={{0,1},{1,0},{2,3},{3,2},{4,5},{5,4},{6,7},{7,6},{8,9},{9,8},{10,11... | collective-permute-start | bytes 786440 | tf_op jit(solution)/shard_map/ppermute | solution.py:619
  7.4 15.2 %collective-permute-start.1 = (bf16[512,256]{1,0:T(8,128)(2,1)S(1)}, bf16[512,256]{1,0:T(8,128)(2,1)S(1)}, u32[]{:S(2)}, u32[]{:S(2)}) collective-permute-start(bf16[512,256]{1,0:T(8,128)(2,1)S(1)} %get-tuple-element.51), channel_id=1, source_target_pairs={{0,1},{1,0},{2,3},{3,2},{4,5},{5,4},{6,7},{7,6},{8,9},{9,8},{10,11... | collective-permute-start | bytes 786440 | tf_op jit(solution)/shard_map/ppermute | solution.py:619
  12.9 11.5 %collective-permute-start.2 = (bf16[512,256]{1,0:T(8,128)(2,1)S(1)}, bf16[512,256]{1,0:T(8,128)(2,1)S(1)}, u32[]{:S(2)}, u32[]{:S(2)}) collective-permute-start(bf16[512,256]{1,0:T(8,128)(2,1)S(1)} %get-tuple-element.52), channel_id=1, source_target_pairs={{0,2},{1,3},{2,0},{3,1},{4,6},{5,7},{6,4},{7,5},{8,10},{9,11},{10,... | collective-permute-start | bytes 786440 | tf_op jit(solution)/shard_map/ppermute | solution.py:622
  12.9 11.4 %collective-permute-start.3 = (bf16[512,256]{1,0:T(8,128)(2,1)S(1)}, bf16[512,256]{1,0:T(8,128)(2,1)S(1)}, u32[]{:S(2)}, u32[]{:S(2)}) collective-permute-start(bf16[512,256]{1,0:T(8,128)(2,1)S(1)} %get-tuple-element.53), channel_id=1, source_target_pairs={{2,4},{3,5},{4,2},{5,3},{6,8},{7,9},{8,6},{9,7},{10,12},{11,13},{1... | collective-permute-start | bytes 786440 | tf_op jit(solution)/shard_map/ppermute | solution.py:625
  18.5 13.0 %collective-permute-start.5 = (bf16[512,256]{1,0:T(8,128)(2,1)S(1)}, bf16[512,256]{1,0:T(8,128)(2,1)S(1)}, u32[]{:S(2)}, u32[]{:S(2)}) collective-permute-start(bf16[512,256]{1,0:T(8,128)(2,1)S(1)} %get-tuple-element.61), channel_id=1, source_target_pairs={{0,2},{1,3},{2,0},{3,1},{4,6},{5,7},{6,4},{7,5},{8,10},{9,11},{10,... | collective-permute-start | bytes 786440 | tf_op jit(solution)/shard_map/ppermute | solution.py:622
  18.5 13.0 %collective-permute-start.6 = (bf16[512,256]{1,0:T(8,128)(2,1)S(1)}, bf16[512,256]{1,0:T(8,128)(2,1)S(1)}, u32[]{:S(2)}, u32[]{:S(2)}) collective-permute-start(bf16[512,256]{1,0:T(8,128)(2,1)S(1)} %get-tuple-element.62), channel_id=1, source_target_pairs={{2,4},{3,5},{4,2},{5,3},{6,8},{7,9},{8,6},{9,7},{10,12},{11,13},{1... | collective-permute-start | bytes 786440 | tf_op jit(solution)/shard_map/ppermute | solution.py:625
  22.6 9.0 %collective-permute-start.7 = (bf16[512,256]{1,0:T(8,128)(2,1)S(1)}, bf16[512,256]{1,0:T(8,128)(2,1)S(1)}, u32[]{:S(2)}, u32[]{:S(2)}) collective-permute-start(bf16[512,256]{1,0:T(8,128)(2,1)S(1)} %get-tuple-element.64), channel_id=1, source_target_pairs={{0,1},{1,0},{2,3},{3,2},{4,5},{5,4},{6,7},{7,6},{8,9},{9,8},{10,11... | collective-permute-start | bytes 786440 | tf_op jit(solution)/shard_map/ppermute | solution.py:619
  30.3 7.9 %collective-permute-start.8 = (bf16[2,2,128,256]{3,2,1,0:T(8,128)(2,1)S(1)}, bf16[2,2,128,256]{3,2,1,0:T(8,128)(2,1)S(1)}, u32[]{:S(2)}, u32[]{:S(2)}) collective-permute-start(bf16[2,2,128,256]{3,2,1,0:T(8,128)(2,1)S(1)} %get-tuple-element.66), channel_id=1, source_target_pairs={{0,1},{1,0},{2,3},{3,2},{4,5},{5,4},{6,7},{7,6},{8,9},{9,8},{10,11... | collective-permute-start | bytes 786440 | tf_op jit(solution)/shard_map/ppermute | solution.py:619
  30.6 12.2 %collective-permute-start.14 = (bf16[512,256]{1,0:T(8,128)(2,1)S(1)}, bf16[512,256]{1,0:T(8,128)(2,1)S(1)}, u32[]{:S(2)}, u32[]{:S(2)}) collective-permute-start(bf16[512,256]{1,0:T(8,128)(2,1)S(1)} %get-tuple-element.84), channel_id=1, source_target_pairs={{2,4},{3,5},{4,2},{5,3},{6,8},{7,9},{8,6},{9,7},{10,12},{11,13},{1... | collective-permute-start | bytes 786440 | tf_op jit(solution)/shard_map/ppermute | solution.py:625
  38.2 4.7 %collective-permute-start.13 = (bf16[512,256]{1,0:T(8,128)(2,1)S(1)}, bf16[512,256]{1,0:T(8,128)(2,1)S(1)}, u32[]{:S(2)}, u32[]{:S(2)}) collective-permute-start(bf16[512,256]{1,0:T(8,128)(2,1)S(1)} %get-tuple-element.83), channel_id=1, source_target_pairs={{0,2},{1,3},{2,0},{3,1},{4,6},{5,7},{6,4},{7,5},{8,10},{9,11},{10,... | collective-permute-start | bytes 786440 | tf_op jit(solution)/shard_map/ppermute | solution.py:622
  41.3 8.7 %collective-permute-start.9 = (bf16[2,2,128,256]{3,2,1,0:T(8,128)(2,1)S(1)}, bf16[2,2,128,256]{3,2,1,0:T(8,128)(2,1)S(1)}, u32[]{:S(2)}, u32[]{:S(2)}) collective-permute-start(bf16[2,2,128,256]{3,2,1,0:T(8,128)(2,1)S(1)} %get-tuple-element.71), channel_id=1, source_target_pairs={{0,1},{1,0},{2,3},{3,2},{4,5},{5,4},{6,7},{7,6},{8,9},{9,8},{10,11... | collective-permute-start | bytes 786440 | tf_op jit(solution)/shard_map/ppermute | solution.py:619
  42.2 7.9 %collective-permute-start.10 = (bf16[512,256]{1,0:T(8,128)(2,1)S(1)}, bf16[512,256]{1,0:T(8,128)(2,1)S(1)}, u32[]{:S(2)}, u32[]{:S(2)}) collective-permute-start(bf16[512,256]{1,0:T(8,128)(2,1)S(1)} %get-tuple-element.73), channel_id=1, source_target_pairs={{0,2},{1,3},{2,0},{3,1},{4,6},{5,7},{6,4},{7,5},{8,10},{9,11},{10,... | collective-permute-start | bytes 786440 | tf_op jit(solution)/shard_map/ppermute | solution.py:622
  42.2 7.9 %collective-permute-start.11 = (bf16[512,256]{1,0:T(8,128)(2,1)S(1)}, bf16[512,256]{1,0:T(8,128)(2,1)S(1)}, u32[]{:S(2)}, u32[]{:S(2)}) collective-permute-start(bf16[512,256]{1,0:T(8,128)(2,1)S(1)} %get-tuple-element.74), channel_id=1, source_target_pairs={{2,4},{3,5},{4,2},{5,3},{6,8},{7,9},{8,6},{9,7},{10,12},{11,13},{1... | collective-permute-start | bytes 786440 | tf_op jit(solution)/shard_map/ppermute | solution.py:625
  43.6 11.7 %collective-permute-start.15 = (bf16[512,256]{1,0:T(8,128)(2,1)S(1)}, bf16[512,256]{1,0:T(8,128)(2,1)S(1)}, u32[]{:S(2)}, u32[]{:S(2)}) collective-permute-start(bf16[512,256]{1,0:T(8,128)(2,1)S(1)} %get-tuple-element.87), channel_id=1, source_target_pairs={{0,1},{1,0},{2,3},{3,2},{4,5},{5,4},{6,7},{7,6},{8,9},{9,8},{10,11... | collective-permute-start | bytes 786440 | tf_op jit(solution)/shard_map/ppermute | solution.py:619
  50.8 10.1 %collective-permute-start.12 = (bf16[512,256]{1,0:T(8,128)(2,1)S(1)}, bf16[512,256]{1,0:T(8,128)(2,1)S(1)}, u32[]{:S(2)}, u32[]{:S(2)}) collective-permute-start(bf16[512,256]{1,0:T(8,128)(2,1)S(1)} %get-tuple-element.81), channel_id=1, source_target_pairs={{0,1},{1,0},{2,3},{3,2},{4,5},{5,4},{6,7},{7,6},{8,9},{9,8},{10,11... | collective-permute-start | bytes 786440 | tf_op jit(solution)/shard_map/ppermute | solution.py:619

commit v16 on v13

--- a/solution.py
+++ b/solution.py
@@ -240,7 +240,7 @@
 def one_chunk(
     where, kv_own, kv_got, near_got, wide_got, qg_own, qg_got,
     oq_own, oq_far, grad, near_out, wide_out,
-    raw, raw_t, one, one_t, two, two_t, qs, gs, p0, p1, p2, acc0, acc1, acc2, oq, halos,
+    raw, raw_t, one, one_t, two, two_t, qs, gs, p0, p1, p2, f0_rows, dr_rows, dq0, acc0, acc1, acc2, oq, halos,
 ):
     side = where[0]
     odd = where[3]
@@ -314,7 +314,6 @@
         acc0[...] = jnp.zeros_like(acc0)
         g1_t, ec1, f1 = [], [], []
         g2_t, ec2, low2 = [], [], []
-        dq0 = []
         for i in range(4):
             rows = slice(i * PARENT, i * PARENT + 3 * PARENT)
             q = q_parents[i]
@@ -330,7 +329,7 @@
             )
             e = [jnp.exp2((x - m0) * TO_LOG2) for x in pieces]
             for n in range(3):
-                p0[n * PARENT : (n + 1) * PARENT, :] = e[n]
+                p0[i, n * PARENT : (n + 1) * PARENT, :] = e[n]
             z0 = jnp.sum(e[0] + e[1] + e[2], axis=0, keepdims=True)
             u0 = dot_nn(raw_t[1, :, rows], jnp.concatenate([x.astype(BF) for x in e], axis=0))
             j, half = i // 2, i % 2
@@ -365,14 +364,23 @@
             part = w_a * dr_a + w_b * dr_b
             ec2.append(part + swap64(part))
             low2.append(lower)
-            f0 = jnp.exp2(m0 * TO_LOG2 - lg)
+            f0_rows[i] = jnp.exp2(m0 * TO_LOG2 - lg)
+            dr_rows[i] = dr
+
+        @pl.loop(0, 4)
+        def _(i):
+            at = pl.multiple_of(i * PARENT, PARENT)
+            rows = pl.ds(at, 3 * PARENT)
+            q = qs[pl.ds(at, PARENT), :]
+            g = gs[pl.ds(at, PARENT), :]
             products = dot_nt(raw[1, rows, :], g)
-            weights = p0[...] * f0
+            weights = p0[i] * f0_rows[i]
             eb = weights.astype(BF)
-            r = (weights * (products - dr)).astype(BF)
+            r = (weights * (products - dr_rows[i])).astype(BF)
             acc0[1, rows, :] += dot_nn(eb, g)
             acc0[0, rows, :] += dot_nn(r, q)
-            dq0.append(dot_nn(raw_t[0, :, rows], r))
+            dq0[i] = dot_nn(raw_t[0, :, rows], r)
+
         acc1[...] = jnp.zeros_like(acc1)
         dq1 = []
         for j in range(2):
@@ -461,9 +469,12 @@
             pltpu.VMEM((2, HEAD, 512), BF),
             pltpu.VMEM((1024, HEAD), BF),
             pltpu.VMEM((1024, HEAD), BF),
-            pltpu.VMEM((768, PARENT), F32),
+            pltpu.VMEM((4, 768, PARENT), F32),
             pltpu.VMEM((2, 384, PARENT), F32),
             pltpu.VMEM((384, PARENT), F32),
+            pltpu.VMEM((4, 1, PARENT), F32),
+            pltpu.VMEM((4, 1, PARENT), F32),
+            pltpu.VMEM((4, HEAD, PARENT), F32),
             pltpu.VMEM((2, 1536, HEAD), F32),
             pltpu.VMEM((2, 1024, HEAD), F32),
             pltpu.VMEM((2, 512, HEAD), F32),

time: 61.2 us -> 64.8 us (1.059)
  Pallas kernels: 23.8 us -> 27.4 us
    pallas_call x2, Pallas kernels: 11.9 us -> 15.5 us  [main(): pl.pallas_call(functools.partial(main_kernel, qg_first), in_specs=[smem()...]
  transfers between devices with their start and end apart: 16 -> 16, of which waited for: 6 -> 6; matrix products, arithmetic and copies ran while one was open for 0% -> 0% of each run, Pallas kernels for 36% -> 40%
where the time goes in v16:
time: 64.8 us; the launch traced here: 64.2 us
  Pallas kernels  27.4 us (42%)
  starting transfers between devices  21.3 us (33%)
  waiting for transfers between devices  13.3 us (21%)
  local copies, waits for them, and re-layouts  1.16 us (2%)
  between operations  1.02 us (2%)
    pallas_call x2, Pallas kernels, main(): pl.pallas_call(functools.partial(main_kernel, qg_first), in_specs=[smem()...  15.5 us
    ppermute x8, starting transfers between devices, swap(): return lax.ppermute(x, axes, across)  10.3 us
    ppermute x4, starting transfers between devices, beside(): return (near, lax.ppermute(wide, axes, wide_edges))  10.1 us
    ppermute x8, waiting for transfers between devices, swap(): return lax.ppermute(x, axes, across)  9.65 us
    ppermute x4, waiting for transfers between devices, beside(): return (near, lax.ppermute(wide, axes, wide_edges))  3.68 us
    pallas_call x2, Pallas kernels, pack(): pl.pallas_call(functools.partial(pack_kernel, own), in_specs=[smem()] + [...  2.76 us
    pallas_call x1, Pallas kernels, unpack_columns(): pl.pallas_call(unpack_columns_kernel, in_specs=[smem()] + [vmem()] * (2 *...  2.21 us
    pallas_call x1, Pallas kernels, unpack_rows(): pl.pallas_call(unpack_rows_kernel, in_specs=[smem()] + [vmem()] * (CHUNKS...  2.07 us
  transfers between devices with their start and end apart: 16, of which 6 were waited for; matrix products, arithmetic and copies ran while one was open for 0% of the time, Pallas kernels for 40%

profile of v16, /device:TPU:12, one launch (start us, length us, event | category | flops | bytes accessed | tf_op | source)
XLA Modules:
  0.0 64.2 jit_solution(18232297727413691751)
XLA Ops:
  2.0 1.6 %collective-permute-start = (bf16[512,256]{1,0:T(8,128)(2,1)S(1)}, bf16[512,256]{1,0:T(8,128)(2,1)S(1)}, u32[]{:S(2)}, u32[]{:S(2)}) collective-permute-start(bf16[512,256]{1,0:T(8,128)(2,1)S(1)} %shard_map.76), channel_id=1, source_target_pairs={{0,1},{1,0},{2,3},{3,2},{4,5},{5,4},{6,7},{7,6},{8,9},{9,8},{10,11... | collective-permute-start | bytes 786440 | tf_op jit(solution)/shard_map/ppermute | solution.py:630
  4.8 1.1 %shard_map.77 = (bf16[512,256]{1,0:T(8,128)(2,1)S(1)}, bf16[512,256]{1,0:T(8,128)(2,1)S(1)}) custom-call(s32[4]{0:T(128)S(1)} %pad_add_fusion.where, bf16[512,512]{1,0:T(8,128)(2,1)S(1)} %copy-done, bf16[512,512]{1,0:T(8,128)(2,1)S(1)} %copy-done.1), custom_call_target="tpu_custom_call" | custom-call | flops 1000 | bytes 1000 | tf_op jit(solution)/shard_map/pallas_call | solution.py:86
  5.9 1.4 %collective-permute-start.1 = (bf16[512,256]{1,0:T(8,128)(2,1)S(1)}, bf16[512,256]{1,0:T(8,128)(2,1)S(1)}, u32[]{:S(2)}, u32[]{:S(2)}) collective-permute-start(bf16[512,256]{1,0:T(8,128)(2,1)S(1)} %get-tuple-element.50), channel_id=1, source_target_pairs={{0,1},{1,0},{2,3},{3,2},{4,5},{5,4},{6,7},{7,6},{8,9},{9,8},{10,11... | collective-permute-start | bytes 786440 | tf_op jit(solution)/shard_map/ppermute | solution.py:630
  7.3 1.6 %shard_map.75 = (bf16[512,256]{1,0:T(8,128)(2,1)S(1)}, bf16[512,256]{1,0:T(8,128)(2,1)S(1)}, bf16[512,256]{1,0:T(8,128)(2,1)S(1)}, bf16[512,256]{1,0:T(8,128)(2,1)S(1)}) custom-call(s32[4]{0:T(128)S(1)} %pad_add_fusion.where, bf16[512,512]{1,0:T(8,128)(2,1)S(1)} %copy-done.2, bf16[512,512]{1,0:T(8,128)(2,1)S(1)} %copy-done.3, bf16[512,512]{1,0:T(8,128)(2,1)S(1)} %copy-done, ...), custom_call_target="tpu_custom_call" | custom-call | flops 1000 | bytes 1000 | tf_op jit(solution)/shard_map/pallas_call | solution.py:86
  9.0 2.3 %collective-permute-done.got.kv_got = bf16[512,256]{1,0:T(8,128)(2,1)S(1)} collective-permute-done((bf16[512,256]{1,0:T(8,128)(2,1)S(1)}, bf16[512,256]{1,0:T(8,128)(2,1)S(1)}, u32[]{:S(2)}, u32[]{:S(2)}) %collective-permute-start) | collective-permute-done | bytes 262176 | tf_op jit(solution)/shard_map/ppermute | solution.py:630
  12.0 2.5 %collective-permute-start.3 = (bf16[512,256]{1,0:T(8,128)(2,1)S(1)}, bf16[512,256]{1,0:T(8,128)(2,1)S(1)}, u32[]{:S(2)}, u32[]{:S(2)}) collective-permute-start(bf16[512,256]{1,0:T(8,128)(2,1)S(1)} %get-tuple-element.52), channel_id=1, source_target_pairs={{2,4},{3,5},{4,2},{5,3},{6,8},{7,9},{8,6},{9,7},{10,12},{11,13},{1... | collective-permute-start | bytes 786440 | tf_op jit(solution)/shard_map/ppermute | solution.py:634
  14.6 2.3 %collective-permute-done.4.got.kv_got = bf16[512,256]{1,0:T(8,128)(2,1)S(1)} collective-permute-done((bf16[512,256]{1,0:T(8,128)(2,1)S(1)}, bf16[512,256]{1,0:T(8,128)(2,1)S(1)}, u32[]{:S(2)}, u32[]{:S(2)}) %collective-permute-start.4) | collective-permute-done | bytes 262176 | tf_op jit(solution)/shard_map/ppermute | solution.py:630
  17.7 2.5 %collective-permute-start.6 = (bf16[512,256]{1,0:T(8,128)(2,1)S(1)}, bf16[512,256]{1,0:T(8,128)(2,1)S(1)}, u32[]{:S(2)}, u32[]{:S(2)}) collective-permute-start(bf16[512,256]{1,0:T(8,128)(2,1)S(1)} %get-tuple-element.61), channel_id=1, source_target_pairs={{2,4},{3,5},{4,2},{5,3},{6,8},{7,9},{8,6},{9,7},{10,12},{11,13},{1... | collective-permute-start | bytes 786440 | tf_op jit(solution)/shard_map/ppermute | solution.py:634
  20.2 1.2 %collective-permute-done.1.refs_1_ = bf16[512,256]{1,0:T(8,128)(2,1)S(1)} collective-permute-done((bf16[512,256]{1,0:T(8,128)(2,1)S(1)}, bf16[512,256]{1,0:T(8,128)(2,1)S(1)}, u32[]{:S(2)}, u32[]{:S(2)}) %collective-permute-start.1) | collective-permute-done | bytes 262176 | tf_op jit(solution)/shard_map/ppermute | solution.py:630
  21.4 1.5 %collective-permute-start.7 = (bf16[512,256]{1,0:T(8,128)(2,1)S(1)}, bf16[512,256]{1,0:T(8,128)(2,1)S(1)}, u32[]{:S(2)}, u32[]{:S(2)}) collective-permute-start(bf16[512,256]{1,0:T(8,128)(2,1)S(1)} %get-tuple-element.63), channel_id=1, source_target_pairs={{0,1},{1,0},{2,3},{3,2},{4,5},{5,4},{6,7},{7,6},{8,9},{9,8},{10,11... | collective-permute-start | bytes 786440 | tf_op jit(solution)/shard_map/ppermute | solution.py:630
  22.9 7.8 %shard_map.79 = (bf16[2,2,128,256]{3,2,1,0:T(8,128)(2,1)S(1)}, bf16[2,2,128,256]{3,2,1,0:T(8,128)(2,1)S(1)}, f32[1024,256]{1,0:T(8,128)S(1)}, bf16[512,256]{1,0:T(8,128)(2,1)S(1)}, bf16[512,256]{1,0:T(8,128)(2,1)S(1)}) custom-call(s32[4]{0:T(128)S(1)} %pad_add_fusion.where, bf16[512,256]{1,0:T(8,128)(2,1)S(1)} %get-tuple-element.47.own.kv_own, ...), custom_call_target="tpu_custom_call" | custom-call | flops 1000 | bytes 1000 | tf_op jit(solution)/shard_map/pallas_call | solution.py:452
  30.6 1.2 %collective-permute-start.8 = (bf16[2,2,128,256]{3,2,1,0:T(8,128)(2,1)S(1)}, bf16[2,2,128,256]{3,2,1,0:T(8,128)(2,1)S(1)}, u32[]{:S(2)}, u32[]{:S(2)}) collective-permute-start(bf16[2,2,128,256]{3,2,1,0:T(8,128)(2,1)S(1)} %get-tuple-element.65), channel_id=1, source_target_pairs={{0,1},{1,0},{2,3},{3,2},{4,5},{5,4},{6,7},{7,6},{8,9},{9,8},{10,11... | collective-permute-start | bytes 786440 | tf_op jit(solution)/shard_map/ppermute | solution.py:630
  31.9 2.4 %collective-permute-start.14 = (bf16[512,256]{1,0:T(8,128)(2,1)S(1)}, bf16[512,256]{1,0:T(8,128)(2,1)S(1)}, u32[]{:S(2)}, u32[]{:S(2)}) collective-permute-start(bf16[512,256]{1,0:T(8,128)(2,1)S(1)} %get-tuple-element.82), channel_id=1, source_target_pairs={{2,4},{3,5},{4,2},{5,3},{6,8},{7,9},{8,6},{9,7},{10,12},{11,13},{1... | collective-permute-start | bytes 786440 | tf_op jit(solution)/shard_map/ppermute | solution.py:634
  34.3 7.8 %shard_map.82 = (bf16[2,2,128,256]{3,2,1,0:T(8,128)(2,1)S(1)}, bf16[2,2,128,256]{3,2,1,0:T(8,128)(2,1)S(1)}, f32[1024,256]{1,0:T(8,128)S(1)}, bf16[512,256]{1,0:T(8,128)(2,1)S(1)}, bf16[512,256]{1,0:T(8,128)(2,1)S(1)}) custom-call(s32[4]{0:T(128)S(1)} %pad_add_fusion.where, bf16[512,256]{1,0:T(8,128)(2,1)S(1)} %get-tuple-element.54.own.kv_own, ...), custom_call_target="tpu_custom_call" | custom-call | flops 1000 | bytes 1000 | tf_op jit(solution)/shard_map/pallas_call | solution.py:452
  42.1 1.2 %collective-permute-start.9 = (bf16[2,2,128,256]{3,2,1,0:T(8,128)(2,1)S(1)}, bf16[2,2,128,256]{3,2,1,0:T(8,128)(2,1)S(1)}, u32[]{:S(2)}, u32[]{:S(2)}) collective-permute-start(bf16[2,2,128,256]{3,2,1,0:T(8,128)(2,1)S(1)} %get-tuple-element.69), channel_id=1, source_target_pairs={{0,1},{1,0},{2,3},{3,2},{4,5},{5,4},{6,7},{7,6},{8,9},{9,8},{10,11... | collective-permute-start | bytes 786440 | tf_op jit(solution)/shard_map/ppermute | solution.py:630
  44.1 2.7 %collective-permute-start.11 = (bf16[512,256]{1,0:T(8,128)(2,1)S(1)}, bf16[512,256]{1,0:T(8,128)(2,1)S(1)}, u32[]{:S(2)}, u32[]{:S(2)}) collective-permute-start(bf16[512,256]{1,0:T(8,128)(2,1)S(1)} %get-tuple-element.72), channel_id=1, source_target_pairs={{2,4},{3,5},{4,2},{5,3},{6,8},{7,9},{8,6},{9,7},{10,12},{11,13},{1... | collective-permute-start | bytes 786440 | tf_op jit(solution)/shard_map/ppermute | solution.py:634
  47.5 1.2 %collective-permute-start.15 = (bf16[512,256]{1,0:T(8,128)(2,1)S(1)}, bf16[512,256]{1,0:T(8,128)(2,1)S(1)}, u32[]{:S(2)}, u32[]{:S(2)}) collective-permute-start(bf16[512,256]{1,0:T(8,128)(2,1)S(1)} %get-tuple-element.85), channel_id=1, source_target_pairs={{0,1},{1,0},{2,3},{3,2},{4,5},{5,4},{6,7},{7,6},{8,9},{9,8},{10,11... | collective-permute-start | bytes 786440 | tf_op jit(solution)/shard_map/ppermute | solution.py:630
  48.7 2.2 %collective-permute-done.9.refs_3_ = bf16[2,2,128,256]{3,2,1,0:T(8,128)(2,1)S(1)} collective-permute-done((bf16[2,2,128,256]{3,2,1,0:T(8,128)(2,1)S(1)}, bf16[2,2,128,256]{3,2,1,0:T(8,128)(2,1)S(1)}, u32[]{:S(2)}, u32[]{:S(2)}) %collective-permute-start.9) | collective-permute-done | bytes 262176 | tf_op jit(solution)/shard_map/ppermute | solution.py:630
  50.9 3.7 %collective-permute-done.11.wide_got = bf16[512,256]{1,0:T(8,128)(2,1)S(1)} collective-permute-done((bf16[512,256]{1,0:T(8,128)(2,1)S(1)}, bf16[512,256]{1,0:T(8,128)(2,1)S(1)}, u32[]{:S(2)}, u32[]{:S(2)}) %collective-permute-start.11) | collective-permute-done | bytes 262176 | tf_op jit(solution)/shard_map/ppermute | solution.py:634
  55.2 1.4 %collective-permute-start.12 = (bf16[512,256]{1,0:T(8,128)(2,1)S(1)}, bf16[512,256]{1,0:T(8,128)(2,1)S(1)}, u32[]{:S(2)}, u32[]{:S(2)}) collective-permute-start(bf16[512,256]{1,0:T(8,128)(2,1)S(1)} %get-tuple-element.79), channel_id=1, source_target_pairs={{0,1},{1,0},{2,3},{3,2},{4,5},{5,4},{6,7},{7,6},{8,9},{9,8},{10,11... | collective-permute-start | bytes 786440 | tf_op jit(solution)/shard_map/ppermute | solution.py:630
  56.7 2.2 %shard_map.83 = (bf16[512,512]{1,0:T(8,128)(2,1)}, bf16[512,512]{1,0:T(8,128)(2,1)}) custom-call(s32[4]{0:T(128)S(1)} %pad_add_fusion.where, bf16[2,2,128,256]{3,2,1,0:T(8,128)(2,1)S(1)} %get-tuple-element.53.refs_0_, bf16[2,2,128,256]{3,2,1,0:T(8,128)(2,1)S(1)} %get-tuple-element.64.refs_1_, bf16[2,2,128,256]{3,2,1,0:T(8,128)(2,1)S(1)} %collective-permute-done.8.refs_2_, ...), custom_call_target="tpu_custom_call" | custom-call | flops 1000 | bytes 1000 | tf_op jit(solution)/shard_map/pallas_call | solution.py:608
  58.9 2.1 %shard_map.86 = (bf16[512,512]{1,0:T(8,128)(2,1)}, bf16[512,512]{1,0:T(8,128)(2,1)}) custom-call(s32[4]{0:T(128)S(1)} %pad_add_fusion.where, bf16[512,256]{1,0:T(8,128)(2,1)S(1)} %get-tuple-element.83.refs_0_, bf16[512,256]{1,0:T(8,128)(2,1)S(1)} %get-tuple-element.84.refs_1_, bf16[512,256]{1,0:T(8,128)(2,1)S(1)} %collective-permute-done.15.refs_2_), custom_call_target="tpu_custom_call" | custom-call | flops 1000 | bytes 1000 | tf_op jit(solution)/shard_map/pallas_call | solution.py:548
  61.0 1.6 %collective-permute-done.12.got = bf16[512,256]{1,0:T(8,128)(2,1)S(1)} collective-permute-done((bf16[512,256]{1,0:T(8,128)(2,1)S(1)}, bf16[512,256]{1,0:T(8,128)(2,1)S(1)}, u32[]{:S(2)}, u32[]{:S(2)}) %collective-permute-start.12) | collective-permute-done | bytes 262176 | tf_op jit(solution)/shard_map/ppermute | solution.py:630
  62.6 1.5 %shard_map.87 = (bf16[512,512]{1,0:T(8,128)(2,1)}, bf16[512,512]{1,0:T(8,128)(2,1)}) custom-call(s32[4]{0:T(128)S(1)} %pad_add_fusion.where, bf16[512,256]{1,0:T(8,128)(2,1)S(1)} %collective-permute-done.12.got, bf16[512,512]{1,0:T(8,128)(2,1)} %get-tuple-element.86.first_in, ...), custom_call_target="tpu_custom_call", output_to_operand_aliasing={{0}: (2, {}), {1}: (3, {})} | custom-call | flops 1000 | bytes 1000 | tf_op jit(solution)/shard_map/pallas_call | solution.py:578
  (33 shorter events, 6.1 us)
Async XLA Ops:
  0.7 2.9 %copy-start.2 = (bf16[512,512]{1,0:T(8,128)(2,1)S(1)}, bf16[512,512]{1,0:T(8,128)(2,1)}, u32[]{:S(2)}) copy-start(bf16[512,512]{1,0:T(8,128)(2,1)} %refs_0_.2) | copy-start | bytes 1572868
  1.7 1.9 %copy-start.3 = (bf16[512,512]{1,0:T(8,128)(2,1)S(1)}, bf16[512,512]{1,0:T(8,128)(2,1)}, u32[]{:S(2)}) copy-start(bf16[512,512]{1,0:T(8,128)(2,1)} %refs_1_.2) | copy-start | bytes 1572868
  2.0 9.3 %collective-permute-start = (bf16[512,256]{1,0:T(8,128)(2,1)S(1)}, bf16[512,256]{1,0:T(8,128)(2,1)S(1)}, u32[]{:S(2)}, u32[]{:S(2)}) collective-permute-start(bf16[512,256]{1,0:T(8,128)(2,1)S(1)} %shard_map.76), channel_id=1, source_target_pairs={{0,1},{1,0},{2,3},{3,2},{4,5},{5,4},{6,7},{7,6},{8,9},{9,8},{10,11... | collective-permute-start | bytes 786440 | tf_op jit(solution)/shard_map/ppermute | solution.py:630
  3.6 1.2 %copy-start = (bf16[512,512]{1,0:T(8,128)(2,1)S(1)}, bf16[512,512]{1,0:T(8,128)(2,1)}, u32[]{:S(2)}) copy-start(bf16[512,512]{1,0:T(8,128)(2,1)} %refs_0_.3) | copy-start | bytes 1572868
  3.6 1.2 %copy-start.1 = (bf16[512,512]{1,0:T(8,128)(2,1)S(1)}, bf16[512,512]{1,0:T(8,128)(2,1)}, u32[]{:S(2)}) copy-start(bf16[512,512]{1,0:T(8,128)(2,1)} %refs_1_.3) | copy-start | bytes 1572868
  3.9 13.0 %collective-permute-start.4 = (bf16[512,256]{1,0:T(8,128)(2,1)S(1)}, bf16[512,256]{1,0:T(8,128)(2,1)S(1)}, u32[]{:S(2)}, u32[]{:S(2)}) collective-permute-start(bf16[512,256]{1,0:T(8,128)(2,1)S(1)} %shard_map.80), channel_id=1, source_target_pairs={{0,1},{1,0},{2,3},{3,2},{4,5},{5,4},{6,7},{7,6},{8,9},{9,8},{10,11... | collective-permute-start | bytes 786440 | tf_op jit(solution)/shard_map/ppermute | solution.py:630
  5.9 15.4 %collective-permute-start.1 = (bf16[512,256]{1,0:T(8,128)(2,1)S(1)}, bf16[512,256]{1,0:T(8,128)(2,1)S(1)}, u32[]{:S(2)}, u32[]{:S(2)}) collective-permute-start(bf16[512,256]{1,0:T(8,128)(2,1)S(1)} %get-tuple-element.50), channel_id=1, source_target_pairs={{0,1},{1,0},{2,3},{3,2},{4,5},{5,4},{6,7},{7,6},{8,9},{9,8},{10,11... | collective-permute-start | bytes 786440 | tf_op jit(solution)/shard_map/ppermute | solution.py:630
  12.0 10.9 %collective-permute-start.2 = (bf16[512,256]{1,0:T(8,128)(2,1)S(1)}, bf16[512,256]{1,0:T(8,128)(2,1)S(1)}, u32[]{:S(2)}, u32[]{:S(2)}) collective-permute-start(bf16[512,256]{1,0:T(8,128)(2,1)S(1)} %get-tuple-element.51), channel_id=1, source_target_pairs={{0,2},{1,3},{2,0},{3,1},{4,6},{5,7},{6,4},{7,5},{8,10},{9,11},{10,... | collective-permute-start | bytes 786440 | tf_op jit(solution)/shard_map/ppermute | solution.py:633
  12.0 10.8 %collective-permute-start.3 = (bf16[512,256]{1,0:T(8,128)(2,1)S(1)}, bf16[512,256]{1,0:T(8,128)(2,1)S(1)}, u32[]{:S(2)}, u32[]{:S(2)}) collective-permute-start(bf16[512,256]{1,0:T(8,128)(2,1)S(1)} %get-tuple-element.52), channel_id=1, source_target_pairs={{2,4},{3,5},{4,2},{5,3},{6,8},{7,9},{8,6},{9,7},{10,12},{11,13},{1... | collective-permute-start | bytes 786440 | tf_op jit(solution)/shard_map/ppermute | solution.py:634
  17.6 14.3 %collective-permute-start.5 = (bf16[512,256]{1,0:T(8,128)(2,1)S(1)}, bf16[512,256]{1,0:T(8,128)(2,1)S(1)}, u32[]{:S(2)}, u32[]{:S(2)}) collective-permute-start(bf16[512,256]{1,0:T(8,128)(2,1)S(1)} %get-tuple-element.60), channel_id=1, source_target_pairs={{0,2},{1,3},{2,0},{3,1},{4,6},{5,7},{6,4},{7,5},{8,10},{9,11},{10,... | collective-permute-start | bytes 786440 | tf_op jit(solution)/shard_map/ppermute | solution.py:633
  17.7 16.6 %collective-permute-start.6 = (bf16[512,256]{1,0:T(8,128)(2,1)S(1)}, bf16[512,256]{1,0:T(8,128)(2,1)S(1)}, u32[]{:S(2)}, u32[]{:S(2)}) collective-permute-start(bf16[512,256]{1,0:T(8,128)(2,1)S(1)} %get-tuple-element.61), channel_id=1, source_target_pairs={{2,4},{3,5},{4,2},{5,3},{6,8},{7,9},{8,6},{9,7},{10,12},{11,13},{1... | collective-permute-start | bytes 786440 | tf_op jit(solution)/shard_map/ppermute | solution.py:634
  21.4 12.9 %collective-permute-start.7 = (bf16[512,256]{1,0:T(8,128)(2,1)S(1)}, bf16[512,256]{1,0:T(8,128)(2,1)S(1)}, u32[]{:S(2)}, u32[]{:S(2)}) collective-permute-start(bf16[512,256]{1,0:T(8,128)(2,1)S(1)} %get-tuple-element.63), channel_id=1, source_target_pairs={{0,1},{1,0},{2,3},{3,2},{4,5},{5,4},{6,7},{7,6},{8,9},{9,8},{10,11... | collective-permute-start | bytes 786440 | tf_op jit(solution)/shard_map/ppermute | solution.py:630
  30.6 12.7 %collective-permute-start.8 = (bf16[2,2,128,256]{3,2,1,0:T(8,128)(2,1)S(1)}, bf16[2,2,128,256]{3,2,1,0:T(8,128)(2,1)S(1)}, u32[]{:S(2)}, u32[]{:S(2)}) collective-permute-start(bf16[2,2,128,256]{3,2,1,0:T(8,128)(2,1)S(1)} %get-tuple-element.65), channel_id=1, source_target_pairs={{0,1},{1,0},{2,3},{3,2},{4,5},{5,4},{6,7},{7,6},{8,9},{9,8},{10,11... | collective-permute-start | bytes 786440 | tf_op jit(solution)/shard_map/ppermute | solution.py:630
  31.9 14.9 %collective-permute-start.13 = (bf16[512,256]{1,0:T(8,128)(2,1)S(1)}, bf16[512,256]{1,0:T(8,128)(2,1)S(1)}, u32[]{:S(2)}, u32[]{:S(2)}) collective-permute-start(bf16[512,256]{1,0:T(8,128)(2,1)S(1)} %get-tuple-element.81), channel_id=1, source_target_pairs={{0,2},{1,3},{2,0},{3,1},{4,6},{5,7},{6,4},{7,5},{8,10},{9,11},{10,... | collective-permute-start | bytes 786440 | tf_op jit(solution)/shard_map/ppermute | solution.py:633
  31.9 14.9 %collective-permute-start.14 = (bf16[512,256]{1,0:T(8,128)(2,1)S(1)}, bf16[512,256]{1,0:T(8,128)(2,1)S(1)}, u32[]{:S(2)}, u32[]{:S(2)}) collective-permute-start(bf16[512,256]{1,0:T(8,128)(2,1)S(1)} %get-tuple-element.82), channel_id=1, source_target_pairs={{2,4},{3,5},{4,2},{5,3},{6,8},{7,9},{8,6},{9,7},{10,12},{11,13},{1... | collective-permute-start | bytes 786440 | tf_op jit(solution)/shard_map/ppermute | solution.py:634
  42.1 8.8 %collective-permute-start.9 = (bf16[2,2,128,256]{3,2,1,0:T(8,128)(2,1)S(1)}, bf16[2,2,128,256]{3,2,1,0:T(8,128)(2,1)S(1)}, u32[]{:S(2)}, u32[]{:S(2)}) collective-permute-start(bf16[2,2,128,256]{3,2,1,0:T(8,128)(2,1)S(1)} %get-tuple-element.69), channel_id=1, source_target_pairs={{0,1},{1,0},{2,3},{3,2},{4,5},{5,4},{6,7},{7,6},{8,9},{9,8},{10,11... | collective-permute-start | bytes 786440 | tf_op jit(solution)/shard_map/ppermute | solution.py:630
  43.3 7.6 %collective-permute-start.10 = (bf16[512,256]{1,0:T(8,128)(2,1)S(1)}, bf16[512,256]{1,0:T(8,128)(2,1)S(1)}, u32[]{:S(2)}, u32[]{:S(2)}) collective-permute-start(bf16[512,256]{1,0:T(8,128)(2,1)S(1)} %get-tuple-element.71), channel_id=1, source_target_pairs={{0,2},{1,3},{2,0},{3,1},{4,6},{5,7},{6,4},{7,5},{8,10},{9,11},{10,... | collective-permute-start | bytes 786440 | tf_op jit(solution)/shard_map/ppermute | solution.py:633
  44.1 10.5 %collective-permute-start.11 = (bf16[512,256]{1,0:T(8,128)(2,1)S(1)}, bf16[512,256]{1,0:T(8,128)(2,1)S(1)}, u32[]{:S(2)}, u32[]{:S(2)}) collective-permute-start(bf16[512,256]{1,0:T(8,128)(2,1)S(1)} %get-tuple-element.72), channel_id=1, source_target_pairs={{2,4},{3,5},{4,2},{5,3},{6,8},{7,9},{8,6},{9,7},{10,12},{11,13},{1... | collective-permute-start | bytes 786440 | tf_op jit(solution)/shard_map/ppermute | solution.py:634
  47.5 11.4 %collective-permute-start.15 = (bf16[512,256]{1,0:T(8,128)(2,1)S(1)}, bf16[512,256]{1,0:T(8,128)(2,1)S(1)}, u32[]{:S(2)}, u32[]{:S(2)}) collective-permute-start(bf16[512,256]{1,0:T(8,128)(2,1)S(1)} %get-tuple-element.85), channel_id=1, source_target_pairs={{0,1},{1,0},{2,3},{3,2},{4,5},{5,4},{6,7},{7,6},{8,9},{9,8},{10,11... | collective-permute-start | bytes 786440 | tf_op jit(solution)/shard_map/ppermute | solution.py:630
  55.2 7.3 %collective-permute-start.12 = (bf16[512,256]{1,0:T(8,128)(2,1)S(1)}, bf16[512,256]{1,0:T(8,128)(2,1)S(1)}, u32[]{:S(2)}, u32[]{:S(2)}) collective-permute-start(bf16[512,256]{1,0:T(8,128)(2,1)S(1)} %get-tuple-element.79), channel_id=1, source_target_pairs={{0,1},{1,0},{2,3},{3,2},{4,5},{5,4},{6,7},{7,6},{8,9},{9,8},{10,11... | collective-permute-start | bytes 786440 | tf_op jit(solution)/shard_map/ppermute | solution.py:630

commit v17 on v13

--- a/solution.py
+++ b/solution.py
@@ -311,7 +311,6 @@
         far2 = far_forward(
             blocks(two, 0, which2), blocks_t(two_t, 1, which2), q2, (left_bias, right_bias), p2
         )
-        acc0[...] = jnp.zeros_like(acc0)
         g1_t, ec1, f1 = [], [], []
         g2_t, ec2, low2 = [], [], []
         dq0 = []
@@ -330,7 +329,7 @@
             )
             e = [jnp.exp2((x - m0) * TO_LOG2) for x in pieces]
             for n in range(3):
-                p0[n * PARENT : (n + 1) * PARENT, :] = e[n]
+                p0[i % 2, n * PARENT : (n + 1) * PARENT, :] = e[n]
             z0 = jnp.sum(e[0] + e[1] + e[2], axis=0, keepdims=True)
             u0 = dot_nn(raw_t[1, :, rows], jnp.concatenate([x.astype(BF) for x in e], axis=0))
             j, half = i // 2, i % 2
@@ -367,13 +366,17 @@
             low2.append(lower)
             f0 = jnp.exp2(m0 * TO_LOG2 - lg)
             products = dot_nt(raw[1, rows, :], g)
-            weights = p0[...] * f0
+            weights = p0[i % 2] * f0
             eb = weights.astype(BF)
             r = (weights * (products - dr)).astype(BF)
-            acc0[1, rows, :] += dot_nn(eb, g)
-            acc0[0, rows, :] += dot_nn(r, q)
+            for n, x in ((1, dot_nn(eb, g)), (0, dot_nn(r, q))):
+                if i == 0:
+                    acc0[n, rows, :] = x
+                else:
+                    old = slice(i * PARENT, (i + 2) * PARENT)
+                    acc0[n, old, :] += x[: 2 * PARENT]
+                    acc0[n, (i + 2) * PARENT : (i + 3) * PARENT, :] = x[2 * PARENT :]
             dq0.append(dot_nn(raw_t[0, :, rows], r))
-        acc1[...] = jnp.zeros_like(acc1)
         dq1 = []
         for j in range(2):
             pair = slice(2 * j, 2 * j + 2)
@@ -383,8 +386,8 @@
                 jnp.concatenate(f1[pair], axis=1), g1, jnp.concatenate(ec1[pair], axis=1),
             )
             for n, b in enumerate(which1[j]):
-                acc1[0, b * BLOCK : (b + 1) * BLOCK, :] += dk[n]
-                acc1[1, b * BLOCK : (b + 1) * BLOCK, :] += dv[n]
+                acc1[0, b * BLOCK : (b + 1) * BLOCK, :] = dk[n]
+                acc1[1, b * BLOCK : (b + 1) * BLOCK, :] = dv[n]
             dq1.append(dq)
 
         def joined(parts):
@@ -461,7 +464,7 @@
             pltpu.VMEM((2, HEAD, 512), BF),
             pltpu.VMEM((1024, HEAD), BF),
             pltpu.VMEM((1024, HEAD), BF),
-            pltpu.VMEM((768, PARENT), F32),
+            pltpu.VMEM((2, 768, PARENT), F32),
             pltpu.VMEM((2, 384, PARENT), F32),
             pltpu.VMEM((384, PARENT), F32),
             pltpu.VMEM((2, 1536, HEAD), F32),
@@ -551,12 +554,15 @@
     block = (1 - where[0]) * CHUNKS + LATE_CHUNK
     at = pl.ds(pl.multiple_of(block * width, width), width)
     copies = []
-    for m, ref in enumerate((first, second)):
-        for i in range(2):
-            rows = slice(i * PARENT, (i + 1) * PARENT)
-            held[m, rows, :] = dot_nn(order, got[rows, m * width : (m + 1) * width]).astype(BF)
-        copies.append(pltpu.make_async_copy(held.at[m], ref.at[:, at], sems.at[m]))
-        copies[-1].start()
+    for i in range(2):
+        rows = slice(i * PARENT, (i + 1) * PARENT)
+        x = dot_nn(order, got[rows, :]).astype(BF)
+        for m, ref in enumerate((first, second)):
+            held[m, rows, :] = x[:, m * width : (m + 1) * width]
+            copies.append(
+                pltpu.make_async_copy(held.at[m, rows, :], ref.at[rows, at], sems.at[2 * i + m])
+            )
+            copies[-1].start()
     for copy in copies:
         copy.wait()
 
@@ -572,7 +578,7 @@
         input_output_aliases={2: 0, 3: 1},
         scratch_shapes=[
             pltpu.VMEM((2, got.shape[0], got.shape[1] // 2), BF),
-            pltpu.SemaphoreType.DMA((2,)),
+            pltpu.SemaphoreType.DMA((4,)),
         ],
         compiler_params=small(),
         cost_estimate=light(),

time: 61.2 us -> 61.2 us (level)
  no operation moved by 1% of the time
where the time goes in v17:
time: 61.2 us; the launch traced here: 60.6 us
  Pallas kernels  23.8 us (39%)
  starting transfers between devices  21.3 us (35%)
  waiting for transfers between devices  13.3 us (22%)
  local copies, waits for them, and re-layouts  1.16 us (2%)
  between operations  1.02 us (2%)
    pallas_call x2, Pallas kernels, main(): pl.pallas_call(functools.partial(main_kernel, qg_first), in_specs=[smem()...  11.9 us
    ppermute x8, starting transfers between devices, swap(): return lax.ppermute(x, axes, across)  10.3 us
    ppermute x4, starting transfers between devices, beside(): return (near, lax.ppermute(wide, axes, wide_edges))  10.1 us
    ppermute x8, waiting for transfers between devices, swap(): return lax.ppermute(x, axes, across)  9.62 us
    ppermute x4, waiting for transfers between devices, beside(): return (near, lax.ppermute(wide, axes, wide_edges))  3.7 us
    pallas_call x2, Pallas kernels, pack(): pl.pallas_call(functools.partial(pack_kernel, own), in_specs=[smem()] + [...  2.76 us
    pallas_call x1, Pallas kernels, unpack_columns(): pl.pallas_call(unpack_columns_kernel, in_specs=[smem()] + [vmem()] * (2 *...  2.21 us
    pallas_call x1, Pallas kernels, unpack_rows(): pl.pallas_call(unpack_rows_kernel, in_specs=[smem()] + [vmem()] * (CHUNKS...  2.07 us
  transfers between devices with their start and end apart: 16, of which 6 were waited for; matrix products, arithmetic and copies ran while one was open for 0% of the time, Pallas kernels for 36%

profile of v17, /device:TPU:12, one launch (start us, length us, event | category | flops | bytes accessed | tf_op | source)
XLA Modules:
  0.0 60.6 jit_solution(7230623641039765746)
XLA Ops:
  2.0 1.6 %collective-permute-start = (bf16[512,256]{1,0:T(8,128)(2,1)S(1)}, bf16[512,256]{1,0:T(8,128)(2,1)S(1)}, u32[]{:S(2)}, u32[]{:S(2)}) collective-permute-start(bf16[512,256]{1,0:T(8,128)(2,1)S(1)} %shard_map.76), channel_id=1, source_target_pairs={{0,1},{1,0},{2,3},{3,2},{4,5},{5,4},{6,7},{7,6},{8,9},{9,8},{10,11... | collective-permute-start | bytes 786440 | tf_op jit(solution)/shard_map/ppermute | solution.py:625
  4.8 1.1 %shard_map.77 = (bf16[512,256]{1,0:T(8,128)(2,1)S(1)}, bf16[512,256]{1,0:T(8,128)(2,1)S(1)}) custom-call(s32[4]{0:T(128)S(1)} %pad_add_fusion.where, bf16[512,512]{1,0:T(8,128)(2,1)S(1)} %copy-done, bf16[512,512]{1,0:T(8,128)(2,1)S(1)} %copy-done.1), custom_call_target="tpu_custom_call" | custom-call | flops 1000 | bytes 1000 | tf_op jit(solution)/shard_map/pallas_call | solution.py:86
  5.9 1.4 %collective-permute-start.1 = (bf16[512,256]{1,0:T(8,128)(2,1)S(1)}, bf16[512,256]{1,0:T(8,128)(2,1)S(1)}, u32[]{:S(2)}, u32[]{:S(2)}) collective-permute-start(bf16[512,256]{1,0:T(8,128)(2,1)S(1)} %get-tuple-element.50), channel_id=1, source_target_pairs={{0,1},{1,0},{2,3},{3,2},{4,5},{5,4},{6,7},{7,6},{8,9},{9,8},{10,11... | collective-permute-start | bytes 786440 | tf_op jit(solution)/shard_map/ppermute | solution.py:625
  7.3 1.6 %shard_map.75 = (bf16[512,256]{1,0:T(8,128)(2,1)S(1)}, bf16[512,256]{1,0:T(8,128)(2,1)S(1)}, bf16[512,256]{1,0:T(8,128)(2,1)S(1)}, bf16[512,256]{1,0:T(8,128)(2,1)S(1)}) custom-call(s32[4]{0:T(128)S(1)} %pad_add_fusion.where, bf16[512,512]{1,0:T(8,128)(2,1)S(1)} %copy-done.2, bf16[512,512]{1,0:T(8,128)(2,1)S(1)} %copy-done.3, bf16[512,512]{1,0:T(8,128)(2,1)S(1)} %copy-done, ...), custom_call_target="tpu_custom_call" | custom-call | flops 1000 | bytes 1000 | tf_op jit(solution)/shard_map/pallas_call | solution.py:86
  9.0 2.3 %collective-permute-done.got.kv_got = bf16[512,256]{1,0:T(8,128)(2,1)S(1)} collective-permute-done((bf16[512,256]{1,0:T(8,128)(2,1)S(1)}, bf16[512,256]{1,0:T(8,128)(2,1)S(1)}, u32[]{:S(2)}, u32[]{:S(2)}) %collective-permute-start) | collective-permute-done | bytes 262176 | tf_op jit(solution)/shard_map/ppermute | solution.py:625
  12.0 2.5 %collective-permute-start.3 = (bf16[512,256]{1,0:T(8,128)(2,1)S(1)}, bf16[512,256]{1,0:T(8,128)(2,1)S(1)}, u32[]{:S(2)}, u32[]{:S(2)}) collective-permute-start(bf16[512,256]{1,0:T(8,128)(2,1)S(1)} %get-tuple-element.52), channel_id=1, source_target_pairs={{2,4},{3,5},{4,2},{5,3},{6,8},{7,9},{8,6},{9,7},{10,12},{11,13},{1... | collective-permute-start | bytes 786440 | tf_op jit(solution)/shard_map/ppermute | solution.py:629
  14.6 2.3 %collective-permute-done.4.got.kv_got = bf16[512,256]{1,0:T(8,128)(2,1)S(1)} collective-permute-done((bf16[512,256]{1,0:T(8,128)(2,1)S(1)}, bf16[512,256]{1,0:T(8,128)(2,1)S(1)}, u32[]{:S(2)}, u32[]{:S(2)}) %collective-permute-start.4) | collective-permute-done | bytes 262176 | tf_op jit(solution)/shard_map/ppermute | solution.py:625
  17.7 2.5 %collective-permute-start.6 = (bf16[512,256]{1,0:T(8,128)(2,1)S(1)}, bf16[512,256]{1,0:T(8,128)(2,1)S(1)}, u32[]{:S(2)}, u32[]{:S(2)}) collective-permute-start(bf16[512,256]{1,0:T(8,128)(2,1)S(1)} %get-tuple-element.61), channel_id=1, source_target_pairs={{2,4},{3,5},{4,2},{5,3},{6,8},{7,9},{8,6},{9,7},{10,12},{11,13},{1... | collective-permute-start | bytes 786440 | tf_op jit(solution)/shard_map/ppermute | solution.py:629
  20.2 1.2 %collective-permute-done.1.refs_1_ = bf16[512,256]{1,0:T(8,128)(2,1)S(1)} collective-permute-done((bf16[512,256]{1,0:T(8,128)(2,1)S(1)}, bf16[512,256]{1,0:T(8,128)(2,1)S(1)}, u32[]{:S(2)}, u32[]{:S(2)}) %collective-permute-start.1) | collective-permute-done | bytes 262176 | tf_op jit(solution)/shard_map/ppermute | solution.py:625
  21.4 1.5 %collective-permute-start.7 = (bf16[512,256]{1,0:T(8,128)(2,1)S(1)}, bf16[512,256]{1,0:T(8,128)(2,1)S(1)}, u32[]{:S(2)}, u32[]{:S(2)}) collective-permute-start(bf16[512,256]{1,0:T(8,128)(2,1)S(1)} %get-tuple-element.63), channel_id=1, source_target_pairs={{0,1},{1,0},{2,3},{3,2},{4,5},{5,4},{6,7},{7,6},{8,9},{9,8},{10,11... | collective-permute-start | bytes 786440 | tf_op jit(solution)/shard_map/ppermute | solution.py:625
  22.9 6.0 %shard_map.79 = (bf16[2,2,128,256]{3,2,1,0:T(8,128)(2,1)S(1)}, bf16[2,2,128,256]{3,2,1,0:T(8,128)(2,1)S(1)}, f32[1024,256]{1,0:T(8,128)S(1)}, bf16[512,256]{1,0:T(8,128)(2,1)S(1)}, bf16[512,256]{1,0:T(8,128)(2,1)S(1)}) custom-call(s32[4]{0:T(128)S(1)} %pad_add_fusion.where, bf16[512,256]{1,0:T(8,128)(2,1)S(1)} %get-tuple-element.47.own.kv_own, ...), custom_call_target="tpu_custom_call" | custom-call | flops 1000 | bytes 1000 | tf_op jit(solution)/shard_map/pallas_call | solution.py:447
  28.8 1.2 %collective-permute-start.8 = (bf16[2,2,128,256]{3,2,1,0:T(8,128)(2,1)S(1)}, bf16[2,2,128,256]{3,2,1,0:T(8,128)(2,1)S(1)}, u32[]{:S(2)}, u32[]{:S(2)}) collective-permute-start(bf16[2,2,128,256]{3,2,1,0:T(8,128)(2,1)S(1)} %get-tuple-element.65), channel_id=1, source_target_pairs={{0,1},{1,0},{2,3},{3,2},{4,5},{5,4},{6,7},{7,6},{8,9},{9,8},{10,11... | collective-permute-start | bytes 786440 | tf_op jit(solution)/shard_map/ppermute | solution.py:625
  30.1 2.4 %collective-permute-start.14 = (bf16[512,256]{1,0:T(8,128)(2,1)S(1)}, bf16[512,256]{1,0:T(8,128)(2,1)S(1)}, u32[]{:S(2)}, u32[]{:S(2)}) collective-permute-start(bf16[512,256]{1,0:T(8,128)(2,1)S(1)} %get-tuple-element.82), channel_id=1, source_target_pairs={{2,4},{3,5},{4,2},{5,3},{6,8},{7,9},{8,6},{9,7},{10,12},{11,13},{1... | collective-permute-start | bytes 786440 | tf_op jit(solution)/shard_map/ppermute | solution.py:629
  32.5 6.0 %shard_map.82 = (bf16[2,2,128,256]{3,2,1,0:T(8,128)(2,1)S(1)}, bf16[2,2,128,256]{3,2,1,0:T(8,128)(2,1)S(1)}, f32[1024,256]{1,0:T(8,128)S(1)}, bf16[512,256]{1,0:T(8,128)(2,1)S(1)}, bf16[512,256]{1,0:T(8,128)(2,1)S(1)}) custom-call(s32[4]{0:T(128)S(1)} %pad_add_fusion.where, bf16[512,256]{1,0:T(8,128)(2,1)S(1)} %get-tuple-element.54.own.kv_own, ...), custom_call_target="tpu_custom_call" | custom-call | flops 1000 | bytes 1000 | tf_op jit(solution)/shard_map/pallas_call | solution.py:447
  38.5 1.2 %collective-permute-start.9 = (bf16[2,2,128,256]{3,2,1,0:T(8,128)(2,1)S(1)}, bf16[2,2,128,256]{3,2,1,0:T(8,128)(2,1)S(1)}, u32[]{:S(2)}, u32[]{:S(2)}) collective-permute-start(bf16[2,2,128,256]{3,2,1,0:T(8,128)(2,1)S(1)} %get-tuple-element.69), channel_id=1, source_target_pairs={{0,1},{1,0},{2,3},{3,2},{4,5},{5,4},{6,7},{7,6},{8,9},{9,8},{10,11... | collective-permute-start | bytes 786440 | tf_op jit(solution)/shard_map/ppermute | solution.py:625
  40.5 2.7 %collective-permute-start.11 = (bf16[512,256]{1,0:T(8,128)(2,1)S(1)}, bf16[512,256]{1,0:T(8,128)(2,1)S(1)}, u32[]{:S(2)}, u32[]{:S(2)}) collective-permute-start(bf16[512,256]{1,0:T(8,128)(2,1)S(1)} %get-tuple-element.72), channel_id=1, source_target_pairs={{2,4},{3,5},{4,2},{5,3},{6,8},{7,9},{8,6},{9,7},{10,12},{11,13},{1... | collective-permute-start | bytes 786440 | tf_op jit(solution)/shard_map/ppermute | solution.py:629
  43.9 1.2 %collective-permute-start.15 = (bf16[512,256]{1,0:T(8,128)(2,1)S(1)}, bf16[512,256]{1,0:T(8,128)(2,1)S(1)}, u32[]{:S(2)}, u32[]{:S(2)}) collective-permute-start(bf16[512,256]{1,0:T(8,128)(2,1)S(1)} %get-tuple-element.85), channel_id=1, source_target_pairs={{0,1},{1,0},{2,3},{3,2},{4,5},{5,4},{6,7},{7,6},{8,9},{9,8},{10,11... | collective-permute-start | bytes 786440 | tf_op jit(solution)/shard_map/ppermute | solution.py:625
  45.1 2.2 %collective-permute-done.9.refs_3_ = bf16[2,2,128,256]{3,2,1,0:T(8,128)(2,1)S(1)} collective-permute-done((bf16[2,2,128,256]{3,2,1,0:T(8,128)(2,1)S(1)}, bf16[2,2,128,256]{3,2,1,0:T(8,128)(2,1)S(1)}, u32[]{:S(2)}, u32[]{:S(2)}) %collective-permute-start.9) | collective-permute-done | bytes 262176 | tf_op jit(solution)/shard_map/ppermute | solution.py:625
  47.2 3.7 %collective-permute-done.11.wide_got = bf16[512,256]{1,0:T(8,128)(2,1)S(1)} collective-permute-done((bf16[512,256]{1,0:T(8,128)(2,1)S(1)}, bf16[512,256]{1,0:T(8,128)(2,1)S(1)}, u32[]{:S(2)}, u32[]{:S(2)}) %collective-permute-start.11) | collective-permute-done | bytes 262176 | tf_op jit(solution)/shard_map/ppermute | solution.py:629
  51.6 1.4 %collective-permute-start.12 = (bf16[512,256]{1,0:T(8,128)(2,1)S(1)}, bf16[512,256]{1,0:T(8,128)(2,1)S(1)}, u32[]{:S(2)}, u32[]{:S(2)}) collective-permute-start(bf16[512,256]{1,0:T(8,128)(2,1)S(1)} %get-tuple-element.79), channel_id=1, source_target_pairs={{0,1},{1,0},{2,3},{3,2},{4,5},{5,4},{6,7},{7,6},{8,9},{9,8},{10,11... | collective-permute-start | bytes 786440 | tf_op jit(solution)/shard_map/ppermute | solution.py:625
  53.1 2.2 %shard_map.83 = (bf16[512,512]{1,0:T(8,128)(2,1)}, bf16[512,512]{1,0:T(8,128)(2,1)}) custom-call(s32[4]{0:T(128)S(1)} %pad_add_fusion.where, bf16[2,2,128,256]{3,2,1,0:T(8,128)(2,1)S(1)} %get-tuple-element.53.refs_0_, bf16[2,2,128,256]{3,2,1,0:T(8,128)(2,1)S(1)} %get-tuple-element.64.refs_1_, bf16[2,2,128,256]{3,2,1,0:T(8,128)(2,1)S(1)} %collective-permute-done.8.refs_2_, ...), custom_call_target="tpu_custom_call" | custom-call | flops 1000 | bytes 1000 | tf_op jit(solution)/shard_map/pallas_call | solution.py:603
  55.3 2.1 %shard_map.86 = (bf16[512,512]{1,0:T(8,128)(2,1)}, bf16[512,512]{1,0:T(8,128)(2,1)}) custom-call(s32[4]{0:T(128)S(1)} %pad_add_fusion.where, bf16[512,256]{1,0:T(8,128)(2,1)S(1)} %get-tuple-element.83.refs_0_, bf16[512,256]{1,0:T(8,128)(2,1)S(1)} %get-tuple-element.84.refs_1_, bf16[512,256]{1,0:T(8,128)(2,1)S(1)} %collective-permute-done.15.refs_2_), custom_call_target="tpu_custom_call" | custom-call | flops 1000 | bytes 1000 | tf_op jit(solution)/shard_map/pallas_call | solution.py:540
  57.4 1.6 %collective-permute-done.12.got = bf16[512,256]{1,0:T(8,128)(2,1)S(1)} collective-permute-done((bf16[512,256]{1,0:T(8,128)(2,1)S(1)}, bf16[512,256]{1,0:T(8,128)(2,1)S(1)}, u32[]{:S(2)}, u32[]{:S(2)}) %collective-permute-start.12) | collective-permute-done | bytes 262176 | tf_op jit(solution)/shard_map/ppermute | solution.py:625
  59.0 1.5 %shard_map.87 = (bf16[512,512]{1,0:T(8,128)(2,1)}, bf16[512,512]{1,0:T(8,128)(2,1)}) custom-call(s32[4]{0:T(128)S(1)} %pad_add_fusion.where, bf16[512,256]{1,0:T(8,128)(2,1)S(1)} %collective-permute-done.12.got, bf16[512,512]{1,0:T(8,128)(2,1)} %get-tuple-element.86.first_in, ...), custom_call_target="tpu_custom_call", output_to_operand_aliasing={{0}: (2, {}), {1}: (3, {})} | custom-call | flops 1000 | bytes 1000 | tf_op jit(solution)/shard_map/pallas_call | solution.py:573
  (33 shorter events, 6.1 us)
Async XLA Ops:
  0.7 2.9 %copy-start.2 = (bf16[512,512]{1,0:T(8,128)(2,1)S(1)}, bf16[512,512]{1,0:T(8,128)(2,1)}, u32[]{:S(2)}) copy-start(bf16[512,512]{1,0:T(8,128)(2,1)} %refs_0_.2) | copy-start | bytes 1572868
  1.7 1.9 %copy-start.3 = (bf16[512,512]{1,0:T(8,128)(2,1)S(1)}, bf16[512,512]{1,0:T(8,128)(2,1)}, u32[]{:S(2)}) copy-start(bf16[512,512]{1,0:T(8,128)(2,1)} %refs_1_.2) | copy-start | bytes 1572868
  2.0 9.3 %collective-permute-start = (bf16[512,256]{1,0:T(8,128)(2,1)S(1)}, bf16[512,256]{1,0:T(8,128)(2,1)S(1)}, u32[]{:S(2)}, u32[]{:S(2)}) collective-permute-start(bf16[512,256]{1,0:T(8,128)(2,1)S(1)} %shard_map.76), channel_id=1, source_target_pairs={{0,1},{1,0},{2,3},{3,2},{4,5},{5,4},{6,7},{7,6},{8,9},{9,8},{10,11... | collective-permute-start | bytes 786440 | tf_op jit(solution)/shard_map/ppermute | solution.py:625
  3.6 1.2 %copy-start = (bf16[512,512]{1,0:T(8,128)(2,1)S(1)}, bf16[512,512]{1,0:T(8,128)(2,1)}, u32[]{:S(2)}) copy-start(bf16[512,512]{1,0:T(8,128)(2,1)} %refs_0_.3) | copy-start | bytes 1572868
  3.6 1.2 %copy-start.1 = (bf16[512,512]{1,0:T(8,128)(2,1)S(1)}, bf16[512,512]{1,0:T(8,128)(2,1)}, u32[]{:S(2)}) copy-start(bf16[512,512]{1,0:T(8,128)(2,1)} %refs_1_.3) | copy-start | bytes 1572868
  3.9 13.0 %collective-permute-start.4 = (bf16[512,256]{1,0:T(8,128)(2,1)S(1)}, bf16[512,256]{1,0:T(8,128)(2,1)S(1)}, u32[]{:S(2)}, u32[]{:S(2)}) collective-permute-start(bf16[512,256]{1,0:T(8,128)(2,1)S(1)} %shard_map.80), channel_id=1, source_target_pairs={{0,1},{1,0},{2,3},{3,2},{4,5},{5,4},{6,7},{7,6},{8,9},{9,8},{10,11... | collective-permute-start | bytes 786440 | tf_op jit(solution)/shard_map/ppermute | solution.py:625
  5.9 15.4 %collective-permute-start.1 = (bf16[512,256]{1,0:T(8,128)(2,1)S(1)}, bf16[512,256]{1,0:T(8,128)(2,1)S(1)}, u32[]{:S(2)}, u32[]{:S(2)}) collective-permute-start(bf16[512,256]{1,0:T(8,128)(2,1)S(1)} %get-tuple-element.50), channel_id=1, source_target_pairs={{0,1},{1,0},{2,3},{3,2},{4,5},{5,4},{6,7},{7,6},{8,9},{9,8},{10,11... | collective-permute-start | bytes 786440 | tf_op jit(solution)/shard_map/ppermute | solution.py:625
  12.0 10.9 %collective-permute-start.2 = (bf16[512,256]{1,0:T(8,128)(2,1)S(1)}, bf16[512,256]{1,0:T(8,128)(2,1)S(1)}, u32[]{:S(2)}, u32[]{:S(2)}) collective-permute-start(bf16[512,256]{1,0:T(8,128)(2,1)S(1)} %get-tuple-element.51), channel_id=1, source_target_pairs={{0,2},{1,3},{2,0},{3,1},{4,6},{5,7},{6,4},{7,5},{8,10},{9,11},{10,... | collective-permute-start | bytes 786440 | tf_op jit(solution)/shard_map/ppermute | solution.py:628
  12.0 10.8 %collective-permute-start.3 = (bf16[512,256]{1,0:T(8,128)(2,1)S(1)}, bf16[512,256]{1,0:T(8,128)(2,1)S(1)}, u32[]{:S(2)}, u32[]{:S(2)}) collective-permute-start(bf16[512,256]{1,0:T(8,128)(2,1)S(1)} %get-tuple-element.52), channel_id=1, source_target_pairs={{2,4},{3,5},{4,2},{5,3},{6,8},{7,9},{8,6},{9,7},{10,12},{11,13},{1... | collective-permute-start | bytes 786440 | tf_op jit(solution)/shard_map/ppermute | solution.py:629
  17.6 12.5 %collective-permute-start.5 = (bf16[512,256]{1,0:T(8,128)(2,1)S(1)}, bf16[512,256]{1,0:T(8,128)(2,1)S(1)}, u32[]{:S(2)}, u32[]{:S(2)}) collective-permute-start(bf16[512,256]{1,0:T(8,128)(2,1)S(1)} %get-tuple-element.60), channel_id=1, source_target_pairs={{0,2},{1,3},{2,0},{3,1},{4,6},{5,7},{6,4},{7,5},{8,10},{9,11},{10,... | collective-permute-start | bytes 786440 | tf_op jit(solution)/shard_map/ppermute | solution.py:628
  17.7 14.8 %collective-permute-start.6 = (bf16[512,256]{1,0:T(8,128)(2,1)S(1)}, bf16[512,256]{1,0:T(8,128)(2,1)S(1)}, u32[]{:S(2)}, u32[]{:S(2)}) collective-permute-start(bf16[512,256]{1,0:T(8,128)(2,1)S(1)} %get-tuple-element.61), channel_id=1, source_target_pairs={{2,4},{3,5},{4,2},{5,3},{6,8},{7,9},{8,6},{9,7},{10,12},{11,13},{1... | collective-permute-start | bytes 786440 | tf_op jit(solution)/shard_map/ppermute | solution.py:629
  21.4 11.1 %collective-permute-start.7 = (bf16[512,256]{1,0:T(8,128)(2,1)S(1)}, bf16[512,256]{1,0:T(8,128)(2,1)S(1)}, u32[]{:S(2)}, u32[]{:S(2)}) collective-permute-start(bf16[512,256]{1,0:T(8,128)(2,1)S(1)} %get-tuple-element.63), channel_id=1, source_target_pairs={{0,1},{1,0},{2,3},{3,2},{4,5},{5,4},{6,7},{7,6},{8,9},{9,8},{10,11... | collective-permute-start | bytes 786440 | tf_op jit(solution)/shard_map/ppermute | solution.py:625
  28.8 10.9 %collective-permute-start.8 = (bf16[2,2,128,256]{3,2,1,0:T(8,128)(2,1)S(1)}, bf16[2,2,128,256]{3,2,1,0:T(8,128)(2,1)S(1)}, u32[]{:S(2)}, u32[]{:S(2)}) collective-permute-start(bf16[2,2,128,256]{3,2,1,0:T(8,128)(2,1)S(1)} %get-tuple-element.65), channel_id=1, source_target_pairs={{0,1},{1,0},{2,3},{3,2},{4,5},{5,4},{6,7},{7,6},{8,9},{9,8},{10,11... | collective-permute-start | bytes 786440 | tf_op jit(solution)/shard_map/ppermute | solution.py:625
  30.1 13.1 %collective-permute-start.13 = (bf16[512,256]{1,0:T(8,128)(2,1)S(1)}, bf16[512,256]{1,0:T(8,128)(2,1)S(1)}, u32[]{:S(2)}, u32[]{:S(2)}) collective-permute-start(bf16[512,256]{1,0:T(8,128)(2,1)S(1)} %get-tuple-element.81), channel_id=1, source_target_pairs={{0,2},{1,3},{2,0},{3,1},{4,6},{5,7},{6,4},{7,5},{8,10},{9,11},{10,... | collective-permute-start | bytes 786440 | tf_op jit(solution)/shard_map/ppermute | solution.py:628
  30.1 13.1 %collective-permute-start.14 = (bf16[512,256]{1,0:T(8,128)(2,1)S(1)}, bf16[512,256]{1,0:T(8,128)(2,1)S(1)}, u32[]{:S(2)}, u32[]{:S(2)}) collective-permute-start(bf16[512,256]{1,0:T(8,128)(2,1)S(1)} %get-tuple-element.82), channel_id=1, source_target_pairs={{2,4},{3,5},{4,2},{5,3},{6,8},{7,9},{8,6},{9,7},{10,12},{11,13},{1... | collective-permute-start | bytes 786440 | tf_op jit(solution)/shard_map/ppermute | solution.py:629
  38.5 8.8 %collective-permute-start.9 = (bf16[2,2,128,256]{3,2,1,0:T(8,128)(2,1)S(1)}, bf16[2,2,128,256]{3,2,1,0:T(8,128)(2,1)S(1)}, u32[]{:S(2)}, u32[]{:S(2)}) collective-permute-start(bf16[2,2,128,256]{3,2,1,0:T(8,128)(2,1)S(1)} %get-tuple-element.69), channel_id=1, source_target_pairs={{0,1},{1,0},{2,3},{3,2},{4,5},{5,4},{6,7},{7,6},{8,9},{9,8},{10,11... | collective-permute-start | bytes 786440 | tf_op jit(solution)/shard_map/ppermute | solution.py:625
  39.7 7.5 %collective-permute-start.10 = (bf16[512,256]{1,0:T(8,128)(2,1)S(1)}, bf16[512,256]{1,0:T(8,128)(2,1)S(1)}, u32[]{:S(2)}, u32[]{:S(2)}) collective-permute-start(bf16[512,256]{1,0:T(8,128)(2,1)S(1)} %get-tuple-element.71), channel_id=1, source_target_pairs={{0,2},{1,3},{2,0},{3,1},{4,6},{5,7},{6,4},{7,5},{8,10},{9,11},{10,... | collective-permute-start | bytes 786440 | tf_op jit(solution)/shard_map/ppermute | solution.py:628
  40.5 10.5 %collective-permute-start.11 = (bf16[512,256]{1,0:T(8,128)(2,1)S(1)}, bf16[512,256]{1,0:T(8,128)(2,1)S(1)}, u32[]{:S(2)}, u32[]{:S(2)}) collective-permute-start(bf16[512,256]{1,0:T(8,128)(2,1)S(1)} %get-tuple-element.72), channel_id=1, source_target_pairs={{2,4},{3,5},{4,2},{5,3},{6,8},{7,9},{8,6},{9,7},{10,12},{11,13},{1... | collective-permute-start | bytes 786440 | tf_op jit(solution)/shard_map/ppermute | solution.py:629
  43.9 11.4 %collective-permute-start.15 = (bf16[512,256]{1,0:T(8,128)(2,1)S(1)}, bf16[512,256]{1,0:T(8,128)(2,1)S(1)}, u32[]{:S(2)}, u32[]{:S(2)}) collective-permute-start(bf16[512,256]{1,0:T(8,128)(2,1)S(1)} %get-tuple-element.85), channel_id=1, source_target_pairs={{0,1},{1,0},{2,3},{3,2},{4,5},{5,4},{6,7},{7,6},{8,9},{9,8},{10,11... | collective-permute-start | bytes 786440 | tf_op jit(solution)/shard_map/ppermute | solution.py:625
  51.6 7.3 %collective-permute-start.12 = (bf16[512,256]{1,0:T(8,128)(2,1)S(1)}, bf16[512,256]{1,0:T(8,128)(2,1)S(1)}, u32[]{:S(2)}, u32[]{:S(2)}) collective-permute-start(bf16[512,256]{1,0:T(8,128)(2,1)S(1)} %get-tuple-element.79), channel_id=1, source_target_pairs={{0,1},{1,0},{2,3},{3,2},{4,5},{5,4},{6,7},{7,6},{8,9},{9,8},{10,11... | collective-permute-start | bytes 786440 | tf_op jit(solution)/shard_map/ppermute | solution.py:625

commit v18 on v17

--- a/solution.py
+++ b/solution.py
@@ -647,9 +647,10 @@
         oq_own.append(own)
         oq_got.append(swap(far))
         if c > 0:
-            oq_got[c - 1], near, wide = lax.optimization_barrier((oq_got[c - 1], near, wide))
+            back[c - 1], near, wide = lax.optimization_barrier((back[c - 1], near, wide))
         back.append([grad, *beside(near, wide)])
-    oq_got[-1], back[-1] = lax.optimization_barrier((oq_got[-1], back[-1]))
+    for c in range(CHUNKS):
+        oq_got[c], back[c] = lax.optimization_barrier((oq_got[c], back[c]))
     kv_own, kv_got = [], []
     for c in range(CHUNKS):
         own, far = join(where, *back[c])

time: 61.2 us -> 61.2 us (level)
    ppermute x8, waiting for transfers between devices: 9.62 us -> 10.5 us  [swap(): return lax.ppermute(x, axes, across)]
    ppermute x4, waiting for transfers between devices: 3.7 us -> 3.04 us  [beside(): return (near, lax.ppermute(wide, axes, wide_edges))]
where the time goes in v18:
time: 61.2 us; the launch traced here: 61 us
  Pallas kernels  23.8 us (39%)
  starting transfers between devices  21.4 us (35%)
  waiting for transfers between devices  13.5 us (22%)
  local copies, waits for them, and re-layouts  1.16 us (2%)
  between operations  1.02 us (2%)
    pallas_call x2, Pallas kernels, main(): pl.pallas_call(functools.partial(main_kernel, qg_first), in_specs=[smem()...  11.9 us
    ppermute x4, starting transfers between devices, beside(): return (near, lax.ppermute(wide, axes, wide_edges))  10.5 us
    ppermute x8, waiting for transfers between devices, swap(): return lax.ppermute(x, axes, across)  10.5 us
    ppermute x8, starting transfers between devices, swap(): return lax.ppermute(x, axes, across)  10.1 us
    ppermute x4, waiting for transfers between devices, beside(): return (near, lax.ppermute(wide, axes, wide_edges))  3.04 us
    pallas_call x2, Pallas kernels, pack(): pl.pallas_call(functools.partial(pack_kernel, own), in_specs=[smem()] + [...  2.76 us
    pallas_call x1, Pallas kernels, unpack_columns(): pl.pallas_call(unpack_columns_kernel, in_specs=[smem()] + [vmem()] * (2 *...  2.21 us
    pallas_call x1, Pallas kernels, unpack_rows(): pl.pallas_call(unpack_rows_kernel, in_specs=[smem()] + [vmem()] * (CHUNKS...  2.07 us
  transfers between devices with their start and end apart: 16, of which 6 were waited for; matrix products, arithmetic and copies ran while one was open for 0% of the time, Pallas kernels for 36%

profile of v18, /device:TPU:12, one launch (start us, length us, event | category | flops | bytes accessed | tf_op | source)
XLA Modules:
  0.0 61.0 jit_solution(2216393250285530389)
XLA Ops:
  0.7 1.1 %constant_dynamic-slice_fusion.2 = (bf16[512,128]{1,0:T(8,128)(2,1)S(1)}, bf16[512,128]{1,0:T(8,128)(2,1)S(1)}) fusion(bf16[512,512]{1,0:T(8,128)(2,1)} %refs_1_.2, s32[]{:T(128)S(6)} %select_n.30, bf16[512,512]{1,0:T(8,128)(2,1)} %refs_0_.2), kind=kLoop, calls=%fused_computation.2 | loop fusion | bytes 524292 | tf_op jit(solution)/shard_map/dynamic_slice | solution.py:112
  2.0 1.6 %collective-permute-start = (bf16[512,256]{1,0:T(8,128)(2,1)S(1)}, bf16[512,256]{1,0:T(8,128)(2,1)S(1)}, u32[]{:S(2)}, u32[]{:S(2)}) collective-permute-start(bf16[512,256]{1,0:T(8,128)(2,1)S(1)} %shard_map.76), channel_id=1, source_target_pairs={{0,1},{1,0},{2,3},{3,2},{4,5},{5,4},{6,7},{7,6},{8,9},{9,8},{10,11... | collective-permute-start | bytes 786440 | tf_op jit(solution)/shard_map/ppermute | solution.py:625
  4.8 1.1 %shard_map.77 = (bf16[512,256]{1,0:T(8,128)(2,1)S(1)}, bf16[512,256]{1,0:T(8,128)(2,1)S(1)}) custom-call(s32[4]{0:T(128)S(1)} %pad_add_fusion.where, bf16[512,512]{1,0:T(8,128)(2,1)S(1)} %copy-done, bf16[512,512]{1,0:T(8,128)(2,1)S(1)} %copy-done.1), custom_call_target="tpu_custom_call" | custom-call | flops 1000 | bytes 1000 | tf_op jit(solution)/shard_map/pallas_call | solution.py:86
  5.9 1.4 %collective-permute-start.1 = (bf16[512,256]{1,0:T(8,128)(2,1)S(1)}, bf16[512,256]{1,0:T(8,128)(2,1)S(1)}, u32[]{:S(2)}, u32[]{:S(2)}) collective-permute-start(bf16[512,256]{1,0:T(8,128)(2,1)S(1)} %get-tuple-element.56), channel_id=1, source_target_pairs={{0,1},{1,0},{2,3},{3,2},{4,5},{5,4},{6,7},{7,6},{8,9},{9,8},{10,11... | collective-permute-start | bytes 786440 | tf_op jit(solution)/shard_map/ppermute | solution.py:625
  7.3 1.6 %shard_map.75 = (bf16[512,256]{1,0:T(8,128)(2,1)S(1)}, bf16[512,256]{1,0:T(8,128)(2,1)S(1)}, bf16[512,256]{1,0:T(8,128)(2,1)S(1)}, bf16[512,256]{1,0:T(8,128)(2,1)S(1)}) custom-call(s32[4]{0:T(128)S(1)} %pad_add_fusion.where, bf16[512,512]{1,0:T(8,128)(2,1)S(1)} %copy-done.2, bf16[512,512]{1,0:T(8,128)(2,1)S(1)} %copy-done.3, bf16[512,512]{1,0:T(8,128)(2,1)S(1)} %copy-done, ...), custom_call_target="tpu_custom_call" | custom-call | flops 1000 | bytes 1000 | tf_op jit(solution)/shard_map/pallas_call | solution.py:86
  9.0 2.3 %collective-permute-done.got.kv_got = bf16[512,256]{1,0:T(8,128)(2,1)S(1)} collective-permute-done((bf16[512,256]{1,0:T(8,128)(2,1)S(1)}, bf16[512,256]{1,0:T(8,128)(2,1)S(1)}, u32[]{:S(2)}, u32[]{:S(2)}) %collective-permute-start) | collective-permute-done | bytes 262176 | tf_op jit(solution)/shard_map/ppermute | solution.py:625
  12.0 2.5 %collective-permute-start.3 = (bf16[512,256]{1,0:T(8,128)(2,1)S(1)}, bf16[512,256]{1,0:T(8,128)(2,1)S(1)}, u32[]{:S(2)}, u32[]{:S(2)}) collective-permute-start(bf16[512,256]{1,0:T(8,128)(2,1)S(1)} %get-tuple-element.58), channel_id=1, source_target_pairs={{2,4},{3,5},{4,2},{5,3},{6,8},{7,9},{8,6},{9,7},{10,12},{11,13},{1... | collective-permute-start | bytes 786440 | tf_op jit(solution)/shard_map/ppermute | solution.py:629
  14.6 2.3 %collective-permute-done.4.got.kv_got = bf16[512,256]{1,0:T(8,128)(2,1)S(1)} collective-permute-done((bf16[512,256]{1,0:T(8,128)(2,1)S(1)}, bf16[512,256]{1,0:T(8,128)(2,1)S(1)}, u32[]{:S(2)}, u32[]{:S(2)}) %collective-permute-start.4) | collective-permute-done | bytes 262176 | tf_op jit(solution)/shard_map/ppermute | solution.py:625
  17.7 2.5 %collective-permute-start.6 = (bf16[512,256]{1,0:T(8,128)(2,1)S(1)}, bf16[512,256]{1,0:T(8,128)(2,1)S(1)}, u32[]{:S(2)}, u32[]{:S(2)}) collective-permute-start(bf16[512,256]{1,0:T(8,128)(2,1)S(1)} %get-tuple-element.67), channel_id=1, source_target_pairs={{2,4},{3,5},{4,2},{5,3},{6,8},{7,9},{8,6},{9,7},{10,12},{11,13},{1... | collective-permute-start | bytes 786440 | tf_op jit(solution)/shard_map/ppermute | solution.py:629
  20.2 1.2 %collective-permute-done.1.refs_1_ = bf16[512,256]{1,0:T(8,128)(2,1)S(1)} collective-permute-done((bf16[512,256]{1,0:T(8,128)(2,1)S(1)}, bf16[512,256]{1,0:T(8,128)(2,1)S(1)}, u32[]{:S(2)}, u32[]{:S(2)}) %collective-permute-start.1) | collective-permute-done | bytes 262176 | tf_op jit(solution)/shard_map/ppermute | solution.py:625
  21.4 1.5 %collective-permute-start.7 = (bf16[512,256]{1,0:T(8,128)(2,1)S(1)}, bf16[512,256]{1,0:T(8,128)(2,1)S(1)}, u32[]{:S(2)}, u32[]{:S(2)}) collective-permute-start(bf16[512,256]{1,0:T(8,128)(2,1)S(1)} %get-tuple-element.69), channel_id=1, source_target_pairs={{0,1},{1,0},{2,3},{3,2},{4,5},{5,4},{6,7},{7,6},{8,9},{9,8},{10,11... | collective-permute-start | bytes 786440 | tf_op jit(solution)/shard_map/ppermute | solution.py:625
  22.9 6.0 %shard_map.79 = (bf16[2,2,128,256]{3,2,1,0:T(8,128)(2,1)S(1)}, bf16[2,2,128,256]{3,2,1,0:T(8,128)(2,1)S(1)}, f32[1024,256]{1,0:T(8,128)S(1)}, bf16[512,256]{1,0:T(8,128)(2,1)S(1)}, bf16[512,256]{1,0:T(8,128)(2,1)S(1)}) custom-call(s32[4]{0:T(128)S(1)} %pad_add_fusion.where, bf16[512,256]{1,0:T(8,128)(2,1)S(1)} %get-tuple-element.53.own.kv_own, ...), custom_call_target="tpu_custom_call" | custom-call | flops 1000 | bytes 1000 | tf_op jit(solution)/shard_map/pallas_call | solution.py:447
  28.9 2.7 %collective-permute-start.10 = (bf16[512,256]{1,0:T(8,128)(2,1)S(1)}, bf16[512,256]{1,0:T(8,128)(2,1)S(1)}, u32[]{:S(2)}, u32[]{:S(2)}) collective-permute-start(bf16[512,256]{1,0:T(8,128)(2,1)S(1)} %get-tuple-element.74), channel_id=1, source_target_pairs={{2,4},{3,5},{4,2},{5,3},{6,8},{7,9},{8,6},{9,7},{10,12},{11,13},{1... | collective-permute-start | bytes 786440 | tf_op jit(solution)/shard_map/ppermute | solution.py:629
  31.6 1.2 %collective-permute-start.8 = (bf16[2,2,128,256]{3,2,1,0:T(8,128)(2,1)S(1)}, bf16[2,2,128,256]{3,2,1,0:T(8,128)(2,1)S(1)}, u32[]{:S(2)}, u32[]{:S(2)}) collective-permute-start(bf16[2,2,128,256]{3,2,1,0:T(8,128)(2,1)S(1)} %get-tuple-element.71), channel_id=1, source_target_pairs={{0,1},{1,0},{2,3},{3,2},{4,5},{5,4},{6,7},{7,6},{8,9},{9,8},{10,11... | collective-permute-start | bytes 786440 | tf_op jit(solution)/shard_map/ppermute | solution.py:625
  32.9 6.0 %shard_map.82 = (bf16[2,2,128,256]{3,2,1,0:T(8,128)(2,1)S(1)}, bf16[2,2,128,256]{3,2,1,0:T(8,128)(2,1)S(1)}, f32[1024,256]{1,0:T(8,128)S(1)}, bf16[512,256]{1,0:T(8,128)(2,1)S(1)}, bf16[512,256]{1,0:T(8,128)(2,1)S(1)}) custom-call(s32[4]{0:T(128)S(1)} %pad_add_fusion.where, bf16[512,256]{1,0:T(8,128)(2,1)S(1)} %get-tuple-element.60.own.kv_own, ...), custom_call_target="tpu_custom_call" | custom-call | flops 1000 | bytes 1000 | tf_op jit(solution)/shard_map/pallas_call | solution.py:447
  40.4 2.8 %collective-permute-start.13 = (bf16[512,256]{1,0:T(8,128)(2,1)S(1)}, bf16[512,256]{1,0:T(8,128)(2,1)S(1)}, u32[]{:S(2)}, u32[]{:S(2)}) collective-permute-start(bf16[512,256]{1,0:T(8,128)(2,1)S(1)} %get-tuple-element.84), channel_id=1, source_target_pairs={{2,4},{3,5},{4,2},{5,3},{6,8},{7,9},{8,6},{9,7},{10,12},{11,13},{1... | collective-permute-start | bytes 786440 | tf_op jit(solution)/shard_map/ppermute | solution.py:629
  43.9 1.2 %collective-permute-start.15 = (bf16[512,256]{1,0:T(8,128)(2,1)S(1)}, bf16[512,256]{1,0:T(8,128)(2,1)S(1)}, u32[]{:S(2)}, u32[]{:S(2)}) collective-permute-start(bf16[512,256]{1,0:T(8,128)(2,1)S(1)} %get-tuple-element.97), channel_id=1, source_target_pairs={{0,1},{1,0},{2,3},{3,2},{4,5},{5,4},{6,7},{7,6},{8,9},{9,8},{10,11... | collective-permute-start | bytes 786440 | tf_op jit(solution)/shard_map/ppermute | solution.py:625
  45.1 2.7 %collective-permute-done.11.refs_3_ = bf16[2,2,128,256]{3,2,1,0:T(8,128)(2,1)S(1)} collective-permute-done((bf16[2,2,128,256]{3,2,1,0:T(8,128)(2,1)S(1)}, bf16[2,2,128,256]{3,2,1,0:T(8,128)(2,1)S(1)}, u32[]{:S(2)}, u32[]{:S(2)}) %collective-permute-start.11) | collective-permute-done | bytes 262176 | tf_op jit(solution)/shard_map/ppermute | solution.py:625
  47.8 3.0 %collective-permute-done.13.wide_got = bf16[512,256]{1,0:T(8,128)(2,1)S(1)} collective-permute-done((bf16[512,256]{1,0:T(8,128)(2,1)S(1)}, bf16[512,256]{1,0:T(8,128)(2,1)S(1)}, u32[]{:S(2)}, u32[]{:S(2)}) %collective-permute-start.13) | collective-permute-done | bytes 262176 | tf_op jit(solution)/shard_map/ppermute | solution.py:629
  51.6 1.6 %collective-permute-start.14 = (bf16[512,256]{1,0:T(8,128)(2,1)S(1)}, bf16[512,256]{1,0:T(8,128)(2,1)S(1)}, u32[]{:S(2)}, u32[]{:S(2)}) collective-permute-start(bf16[512,256]{1,0:T(8,128)(2,1)S(1)} %get-tuple-element.91), channel_id=1, source_target_pairs={{0,1},{1,0},{2,3},{3,2},{4,5},{5,4},{6,7},{7,6},{8,9},{9,8},{10,11... | collective-permute-start | bytes 786440 | tf_op jit(solution)/shard_map/ppermute | solution.py:625
  53.1 2.2 %shard_map.83 = (bf16[512,512]{1,0:T(8,128)(2,1)}, bf16[512,512]{1,0:T(8,128)(2,1)}) custom-call(s32[4]{0:T(128)S(1)} %pad_add_fusion.where, bf16[2,2,128,256]{3,2,1,0:T(8,128)(2,1)S(1)} %get-tuple-element.59.refs_0_, bf16[2,2,128,256]{3,2,1,0:T(8,128)(2,1)S(1)} %get-tuple-element.70.refs_1_, bf16[2,2,128,256]{3,2,1,0:T(8,128)(2,1)S(1)} %collective-permute-done.8.refs_2_, ...), custom_call_target="tpu_custom_call" | custom-call | flops 1000 | bytes 1000 | tf_op jit(solution)/shard_map/pallas_call | solution.py:603
  55.3 2.1 %shard_map.86 = (bf16[512,512]{1,0:T(8,128)(2,1)}, bf16[512,512]{1,0:T(8,128)(2,1)}) custom-call(s32[4]{0:T(128)S(1)} %pad_add_fusion.where, bf16[512,256]{1,0:T(8,128)(2,1)S(1)} %get-tuple-element.95.refs_0_, bf16[512,256]{1,0:T(8,128)(2,1)S(1)} %get-tuple-element.96.refs_1_, bf16[512,256]{1,0:T(8,128)(2,1)S(1)} %collective-permute-done.15.refs_2_), custom_call_target="tpu_custom_call" | custom-call | flops 1000 | bytes 1000 | tf_op jit(solution)/shard_map/pallas_call | solution.py:540
  57.4 1.9 %collective-permute-done.14.got = bf16[512,256]{1,0:T(8,128)(2,1)S(1)} collective-permute-done((bf16[512,256]{1,0:T(8,128)(2,1)S(1)}, bf16[512,256]{1,0:T(8,128)(2,1)S(1)}, u32[]{:S(2)}, u32[]{:S(2)}) %collective-permute-start.14) | collective-permute-done | bytes 262176 | tf_op jit(solution)/shard_map/ppermute | solution.py:625
  59.3 1.5 %shard_map.87 = (bf16[512,512]{1,0:T(8,128)(2,1)}, bf16[512,512]{1,0:T(8,128)(2,1)}) custom-call(s32[4]{0:T(128)S(1)} %pad_add_fusion.where, bf16[512,256]{1,0:T(8,128)(2,1)S(1)} %collective-permute-done.14.got, bf16[512,512]{1,0:T(8,128)(2,1)} %get-tuple-element.98.first_in, ...), custom_call_target="tpu_custom_call", output_to_operand_aliasing={{0}: (2, {}), {1}: (3, {})} | custom-call | flops 1000 | bytes 1000 | tf_op jit(solution)/shard_map/pallas_call | solution.py:573
  (33 shorter events, 6.0 us)
Async XLA Ops:
  0.7 2.9 %copy-start.2 = (bf16[512,512]{1,0:T(8,128)(2,1)S(1)}, bf16[512,512]{1,0:T(8,128)(2,1)}, u32[]{:S(2)}) copy-start(bf16[512,512]{1,0:T(8,128)(2,1)} %refs_0_.2) | copy-start | bytes 1572868
  1.7 1.9 %copy-start.3 = (bf16[512,512]{1,0:T(8,128)(2,1)S(1)}, bf16[512,512]{1,0:T(8,128)(2,1)}, u32[]{:S(2)}) copy-start(bf16[512,512]{1,0:T(8,128)(2,1)} %refs_1_.2) | copy-start | bytes 1572868
  2.0 9.3 %collective-permute-start = (bf16[512,256]{1,0:T(8,128)(2,1)S(1)}, bf16[512,256]{1,0:T(8,128)(2,1)S(1)}, u32[]{:S(2)}, u32[]{:S(2)}) collective-permute-start(bf16[512,256]{1,0:T(8,128)(2,1)S(1)} %shard_map.76), channel_id=1, source_target_pairs={{0,1},{1,0},{2,3},{3,2},{4,5},{5,4},{6,7},{7,6},{8,9},{9,8},{10,11... | collective-permute-start | bytes 786440 | tf_op jit(solution)/shard_map/ppermute | solution.py:625
  3.6 1.2 %copy-start = (bf16[512,512]{1,0:T(8,128)(2,1)S(1)}, bf16[512,512]{1,0:T(8,128)(2,1)}, u32[]{:S(2)}) copy-start(bf16[512,512]{1,0:T(8,128)(2,1)} %refs_0_.3) | copy-start | bytes 1572868
  3.6 1.2 %copy-start.1 = (bf16[512,512]{1,0:T(8,128)(2,1)S(1)}, bf16[512,512]{1,0:T(8,128)(2,1)}, u32[]{:S(2)}) copy-start(bf16[512,512]{1,0:T(8,128)(2,1)} %refs_1_.3) | copy-start | bytes 1572868
  3.9 13.0 %collective-permute-start.4 = (bf16[512,256]{1,0:T(8,128)(2,1)S(1)}, bf16[512,256]{1,0:T(8,128)(2,1)S(1)}, u32[]{:S(2)}, u32[]{:S(2)}) collective-permute-start(bf16[512,256]{1,0:T(8,128)(2,1)S(1)} %shard_map.80), channel_id=1, source_target_pairs={{0,1},{1,0},{2,3},{3,2},{4,5},{5,4},{6,7},{7,6},{8,9},{9,8},{10,11... | collective-permute-start | bytes 786440 | tf_op jit(solution)/shard_map/ppermute | solution.py:625
  5.9 15.4 %collective-permute-start.1 = (bf16[512,256]{1,0:T(8,128)(2,1)S(1)}, bf16[512,256]{1,0:T(8,128)(2,1)S(1)}, u32[]{:S(2)}, u32[]{:S(2)}) collective-permute-start(bf16[512,256]{1,0:T(8,128)(2,1)S(1)} %get-tuple-element.56), channel_id=1, source_target_pairs={{0,1},{1,0},{2,3},{3,2},{4,5},{5,4},{6,7},{7,6},{8,9},{9,8},{10,11... | collective-permute-start | bytes 786440 | tf_op jit(solution)/shard_map/ppermute | solution.py:625
  12.0 10.9 %collective-permute-start.2 = (bf16[512,256]{1,0:T(8,128)(2,1)S(1)}, bf16[512,256]{1,0:T(8,128)(2,1)S(1)}, u32[]{:S(2)}, u32[]{:S(2)}) collective-permute-start(bf16[512,256]{1,0:T(8,128)(2,1)S(1)} %get-tuple-element.57), channel_id=1, source_target_pairs={{0,2},{1,3},{2,0},{3,1},{4,6},{5,7},{6,4},{7,5},{8,10},{9,11},{10,... | collective-permute-start | bytes 786440 | tf_op jit(solution)/shard_map/ppermute | solution.py:628
  12.0 10.8 %collective-permute-start.3 = (bf16[512,256]{1,0:T(8,128)(2,1)S(1)}, bf16[512,256]{1,0:T(8,128)(2,1)S(1)}, u32[]{:S(2)}, u32[]{:S(2)}) collective-permute-start(bf16[512,256]{1,0:T(8,128)(2,1)S(1)} %get-tuple-element.58), channel_id=1, source_target_pairs={{2,4},{3,5},{4,2},{5,3},{6,8},{7,9},{8,6},{9,7},{10,12},{11,13},{1... | collective-permute-start | bytes 786440 | tf_op jit(solution)/shard_map/ppermute | solution.py:629
  17.6 14.0 %collective-permute-start.5 = (bf16[512,256]{1,0:T(8,128)(2,1)S(1)}, bf16[512,256]{1,0:T(8,128)(2,1)S(1)}, u32[]{:S(2)}, u32[]{:S(2)}) collective-permute-start(bf16[512,256]{1,0:T(8,128)(2,1)S(1)} %get-tuple-element.66), channel_id=1, source_target_pairs={{0,2},{1,3},{2,0},{3,1},{4,6},{5,7},{6,4},{7,5},{8,10},{9,11},{10,... | collective-permute-start | bytes 786440 | tf_op jit(solution)/shard_map/ppermute | solution.py:628
  17.7 15.2 %collective-permute-start.6 = (bf16[512,256]{1,0:T(8,128)(2,1)S(1)}, bf16[512,256]{1,0:T(8,128)(2,1)S(1)}, u32[]{:S(2)}, u32[]{:S(2)}) collective-permute-start(bf16[512,256]{1,0:T(8,128)(2,1)S(1)} %get-tuple-element.67), channel_id=1, source_target_pairs={{2,4},{3,5},{4,2},{5,3},{6,8},{7,9},{8,6},{9,7},{10,12},{11,13},{1... | collective-permute-start | bytes 786440 | tf_op jit(solution)/shard_map/ppermute | solution.py:629
  21.4 11.5 %collective-permute-start.7 = (bf16[512,256]{1,0:T(8,128)(2,1)S(1)}, bf16[512,256]{1,0:T(8,128)(2,1)S(1)}, u32[]{:S(2)}, u32[]{:S(2)}) collective-permute-start(bf16[512,256]{1,0:T(8,128)(2,1)S(1)} %get-tuple-element.69), channel_id=1, source_target_pairs={{0,1},{1,0},{2,3},{3,2},{4,5},{5,4},{6,7},{7,6},{8,9},{9,8},{10,11... | collective-permute-start | bytes 786440 | tf_op jit(solution)/shard_map/ppermute | solution.py:625
  28.8 10.9 %collective-permute-start.9 = (bf16[512,256]{1,0:T(8,128)(2,1)S(1)}, bf16[512,256]{1,0:T(8,128)(2,1)S(1)}, u32[]{:S(2)}, u32[]{:S(2)}) collective-permute-start(bf16[512,256]{1,0:T(8,128)(2,1)S(1)} %get-tuple-element.73), channel_id=1, source_target_pairs={{0,2},{1,3},{2,0},{3,1},{4,6},{5,7},{6,4},{7,5},{8,10},{9,11},{10,... | collective-permute-start | bytes 786440 | tf_op jit(solution)/shard_map/ppermute | solution.py:628
  28.9 10.8 %collective-permute-start.10 = (bf16[512,256]{1,0:T(8,128)(2,1)S(1)}, bf16[512,256]{1,0:T(8,128)(2,1)S(1)}, u32[]{:S(2)}, u32[]{:S(2)}) collective-permute-start(bf16[512,256]{1,0:T(8,128)(2,1)S(1)} %get-tuple-element.74), channel_id=1, source_target_pairs={{2,4},{3,5},{4,2},{5,3},{6,8},{7,9},{8,6},{9,7},{10,12},{11,13},{1... | collective-permute-start | bytes 786440 | tf_op jit(solution)/shard_map/ppermute | solution.py:629
  31.6 11.6 %collective-permute-start.8 = (bf16[2,2,128,256]{3,2,1,0:T(8,128)(2,1)S(1)}, bf16[2,2,128,256]{3,2,1,0:T(8,128)(2,1)S(1)}, u32[]{:S(2)}, u32[]{:S(2)}) collective-permute-start(bf16[2,2,128,256]{3,2,1,0:T(8,128)(2,1)S(1)} %get-tuple-element.71), channel_id=1, source_target_pairs={{0,1},{1,0},{2,3},{3,2},{4,5},{5,4},{6,7},{7,6},{8,9},{9,8},{10,11... | collective-permute-start | bytes 786440 | tf_op jit(solution)/shard_map/ppermute | solution.py:625
  38.8 9.0 %collective-permute-start.11 = (bf16[2,2,128,256]{3,2,1,0:T(8,128)(2,1)S(1)}, bf16[2,2,128,256]{3,2,1,0:T(8,128)(2,1)S(1)}, u32[]{:S(2)}, u32[]{:S(2)}) collective-permute-start(bf16[2,2,128,256]{3,2,1,0:T(8,128)(2,1)S(1)} %get-tuple-element.81), channel_id=1, source_target_pairs={{0,1},{1,0},{2,3},{3,2},{4,5},{5,4},{6,7},{7,6},{8,9},{9,8},{10,11... | collective-permute-start | bytes 786440 | tf_op jit(solution)/shard_map/ppermute | solution.py:625
  39.8 8.1 %collective-permute-start.12 = (bf16[512,256]{1,0:T(8,128)(2,1)S(1)}, bf16[512,256]{1,0:T(8,128)(2,1)S(1)}, u32[]{:S(2)}, u32[]{:S(2)}) collective-permute-start(bf16[512,256]{1,0:T(8,128)(2,1)S(1)} %get-tuple-element.83), channel_id=1, source_target_pairs={{0,2},{1,3},{2,0},{3,1},{4,6},{5,7},{6,4},{7,5},{8,10},{9,11},{10,... | collective-permute-start | bytes 786440 | tf_op jit(solution)/shard_map/ppermute | solution.py:628
  40.4 10.5 %collective-permute-start.13 = (bf16[512,256]{1,0:T(8,128)(2,1)S(1)}, bf16[512,256]{1,0:T(8,128)(2,1)S(1)}, u32[]{:S(2)}, u32[]{:S(2)}) collective-permute-start(bf16[512,256]{1,0:T(8,128)(2,1)S(1)} %get-tuple-element.84), channel_id=1, source_target_pairs={{2,4},{3,5},{4,2},{5,3},{6,8},{7,9},{8,6},{9,7},{10,12},{11,13},{1... | collective-permute-start | bytes 786440 | tf_op jit(solution)/shard_map/ppermute | solution.py:629
  43.9 11.4 %collective-permute-start.15 = (bf16[512,256]{1,0:T(8,128)(2,1)S(1)}, bf16[512,256]{1,0:T(8,128)(2,1)S(1)}, u32[]{:S(2)}, u32[]{:S(2)}) collective-permute-start(bf16[512,256]{1,0:T(8,128)(2,1)S(1)} %get-tuple-element.97), channel_id=1, source_target_pairs={{0,1},{1,0},{2,3},{3,2},{4,5},{5,4},{6,7},{7,6},{8,9},{9,8},{10,11... | collective-permute-start | bytes 786440 | tf_op jit(solution)/shard_map/ppermute | solution.py:625
  51.6 7.8 %collective-permute-start.14 = (bf16[512,256]{1,0:T(8,128)(2,1)S(1)}, bf16[512,256]{1,0:T(8,128)(2,1)S(1)}, u32[]{:S(2)}, u32[]{:S(2)}) collective-permute-start(bf16[512,256]{1,0:T(8,128)(2,1)S(1)} %get-tuple-element.91), channel_id=1, source_target_pairs={{0,1},{1,0},{2,3},{3,2},{4,5},{5,4},{6,7},{7,6},{8,9},{9,8},{10,11... | collective-permute-start | bytes 786440 | tf_op jit(solution)/shard_map/ppermute | solution.py:625

commit v19 on v18

--- a/solution.py
+++ b/solution.py
@@ -84,8 +84,8 @@
     rows, columns = arrays[0].shape
     count = len(arrays)
     return pl.pallas_call(
-        functools.partial(pack_kernel, own),
-        in_specs=[smem()] + [pl.BlockSpec(memory_space=pltpu.HBM)] * count,
+        placed(functools.partial(pack_kernel, own), where),
+        in_specs=[pl.BlockSpec(memory_space=pltpu.HBM)] * count,
         out_specs=[vmem()] * (count // 2 * CHUNKS),
         out_shape=[jax.ShapeDtypeStruct((rows, columns // CHUNKS), BF)] * (count // 2 * CHUNKS),
         scratch_shapes=[
@@ -94,7 +94,7 @@
         ],
         compiler_params=small(),
         cost_estimate=light(),
-    )(where, *arrays)
+    )(*arrays)
 
 
 def pack_cut_kernel(a, b, out):
@@ -120,8 +120,17 @@
     )(*cut)
 
 
-def smem():
-    return pl.BlockSpec(memory_space=pltpu.SMEM)
+def placed(kernel, grid):
+    inner, count = grid
+
+    def body(*refs):
+        device = lax.axis_index("outer") * inner + lax.axis_index("inner")
+        pair = device // 2
+        left = jnp.where(pair > 0, 1, 0)
+        right = jnp.where(pair < count // 2 - 1, 1, 0)
+        kernel((device % 2, left, right, pair % 2), *refs)
+
+    return body
 
 
 def vmem():
@@ -159,13 +168,13 @@
 def halo(where, own, got):
     shape = jax.ShapeDtypeStruct(own.shape, BF)
     return pl.pallas_call(
-        halo_kernel,
-        in_specs=[smem(), vmem(), vmem()],
+        placed(halo_kernel, where),
+        in_specs=[vmem(), vmem()],
         out_specs=[vmem(), vmem()],
         out_shape=[shape, shape],
         compiler_params=small(),
         cost_estimate=light(),
-    )(where, own, got)
+    )(own, got)
 
 
 def swap64(x):
@@ -445,8 +454,8 @@
     if qg_first:
         operands = operands[:2] + operands[4:] + operands[2:4]
     return pl.pallas_call(
-        functools.partial(main_kernel, qg_first),
-        in_specs=[smem()] + [vmem()] * 6,
+        placed(functools.partial(main_kernel, qg_first), where),
+        in_specs=[vmem()] * 6,
         out_specs=[vmem()] * 5,
         out_shape=[
             oq_shape,
@@ -475,7 +484,7 @@
         ],
         compiler_params=pltpu.CompilerParams(vmem_limit_bytes=24 * 1024 * 1024),
         cost_estimate=light(),
-    )(where, *operands)
+    )(*operands)
 
 
 def join_kernel(where, grad, near_got, wide_got, own, far):
@@ -511,13 +520,13 @@
 def join(where, grad, near_got, wide_got):
     shape = jax.ShapeDtypeStruct(near_got.shape, BF)
     return pl.pallas_call(
-        join_kernel,
-        in_specs=[smem(), vmem(), vmem(), vmem()],
+        placed(join_kernel, where),
+        in_specs=[vmem(), vmem(), vmem()],
         out_specs=[vmem(), vmem()],
         out_shape=[shape, shape],
         compiler_params=small(),
         cost_estimate=light(),
-    )(where, grad, near_got, wide_got)
+    )(grad, near_got, wide_got)
 
 
 def unpack_rows_kernel(where, *refs):
@@ -538,13 +547,13 @@
 def unpack_rows(where, own, got, shape):
     out = jax.ShapeDtypeStruct(shape, BF)
     return pl.pallas_call(
-        unpack_rows_kernel,
-        in_specs=[smem()] + [vmem()] * (CHUNKS + 1),
+        placed(unpack_rows_kernel, where),
+        in_specs=[vmem()] * (CHUNKS + 1),
         out_specs=[vmem(), vmem()],
         out_shape=[out, out],
         compiler_params=small(),
         cost_estimate=light(),
-    )(where, *own, got)
+    )(*own, got)
 
 
 def unpack_last_kernel(where, got, first_in, second_in, first, second, held, sems):
@@ -571,18 +580,18 @@
     out = jax.ShapeDtypeStruct(first.shape, BF)
     hbm = pl.BlockSpec(memory_space=pltpu.HBM)
     return pl.pallas_call(
-        unpack_last_kernel,
-        in_specs=[smem(), vmem(), hbm, hbm],
+        placed(unpack_last_kernel, where),
+        in_specs=[vmem(), hbm, hbm],
         out_specs=[hbm, hbm],
         out_shape=[out, out],
-        input_output_aliases={2: 0, 3: 1},
+        input_output_aliases={1: 0, 2: 1},
         scratch_shapes=[
             pltpu.VMEM((2, got.shape[0], got.shape[1] // 2), BF),
             pltpu.SemaphoreType.DMA((4,)),
         ],
         compiler_params=small(),
         cost_estimate=light(),
-    )(where, got, first, second)
+    )(got, first, second)
 
 
 def unpack_columns_kernel(where, *refs):
@@ -601,21 +610,20 @@
 def unpack_columns(where, own, got, shape):
     out = jax.ShapeDtypeStruct(shape, BF)
     return pl.pallas_call(
-        unpack_columns_kernel,
-        in_specs=[smem()] + [vmem()] * (2 * CHUNKS),
+        placed(unpack_columns_kernel, where),
+        in_specs=[vmem()] * (2 * CHUNKS),
         out_specs=[vmem(), vmem()],
         out_shape=[out, out],
         compiler_params=small(),
         cost_estimate=light(),
-    )(where, *own, *got)
+    )(*own, *got)
 
 
 def on_device(queries, key_matrix, value_matrix, cotangent):
     axes = ("outer", "inner")
     count = lax.axis_size("outer") * lax.axis_size("inner")
     device = lax.axis_index("outer") * lax.axis_size("inner") + lax.axis_index("inner")
-    pair = device // 2
-    where = jnp.stack([device % 2, pair > 0, pair < count // 2 - 1, pair % 2]).astype(jnp.int32)
+    where = (lax.axis_size("inner"), count)
     across = [(i, i ^ 1) for i in range(count)]
     near_edges = [(i, i ^ 2) for i in range(count) if i ^ 2 < count]
     wide_edges = [(i, i + 2 if i // 2 % 2 else i - 2) for i in range(count)]

time: 61.2 us -> 59.5 us (0.972)
  Pallas kernels: 23.8 us -> 18.2 us
  waiting for transfers between devices: 13.5 us -> 18.4 us
  starting transfers between devices: 21.4 us -> 20.4 us
    pallas_call x11, Pallas kernels: 23.2 us -> 17.7 us  [the longest x2 11.3 us: main(): pl.pallas_call(placed(functools.partial(main_kernel, qg_first), where), i...]
    ppermute x8, waiting for transfers between devices: 10.5 us -> 14.9 us  [swap(): return lax.ppermute(x, axes, across)]
    ppermute x8, starting transfers between devices: 10.1 us -> 9.03 us  [swap(): return lax.ppermute(x, axes, across)]
  transfers between devices with their start and end apart: 16 -> 16, of which waited for: 6 -> 6; matrix products, arithmetic and copies ran while one was open for 0% -> 0% of each run, Pallas kernels for 36% -> 29%
where the time goes in v19:
time: 59.5 us; the launch traced here: 59.3 us
  starting transfers between devices  20.4 us (34%)
  waiting for transfers between devices  18.4 us (31%)
  Pallas kernels  18.2 us (31%)
  local copies, waits for them, and re-layouts  1.23 us (2%)
  between operations  1.01 us (2%)
    ppermute x8, waiting for transfers between devices, swap(): return lax.ppermute(x, axes, across)  14.9 us
    pallas_call x2, Pallas kernels, main(): pl.pallas_call(placed(functools.partial(main_kernel, qg_first), where), i...  11.3 us
    ppermute x4, starting transfers between devices, beside(): return (near, lax.ppermute(wide, axes, wide_edges))  10.6 us
    ppermute x8, starting transfers between devices, swap(): return lax.ppermute(x, axes, across)  9.03 us
    ppermute x4, waiting for transfers between devices, beside(): return (near, lax.ppermute(wide, axes, wide_edges))  3.46 us
    pallas_call x1, Pallas kernels, unpack_columns(): pl.pallas_call(placed(unpack_columns_kernel, where), in_specs=[vmem()] *...  1.67 us
    pallas_call x2, Pallas kernels, pack(): pl.pallas_call(placed(functools.partial(pack_kernel, own), where), in_spe...  1.65 us
    pallas_call x1, Pallas kernels, unpack_rows(): pl.pallas_call(placed(unpack_rows_kernel, where), in_specs=[vmem()] * (CH...  1.53 us
  transfers between devices with their start and end apart: 16, of which 6 were waited for; matrix products, arithmetic and copies ran while one was open for 0% of the time, Pallas kernels for 29%

profile of v19, /device:TPU:12, one launch (start us, length us, event | category | flops | bytes accessed | tf_op | source)
XLA Modules:
  0.0 59.3 jit_solution(10922314269766889484)
XLA Ops:
  0.7 1.1 %constant_dynamic-slice_fusion.2 = (bf16[512,128]{1,0:T(8,128)(2,1)S(1)}, bf16[512,128]{1,0:T(8,128)(2,1)S(1)}) fusion(bf16[512,512]{1,0:T(8,128)(2,1)} %refs_1_.2, s32[]{:T(128)S(6)} %select_n.18, bf16[512,512]{1,0:T(8,128)(2,1)} %refs_0_.2), kind=kLoop, calls=%fused_computation.2 | loop fusion | bytes 524292 | tf_op jit(solution)/shard_map/dynamic_slice | solution.py:112
  2.0 1.6 %collective-permute-start = (bf16[512,256]{1,0:T(8,128)(2,1)S(1)}, bf16[512,256]{1,0:T(8,128)(2,1)S(1)}, u32[]{:S(2)}, u32[]{:S(2)}) collective-permute-start(bf16[512,256]{1,0:T(8,128)(2,1)S(1)} %shard_map.76), channel_id=1, source_target_pairs={{0,1},{1,0},{2,3},{3,2},{4,5},{5,4},{6,7},{7,6},{8,9},{9,8},{10,11... | collective-permute-start | bytes 786440 | tf_op jit(solution)/shard_map/ppermute | solution.py:633
  3.9 0.7 %collective-permute-start.4 = (bf16[512,256]{1,0:T(8,128)(2,1)S(1)}, bf16[512,256]{1,0:T(8,128)(2,1)S(1)}, u32[]{:S(2)}, u32[]{:S(2)}) collective-permute-start(bf16[512,256]{1,0:T(8,128)(2,1)S(1)} %shard_map.80), channel_id=1, source_target_pairs={{0,1},{1,0},{2,3},{3,2},{4,5},{5,4},{6,7},{7,6},{8,9},{9,8},{10,11... | collective-permute-start | bytes 786440 | tf_op jit(solution)/shard_map/ppermute | solution.py:633
  5.4 1.3 %collective-permute-start.1 = (bf16[512,256]{1,0:T(8,128)(2,1)S(1)}, bf16[512,256]{1,0:T(8,128)(2,1)S(1)}, u32[]{:S(2)}, u32[]{:S(2)}) collective-permute-start(bf16[512,256]{1,0:T(8,128)(2,1)S(1)} %get-tuple-element.56), channel_id=1, source_target_pairs={{0,1},{1,0},{2,3},{3,2},{4,5},{5,4},{6,7},{7,6},{8,9},{9,8},{10,11... | collective-permute-start | bytes 786440 | tf_op jit(solution)/shard_map/ppermute | solution.py:633
  6.7 1.1 %shard_map.75 = (bf16[512,256]{1,0:T(8,128)(2,1)S(1)}, bf16[512,256]{1,0:T(8,128)(2,1)S(1)}, bf16[512,256]{1,0:T(8,128)(2,1)S(1)}, bf16[512,256]{1,0:T(8,128)(2,1)S(1)}) custom-call(bf16[512,512]{1,0:T(8,128)(2,1)S(1)} %copy-done.2, bf16[512,512]{1,0:T(8,128)(2,1)S(1)} %copy-done.3, bf16[512,512]{1,0:T(8,128)(2,1)S(1)} %copy-done, bf16[512,512]{1,0:T(8,128)(2,1)S(1)} %copy-done.1), custom_call_target="tpu_custom_call" | custom-call | flops 1000 | bytes 1000 | tf_op jit(solution)/shard_map/pallas_call | solution.py:86
  7.8 3.5 %collective-permute-done.refs_1_ = bf16[512,256]{1,0:T(8,128)(2,1)S(1)} collective-permute-done((bf16[512,256]{1,0:T(8,128)(2,1)S(1)}, bf16[512,256]{1,0:T(8,128)(2,1)S(1)}, u32[]{:S(2)}, u32[]{:S(2)}) %collective-permute-start) | collective-permute-done | bytes 262176 | tf_op jit(solution)/shard_map/ppermute | solution.py:633
  11.5 2.5 %collective-permute-start.3 = (bf16[512,256]{1,0:T(8,128)(2,1)S(1)}, bf16[512,256]{1,0:T(8,128)(2,1)S(1)}, u32[]{:S(2)}, u32[]{:S(2)}) collective-permute-start(bf16[512,256]{1,0:T(8,128)(2,1)S(1)} %get-tuple-element.58), channel_id=1, source_target_pairs={{2,4},{3,5},{4,2},{5,3},{6,8},{7,9},{8,6},{9,7},{10,12},{11,13},{1... | collective-permute-start | bytes 786440 | tf_op jit(solution)/shard_map/ppermute | solution.py:637
  14.0 2.9 %collective-permute-done.4.refs_1_ = bf16[512,256]{1,0:T(8,128)(2,1)S(1)} collective-permute-done((bf16[512,256]{1,0:T(8,128)(2,1)S(1)}, bf16[512,256]{1,0:T(8,128)(2,1)S(1)}, u32[]{:S(2)}, u32[]{:S(2)}) %collective-permute-start.4) | collective-permute-done | bytes 262176 | tf_op jit(solution)/shard_map/ppermute | solution.py:633
  17.1 2.5 %collective-permute-start.6 = (bf16[512,256]{1,0:T(8,128)(2,1)S(1)}, bf16[512,256]{1,0:T(8,128)(2,1)S(1)}, u32[]{:S(2)}, u32[]{:S(2)}) collective-permute-start(bf16[512,256]{1,0:T(8,128)(2,1)S(1)} %get-tuple-element.67), channel_id=1, source_target_pairs={{2,4},{3,5},{4,2},{5,3},{6,8},{7,9},{8,6},{9,7},{10,12},{11,13},{1... | collective-permute-start | bytes 786440 | tf_op jit(solution)/shard_map/ppermute | solution.py:637
  19.6 1.8 %collective-permute-done.1.refs_3_ = bf16[512,256]{1,0:T(8,128)(2,1)S(1)} collective-permute-done((bf16[512,256]{1,0:T(8,128)(2,1)S(1)}, bf16[512,256]{1,0:T(8,128)(2,1)S(1)}, u32[]{:S(2)}, u32[]{:S(2)}) %collective-permute-start.1) | collective-permute-done | bytes 262176 | tf_op jit(solution)/shard_map/ppermute | solution.py:633
  21.4 1.5 %collective-permute-start.7 = (bf16[512,256]{1,0:T(8,128)(2,1)S(1)}, bf16[512,256]{1,0:T(8,128)(2,1)S(1)}, u32[]{:S(2)}, u32[]{:S(2)}) collective-permute-start(bf16[512,256]{1,0:T(8,128)(2,1)S(1)} %get-tuple-element.69), channel_id=1, source_target_pairs={{0,1},{1,0},{2,3},{3,2},{4,5},{5,4},{6,7},{7,6},{8,9},{9,8},{10,11... | collective-permute-start | bytes 786440 | tf_op jit(solution)/shard_map/ppermute | solution.py:633
  22.9 5.7 %shard_map.79 = (bf16[2,2,128,256]{3,2,1,0:T(8,128)(2,1)S(1)}, bf16[2,2,128,256]{3,2,1,0:T(8,128)(2,1)S(1)}, f32[1024,256]{1,0:T(8,128)S(1)}, bf16[512,256]{1,0:T(8,128)(2,1)S(1)}, bf16[512,256]{1,0:T(8,128)(2,1)S(1)}) custom-call(bf16[512,256]{1,0:T(8,128)(2,1)S(1)} %get-tuple-element.53.refs_0_, bf16[512,256]{1,0:T(8,128)(2,1)S(1)} %collective-permute-done.refs_1_, ...), custom_call_target="tpu_custom_call" | custom-call | flops 1000 | bytes 1000 | tf_op jit(solution)/shard_map/pallas_call | solution.py:456
  28.6 2.7 %collective-permute-start.10 = (bf16[512,256]{1,0:T(8,128)(2,1)S(1)}, bf16[512,256]{1,0:T(8,128)(2,1)S(1)}, u32[]{:S(2)}, u32[]{:S(2)}) collective-permute-start(bf16[512,256]{1,0:T(8,128)(2,1)S(1)} %get-tuple-element.74), channel_id=1, source_target_pairs={{2,4},{3,5},{4,2},{5,3},{6,8},{7,9},{8,6},{9,7},{10,12},{11,13},{1... | collective-permute-start | bytes 786440 | tf_op jit(solution)/shard_map/ppermute | solution.py:637
  32.0 5.7 %shard_map.82 = (bf16[2,2,128,256]{3,2,1,0:T(8,128)(2,1)S(1)}, bf16[2,2,128,256]{3,2,1,0:T(8,128)(2,1)S(1)}, f32[1024,256]{1,0:T(8,128)S(1)}, bf16[512,256]{1,0:T(8,128)(2,1)S(1)}, bf16[512,256]{1,0:T(8,128)(2,1)S(1)}) custom-call(bf16[512,256]{1,0:T(8,128)(2,1)S(1)} %get-tuple-element.60.refs_0_, bf16[512,256]{1,0:T(8,128)(2,1)S(1)} %collective-permute-done.4.refs_1_, ...), custom_call_target="tpu_custom_call" | custom-call | flops 1000 | bytes 1000 | tf_op jit(solution)/shard_map/pallas_call | solution.py:456
  37.7 1.5 %collective-permute-start.11 = (bf16[2,2,128,256]{3,2,1,0:T(8,128)(2,1)S(1)}, bf16[2,2,128,256]{3,2,1,0:T(8,128)(2,1)S(1)}, u32[]{:S(2)}, u32[]{:S(2)}) collective-permute-start(bf16[2,2,128,256]{3,2,1,0:T(8,128)(2,1)S(1)} %get-tuple-element.81), channel_id=1, source_target_pairs={{0,1},{1,0},{2,3},{3,2},{4,5},{5,4},{6,7},{7,6},{8,9},{9,8},{10,11... | collective-permute-start | bytes 786440 | tf_op jit(solution)/shard_map/ppermute | solution.py:633
  39.6 2.9 %collective-permute-start.13 = (bf16[512,256]{1,0:T(8,128)(2,1)S(1)}, bf16[512,256]{1,0:T(8,128)(2,1)S(1)}, u32[]{:S(2)}, u32[]{:S(2)}) collective-permute-start(bf16[512,256]{1,0:T(8,128)(2,1)S(1)} %get-tuple-element.84), channel_id=1, source_target_pairs={{2,4},{3,5},{4,2},{5,3},{6,8},{7,9},{8,6},{9,7},{10,12},{11,13},{1... | collective-permute-start | bytes 786440 | tf_op jit(solution)/shard_map/ppermute | solution.py:637
  42.8 0.7 %collective-permute-start.15 = (bf16[512,256]{1,0:T(8,128)(2,1)S(1)}, bf16[512,256]{1,0:T(8,128)(2,1)S(1)}, u32[]{:S(2)}, u32[]{:S(2)}) collective-permute-start(bf16[512,256]{1,0:T(8,128)(2,1)S(1)} %get-tuple-element.97), channel_id=1, source_target_pairs={{0,1},{1,0},{2,3},{3,2},{4,5},{5,4},{6,7},{7,6},{8,9},{9,8},{10,11... | collective-permute-start | bytes 786440 | tf_op jit(solution)/shard_map/ppermute | solution.py:633
  43.4 3.2 %collective-permute-done.11.refs_3_ = bf16[2,2,128,256]{3,2,1,0:T(8,128)(2,1)S(1)} collective-permute-done((bf16[2,2,128,256]{3,2,1,0:T(8,128)(2,1)S(1)}, bf16[2,2,128,256]{3,2,1,0:T(8,128)(2,1)S(1)}, u32[]{:S(2)}, u32[]{:S(2)}) %collective-permute-start.11) | collective-permute-done | bytes 262176 | tf_op jit(solution)/shard_map/ppermute | solution.py:633
  46.7 3.5 %collective-permute-done.13.refs_2_ = bf16[512,256]{1,0:T(8,128)(2,1)S(1)} collective-permute-done((bf16[512,256]{1,0:T(8,128)(2,1)S(1)}, bf16[512,256]{1,0:T(8,128)(2,1)S(1)}, u32[]{:S(2)}, u32[]{:S(2)}) %collective-permute-start.13) | collective-permute-done | bytes 262176 | tf_op jit(solution)/shard_map/ppermute | solution.py:637
  50.2 1.1 %collective-permute-start.14 = (bf16[512,256]{1,0:T(8,128)(2,1)S(1)}, bf16[512,256]{1,0:T(8,128)(2,1)S(1)}, u32[]{:S(2)}, u32[]{:S(2)}) collective-permute-start(bf16[512,256]{1,0:T(8,128)(2,1)S(1)} %get-tuple-element.91), channel_id=1, source_target_pairs={{0,1},{1,0},{2,3},{3,2},{4,5},{5,4},{6,7},{7,6},{8,9},{9,8},{10,11... | collective-permute-start | bytes 786440 | tf_op jit(solution)/shard_map/ppermute | solution.py:633
  51.4 1.7 %shard_map.83 = (bf16[512,512]{1,0:T(8,128)(2,1)}, bf16[512,512]{1,0:T(8,128)(2,1)}) custom-call(bf16[2,2,128,256]{3,2,1,0:T(8,128)(2,1)S(1)} %get-tuple-element.59.refs_0_, bf16[2,2,128,256]{3,2,1,0:T(8,128)(2,1)S(1)} %get-tuple-element.70.refs_1_, bf16[2,2,128,256]{3,2,1,0:T(8,128)(2,1)S(1)} %collective-permute-done.8.refs_2_, ...), custom_call_target="tpu_custom_call" | custom-call | flops 1000 | bytes 1000 | tf_op jit(solution)/shard_map/pallas_call | solution.py:612
  53.0 1.5 %shard_map.86 = (bf16[512,512]{1,0:T(8,128)(2,1)}, bf16[512,512]{1,0:T(8,128)(2,1)}) custom-call(bf16[512,256]{1,0:T(8,128)(2,1)S(1)} %get-tuple-element.95.refs_0_, bf16[512,256]{1,0:T(8,128)(2,1)S(1)} %get-tuple-element.96.refs_1_, bf16[512,256]{1,0:T(8,128)(2,1)S(1)} %collective-permute-done.15.refs_2_), custom_call_target="tpu_custom_call" | custom-call | flops 1000 | bytes 1000 | tf_op jit(solution)/shard_map/pallas_call | solution.py:549
  54.6 3.6 %collective-permute-done.14.refs_0_ = bf16[512,256]{1,0:T(8,128)(2,1)S(1)} collective-permute-done((bf16[512,256]{1,0:T(8,128)(2,1)S(1)}, bf16[512,256]{1,0:T(8,128)(2,1)S(1)}, u32[]{:S(2)}, u32[]{:S(2)}) %collective-permute-start.14) | collective-permute-done | bytes 262176 | tf_op jit(solution)/shard_map/ppermute | solution.py:633
  58.1 1.0 %shard_map.87 = (bf16[512,512]{1,0:T(8,128)(2,1)}, bf16[512,512]{1,0:T(8,128)(2,1)}) custom-call(bf16[512,256]{1,0:T(8,128)(2,1)S(1)} %collective-permute-done.14.refs_0_, bf16[512,512]{1,0:T(8,128)(2,1)} %get-tuple-element.98.refs_1_, bf16[512,512]{1,0:T(8,128)(2,1)} %get-tuple-element.99.refs_2_), custom_call_target="tpu_custom_call", output_to_operand_aliasing={{0}: (1, {}), {1}: (2, {})} | custom-call | flops 1000 | bytes 1000 | tf_op jit(solution)/shard_map/pallas_call | solution.py:582
  (32 shorter events, 3.2 us)
Async XLA Ops:
  0.6 2.9 %copy-start.2 = (bf16[512,512]{1,0:T(8,128)(2,1)S(1)}, bf16[512,512]{1,0:T(8,128)(2,1)}, u32[]{:S(2)}) copy-start(bf16[512,512]{1,0:T(8,128)(2,1)} %refs_0_.2) | copy-start | bytes 1572868
  1.7 1.9 %copy-start.3 = (bf16[512,512]{1,0:T(8,128)(2,1)S(1)}, bf16[512,512]{1,0:T(8,128)(2,1)}, u32[]{:S(2)}) copy-start(bf16[512,512]{1,0:T(8,128)(2,1)} %refs_1_.2) | copy-start | bytes 1572868
  2.0 9.3 %collective-permute-start = (bf16[512,256]{1,0:T(8,128)(2,1)S(1)}, bf16[512,256]{1,0:T(8,128)(2,1)S(1)}, u32[]{:S(2)}, u32[]{:S(2)}) collective-permute-start(bf16[512,256]{1,0:T(8,128)(2,1)S(1)} %shard_map.76), channel_id=1, source_target_pairs={{0,1},{1,0},{2,3},{3,2},{4,5},{5,4},{6,7},{7,6},{8,9},{9,8},{10,11... | collective-permute-start | bytes 786440 | tf_op jit(solution)/shard_map/ppermute | solution.py:633
  3.6 1.1 %copy-start = (bf16[512,512]{1,0:T(8,128)(2,1)S(1)}, bf16[512,512]{1,0:T(8,128)(2,1)}, u32[]{:S(2)}) copy-start(bf16[512,512]{1,0:T(8,128)(2,1)} %refs_0_.3) | copy-start | bytes 1572868
  3.6 1.2 %copy-start.1 = (bf16[512,512]{1,0:T(8,128)(2,1)S(1)}, bf16[512,512]{1,0:T(8,128)(2,1)}, u32[]{:S(2)}) copy-start(bf16[512,512]{1,0:T(8,128)(2,1)} %refs_1_.3) | copy-start | bytes 1572868
  3.9 13.0 %collective-permute-start.4 = (bf16[512,256]{1,0:T(8,128)(2,1)S(1)}, bf16[512,256]{1,0:T(8,128)(2,1)S(1)}, u32[]{:S(2)}, u32[]{:S(2)}) collective-permute-start(bf16[512,256]{1,0:T(8,128)(2,1)S(1)} %shard_map.80), channel_id=1, source_target_pairs={{0,1},{1,0},{2,3},{3,2},{4,5},{5,4},{6,7},{7,6},{8,9},{9,8},{10,11... | collective-permute-start | bytes 786440 | tf_op jit(solution)/shard_map/ppermute | solution.py:633
  5.4 16.0 %collective-permute-start.1 = (bf16[512,256]{1,0:T(8,128)(2,1)S(1)}, bf16[512,256]{1,0:T(8,128)(2,1)S(1)}, u32[]{:S(2)}, u32[]{:S(2)}) collective-permute-start(bf16[512,256]{1,0:T(8,128)(2,1)S(1)} %get-tuple-element.56), channel_id=1, source_target_pairs={{0,1},{1,0},{2,3},{3,2},{4,5},{5,4},{6,7},{7,6},{8,9},{9,8},{10,11... | collective-permute-start | bytes 786440 | tf_op jit(solution)/shard_map/ppermute | solution.py:633
  11.4 11.5 %collective-permute-start.2 = (bf16[512,256]{1,0:T(8,128)(2,1)S(1)}, bf16[512,256]{1,0:T(8,128)(2,1)S(1)}, u32[]{:S(2)}, u32[]{:S(2)}) collective-permute-start(bf16[512,256]{1,0:T(8,128)(2,1)S(1)} %get-tuple-element.57), channel_id=1, source_target_pairs={{0,2},{1,3},{2,0},{3,1},{4,6},{5,7},{6,4},{7,5},{8,10},{9,11},{10,... | collective-permute-start | bytes 786440 | tf_op jit(solution)/shard_map/ppermute | solution.py:636
  11.5 11.4 %collective-permute-start.3 = (bf16[512,256]{1,0:T(8,128)(2,1)S(1)}, bf16[512,256]{1,0:T(8,128)(2,1)S(1)}, u32[]{:S(2)}, u32[]{:S(2)}) collective-permute-start(bf16[512,256]{1,0:T(8,128)(2,1)S(1)} %get-tuple-element.58), channel_id=1, source_target_pairs={{2,4},{3,5},{4,2},{5,3},{6,8},{7,9},{8,6},{9,7},{10,12},{11,13},{1... | collective-permute-start | bytes 786440 | tf_op jit(solution)/shard_map/ppermute | solution.py:637
  17.0 14.3 %collective-permute-start.5 = (bf16[512,256]{1,0:T(8,128)(2,1)S(1)}, bf16[512,256]{1,0:T(8,128)(2,1)S(1)}, u32[]{:S(2)}, u32[]{:S(2)}) collective-permute-start(bf16[512,256]{1,0:T(8,128)(2,1)S(1)} %get-tuple-element.66), channel_id=1, source_target_pairs={{0,2},{1,3},{2,0},{3,1},{4,6},{5,7},{6,4},{7,5},{8,10},{9,11},{10,... | collective-permute-start | bytes 786440 | tf_op jit(solution)/shard_map/ppermute | solution.py:636
  17.1 14.9 %collective-permute-start.6 = (bf16[512,256]{1,0:T(8,128)(2,1)S(1)}, bf16[512,256]{1,0:T(8,128)(2,1)S(1)}, u32[]{:S(2)}, u32[]{:S(2)}) collective-permute-start(bf16[512,256]{1,0:T(8,128)(2,1)S(1)} %get-tuple-element.67), channel_id=1, source_target_pairs={{2,4},{3,5},{4,2},{5,3},{6,8},{7,9},{8,6},{9,7},{10,12},{11,13},{1... | collective-permute-start | bytes 786440 | tf_op jit(solution)/shard_map/ppermute | solution.py:637
  21.4 10.6 %collective-permute-start.7 = (bf16[512,256]{1,0:T(8,128)(2,1)S(1)}, bf16[512,256]{1,0:T(8,128)(2,1)S(1)}, u32[]{:S(2)}, u32[]{:S(2)}) collective-permute-start(bf16[512,256]{1,0:T(8,128)(2,1)S(1)} %get-tuple-element.69), channel_id=1, source_target_pairs={{0,1},{1,0},{2,3},{3,2},{4,5},{5,4},{6,7},{7,6},{8,9},{9,8},{10,11... | collective-permute-start | bytes 786440 | tf_op jit(solution)/shard_map/ppermute | solution.py:633
  28.5 10.6 %collective-permute-start.9 = (bf16[512,256]{1,0:T(8,128)(2,1)S(1)}, bf16[512,256]{1,0:T(8,128)(2,1)S(1)}, u32[]{:S(2)}, u32[]{:S(2)}) collective-permute-start(bf16[512,256]{1,0:T(8,128)(2,1)S(1)} %get-tuple-element.73), channel_id=1, source_target_pairs={{0,2},{1,3},{2,0},{3,1},{4,6},{5,7},{6,4},{7,5},{8,10},{9,11},{10,... | collective-permute-start | bytes 786440 | tf_op jit(solution)/shard_map/ppermute | solution.py:636
  28.6 10.5 %collective-permute-start.10 = (bf16[512,256]{1,0:T(8,128)(2,1)S(1)}, bf16[512,256]{1,0:T(8,128)(2,1)S(1)}, u32[]{:S(2)}, u32[]{:S(2)}) collective-permute-start(bf16[512,256]{1,0:T(8,128)(2,1)S(1)} %get-tuple-element.74), channel_id=1, source_target_pairs={{2,4},{3,5},{4,2},{5,3},{6,8},{7,9},{8,6},{9,7},{10,12},{11,13},{1... | collective-permute-start | bytes 786440 | tf_op jit(solution)/shard_map/ppermute | solution.py:637
  31.3 11.3 %collective-permute-start.8 = (bf16[2,2,128,256]{3,2,1,0:T(8,128)(2,1)S(1)}, bf16[2,2,128,256]{3,2,1,0:T(8,128)(2,1)S(1)}, u32[]{:S(2)}, u32[]{:S(2)}) collective-permute-start(bf16[2,2,128,256]{3,2,1,0:T(8,128)(2,1)S(1)} %get-tuple-element.71), channel_id=1, source_target_pairs={{0,1},{1,0},{2,3},{3,2},{4,5},{5,4},{6,7},{7,6},{8,9},{9,8},{10,11... | collective-permute-start | bytes 786440 | tf_op jit(solution)/shard_map/ppermute | solution.py:633
  37.7 9.0 %collective-permute-start.11 = (bf16[2,2,128,256]{3,2,1,0:T(8,128)(2,1)S(1)}, bf16[2,2,128,256]{3,2,1,0:T(8,128)(2,1)S(1)}, u32[]{:S(2)}, u32[]{:S(2)}) collective-permute-start(bf16[2,2,128,256]{3,2,1,0:T(8,128)(2,1)S(1)} %get-tuple-element.81), channel_id=1, source_target_pairs={{0,1},{1,0},{2,3},{3,2},{4,5},{5,4},{6,7},{7,6},{8,9},{9,8},{10,11... | collective-permute-start | bytes 786440 | tf_op jit(solution)/shard_map/ppermute | solution.py:633
  39.2 7.5 %collective-permute-start.12 = (bf16[512,256]{1,0:T(8,128)(2,1)S(1)}, bf16[512,256]{1,0:T(8,128)(2,1)S(1)}, u32[]{:S(2)}, u32[]{:S(2)}) collective-permute-start(bf16[512,256]{1,0:T(8,128)(2,1)S(1)} %get-tuple-element.83), channel_id=1, source_target_pairs={{0,2},{1,3},{2,0},{3,1},{4,6},{5,7},{6,4},{7,5},{8,10},{9,11},{10,... | collective-permute-start | bytes 786440 | tf_op jit(solution)/shard_map/ppermute | solution.py:636
  39.6 10.5 %collective-permute-start.13 = (bf16[512,256]{1,0:T(8,128)(2,1)S(1)}, bf16[512,256]{1,0:T(8,128)(2,1)S(1)}, u32[]{:S(2)}, u32[]{:S(2)}) collective-permute-start(bf16[512,256]{1,0:T(8,128)(2,1)S(1)} %get-tuple-element.84), channel_id=1, source_target_pairs={{2,4},{3,5},{4,2},{5,3},{6,8},{7,9},{8,6},{9,7},{10,12},{11,13},{1... | collective-permute-start | bytes 786440 | tf_op jit(solution)/shard_map/ppermute | solution.py:637
  42.8 10.3 %collective-permute-start.15 = (bf16[512,256]{1,0:T(8,128)(2,1)S(1)}, bf16[512,256]{1,0:T(8,128)(2,1)S(1)}, u32[]{:S(2)}, u32[]{:S(2)}) collective-permute-start(bf16[512,256]{1,0:T(8,128)(2,1)S(1)} %get-tuple-element.97), channel_id=1, source_target_pairs={{0,1},{1,0},{2,3},{3,2},{4,5},{5,4},{6,7},{7,6},{8,9},{9,8},{10,11... | collective-permute-start | bytes 786440 | tf_op jit(solution)/shard_map/ppermute | solution.py:633
  50.2 7.9 %collective-permute-start.14 = (bf16[512,256]{1,0:T(8,128)(2,1)S(1)}, bf16[512,256]{1,0:T(8,128)(2,1)S(1)}, u32[]{:S(2)}, u32[]{:S(2)}) collective-permute-start(bf16[512,256]{1,0:T(8,128)(2,1)S(1)} %get-tuple-element.91), channel_id=1, source_target_pairs={{0,1},{1,0},{2,3},{3,2},{4,5},{5,4},{6,7},{7,6},{8,9},{9,8},{10,11... | collective-permute-start | bytes 786440 | tf_op jit(solution)/shard_map/ppermute | solution.py:633

commit v20 on v19

--- a/solution.py
+++ b/solution.py
@@ -653,12 +653,14 @@
         near, wide = beside(near, wide)
         own, far, grad, near, wide = main(where, kv[c], got_kv, near, wide, qg[c], swap(far), c == 0)
         oq_own.append(own)
+        if c > 0:
+            back[c - 1], near, wide, far = lax.optimization_barrier(
+                (back[c - 1], near, wide, far)
+            )
+        back.append([grad, *beside(near, wide)])
         oq_got.append(swap(far))
-        if c > 0:
-            back[c - 1], near, wide = lax.optimization_barrier((back[c - 1], near, wide))
-        back.append([grad, *beside(near, wide)])
     for c in range(CHUNKS):
-        oq_got[c], back[c] = lax.optimization_barrier((oq_got[c], back[c]))
+        back[c], oq_got[c] = lax.optimization_barrier((back[c], oq_got[c]))
     kv_own, kv_got = [], []
     for c in range(CHUNKS):
         own, far = join(where, *back[c])

time: 59.5 us -> 63.7 us (1.071)
  waiting for transfers between devices: 18.4 us -> 23.1 us
  starting transfers between devices: 20.4 us -> 19.4 us
    ppermute x4, waiting for transfers between devices: 3.46 us -> 6.86 us  [beside(): return (near, lax.ppermute(wide, axes, wide_edges))]
    ppermute x8, waiting for transfers between devices: 14.9 us -> 16.3 us  [swap(): return lax.ppermute(x, axes, across)]
  transfers between devices with their start and end apart: 16 -> 16, of which waited for: 6 -> 8; matrix products, arithmetic and copies ran while one was open for 0% -> 0% of each run, Pallas kernels for 29% -> 27%
where the time goes in v20:
time: 63.7 us; the launch traced here: 63 us
  waiting for transfers between devices  23.1 us (36%)
  starting transfers between devices  19.4 us (30%)
  Pallas kernels  18.2 us (29%)
  local copies, waits for them, and re-layouts  1.23 us (2%)
  between operations  1.01 us (2%)
    ppermute x8, waiting for transfers between devices, swap(): return lax.ppermute(x, axes, across)  16.3 us
    pallas_call x2, Pallas kernels, main(): pl.pallas_call(placed(functools.partial(main_kernel, qg_first), where), i...  11.3 us
    ppermute x4, starting transfers between devices, beside(): return (near, lax.ppermute(wide, axes, wide_edges))  10.5 us
    ppermute x8, starting transfers between devices, swap(): return lax.ppermute(x, axes, across)  8.75 us
    ppermute x4, waiting for transfers between devices, beside(): return (near, lax.ppermute(wide, axes, wide_edges))  6.86 us
    pallas_call x1, Pallas kernels, unpack_columns(): pl.pallas_call(placed(unpack_columns_kernel, where), in_specs=[vmem()] *...  1.67 us
    pallas_call x2, Pallas kernels, pack(): pl.pallas_call(placed(functools.partial(pack_kernel, own), where), in_spe...  1.65 us
    pallas_call x1, Pallas kernels, unpack_rows(): pl.pallas_call(placed(unpack_rows_kernel, where), in_specs=[vmem()] * (CH...  1.53 us
  transfers between devices with their start and end apart: 16, of which 8 were waited for; matrix products, arithmetic and copies ran while one was open for 0% of the time, Pallas kernels for 27%

profile of v20, /device:TPU:12, one launch (start us, length us, event | category | flops | bytes accessed | tf_op | source)
XLA Modules:
  0.0 63.0 jit_solution(12099566297626584625)
XLA Ops:
  0.7 1.1 %constant_dynamic-slice_fusion.2 = (bf16[512,128]{1,0:T(8,128)(2,1)S(1)}, bf16[512,128]{1,0:T(8,128)(2,1)S(1)}) fusion(bf16[512,512]{1,0:T(8,128)(2,1)} %refs_1_.2, s32[]{:T(128)S(6)} %select_n.18, bf16[512,512]{1,0:T(8,128)(2,1)} %refs_0_.2), kind=kLoop, calls=%fused_computation.2 | loop fusion | bytes 524292 | tf_op jit(solution)/shard_map/dynamic_slice | solution.py:112
  2.0 1.6 %collective-permute-start = (bf16[512,256]{1,0:T(8,128)(2,1)S(1)}, bf16[512,256]{1,0:T(8,128)(2,1)S(1)}, u32[]{:S(2)}, u32[]{:S(2)}) collective-permute-start(bf16[512,256]{1,0:T(8,128)(2,1)S(1)} %shard_map.76), channel_id=1, source_target_pairs={{0,1},{1,0},{2,3},{3,2},{4,5},{5,4},{6,7},{7,6},{8,9},{9,8},{10,11... | collective-permute-start | bytes 786440 | tf_op jit(solution)/shard_map/ppermute | solution.py:633
  5.4 1.3 %collective-permute-start.1 = (bf16[512,256]{1,0:T(8,128)(2,1)S(1)}, bf16[512,256]{1,0:T(8,128)(2,1)S(1)}, u32[]{:S(2)}, u32[]{:S(2)}) collective-permute-start(bf16[512,256]{1,0:T(8,128)(2,1)S(1)} %get-tuple-element.57), channel_id=1, source_target_pairs={{0,1},{1,0},{2,3},{3,2},{4,5},{5,4},{6,7},{7,6},{8,9},{9,8},{10,11... | collective-permute-start | bytes 786440 | tf_op jit(solution)/shard_map/ppermute | solution.py:633
  6.7 1.1 %shard_map.75 = (bf16[512,256]{1,0:T(8,128)(2,1)S(1)}, bf16[512,256]{1,0:T(8,128)(2,1)S(1)}, bf16[512,256]{1,0:T(8,128)(2,1)S(1)}, bf16[512,256]{1,0:T(8,128)(2,1)S(1)}) custom-call(bf16[512,512]{1,0:T(8,128)(2,1)S(1)} %copy-done.2, bf16[512,512]{1,0:T(8,128)(2,1)S(1)} %copy-done.3, bf16[512,512]{1,0:T(8,128)(2,1)S(1)} %copy-done, bf16[512,512]{1,0:T(8,128)(2,1)S(1)} %copy-done.1), custom_call_target="tpu_custom_call" | custom-call | flops 1000 | bytes 1000 | tf_op jit(solution)/shard_map/pallas_call | solution.py:86
  7.8 3.5 %collective-permute-done.refs_1_ = bf16[512,256]{1,0:T(8,128)(2,1)S(1)} collective-permute-done((bf16[512,256]{1,0:T(8,128)(2,1)S(1)}, bf16[512,256]{1,0:T(8,128)(2,1)S(1)}, u32[]{:S(2)}, u32[]{:S(2)}) %collective-permute-start) | collective-permute-done | bytes 262176 | tf_op jit(solution)/shard_map/ppermute | solution.py:633
  11.5 2.5 %collective-permute-start.3 = (bf16[512,256]{1,0:T(8,128)(2,1)S(1)}, bf16[512,256]{1,0:T(8,128)(2,1)S(1)}, u32[]{:S(2)}, u32[]{:S(2)}) collective-permute-start(bf16[512,256]{1,0:T(8,128)(2,1)S(1)} %get-tuple-element.59), channel_id=1, source_target_pairs={{2,4},{3,5},{4,2},{5,3},{6,8},{7,9},{8,6},{9,7},{10,12},{11,13},{1... | collective-permute-start | bytes 786440 | tf_op jit(solution)/shard_map/ppermute | solution.py:637
  14.0 2.9 %collective-permute-done.4.refs_1_ = bf16[512,256]{1,0:T(8,128)(2,1)S(1)} collective-permute-done((bf16[512,256]{1,0:T(8,128)(2,1)S(1)}, bf16[512,256]{1,0:T(8,128)(2,1)S(1)}, u32[]{:S(2)}, u32[]{:S(2)}) %collective-permute-start.4) | collective-permute-done | bytes 262176 | tf_op jit(solution)/shard_map/ppermute | solution.py:633
  17.1 2.5 %collective-permute-start.6 = (bf16[512,256]{1,0:T(8,128)(2,1)S(1)}, bf16[512,256]{1,0:T(8,128)(2,1)S(1)}, u32[]{:S(2)}, u32[]{:S(2)}) collective-permute-start(bf16[512,256]{1,0:T(8,128)(2,1)S(1)} %get-tuple-element.68), channel_id=1, source_target_pairs={{2,4},{3,5},{4,2},{5,3},{6,8},{7,9},{8,6},{9,7},{10,12},{11,13},{1... | collective-permute-start | bytes 786440 | tf_op jit(solution)/shard_map/ppermute | solution.py:637
  19.6 1.8 %collective-permute-done.1.refs_3_ = bf16[512,256]{1,0:T(8,128)(2,1)S(1)} collective-permute-done((bf16[512,256]{1,0:T(8,128)(2,1)S(1)}, bf16[512,256]{1,0:T(8,128)(2,1)S(1)}, u32[]{:S(2)}, u32[]{:S(2)}) %collective-permute-start.1) | collective-permute-done | bytes 262176 | tf_op jit(solution)/shard_map/ppermute | solution.py:633
  21.4 1.5 %collective-permute-start.7 = (bf16[512,256]{1,0:T(8,128)(2,1)S(1)}, bf16[512,256]{1,0:T(8,128)(2,1)S(1)}, u32[]{:S(2)}, u32[]{:S(2)}) collective-permute-start(bf16[512,256]{1,0:T(8,128)(2,1)S(1)} %get-tuple-element.70), channel_id=1, source_target_pairs={{0,1},{1,0},{2,3},{3,2},{4,5},{5,4},{6,7},{7,6},{8,9},{9,8},{10,11... | collective-permute-start | bytes 786440 | tf_op jit(solution)/shard_map/ppermute | solution.py:633
  22.9 5.7 %shard_map.79 = (bf16[2,2,128,256]{3,2,1,0:T(8,128)(2,1)S(1)}, bf16[2,2,128,256]{3,2,1,0:T(8,128)(2,1)S(1)}, f32[1024,256]{1,0:T(8,128)S(1)}, bf16[512,256]{1,0:T(8,128)(2,1)S(1)}, bf16[512,256]{1,0:T(8,128)(2,1)S(1)}) custom-call(bf16[512,256]{1,0:T(8,128)(2,1)S(1)} %get-tuple-element.54.refs_0_, bf16[512,256]{1,0:T(8,128)(2,1)S(1)} %collective-permute-done.refs_1_, ...), custom_call_target="tpu_custom_call" | custom-call | flops 1000 | bytes 1000 | tf_op jit(solution)/shard_map/pallas_call | solution.py:456
  28.6 2.7 %collective-permute-start.9 = (bf16[512,256]{1,0:T(8,128)(2,1)S(1)}, bf16[512,256]{1,0:T(8,128)(2,1)S(1)}, u32[]{:S(2)}, u32[]{:S(2)}) collective-permute-start(bf16[512,256]{1,0:T(8,128)(2,1)S(1)} %get-tuple-element.74), channel_id=1, source_target_pairs={{2,4},{3,5},{4,2},{5,3},{6,8},{7,9},{8,6},{9,7},{10,12},{11,13},{1... | collective-permute-start | bytes 786440 | tf_op jit(solution)/shard_map/ppermute | solution.py:637
  32.0 5.7 %shard_map.82 = (bf16[2,2,128,256]{3,2,1,0:T(8,128)(2,1)S(1)}, bf16[2,2,128,256]{3,2,1,0:T(8,128)(2,1)S(1)}, f32[1024,256]{1,0:T(8,128)S(1)}, bf16[512,256]{1,0:T(8,128)(2,1)S(1)}, bf16[512,256]{1,0:T(8,128)(2,1)S(1)}) custom-call(bf16[512,256]{1,0:T(8,128)(2,1)S(1)} %get-tuple-element.61.refs_0_, bf16[512,256]{1,0:T(8,128)(2,1)S(1)} %collective-permute-done.4.refs_1_, ...), custom_call_target="tpu_custom_call" | custom-call | flops 1000 | bytes 1000 | tf_op jit(solution)/shard_map/pallas_call | solution.py:456
  37.7 1.4 %collective-permute-done.9.refs_2_ = bf16[512,256]{1,0:T(8,128)(2,1)S(1)} collective-permute-done((bf16[512,256]{1,0:T(8,128)(2,1)S(1)}, bf16[512,256]{1,0:T(8,128)(2,1)S(1)}, u32[]{:S(2)}, u32[]{:S(2)}) %collective-permute-start.9) | collective-permute-done | bytes 262176 | tf_op jit(solution)/shard_map/ppermute | solution.py:637
  39.1 2.8 %collective-permute-start.12 = (bf16[512,256]{1,0:T(8,128)(2,1)S(1)}, bf16[512,256]{1,0:T(8,128)(2,1)S(1)}, u32[]{:S(2)}, u32[]{:S(2)}) collective-permute-start(bf16[512,256]{1,0:T(8,128)(2,1)S(1)} %get-tuple-element.85), channel_id=1, source_target_pairs={{2,4},{3,5},{4,2},{5,3},{6,8},{7,9},{8,6},{9,7},{10,12},{11,13},{1... | collective-permute-start | bytes 786440 | tf_op jit(solution)/shard_map/ppermute | solution.py:637
  42.8 1.4 %collective-permute-start.15 = (bf16[512,256]{1,0:T(8,128)(2,1)S(1)}, bf16[512,256]{1,0:T(8,128)(2,1)S(1)}, u32[]{:S(2)}, u32[]{:S(2)}) collective-permute-start(bf16[512,256]{1,0:T(8,128)(2,1)S(1)} %get-tuple-element.99), channel_id=1, source_target_pairs={{0,1},{1,0},{2,3},{3,2},{4,5},{5,4},{6,7},{7,6},{8,9},{9,8},{10,11... | collective-permute-start | bytes 786440 | tf_op jit(solution)/shard_map/ppermute | solution.py:633
  44.2 5.4 %collective-permute-done.12.refs_2_ = bf16[512,256]{1,0:T(8,128)(2,1)S(1)} collective-permute-done((bf16[512,256]{1,0:T(8,128)(2,1)S(1)}, bf16[512,256]{1,0:T(8,128)(2,1)S(1)}, u32[]{:S(2)}, u32[]{:S(2)}) %collective-permute-start.12) | collective-permute-done | bytes 262176 | tf_op jit(solution)/shard_map/ppermute | solution.py:637
  49.6 1.1 %collective-permute-done.13.refs_3_ = bf16[2,2,128,256]{3,2,1,0:T(8,128)(2,1)S(1)} collective-permute-done((bf16[2,2,128,256]{3,2,1,0:T(8,128)(2,1)S(1)}, bf16[2,2,128,256]{3,2,1,0:T(8,128)(2,1)S(1)}, u32[]{:S(2)}, u32[]{:S(2)}) %collective-permute-start.13) | collective-permute-done | bytes 262176 | tf_op jit(solution)/shard_map/ppermute | solution.py:633
  50.8 0.8 %collective-permute-start.14 = (bf16[512,256]{1,0:T(8,128)(2,1)S(1)}, bf16[512,256]{1,0:T(8,128)(2,1)S(1)}, u32[]{:S(2)}, u32[]{:S(2)}) collective-permute-start(bf16[512,256]{1,0:T(8,128)(2,1)S(1)} %get-tuple-element.93), channel_id=1, source_target_pairs={{0,1},{1,0},{2,3},{3,2},{4,5},{5,4},{6,7},{7,6},{8,9},{9,8},{10,11... | collective-permute-start | bytes 786440 | tf_op jit(solution)/shard_map/ppermute | solution.py:633
  51.6 1.7 %shard_map.83 = (bf16[512,512]{1,0:T(8,128)(2,1)}, bf16[512,512]{1,0:T(8,128)(2,1)}) custom-call(bf16[2,2,128,256]{3,2,1,0:T(8,128)(2,1)S(1)} %get-tuple-element.60.refs_0_, bf16[2,2,128,256]{3,2,1,0:T(8,128)(2,1)S(1)} %get-tuple-element.71.refs_1_, bf16[2,2,128,256]{3,2,1,0:T(8,128)(2,1)S(1)} %collective-permute-done.10.refs_2_, ...), custom_call_target="tpu_custom_call" | custom-call | flops 1000 | bytes 1000 | tf_op jit(solution)/shard_map/pallas_call | solution.py:612
  53.3 3.0 %collective-permute-done.15.refs_2_ = bf16[512,256]{1,0:T(8,128)(2,1)S(1)} collective-permute-done((bf16[512,256]{1,0:T(8,128)(2,1)S(1)}, bf16[512,256]{1,0:T(8,128)(2,1)S(1)}, u32[]{:S(2)}, u32[]{:S(2)}) %collective-permute-start.15) | collective-permute-done | bytes 262176 | tf_op jit(solution)/shard_map/ppermute | solution.py:633
  56.3 1.5 %shard_map.86 = (bf16[512,512]{1,0:T(8,128)(2,1)}, bf16[512,512]{1,0:T(8,128)(2,1)}) custom-call(bf16[512,256]{1,0:T(8,128)(2,1)S(1)} %get-tuple-element.97.refs_0_, bf16[512,256]{1,0:T(8,128)(2,1)S(1)} %get-tuple-element.98.refs_1_, bf16[512,256]{1,0:T(8,128)(2,1)S(1)} %collective-permute-done.15.refs_2_), custom_call_target="tpu_custom_call" | custom-call | flops 1000 | bytes 1000 | tf_op jit(solution)/shard_map/pallas_call | solution.py:549
  57.8 4.1 %collective-permute-done.14.refs_0_ = bf16[512,256]{1,0:T(8,128)(2,1)S(1)} collective-permute-done((bf16[512,256]{1,0:T(8,128)(2,1)S(1)}, bf16[512,256]{1,0:T(8,128)(2,1)S(1)}, u32[]{:S(2)}, u32[]{:S(2)}) %collective-permute-start.14) | collective-permute-done | bytes 262176 | tf_op jit(solution)/shard_map/ppermute | solution.py:633
  61.9 1.0 %shard_map.87 = (bf16[512,512]{1,0:T(8,128)(2,1)}, bf16[512,512]{1,0:T(8,128)(2,1)}) custom-call(bf16[512,256]{1,0:T(8,128)(2,1)S(1)} %collective-permute-done.14.refs_0_, bf16[512,512]{1,0:T(8,128)(2,1)} %get-tuple-element.100.refs_1_, bf16[512,512]{1,0:T(8,128)(2,1)} %get-tuple-element.101.refs_2_), custom_call_target="tpu_custom_call", output_to_operand_aliasing={{0}: (1, {}), {1}: (2, {})} | custom-call | flops 1000 | bytes 1000 | tf_op jit(solution)/shard_map/pallas_call | solution.py:582
  (32 shorter events, 4.2 us)
Async XLA Ops:
  0.6 2.9 %copy-start.2 = (bf16[512,512]{1,0:T(8,128)(2,1)S(1)}, bf16[512,512]{1,0:T(8,128)(2,1)}, u32[]{:S(2)}) copy-start(bf16[512,512]{1,0:T(8,128)(2,1)} %refs_0_.2) | copy-start | bytes 1572868
  1.7 1.9 %copy-start.3 = (bf16[512,512]{1,0:T(8,128)(2,1)S(1)}, bf16[512,512]{1,0:T(8,128)(2,1)}, u32[]{:S(2)}) copy-start(bf16[512,512]{1,0:T(8,128)(2,1)} %refs_1_.2) | copy-start | bytes 1572868
  2.0 9.3 %collective-permute-start = (bf16[512,256]{1,0:T(8,128)(2,1)S(1)}, bf16[512,256]{1,0:T(8,128)(2,1)S(1)}, u32[]{:S(2)}, u32[]{:S(2)}) collective-permute-start(bf16[512,256]{1,0:T(8,128)(2,1)S(1)} %shard_map.76), channel_id=1, source_target_pairs={{0,1},{1,0},{2,3},{3,2},{4,5},{5,4},{6,7},{7,6},{8,9},{9,8},{10,11... | collective-permute-start | bytes 786440 | tf_op jit(solution)/shard_map/ppermute | solution.py:633
  3.6 1.1 %copy-start = (bf16[512,512]{1,0:T(8,128)(2,1)S(1)}, bf16[512,512]{1,0:T(8,128)(2,1)}, u32[]{:S(2)}) copy-start(bf16[512,512]{1,0:T(8,128)(2,1)} %refs_0_.3) | copy-start | bytes 1572868
  3.6 1.2 %copy-start.1 = (bf16[512,512]{1,0:T(8,128)(2,1)S(1)}, bf16[512,512]{1,0:T(8,128)(2,1)}, u32[]{:S(2)}) copy-start(bf16[512,512]{1,0:T(8,128)(2,1)} %refs_1_.3) | copy-start | bytes 1572868
  3.9 13.0 %collective-permute-start.4 = (bf16[512,256]{1,0:T(8,128)(2,1)S(1)}, bf16[512,256]{1,0:T(8,128)(2,1)S(1)}, u32[]{:S(2)}, u32[]{:S(2)}) collective-permute-start(bf16[512,256]{1,0:T(8,128)(2,1)S(1)} %shard_map.80), channel_id=1, source_target_pairs={{0,1},{1,0},{2,3},{3,2},{4,5},{5,4},{6,7},{7,6},{8,9},{9,8},{10,11... | collective-permute-start | bytes 786440 | tf_op jit(solution)/shard_map/ppermute | solution.py:633
  5.4 16.0 %collective-permute-start.1 = (bf16[512,256]{1,0:T(8,128)(2,1)S(1)}, bf16[512,256]{1,0:T(8,128)(2,1)S(1)}, u32[]{:S(2)}, u32[]{:S(2)}) collective-permute-start(bf16[512,256]{1,0:T(8,128)(2,1)S(1)} %get-tuple-element.57), channel_id=1, source_target_pairs={{0,1},{1,0},{2,3},{3,2},{4,5},{5,4},{6,7},{7,6},{8,9},{9,8},{10,11... | collective-permute-start | bytes 786440 | tf_op jit(solution)/shard_map/ppermute | solution.py:633
  11.4 11.5 %collective-permute-start.2 = (bf16[512,256]{1,0:T(8,128)(2,1)S(1)}, bf16[512,256]{1,0:T(8,128)(2,1)S(1)}, u32[]{:S(2)}, u32[]{:S(2)}) collective-permute-start(bf16[512,256]{1,0:T(8,128)(2,1)S(1)} %get-tuple-element.58), channel_id=1, source_target_pairs={{0,2},{1,3},{2,0},{3,1},{4,6},{5,7},{6,4},{7,5},{8,10},{9,11},{10,... | collective-permute-start | bytes 786440 | tf_op jit(solution)/shard_map/ppermute | solution.py:636
  11.5 11.4 %collective-permute-start.3 = (bf16[512,256]{1,0:T(8,128)(2,1)S(1)}, bf16[512,256]{1,0:T(8,128)(2,1)S(1)}, u32[]{:S(2)}, u32[]{:S(2)}) collective-permute-start(bf16[512,256]{1,0:T(8,128)(2,1)S(1)} %get-tuple-element.59), channel_id=1, source_target_pairs={{2,4},{3,5},{4,2},{5,3},{6,8},{7,9},{8,6},{9,7},{10,12},{11,13},{1... | collective-permute-start | bytes 786440 | tf_op jit(solution)/shard_map/ppermute | solution.py:637
  17.0 14.3 %collective-permute-start.5 = (bf16[512,256]{1,0:T(8,128)(2,1)S(1)}, bf16[512,256]{1,0:T(8,128)(2,1)S(1)}, u32[]{:S(2)}, u32[]{:S(2)}) collective-permute-start(bf16[512,256]{1,0:T(8,128)(2,1)S(1)} %get-tuple-element.67), channel_id=1, source_target_pairs={{0,2},{1,3},{2,0},{3,1},{4,6},{5,7},{6,4},{7,5},{8,10},{9,11},{10,... | collective-permute-start | bytes 786440 | tf_op jit(solution)/shard_map/ppermute | solution.py:636
  17.1 14.9 %collective-permute-start.6 = (bf16[512,256]{1,0:T(8,128)(2,1)S(1)}, bf16[512,256]{1,0:T(8,128)(2,1)S(1)}, u32[]{:S(2)}, u32[]{:S(2)}) collective-permute-start(bf16[512,256]{1,0:T(8,128)(2,1)S(1)} %get-tuple-element.68), channel_id=1, source_target_pairs={{2,4},{3,5},{4,2},{5,3},{6,8},{7,9},{8,6},{9,7},{10,12},{11,13},{1... | collective-permute-start | bytes 786440 | tf_op jit(solution)/shard_map/ppermute | solution.py:637
  21.4 10.6 %collective-permute-start.7 = (bf16[512,256]{1,0:T(8,128)(2,1)S(1)}, bf16[512,256]{1,0:T(8,128)(2,1)S(1)}, u32[]{:S(2)}, u32[]{:S(2)}) collective-permute-start(bf16[512,256]{1,0:T(8,128)(2,1)S(1)} %get-tuple-element.70), channel_id=1, source_target_pairs={{0,1},{1,0},{2,3},{3,2},{4,5},{5,4},{6,7},{7,6},{8,9},{9,8},{10,11... | collective-permute-start | bytes 786440 | tf_op jit(solution)/shard_map/ppermute | solution.py:633
  28.5 9.1 %collective-permute-start.8 = (bf16[512,256]{1,0:T(8,128)(2,1)S(1)}, bf16[512,256]{1,0:T(8,128)(2,1)S(1)}, u32[]{:S(2)}, u32[]{:S(2)}) collective-permute-start(bf16[512,256]{1,0:T(8,128)(2,1)S(1)} %get-tuple-element.73), channel_id=1, source_target_pairs={{0,2},{1,3},{2,0},{3,1},{4,6},{5,7},{6,4},{7,5},{8,10},{9,11},{10,... | collective-permute-start | bytes 786440 | tf_op jit(solution)/shard_map/ppermute | solution.py:636
  28.6 10.5 %collective-permute-start.9 = (bf16[512,256]{1,0:T(8,128)(2,1)S(1)}, bf16[512,256]{1,0:T(8,128)(2,1)S(1)}, u32[]{:S(2)}, u32[]{:S(2)}) collective-permute-start(bf16[512,256]{1,0:T(8,128)(2,1)S(1)} %get-tuple-element.74), channel_id=1, source_target_pairs={{2,4},{3,5},{4,2},{5,3},{6,8},{7,9},{8,6},{9,7},{10,12},{11,13},{1... | collective-permute-start | bytes 786440 | tf_op jit(solution)/shard_map/ppermute | solution.py:637
  31.3 11.3 %collective-permute-start.10 = (bf16[2,2,128,256]{3,2,1,0:T(8,128)(2,1)S(1)}, bf16[2,2,128,256]{3,2,1,0:T(8,128)(2,1)S(1)}, u32[]{:S(2)}, u32[]{:S(2)}) collective-permute-start(bf16[2,2,128,256]{3,2,1,0:T(8,128)(2,1)S(1)} %get-tuple-element.81), channel_id=1, source_target_pairs={{0,1},{1,0},{2,3},{3,2},{4,5},{5,4},{6,7},{7,6},{8,9},{9,8},{10,11... | collective-permute-start | bytes 786440 | tf_op jit(solution)/shard_map/ppermute | solution.py:633
  39.1 5.1 %collective-permute-start.11 = (bf16[512,256]{1,0:T(8,128)(2,1)S(1)}, bf16[512,256]{1,0:T(8,128)(2,1)S(1)}, u32[]{:S(2)}, u32[]{:S(2)}) collective-permute-start(bf16[512,256]{1,0:T(8,128)(2,1)S(1)} %get-tuple-element.84), channel_id=1, source_target_pairs={{0,2},{1,3},{2,0},{3,1},{4,6},{5,7},{6,4},{7,5},{8,10},{9,11},{10,... | collective-permute-start | bytes 786440 | tf_op jit(solution)/shard_map/ppermute | solution.py:636
  39.1 10.5 %collective-permute-start.12 = (bf16[512,256]{1,0:T(8,128)(2,1)S(1)}, bf16[512,256]{1,0:T(8,128)(2,1)S(1)}, u32[]{:S(2)}, u32[]{:S(2)}) collective-permute-start(bf16[512,256]{1,0:T(8,128)(2,1)S(1)} %get-tuple-element.85), channel_id=1, source_target_pairs={{2,4},{3,5},{4,2},{5,3},{6,8},{7,9},{8,6},{9,7},{10,12},{11,13},{1... | collective-permute-start | bytes 786440 | tf_op jit(solution)/shard_map/ppermute | solution.py:637
  41.9 8.8 %collective-permute-start.13 = (bf16[2,2,128,256]{3,2,1,0:T(8,128)(2,1)S(1)}, bf16[2,2,128,256]{3,2,1,0:T(8,128)(2,1)S(1)}, u32[]{:S(2)}, u32[]{:S(2)}) collective-permute-start(bf16[2,2,128,256]{3,2,1,0:T(8,128)(2,1)S(1)} %get-tuple-element.86), channel_id=1, source_target_pairs={{0,1},{1,0},{2,3},{3,2},{4,5},{5,4},{6,7},{7,6},{8,9},{9,8},{10,11... | collective-permute-start | bytes 786440 | tf_op jit(solution)/shard_map/ppermute | solution.py:633
  42.8 13.5 %collective-permute-start.15 = (bf16[512,256]{1,0:T(8,128)(2,1)S(1)}, bf16[512,256]{1,0:T(8,128)(2,1)S(1)}, u32[]{:S(2)}, u32[]{:S(2)}) collective-permute-start(bf16[512,256]{1,0:T(8,128)(2,1)S(1)} %get-tuple-element.99), channel_id=1, source_target_pairs={{0,1},{1,0},{2,3},{3,2},{4,5},{5,4},{6,7},{7,6},{8,9},{9,8},{10,11... | collective-permute-start | bytes 786440 | tf_op jit(solution)/shard_map/ppermute | solution.py:633
  50.8 11.1 %collective-permute-start.14 = (bf16[512,256]{1,0:T(8,128)(2,1)S(1)}, bf16[512,256]{1,0:T(8,128)(2,1)S(1)}, u32[]{:S(2)}, u32[]{:S(2)}) collective-permute-start(bf16[512,256]{1,0:T(8,128)(2,1)S(1)} %get-tuple-element.93), channel_id=1, source_target_pairs={{0,1},{1,0},{2,3},{3,2},{4,5},{5,4},{6,7},{7,6},{8,9},{9,8},{10,11... | collective-permute-start | bytes 786440 | tf_op jit(solution)/shard_map/ppermute | solution.py:633

commit v21 on v19

--- a/solution.py
+++ b/solution.py
@@ -172,6 +172,32 @@
         in_specs=[vmem(), vmem()],
         out_specs=[vmem(), vmem()],
         out_shape=[shape, shape],
+        compiler_params=small(),
+        cost_estimate=light(),
+    )(own, got)
+
+
+def turn_kernel(where, own, got, raw_t, one, one_t):
+    for side, ref in ((where[0], own), (1 - where[0], got)):
+        for i in range(2):
+            rows = slice(i * PARENT, (i + 1) * PARENT)
+            at = pl.ds(pl.multiple_of((side * 2 + i) * PARENT, PARENT), PARENT)
+            half = pl.ds(pl.multiple_of((side * 2 + i) * BLOCK, BLOCK), BLOCK)
+            for n in range(2):
+                x = ref[rows, n * HEAD : (n + 1) * HEAD]
+                raw_t[n, :, at] = x.T
+                x = pool1(x)
+                one[n, half, :] = x
+                one_t[n, :, half] = x.T
+
+
+def turn(where, own, got):
+    shapes = ((2, HEAD, 1024), (2, 512, HEAD), (2, HEAD, 512))
+    return pl.pallas_call(
+        placed(turn_kernel, where),
+        in_specs=[vmem()] * 2,
+        out_specs=[vmem()] * 3,
+        out_shape=[jax.ShapeDtypeStruct(shape, BF) for shape in shapes],
         compiler_params=small(),
         cost_estimate=light(),
     )(own, got)
@@ -241,13 +267,14 @@
 
 
 def main_kernel(qg_first, where, kv_own, kv_got, *refs):
+    turned, refs = refs[:3], refs[3:]
     if qg_first:
         refs = (*refs[2:4], *refs[:2], *refs[4:])
-    one_chunk(where, kv_own, kv_got, *refs)
+    one_chunk(where, turned, kv_own, kv_got, *refs)
 
 
 def one_chunk(
-    where, kv_own, kv_got, near_got, wide_got, qg_own, qg_got,
+    where, turned, kv_own, kv_got, near_got, wide_got, qg_own, qg_got,
     oq_own, oq_far, grad, near_out, wide_out,
     raw, raw_t, one, one_t, two, two_t, qs, gs, p0, p1, p2, acc0, acc1, acc2, oq, halos,
 ):
@@ -270,11 +297,12 @@
             raw[n, pl.ds(256 + own_at, 512), :] = kv_own[:, cols]
             raw[n, pl.ds(256 + got_at, 512), :] = kv_got[:, cols]
             raw[n, 1280:1536, :] = from_right[0:256, cols]
+            raw_t[n, :, 256:1280] = turned[0][n]
+            one[n, 256:768, :] = turned[1][n]
+            one_t[n, :, 256:768] = turned[2][n]
             one[n, 0:128, :] = from_left[256:384, cols]
-            for i in range(6):
-                block = pool1(raw[n, i * PARENT : (i + 1) * PARENT, :])
-                at = (i + 1) * BLOCK
-                one[n, at : at + BLOCK, :] = block
+            one[n, 128:256, :] = pool1(raw[n, 0:256, :])
+            one[n, 768:896, :] = pool1(raw[n, 1280:1536, :])
             one[n, 896:1024, :] = from_right[256:384, cols]
             two[n, 0:128, :] = from_left[384:512, cols]
             two[n, 128:192, :] = pool12(one[n, 0:128, :])
@@ -282,10 +310,10 @@
             two[n, 256:320, :] = pool2(raw[n, 1280:1536, :])
             two[n, 320:384, :] = pool12(one[n, 896:1024, :])
             two[n, 384:512, :] = from_right[384:512, cols]
-            for i in range(6):
+            for i in (0, 5):
                 rows = slice(i * PARENT, (i + 1) * PARENT)
                 raw_t[n, :, rows] = raw[n, rows, :].T
-            for i in range(8):
+            for i in (0, 1, 6, 7):
                 rows = slice(i * BLOCK, (i + 1) * BLOCK)
                 one_t[n, :, rows] = one[n, rows, :].T
             for i in range(4):
@@ -445,7 +473,7 @@
     wide_out[...] = halos[odd]
 
 
-def main(where, kv_own, kv_got, near_got, wide_got, qg_own, qg_got, qg_first):
+def main(where, turned, kv_own, kv_got, near_got, wide_got, qg_own, qg_got, qg_first):
     rows, both = kv_own.shape
     width = both // 2
     oq_shape = jax.ShapeDtypeStruct((2, 2, width, PARENT), BF)
@@ -453,9 +481,10 @@
     operands = [kv_own, kv_got, near_got, wide_got, qg_own, qg_got]
     if qg_first:
         operands = operands[:2] + operands[4:] + operands[2:4]
+    operands[2:2] = turned
     return pl.pallas_call(
         placed(functools.partial(main_kernel, qg_first), where),
-        in_specs=[vmem()] * 6,
+        in_specs=[vmem()] * 9,
         out_specs=[vmem()] * 5,
         out_shape=[
             oq_shape,
@@ -651,7 +680,7 @@
         if c > 0:
             near, wide, far = lax.optimization_barrier((near, wide, far))
         near, wide = beside(near, wide)
-        own, far, grad, near, wide = main(where, kv[c], got_kv, near, wide, qg[c], swap(far), c == 0)
+        own, far, grad, near, wide = main(where, turn(where, kv[c], got_kv), kv[c], got_kv, near, wide, qg[c], swap(far), c == 0)
         oq_own.append(own)
         oq_got.append(swap(far))
         if c > 0:

time: 59.5 us -> 59.5 us (level)
  no operation moved by 1% of the time
where the time goes in v21:
time: 59.5 us; the launch traced here: 59.3 us
  starting transfers between devices  20.4 us (34%)
  Pallas kernels  18.5 us (31%)
  waiting for transfers between devices  18.2 us (31%)
  local copies, waits for them, and re-layouts  1.23 us (2%)
  between operations  1.02 us (2%)
    ppermute x8, waiting for transfers between devices, swap(): return lax.ppermute(x, axes, across)  14.7 us
    pallas_call x2, Pallas kernels, main(): pl.pallas_call(placed(functools.partial(main_kernel, qg_first), where), i...  11.1 us
    ppermute x4, starting transfers between devices, beside(): return (near, lax.ppermute(wide, axes, wide_edges))  10.6 us
    ppermute x8, starting transfers between devices, swap(): return lax.ppermute(x, axes, across)  9.03 us
    ppermute x4, waiting for transfers between devices, beside(): return (near, lax.ppermute(wide, axes, wide_edges))  3.46 us
    pallas_call x1, Pallas kernels, unpack_columns(): pl.pallas_call(placed(unpack_columns_kernel, where), in_specs=[vmem()] *...  1.68 us
    pallas_call x2, Pallas kernels, pack(): pl.pallas_call(placed(functools.partial(pack_kernel, own), where), in_spe...  1.65 us
    pallas_call x1, Pallas kernels, unpack_rows(): pl.pallas_call(placed(unpack_rows_kernel, where), in_specs=[vmem()] * (CH...  1.53 us
  transfers between devices with their start and end apart: 16, of which 6 were waited for; matrix products, arithmetic and copies ran while one was open for 0% of the time, Pallas kernels for 29%

profile of v21, /device:TPU:12, one launch (start us, length us, event | category | flops | bytes accessed | tf_op | source)
XLA Modules:
  0.0 59.3 jit_solution(9122420120796946784)
XLA Ops:
  0.7 1.1 %constant_dynamic-slice_fusion.2 = (bf16[512,128]{1,0:T(8,128)(2,1)S(1)}, bf16[512,128]{1,0:T(8,128)(2,1)S(1)}) fusion(bf16[512,512]{1,0:T(8,128)(2,1)} %refs_1_.2, s32[]{:T(128)S(6)} %select_n.18, bf16[512,512]{1,0:T(8,128)(2,1)} %refs_0_.2), kind=kLoop, calls=%fused_computation.2 | loop fusion | bytes 524292 | tf_op jit(solution)/shard_map/dynamic_slice | solution.py:112
  2.0 1.6 %collective-permute-start = (bf16[512,256]{1,0:T(8,128)(2,1)S(1)}, bf16[512,256]{1,0:T(8,128)(2,1)S(1)}, u32[]{:S(2)}, u32[]{:S(2)}) collective-permute-start(bf16[512,256]{1,0:T(8,128)(2,1)S(1)} %shard_map.76), channel_id=1, source_target_pairs={{0,1},{1,0},{2,3},{3,2},{4,5},{5,4},{6,7},{7,6},{8,9},{9,8},{10,11... | collective-permute-start | bytes 786440 | tf_op jit(solution)/shard_map/ppermute | solution.py:662
  3.9 0.7 %collective-permute-start.4 = (bf16[512,256]{1,0:T(8,128)(2,1)S(1)}, bf16[512,256]{1,0:T(8,128)(2,1)S(1)}, u32[]{:S(2)}, u32[]{:S(2)}) collective-permute-start(bf16[512,256]{1,0:T(8,128)(2,1)S(1)} %shard_map.81), channel_id=1, source_target_pairs={{0,1},{1,0},{2,3},{3,2},{4,5},{5,4},{6,7},{7,6},{8,9},{9,8},{10,11... | collective-permute-start | bytes 786440 | tf_op jit(solution)/shard_map/ppermute | solution.py:662
  5.4 1.3 %collective-permute-start.1 = (bf16[512,256]{1,0:T(8,128)(2,1)S(1)}, bf16[512,256]{1,0:T(8,128)(2,1)S(1)}, u32[]{:S(2)}, u32[]{:S(2)}) collective-permute-start(bf16[512,256]{1,0:T(8,128)(2,1)S(1)} %get-tuple-element.65), channel_id=1, source_target_pairs={{0,1},{1,0},{2,3},{3,2},{4,5},{5,4},{6,7},{7,6},{8,9},{9,8},{10,11... | collective-permute-start | bytes 786440 | tf_op jit(solution)/shard_map/ppermute | solution.py:662
  6.7 1.1 %shard_map.75 = (bf16[512,256]{1,0:T(8,128)(2,1)S(1)}, bf16[512,256]{1,0:T(8,128)(2,1)S(1)}, bf16[512,256]{1,0:T(8,128)(2,1)S(1)}, bf16[512,256]{1,0:T(8,128)(2,1)S(1)}) custom-call(bf16[512,512]{1,0:T(8,128)(2,1)S(1)} %copy-done.2, bf16[512,512]{1,0:T(8,128)(2,1)S(1)} %copy-done.3, bf16[512,512]{1,0:T(8,128)(2,1)S(1)} %copy-done, bf16[512,512]{1,0:T(8,128)(2,1)S(1)} %copy-done.1), custom_call_target="tpu_custom_call" | custom-call | flops 1000 | bytes 1000 | tf_op jit(solution)/shard_map/pallas_call | solution.py:86
  7.8 3.5 %collective-permute-done.refs_1_ = bf16[512,256]{1,0:T(8,128)(2,1)S(1)} collective-permute-done((bf16[512,256]{1,0:T(8,128)(2,1)S(1)}, bf16[512,256]{1,0:T(8,128)(2,1)S(1)}, u32[]{:S(2)}, u32[]{:S(2)}) %collective-permute-start) | collective-permute-done | bytes 262176 | tf_op jit(solution)/shard_map/ppermute | solution.py:662
  11.5 2.5 %collective-permute-start.3 = (bf16[512,256]{1,0:T(8,128)(2,1)S(1)}, bf16[512,256]{1,0:T(8,128)(2,1)S(1)}, u32[]{:S(2)}, u32[]{:S(2)}) collective-permute-start(bf16[512,256]{1,0:T(8,128)(2,1)S(1)} %get-tuple-element.67), channel_id=1, source_target_pairs={{2,4},{3,5},{4,2},{5,3},{6,8},{7,9},{8,6},{9,7},{10,12},{11,13},{1... | collective-permute-start | bytes 786440 | tf_op jit(solution)/shard_map/ppermute | solution.py:666
  14.0 2.9 %collective-permute-done.4.refs_1_ = bf16[512,256]{1,0:T(8,128)(2,1)S(1)} collective-permute-done((bf16[512,256]{1,0:T(8,128)(2,1)S(1)}, bf16[512,256]{1,0:T(8,128)(2,1)S(1)}, u32[]{:S(2)}, u32[]{:S(2)}) %collective-permute-start.4) | collective-permute-done | bytes 262176 | tf_op jit(solution)/shard_map/ppermute | solution.py:662
  17.1 2.5 %collective-permute-start.6 = (bf16[512,256]{1,0:T(8,128)(2,1)S(1)}, bf16[512,256]{1,0:T(8,128)(2,1)S(1)}, u32[]{:S(2)}, u32[]{:S(2)}) collective-permute-start(bf16[512,256]{1,0:T(8,128)(2,1)S(1)} %get-tuple-element.79), channel_id=1, source_target_pairs={{2,4},{3,5},{4,2},{5,3},{6,8},{7,9},{8,6},{9,7},{10,12},{11,13},{1... | collective-permute-start | bytes 786440 | tf_op jit(solution)/shard_map/ppermute | solution.py:666
  19.9 1.5 %collective-permute-done.1.refs_6_ = bf16[512,256]{1,0:T(8,128)(2,1)S(1)} collective-permute-done((bf16[512,256]{1,0:T(8,128)(2,1)S(1)}, bf16[512,256]{1,0:T(8,128)(2,1)S(1)}, u32[]{:S(2)}, u32[]{:S(2)}) %collective-permute-start.1) | collective-permute-done | bytes 262176 | tf_op jit(solution)/shard_map/ppermute | solution.py:662
  21.4 1.5 %collective-permute-start.7 = (bf16[512,256]{1,0:T(8,128)(2,1)S(1)}, bf16[512,256]{1,0:T(8,128)(2,1)S(1)}, u32[]{:S(2)}, u32[]{:S(2)}) collective-permute-start(bf16[512,256]{1,0:T(8,128)(2,1)S(1)} %get-tuple-element.81), channel_id=1, source_target_pairs={{0,1},{1,0},{2,3},{3,2},{4,5},{5,4},{6,7},{7,6},{8,9},{9,8},{10,11... | collective-permute-start | bytes 786440 | tf_op jit(solution)/shard_map/ppermute | solution.py:662
  22.9 5.5 %shard_map.80 = (bf16[2,2,128,256]{3,2,1,0:T(8,128)(2,1)S(1)}, bf16[2,2,128,256]{3,2,1,0:T(8,128)(2,1)S(1)}, f32[1024,256]{1,0:T(8,128)S(1)}, bf16[512,256]{1,0:T(8,128)(2,1)S(1)}, bf16[512,256]{1,0:T(8,128)(2,1)S(1)}) custom-call(bf16[512,256]{1,0:T(8,128)(2,1)S(1)} %get-tuple-element.59.refs_0_, bf16[512,256]{1,0:T(8,128)(2,1)S(1)} %collective-permute-done.refs_1_, ...), custom_call_target="tpu_custom_call" | custom-call | flops 1000 | bytes 1000 | tf_op jit(solution)/shard_map/pallas_call | solution.py:485
  28.5 2.7 %collective-permute-start.10 = (bf16[512,256]{1,0:T(8,128)(2,1)S(1)}, bf16[512,256]{1,0:T(8,128)(2,1)S(1)}, u32[]{:S(2)}, u32[]{:S(2)}) collective-permute-start(bf16[512,256]{1,0:T(8,128)(2,1)S(1)} %get-tuple-element.86), channel_id=1, source_target_pairs={{2,4},{3,5},{4,2},{5,3},{6,8},{7,9},{8,6},{9,7},{10,12},{11,13},{1... | collective-permute-start | bytes 786440 | tf_op jit(solution)/shard_map/ppermute | solution.py:666
  31.5 0.7 %collective-permute-start.8 = (bf16[2,2,128,256]{3,2,1,0:T(8,128)(2,1)S(1)}, bf16[2,2,128,256]{3,2,1,0:T(8,128)(2,1)S(1)}, u32[]{:S(2)}, u32[]{:S(2)}) collective-permute-start(bf16[2,2,128,256]{3,2,1,0:T(8,128)(2,1)S(1)} %get-tuple-element.83), channel_id=1, source_target_pairs={{0,1},{1,0},{2,3},{3,2},{4,5},{5,4},{6,7},{7,6},{8,9},{9,8},{10,11... | collective-permute-start | bytes 786440 | tf_op jit(solution)/shard_map/ppermute | solution.py:662
  32.1 5.5 %shard_map.84 = (bf16[2,2,128,256]{3,2,1,0:T(8,128)(2,1)S(1)}, bf16[2,2,128,256]{3,2,1,0:T(8,128)(2,1)S(1)}, f32[1024,256]{1,0:T(8,128)S(1)}, bf16[512,256]{1,0:T(8,128)(2,1)S(1)}, bf16[512,256]{1,0:T(8,128)(2,1)S(1)}) custom-call(bf16[512,256]{1,0:T(8,128)(2,1)S(1)} %get-tuple-element.69.refs_0_, bf16[512,256]{1,0:T(8,128)(2,1)S(1)} %collective-permute-done.4.refs_1_, ...), custom_call_target="tpu_custom_call" | custom-call | flops 1000 | bytes 1000 | tf_op jit(solution)/shard_map/pallas_call | solution.py:485
  37.7 1.5 %collective-permute-start.11 = (bf16[2,2,128,256]{3,2,1,0:T(8,128)(2,1)S(1)}, bf16[2,2,128,256]{3,2,1,0:T(8,128)(2,1)S(1)}, u32[]{:S(2)}, u32[]{:S(2)}) collective-permute-start(bf16[2,2,128,256]{3,2,1,0:T(8,128)(2,1)S(1)} %get-tuple-element.93), channel_id=1, source_target_pairs={{0,1},{1,0},{2,3},{3,2},{4,5},{5,4},{6,7},{7,6},{8,9},{9,8},{10,11... | collective-permute-start | bytes 786440 | tf_op jit(solution)/shard_map/ppermute | solution.py:662
  39.6 2.9 %collective-permute-start.13 = (bf16[512,256]{1,0:T(8,128)(2,1)S(1)}, bf16[512,256]{1,0:T(8,128)(2,1)S(1)}, u32[]{:S(2)}, u32[]{:S(2)}) collective-permute-start(bf16[512,256]{1,0:T(8,128)(2,1)S(1)} %get-tuple-element.96), channel_id=1, source_target_pairs={{2,4},{3,5},{4,2},{5,3},{6,8},{7,9},{8,6},{9,7},{10,12},{11,13},{1... | collective-permute-start | bytes 786440 | tf_op jit(solution)/shard_map/ppermute | solution.py:666
  43.4 3.2 %collective-permute-done.11.refs_3_ = bf16[2,2,128,256]{3,2,1,0:T(8,128)(2,1)S(1)} collective-permute-done((bf16[2,2,128,256]{3,2,1,0:T(8,128)(2,1)S(1)}, bf16[2,2,128,256]{3,2,1,0:T(8,128)(2,1)S(1)}, u32[]{:S(2)}, u32[]{:S(2)}) %collective-permute-start.11) | collective-permute-done | bytes 262176 | tf_op jit(solution)/shard_map/ppermute | solution.py:662
  46.7 3.5 %collective-permute-done.13.refs_2_ = bf16[512,256]{1,0:T(8,128)(2,1)S(1)} collective-permute-done((bf16[512,256]{1,0:T(8,128)(2,1)S(1)}, bf16[512,256]{1,0:T(8,128)(2,1)S(1)}, u32[]{:S(2)}, u32[]{:S(2)}) %collective-permute-start.13) | collective-permute-done | bytes 262176 | tf_op jit(solution)/shard_map/ppermute | solution.py:666
  50.3 1.1 %collective-permute-start.14 = (bf16[512,256]{1,0:T(8,128)(2,1)S(1)}, bf16[512,256]{1,0:T(8,128)(2,1)S(1)}, u32[]{:S(2)}, u32[]{:S(2)}) collective-permute-start(bf16[512,256]{1,0:T(8,128)(2,1)S(1)} %get-tuple-element.103), channel_id=1, source_target_pairs={{0,1},{1,0},{2,3},{3,2},{4,5},{5,4},{6,7},{7,6},{8,9},{9,8},{10,11... | collective-permute-start | bytes 786440 | tf_op jit(solution)/shard_map/ppermute | solution.py:662
  51.4 1.7 %shard_map.85 = (bf16[512,512]{1,0:T(8,128)(2,1)}, bf16[512,512]{1,0:T(8,128)(2,1)}) custom-call(bf16[2,2,128,256]{3,2,1,0:T(8,128)(2,1)S(1)} %get-tuple-element.68.refs_0_, bf16[2,2,128,256]{3,2,1,0:T(8,128)(2,1)S(1)} %get-tuple-element.82.refs_1_, bf16[2,2,128,256]{3,2,1,0:T(8,128)(2,1)S(1)} %collective-permute-done.8.refs_2_, ...), custom_call_target="tpu_custom_call" | custom-call | flops 1000 | bytes 1000 | tf_op jit(solution)/shard_map/pallas_call | solution.py:641
  53.1 1.5 %shard_map.88 = (bf16[512,512]{1,0:T(8,128)(2,1)}, bf16[512,512]{1,0:T(8,128)(2,1)}) custom-call(bf16[512,256]{1,0:T(8,128)(2,1)S(1)} %get-tuple-element.107.refs_0_, bf16[512,256]{1,0:T(8,128)(2,1)S(1)} %get-tuple-element.108.refs_1_, bf16[512,256]{1,0:T(8,128)(2,1)S(1)} %collective-permute-done.15.refs_2_), custom_call_target="tpu_custom_call" | custom-call | flops 1000 | bytes 1000 | tf_op jit(solution)/shard_map/pallas_call | solution.py:578
  54.6 3.6 %collective-permute-done.14.refs_0_ = bf16[512,256]{1,0:T(8,128)(2,1)S(1)} collective-permute-done((bf16[512,256]{1,0:T(8,128)(2,1)S(1)}, bf16[512,256]{1,0:T(8,128)(2,1)S(1)}, u32[]{:S(2)}, u32[]{:S(2)}) %collective-permute-start.14) | collective-permute-done | bytes 262176 | tf_op jit(solution)/shard_map/ppermute | solution.py:662
  58.1 1.0 %shard_map.89 = (bf16[512,512]{1,0:T(8,128)(2,1)}, bf16[512,512]{1,0:T(8,128)(2,1)}) custom-call(bf16[512,256]{1,0:T(8,128)(2,1)S(1)} %collective-permute-done.14.refs_0_, bf16[512,512]{1,0:T(8,128)(2,1)} %get-tuple-element.110.refs_1_, bf16[512,512]{1,0:T(8,128)(2,1)} %get-tuple-element.111.refs_2_), custom_call_target="tpu_custom_call", output_to_operand_aliasing={{0}: (1, {}), {1}: (2, {})} | custom-call | flops 1000 | bytes 1000 | tf_op jit(solution)/shard_map/pallas_call | solution.py:611
  (34 shorter events, 3.8 us)
Async XLA Ops:
  0.6 2.9 %copy-start.2 = (bf16[512,512]{1,0:T(8,128)(2,1)S(1)}, bf16[512,512]{1,0:T(8,128)(2,1)}, u32[]{:S(2)}) copy-start(bf16[512,512]{1,0:T(8,128)(2,1)} %refs_0_.2) | copy-start | bytes 1572868
  1.7 1.9 %copy-start.3 = (bf16[512,512]{1,0:T(8,128)(2,1)S(1)}, bf16[512,512]{1,0:T(8,128)(2,1)}, u32[]{:S(2)}) copy-start(bf16[512,512]{1,0:T(8,128)(2,1)} %refs_1_.2) | copy-start | bytes 1572868
  2.0 9.3 %collective-permute-start = (bf16[512,256]{1,0:T(8,128)(2,1)S(1)}, bf16[512,256]{1,0:T(8,128)(2,1)S(1)}, u32[]{:S(2)}, u32[]{:S(2)}) collective-permute-start(bf16[512,256]{1,0:T(8,128)(2,1)S(1)} %shard_map.76), channel_id=1, source_target_pairs={{0,1},{1,0},{2,3},{3,2},{4,5},{5,4},{6,7},{7,6},{8,9},{9,8},{10,11... | collective-permute-start | bytes 786440 | tf_op jit(solution)/shard_map/ppermute | solution.py:662
  3.6 1.1 %copy-start = (bf16[512,512]{1,0:T(8,128)(2,1)S(1)}, bf16[512,512]{1,0:T(8,128)(2,1)}, u32[]{:S(2)}) copy-start(bf16[512,512]{1,0:T(8,128)(2,1)} %refs_0_.3) | copy-start | bytes 1572868
  3.6 1.2 %copy-start.1 = (bf16[512,512]{1,0:T(8,128)(2,1)S(1)}, bf16[512,512]{1,0:T(8,128)(2,1)}, u32[]{:S(2)}) copy-start(bf16[512,512]{1,0:T(8,128)(2,1)} %refs_1_.3) | copy-start | bytes 1572868
  3.9 13.0 %collective-permute-start.4 = (bf16[512,256]{1,0:T(8,128)(2,1)S(1)}, bf16[512,256]{1,0:T(8,128)(2,1)S(1)}, u32[]{:S(2)}, u32[]{:S(2)}) collective-permute-start(bf16[512,256]{1,0:T(8,128)(2,1)S(1)} %shard_map.81), channel_id=1, source_target_pairs={{0,1},{1,0},{2,3},{3,2},{4,5},{5,4},{6,7},{7,6},{8,9},{9,8},{10,11... | collective-permute-start | bytes 786440 | tf_op jit(solution)/shard_map/ppermute | solution.py:662
  5.4 16.0 %collective-permute-start.1 = (bf16[512,256]{1,0:T(8,128)(2,1)S(1)}, bf16[512,256]{1,0:T(8,128)(2,1)S(1)}, u32[]{:S(2)}, u32[]{:S(2)}) collective-permute-start(bf16[512,256]{1,0:T(8,128)(2,1)S(1)} %get-tuple-element.65), channel_id=1, source_target_pairs={{0,1},{1,0},{2,3},{3,2},{4,5},{5,4},{6,7},{7,6},{8,9},{9,8},{10,11... | collective-permute-start | bytes 786440 | tf_op jit(solution)/shard_map/ppermute | solution.py:662
  11.4 11.5 %collective-permute-start.2 = (bf16[512,256]{1,0:T(8,128)(2,1)S(1)}, bf16[512,256]{1,0:T(8,128)(2,1)S(1)}, u32[]{:S(2)}, u32[]{:S(2)}) collective-permute-start(bf16[512,256]{1,0:T(8,128)(2,1)S(1)} %get-tuple-element.66), channel_id=1, source_target_pairs={{0,2},{1,3},{2,0},{3,1},{4,6},{5,7},{6,4},{7,5},{8,10},{9,11},{10,... | collective-permute-start | bytes 786440 | tf_op jit(solution)/shard_map/ppermute | solution.py:665
  11.5 11.4 %collective-permute-start.3 = (bf16[512,256]{1,0:T(8,128)(2,1)S(1)}, bf16[512,256]{1,0:T(8,128)(2,1)S(1)}, u32[]{:S(2)}, u32[]{:S(2)}) collective-permute-start(bf16[512,256]{1,0:T(8,128)(2,1)S(1)} %get-tuple-element.67), channel_id=1, source_target_pairs={{2,4},{3,5},{4,2},{5,3},{6,8},{7,9},{8,6},{9,7},{10,12},{11,13},{1... | collective-permute-start | bytes 786440 | tf_op jit(solution)/shard_map/ppermute | solution.py:666
  17.0 14.4 %collective-permute-start.5 = (bf16[512,256]{1,0:T(8,128)(2,1)S(1)}, bf16[512,256]{1,0:T(8,128)(2,1)S(1)}, u32[]{:S(2)}, u32[]{:S(2)}) collective-permute-start(bf16[512,256]{1,0:T(8,128)(2,1)S(1)} %get-tuple-element.78), channel_id=1, source_target_pairs={{0,2},{1,3},{2,0},{3,1},{4,6},{5,7},{6,4},{7,5},{8,10},{9,11},{10,... | collective-permute-start | bytes 786440 | tf_op jit(solution)/shard_map/ppermute | solution.py:665
  17.1 15.0 %collective-permute-start.6 = (bf16[512,256]{1,0:T(8,128)(2,1)S(1)}, bf16[512,256]{1,0:T(8,128)(2,1)S(1)}, u32[]{:S(2)}, u32[]{:S(2)}) collective-permute-start(bf16[512,256]{1,0:T(8,128)(2,1)S(1)} %get-tuple-element.79), channel_id=1, source_target_pairs={{2,4},{3,5},{4,2},{5,3},{6,8},{7,9},{8,6},{9,7},{10,12},{11,13},{1... | collective-permute-start | bytes 786440 | tf_op jit(solution)/shard_map/ppermute | solution.py:666
  21.4 10.8 %collective-permute-start.7 = (bf16[512,256]{1,0:T(8,128)(2,1)S(1)}, bf16[512,256]{1,0:T(8,128)(2,1)S(1)}, u32[]{:S(2)}, u32[]{:S(2)}) collective-permute-start(bf16[512,256]{1,0:T(8,128)(2,1)S(1)} %get-tuple-element.81), channel_id=1, source_target_pairs={{0,1},{1,0},{2,3},{3,2},{4,5},{5,4},{6,7},{7,6},{8,9},{9,8},{10,11... | collective-permute-start | bytes 786440 | tf_op jit(solution)/shard_map/ppermute | solution.py:662
  28.4 10.8 %collective-permute-start.9 = (bf16[512,256]{1,0:T(8,128)(2,1)S(1)}, bf16[512,256]{1,0:T(8,128)(2,1)S(1)}, u32[]{:S(2)}, u32[]{:S(2)}) collective-permute-start(bf16[512,256]{1,0:T(8,128)(2,1)S(1)} %get-tuple-element.85), channel_id=1, source_target_pairs={{0,2},{1,3},{2,0},{3,1},{4,6},{5,7},{6,4},{7,5},{8,10},{9,11},{10,... | collective-permute-start | bytes 786440 | tf_op jit(solution)/shard_map/ppermute | solution.py:665
  28.5 10.7 %collective-permute-start.10 = (bf16[512,256]{1,0:T(8,128)(2,1)S(1)}, bf16[512,256]{1,0:T(8,128)(2,1)S(1)}, u32[]{:S(2)}, u32[]{:S(2)}) collective-permute-start(bf16[512,256]{1,0:T(8,128)(2,1)S(1)} %get-tuple-element.86), channel_id=1, source_target_pairs={{2,4},{3,5},{4,2},{5,3},{6,8},{7,9},{8,6},{9,7},{10,12},{11,13},{1... | collective-permute-start | bytes 786440 | tf_op jit(solution)/shard_map/ppermute | solution.py:666
  31.5 11.1 %collective-permute-start.8 = (bf16[2,2,128,256]{3,2,1,0:T(8,128)(2,1)S(1)}, bf16[2,2,128,256]{3,2,1,0:T(8,128)(2,1)S(1)}, u32[]{:S(2)}, u32[]{:S(2)}) collective-permute-start(bf16[2,2,128,256]{3,2,1,0:T(8,128)(2,1)S(1)} %get-tuple-element.83), channel_id=1, source_target_pairs={{0,1},{1,0},{2,3},{3,2},{4,5},{5,4},{6,7},{7,6},{8,9},{9,8},{10,11... | collective-permute-start | bytes 786440 | tf_op jit(solution)/shard_map/ppermute | solution.py:662
  37.7 9.0 %collective-permute-start.11 = (bf16[2,2,128,256]{3,2,1,0:T(8,128)(2,1)S(1)}, bf16[2,2,128,256]{3,2,1,0:T(8,128)(2,1)S(1)}, u32[]{:S(2)}, u32[]{:S(2)}) collective-permute-start(bf16[2,2,128,256]{3,2,1,0:T(8,128)(2,1)S(1)} %get-tuple-element.93), channel_id=1, source_target_pairs={{0,1},{1,0},{2,3},{3,2},{4,5},{5,4},{6,7},{7,6},{8,9},{9,8},{10,11... | collective-permute-start | bytes 786440 | tf_op jit(solution)/shard_map/ppermute | solution.py:662
  39.2 7.5 %collective-permute-start.12 = (bf16[512,256]{1,0:T(8,128)(2,1)S(1)}, bf16[512,256]{1,0:T(8,128)(2,1)S(1)}, u32[]{:S(2)}, u32[]{:S(2)}) collective-permute-start(bf16[512,256]{1,0:T(8,128)(2,1)S(1)} %get-tuple-element.95), channel_id=1, source_target_pairs={{0,2},{1,3},{2,0},{3,1},{4,6},{5,7},{6,4},{7,5},{8,10},{9,11},{10,... | collective-permute-start | bytes 786440 | tf_op jit(solution)/shard_map/ppermute | solution.py:665
  39.6 10.5 %collective-permute-start.13 = (bf16[512,256]{1,0:T(8,128)(2,1)S(1)}, bf16[512,256]{1,0:T(8,128)(2,1)S(1)}, u32[]{:S(2)}, u32[]{:S(2)}) collective-permute-start(bf16[512,256]{1,0:T(8,128)(2,1)S(1)} %get-tuple-element.96), channel_id=1, source_target_pairs={{2,4},{3,5},{4,2},{5,3},{6,8},{7,9},{8,6},{9,7},{10,12},{11,13},{1... | collective-permute-start | bytes 786440 | tf_op jit(solution)/shard_map/ppermute | solution.py:666
  42.8 10.3 %collective-permute-start.15 = (bf16[512,256]{1,0:T(8,128)(2,1)S(1)}, bf16[512,256]{1,0:T(8,128)(2,1)S(1)}, u32[]{:S(2)}, u32[]{:S(2)}) collective-permute-start(bf16[512,256]{1,0:T(8,128)(2,1)S(1)} %get-tuple-element.109), channel_id=1, source_target_pairs={{0,1},{1,0},{2,3},{3,2},{4,5},{5,4},{6,7},{7,6},{8,9},{9,8},{10,11... | collective-permute-start | bytes 786440 | tf_op jit(solution)/shard_map/ppermute | solution.py:662
  50.3 7.9 %collective-permute-start.14 = (bf16[512,256]{1,0:T(8,128)(2,1)S(1)}, bf16[512,256]{1,0:T(8,128)(2,1)S(1)}, u32[]{:S(2)}, u32[]{:S(2)}) collective-permute-start(bf16[512,256]{1,0:T(8,128)(2,1)S(1)} %get-tuple-element.103), channel_id=1, source_target_pairs={{0,1},{1,0},{2,3},{3,2},{4,5},{5,4},{6,7},{7,6},{8,9},{9,8},{10,11... | collective-permute-start | bytes 786440 | tf_op jit(solution)/shard_map/ppermute | solution.py:662

commit v22 on v21

--- a/solution.py
+++ b/solution.py
@@ -672,15 +672,24 @@
     qg_far = pack(False, where, queries, cotangent)
     packed = pack(True, where, key_matrix, value_matrix, queries, cotangent)
     kv, qg = packed[:CHUNKS], packed[CHUNKS:]
-    oq_own, oq_got, back = [], [], []
+    oq_own, oq_got, back, turned, halos, kv_got = [], [], [], [], [], []
     for c in range(CHUNKS):
         got_kv = swap(kv_far[c])
+        if c > 0:
+            got_kv, turned[0] = lax.optimization_barrier((got_kv, turned[0]))
+        turned.append(turn(where, kv[c], got_kv))
         near, wide = halo(where, kv[c], got_kv)
         far = qg_far[c]
         if c > 0:
-            near, wide, far = lax.optimization_barrier((near, wide, far))
+            near, wide, far, turned[c] = lax.optimization_barrier((near, wide, far, turned[c]))
         near, wide = beside(near, wide)
-        own, far, grad, near, wide = main(where, turn(where, kv[c], got_kv), kv[c], got_kv, near, wide, qg[c], swap(far), c == 0)
+        halos.append((near, wide, swap(far)))
+        kv_got.append(got_kv)
+    for c in range(CHUNKS):
+        near, wide, got_qg = halos[c]
+        own, far, grad, near, wide = main(
+            where, turned[c], kv[c], kv_got[c], near, wide, qg[c], got_qg, c == 0
+        )
         oq_own.append(own)
         oq_got.append(swap(far))
         if c > 0:

time: 59.5 us -> 59.2 us (level)
  transfers between devices with their start and end apart: 16 -> 16, of which waited for: 6 -> 7; matrix products, arithmetic and copies ran while one was open for 0% -> 0% of each run, Pallas kernels for 29% -> 29%
where the time goes in v22:
time: 59.2 us; the launch traced here: 59 us
  starting transfers between devices  20.3 us (34%)
  Pallas kernels  18.5 us (31%)
  waiting for transfers between devices  18 us (30%)
  local copies, waits for them, and re-layouts  1.23 us (2%)
  between operations  1.02 us (2%)
    ppermute x8, waiting for transfers between devices, swap(): return lax.ppermute(x, axes, across)  14.4 us
    pallas_call x2, Pallas kernels, main(): pl.pallas_call(placed(functools.partial(main_kernel, qg_first), where), i...  11.1 us
    ppermute x4, starting transfers between devices, beside(): return (near, lax.ppermute(wide, axes, wide_edges))  10.6 us
    ppermute x8, starting transfers between devices, swap(): return lax.ppermute(x, axes, across)  9.04 us
    ppermute x4, waiting for transfers between devices, beside(): return (near, lax.ppermute(wide, axes, wide_edges))  3.54 us
    pallas_call x1, Pallas kernels, unpack_columns(): pl.pallas_call(placed(unpack_columns_kernel, where), in_specs=[vmem()] *...  1.68 us
    pallas_call x2, Pallas kernels, pack(): pl.pallas_call(placed(functools.partial(pack_kernel, own), where), in_spe...  1.65 us
    pallas_call x1, Pallas kernels, unpack_rows(): pl.pallas_call(placed(unpack_rows_kernel, where), in_specs=[vmem()] * (CH...  1.53 us
  transfers between devices with their start and end apart: 16, of which 7 were waited for; matrix products, arithmetic and copies ran while one was open for 0% of the time, Pallas kernels for 29%

profile of v22, /device:TPU:12, one launch (start us, length us, event | category | flops | bytes accessed | tf_op | source)
XLA Modules:
  0.0 59.0 jit_solution(6420688624185702851)
XLA Ops:
  0.7 1.1 %constant_dynamic-slice_fusion.2 = (bf16[512,128]{1,0:T(8,128)(2,1)S(1)}, bf16[512,128]{1,0:T(8,128)(2,1)S(1)}) fusion(bf16[512,512]{1,0:T(8,128)(2,1)} %refs_1_.2, s32[]{:T(128)S(6)} %select_n.18, bf16[512,512]{1,0:T(8,128)(2,1)} %refs_0_.2), kind=kLoop, calls=%fused_computation.2 | loop fusion | bytes 524292 | tf_op jit(solution)/shard_map/dynamic_slice | solution.py:112
  2.0 1.6 %collective-permute-start = (bf16[512,256]{1,0:T(8,128)(2,1)S(1)}, bf16[512,256]{1,0:T(8,128)(2,1)S(1)}, u32[]{:S(2)}, u32[]{:S(2)}) collective-permute-start(bf16[512,256]{1,0:T(8,128)(2,1)S(1)} %shard_map.76), channel_id=1, source_target_pairs={{0,1},{1,0},{2,3},{3,2},{4,5},{5,4},{6,7},{7,6},{8,9},{9,8},{10,11... | collective-permute-start | bytes 786440 | tf_op jit(solution)/shard_map/ppermute | solution.py:662
  3.9 0.7 %collective-permute-start.1 = (bf16[512,256]{1,0:T(8,128)(2,1)S(1)}, bf16[512,256]{1,0:T(8,128)(2,1)S(1)}, u32[]{:S(2)}, u32[]{:S(2)}) collective-permute-start(bf16[512,256]{1,0:T(8,128)(2,1)S(1)} %shard_map.77), channel_id=1, source_target_pairs={{0,1},{1,0},{2,3},{3,2},{4,5},{5,4},{6,7},{7,6},{8,9},{9,8},{10,11... | collective-permute-start | bytes 786440 | tf_op jit(solution)/shard_map/ppermute | solution.py:662
  5.4 1.3 %collective-permute-start.2 = (bf16[512,256]{1,0:T(8,128)(2,1)S(1)}, bf16[512,256]{1,0:T(8,128)(2,1)S(1)}, u32[]{:S(2)}, u32[]{:S(2)}) collective-permute-start(bf16[512,256]{1,0:T(8,128)(2,1)S(1)} %get-tuple-element.77), channel_id=1, source_target_pairs={{0,1},{1,0},{2,3},{3,2},{4,5},{5,4},{6,7},{7,6},{8,9},{9,8},{10,11... | collective-permute-start | bytes 786440 | tf_op jit(solution)/shard_map/ppermute | solution.py:662
  6.7 1.1 %shard_map.75 = (bf16[512,256]{1,0:T(8,128)(2,1)S(1)}, bf16[512,256]{1,0:T(8,128)(2,1)S(1)}, bf16[512,256]{1,0:T(8,128)(2,1)S(1)}, bf16[512,256]{1,0:T(8,128)(2,1)S(1)}) custom-call(bf16[512,512]{1,0:T(8,128)(2,1)S(1)} %copy-done.2, bf16[512,512]{1,0:T(8,128)(2,1)S(1)} %copy-done.3, bf16[512,512]{1,0:T(8,128)(2,1)S(1)} %copy-done, bf16[512,512]{1,0:T(8,128)(2,1)S(1)} %copy-done.1), custom_call_target="tpu_custom_call" | custom-call | flops 1000 | bytes 1000 | tf_op jit(solution)/shard_map/pallas_call | solution.py:86
  7.8 3.5 %collective-permute-done.refs_1_ = bf16[512,256]{1,0:T(8,128)(2,1)S(1)} collective-permute-done((bf16[512,256]{1,0:T(8,128)(2,1)S(1)}, bf16[512,256]{1,0:T(8,128)(2,1)S(1)}, u32[]{:S(2)}, u32[]{:S(2)}) %collective-permute-start) | collective-permute-done | bytes 262176 | tf_op jit(solution)/shard_map/ppermute | solution.py:662
  11.5 2.5 %collective-permute-start.4 = (bf16[512,256]{1,0:T(8,128)(2,1)S(1)}, bf16[512,256]{1,0:T(8,128)(2,1)S(1)}, u32[]{:S(2)}, u32[]{:S(2)}) collective-permute-start(bf16[512,256]{1,0:T(8,128)(2,1)S(1)} %get-tuple-element.79), channel_id=1, source_target_pairs={{2,4},{3,5},{4,2},{5,3},{6,8},{7,9},{8,6},{9,7},{10,12},{11,13},{1... | collective-permute-start | bytes 786440 | tf_op jit(solution)/shard_map/ppermute | solution.py:666
  14.3 2.6 %collective-permute-done.1.refs_1_ = bf16[512,256]{1,0:T(8,128)(2,1)S(1)} collective-permute-done((bf16[512,256]{1,0:T(8,128)(2,1)S(1)}, bf16[512,256]{1,0:T(8,128)(2,1)S(1)}, u32[]{:S(2)}, u32[]{:S(2)}) %collective-permute-start.1) | collective-permute-done | bytes 262176 | tf_op jit(solution)/shard_map/ppermute | solution.py:662
  17.4 2.5 %collective-permute-start.6 = (bf16[512,256]{1,0:T(8,128)(2,1)S(1)}, bf16[512,256]{1,0:T(8,128)(2,1)S(1)}, u32[]{:S(2)}, u32[]{:S(2)}) collective-permute-start(bf16[512,256]{1,0:T(8,128)(2,1)S(1)} %get-tuple-element.93), channel_id=1, source_target_pairs={{2,4},{3,5},{4,2},{5,3},{6,8},{7,9},{8,6},{9,7},{10,12},{11,13},{1... | collective-permute-start | bytes 786440 | tf_op jit(solution)/shard_map/ppermute | solution.py:666
  19.9 1.5 %collective-permute-done.2.refs_6_ = bf16[512,256]{1,0:T(8,128)(2,1)S(1)} collective-permute-done((bf16[512,256]{1,0:T(8,128)(2,1)S(1)}, bf16[512,256]{1,0:T(8,128)(2,1)S(1)}, u32[]{:S(2)}, u32[]{:S(2)}) %collective-permute-start.2) | collective-permute-done | bytes 262176 | tf_op jit(solution)/shard_map/ppermute | solution.py:662
  21.4 1.5 %collective-permute-start.7 = (bf16[512,256]{1,0:T(8,128)(2,1)S(1)}, bf16[512,256]{1,0:T(8,128)(2,1)S(1)}, u32[]{:S(2)}, u32[]{:S(2)}) collective-permute-start(bf16[512,256]{1,0:T(8,128)(2,1)S(1)} %get-tuple-element.95), channel_id=1, source_target_pairs={{0,1},{1,0},{2,3},{3,2},{4,5},{5,4},{6,7},{7,6},{8,9},{9,8},{10,11... | collective-permute-start | bytes 786440 | tf_op jit(solution)/shard_map/ppermute | solution.py:662
  22.9 5.5 %shard_map.81 = (bf16[2,2,128,256]{3,2,1,0:T(8,128)(2,1)S(1)}, bf16[2,2,128,256]{3,2,1,0:T(8,128)(2,1)S(1)}, f32[1024,256]{1,0:T(8,128)S(1)}, bf16[512,256]{1,0:T(8,128)(2,1)S(1)}, bf16[512,256]{1,0:T(8,128)(2,1)S(1)}) custom-call(bf16[512,256]{1,0:T(8,128)(2,1)S(1)} %get-tuple-element.66.refs_0_, bf16[512,256]{1,0:T(8,128)(2,1)S(1)} %collective-permute-done.refs_1_, ...), custom_call_target="tpu_custom_call" | custom-call | flops 1000 | bytes 1000 | tf_op jit(solution)/shard_map/pallas_call | solution.py:485
  28.5 2.7 %collective-permute-start.10 = (bf16[512,256]{1,0:T(8,128)(2,1)S(1)}, bf16[512,256]{1,0:T(8,128)(2,1)S(1)}, u32[]{:S(2)}, u32[]{:S(2)}) collective-permute-start(bf16[512,256]{1,0:T(8,128)(2,1)S(1)} %get-tuple-element.100), channel_id=1, source_target_pairs={{2,4},{3,5},{4,2},{5,3},{6,8},{7,9},{8,6},{9,7},{10,12},{11,13},{1... | collective-permute-start | bytes 786440 | tf_op jit(solution)/shard_map/ppermute | solution.py:666
  31.2 0.7 %collective-permute-start.8 = (bf16[2,2,128,256]{3,2,1,0:T(8,128)(2,1)S(1)}, bf16[2,2,128,256]{3,2,1,0:T(8,128)(2,1)S(1)}, u32[]{:S(2)}, u32[]{:S(2)}) collective-permute-start(bf16[2,2,128,256]{3,2,1,0:T(8,128)(2,1)S(1)} %get-tuple-element.97), channel_id=1, source_target_pairs={{0,1},{1,0},{2,3},{3,2},{4,5},{5,4},{6,7},{7,6},{8,9},{9,8},{10,11... | collective-permute-start | bytes 786440 | tf_op jit(solution)/shard_map/ppermute | solution.py:662
  31.9 5.5 %shard_map.84 = (bf16[2,2,128,256]{3,2,1,0:T(8,128)(2,1)S(1)}, bf16[2,2,128,256]{3,2,1,0:T(8,128)(2,1)S(1)}, f32[1024,256]{1,0:T(8,128)S(1)}, bf16[512,256]{1,0:T(8,128)(2,1)S(1)}, bf16[512,256]{1,0:T(8,128)(2,1)S(1)}) custom-call(bf16[512,256]{1,0:T(8,128)(2,1)S(1)} %get-tuple-element.81.refs_0_, bf16[512,256]{1,0:T(8,128)(2,1)S(1)} %collective-permute-done.1.refs_1_, ...), custom_call_target="tpu_custom_call" | custom-call | flops 1000 | bytes 1000 | tf_op jit(solution)/shard_map/pallas_call | solution.py:485
  37.4 1.5 %collective-permute-start.11 = (bf16[2,2,128,256]{3,2,1,0:T(8,128)(2,1)S(1)}, bf16[2,2,128,256]{3,2,1,0:T(8,128)(2,1)S(1)}, u32[]{:S(2)}, u32[]{:S(2)}) collective-permute-start(bf16[2,2,128,256]{3,2,1,0:T(8,128)(2,1)S(1)} %get-tuple-element.107), channel_id=1, source_target_pairs={{0,1},{1,0},{2,3},{3,2},{4,5},{5,4},{6,7},{7,6},{8,9},{9,8},{10,11... | collective-permute-start | bytes 786440 | tf_op jit(solution)/shard_map/ppermute | solution.py:662
  39.4 2.9 %collective-permute-start.13 = (bf16[512,256]{1,0:T(8,128)(2,1)S(1)}, bf16[512,256]{1,0:T(8,128)(2,1)S(1)}, u32[]{:S(2)}, u32[]{:S(2)}) collective-permute-start(bf16[512,256]{1,0:T(8,128)(2,1)S(1)} %get-tuple-element.110), channel_id=1, source_target_pairs={{2,4},{3,5},{4,2},{5,3},{6,8},{7,9},{8,6},{9,7},{10,12},{11,13},{1... | collective-permute-start | bytes 786440 | tf_op jit(solution)/shard_map/ppermute | solution.py:666
  43.2 3.3 %collective-permute-done.11.refs_3_ = bf16[2,2,128,256]{3,2,1,0:T(8,128)(2,1)S(1)} collective-permute-done((bf16[2,2,128,256]{3,2,1,0:T(8,128)(2,1)S(1)}, bf16[2,2,128,256]{3,2,1,0:T(8,128)(2,1)S(1)}, u32[]{:S(2)}, u32[]{:S(2)}) %collective-permute-start.11) | collective-permute-done | bytes 262176 | tf_op jit(solution)/shard_map/ppermute | solution.py:662
  46.4 3.4 %collective-permute-done.13.refs_2_ = bf16[512,256]{1,0:T(8,128)(2,1)S(1)} collective-permute-done((bf16[512,256]{1,0:T(8,128)(2,1)S(1)}, bf16[512,256]{1,0:T(8,128)(2,1)S(1)}, u32[]{:S(2)}, u32[]{:S(2)}) %collective-permute-start.13) | collective-permute-done | bytes 262176 | tf_op jit(solution)/shard_map/ppermute | solution.py:666
  50.0 1.1 %collective-permute-start.14 = (bf16[512,256]{1,0:T(8,128)(2,1)S(1)}, bf16[512,256]{1,0:T(8,128)(2,1)S(1)}, u32[]{:S(2)}, u32[]{:S(2)}) collective-permute-start(bf16[512,256]{1,0:T(8,128)(2,1)S(1)} %get-tuple-element.117), channel_id=1, source_target_pairs={{0,1},{1,0},{2,3},{3,2},{4,5},{5,4},{6,7},{7,6},{8,9},{9,8},{10,11... | collective-permute-start | bytes 786440 | tf_op jit(solution)/shard_map/ppermute | solution.py:662
  51.1 1.7 %shard_map.85 = (bf16[512,512]{1,0:T(8,128)(2,1)}, bf16[512,512]{1,0:T(8,128)(2,1)}) custom-call(bf16[2,2,128,256]{3,2,1,0:T(8,128)(2,1)S(1)} %get-tuple-element.80.refs_0_, bf16[2,2,128,256]{3,2,1,0:T(8,128)(2,1)S(1)} %get-tuple-element.96.refs_1_, bf16[2,2,128,256]{3,2,1,0:T(8,128)(2,1)S(1)} %collective-permute-done.8.refs_2_, ...), custom_call_target="tpu_custom_call" | custom-call | flops 1000 | bytes 1000 | tf_op jit(solution)/shard_map/pallas_call | solution.py:641
  52.8 1.5 %shard_map.88 = (bf16[512,512]{1,0:T(8,128)(2,1)}, bf16[512,512]{1,0:T(8,128)(2,1)}) custom-call(bf16[512,256]{1,0:T(8,128)(2,1)S(1)} %get-tuple-element.121.refs_0_, bf16[512,256]{1,0:T(8,128)(2,1)S(1)} %get-tuple-element.122.refs_1_, bf16[512,256]{1,0:T(8,128)(2,1)S(1)} %collective-permute-done.15.refs_2_), custom_call_target="tpu_custom_call" | custom-call | flops 1000 | bytes 1000 | tf_op jit(solution)/shard_map/pallas_call | solution.py:578
  54.3 3.6 %collective-permute-done.14.refs_0_ = bf16[512,256]{1,0:T(8,128)(2,1)S(1)} collective-permute-done((bf16[512,256]{1,0:T(8,128)(2,1)S(1)}, bf16[512,256]{1,0:T(8,128)(2,1)S(1)}, u32[]{:S(2)}, u32[]{:S(2)}) %collective-permute-start.14) | collective-permute-done | bytes 262176 | tf_op jit(solution)/shard_map/ppermute | solution.py:662
  57.9 1.0 %shard_map.89 = (bf16[512,512]{1,0:T(8,128)(2,1)}, bf16[512,512]{1,0:T(8,128)(2,1)}) custom-call(bf16[512,256]{1,0:T(8,128)(2,1)S(1)} %collective-permute-done.14.refs_0_, bf16[512,512]{1,0:T(8,128)(2,1)} %get-tuple-element.124.refs_1_, bf16[512,512]{1,0:T(8,128)(2,1)} %get-tuple-element.125.refs_2_), custom_call_target="tpu_custom_call", output_to_operand_aliasing={{0}: (1, {}), {1}: (2, {})} | custom-call | flops 1000 | bytes 1000 | tf_op jit(solution)/shard_map/pallas_call | solution.py:611
  (34 shorter events, 3.8 us)
Async XLA Ops:
  0.6 2.9 %copy-start.2 = (bf16[512,512]{1,0:T(8,128)(2,1)S(1)}, bf16[512,512]{1,0:T(8,128)(2,1)}, u32[]{:S(2)}) copy-start(bf16[512,512]{1,0:T(8,128)(2,1)} %refs_0_.2) | copy-start | bytes 1572868
  1.7 1.9 %copy-start.3 = (bf16[512,512]{1,0:T(8,128)(2,1)S(1)}, bf16[512,512]{1,0:T(8,128)(2,1)}, u32[]{:S(2)}) copy-start(bf16[512,512]{1,0:T(8,128)(2,1)} %refs_1_.2) | copy-start | bytes 1572868
  2.0 9.3 %collective-permute-start = (bf16[512,256]{1,0:T(8,128)(2,1)S(1)}, bf16[512,256]{1,0:T(8,128)(2,1)S(1)}, u32[]{:S(2)}, u32[]{:S(2)}) collective-permute-start(bf16[512,256]{1,0:T(8,128)(2,1)S(1)} %shard_map.76), channel_id=1, source_target_pairs={{0,1},{1,0},{2,3},{3,2},{4,5},{5,4},{6,7},{7,6},{8,9},{9,8},{10,11... | collective-permute-start | bytes 786440 | tf_op jit(solution)/shard_map/ppermute | solution.py:662
  3.6 1.1 %copy-start = (bf16[512,512]{1,0:T(8,128)(2,1)S(1)}, bf16[512,512]{1,0:T(8,128)(2,1)}, u32[]{:S(2)}) copy-start(bf16[512,512]{1,0:T(8,128)(2,1)} %refs_0_.3) | copy-start | bytes 1572868
  3.6 1.2 %copy-start.1 = (bf16[512,512]{1,0:T(8,128)(2,1)S(1)}, bf16[512,512]{1,0:T(8,128)(2,1)}, u32[]{:S(2)}) copy-start(bf16[512,512]{1,0:T(8,128)(2,1)} %refs_1_.3) | copy-start | bytes 1572868
  3.9 13.0 %collective-permute-start.1 = (bf16[512,256]{1,0:T(8,128)(2,1)S(1)}, bf16[512,256]{1,0:T(8,128)(2,1)S(1)}, u32[]{:S(2)}, u32[]{:S(2)}) collective-permute-start(bf16[512,256]{1,0:T(8,128)(2,1)S(1)} %shard_map.77), channel_id=1, source_target_pairs={{0,1},{1,0},{2,3},{3,2},{4,5},{5,4},{6,7},{7,6},{8,9},{9,8},{10,11... | collective-permute-start | bytes 786440 | tf_op jit(solution)/shard_map/ppermute | solution.py:662
  5.4 16.0 %collective-permute-start.2 = (bf16[512,256]{1,0:T(8,128)(2,1)S(1)}, bf16[512,256]{1,0:T(8,128)(2,1)S(1)}, u32[]{:S(2)}, u32[]{:S(2)}) collective-permute-start(bf16[512,256]{1,0:T(8,128)(2,1)S(1)} %get-tuple-element.77), channel_id=1, source_target_pairs={{0,1},{1,0},{2,3},{3,2},{4,5},{5,4},{6,7},{7,6},{8,9},{9,8},{10,11... | collective-permute-start | bytes 786440 | tf_op jit(solution)/shard_map/ppermute | solution.py:662
  11.4 11.5 %collective-permute-start.3 = (bf16[512,256]{1,0:T(8,128)(2,1)S(1)}, bf16[512,256]{1,0:T(8,128)(2,1)S(1)}, u32[]{:S(2)}, u32[]{:S(2)}) collective-permute-start(bf16[512,256]{1,0:T(8,128)(2,1)S(1)} %get-tuple-element.78), channel_id=1, source_target_pairs={{0,2},{1,3},{2,0},{3,1},{4,6},{5,7},{6,4},{7,5},{8,10},{9,11},{10,... | collective-permute-start | bytes 786440 | tf_op jit(solution)/shard_map/ppermute | solution.py:665
  11.5 11.4 %collective-permute-start.4 = (bf16[512,256]{1,0:T(8,128)(2,1)S(1)}, bf16[512,256]{1,0:T(8,128)(2,1)S(1)}, u32[]{:S(2)}, u32[]{:S(2)}) collective-permute-start(bf16[512,256]{1,0:T(8,128)(2,1)S(1)} %get-tuple-element.79), channel_id=1, source_target_pairs={{2,4},{3,5},{4,2},{5,3},{6,8},{7,9},{8,6},{9,7},{10,12},{11,13},{1... | collective-permute-start | bytes 786440 | tf_op jit(solution)/shard_map/ppermute | solution.py:666
  17.3 13.9 %collective-permute-start.5 = (bf16[512,256]{1,0:T(8,128)(2,1)S(1)}, bf16[512,256]{1,0:T(8,128)(2,1)S(1)}, u32[]{:S(2)}, u32[]{:S(2)}) collective-permute-start(bf16[512,256]{1,0:T(8,128)(2,1)S(1)} %get-tuple-element.92), channel_id=1, source_target_pairs={{0,2},{1,3},{2,0},{3,1},{4,6},{5,7},{6,4},{7,5},{8,10},{9,11},{10,... | collective-permute-start | bytes 786440 | tf_op jit(solution)/shard_map/ppermute | solution.py:665
  17.4 14.5 %collective-permute-start.6 = (bf16[512,256]{1,0:T(8,128)(2,1)S(1)}, bf16[512,256]{1,0:T(8,128)(2,1)S(1)}, u32[]{:S(2)}, u32[]{:S(2)}) collective-permute-start(bf16[512,256]{1,0:T(8,128)(2,1)S(1)} %get-tuple-element.93), channel_id=1, source_target_pairs={{2,4},{3,5},{4,2},{5,3},{6,8},{7,9},{8,6},{9,7},{10,12},{11,13},{1... | collective-permute-start | bytes 786440 | tf_op jit(solution)/shard_map/ppermute | solution.py:666
  21.4 10.5 %collective-permute-start.7 = (bf16[512,256]{1,0:T(8,128)(2,1)S(1)}, bf16[512,256]{1,0:T(8,128)(2,1)S(1)}, u32[]{:S(2)}, u32[]{:S(2)}) collective-permute-start(bf16[512,256]{1,0:T(8,128)(2,1)S(1)} %get-tuple-element.95), channel_id=1, source_target_pairs={{0,1},{1,0},{2,3},{3,2},{4,5},{5,4},{6,7},{7,6},{8,9},{9,8},{10,11... | collective-permute-start | bytes 786440 | tf_op jit(solution)/shard_map/ppermute | solution.py:662
  28.4 10.5 %collective-permute-start.9 = (bf16[512,256]{1,0:T(8,128)(2,1)S(1)}, bf16[512,256]{1,0:T(8,128)(2,1)S(1)}, u32[]{:S(2)}, u32[]{:S(2)}) collective-permute-start(bf16[512,256]{1,0:T(8,128)(2,1)S(1)} %get-tuple-element.99), channel_id=1, source_target_pairs={{0,2},{1,3},{2,0},{3,1},{4,6},{5,7},{6,4},{7,5},{8,10},{9,11},{10,... | collective-permute-start | bytes 786440 | tf_op jit(solution)/shard_map/ppermute | solution.py:665
  28.5 10.5 %collective-permute-start.10 = (bf16[512,256]{1,0:T(8,128)(2,1)S(1)}, bf16[512,256]{1,0:T(8,128)(2,1)S(1)}, u32[]{:S(2)}, u32[]{:S(2)}) collective-permute-start(bf16[512,256]{1,0:T(8,128)(2,1)S(1)} %get-tuple-element.100), channel_id=1, source_target_pairs={{2,4},{3,5},{4,2},{5,3},{6,8},{7,9},{8,6},{9,7},{10,12},{11,13},{1... | collective-permute-start | bytes 786440 | tf_op jit(solution)/shard_map/ppermute | solution.py:666
  31.2 11.1 %collective-permute-start.8 = (bf16[2,2,128,256]{3,2,1,0:T(8,128)(2,1)S(1)}, bf16[2,2,128,256]{3,2,1,0:T(8,128)(2,1)S(1)}, u32[]{:S(2)}, u32[]{:S(2)}) collective-permute-start(bf16[2,2,128,256]{3,2,1,0:T(8,128)(2,1)S(1)} %get-tuple-element.97), channel_id=1, source_target_pairs={{0,1},{1,0},{2,3},{3,2},{4,5},{5,4},{6,7},{7,6},{8,9},{9,8},{10,11... | collective-permute-start | bytes 786440 | tf_op jit(solution)/shard_map/ppermute | solution.py:662
  37.4 9.0 %collective-permute-start.11 = (bf16[2,2,128,256]{3,2,1,0:T(8,128)(2,1)S(1)}, bf16[2,2,128,256]{3,2,1,0:T(8,128)(2,1)S(1)}, u32[]{:S(2)}, u32[]{:S(2)}) collective-permute-start(bf16[2,2,128,256]{3,2,1,0:T(8,128)(2,1)S(1)} %get-tuple-element.107), channel_id=1, source_target_pairs={{0,1},{1,0},{2,3},{3,2},{4,5},{5,4},{6,7},{7,6},{8,9},{9,8},{10,11... | collective-permute-start | bytes 786440 | tf_op jit(solution)/shard_map/ppermute | solution.py:662
  39.0 7.4 %collective-permute-start.12 = (bf16[512,256]{1,0:T(8,128)(2,1)S(1)}, bf16[512,256]{1,0:T(8,128)(2,1)S(1)}, u32[]{:S(2)}, u32[]{:S(2)}) collective-permute-start(bf16[512,256]{1,0:T(8,128)(2,1)S(1)} %get-tuple-element.109), channel_id=1, source_target_pairs={{0,2},{1,3},{2,0},{3,1},{4,6},{5,7},{6,4},{7,5},{8,10},{9,11},{10,... | collective-permute-start | bytes 786440 | tf_op jit(solution)/shard_map/ppermute | solution.py:665
  39.4 10.5 %collective-permute-start.13 = (bf16[512,256]{1,0:T(8,128)(2,1)S(1)}, bf16[512,256]{1,0:T(8,128)(2,1)S(1)}, u32[]{:S(2)}, u32[]{:S(2)}) collective-permute-start(bf16[512,256]{1,0:T(8,128)(2,1)S(1)} %get-tuple-element.110), channel_id=1, source_target_pairs={{2,4},{3,5},{4,2},{5,3},{6,8},{7,9},{8,6},{9,7},{10,12},{11,13},{1... | collective-permute-start | bytes 786440 | tf_op jit(solution)/shard_map/ppermute | solution.py:666
  42.5 10.3 %collective-permute-start.15 = (bf16[512,256]{1,0:T(8,128)(2,1)S(1)}, bf16[512,256]{1,0:T(8,128)(2,1)S(1)}, u32[]{:S(2)}, u32[]{:S(2)}) collective-permute-start(bf16[512,256]{1,0:T(8,128)(2,1)S(1)} %get-tuple-element.123), channel_id=1, source_target_pairs={{0,1},{1,0},{2,3},{3,2},{4,5},{5,4},{6,7},{7,6},{8,9},{9,8},{10,11... | collective-permute-start | bytes 786440 | tf_op jit(solution)/shard_map/ppermute | solution.py:662
  50.0 7.9 %collective-permute-start.14 = (bf16[512,256]{1,0:T(8,128)(2,1)S(1)}, bf16[512,256]{1,0:T(8,128)(2,1)S(1)}, u32[]{:S(2)}, u32[]{:S(2)}) collective-permute-start(bf16[512,256]{1,0:T(8,128)(2,1)S(1)} %get-tuple-element.117), channel_id=1, source_target_pairs={{0,1},{1,0},{2,3},{3,2},{4,5},{5,4},{6,7},{7,6},{8,9},{9,8},{10,11... | collective-permute-start | bytes 786440 | tf_op jit(solution)/shard_map/ppermute | solution.py:662

commit v23 on v22

--- a/solution.py
+++ b/solution.py
@@ -676,12 +676,14 @@
     for c in range(CHUNKS):
         got_kv = swap(kv_far[c])
         if c > 0:
+            far, turned[0] = lax.optimization_barrier((qg_far[c], turned[0]))
             got_kv, turned[0] = lax.optimization_barrier((got_kv, turned[0]))
         turned.append(turn(where, kv[c], got_kv))
         near, wide = halo(where, kv[c], got_kv)
-        far = qg_far[c]
-        if c > 0:
-            near, wide, far, turned[c] = lax.optimization_barrier((near, wide, far, turned[c]))
+        if c == 0:
+            far = qg_far[c]
+        else:
+            near, wide, turned[c] = lax.optimization_barrier((near, wide, turned[c]))
         near, wide = beside(near, wide)
         halos.append((near, wide, swap(far)))
         kv_got.append(got_kv)

time: 59.2 us -> 63.1 us (1.066)
  waiting for transfers between devices: 18 us -> 20.2 us
  starting transfers between devices: 20.3 us -> 21.7 us
    ppermute x8, waiting for transfers between devices: 14.4 us -> 16.6 us  [swap(): return lax.ppermute(x, axes, across)]
    ppermute x4, starting transfers between devices: 0.6 us -> 2.14 us  [beside(): near = lax.ppermute(near, axes, near_edges)]
    ppermute x4, starting transfers between devices: 10.6 us -> 9.11 us  [beside(): return (near, lax.ppermute(wide, axes, wide_edges))]
    ppermute x8, starting transfers between devices: 9.04 us -> 10.4 us  [swap(): return lax.ppermute(x, axes, across)]
  transfers between devices with their start and end apart: 16 -> 16, of which waited for: 7 -> 7; matrix products, arithmetic and copies ran while one was open for 0% -> 0% of each run, Pallas kernels for 29% -> 28%
where the time goes in v23:
time: 63.1 us; the launch traced here: 62.6 us
  starting transfers between devices  21.7 us (34%)
  waiting for transfers between devices  20.2 us (32%)
  Pallas kernels  18.5 us (29%)
  local copies, waits for them, and re-layouts  1.23 us (2%)
  between operations  1.02 us (2%)
    ppermute x8, waiting for transfers between devices, swap(): return lax.ppermute(x, axes, across)  16.6 us
    pallas_call x2, Pallas kernels, main(): pl.pallas_call(placed(functools.partial(main_kernel, qg_first), where), i...  11.1 us
    ppermute x8, starting transfers between devices, swap(): return lax.ppermute(x, axes, across)  10.4 us
    ppermute x4, starting transfers between devices, beside(): return (near, lax.ppermute(wide, axes, wide_edges))  9.11 us
    ppermute x4, waiting for transfers between devices, beside(): return (near, lax.ppermute(wide, axes, wide_edges))  3.57 us
    ppermute x4, starting transfers between devices, beside(): near = lax.ppermute(near, axes, near_edges)  2.14 us
    pallas_call x1, Pallas kernels, unpack_columns(): pl.pallas_call(placed(unpack_columns_kernel, where), in_specs=[vmem()] *...  1.68 us
    pallas_call x2, Pallas kernels, pack(): pl.pallas_call(placed(functools.partial(pack_kernel, own), where), in_spe...  1.65 us
  transfers between devices with their start and end apart: 16, of which 7 were waited for; matrix products, arithmetic and copies ran while one was open for 0% of the time, Pallas kernels for 28%

profile of v23, /device:TPU:12, one launch (start us, length us, event | category | flops | bytes accessed | tf_op | source)
XLA Modules:
  0.0 62.6 jit_solution(5621539581220635967)
XLA Ops:
  0.7 1.1 %constant_dynamic-slice_fusion.2 = (bf16[512,128]{1,0:T(8,128)(2,1)S(1)}, bf16[512,128]{1,0:T(8,128)(2,1)S(1)}) fusion(bf16[512,512]{1,0:T(8,128)(2,1)} %refs_1_.2, s32[]{:T(128)S(6)} %select_n.18, bf16[512,512]{1,0:T(8,128)(2,1)} %refs_0_.2), kind=kLoop, calls=%fused_computation.2 | loop fusion | bytes 524292 | tf_op jit(solution)/shard_map/dynamic_slice | solution.py:112
  2.0 1.6 %collective-permute-start = (bf16[512,256]{1,0:T(8,128)(2,1)S(1)}, bf16[512,256]{1,0:T(8,128)(2,1)S(1)}, u32[]{:S(2)}, u32[]{:S(2)}) collective-permute-start(bf16[512,256]{1,0:T(8,128)(2,1)S(1)} %shard_map.76), channel_id=1, source_target_pairs={{0,1},{1,0},{2,3},{3,2},{4,5},{5,4},{6,7},{7,6},{8,9},{9,8},{10,11... | collective-permute-start | bytes 786440 | tf_op jit(solution)/shard_map/ppermute | solution.py:662
  5.4 1.3 %collective-permute-start.2 = (bf16[512,256]{1,0:T(8,128)(2,1)S(1)}, bf16[512,256]{1,0:T(8,128)(2,1)S(1)}, u32[]{:S(2)}, u32[]{:S(2)}) collective-permute-start(bf16[512,256]{1,0:T(8,128)(2,1)S(1)} %get-tuple-element.84), channel_id=1, source_target_pairs={{0,1},{1,0},{2,3},{3,2},{4,5},{5,4},{6,7},{7,6},{8,9},{9,8},{10,11... | collective-permute-start | bytes 786440 | tf_op jit(solution)/shard_map/ppermute | solution.py:662
  6.7 1.1 %shard_map.75 = (bf16[512,256]{1,0:T(8,128)(2,1)S(1)}, bf16[512,256]{1,0:T(8,128)(2,1)S(1)}, bf16[512,256]{1,0:T(8,128)(2,1)S(1)}, bf16[512,256]{1,0:T(8,128)(2,1)S(1)}) custom-call(bf16[512,512]{1,0:T(8,128)(2,1)S(1)} %copy-done.2, bf16[512,512]{1,0:T(8,128)(2,1)S(1)} %copy-done.3, bf16[512,512]{1,0:T(8,128)(2,1)S(1)} %copy-done, bf16[512,512]{1,0:T(8,128)(2,1)S(1)} %copy-done.1), custom_call_target="tpu_custom_call" | custom-call | flops 1000 | bytes 1000 | tf_op jit(solution)/shard_map/pallas_call | solution.py:86
  7.8 3.5 %collective-permute-done.refs_1_ = bf16[512,256]{1,0:T(8,128)(2,1)S(1)} collective-permute-done((bf16[512,256]{1,0:T(8,128)(2,1)S(1)}, bf16[512,256]{1,0:T(8,128)(2,1)S(1)}, u32[]{:S(2)}, u32[]{:S(2)}) %collective-permute-start) | collective-permute-done | bytes 262176 | tf_op jit(solution)/shard_map/ppermute | solution.py:662
  11.5 2.5 %collective-permute-start.4 = (bf16[512,256]{1,0:T(8,128)(2,1)S(1)}, bf16[512,256]{1,0:T(8,128)(2,1)S(1)}, u32[]{:S(2)}, u32[]{:S(2)}) collective-permute-start(bf16[512,256]{1,0:T(8,128)(2,1)S(1)} %get-tuple-element.86), channel_id=1, source_target_pairs={{2,4},{3,5},{4,2},{5,3},{6,8},{7,9},{8,6},{9,7},{10,12},{11,13},{1... | collective-permute-start | bytes 786440 | tf_op jit(solution)/shard_map/ppermute | solution.py:666
  14.3 2.6 %collective-permute-done.1.refs_1_ = bf16[512,256]{1,0:T(8,128)(2,1)S(1)} collective-permute-done((bf16[512,256]{1,0:T(8,128)(2,1)S(1)}, bf16[512,256]{1,0:T(8,128)(2,1)S(1)}, u32[]{:S(2)}, u32[]{:S(2)}) %collective-permute-start.1) | collective-permute-done | bytes 262176 | tf_op jit(solution)/shard_map/ppermute | solution.py:662
  17.3 1.5 %collective-permute-start.7 = (bf16[512,256]{1,0:T(8,128)(2,1)S(1)}, bf16[512,256]{1,0:T(8,128)(2,1)S(1)}, u32[]{:S(2)}, u32[]{:S(2)}) collective-permute-start(bf16[512,256]{1,0:T(8,128)(2,1)S(1)} %get-tuple-element.101), channel_id=1, source_target_pairs={{0,1},{1,0},{2,3},{3,2},{4,5},{5,4},{6,7},{7,6},{8,9},{9,8},{10,11... | collective-permute-start | bytes 786440 | tf_op jit(solution)/shard_map/ppermute | solution.py:662
  18.8 3.7 %collective-permute-done.2.refs_6_ = bf16[512,256]{1,0:T(8,128)(2,1)S(1)} collective-permute-done((bf16[512,256]{1,0:T(8,128)(2,1)S(1)}, bf16[512,256]{1,0:T(8,128)(2,1)S(1)}, u32[]{:S(2)}, u32[]{:S(2)}) %collective-permute-start.2) | collective-permute-done | bytes 262176 | tf_op jit(solution)/shard_map/ppermute | solution.py:662
  22.5 1.9 %collective-permute-start.6 = (bf16[512,256]{1,0:T(8,128)(2,1)S(1)}, bf16[512,256]{1,0:T(8,128)(2,1)S(1)}, u32[]{:S(2)}, u32[]{:S(2)}) collective-permute-start(bf16[512,256]{1,0:T(8,128)(2,1)S(1)} %get-tuple-element.99), channel_id=1, source_target_pairs={{2,4},{3,5},{4,2},{5,3},{6,8},{7,9},{8,6},{9,7},{10,12},{11,13},{1... | collective-permute-start | bytes 786440 | tf_op jit(solution)/shard_map/ppermute | solution.py:666
  24.5 5.5 %shard_map.81 = (bf16[2,2,128,256]{3,2,1,0:T(8,128)(2,1)S(1)}, bf16[2,2,128,256]{3,2,1,0:T(8,128)(2,1)S(1)}, f32[1024,256]{1,0:T(8,128)S(1)}, bf16[512,256]{1,0:T(8,128)(2,1)S(1)}, bf16[512,256]{1,0:T(8,128)(2,1)S(1)}) custom-call(bf16[512,256]{1,0:T(8,128)(2,1)S(1)} %get-tuple-element.69.refs_0_, bf16[512,256]{1,0:T(8,128)(2,1)S(1)} %collective-permute-done.refs_1_, ...), custom_call_target="tpu_custom_call" | custom-call | flops 1000 | bytes 1000 | tf_op jit(solution)/shard_map/pallas_call | solution.py:485
  30.0 1.7 %collective-permute-start.9 = (bf16[512,256]{1,0:T(8,128)(2,1)S(1)}, bf16[512,256]{1,0:T(8,128)(2,1)S(1)}, u32[]{:S(2)}, u32[]{:S(2)}) collective-permute-start(bf16[512,256]{1,0:T(8,128)(2,1)S(1)} %get-tuple-element.105), channel_id=1, source_target_pairs={{0,2},{1,3},{2,0},{3,1},{4,6},{5,7},{6,4},{7,5},{8,10},{9,11},{10,... | collective-permute-start | bytes 786440 | tf_op jit(solution)/shard_map/ppermute | solution.py:665
  31.7 2.2 %collective-permute-start.10 = (bf16[512,256]{1,0:T(8,128)(2,1)S(1)}, bf16[512,256]{1,0:T(8,128)(2,1)S(1)}, u32[]{:S(2)}, u32[]{:S(2)}) collective-permute-start(bf16[512,256]{1,0:T(8,128)(2,1)S(1)} %get-tuple-element.106), channel_id=1, source_target_pairs={{2,4},{3,5},{4,2},{5,3},{6,8},{7,9},{8,6},{9,7},{10,12},{11,13},{1... | collective-permute-start | bytes 786440 | tf_op jit(solution)/shard_map/ppermute | solution.py:666
  33.9 1.6 %collective-permute-start.8 = (bf16[2,2,128,256]{3,2,1,0:T(8,128)(2,1)S(1)}, bf16[2,2,128,256]{3,2,1,0:T(8,128)(2,1)S(1)}, u32[]{:S(2)}, u32[]{:S(2)}) collective-permute-start(bf16[2,2,128,256]{3,2,1,0:T(8,128)(2,1)S(1)} %get-tuple-element.103), channel_id=1, source_target_pairs={{0,1},{1,0},{2,3},{3,2},{4,5},{5,4},{6,7},{7,6},{8,9},{9,8},{10,11... | collective-permute-start | bytes 786440 | tf_op jit(solution)/shard_map/ppermute | solution.py:662
  35.5 5.5 %shard_map.84 = (bf16[2,2,128,256]{3,2,1,0:T(8,128)(2,1)S(1)}, bf16[2,2,128,256]{3,2,1,0:T(8,128)(2,1)S(1)}, f32[1024,256]{1,0:T(8,128)S(1)}, bf16[512,256]{1,0:T(8,128)(2,1)S(1)}, bf16[512,256]{1,0:T(8,128)(2,1)S(1)}) custom-call(bf16[512,256]{1,0:T(8,128)(2,1)S(1)} %get-tuple-element.88.refs_0_, bf16[512,256]{1,0:T(8,128)(2,1)S(1)} %collective-permute-done.1.refs_1_, ...), custom_call_target="tpu_custom_call" | custom-call | flops 1000 | bytes 1000 | tf_op jit(solution)/shard_map/pallas_call | solution.py:485
  42.5 2.5 %collective-permute-start.13 = (bf16[512,256]{1,0:T(8,128)(2,1)S(1)}, bf16[512,256]{1,0:T(8,128)(2,1)S(1)}, u32[]{:S(2)}, u32[]{:S(2)}) collective-permute-start(bf16[512,256]{1,0:T(8,128)(2,1)S(1)} %get-tuple-element.116), channel_id=1, source_target_pairs={{2,4},{3,5},{4,2},{5,3},{6,8},{7,9},{8,6},{9,7},{10,12},{11,13},{1... | collective-permute-start | bytes 786440 | tf_op jit(solution)/shard_map/ppermute | solution.py:666
  45.2 1.6 %collective-permute-start.15 = (bf16[512,256]{1,0:T(8,128)(2,1)S(1)}, bf16[512,256]{1,0:T(8,128)(2,1)S(1)}, u32[]{:S(2)}, u32[]{:S(2)}) collective-permute-start(bf16[512,256]{1,0:T(8,128)(2,1)S(1)} %get-tuple-element.129), channel_id=1, source_target_pairs={{0,1},{1,0},{2,3},{3,2},{4,5},{5,4},{6,7},{7,6},{8,9},{9,8},{10,11... | collective-permute-start | bytes 786440 | tf_op jit(solution)/shard_map/ppermute | solution.py:662
  46.8 3.2 %collective-permute-done.11.refs_3_ = bf16[2,2,128,256]{3,2,1,0:T(8,128)(2,1)S(1)} collective-permute-done((bf16[2,2,128,256]{3,2,1,0:T(8,128)(2,1)S(1)}, bf16[2,2,128,256]{3,2,1,0:T(8,128)(2,1)S(1)}, u32[]{:S(2)}, u32[]{:S(2)}) %collective-permute-start.11) | collective-permute-done | bytes 262176 | tf_op jit(solution)/shard_map/ppermute | solution.py:662
  50.0 3.0 %collective-permute-done.13.refs_2_ = bf16[512,256]{1,0:T(8,128)(2,1)S(1)} collective-permute-done((bf16[512,256]{1,0:T(8,128)(2,1)S(1)}, bf16[512,256]{1,0:T(8,128)(2,1)S(1)}, u32[]{:S(2)}, u32[]{:S(2)}) %collective-permute-start.13) | collective-permute-done | bytes 262176 | tf_op jit(solution)/shard_map/ppermute | solution.py:666
  53.2 1.5 %collective-permute-start.14 = (bf16[512,256]{1,0:T(8,128)(2,1)S(1)}, bf16[512,256]{1,0:T(8,128)(2,1)S(1)}, u32[]{:S(2)}, u32[]{:S(2)}) collective-permute-start(bf16[512,256]{1,0:T(8,128)(2,1)S(1)} %get-tuple-element.123), channel_id=1, source_target_pairs={{0,1},{1,0},{2,3},{3,2},{4,5},{5,4},{6,7},{7,6},{8,9},{9,8},{10,11... | collective-permute-start | bytes 786440 | tf_op jit(solution)/shard_map/ppermute | solution.py:662
  54.7 1.7 %shard_map.85 = (bf16[512,512]{1,0:T(8,128)(2,1)}, bf16[512,512]{1,0:T(8,128)(2,1)}) custom-call(bf16[2,2,128,256]{3,2,1,0:T(8,128)(2,1)S(1)} %get-tuple-element.87.refs_0_, bf16[2,2,128,256]{3,2,1,0:T(8,128)(2,1)S(1)} %get-tuple-element.102.refs_1_, bf16[2,2,128,256]{3,2,1,0:T(8,128)(2,1)S(1)} %collective-permute-done.8.refs_2_, ...), custom_call_target="tpu_custom_call" | custom-call | flops 1000 | bytes 1000 | tf_op jit(solution)/shard_map/pallas_call | solution.py:641
  56.4 1.5 %shard_map.88 = (bf16[512,512]{1,0:T(8,128)(2,1)}, bf16[512,512]{1,0:T(8,128)(2,1)}) custom-call(bf16[512,256]{1,0:T(8,128)(2,1)S(1)} %get-tuple-element.127.refs_0_, bf16[512,256]{1,0:T(8,128)(2,1)S(1)} %get-tuple-element.128.refs_1_, bf16[512,256]{1,0:T(8,128)(2,1)S(1)} %collective-permute-done.15.refs_2_), custom_call_target="tpu_custom_call" | custom-call | flops 1000 | bytes 1000 | tf_op jit(solution)/shard_map/pallas_call | solution.py:578
  57.9 3.6 %collective-permute-done.14.refs_0_ = bf16[512,256]{1,0:T(8,128)(2,1)S(1)} collective-permute-done((bf16[512,256]{1,0:T(8,128)(2,1)S(1)}, bf16[512,256]{1,0:T(8,128)(2,1)S(1)}, u32[]{:S(2)}, u32[]{:S(2)}) %collective-permute-start.14) | collective-permute-done | bytes 262176 | tf_op jit(solution)/shard_map/ppermute | solution.py:662
  61.5 1.0 %shard_map.89 = (bf16[512,512]{1,0:T(8,128)(2,1)}, bf16[512,512]{1,0:T(8,128)(2,1)}) custom-call(bf16[512,256]{1,0:T(8,128)(2,1)S(1)} %collective-permute-done.14.refs_0_, bf16[512,512]{1,0:T(8,128)(2,1)} %get-tuple-element.130.refs_1_, bf16[512,512]{1,0:T(8,128)(2,1)} %get-tuple-element.131.refs_2_), custom_call_target="tpu_custom_call", output_to_operand_aliasing={{0}: (1, {}), {1}: (2, {})} | custom-call | flops 1000 | bytes 1000 | tf_op jit(solution)/shard_map/pallas_call | solution.py:611
  (34 shorter events, 4.7 us)
Async XLA Ops:
  0.6 2.9 %copy-start.2 = (bf16[512,512]{1,0:T(8,128)(2,1)S(1)}, bf16[512,512]{1,0:T(8,128)(2,1)}, u32[]{:S(2)}) copy-start(bf16[512,512]{1,0:T(8,128)(2,1)} %refs_0_.2) | copy-start | bytes 1572868
  1.7 1.9 %copy-start.3 = (bf16[512,512]{1,0:T(8,128)(2,1)S(1)}, bf16[512,512]{1,0:T(8,128)(2,1)}, u32[]{:S(2)}) copy-start(bf16[512,512]{1,0:T(8,128)(2,1)} %refs_1_.2) | copy-start | bytes 1572868
  2.0 9.3 %collective-permute-start = (bf16[512,256]{1,0:T(8,128)(2,1)S(1)}, bf16[512,256]{1,0:T(8,128)(2,1)S(1)}, u32[]{:S(2)}, u32[]{:S(2)}) collective-permute-start(bf16[512,256]{1,0:T(8,128)(2,1)S(1)} %shard_map.76), channel_id=1, source_target_pairs={{0,1},{1,0},{2,3},{3,2},{4,5},{5,4},{6,7},{7,6},{8,9},{9,8},{10,11... | collective-permute-start | bytes 786440 | tf_op jit(solution)/shard_map/ppermute | solution.py:662
  3.6 1.1 %copy-start = (bf16[512,512]{1,0:T(8,128)(2,1)S(1)}, bf16[512,512]{1,0:T(8,128)(2,1)}, u32[]{:S(2)}) copy-start(bf16[512,512]{1,0:T(8,128)(2,1)} %refs_0_.3) | copy-start | bytes 1572868
  3.6 1.2 %copy-start.1 = (bf16[512,512]{1,0:T(8,128)(2,1)S(1)}, bf16[512,512]{1,0:T(8,128)(2,1)}, u32[]{:S(2)}) copy-start(bf16[512,512]{1,0:T(8,128)(2,1)} %refs_1_.3) | copy-start | bytes 1572868
  3.9 13.0 %collective-permute-start.1 = (bf16[512,256]{1,0:T(8,128)(2,1)S(1)}, bf16[512,256]{1,0:T(8,128)(2,1)S(1)}, u32[]{:S(2)}, u32[]{:S(2)}) collective-permute-start(bf16[512,256]{1,0:T(8,128)(2,1)S(1)} %shard_map.77), channel_id=1, source_target_pairs={{0,1},{1,0},{2,3},{3,2},{4,5},{5,4},{6,7},{7,6},{8,9},{9,8},{10,11... | collective-permute-start | bytes 786440 | tf_op jit(solution)/shard_map/ppermute | solution.py:662
  5.4 17.2 %collective-permute-start.2 = (bf16[512,256]{1,0:T(8,128)(2,1)S(1)}, bf16[512,256]{1,0:T(8,128)(2,1)S(1)}, u32[]{:S(2)}, u32[]{:S(2)}) collective-permute-start(bf16[512,256]{1,0:T(8,128)(2,1)S(1)} %get-tuple-element.84), channel_id=1, source_target_pairs={{0,1},{1,0},{2,3},{3,2},{4,5},{5,4},{6,7},{7,6},{8,9},{9,8},{10,11... | collective-permute-start | bytes 786440 | tf_op jit(solution)/shard_map/ppermute | solution.py:662
  11.4 13.0 %collective-permute-start.3 = (bf16[512,256]{1,0:T(8,128)(2,1)S(1)}, bf16[512,256]{1,0:T(8,128)(2,1)S(1)}, u32[]{:S(2)}, u32[]{:S(2)}) collective-permute-start(bf16[512,256]{1,0:T(8,128)(2,1)S(1)} %get-tuple-element.85), channel_id=1, source_target_pairs={{0,2},{1,3},{2,0},{3,1},{4,6},{5,7},{6,4},{7,5},{8,10},{9,11},{10,... | collective-permute-start | bytes 786440 | tf_op jit(solution)/shard_map/ppermute | solution.py:665
  11.5 13.0 %collective-permute-start.4 = (bf16[512,256]{1,0:T(8,128)(2,1)S(1)}, bf16[512,256]{1,0:T(8,128)(2,1)S(1)}, u32[]{:S(2)}, u32[]{:S(2)}) collective-permute-start(bf16[512,256]{1,0:T(8,128)(2,1)S(1)} %get-tuple-element.86), channel_id=1, source_target_pairs={{2,4},{3,5},{4,2},{5,3},{6,8},{7,9},{8,6},{9,7},{10,12},{11,13},{1... | collective-permute-start | bytes 786440 | tf_op jit(solution)/shard_map/ppermute | solution.py:666
  17.3 16.6 %collective-permute-start.7 = (bf16[512,256]{1,0:T(8,128)(2,1)S(1)}, bf16[512,256]{1,0:T(8,128)(2,1)S(1)}, u32[]{:S(2)}, u32[]{:S(2)}) collective-permute-start(bf16[512,256]{1,0:T(8,128)(2,1)S(1)} %get-tuple-element.101), channel_id=1, source_target_pairs={{0,1},{1,0},{2,3},{3,2},{4,5},{5,4},{6,7},{7,6},{8,9},{9,8},{10,11... | collective-permute-start | bytes 786440 | tf_op jit(solution)/shard_map/ppermute | solution.py:662
  18.8 16.6 %collective-permute-start.5 = (bf16[512,256]{1,0:T(8,128)(2,1)S(1)}, bf16[512,256]{1,0:T(8,128)(2,1)S(1)}, u32[]{:S(2)}, u32[]{:S(2)}) collective-permute-start(bf16[512,256]{1,0:T(8,128)(2,1)S(1)} %get-tuple-element.98), channel_id=1, source_target_pairs={{0,2},{1,3},{2,0},{3,1},{4,6},{5,7},{6,4},{7,5},{8,10},{9,11},{10,... | collective-permute-start | bytes 786440 | tf_op jit(solution)/shard_map/ppermute | solution.py:665
  22.5 13.0 %collective-permute-start.6 = (bf16[512,256]{1,0:T(8,128)(2,1)S(1)}, bf16[512,256]{1,0:T(8,128)(2,1)S(1)}, u32[]{:S(2)}, u32[]{:S(2)}) collective-permute-start(bf16[512,256]{1,0:T(8,128)(2,1)S(1)} %get-tuple-element.99), channel_id=1, source_target_pairs={{2,4},{3,5},{4,2},{5,3},{6,8},{7,9},{8,6},{9,7},{10,12},{11,13},{1... | collective-permute-start | bytes 786440 | tf_op jit(solution)/shard_map/ppermute | solution.py:666
  30.0 11.6 %collective-permute-start.9 = (bf16[512,256]{1,0:T(8,128)(2,1)S(1)}, bf16[512,256]{1,0:T(8,128)(2,1)S(1)}, u32[]{:S(2)}, u32[]{:S(2)}) collective-permute-start(bf16[512,256]{1,0:T(8,128)(2,1)S(1)} %get-tuple-element.105), channel_id=1, source_target_pairs={{0,2},{1,3},{2,0},{3,1},{4,6},{5,7},{6,4},{7,5},{8,10},{9,11},{10,... | collective-permute-start | bytes 786440 | tf_op jit(solution)/shard_map/ppermute | solution.py:665
  31.7 10.5 %collective-permute-start.10 = (bf16[512,256]{1,0:T(8,128)(2,1)S(1)}, bf16[512,256]{1,0:T(8,128)(2,1)S(1)}, u32[]{:S(2)}, u32[]{:S(2)}) collective-permute-start(bf16[512,256]{1,0:T(8,128)(2,1)S(1)} %get-tuple-element.106), channel_id=1, source_target_pairs={{2,4},{3,5},{4,2},{5,3},{6,8},{7,9},{8,6},{9,7},{10,12},{11,13},{1... | collective-permute-start | bytes 786440 | tf_op jit(solution)/shard_map/ppermute | solution.py:666
  33.9 11.1 %collective-permute-start.8 = (bf16[2,2,128,256]{3,2,1,0:T(8,128)(2,1)S(1)}, bf16[2,2,128,256]{3,2,1,0:T(8,128)(2,1)S(1)}, u32[]{:S(2)}, u32[]{:S(2)}) collective-permute-start(bf16[2,2,128,256]{3,2,1,0:T(8,128)(2,1)S(1)} %get-tuple-element.103), channel_id=1, source_target_pairs={{0,1},{1,0},{2,3},{3,2},{4,5},{5,4},{6,7},{7,6},{8,9},{9,8},{10,11... | collective-permute-start | bytes 786440 | tf_op jit(solution)/shard_map/ppermute | solution.py:662
  41.0 9.0 %collective-permute-start.11 = (bf16[2,2,128,256]{3,2,1,0:T(8,128)(2,1)S(1)}, bf16[2,2,128,256]{3,2,1,0:T(8,128)(2,1)S(1)}, u32[]{:S(2)}, u32[]{:S(2)}) collective-permute-start(bf16[2,2,128,256]{3,2,1,0:T(8,128)(2,1)S(1)} %get-tuple-element.113), channel_id=1, source_target_pairs={{0,1},{1,0},{2,3},{3,2},{4,5},{5,4},{6,7},{7,6},{8,9},{9,8},{10,11... | collective-permute-start | bytes 786440 | tf_op jit(solution)/shard_map/ppermute | solution.py:662
  42.2 7.9 %collective-permute-start.12 = (bf16[512,256]{1,0:T(8,128)(2,1)S(1)}, bf16[512,256]{1,0:T(8,128)(2,1)S(1)}, u32[]{:S(2)}, u32[]{:S(2)}) collective-permute-start(bf16[512,256]{1,0:T(8,128)(2,1)S(1)} %get-tuple-element.115), channel_id=1, source_target_pairs={{0,2},{1,3},{2,0},{3,1},{4,6},{5,7},{6,4},{7,5},{8,10},{9,11},{10,... | collective-permute-start | bytes 786440 | tf_op jit(solution)/shard_map/ppermute | solution.py:665
  42.5 10.5 %collective-permute-start.13 = (bf16[512,256]{1,0:T(8,128)(2,1)S(1)}, bf16[512,256]{1,0:T(8,128)(2,1)S(1)}, u32[]{:S(2)}, u32[]{:S(2)}) collective-permute-start(bf16[512,256]{1,0:T(8,128)(2,1)S(1)} %get-tuple-element.116), channel_id=1, source_target_pairs={{2,4},{3,5},{4,2},{5,3},{6,8},{7,9},{8,6},{9,7},{10,12},{11,13},{1... | collective-permute-start | bytes 786440 | tf_op jit(solution)/shard_map/ppermute | solution.py:666
  45.2 11.2 %collective-permute-start.15 = (bf16[512,256]{1,0:T(8,128)(2,1)S(1)}, bf16[512,256]{1,0:T(8,128)(2,1)S(1)}, u32[]{:S(2)}, u32[]{:S(2)}) collective-permute-start(bf16[512,256]{1,0:T(8,128)(2,1)S(1)} %get-tuple-element.129), channel_id=1, source_target_pairs={{0,1},{1,0},{2,3},{3,2},{4,5},{5,4},{6,7},{7,6},{8,9},{9,8},{10,11... | collective-permute-start | bytes 786440 | tf_op jit(solution)/shard_map/ppermute | solution.py:662
  53.2 8.3 %collective-permute-start.14 = (bf16[512,256]{1,0:T(8,128)(2,1)S(1)}, bf16[512,256]{1,0:T(8,128)(2,1)S(1)}, u32[]{:S(2)}, u32[]{:S(2)}) collective-permute-start(bf16[512,256]{1,0:T(8,128)(2,1)S(1)} %get-tuple-element.123), channel_id=1, source_target_pairs={{0,1},{1,0},{2,3},{3,2},{4,5},{5,4},{6,7},{7,6},{8,9},{9,8},{10,11... | collective-permute-start | bytes 786440 | tf_op jit(solution)/shard_map/ppermute | solution.py:662
